TPU v7x, 32 devices: a whole 2x2x4 slice. The times are simulated.
32 devices in a mesh: seg: 8 (over y, x, core), row: 4 (over z).
Axes of the slice: x: 2, y: 2, z: 4, core: 2. Of those that a mesh axis runs over, the one named last changes fastest.
Arguments:
- fill_blocks: int32 [16, 4], P('seg'), may hold values from 0 to 7, all different within a row
- fill_mask: int32 [16, 4], P('seg'), may hold values 0 or 1
- inv_diag: float32 [16, 512, 512], P('seg'), as said below
- factor_off: float32 [16, 256, 512], P('seg', 'row'), may hold values from -1.4375 to 1.4375
Outputs:
- cov_diag: float32 [16, 512, 512], P('seg', 'row')
- cov_off: float32 [16, 256, 512], P('seg', 'row')
Inputs may be any that keep to these rules, and one draw needn't show every extreme that they name: The 4 entries of a row of fill_blocks are different. Each inv_diag[k] is lower triangular with a positive diagonal.
All inputs are finite; a program needn't handle non-finite values. No bound on the sum of `fill_mask` on one device may be relied on, other than what follows from the above.
Results may differ from a plain program's by a relative error of at most 0.0003.
Values sent between devices are 32-bit elements; how exact they have to be, the bound alone decides.
No kernel may reach another device: no remote copies, remote signals or barrier semaphores. Data moves between devices by JAX's collectives and lax.ppermute only.
A program may use at most 64 MiB of HBM per device.

v0:
```python
import jax
import jax.numpy as jnp
from jax import lax
from jax.sharding import PartitionSpec as P

BLOCK = 64


def from_behind(block, axis, distance):
    devices = range(lax.axis_size(axis))
    route = [(i - distance, i) for i in devices if i - distance in devices]
    return lax.ppermute(block, axis, route)


def product(left, right):
    return jnp.dot(left, right, precision=lax.Precision.HIGHEST, preferred_element_type=jnp.float32)


def pick_columns(matrix, chosen_blocks):
    col_blocks = matrix.shape[1] // BLOCK
    tiles = jnp.take(matrix.reshape(matrix.shape[0], col_blocks, BLOCK), chosen_blocks, axis=1)
    return tiles.reshape(matrix.shape[0], chosen_blocks.shape[0] * BLOCK)


def body(fill_blocks, fill_mask, inv_diag, factor_off):
    panels = inv_diag.shape[0]
    panel_width = inv_diag.shape[2]
    seg_count = lax.axis_size("seg")
    row_count = lax.axis_size("row")
    seg_at = lax.axis_index("seg")
    row_at = lax.axis_index("row")
    local_rows = factor_off.shape[1]
    slots_here = local_rows // BLOCK
    cols_here = panel_width // row_count
    slot_live = fill_mask.astype(jnp.float32)
    global_panel = seg_at * panels + jnp.arange(panels, dtype=jnp.int32)
    not_last = (global_panel < seg_count * panels - 1).astype(jnp.float32)
    live_here = lax.dynamic_slice_in_dim(slot_live, row_at * slots_here, slots_here, 1)
    row_keep = jnp.repeat(live_here * not_last[:, None], BLOCK, axis=1)
    slot_keep = jnp.repeat(live_here, BLOCK, axis=1)
    local_map = jnp.einsum(
        "prw,pwv->prv",
        factor_off * row_keep[:, :, None],
        inv_diag,
        precision=lax.Precision.HIGHEST,
        preferred_element_type=jnp.float32,
    )
    factor_map = lax.all_gather(local_map, "row", axis=1, tiled=True)
    prior_fill = from_behind(fill_blocks[panels - 1 :], "seg", 1)
    before_fill = jnp.concatenate([prior_fill, fill_blocks[: panels - 1]], 0)
    link_maps = []
    base_terms = []
    for position in range(panels):
        link_maps.append(pick_columns(factor_map[position], before_fill[position]))
        chosen = pick_columns(inv_diag[position], before_fill[position])
        base_terms.append(product(chosen.T, chosen))
    carried = link_maps[panels - 1]
    constant = base_terms[panels - 1]
    position = 0
    constant = (
        product(link_maps[position].T, product(constant, link_maps[position]))
        + base_terms[position]
    )
    carried = product(carried, link_maps[position])
    nothing = jnp.zeros_like(constant)

    def advance(counter, incoming):
        outgoing = product(carried.T, product(incoming, carried)) + constant
        return from_behind(outgoing, "seg", -1)

    incoming_cov = lax.fori_loop(0, seg_count - 1, advance, nothing)
    diag_parts = [None] * panels
    cross_parts = [None] * panels
    for position in range(panels - 1, -1, -1):
        weighted = product(incoming_cov, factor_map[position])
        own_rows = lax.dynamic_slice_in_dim(weighted, row_at * local_rows, local_rows, 0)
        cross_parts[position] = -own_rows * slot_keep[position][:, None]
        inverse_cols = lax.dynamic_slice_in_dim(
            inv_diag[position], row_at * cols_here, cols_here, 1
        )
        factor_cols = lax.dynamic_slice_in_dim(
            factor_map[position], row_at * cols_here, cols_here, 1
        )
        diag_parts[position] = product(inverse_cols.T, inv_diag[position]) + product(
            factor_cols.T, weighted
        )
        incoming_cov = (
            product(link_maps[position].T, product(incoming_cov, link_maps[position]))
            + base_terms[position]
        )
    return (jnp.stack(diag_parts), jnp.stack(cross_parts))


def solution(mesh):
    placed = (P("seg", None), P("seg", None), P("seg", None, None), P("seg", "row", None))
    return jax.shard_map(
        body,
        mesh=mesh,
        in_specs=placed,
        out_specs=(P("seg", "row", None), P("seg", "row", None)),
        check_vma=False,
    )
```

profile of v0, /device:TPU:3, one launch (start us, length us, event | category | flops | bytes accessed | tf_op | source)
XLA Modules:
  0.0 127.6 jit_solution(1706380142592881144)
XLA Ops:
  7.2 0.8 convert_element_type.5
  8.1 0.2 fusion.26
  8.2 3.8 %fusion.14 = f32[2,64,512]{2,1,0:T(8,128)} fusion(f32[2,512,512]{2,1,0:T(8,128)} %param.12, f32[2,64,512]{2,1,0:T(8,128)} %param.13, f32[2]{0:T(128)S(1)} %get-tuple-element.45), kind=kOutput, calls=%fused_computation.27 | convolution fusion | flops 402718720 | bytes 2621448 | tf_op jit(solution)/shard_map/prw,pwv->prv/dot_general | solution.py:41
  12.1 3.7 %collective-permute-start.1 = (s32[1,4]{1,0:T(1,128)S(1)}, s32[1,4]{1,0:T(1,128)S(1)}, u32[]{:S(2)}, u32[]{:S(2)}) collective-permute-start(s32[1,4]{1,0:T(1,128)S(1)} %slice.40), channel_id=1, source_target_pairs={{0,4},{4,8},{8,12},{12,16},{16,20},{20,24},{24,28},{1,5},{5,9},{9,... | collective-permute-start | bytes 56 | tf_op jit(solution)/shard_map/ppermute | solution.py:12
  15.8 1.5 %fusion.31 = (f32[1,512,512]{2,1,0:T(8,128)}, f32[1,512,512]{2,1,0:T(8,128)}) fusion(f32[2,512,512]{2,1,0:T(8,128)S(1)} %copy-done), kind=kLoop, calls=%fused_computation.56 | loop fusion | bytes 4194304 | tf_op jit(solution)/shard_map/slice | solution.py:79
  17.3 1.6 %copy.13 = f32[1,512,512]{1,2,0:T(8,128)S(1)} copy(f32[1,512,512]{2,1,0:T(8,128)} %get-tuple-element.48) | data formatting | bytes 2097152
  18.9 1.4 %gather_fusion.2 = f32[4,512,64]{1,2,0:T(8,128)} fusion(f32[512,8,64]{0,2,1:T(8,128)S(1)} %bitcast.96, s32[1024]{0:T(1024)S(1)} %pad_clamp_fusion.1), kind=kCustom, calls=%fused_computation.1.clone | custom fusion | bytes 1048592 | tf_op jit(solution)/shard_map/jit(_take)/gather | solution.py:21
  20.3 1.2 broadcast_select_fusion.1
  21.5 0.6 fusion.36
  22.1 2.6 %copy.12 = f32[1,512,512]{1,2,0:T(8,128)} copy(f32[1,512,512]{2,1,0:T(8,128)} %get-tuple-element.47) | data formatting | bytes 2097152
  24.7 0.5 fusion.33
  25.2 1.4 %fusion.3 = f32[128,512]{1,0:T(8,128)} fusion(f32[1,512,512]{1,2,0:T(8,128)S(1)} %copy.13, s32[]{:T(128)S(6)} %select_n.26, f32[2,512,512]{2,1,0:T(8,128)S(1)} %copy-done), kind=kOutput, calls=%fused_computation.12 | convolution fusion | flops 402653184 | bytes 1572868 | tf_op jit(solution)/shard_map/dot_general | solution.py:16
  26.6 2.5 %fusion.5 = f32[128,512]{1,0:T(8,128)} fusion(f32[1,512,512]{1,2,0:T(8,128)} %copy.12, s32[]{:T(128)S(6)} %select_n.26, f32[2,512,512]{2,1,0:T(8,128)S(1)} %copy-done), kind=kOutput, calls=%fused_computation.14 | convolution fusion | flops 402653184 | bytes 1572868 | tf_op jit(solution)/shard_map/dot_general | solution.py:16
  29.1 0.6 gather_fusion.3
  29.8 0.6 fusion.38
  30.4 10.8 %all-gather.2.cloned.1.call-done = f32[2,256,512]{2,1,0:T(8,128)} async-done(((f32[2,64,512]{2,1,0:T(8,128)}), f32[2,256,512]{2,1,0:T(8,128)}) %all-gather.2.cloned.1.call-update) | async-done | bytes 1048592 | tf_op jit(solution)/shard_map/all_gather | solution.py:48
  41.3 1.3 fusion.32
  42.5 0.2 copy.9
  42.7 0.6 gather_fusion.1
  43.4 0.4 fusion.37
  43.8 0.4 convolution_add_fusion.3
  44.2 0.1 copy.11
  44.4 0.2 copy.8
  44.6 0.6 gather_fusion
  45.2 0.6 fusion.35
  45.9 68.6 %while.10 = (s32[]{:T(128)}, f32[256,256]{0,1:T(8,128)S(1)}, f32[256,256]{1,0:T(8,128)S(1)}, f32[256,256]{0,1:T(8,128)S(1)}, s32[]{:T(128)}) while((s32[]{:T(128)}, f32[256,256]{0,1:T(8,128)S(1)}, f32[256,256]{1,0:T(8,128)S(1)}, f32[256,256]{0,1:T(8,128)S(1)}, s32[]{:T(128)}) %tuple.32), condition=%wide.region_1.0_spmd, body=%wide.region_0.3_spmd.sunk | while | flops 402718720 | bytes 2883685 | solution.py:71
  45.9 0.6 fusion.73
  46.5 0.6 fusion.74
  47.1 2.7 %collective-permute-start = (f32[256,256]{0,1:T(8,128)S(1)}, f32[256,256]{0,1:T(8,128)S(1)}, u32[]{:S(2)}, u32[]{:S(2)}) collective-permute-start(f32[256,256]{0,1:T(8,128)S(1)} %fusion.74), channel_id=1, source_target_pairs={{4,0},{8,4},{12,8},{16,12},{20,16},{24,20},{28,24},{5,1},{9,5},{13... | collective-permute-start | bytes 786440 | tf_op jit(solution)/shard_map/while/body/eval_jaxpr/ppermute | solution.py:12
  49.8 5.9 %collective-permute-done = f32[256,256]{0,1:T(8,128)S(1)} collective-permute-done((f32[256,256]{0,1:T(8,128)S(1)}, f32[256,256]{0,1:T(8,128)S(1)}, u32[]{:S(2)}, u32[]{:S(2)}) %collective-permute-start) | collective-permute-done | bytes 262176 | tf_op jit(solution)/shard_map/while/body/eval_jaxpr/ppermute | solution.py:12
  55.7 0.6 fusion.73
  56.3 0.6 fusion.74
  56.9 1.9 %collective-permute-start = (f32[256,256]{0,1:T(8,128)S(1)}, f32[256,256]{0,1:T(8,128)S(1)}, u32[]{:S(2)}, u32[]{:S(2)}) collective-permute-start(f32[256,256]{0,1:T(8,128)S(1)} %fusion.74), channel_id=1, source_target_pairs={{4,0},{8,4},{12,8},{16,12},{20,16},{24,20},{28,24},{5,1},{9,5},{13... | collective-permute-start | bytes 786440 | tf_op jit(solution)/shard_map/while/body/eval_jaxpr/ppermute | solution.py:12
  58.8 6.7 %collective-permute-done = f32[256,256]{0,1:T(8,128)S(1)} collective-permute-done((f32[256,256]{0,1:T(8,128)S(1)}, f32[256,256]{0,1:T(8,128)S(1)}, u32[]{:S(2)}, u32[]{:S(2)}) %collective-permute-start) | collective-permute-done | bytes 262176 | tf_op jit(solution)/shard_map/while/body/eval_jaxpr/ppermute | solution.py:12
  65.5 0.6 fusion.73
  66.1 0.6 fusion.74
  66.7 1.9 %collective-permute-start = (f32[256,256]{0,1:T(8,128)S(1)}, f32[256,256]{0,1:T(8,128)S(1)}, u32[]{:S(2)}, u32[]{:S(2)}) collective-permute-start(f32[256,256]{0,1:T(8,128)S(1)} %fusion.74), channel_id=1, source_target_pairs={{4,0},{8,4},{12,8},{16,12},{20,16},{24,20},{28,24},{5,1},{9,5},{13... | collective-permute-start | bytes 786440 | tf_op jit(solution)/shard_map/while/body/eval_jaxpr/ppermute | solution.py:12
  68.6 6.7 %collective-permute-done = f32[256,256]{0,1:T(8,128)S(1)} collective-permute-done((f32[256,256]{0,1:T(8,128)S(1)}, f32[256,256]{0,1:T(8,128)S(1)}, u32[]{:S(2)}, u32[]{:S(2)}) %collective-permute-start) | collective-permute-done | bytes 262176 | tf_op jit(solution)/shard_map/while/body/eval_jaxpr/ppermute | solution.py:12
  75.3 0.6 fusion.73
  75.9 0.6 fusion.74
  76.5 1.9 %collective-permute-start = (f32[256,256]{0,1:T(8,128)S(1)}, f32[256,256]{0,1:T(8,128)S(1)}, u32[]{:S(2)}, u32[]{:S(2)}) collective-permute-start(f32[256,256]{0,1:T(8,128)S(1)} %fusion.74), channel_id=1, source_target_pairs={{4,0},{8,4},{12,8},{16,12},{20,16},{24,20},{28,24},{5,1},{9,5},{13... | collective-permute-start | bytes 786440 | tf_op jit(solution)/shard_map/while/body/eval_jaxpr/ppermute | solution.py:12
  78.4 6.7 %collective-permute-done = f32[256,256]{0,1:T(8,128)S(1)} collective-permute-done((f32[256,256]{0,1:T(8,128)S(1)}, f32[256,256]{0,1:T(8,128)S(1)}, u32[]{:S(2)}, u32[]{:S(2)}) %collective-permute-start) | collective-permute-done | bytes 262176 | tf_op jit(solution)/shard_map/while/body/eval_jaxpr/ppermute | solution.py:12
  85.1 0.6 fusion.73
  85.7 0.6 fusion.74
  86.3 1.9 %collective-permute-start = (f32[256,256]{0,1:T(8,128)S(1)}, f32[256,256]{0,1:T(8,128)S(1)}, u32[]{:S(2)}, u32[]{:S(2)}) collective-permute-start(f32[256,256]{0,1:T(8,128)S(1)} %fusion.74), channel_id=1, source_target_pairs={{4,0},{8,4},{12,8},{16,12},{20,16},{24,20},{28,24},{5,1},{9,5},{13... | collective-permute-start | bytes 786440 | tf_op jit(solution)/shard_map/while/body/eval_jaxpr/ppermute | solution.py:12
  88.2 6.7 %collective-permute-done = f32[256,256]{0,1:T(8,128)S(1)} collective-permute-done((f32[256,256]{0,1:T(8,128)S(1)}, f32[256,256]{0,1:T(8,128)S(1)}, u32[]{:S(2)}, u32[]{:S(2)}) %collective-permute-start) | collective-permute-done | bytes 262176 | tf_op jit(solution)/shard_map/while/body/eval_jaxpr/ppermute | solution.py:12
  94.9 0.6 fusion.73
  95.5 0.6 fusion.74
  96.1 1.9 %collective-permute-start = (f32[256,256]{0,1:T(8,128)S(1)}, f32[256,256]{0,1:T(8,128)S(1)}, u32[]{:S(2)}, u32[]{:S(2)}) collective-permute-start(f32[256,256]{0,1:T(8,128)S(1)} %fusion.74), channel_id=1, source_target_pairs={{4,0},{8,4},{12,8},{16,12},{20,16},{24,20},{28,24},{5,1},{9,5},{13... | collective-permute-start | bytes 786440 | tf_op jit(solution)/shard_map/while/body/eval_jaxpr/ppermute | solution.py:12
  98.0 6.7 %collective-permute-done = f32[256,256]{0,1:T(8,128)S(1)} collective-permute-done((f32[256,256]{0,1:T(8,128)S(1)}, f32[256,256]{0,1:T(8,128)S(1)}, u32[]{:S(2)}, u32[]{:S(2)}) %collective-permute-start) | collective-permute-done | bytes 262176 | tf_op jit(solution)/shard_map/while/body/eval_jaxpr/ppermute | solution.py:12
  104.7 0.6 fusion.73
  105.3 0.6 fusion.74
  105.9 1.9 %collective-permute-start = (f32[256,256]{0,1:T(8,128)S(1)}, f32[256,256]{0,1:T(8,128)S(1)}, u32[]{:S(2)}, u32[]{:S(2)}) collective-permute-start(f32[256,256]{0,1:T(8,128)S(1)} %fusion.74), channel_id=1, source_target_pairs={{4,0},{8,4},{12,8},{16,12},{20,16},{24,20},{28,24},{5,1},{9,5},{13... | collective-permute-start | bytes 786440 | tf_op jit(solution)/shard_map/while/body/eval_jaxpr/ppermute | solution.py:12
  107.8 6.7 %collective-permute-done = f32[256,256]{0,1:T(8,128)S(1)} collective-permute-done((f32[256,256]{0,1:T(8,128)S(1)}, f32[256,256]{0,1:T(8,128)S(1)}, u32[]{:S(2)}, u32[]{:S(2)}) %collective-permute-start) | collective-permute-done | bytes 262176 | tf_op jit(solution)/shard_map/while/body/eval_jaxpr/ppermute | solution.py:12
  114.5 0.6 fusion.39
  115.1 0.4 convolution_add_fusion.2
  115.5 0.2 copy-done.2
  115.7 0.6 fusion.9
  116.3 0.5 fusion.2
  116.8 0.6 fusion.7
  117.5 0.5 fusion.1
  117.9 1.2 multiply_bitcast_fusion
  119.2 0.7 pad_maximum_fusion.1
  119.9 0.8 pad_maximum_fusion
  (24 shorter events, 0.4 us)
Async XLA Ops:
  7.2 8.6 %copy-start = (f32[2,512,512]{2,1,0:T(8,128)S(1)}, f32[2,512,512]{2,1,0:T(8,128)}, u32[]{:S(2)}) copy-start(f32[2,512,512]{2,1,0:T(8,128)} %param.12) | copy-start | bytes 6291460
  7.2 4.9 %copy-start.5 = (s32[2,4]{1,0:T(2,128)S(1)}, s32[2,4]{1,0:T(2,128)}, u32[]{:S(2)}) copy-start(s32[2,4]{1,0:T(2,128)} %param.10) | copy-start | bytes 100
  7.2 34.1 %all-gather.2.cloned.1.call-start = ((), (), s32[]{:S(2)}) async-start(), calls=%async_computation | async-start | bytes 1310720 | tf_op jit(solution)/shard_map/all_gather | solution.py:48
  12.1 16.9 %collective-permute-start.1 = (s32[1,4]{1,0:T(1,128)S(1)}, s32[1,4]{1,0:T(1,128)S(1)}, u32[]{:S(2)}, u32[]{:S(2)}) collective-permute-start(s32[1,4]{1,0:T(1,128)S(1)} %slice.40), channel_id=1, source_target_pairs={{0,4},{4,8},{8,12},{12,16},{16,20},{20,24},{24,28},{1,5},{5,9},{9,... | collective-permute-start | bytes 56 | tf_op jit(solution)/shard_map/ppermute | solution.py:12
  26.6 2.5 %copy-start.1 = (f32[1,512,512]{1,2,0:T(8,128)S(1)}, f32[1,512,512]{1,2,0:T(8,128)}, u32[]{:S(2)}) copy-start(f32[1,512,512]{1,2,0:T(8,128)} %copy.12) | copy-start | bytes 3145732
  47.1 8.6 %collective-permute-start = (f32[256,256]{0,1:T(8,128)S(1)}, f32[256,256]{0,1:T(8,128)S(1)}, u32[]{:S(2)}, u32[]{:S(2)}) collective-permute-start(f32[256,256]{0,1:T(8,128)S(1)} %fusion.74), channel_id=1, source_target_pairs={{4,0},{8,4},{12,8},{16,12},{20,16},{24,20},{28,24},{5,1},{9,5},{13... | collective-permute-start | bytes 786440 | tf_op jit(solution)/shard_map/while/body/eval_jaxpr/ppermute | solution.py:12
  56.9 8.6 %collective-permute-start = (f32[256,256]{0,1:T(8,128)S(1)}, f32[256,256]{0,1:T(8,128)S(1)}, u32[]{:S(2)}, u32[]{:S(2)}) collective-permute-start(f32[256,256]{0,1:T(8,128)S(1)} %fusion.74), channel_id=1, source_target_pairs={{4,0},{8,4},{12,8},{16,12},{20,16},{24,20},{28,24},{5,1},{9,5},{13... | collective-permute-start | bytes 786440 | tf_op jit(solution)/shard_map/while/body/eval_jaxpr/ppermute | solution.py:12
  66.7 8.6 %collective-permute-start = (f32[256,256]{0,1:T(8,128)S(1)}, f32[256,256]{0,1:T(8,128)S(1)}, u32[]{:S(2)}, u32[]{:S(2)}) collective-permute-start(f32[256,256]{0,1:T(8,128)S(1)} %fusion.74), channel_id=1, source_target_pairs={{4,0},{8,4},{12,8},{16,12},{20,16},{24,20},{28,24},{5,1},{9,5},{13... | collective-permute-start | bytes 786440 | tf_op jit(solution)/shard_map/while/body/eval_jaxpr/ppermute | solution.py:12
  76.5 8.6 %collective-permute-start = (f32[256,256]{0,1:T(8,128)S(1)}, f32[256,256]{0,1:T(8,128)S(1)}, u32[]{:S(2)}, u32[]{:S(2)}) collective-permute-start(f32[256,256]{0,1:T(8,128)S(1)} %fusion.74), channel_id=1, source_target_pairs={{4,0},{8,4},{12,8},{16,12},{20,16},{24,20},{28,24},{5,1},{9,5},{13... | collective-permute-start | bytes 786440 | tf_op jit(solution)/shard_map/while/body/eval_jaxpr/ppermute | solution.py:12
  86.3 8.6 %collective-permute-start = (f32[256,256]{0,1:T(8,128)S(1)}, f32[256,256]{0,1:T(8,128)S(1)}, u32[]{:S(2)}, u32[]{:S(2)}) collective-permute-start(f32[256,256]{0,1:T(8,128)S(1)} %fusion.74), channel_id=1, source_target_pairs={{4,0},{8,4},{12,8},{16,12},{20,16},{24,20},{28,24},{5,1},{9,5},{13... | collective-permute-start | bytes 786440 | tf_op jit(solution)/shard_map/while/body/eval_jaxpr/ppermute | solution.py:12
  96.1 8.6 %collective-permute-start = (f32[256,256]{0,1:T(8,128)S(1)}, f32[256,256]{0,1:T(8,128)S(1)}, u32[]{:S(2)}, u32[]{:S(2)}) collective-permute-start(f32[256,256]{0,1:T(8,128)S(1)} %fusion.74), channel_id=1, source_target_pairs={{4,0},{8,4},{12,8},{16,12},{20,16},{24,20},{28,24},{5,1},{9,5},{13... | collective-permute-start | bytes 786440 | tf_op jit(solution)/shard_map/while/body/eval_jaxpr/ppermute | solution.py:12
  105.9 8.6 %collective-permute-start = (f32[256,256]{0,1:T(8,128)S(1)}, f32[256,256]{0,1:T(8,128)S(1)}, u32[]{:S(2)}, u32[]{:S(2)}) collective-permute-start(f32[256,256]{0,1:T(8,128)S(1)} %fusion.74), channel_id=1, source_target_pairs={{4,0},{8,4},{12,8},{16,12},{20,16},{24,20},{28,24},{5,1},{9,5},{13... | collective-permute-start | bytes 786440 | tf_op jit(solution)/shard_map/while/body/eval_jaxpr/ppermute | solution.py:12
  114.5 1.2 copy-start.2
  114.5 1.8 %copy-start.4 = (f32[128,512]{1,0:T(8,128)S(1)}, f32[128,512]{1,0:T(8,128)}, u32[]{:S(2)}) copy-start(f32[128,512]{1,0:T(8,128)} %fusion.5) | copy-start | bytes 786436
  115.7 1.7 %copy-start.3 = (f32[128,512]{1,0:T(8,128)S(1)}, f32[128,512]{1,0:T(8,128)}, u32[]{:S(2)}) copy-start(f32[128,512]{1,0:T(8,128)} %fusion.3) | copy-start | bytes 786436
Sparse Core Ops, SparseCore 0:
  12.2 29.0 all-gather.1
where the time goes:
time: 128 us
  waiting for transfers between devices  56.7 us (44%)
  matrix products  21.8 us (17%)
  starting transfers between devices  18 us (14%)
  between operations  14.3 us (11%)
  local copies, waits for them, and re-layouts  11.3 us (9%)
  other arithmetic  5.29 us (4%)
    ppermute x8, waiting for transfers between devices, from_behind(): return lax.ppermute(block, axis, route)  45.8 us
    dot_general x27, matrix products, product(): jnp.dot(left, right, precision=lax.Precision.HIGHEST, preferred_element_t...  18 us
    ppermute x8, starting transfers between devices, from_behind(): return lax.ppermute(block, axis, route)  17.9 us
    all_gather x1, waiting for transfers between devices, body(): factor_map = lax.all_gather(local_map, 'row', axis=1, tiled=True)  10.8 us
    unnamed x14, local copies, waits for them, and re-layouts  4.37 us
    dot_general x1, matrix products, body(): jnp.einsum('prw,pwv->prv', factor_off * row_keep[:, :, None], inv_diag, p...  3.83 us
    gather x4, local copies, waits for them, and re-layouts, pick_columns(): jnp.take(matrix.reshape(matrix.shape[0], col_blocks, BLOCK), chosen_block...  3.09 us
    another operation x3, other arithmetic, body(): return (jnp.stack(diag_parts), jnp.stack(cross_parts))  2.76 us
  transfers between devices with their start and end apart: 9, of which 8 were waited for; matrix products, arithmetic and copies ran while one was open for 11% of the time, Pallas kernels for 0%

commit v1 on v0

v1 whole, which is shorter than its diff:
```python
import functools

import jax
import jax.numpy as jnp
from jax import lax
from jax.experimental import pallas as pl
from jax.experimental.pallas import tpu as pltpu
from jax.sharding import PartitionSpec as P

BLOCK = 64
LANES = 128
F32 = jnp.float32
BF16 = jnp.bfloat16
NN = (((1,), (0,)), ((), ()))
NT = (((1,), (1,)), ((), ()))
TN = (((0,), (0,)), ((), ()))


def split(x):
    high = x.astype(BF16)
    return high, (x - high.astype(F32)).astype(BF16)


def mm(a, b, dims=NN):
    a = a if isinstance(a, tuple) else split(a)
    b = b if isinstance(b, tuple) else split(b)
    dot = functools.partial(lax.dot_general, dimension_numbers=dims, preferred_element_type=F32)
    return dot(a[0], b[0]) + (dot(a[0], b[1]) + dot(a[1], b[0]))


def carry(link_t, cov, base):
    link_t = link_t if isinstance(link_t, tuple) else split(link_t)
    return mm(mm(link_t, cov), link_t, NT) + base


def pack(cov):
    half = cov.shape[0] // 2
    return jnp.concatenate([cov[:half, :half], cov[:half, half:], cov[half:, half:]], 0)


def unpack(packed):
    half = packed.shape[0] // 3
    first, cross, second = packed[:half], packed[half : 2 * half], packed[2 * half :]
    top = jnp.concatenate([first, cross], 1)
    bottom = jnp.concatenate([cross.T, second], 1)
    return jnp.concatenate([top, bottom], 0)


def two_blocks(load, left, right):
    def placed(block, half):
        slab = load(lax.shift_right_logical(block, 1))
        return jnp.where((block & 1) == half, slab, pltpu.roll(slab, BLOCK, 1))

    a, b = placed(left, 0), placed(right, 1)
    lane = lax.broadcasted_iota(jnp.int32, a.shape, 1)
    return jnp.where(lane < BLOCK, a, b)


def tile_of(ref, *lead):
    def load(tile):
        return ref[(*lead, slice(None), pl.ds(pl.multiple_of(tile * LANES, LANES), LANES))]

    return load


def chosen_of(fill_ref, prior_ref, panel):
    slots = fill_ref.shape[1]
    if panel > 0:
        return [fill_ref[panel - 1, j] for j in range(slots)]
    first = lax.axis_index("seg") == 0
    return [jnp.where(first, fill_ref[0, j], prior_ref[0, j]) for j in range(slots)]


def order_of(chosen, blocks):
    slots = len(chosen)
    rest = [jnp.int32(0)] * (blocks - slots)
    place = []
    seen = jnp.int32(0)
    for b in range(blocks):
        hit = jnp.int32(0)
        where = jnp.int32(0)
        for j in range(slots):
            same = (chosen[j] == b).astype(jnp.int32)
            hit = hit + same
            where = where + same * j
        free = 1 - hit
        for q in range(blocks - slots):
            rest[q] = rest[q] + jnp.where(seen == q, free * b, 0)
        place.append(jnp.where(hit > 0, where, slots + seen))
        seen = seen + free
    return rest, place


def vmem(count):
    return [pl.BlockSpec(memory_space=pltpu.VMEM)] * count


def smem(count):
    return [pl.BlockSpec(memory_space=pltpu.SMEM)] * count


def call(kernel, outs, scalars, arrays, scratch=(), flops=0, mib=16, name=None):
    moved = sum(a.size * 4 for a in arrays) + sum(o.size * 4 for o in outs)
    return pl.pallas_call(
        kernel,
        out_shape=outs,
        in_specs=smem(len(scalars)) + vmem(len(arrays)),
        out_specs=vmem(len(outs)),
        scratch_shapes=list(scratch),
        cost_estimate=pl.CostEstimate(flops=flops, bytes_accessed=moved, transcendentals=0),
        compiler_params=pltpu.CompilerParams(vmem_limit_bytes=mib << 20),
        name=name,
    )(*scalars, *arrays)


def shape(*dims):
    return jax.ShapeDtypeStruct(dims, F32)


def local_map_kernel(mask_ref, factor_ref, inv_ref, map_ref):
    panels, rows, _ = factor_ref.shape
    seg_at, seg_count = lax.axis_index("seg"), lax.axis_size("seg")
    slots = rows // BLOCK
    row_at = lax.axis_index("row")
    for p in range(panels):
        alive = (seg_at * panels + p < seg_count * panels - 1).astype(F32)
        kept = []
        for s in range(slots):
            keep = mask_ref[p, row_at * slots + s].astype(F32) * alive
            kept.append(factor_ref[p, s * BLOCK : (s + 1) * BLOCK, :] * keep)
        kept = kept[0] if slots == 1 else jnp.concatenate(kept, 0)
        map_ref[p] = mm(kept, inv_ref[p])


def column_split_kernel(fill_ref, prior_ref, map_ref, link_ref, rest_ref):
    panels = map_ref.shape[0]
    blocks = map_ref.shape[2] // BLOCK
    for p in range(panels):
        chosen = chosen_of(fill_ref, prior_ref, p)
        rest, _ = order_of(chosen, blocks)
        for out_ref, wanted in ((link_ref, chosen), (rest_ref, rest)):
            for t in range(len(wanted) // 2):
                out_ref[p, :, t * LANES : (t + 1) * LANES] = two_blocks(
                    tile_of(map_ref, p), wanted[2 * t], wanted[2 * t + 1]
                )


def prior_kernel(fill_ref, prior_ref, inv_ref, base_ref, own_ref):
    panels = inv_ref.shape[0]
    own_cols = own_ref.shape[1]
    row_at = lax.axis_index("row")
    for p in range(panels):
        chosen = chosen_of(fill_ref, prior_ref, p)
        picked = split(
            jnp.concatenate(
                [
                    two_blocks(tile_of(inv_ref, p), chosen[2 * t], chosen[2 * t + 1])
                    for t in range(len(chosen) // 2)
                ],
                1,
            )
        )
        base_ref[p] = mm(picked, picked, TN)
        own = inv_ref[p, :, pl.ds(pl.multiple_of(row_at * own_cols, own_cols), own_cols)]
        own_ref[p] = mm(own, inv_ref[p], TN)


def segment_kernel(row_count, *refs):
    parts = refs[:row_count]
    base_ref, links_ref, links_t_ref, whole_ref = refs[row_count:]
    panels, rows, _ = parts[0].shape
    size = base_ref.shape[1]
    row_at = lax.axis_index("row")
    for d, part in enumerate(parts):
        at = lax.rem(row_at + (row_count - d), row_count) * rows
        links_ref[:, pl.ds(pl.multiple_of(at, rows), rows), :] = part[...]
    cov = base_ref[panels - 1]
    link_t = links_ref[panels - 1].T
    links_t_ref[panels - 1] = link_t
    for p in range(panels - 2, -1, -1):
        own_t = links_ref[p].T
        links_t_ref[p] = own_t
        own_t = split(own_t)
        cov = carry(own_t, cov, base_ref[p])
        link_t = mm(own_t, link_t)
    whole_ref[:size] = link_t
    whole_ref[size:] = cov


def chip_kernel(own_ref, other_ref, link_t_ref, cov_ref, packed_ref):
    size = cov_ref.shape[0]
    lower = (lax.axis_index("seg") & 1) == 0
    own, other = own_ref[...], other_ref[...]
    down = jnp.where(lower, own, other)
    up = jnp.where(lower, other, own)
    down_t = split(down[:size])
    cov = carry(down_t, up[size:], down[size:])
    link_t_ref[...] = mm(down_t, up[:size])
    cov_ref[...] = cov
    packed_ref[...] = pack(cov)


def extend_kernel(link_t_ref, cov_ref, after_ref, packed_ref):
    packed_ref[...] = pack(carry(link_t_ref[...], unpack(after_ref[...]), cov_ref[...]))


def extend_link_kernel(link_t_ref, after_t_ref, out_ref):
    out_ref[...] = mm(link_t_ref[...], after_t_ref[...])


def join_kernel(level, past_t_ref, past_ref, link_t_ref, cov_ref, out_t_ref, out_ref):
    chip = lax.axis_index("seg") // 2
    below = (lax.shift_right_logical(chip, level) & 1) == 0
    known = (chip & ((1 << level) - 1)) != (1 << level) - 1
    past_t, past = past_t_ref[...], past_ref[...]
    link_t, cov = link_t_ref[...], cov_ref[...]
    past_parts = split(past_t)
    joined = pack(carry(past_parts, unpack(cov), unpack(past)))
    joined_t = mm(past_parts, link_t)
    out_t_ref[...] = jnp.where(below, jnp.where(known, joined_t, link_t), past_t)
    out_ref[...] = jnp.where(below, jnp.where(known, joined, cov), past)


def prepare_kernel(
    has_past, fill_ref, prior_ref, links_ref, links_t_ref, rest_ref, base_ref, own_ref,
    other_ref, *refs
):
    if has_past:
        past_t_ref, past_ref = refs[:2]
        refs = refs[2:]
    left_ref, right_ref, const_ref, scratch = refs
    panels, size, _ = links_ref.shape
    own_cols = own_ref.shape[1]
    width = own_ref.shape[2]
    blocks = width // BLOCK
    row_count = lax.axis_size("row")
    row_at = lax.axis_index("row")
    rows = size // row_count
    seg_at = lax.axis_index("seg")
    chip_last = lax.axis_size("seg") // 2 - 1
    top = 1 << max(chip_last.bit_length() - 1, 0)
    at_row = lax.broadcasted_iota(jnp.int32, (size, size), 0)
    at_col = lax.broadcasted_iota(jnp.int32, (size, size), 1)
    eye = (at_row == at_col).astype(F32)
    if has_past:
        chip = seg_at // 2
        known = (chip & (top - 1)) != top - 1
        to_t = jnp.where(known, past_t_ref[...], eye)
        gain = unpack(past_ref[...])
    else:
        to_t = eye
        gain = jnp.zeros((size, size), F32)
    lower = (seg_at & 1) == 0
    other_t = split(other_ref[:size, :])
    to_t = jnp.where(lower, mm(other_t, to_t), to_t)
    gain = jnp.where(lower, carry(other_t, gain, other_ref[size:, :]), gain)
    for p in range(panels - 1, -1, -1):
        chosen = chosen_of(fill_ref, prior_ref, p)
        _, place = order_of(chosen, blocks)
        scratch[:, :size] = links_ref[p]
        scratch[:, size:] = rest_ref[p]
        whole = jnp.concatenate(
            [
                two_blocks(tile_of(scratch), place[2 * t], place[2 * t + 1])
                for t in range(blocks // 2)
            ],
            1,
        )
        scratch[...] = whole
        own_map = scratch[:, pl.ds(pl.multiple_of(row_at * own_cols, own_cols), own_cols)]
        own_t = split(own_map.T)
        whole = split(whole)
        scratch[:, :size] = to_t
        scratch[:, size:] = gain
        own_rows = pl.ds(pl.multiple_of(row_at * rows, rows), rows)
        to_parts = split(to_t)
        left_ref[p, :rows, :] = scratch[own_rows, :size]
        left_ref[p, rows:, :] = mm(own_t, to_parts)
        right_ref[p] = mm(to_parts, whole, TN)
        gains = jnp.concatenate([scratch[own_rows, size:], mm(own_t, gain)], 0)
        const = mm(gains, whole)
        const_ref[p, :rows, :] = const[:rows]
        const_ref[p, rows:, :] = const[rows:] + own_ref[p]
        if p > 0:
            link_t = split(links_t_ref[p])
            to_t = mm(link_t, to_t)
            gain = carry(link_t, gain, base_ref[p])


def finish_kernel(mask_ref, after_ref, left_ref, right_ref, const_ref, diag_ref, off_ref):
    panels, total, _ = left_ref.shape
    rows = off_ref.shape[1]
    slots = rows // BLOCK
    row_at = lax.axis_index("row")
    after = split(unpack(after_ref[...]))
    for p in range(panels):
        result = mm(mm(left_ref[p], after), right_ref[p]) + const_ref[p]
        diag_ref[p] = result[rows:]
        for s in range(slots):
            keep = mask_ref[p, row_at * slots + s].astype(F32)
            off_ref[p, s * BLOCK : (s + 1) * BLOCK, :] = -result[s * BLOCK : (s + 1) * BLOCK] * keep


def body(fill_blocks, fill_mask, inv_diag, factor_off):
    panels, width, _ = inv_diag.shape
    rows = factor_off.shape[1]
    seg_count = lax.axis_size("seg")
    row_count = lax.axis_size("row")
    size = rows * row_count
    own_cols = width // row_count
    slots = fill_blocks.shape[1]
    chosen_cols = slots * BLOCK
    rest_cols = width - chosen_cols
    chips = seg_count // 2

    prior_fill = lax.ppermute(
        fill_blocks[panels - 1 :], "seg", [(i, i + 1) for i in range(seg_count - 1)]
    )
    (local_map,) = call(
        local_map_kernel,
        [shape(panels, rows, width)],
        [fill_mask],
        [factor_off, inv_diag],
        flops=6 * panels * rows * width * width,
        name="local_map",
    )
    link_own, rest_own = call(
        column_split_kernel,
        [shape(panels, rows, chosen_cols), shape(panels, rows, rest_cols)],
        [fill_blocks, prior_fill],
        [local_map],
        name="column_split",
    )
    parts = [link_own] + [
        lax.ppermute(link_own, "row", [(i, (i + d) % row_count) for i in range(row_count)])
        for d in range(1, row_count)
    ]
    base, own_prior = call(
        prior_kernel,
        [shape(panels, chosen_cols, chosen_cols), shape(panels, own_cols, width)],
        [fill_blocks, prior_fill],
        [inv_diag],
        flops=6 * panels * width * (chosen_cols * chosen_cols + own_cols * width),
        mib=24,
        name="prior",
    )
    links, links_t, own_whole = call(
        functools.partial(segment_kernel, row_count),
        [shape(panels, size, size), shape(panels, size, size), shape(2 * size, size)],
        [],
        parts + [base],
        flops=18 * (panels - 1) * size**3,
        name="segment",
    )
    rest = lax.all_gather(rest_own, "row", axis=1, tiled=True)
    other_whole = lax.ppermute(own_whole, "seg", [(i, i ^ 1) for i in range(seg_count)])
    half = size // 2
    link_t, cov, packed = call(
        chip_kernel,
        [shape(size, size), shape(size, size), shape(3 * half, half)],
        [],
        [own_whole, other_whole],
        flops=18 * size**3,
        name="chip",
    )
    past = None
    send, send_t = packed, link_t
    after = jnp.zeros((3 * half, half), F32)
    levels = (chips - 1).bit_length()
    for level in range(levels):
        bit = 1 << level
        if level > 0:
            (send,) = call(
                extend_kernel, [shape(3 * half, half)], [], [link_t, cov, past[1]],
                flops=12 * size**3, name="extend",
            )
            if level < levels - 1:
                (send_t,) = call(
                    extend_link_kernel, [shape(size, size)], [], [link_t, past[0]],
                    flops=6 * size**3, name="extend_link",
                )
        got = got_t = None
        for step in range(bit):
            route = [
                (2 * (base_chip + bit) + core, 2 * (base_chip + step) + core)
                for base_chip in range(0, chips, 2 * bit)
                for core in range(2)
            ]
            piece = lax.ppermute(send, "seg", route)
            got = piece if got is None else got + piece
            if level < levels - 1:
                piece_t = lax.ppermute(send_t, "seg", route)
                got_t = piece_t if got_t is None else got_t + piece_t
        if level == levels - 1:
            after = got
        elif past is None:
            past = (got_t, got)
        else:
            past = call(
                functools.partial(join_kernel, level),
                [shape(size, size), shape(3 * half, half)],
                [],
                [past[0], past[1], got_t, got],
                flops=18 * size**3,
                name="join",
            )
    total = rows + own_cols
    left, right, const = call(
        functools.partial(prepare_kernel, past is not None),
        [shape(panels, total, size), shape(panels, size, width), shape(panels, total, width)],
        [fill_blocks, prior_fill],
        [links, links_t, rest, base, own_prior, other_whole, *(past or ())],
        scratch=[pltpu.VMEM((size, width), F32)],
        flops=6 * panels * size * (total * size + size * width + total * width + 3 * size * size),
        mib=24,
        name="prepare",
    )
    diag, off = call(
        finish_kernel,
        [shape(panels, own_cols, width), shape(panels, rows, width)],
        [fill_mask],
        [after, left, right, const],
        flops=6 * panels * total * size * (size + width),
        name="finish",
    )
    return diag, off


def solution(mesh):
    placed = (P("seg", None), P("seg", None), P("seg", None, None), P("seg", "row", None))
    return jax.shard_map(
        body,
        mesh=mesh,
        in_specs=placed,
        out_specs=(P("seg", "row", None), P("seg", "row", None)),
        check_vma=False,
    )
```

time: 128 us -> 63.8 us (0.50)
  the two profiles are of different devices: /device:TPU:3 before, /device:TPU:0 now
where the time goes in v1:
time: 63.8 us; the launch traced here: 63.4 us
  waiting for transfers between devices  18.1 us (28%)
  blocking collectives  15.9 us (25%)
  starting transfers between devices  12.6 us (20%)
  Pallas kernels  12.1 us (19%)
  local copies, waits for them, and re-layouts  3.97 us (6%)
  between operations  0.79 us (1%)
    all_gather x1, blocking collectives, body(): rest = lax.all_gather(rest_own, 'row', axis=1, tiled=True)  15.9 us
    pallas_call x8, Pallas kernels, call(): pl.pallas_call(kernel, out_shape=outs, in_specs=smem(len(scalars)) + vmem...  12.1 us
    ppermute x3, waiting for transfers between devices, body(): lax.ppermute(link_own, 'row', [(i, (i + d) % row_count) for i in range(ro...  9.23 us
    ppermute x3, waiting for transfers between devices, body(): piece = lax.ppermute(send, 'seg', route)  7.04 us
    ppermute x3, starting transfers between devices, body(): lax.ppermute(link_own, 'row', [(i, (i + d) % row_count) for i in range(ro...  5.5 us
    ppermute x3, starting transfers between devices, body(): piece = lax.ppermute(send, 'seg', route)  3.26 us
    unnamed x12, local copies, waits for them, and re-layouts  3.23 us
    ppermute x1, starting transfers between devices, body(): lax.ppermute(fill_blocks[panels - 1:], 'seg', [(i, i + 1) for i in range(...  2.34 us
  transfers between devices with their start and end apart: 9, of which 3 were waited for; matrix products, arithmetic and copies ran while one was open for 0% of the time, Pallas kernels for 12%

profile of v1, /device:TPU:0, one launch (start us, length us, event | category | flops | bytes accessed | tf_op | source)
XLA Modules:
  0.0 63.4 jit_solution(14195938824236670813)
XLA Ops:
  0.6 0.0 copy-start.5
  0.6 0.7 %slice.3 = s32[1,4]{1,0:T(1,128)S(1)} slice(s32[2,4]{1,0:T(2,128)} %fill_ref.5), slice={[1:2], [0:4]} | slice | bytes 32 | tf_op jit(solution)/shard_map/slice | solution.py:317
  1.4 2.3 %collective-permute-start = (s32[1,4]{1,0:T(1,128)S(1)}, s32[1,4]{1,0:T(1,128)S(1)}, u32[]{:S(2)}, u32[]{:S(2)}) collective-permute-start(s32[1,4]{1,0:T(1,128)S(1)} %slice.3), channel_id=1, source_target_pairs={{0,4},{4,8},{8,12},{12,16},{16,20},{20,24},{24,28},{1,5},{5,9},{9,... | collective-permute-start | bytes 56 | tf_op jit(solution)/shard_map/ppermute | solution.py:316
  3.7 0.0 copy-start
  3.8 1.6 %copy-done = f32[2,512,512]{2,1,0:T(8,128)S(1)} copy-done((f32[2,512,512]{2,1,0:T(8,128)S(1)}, f32[2,512,512]{2,1,0:T(8,128)}, u32[]{:S(2)}) %copy-start) | copy-done | bytes 2097176
  5.3 0.0 copy-start.2
  5.3 0.9 %copy-done.2 = f32[2,64,512]{2,1,0:T(8,128)S(1)} copy-done((f32[2,64,512]{2,1,0:T(8,128)S(1)}, f32[2,64,512]{2,1,0:T(8,128)}, u32[]{:S(2)}) %copy-start.2) | copy-done | bytes 262168
  6.3 0.0 copy-start.3
  6.3 0.7 %copy-done.3 = s32[2,4]{1,0:T(2,128)S(1)} copy-done((s32[2,4]{1,0:T(2,128)S(1)}, s32[2,4]{1,0:T(2,128)}, u32[]{:S(2)}) %copy-start.3) | copy-done | bytes 56
  7.0 0.0 copy-start.1
  7.0 1.3 %local_map.1.map_ref = f32[2,64,512]{2,1,0:T(8,128)S(1)} custom-call(s32[2,4]{1,0:T(2,128)S(1)} %copy-done.3, f32[2,64,512]{2,1,0:T(8,128)S(1)} %copy-done.2, f32[2,512,512]{2,1,0:T(8,128)S(1)} %copy-done), custom_call_target="tpu_custom_call" | custom-call | flops 201326592 | bytes 2621440 | tf_op jit(solution)/shard_map/local_map/pallas_call | solution.py:104
  8.3 0.0 collective-permute-done.prior_ref
  8.3 0.0 copy-done.5
  8.3 0.8 %column_split.1 = (f32[2,64,256]{2,1,0:T(8,128)S(1)}, f32[2,64,256]{2,1,0:T(8,128)S(1)}) custom-call(s32[2,4]{1,0:T(2,128)S(1)} %copy-done.5, s32[1,4]{1,0:T(1,128)S(1)} %collective-permute-done.prior_ref, f32[2,64,512]{2,1,0:T(8,128)S(1)} %local_map.1.map_ref), custom_call_target="tpu_custom_call" | custom-call | bytes 524288 | tf_op jit(solution)/shard_map/column_split/pallas_call | solution.py:104
  9.1 4.5 %collective-permute-start.3 = (f32[2,64,256]{2,1,0:T(8,128)S(1)}, f32[2,64,256]{2,1,0:T(8,128)S(1)}, u32[]{:S(2)}, u32[]{:S(2)}) collective-permute-start(f32[2,64,256]{2,1,0:T(8,128)S(1)} %get-tuple-element.15.refs_0_), channel_id=1, source_target_pairs={{0,3},{1,0},{2,1},{3,2},{4,7},{5,4},{6,5},{7,6},{8,11},{9,8},{10,9... | collective-permute-start | bytes 393224 | tf_op jit(solution)/shard_map/ppermute | solution.py:335
  13.6 0.0 collective-permute-start.2
  13.6 1.0 %collective-permute-start.1 = (f32[2,64,256]{2,1,0:T(8,128)S(1)}, f32[2,64,256]{2,1,0:T(8,128)S(1)}, u32[]{:S(2)}, u32[]{:S(2)}) collective-permute-start(f32[2,64,256]{2,1,0:T(8,128)S(1)} %get-tuple-element.15.refs_0_), channel_id=1, source_target_pairs={{0,1},{1,2},{2,3},{3,0},{4,5},{5,6},{6,7},{7,4},{8,9},{9,10},{10,1... | collective-permute-start | bytes 393224 | tf_op jit(solution)/shard_map/ppermute | solution.py:335
  14.6 0.0 copy-done.1
  14.6 2.1 %prior.1 = (f32[2,256,256]{2,1,0:T(8,128)S(1)}, f32[2,128,512]{2,1,0:T(8,128)S(1)}) custom-call(s32[2,4]{1,0:T(2,128)S(1)} %copy-done.5, s32[1,4]{1,0:T(1,128)S(1)} %collective-permute-done.prior_ref, f32[2,512,512]{2,1,0:T(8,128)S(1)} %copy-done.1), custom_call_target="tpu_custom_call" | custom-call | flops 805306368 | bytes 3145728 | tf_op jit(solution)/shard_map/prior/pallas_call | solution.py:104
  16.7 0.0 collective-permute-done.3.refs_3_
  16.8 9.2 %collective-permute-done.2.refs_2_ = f32[2,64,256]{2,1,0:T(8,128)S(1)} collective-permute-done((f32[2,64,256]{2,1,0:T(8,128)S(1)}, f32[2,64,256]{2,1,0:T(8,128)S(1)}, u32[]{:S(2)}, u32[]{:S(2)}) %collective-permute-start.2) | collective-permute-done | bytes 131104 | tf_op jit(solution)/shard_map/ppermute | solution.py:335
  26.0 0.0 collective-permute-done.1.refs_1_
  26.0 0.7 %segment.1 = (f32[2,256,256]{2,1,0:T(8,128)S(1)}, f32[2,256,256]{2,1,0:T(8,128)S(1)}, f32[512,256]{1,0:T(8,128)S(1)}) custom-call(f32[2,64,256]{2,1,0:T(8,128)S(1)} %get-tuple-element.15.refs_0_, f32[2,64,256]{2,1,0:T(8,128)S(1)} %collective-permute-done.1.refs_1_, f32[2,64,256]{2,1,0:T(8,128)S(1)} %collective-permute-done.2.refs_2_, ...), custom_call_target="tpu_custom_call" | custom-call | flops 301989888 | bytes 2621440 | tf_op jit(solution)/shard_map/segment/pallas_call | solution.py:104
  26.7 0.2 collective-permute-start.4
  26.9 1.8 %collective-permute-done.4.other_ref = f32[512,256]{1,0:T(8,128)S(1)} collective-permute-done((f32[512,256]{1,0:T(8,128)S(1)}, f32[512,256]{1,0:T(8,128)S(1)}, u32[]{:S(2)}, u32[]{:S(2)}) %collective-permute-start.4) | collective-permute-done | bytes 524320 | tf_op jit(solution)/shard_map/ppermute | solution.py:356
  28.7 0.6 chip.1
  29.3 1.3 %collective-permute-start.5 = (f32[384,128]{1,0:T(8,128)S(1)}, f32[384,128]{1,0:T(8,128)S(1)}, u32[]{:S(2)}, u32[]{:S(2)}) collective-permute-start(f32[384,128]{1,0:T(8,128)S(1)} %get-tuple-element.20), channel_id=1, source_target_pairs={{8,0},{12,4},{24,16},{28,20},{9,1},{13,5},{25,17},{29,21},{10,2},{... | collective-permute-start | bytes 589832 | tf_op jit(solution)/shard_map/ppermute | solution.py:389
  30.6 1.3 %collective-permute-start.8 = (f32[256,256]{1,0:T(8,128)S(1)}, f32[256,256]{1,0:T(8,128)S(1)}, u32[]{:S(2)}, u32[]{:S(2)}) collective-permute-start(f32[256,256]{1,0:T(8,128)S(1)} %get-tuple-element.18.link_t_ref), channel_id=1, source_target_pairs={{8,0},{12,4},{24,16},{28,20},{9,1},{13,5},{25,17},{29,21},{10,2},{... | collective-permute-start | bytes 786440 | tf_op jit(solution)/shard_map/ppermute | solution.py:392
  31.9 7.0 %collective-permute-done.5.after_ref.refs_1_ = f32[384,128]{1,0:T(8,128)S(1)} collective-permute-done((f32[384,128]{1,0:T(8,128)S(1)}, f32[384,128]{1,0:T(8,128)S(1)}, u32[]{:S(2)}, u32[]{:S(2)}) %collective-permute-start.5) | collective-permute-done | bytes 196640 | tf_op jit(solution)/shard_map/ppermute | solution.py:389
  38.9 0.7 %extend.1 = f32[384,128]{1,0:T(8,128)S(1)} custom-call(f32[256,256]{1,0:T(8,128)S(1)} %get-tuple-element.18.link_t_ref, f32[256,256]{1,0:T(8,128)S(1)} %get-tuple-element.19.cov_ref, f32[384,128]{1,0:T(8,128)S(1)} %collective-permute-done.5.after_ref.refs_1_), custom_call_target="tpu_custom_call" | custom-call | flops 201326592 | bytes 917504 | tf_op jit(solution)/shard_map/extend/pallas_call | solution.py:104
  39.6 0.7 %collective-permute-start.7 = (f32[384,128]{1,0:T(8,128)S(1)}, f32[384,128]{1,0:T(8,128)S(1)}, u32[]{:S(2)}, u32[]{:S(2)}) collective-permute-start(f32[384,128]{1,0:T(8,128)S(1)} %extend.1), channel_id=1, source_target_pairs={{16,8},{20,12},{17,9},{21,13},{18,10},{22,14},{19,11},{23,15}} | collective-permute-start | bytes 589832 | tf_op jit(solution)/shard_map/ppermute | solution.py:389
  40.3 1.3 %collective-permute-start.6 = (f32[384,128]{1,0:T(8,128)S(1)}, f32[384,128]{1,0:T(8,128)S(1)}, u32[]{:S(2)}, u32[]{:S(2)}) collective-permute-start(f32[384,128]{1,0:T(8,128)S(1)} %extend.1), channel_id=1, source_target_pairs={{16,0},{20,4},{17,1},{21,5},{18,2},{22,6},{19,3},{23,7}} | collective-permute-start | bytes 589832 | tf_op jit(solution)/shard_map/ppermute | solution.py:389
  41.6 15.9 %all_gather.3.rest_ref = f32[2,256,256]{2,1,0:T(8,128)S(1)} all-gather(f32[2,64,256]{2,1,0:T(8,128)S(1)} %get-tuple-element.23), channel_id=1, replica_groups=mesh['seg'=8,'row'=4] {'row'}, dimensions={1}, use_global_device_ids=true | all-gather | bytes 655360 | tf_op jit(solution)/shard_map/all_gather | solution.py:355
  57.5 0.0 collective-permute-done.8.refs_0_
  57.5 0.0 copy-start.4
  57.5 3.5 %prepare.1 = (f32[2,192,256]{2,1,0:T(8,128)S(1)}, f32[2,256,512]{2,1,0:T(8,128)S(1)}, f32[2,192,512]{2,1,0:T(8,128)S(1)}) custom-call(s32[2,4]{1,0:T(2,128)S(1)} %copy-done.5, s32[1,4]{1,0:T(1,128)S(1)} %collective-permute-done.prior_ref, f32[2,256,256]{2,1,0:T(8,128)S(1)} %get-tuple-element.21.links_ref, f32[2,256,256]{2,1,0:T(8,128)S(1)} %get-tuple-element.22.links_t_ref, ...), custom_call_target="tpu_custom_call" | custom-call | flops 1459617792 | bytes 5832704 | tf_op jit(solution)/shard_map/prepare/pallas_call | solution.py:104
  61.0 0.0 collective-permute-done.7
  61.1 0.0 collective-permute-done.6
  61.1 0.0 copy-done.4
  61.1 2.3 %finish.1 = (f32[2,128,512]{2,1,0:T(8,128)}, f32[2,64,512]{2,1,0:T(8,128)}) custom-call(s32[2,4]{1,0:T(2,128)S(1)} %copy-done.4, f32[384,128]{1,0:T(8,128)S(1)} %add.3.after_ref, f32[2,192,256]{2,1,0:T(8,128)S(1)} %get-tuple-element.25.left_ref, f32[2,256,512]{2,1,0:T(8,128)S(1)} %get-tuple-element.26.right_ref, f32[2,192,512]{2,1,0:T(8,128)S(1)} %get-tuple-element.27.const_ref), custom_call_target="tpu_custom_call" | custom-call | flops 452984832 | bytes 3211264 | tf_op jit(solution)/shard_map/finish/pallas_call | solution.py:104
  (1 shorter events, 0.0 us)
Async XLA Ops:
  0.6 7.6 %copy-start.5 = (s32[2,4]{1,0:T(2,128)S(1)}, s32[2,4]{1,0:T(2,128)}, u32[]{:S(2)}) copy-start(s32[2,4]{1,0:T(2,128)} %fill_ref.5) | copy-start | bytes 100
  1.4 6.9 %collective-permute-start = (s32[1,4]{1,0:T(1,128)S(1)}, s32[1,4]{1,0:T(1,128)S(1)}, u32[]{:S(2)}, u32[]{:S(2)}) collective-permute-start(s32[1,4]{1,0:T(1,128)S(1)} %slice.3), channel_id=1, source_target_pairs={{0,4},{4,8},{8,12},{12,16},{16,20},{20,24},{24,28},{1,5},{5,9},{9,... | collective-permute-start | bytes 56 | tf_op jit(solution)/shard_map/ppermute | solution.py:316
  3.7 1.6 %copy-start = (f32[2,512,512]{2,1,0:T(8,128)S(1)}, f32[2,512,512]{2,1,0:T(8,128)}, u32[]{:S(2)}) copy-start(f32[2,512,512]{2,1,0:T(8,128)} %inv_ref.3) | copy-start | bytes 6291460
  5.3 0.9 %copy-start.2 = (f32[2,64,512]{2,1,0:T(8,128)S(1)}, f32[2,64,512]{2,1,0:T(8,128)}, u32[]{:S(2)}) copy-start(f32[2,64,512]{2,1,0:T(8,128)} %factor_ref.1) | copy-start | bytes 786436
  6.3 0.7 %copy-start.3 = (s32[2,4]{1,0:T(2,128)S(1)}, s32[2,4]{1,0:T(2,128)}, u32[]{:S(2)}) copy-start(s32[2,4]{1,0:T(2,128)} %mask_ref.3) | copy-start | bytes 100
  7.0 7.6 %copy-start.1 = (f32[2,512,512]{2,1,0:T(8,128)S(1)}, f32[2,512,512]{2,1,0:T(8,128)}, u32[]{:S(2)}) copy-start(f32[2,512,512]{2,1,0:T(8,128)} %inv_ref.3) | copy-start | bytes 6291460
  9.1 7.7 %collective-permute-start.3 = (f32[2,64,256]{2,1,0:T(8,128)S(1)}, f32[2,64,256]{2,1,0:T(8,128)S(1)}, u32[]{:S(2)}, u32[]{:S(2)}) collective-permute-start(f32[2,64,256]{2,1,0:T(8,128)S(1)} %get-tuple-element.15.refs_0_), channel_id=1, source_target_pairs={{0,3},{1,0},{2,1},{3,2},{4,7},{5,4},{6,5},{7,6},{8,11},{9,8},{10,9... | collective-permute-start | bytes 393224 | tf_op jit(solution)/shard_map/ppermute | solution.py:335
  13.6 12.4 %collective-permute-start.2 = (f32[2,64,256]{2,1,0:T(8,128)S(1)}, f32[2,64,256]{2,1,0:T(8,128)S(1)}, u32[]{:S(2)}, u32[]{:S(2)}) collective-permute-start(f32[2,64,256]{2,1,0:T(8,128)S(1)} %get-tuple-element.15.refs_0_), channel_id=1, source_target_pairs={{0,2},{1,3},{2,0},{3,1},{4,6},{5,7},{6,4},{7,5},{8,10},{9,11},{10,... | collective-permute-start | bytes 393224 | tf_op jit(solution)/shard_map/ppermute | solution.py:335
  13.6 12.4 %collective-permute-start.1 = (f32[2,64,256]{2,1,0:T(8,128)S(1)}, f32[2,64,256]{2,1,0:T(8,128)S(1)}, u32[]{:S(2)}, u32[]{:S(2)}) collective-permute-start(f32[2,64,256]{2,1,0:T(8,128)S(1)} %get-tuple-element.15.refs_0_), channel_id=1, source_target_pairs={{0,1},{1,2},{2,3},{3,0},{4,5},{5,6},{6,7},{7,4},{8,9},{9,10},{10,1... | collective-permute-start | bytes 393224 | tf_op jit(solution)/shard_map/ppermute | solution.py:335
  26.7 2.0 %collective-permute-start.4 = (f32[512,256]{1,0:T(8,128)S(1)}, f32[512,256]{1,0:T(8,128)S(1)}, u32[]{:S(2)}, u32[]{:S(2)}) collective-permute-start(f32[512,256]{1,0:T(8,128)S(1)} %get-tuple-element.17.own_ref), channel_id=1, source_target_pairs={{0,4},{4,0},{8,12},{12,8},{16,20},{20,16},{24,28},{28,24},{1,5},{5... | collective-permute-start | bytes 1572872 | tf_op jit(solution)/shard_map/ppermute | solution.py:356
  29.3 9.6 %collective-permute-start.5 = (f32[384,128]{1,0:T(8,128)S(1)}, f32[384,128]{1,0:T(8,128)S(1)}, u32[]{:S(2)}, u32[]{:S(2)}) collective-permute-start(f32[384,128]{1,0:T(8,128)S(1)} %get-tuple-element.20), channel_id=1, source_target_pairs={{8,0},{12,4},{24,16},{28,20},{9,1},{13,5},{25,17},{29,21},{10,2},{... | collective-permute-start | bytes 589832 | tf_op jit(solution)/shard_map/ppermute | solution.py:389
  30.6 26.9 %collective-permute-start.8 = (f32[256,256]{1,0:T(8,128)S(1)}, f32[256,256]{1,0:T(8,128)S(1)}, u32[]{:S(2)}, u32[]{:S(2)}) collective-permute-start(f32[256,256]{1,0:T(8,128)S(1)} %get-tuple-element.18.link_t_ref), channel_id=1, source_target_pairs={{8,0},{12,4},{24,16},{28,20},{9,1},{13,5},{25,17},{29,21},{10,2},{... | collective-permute-start | bytes 786440 | tf_op jit(solution)/shard_map/ppermute | solution.py:392
  39.6 21.4 %collective-permute-start.7 = (f32[384,128]{1,0:T(8,128)S(1)}, f32[384,128]{1,0:T(8,128)S(1)}, u32[]{:S(2)}, u32[]{:S(2)}) collective-permute-start(f32[384,128]{1,0:T(8,128)S(1)} %extend.1), channel_id=1, source_target_pairs={{16,8},{20,12},{17,9},{21,13},{18,10},{22,14},{19,11},{23,15}} | collective-permute-start | bytes 589832 | tf_op jit(solution)/shard_map/ppermute | solution.py:389
  40.3 20.8 %collective-permute-start.6 = (f32[384,128]{1,0:T(8,128)S(1)}, f32[384,128]{1,0:T(8,128)S(1)}, u32[]{:S(2)}, u32[]{:S(2)}) collective-permute-start(f32[384,128]{1,0:T(8,128)S(1)} %extend.1), channel_id=1, source_target_pairs={{16,0},{20,4},{17,1},{21,5},{18,2},{22,6},{19,3},{23,7}} | collective-permute-start | bytes 589832 | tf_op jit(solution)/shard_map/ppermute | solution.py:389
  57.5 3.6 %copy-start.4 = (s32[2,4]{1,0:T(2,128)S(1)}, s32[2,4]{1,0:T(2,128)}, u32[]{:S(2)}) copy-start(s32[2,4]{1,0:T(2,128)} %mask_ref.3) | copy-start | bytes 100

commit v2 on v1

--- a/solution.py
+++ b/solution.py
@@ -46,6 +46,24 @@
     return jnp.concatenate([top, bottom], 0)
 
 
+def is_lower():
+    return (lax.axis_index("seg") & 1) == 0
+
+
+def from_halves(own, other):
+    lower = is_lower()
+    return jnp.concatenate([jnp.where(lower, own, other), jnp.where(lower, other, own)], 0)
+
+
+def joined_cores(own, other, halves):
+    return from_halves(own, other) if halves else own + other
+
+
+def own_half(whole):
+    half = whole.shape[0] // 2
+    return jnp.where(is_lower(), whole[:half], whole[half:])
+
+
 def two_blocks(load, left, right):
     def placed(block, half):
         slab = load(lax.shift_right_logical(block, 1))
@@ -68,7 +86,7 @@
     if panel > 0:
         return [fill_ref[panel - 1, j] for j in range(slots)]
     first = lax.axis_index("seg") == 0
-    return [jnp.where(first, fill_ref[0, j], prior_ref[0, j]) for j in range(slots)]
+    return [jnp.where(first, fill_ref[0, j], prior_ref[prior_ref.shape[0] - 1, j]) for j in range(slots)]
 
 
 def order_of(chosen, blocks):
@@ -99,37 +117,74 @@
     return [pl.BlockSpec(memory_space=pltpu.SMEM)] * count
 
 
-def call(kernel, outs, scalars, arrays, scratch=(), flops=0, mib=16, name=None):
-    moved = sum(a.size * 4 for a in arrays) + sum(o.size * 4 for o in outs)
+def call(kernel, outs, scalars, arrays, far=(), through=(), scratch=(), flops=0, mib=16, name=None):
+    moved = sum(a.size * 4 for a in (*arrays, *far)) + sum(o.size * 4 for o in outs)
+    first = len(scalars) + len(arrays) + len(far)
+    count = len(through)
+
+    def inner(*refs):
+        kernel(*refs[:first], *refs[first + count : first + count + len(outs)], *refs[first + 2 * count + len(outs) :])
+
     return pl.pallas_call(
-        kernel,
-        out_shape=outs,
-        in_specs=smem(len(scalars)) + vmem(len(arrays)),
-        out_specs=vmem(len(outs)),
+        inner,
+        out_shape=[*outs, *(jax.ShapeDtypeStruct(a.shape, a.dtype) for a in through)],
+        in_specs=smem(len(scalars))
+        + vmem(len(arrays))
+        + [pl.BlockSpec(memory_space=pltpu.HBM)] * len(far)
+        + [pl.BlockSpec(memory_space=pl.ANY)] * count,
+        out_specs=vmem(len(outs)) + [pl.BlockSpec(memory_space=pl.ANY)] * count,
         scratch_shapes=list(scratch),
+        input_output_aliases={first + i: len(outs) + i for i in range(count)},
         cost_estimate=pl.CostEstimate(flops=flops, bytes_accessed=moved, transcendentals=0),
         compiler_params=pltpu.CompilerParams(vmem_limit_bytes=mib << 20),
         name=name,
-    )(*scalars, *arrays)
+    )(*scalars, *arrays, *(pltpu.with_memory_space_constraint(a, pltpu.HBM) for a in far), *through)
 
 
 def shape(*dims):
     return jax.ShapeDtypeStruct(dims, F32)
 
 
-def local_map_kernel(mask_ref, factor_ref, inv_ref, map_ref):
-    panels, rows, _ = factor_ref.shape
+def local_map_kernel(mask_hbm, factor_hbm, inv_hbm, map_ref, mask_ref, factor_ref, inv_ref, sems):
+    panels, rows, width = factor_ref.shape
+    cut = width // 2
+    first = pltpu.make_async_copy(mask_hbm, mask_ref, sems.at[0, 0])
+    first.start()
+    copies = []
+    for p in range(panels):
+        copies.append(
+            [
+                pltpu.make_async_copy(factor_hbm.at[p], factor_ref.at[p], sems.at[p + 1, 0]),
+                pltpu.make_async_copy(
+                    inv_hbm.at[p, cut:, :], inv_ref.at[p, cut:, :], sems.at[p + 1, 1]
+                ),
+                pltpu.make_async_copy(
+                    inv_hbm.at[p, :cut, :cut], inv_ref.at[p, :cut, :cut], sems.at[p + 1, 2]
+                ),
+            ]
+        )
+    for group in reversed(copies):
+        for copy in group:
+            copy.start()
+    first.wait()
     seg_at, seg_count = lax.axis_index("seg"), lax.axis_size("seg")
     slots = rows // BLOCK
     row_at = lax.axis_index("row")
-    for p in range(panels):
+    for p in range(panels - 1, -1, -1):
+        for copy in copies[p]:
+            copy.wait()
         alive = (seg_at * panels + p < seg_count * panels - 1).astype(F32)
         kept = []
         for s in range(slots):
             keep = mask_ref[p, row_at * slots + s].astype(F32) * alive
             kept.append(factor_ref[p, s * BLOCK : (s + 1) * BLOCK, :] * keep)
         kept = kept[0] if slots == 1 else jnp.concatenate(kept, 0)
-        map_ref[p] = mm(kept, inv_ref[p])
+        left, right = split(kept[:, :cut]), split(kept[:, cut:])
+        lower = split(inv_ref[p, cut:, :])
+        map_ref[p, :, cut:] = mm(right, (lower[0][:, cut:], lower[1][:, cut:]))
+        map_ref[p, :, :cut] = mm(right, (lower[0][:, :cut], lower[1][:, :cut])) + mm(
+            left, inv_ref[p, :cut, :cut]
+        )
 
 
 def column_split_kernel(fill_ref, prior_ref, map_ref, link_ref, rest_ref):
@@ -187,53 +242,63 @@
     whole_ref[size:] = cov
 
 
-def chip_kernel(own_ref, other_ref, link_t_ref, cov_ref, packed_ref):
+def chip_kernel(own_ref, other_ref, link_t_ref, cov_ref, packed_ref, half_t_ref):
     size = cov_ref.shape[0]
-    lower = (lax.axis_index("seg") & 1) == 0
+    lower = is_lower()
     own, other = own_ref[...], other_ref[...]
     down = jnp.where(lower, own, other)
     up = jnp.where(lower, other, own)
     down_t = split(down[:size])
     cov = carry(down_t, up[size:], down[size:])
-    link_t_ref[...] = mm(down_t, up[:size])
+    link_t = mm(down_t, up[:size])
+    link_t_ref[...] = link_t
     cov_ref[...] = cov
-    packed_ref[...] = pack(cov)
-
-
-def extend_kernel(link_t_ref, cov_ref, after_ref, packed_ref):
-    packed_ref[...] = pack(carry(link_t_ref[...], unpack(after_ref[...]), cov_ref[...]))
-
-
-def extend_link_kernel(link_t_ref, after_t_ref, out_ref):
-    out_ref[...] = mm(link_t_ref[...], after_t_ref[...])
-
-
-def join_kernel(level, past_t_ref, past_ref, link_t_ref, cov_ref, out_t_ref, out_ref):
+    packed_ref[...] = own_half(pack(cov))
+    half_t_ref[...] = own_half(link_t)
+
+
+def extend_kernel(link_t_ref, cov_ref, own_ref, other_ref, packed_ref):
+    after = unpack(from_halves(own_ref[...], other_ref[...]))
+    packed_ref[...] = pack(carry(link_t_ref[...], after, cov_ref[...]))
+
+
+def extend_link_kernel(link_t_ref, own_t_ref, other_t_ref, out_ref):
+    out_ref[...] = mm(link_t_ref[...], from_halves(own_t_ref[...], other_t_ref[...]))
+
+
+def join_kernel(level, *refs):
+    past_t, past, link_t, cov = (
+        joined_cores(refs[2 * i][...], refs[2 * i + 1][...], i < 2) for i in range(4)
+    )
     chip = lax.axis_index("seg") // 2
     below = (lax.shift_right_logical(chip, level) & 1) == 0
     known = (chip & ((1 << level) - 1)) != (1 << level) - 1
-    past_t, past = past_t_ref[...], past_ref[...]
-    link_t, cov = link_t_ref[...], cov_ref[...]
     past_parts = split(past_t)
     joined = pack(carry(past_parts, unpack(cov), unpack(past)))
     joined_t = mm(past_parts, link_t)
-    out_t_ref[...] = jnp.where(below, jnp.where(known, joined_t, link_t), past_t)
-    out_ref[...] = jnp.where(below, jnp.where(known, joined, cov), past)
+    out_t = jnp.where(below, jnp.where(known, joined_t, link_t), past_t)
+    out = jnp.where(below, jnp.where(known, joined, cov), past)
+    for ref, whole in zip(refs[8:], (out_t, out_t, out, out)):
+        ref[...] = own_half(whole)
+    for ref, whole in ((refs[9], out_t), (refs[11], out)):
+        half = whole.shape[0] // 2
+        ref[...] = jnp.where(is_lower(), whole[half:], whole[:half])
 
 
 def prepare_kernel(
-    has_past, fill_ref, prior_ref, links_ref, links_t_ref, rest_ref, base_ref, own_ref,
-    other_ref, *refs
+    has_past, row_count, fill_ref, prior_ref, links_ref, links_t_ref, *refs
 ):
+    rest_refs, (base_ref, own_ref, other_ref), refs = (
+        refs[:row_count], refs[row_count : row_count + 3], refs[row_count + 3 :]
+    )
     if has_past:
-        past_t_ref, past_ref = refs[:2]
-        refs = refs[2:]
+        past_refs = refs[:4]
+        refs = refs[4:]
     left_ref, right_ref, const_ref, scratch = refs
     panels, size, _ = links_ref.shape
     own_cols = own_ref.shape[1]
     width = own_ref.shape[2]
     blocks = width // BLOCK
-    row_count = lax.axis_size("row")
     row_at = lax.axis_index("row")
     rows = size // row_count
     seg_at = lax.axis_index("seg")
@@ -245,8 +310,8 @@
     if has_past:
         chip = seg_at // 2
         known = (chip & (top - 1)) != top - 1
-        to_t = jnp.where(known, past_t_ref[...], eye)
-        gain = unpack(past_ref[...])
+        to_t = jnp.where(known, from_halves(past_refs[0][...], past_refs[1][...]), eye)
+        gain = unpack(from_halves(past_refs[2][...], past_refs[3][...]))
     else:
         to_t = eye
         gain = jnp.zeros((size, size), F32)
@@ -258,7 +323,9 @@
         chosen = chosen_of(fill_ref, prior_ref, p)
         _, place = order_of(chosen, blocks)
         scratch[:, :size] = links_ref[p]
-        scratch[:, size:] = rest_ref[p]
+        for d, part in enumerate(rest_refs):
+            at = lax.rem(row_at + (row_count - d), row_count) * rows
+            scratch[pl.ds(pl.multiple_of(at, rows), rows), size:] = part[p]
         whole = jnp.concatenate(
             [
                 two_blocks(tile_of(scratch), place[2 * t], place[2 * t + 1])
@@ -287,12 +354,12 @@
             gain = carry(link_t, gain, base_ref[p])
 
 
-def finish_kernel(mask_ref, after_ref, left_ref, right_ref, const_ref, diag_ref, off_ref):
+def finish_kernel(halves, mask_ref, after_ref, after_other_ref, left_ref, right_ref, const_ref, diag_ref, off_ref):
     panels, total, _ = left_ref.shape
     rows = off_ref.shape[1]
     slots = rows // BLOCK
     row_at = lax.axis_index("row")
-    after = split(unpack(after_ref[...]))
+    after = split(unpack(joined_cores(after_ref[...], after_other_ref[...], halves)))
     for p in range(panels):
         result = mm(mm(left_ref[p], after), right_ref[p]) + const_ref[p]
         diag_ref[p] = result[rows:]
@@ -314,13 +381,20 @@
     chips = seg_count // 2
 
     prior_fill = lax.ppermute(
-        fill_blocks[panels - 1 :], "seg", [(i, i + 1) for i in range(seg_count - 1)]
+        fill_blocks, "seg", [(i, i + 1) for i in range(seg_count - 1)]
     )
     (local_map,) = call(
         local_map_kernel,
         [shape(panels, rows, width)],
-        [fill_mask],
-        [factor_off, inv_diag],
+        [],
+        [],
+        far=[fill_mask, factor_off, inv_diag],
+        scratch=[
+            pltpu.SMEM(fill_mask.shape, jnp.int32),
+            pltpu.VMEM(factor_off.shape, F32),
+            pltpu.VMEM(inv_diag.shape, F32),
+            pltpu.SemaphoreType.DMA((panels + 1, 3)),
+        ],
         flops=6 * panels * rows * width * width,
         name="local_map",
     )
@@ -344,45 +418,51 @@
         mib=24,
         name="prior",
     )
-    links, links_t, own_whole = call(
+    links, links_t, own_whole, rest_own = call(
         functools.partial(segment_kernel, row_count),
         [shape(panels, size, size), shape(panels, size, size), shape(2 * size, size)],
         [],
         parts + [base],
+        through=[rest_own],
         flops=18 * (panels - 1) * size**3,
         name="segment",
     )
-    rest = lax.all_gather(rest_own, "row", axis=1, tiled=True)
-    other_whole = lax.ppermute(own_whole, "seg", [(i, i ^ 1) for i in range(seg_count)])
+    swap = [(i, i ^ 1) for i in range(seg_count)]
+    other_whole = lax.ppermute(own_whole, "seg", swap)
+    rests = [rest_own]
+    for _ in range(1, row_count):
+        ring = [(i, (i + 1) % row_count) for i in range(row_count)]
+        rests.append(lax.ppermute(rests[-1], "row", ring))
     half = size // 2
-    link_t, cov, packed = call(
+    half_packed = shape(3 * half // 2, half)
+    half_link = shape(half, size)
+    link_t, cov, send, send_t = call(
         chip_kernel,
-        [shape(size, size), shape(size, size), shape(3 * half, half)],
+        [shape(size, size), shape(size, size), half_packed, half_link],
         [],
         [own_whole, other_whole],
         flops=18 * size**3,
         name="chip",
     )
     past = None
-    send, send_t = packed, link_t
-    after = jnp.zeros((3 * half, half), F32)
+    after = (jnp.zeros(half_packed.shape, F32),) * 2
     levels = (chips - 1).bit_length()
     for level in range(levels):
         bit = 1 << level
         if level > 0:
             (send,) = call(
-                extend_kernel, [shape(3 * half, half)], [], [link_t, cov, past[1]],
+                extend_kernel, [shape(3 * half, half)], [], [link_t, cov, *past[2:]],
                 flops=12 * size**3, name="extend",
             )
             if level < levels - 1:
                 (send_t,) = call(
-                    extend_link_kernel, [shape(size, size)], [], [link_t, past[0]],
+                    extend_link_kernel, [shape(size, size)], [], [link_t, *past[:2]],
                     flops=6 * size**3, name="extend_link",
                 )
         got = got_t = None
-        for step in range(bit):
+        for step in range(max(bit // 2, 1)):
             route = [
-                (2 * (base_chip + bit) + core, 2 * (base_chip + step) + core)
+                (2 * (base_chip + bit) + core, 2 * (base_chip + min(2 * step + core, bit - 1)) + core)
                 for base_chip in range(0, chips, 2 * bit)
                 for core in range(2)
             ]
@@ -391,35 +471,38 @@
             if level < levels - 1:
                 piece_t = lax.ppermute(send_t, "seg", route)
                 got_t = piece_t if got_t is None else got_t + piece_t
+        got = (got, lax.ppermute(got, "seg", swap))
         if level == levels - 1:
             after = got
-        elif past is None:
-            past = (got_t, got)
+            continue
+        got = (got_t, lax.ppermute(got_t, "seg", swap), *got)
+        if past is None:
+            past = got
         else:
             past = call(
                 functools.partial(join_kernel, level),
-                [shape(size, size), shape(3 * half, half)],
+                [half_link, half_link, half_packed, half_packed],
                 [],
-                [past[0], past[1], got_t, got],
+                [*past, *got],
                 flops=18 * size**3,
                 name="join",
             )
     total = rows + own_cols
     left, right, const = call(
-        functools.partial(prepare_kernel, past is not None),
+        functools.partial(prepare_kernel, past is not None, row_count),
         [shape(panels, total, size), shape(panels, size, width), shape(panels, total, width)],
         [fill_blocks, prior_fill],
-        [links, links_t, rest, base, own_prior, other_whole, *(past or ())],
+        [links, links_t, *rests, base, own_prior, other_whole, *(past or ())],
         scratch=[pltpu.VMEM((size, width), F32)],
         flops=6 * panels * size * (total * size + size * width + total * width + 3 * size * size),
         mib=24,
         name="prepare",
     )
     diag, off = call(
-        finish_kernel,
+        functools.partial(finish_kernel, levels < 2),
         [shape(panels, own_cols, width), shape(panels, rows, width)],
         [fill_mask],
-        [after, left, right, const],
+        [*after, left, right, const],
         flops=6 * panels * total * size * (size + width),
         name="finish",
     )

time: 63.8 us -> 54.9 us (0.86)
  blocking collectives: 15.9 us -> 0 us
  waiting for transfers between devices: 18.1 us -> 27.9 us
  local copies, waits for them, and re-layouts: 3.97 us -> 0.01 us
  Pallas kernels: 12.1 us -> 13.1 us
    all_gather x1 -> x0, blocking collectives: 15.9 us -> none  [body(): rest = lax.all_gather(rest_own, 'row', axis=1, tiled=True)]
    ppermute x2 -> x8, waiting for transfers between devices: 1.8 us -> 11.1 us  [the longest x3 9.25 us: body(): rests.append(lax.ppermute(rests[-1], 'row', ring))]
    unnamed x12 -> x6, local copies, waits for them, and re-layouts: 3.23 us -> 0.01 us
    pallas_call x8, Pallas kernels: 12.1 us -> 13.1 us  [call(): pl.pallas_call(inner, out_shape=[*outs, *(jax.ShapeDtypeStruct(a.shape, a...]
    ppermute x2 -> x8, starting transfers between devices: 2.52 us -> 3.44 us  [the longest x1 2.49 us: body(): lax.ppermute(fill_blocks, 'seg', [(i, i + 1) for i in range(seg_count - 1)])]
    slice x1 -> x0, local copies, waits for them, and re-layouts: 0.75 us -> none  [body(): fill_blocks[panels - 1:]]
    ppermute x3 -> x2, starting transfers between devices: 3.26 us -> 2.58 us  [body(): piece = lax.ppermute(send, 'seg', route)]
    ppermute x3 -> x2, waiting for transfers between devices: 7.04 us -> 7.53 us  [body(): piece = lax.ppermute(send, 'seg', route)]
  transfers between devices with their start and end apart: 9 -> 14, of which waited for: 3 -> 8; matrix products, arithmetic and copies ran while one was open for 0% -> 0% of each run, Pallas kernels for 12% -> 16%
where the time goes in v2:
time: 54.9 us; the launch traced here: 54.6 us
  waiting for transfers between devices  27.9 us (51%)
  Pallas kernels  13.1 us (24%)
  starting transfers between devices  12.8 us (23%)
  between operations  0.79 us (1%)
    pallas_call x8, Pallas kernels, call(): pl.pallas_call(inner, out_shape=[*outs, *(jax.ShapeDtypeStruct(a.shape, a...  13.1 us
    ppermute x3, waiting for transfers between devices, body(): rests.append(lax.ppermute(rests[-1], 'row', ring))  9.25 us
    ppermute x3, waiting for transfers between devices, body(): lax.ppermute(link_own, 'row', [(i, (i + d) % row_count) for i in range(ro...  9.22 us
    ppermute x2, waiting for transfers between devices, body(): piece = lax.ppermute(send, 'seg', route)  7.53 us
    ppermute x3, starting transfers between devices, body(): lax.ppermute(link_own, 'row', [(i, (i + d) % row_count) for i in range(ro...  5.5 us
    ppermute x2, starting transfers between devices, body(): piece = lax.ppermute(send, 'seg', route)  2.58 us
    ppermute x1, starting transfers between devices, body(): lax.ppermute(fill_blocks, 'seg', [(i, i + 1) for i in range(seg_count - 1)])  2.49 us
    ppermute x1, waiting for transfers between devices, body(): other_whole = lax.ppermute(own_whole, 'seg', swap)  1.79 us
  transfers between devices with their start and end apart: 14, of which 8 were waited for; matrix products, arithmetic and copies ran while one was open for 0% of the time, Pallas kernels for 16%

profile of v2, /device:TPU:0, one launch (start us, length us, event | category | flops | bytes accessed | tf_op | source)
XLA Modules:
  0.0 54.6 jit_solution(14873650081779567756)
XLA Ops:
  0.6 0.0 copy-start.2
  0.6 0.0 copy-start
  0.6 2.5 %collective-permute-start = (s32[2,4]{1,0:T(2,128)}, s32[2,4]{1,0:T(2,128)S(1)}, u32[]{:S(2)}, u32[]{:S(2)}) collective-permute-start(s32[2,4]{1,0:T(2,128)} %refs_0_.8), channel_id=1, source_target_pairs={{0,4},{4,8},{8,12},{12,16},{16,20},{20,24},{24,28},{1,5},{5,9},{9,... | collective-permute-start | bytes 104 | tf_op jit(solution)/shard_map/ppermute | solution.py:383
  3.1 2.2 %local_map.1.refs_2_ = f32[2,64,512]{2,1,0:T(8,128)S(1)} custom-call(s32[2,4]{1,0:T(2,128)} %refs_0_.9, f32[2,64,512]{2,1,0:T(8,128)} %refs_1_.1, f32[2,512,512]{2,1,0:T(8,128)} %refs_2_.3), custom_call_target="tpu_custom_call" | custom-call | flops 201326592 | bytes 2621472 | tf_op jit(solution)/shard_map/local_map/pallas_call | solution.py:128
  5.3 0.0 collective-permute-done.refs_1_
  5.4 0.0 copy-done.2
  5.4 0.8 %column_split.1 = (f32[2,64,256]{2,1,0:T(8,128)S(1)}, f32[2,64,256]{2,1,0:T(8,128)S(1)}) custom-call(s32[2,4]{1,0:T(2,128)S(1)} %copy-done.2, s32[2,4]{1,0:T(2,128)S(1)} %collective-permute-done.refs_1_, f32[2,64,512]{2,1,0:T(8,128)S(1)} %local_map.1.refs_2_), custom_call_target="tpu_custom_call" | custom-call | bytes 524288 | tf_op jit(solution)/shard_map/column_split/pallas_call | solution.py:128
  6.2 4.5 %collective-permute-start.3 = (f32[2,64,256]{2,1,0:T(8,128)S(1)}, f32[2,64,256]{2,1,0:T(8,128)S(1)}, u32[]{:S(2)}, u32[]{:S(2)}) collective-permute-start(f32[2,64,256]{2,1,0:T(8,128)S(1)} %get-tuple-element.17.refs_0_), channel_id=1, source_target_pairs={{0,3},{1,0},{2,1},{3,2},{4,7},{5,4},{6,5},{7,6},{8,11},{9,8},{10,9... | collective-permute-start | bytes 393224 | tf_op jit(solution)/shard_map/ppermute | solution.py:409
  10.7 0.0 collective-permute-start.2
  10.7 1.0 %collective-permute-start.1 = (f32[2,64,256]{2,1,0:T(8,128)S(1)}, f32[2,64,256]{2,1,0:T(8,128)S(1)}, u32[]{:S(2)}, u32[]{:S(2)}) collective-permute-start(f32[2,64,256]{2,1,0:T(8,128)S(1)} %get-tuple-element.17.refs_0_), channel_id=1, source_target_pairs={{0,1},{1,2},{2,3},{3,0},{4,5},{5,6},{6,7},{7,4},{8,9},{9,10},{10,1... | collective-permute-start | bytes 393224 | tf_op jit(solution)/shard_map/ppermute | solution.py:409
  11.7 0.0 copy-done
  11.7 2.1 %prior.1 = (f32[2,256,256]{2,1,0:T(8,128)S(1)}, f32[2,128,512]{2,1,0:T(8,128)S(1)}) custom-call(s32[2,4]{1,0:T(2,128)S(1)} %copy-done.2, s32[2,4]{1,0:T(2,128)S(1)} %collective-permute-done.refs_1_, f32[2,512,512]{2,1,0:T(8,128)S(1)} %copy-done), custom_call_target="tpu_custom_call" | custom-call | flops 805306368 | bytes 3145728 | tf_op jit(solution)/shard_map/prior/pallas_call | solution.py:128
  13.8 0.0 collective-permute-done.3.refs_3_
  13.8 9.2 %collective-permute-done.2.refs_2_ = f32[2,64,256]{2,1,0:T(8,128)S(1)} collective-permute-done((f32[2,64,256]{2,1,0:T(8,128)S(1)}, f32[2,64,256]{2,1,0:T(8,128)S(1)}, u32[]{:S(2)}, u32[]{:S(2)}) %collective-permute-start.2) | collective-permute-done | bytes 131104 | tf_op jit(solution)/shard_map/ppermute | solution.py:409
  23.1 0.0 collective-permute-done.1.refs_1_
  23.1 0.7 %segment.1 = (f32[2,256,256]{2,1,0:T(8,128)S(1)}, f32[2,256,256]{2,1,0:T(8,128)S(1)}, f32[512,256]{1,0:T(8,128)S(1)}, f32[2,64,256]{2,1,0:T(8,128)S(1)}) custom-call(f32[2,64,256]{2,1,0:T(8,128)S(1)} %get-tuple-element.17.refs_0_, f32[2,64,256]{2,1,0:T(8,128)S(1)} %collective-permute-done.1.refs_1_, ...), custom_call_target="tpu_custom_call", output_to_operand_aliasing={{3}: (5, {})} | custom-call | flops 301989888 | bytes 2621440 | tf_op jit(solution)/shard_map/segment/pallas_call | solution.py:128
  23.8 0.2 collective-permute-start.4
  24.0 1.8 %collective-permute-done.4.refs_1_.refs_10_ = f32[512,256]{1,0:T(8,128)S(1)} collective-permute-done((f32[512,256]{1,0:T(8,128)S(1)}, f32[512,256]{1,0:T(8,128)S(1)}, u32[]{:S(2)}, u32[]{:S(2)}) %collective-permute-start.4) | collective-permute-done | bytes 524320 | tf_op jit(solution)/shard_map/ppermute | solution.py:431
  25.7 0.6 %chip.1 = (f32[256,256]{1,0:T(8,128)S(1)}, f32[256,256]{1,0:T(8,128)S(1)}, f32[192,128]{1,0:T(8,128)S(1)}, f32[128,256]{1,0:T(8,128)S(1)}) custom-call(f32[512,256]{1,0:T(8,128)S(1)} %get-tuple-element.20.refs_0_, f32[512,256]{1,0:T(8,128)S(1)} %collective-permute-done.4.refs_1_.refs_10_), custom_call_target="tpu_custom_call" | custom-call | flops 301989888 | bytes 1802240 | tf_op jit(solution)/shard_map/chip/pallas_call | solution.py:128
  26.4 1.3 %collective-permute-start.5 = (f32[192,128]{1,0:T(8,128)S(1)}, f32[192,128]{1,0:T(8,128)S(1)}, u32[]{:S(2)}, u32[]{:S(2)}) collective-permute-start(f32[192,128]{1,0:T(8,128)S(1)} %get-tuple-element.23), channel_id=1, source_target_pairs={{8,0},{12,4},{24,16},{28,20},{9,1},{13,5},{25,17},{29,21},{10,2},{... | collective-permute-start | bytes 294920 | tf_op jit(solution)/shard_map/ppermute | solution.py:469
  27.7 0.8 %collective-permute-start.9 = (f32[2,64,256]{2,1,0:T(8,128)S(1)}, f32[2,64,256]{2,1,0:T(8,128)S(1)}, u32[]{:S(2)}, u32[]{:S(2)}) collective-permute-start(f32[2,64,256]{2,1,0:T(8,128)S(1)} %get-tuple-element.26.refs_4_), channel_id=1, source_target_pairs={{0,1},{1,2},{2,3},{3,0},{4,5},{5,6},{6,7},{7,4},{8,9},{9,10},{10,1... | collective-permute-start | bytes 393224 | tf_op jit(solution)/shard_map/ppermute | solution.py:435
  28.4 4.8 %collective-permute-done.5.refs_2_.refs_13_ = f32[192,128]{1,0:T(8,128)S(1)} collective-permute-done((f32[192,128]{1,0:T(8,128)S(1)}, f32[192,128]{1,0:T(8,128)S(1)}, u32[]{:S(2)}, u32[]{:S(2)}) %collective-permute-start.5) | collective-permute-done | bytes 98336 | tf_op jit(solution)/shard_map/ppermute | solution.py:469
  33.3 0.0 collective-permute-start.6
  33.3 1.8 %collective-permute-done.9.refs_5_ = f32[2,64,256]{2,1,0:T(8,128)S(1)} collective-permute-done((f32[2,64,256]{2,1,0:T(8,128)S(1)}, f32[2,64,256]{2,1,0:T(8,128)S(1)}, u32[]{:S(2)}, u32[]{:S(2)}) %collective-permute-start.9) | collective-permute-done | bytes 131104 | tf_op jit(solution)/shard_map/ppermute | solution.py:435
  35.1 0.0 collective-permute-start.10
  35.1 1.3 %collective-permute-start.12 = (f32[128,256]{1,0:T(8,128)S(1)}, f32[128,256]{1,0:T(8,128)S(1)}, u32[]{:S(2)}, u32[]{:S(2)}) collective-permute-start(f32[128,256]{1,0:T(8,128)S(1)} %get-tuple-element.28), channel_id=1, source_target_pairs={{8,0},{12,4},{24,16},{28,20},{9,1},{13,5},{25,17},{29,21},{10,2},{... | collective-permute-start | bytes 393224 | tf_op jit(solution)/shard_map/ppermute | solution.py:472
  36.4 0.0 collective-permute-done.6.refs_3_.refs_14_
  36.4 0.7 %extend.1 = f32[384,128]{1,0:T(8,128)S(1)} custom-call(f32[256,256]{1,0:T(8,128)S(1)} %get-tuple-element.21.refs_0_, f32[256,256]{1,0:T(8,128)S(1)} %get-tuple-element.22.refs_1_, f32[192,128]{1,0:T(8,128)S(1)} %collective-permute-done.5.refs_2_.refs_13_, f32[192,128]{1,0:T(8,128)S(1)} %collective-permute-done.6.refs_3_.refs_14_), custom_call_target="tpu_custom_call" | custom-call | flops 201326592 | bytes 917504 | tf_op jit(solution)/shard_map/extend/pallas_call | solution.py:128
  37.0 1.3 %collective-permute-start.7 = (f32[384,128]{1,0:T(8,128)S(1)}, f32[384,128]{1,0:T(8,128)S(1)}, u32[]{:S(2)}, u32[]{:S(2)}) collective-permute-start(f32[384,128]{1,0:T(8,128)S(1)} %extend.1), channel_id=1, source_target_pairs={{16,0},{20,12},{17,1},{21,13},{18,2},{22,14},{19,3},{23,15}} | collective-permute-start | bytes 589832 | tf_op jit(solution)/shard_map/ppermute | solution.py:469
  38.3 3.5 %collective-permute-done.10.refs_6_ = f32[2,64,256]{2,1,0:T(8,128)S(1)} collective-permute-done((f32[2,64,256]{2,1,0:T(8,128)S(1)}, f32[2,64,256]{2,1,0:T(8,128)S(1)}, u32[]{:S(2)}, u32[]{:S(2)}) %collective-permute-start.10) | collective-permute-done | bytes 131104 | tf_op jit(solution)/shard_map/ppermute | solution.py:435
  41.8 0.0 collective-permute-start.11
  41.8 0.1 collective-permute-done.12.refs_11_
  41.9 0.0 collective-permute-start.13
  41.9 2.7 %collective-permute-done.7.refs_1_ = f32[384,128]{1,0:T(8,128)S(1)} collective-permute-done((f32[384,128]{1,0:T(8,128)S(1)}, f32[384,128]{1,0:T(8,128)S(1)}, u32[]{:S(2)}, u32[]{:S(2)}) %collective-permute-start.7) | collective-permute-done | bytes 196640 | tf_op jit(solution)/shard_map/ppermute | solution.py:469
  44.6 0.0 collective-permute-start.8
  44.6 4.0 %collective-permute-done.11.refs_7_ = f32[2,64,256]{2,1,0:T(8,128)S(1)} collective-permute-done((f32[2,64,256]{2,1,0:T(8,128)S(1)}, f32[2,64,256]{2,1,0:T(8,128)S(1)}, u32[]{:S(2)}, u32[]{:S(2)}) %collective-permute-start.11) | collective-permute-done | bytes 131104 | tf_op jit(solution)/shard_map/ppermute | solution.py:435
  48.6 0.0 collective-permute-done.13.refs_12_
  48.6 0.0 copy-start.1
  48.6 3.6 %prepare.1 = (f32[2,192,256]{2,1,0:T(8,128)S(1)}, f32[2,256,512]{2,1,0:T(8,128)S(1)}, f32[2,192,512]{2,1,0:T(8,128)S(1)}) custom-call(s32[2,4]{1,0:T(2,128)S(1)} %copy-done.2, s32[2,4]{1,0:T(2,128)S(1)} %collective-permute-done.refs_1_, f32[2,256,256]{2,1,0:T(8,128)S(1)} %get-tuple-element.24.refs_2_, f32[2,256,256]{2,1,0:T(8,128)S(1)} %get-tuple-element.25.refs_3_, ...), custom_call_target="tpu_custom_call" | custom-call | flops 1459617792 | bytes 5832704 | tf_op jit(solution)/shard_map/prepare/pallas_call | solution.py:128
  52.2 0.0 collective-permute-done.8.refs_2_
  52.2 0.0 copy-done.1
  52.2 2.3 %finish.1 = (f32[2,128,512]{2,1,0:T(8,128)}, f32[2,64,512]{2,1,0:T(8,128)}) custom-call(s32[2,4]{1,0:T(2,128)S(1)} %copy-done.1, f32[384,128]{1,0:T(8,128)S(1)} %collective-permute-done.7.refs_1_, f32[384,128]{1,0:T(8,128)S(1)} %collective-permute-done.8.refs_2_, f32[2,192,256]{2,1,0:T(8,128)S(1)} %get-tuple-element.29.refs_3_, ...), custom_call_target="tpu_custom_call" | custom-call | flops 452984832 | bytes 3407872 | tf_op jit(solution)/shard_map/finish/pallas_call | solution.py:128
Async XLA Ops:
  0.6 4.7 %copy-start.2 = (s32[2,4]{1,0:T(2,128)S(1)}, s32[2,4]{1,0:T(2,128)}, u32[]{:S(2)}) copy-start(s32[2,4]{1,0:T(2,128)} %refs_0_.8) | copy-start | bytes 100
  0.6 11.0 %copy-start = (f32[2,512,512]{2,1,0:T(8,128)S(1)}, f32[2,512,512]{2,1,0:T(8,128)}, u32[]{:S(2)}) copy-start(f32[2,512,512]{2,1,0:T(8,128)} %refs_2_.3) | copy-start | bytes 6291460
  0.6 4.7 %collective-permute-start = (s32[2,4]{1,0:T(2,128)}, s32[2,4]{1,0:T(2,128)S(1)}, u32[]{:S(2)}, u32[]{:S(2)}) collective-permute-start(s32[2,4]{1,0:T(2,128)} %refs_0_.8), channel_id=1, source_target_pairs={{0,4},{4,8},{8,12},{12,16},{16,20},{20,24},{24,28},{1,5},{5,9},{9,... | collective-permute-start | bytes 104 | tf_op jit(solution)/shard_map/ppermute | solution.py:383
  6.2 7.7 %collective-permute-start.3 = (f32[2,64,256]{2,1,0:T(8,128)S(1)}, f32[2,64,256]{2,1,0:T(8,128)S(1)}, u32[]{:S(2)}, u32[]{:S(2)}) collective-permute-start(f32[2,64,256]{2,1,0:T(8,128)S(1)} %get-tuple-element.17.refs_0_), channel_id=1, source_target_pairs={{0,3},{1,0},{2,1},{3,2},{4,7},{5,4},{6,5},{7,6},{8,11},{9,8},{10,9... | collective-permute-start | bytes 393224 | tf_op jit(solution)/shard_map/ppermute | solution.py:409
  10.7 12.4 %collective-permute-start.2 = (f32[2,64,256]{2,1,0:T(8,128)S(1)}, f32[2,64,256]{2,1,0:T(8,128)S(1)}, u32[]{:S(2)}, u32[]{:S(2)}) collective-permute-start(f32[2,64,256]{2,1,0:T(8,128)S(1)} %get-tuple-element.17.refs_0_), channel_id=1, source_target_pairs={{0,2},{1,3},{2,0},{3,1},{4,6},{5,7},{6,4},{7,5},{8,10},{9,11},{10,... | collective-permute-start | bytes 393224 | tf_op jit(solution)/shard_map/ppermute | solution.py:409
  10.7 12.4 %collective-permute-start.1 = (f32[2,64,256]{2,1,0:T(8,128)S(1)}, f32[2,64,256]{2,1,0:T(8,128)S(1)}, u32[]{:S(2)}, u32[]{:S(2)}) collective-permute-start(f32[2,64,256]{2,1,0:T(8,128)S(1)} %get-tuple-element.17.refs_0_), channel_id=1, source_target_pairs={{0,1},{1,2},{2,3},{3,0},{4,5},{5,6},{6,7},{7,4},{8,9},{9,10},{10,1... | collective-permute-start | bytes 393224 | tf_op jit(solution)/shard_map/ppermute | solution.py:409
  23.8 2.0 %collective-permute-start.4 = (f32[512,256]{1,0:T(8,128)S(1)}, f32[512,256]{1,0:T(8,128)S(1)}, u32[]{:S(2)}, u32[]{:S(2)}) collective-permute-start(f32[512,256]{1,0:T(8,128)S(1)} %get-tuple-element.20.refs_0_), channel_id=1, source_target_pairs={{0,4},{4,0},{8,12},{12,8},{16,20},{20,16},{24,28},{28,24},{1,5},{5... | collective-permute-start | bytes 1572872 | tf_op jit(solution)/shard_map/ppermute | solution.py:431
  26.4 6.9 %collective-permute-start.5 = (f32[192,128]{1,0:T(8,128)S(1)}, f32[192,128]{1,0:T(8,128)S(1)}, u32[]{:S(2)}, u32[]{:S(2)}) collective-permute-start(f32[192,128]{1,0:T(8,128)S(1)} %get-tuple-element.23), channel_id=1, source_target_pairs={{8,0},{12,4},{24,16},{28,20},{9,1},{13,5},{25,17},{29,21},{10,2},{... | collective-permute-start | bytes 294920 | tf_op jit(solution)/shard_map/ppermute | solution.py:469
  27.7 7.4 %collective-permute-start.9 = (f32[2,64,256]{2,1,0:T(8,128)S(1)}, f32[2,64,256]{2,1,0:T(8,128)S(1)}, u32[]{:S(2)}, u32[]{:S(2)}) collective-permute-start(f32[2,64,256]{2,1,0:T(8,128)S(1)} %get-tuple-element.26.refs_4_), channel_id=1, source_target_pairs={{0,1},{1,2},{2,3},{3,0},{4,5},{5,6},{6,7},{7,4},{8,9},{9,10},{10,1... | collective-permute-start | bytes 393224 | tf_op jit(solution)/shard_map/ppermute | solution.py:435
  33.3 3.1 %collective-permute-start.6 = (f32[192,128]{1,0:T(8,128)S(1)}, f32[192,128]{1,0:T(8,128)S(1)}, u32[]{:S(2)}, u32[]{:S(2)}) collective-permute-start(f32[192,128]{1,0:T(8,128)S(1)} %collective-permute-done.5.refs_2_.refs_13_), channel_id=1, source_target_pairs={{0,4},{4,0},{8,12},{12,8},{16,20},{20,16},{24,28},{28,24},{1,5},{5... | collective-permute-start | bytes 294920 | tf_op jit(solution)/shard_map/ppermute | solution.py:474
  35.1 6.8 %collective-permute-start.10 = (f32[2,64,256]{2,1,0:T(8,128)S(1)}, f32[2,64,256]{2,1,0:T(8,128)S(1)}, u32[]{:S(2)}, u32[]{:S(2)}) collective-permute-start(f32[2,64,256]{2,1,0:T(8,128)S(1)} %collective-permute-done.9.refs_5_), channel_id=1, source_target_pairs={{0,1},{1,2},{2,3},{3,0},{4,5},{5,6},{6,7},{7,4},{8,9},{9,10},{10,1... | collective-permute-start | bytes 393224 | tf_op jit(solution)/shard_map/ppermute | solution.py:435
  35.1 6.9 %collective-permute-start.12 = (f32[128,256]{1,0:T(8,128)S(1)}, f32[128,256]{1,0:T(8,128)S(1)}, u32[]{:S(2)}, u32[]{:S(2)}) collective-permute-start(f32[128,256]{1,0:T(8,128)S(1)} %get-tuple-element.28), channel_id=1, source_target_pairs={{8,0},{12,4},{24,16},{28,20},{9,1},{13,5},{25,17},{29,21},{10,2},{... | collective-permute-start | bytes 393224 | tf_op jit(solution)/shard_map/ppermute | solution.py:472
  37.0 7.6 %collective-permute-start.7 = (f32[384,128]{1,0:T(8,128)S(1)}, f32[384,128]{1,0:T(8,128)S(1)}, u32[]{:S(2)}, u32[]{:S(2)}) collective-permute-start(f32[384,128]{1,0:T(8,128)S(1)} %extend.1), channel_id=1, source_target_pairs={{16,0},{20,12},{17,1},{21,13},{18,2},{22,14},{19,3},{23,15}} | collective-permute-start | bytes 589832 | tf_op jit(solution)/shard_map/ppermute | solution.py:469
  41.8 6.8 %collective-permute-start.11 = (f32[2,64,256]{2,1,0:T(8,128)S(1)}, f32[2,64,256]{2,1,0:T(8,128)S(1)}, u32[]{:S(2)}, u32[]{:S(2)}) collective-permute-start(f32[2,64,256]{2,1,0:T(8,128)S(1)} %collective-permute-done.10.refs_6_), channel_id=1, source_target_pairs={{0,1},{1,2},{2,3},{3,0},{4,5},{5,6},{6,7},{7,4},{8,9},{9,10},{10,1... | collective-permute-start | bytes 393224 | tf_op jit(solution)/shard_map/ppermute | solution.py:435
  41.9 6.7 %collective-permute-start.13 = (f32[128,256]{1,0:T(8,128)S(1)}, f32[128,256]{1,0:T(8,128)S(1)}, u32[]{:S(2)}, u32[]{:S(2)}) collective-permute-start(f32[128,256]{1,0:T(8,128)S(1)} %collective-permute-done.12.refs_11_), channel_id=1, source_target_pairs={{0,4},{4,0},{8,12},{12,8},{16,20},{20,16},{24,28},{28,24},{1,5},{5... | collective-permute-start | bytes 393224 | tf_op jit(solution)/shard_map/ppermute | solution.py:478
  44.6 7.6 %collective-permute-start.8 = (f32[384,128]{1,0:T(8,128)S(1)}, f32[384,128]{1,0:T(8,128)S(1)}, u32[]{:S(2)}, u32[]{:S(2)}) collective-permute-start(f32[384,128]{1,0:T(8,128)S(1)} %collective-permute-done.7.refs_1_), channel_id=1, source_target_pairs={{0,4},{4,0},{8,12},{12,8},{16,20},{20,16},{24,28},{28,24},{1,5},{5... | collective-permute-start | bytes 589832 | tf_op jit(solution)/shard_map/ppermute | solution.py:474
  48.6 3.6 %copy-start.1 = (s32[2,4]{1,0:T(2,128)S(1)}, s32[2,4]{1,0:T(2,128)}, u32[]{:S(2)}) copy-start(s32[2,4]{1,0:T(2,128)} %refs_0_.9) | copy-start | bytes 100

commit v3 on v2

v3 whole, which is shorter than its diff:
```python
import functools

import jax
import jax.numpy as jnp
from jax import lax
from jax.experimental import pallas as pl
from jax.experimental.pallas import tpu as pltpu
from jax.sharding import PartitionSpec as P

BLOCK = 64
LANES = 128
F32 = jnp.float32
BF16 = jnp.bfloat16
NN = (((1,), (0,)), ((), ()))
NT = (((1,), (1,)), ((), ()))
TN = (((0,), (0,)), ((), ()))


def split(x):
    high = x.astype(BF16)
    return high, (x - high.astype(F32)).astype(BF16)


def mm(a, b, dims=NN):
    a = a if isinstance(a, tuple) else split(a)
    b = b if isinstance(b, tuple) else split(b)
    dot = functools.partial(lax.dot_general, dimension_numbers=dims, preferred_element_type=F32)
    return dot(a[0], b[0]) + (dot(a[0], b[1]) + dot(a[1], b[0]))


def carry(link_t, cov, base):
    link_t = link_t if isinstance(link_t, tuple) else split(link_t)
    return mm(mm(link_t, cov), link_t, NT) + base


def pack(cov):
    half = cov.shape[0] // 2
    return jnp.concatenate([cov[:half, :half], cov[:half, half:], cov[half:, half:]], 0)


def unpack(packed):
    half = packed.shape[0] // 3
    first, cross, second = packed[:half], packed[half : 2 * half], packed[2 * half :]
    top = jnp.concatenate([first, cross], 1)
    bottom = jnp.concatenate([cross.T, second], 1)
    return jnp.concatenate([top, bottom], 0)


def is_lower():
    return (lax.axis_index("seg") & 1) == 0


def from_halves(own, other):
    lower = is_lower()
    return jnp.concatenate([jnp.where(lower, own, other), jnp.where(lower, other, own)], 0)


def joined_cores(own, other, halves):
    if halves:
        return from_halves(own, other)
    seg_at = lax.axis_index("seg")
    return jnp.where(((seg_at // 2) & 1) == (seg_at & 1), own, other)


def own_half(whole):
    half = whole.shape[0] // 2
    return jnp.where(is_lower(), whole[:half], whole[half:])


def two_blocks(load, left, right):
    def placed(block, half):
        slab = load(lax.shift_right_logical(block, 1))
        return jnp.where((block & 1) == half, slab, pltpu.roll(slab, BLOCK, 1))

    a, b = placed(left, 0), placed(right, 1)
    lane = lax.broadcasted_iota(jnp.int32, a.shape, 1)
    return jnp.where(lane < BLOCK, a, b)


def tile_of(ref, *lead):
    def load(tile):
        return ref[(*lead, slice(None), pl.ds(pl.multiple_of(tile * LANES, LANES), LANES))]

    return load


def chosen_of(fill_ref, prior_ref, panel):
    slots = fill_ref.shape[1]
    if panel > 0:
        return [fill_ref[panel - 1, j] for j in range(slots)]
    first = lax.axis_index("seg") == 0
    return [jnp.where(first, fill_ref[0, j], prior_ref[prior_ref.shape[0] - 1, j]) for j in range(slots)]


def vmem(count):
    return [pl.BlockSpec(memory_space=pltpu.VMEM)] * count


def smem(count):
    return [pl.BlockSpec(memory_space=pltpu.SMEM)] * count


def call(kernel, outs, scalars, arrays, far=(), through=(), scratch=(), flops=0, mib=16, name=None):
    moved = sum(a.size * 4 for a in (*arrays, *far)) + sum(o.size * 4 for o in outs)
    first = len(scalars) + len(arrays) + len(far)
    count = len(through)

    def inner(*refs):
        kernel(*refs[:first], *refs[first + count : first + count + len(outs)], *refs[first + 2 * count + len(outs) :])

    return pl.pallas_call(
        inner,
        out_shape=[*outs, *(jax.ShapeDtypeStruct(a.shape, a.dtype) for a in through)],
        in_specs=smem(len(scalars))
        + vmem(len(arrays))
        + [pl.BlockSpec(memory_space=pltpu.HBM)] * len(far)
        + [pl.BlockSpec(memory_space=pl.ANY)] * count,
        out_specs=vmem(len(outs)) + [pl.BlockSpec(memory_space=pl.ANY)] * count,
        scratch_shapes=list(scratch),
        input_output_aliases={first + i: len(outs) + i for i in range(count)},
        cost_estimate=pl.CostEstimate(flops=flops, bytes_accessed=moved, transcendentals=0),
        compiler_params=pltpu.CompilerParams(vmem_limit_bytes=mib << 20),
        name=name,
    )(*scalars, *arrays, *(pltpu.with_memory_space_constraint(a, pltpu.HBM) for a in far), *through)


def shape(*dims):
    return jax.ShapeDtypeStruct(dims, F32)


def kept_rows(mask_ref, panel, slot, rows):
    alive = lax.axis_index("seg") * mask_ref.shape[0] + panel < (
        lax.axis_size("seg") * mask_ref.shape[0] - 1
    )
    return rows * (mask_ref[panel, slot].astype(F32) * alive.astype(F32))


def triangular_mm(left, lower):
    cut = left.shape[1] // 2
    first, second = split(left[:, :cut]), split(left[:, cut:])
    below = split(lower[cut:, :])
    return jnp.concatenate(
        [
            mm(second, (below[0][:, :cut], below[1][:, :cut])) + mm(first, lower[:cut, :cut]),
            mm(second, (below[0][:, cut:], below[1][:, cut:])),
        ],
        1,
    )


def prior_kernel(
    fill_ref, prior_ref, inv_ref, base_ref, own_ref, pick_high_ref, pick_low_ref, token_ref
):
    panels = inv_ref.shape[0]
    own_cols = own_ref.shape[1]
    row_at = lax.axis_index("row")
    token_ref[...] = jnp.zeros_like(token_ref)
    for p in range(panels):
        chosen = chosen_of(fill_ref, prior_ref, p)
        picked = split(
            jnp.concatenate(
                [
                    two_blocks(tile_of(inv_ref, p), chosen[2 * t], chosen[2 * t + 1])
                    for t in range(len(chosen) // 2)
                ],
                1,
            )
        )
        pick_high_ref[p], pick_low_ref[p] = picked
        base_ref[p] = mm(picked, picked, TN)
        own = inv_ref[p, :, pl.ds(pl.multiple_of(row_at * own_cols, own_cols), own_cols)]
        own_ref[p] = mm(own, inv_ref[p], TN)


def put_rows(mask_ref, panel, distance, part, take):
    row_count = lax.axis_size("row")
    rows = part.shape[1]
    owner = lax.rem(lax.axis_index("row") + (row_count - distance), row_count)
    for s in range(rows // BLOCK):
        slot = owner * (rows // BLOCK) + s
        kept = kept_rows(mask_ref, panel, slot, part[panel, s * BLOCK : (s + 1) * BLOCK, :])
        take(kept, pl.ds(pl.multiple_of(slot * BLOCK, BLOCK), BLOCK))


def links_kernel(distances, mask_ref, *refs):
    parts, (pick_high_ref, pick_low_ref, links_ref) = refs[: len(distances)], refs[len(distances) :]
    for p in range(links_ref.shape[0]):
        pick = (pick_high_ref[p], pick_low_ref[p])

        def take(kept, at):
            links_ref[p, at, :] = mm(kept, pick)

        for d, part in zip(distances, parts):
            put_rows(mask_ref, p, d, part, take)


def segment_kernel(
    distance, mask_ref, part, pick_high_ref, pick_low_ref, early_ref, base_ref,
    links_t_ref, whole_ref, links_ref
):
    panels, size, _ = base_ref.shape
    cov = link_t = None
    for p in range(panels - 1, -1, -1):
        pick = (pick_high_ref[p], pick_low_ref[p])
        links_ref[...] = early_ref[p]

        def take(kept, at):
            links_ref[at, :] = mm(kept, pick)

        put_rows(mask_ref, p, distance, part, take)
        own_t = links_ref[...].T
        links_t_ref[p] = own_t
        if cov is None:
            cov, link_t = base_ref[p], own_t
        else:
            own_t = split(own_t)
            cov = carry(own_t, cov, base_ref[p])
            link_t = mm(own_t, link_t)
    whole_ref[:size] = link_t
    whole_ref[size:] = cov


def maps_kernel(mask_ref, inv_ref, *refs):
    *parts, maps_ref, token_ref, rows_ref = refs
    token_ref[...] = jnp.zeros_like(token_ref)
    for p in range(inv_ref.shape[0]):

        def take(kept, at):
            rows_ref[at, :] = kept

        for d, part in enumerate(parts):
            put_rows(mask_ref, p, d, part, take)
        maps_ref[p] = triangular_mm(rows_ref[...], inv_ref[p])


def chip_kernel(own_ref, other_ref, link_t_ref, cov_ref, packed_ref, half_t_ref):
    size = cov_ref.shape[0]
    lower = is_lower()
    own, other = own_ref[...], other_ref[...]
    down = jnp.where(lower, own, other)
    up = jnp.where(lower, other, own)
    down_t = split(down[:size])
    cov = carry(down_t, up[size:], down[size:])
    link_t = mm(down_t, up[:size])
    link_t_ref[...] = link_t
    cov_ref[...] = cov
    packed_ref[...] = own_half(pack(cov))
    half_t_ref[...] = own_half(link_t)


def extend_kernel(link_t_ref, cov_ref, own_ref, other_ref, packed_ref):
    after = unpack(from_halves(own_ref[...], other_ref[...]))
    packed_ref[...] = pack(carry(link_t_ref[...], after, cov_ref[...]))


def extend_link_kernel(link_t_ref, own_t_ref, other_t_ref, out_ref):
    out_ref[...] = mm(link_t_ref[...], from_halves(own_t_ref[...], other_t_ref[...]))


def join_kernel(level, *refs):
    past_t, past, link_t, cov = (
        joined_cores(refs[2 * i][...], refs[2 * i + 1][...], i < 2) for i in range(4)
    )
    chip = lax.axis_index("seg") // 2
    below = (lax.shift_right_logical(chip, level) & 1) == 0
    known = (chip & ((1 << level) - 1)) != (1 << level) - 1
    past_parts = split(past_t)
    joined = pack(carry(past_parts, unpack(cov), unpack(past)))
    joined_t = mm(past_parts, link_t)
    out_t = jnp.where(below, jnp.where(known, joined_t, link_t), past_t)
    out = jnp.where(below, jnp.where(known, joined, cov), past)
    for ref, whole in zip(refs[8:], (out_t, out_t, out, out)):
        ref[...] = own_half(whole)
    for ref, whole in ((refs[9], out_t), (refs[11], out)):
        half = whole.shape[0] // 2
        ref[...] = jnp.where(is_lower(), whole[half:], whole[:half])


def prepare_kernel(base_ref, own_ref, other_ref, maps_ref, links_t_ref, *refs):
    left_ref, right_ref, const_ref, token_ref, scratch = refs
    token_ref[...] = jnp.zeros_like(token_ref)
    panels, own_cols, _ = own_ref.shape
    size = base_ref.shape[1]
    row_at = lax.axis_index("row")
    rows = left_ref.shape[1] - own_cols
    at_row = lax.broadcasted_iota(jnp.int32, (size, size), 0)
    at_col = lax.broadcasted_iota(jnp.int32, (size, size), 1)
    lower = is_lower()
    to_t = jnp.where(lower, other_ref[:size, :], (at_row == at_col).astype(F32))
    gain = jnp.where(lower, other_ref[size:, :], 0.0)
    own_at = pl.ds(pl.multiple_of(row_at * own_cols, own_cols), own_cols)
    own_rows = pl.ds(pl.multiple_of(row_at * rows, rows), rows)
    for p in range(panels - 1, -1, -1):
        whole = split(maps_ref[p])
        own_t = split(maps_ref[p, :, own_at].T)
        scratch[:, :size] = to_t
        scratch[:, size:] = gain
        to_parts = split(to_t)
        left_ref[p, :rows, :] = scratch[own_rows, :size]
        left_ref[p, rows:, :] = mm(own_t, to_parts)
        right_ref[p] = mm(to_parts, whole, TN)
        gains = jnp.concatenate([scratch[own_rows, size:], mm(own_t, gain)], 0)
        const = mm(gains, whole)
        const_ref[p, :rows, :] = const[:rows]
        const_ref[p, rows:, :] = const[rows:] + own_ref[p]
        if p > 0:
            link_t = split(links_t_ref[p])
            to_t = mm(link_t, to_t)
            gain = carry(link_t, gain, base_ref[p])


def finish_kernel(levels, mask_ref, after_ref, after_other_ref, *refs):
    past_refs, refs = refs[: 4 * (levels > 1)], refs[4 * (levels > 1) :]
    left_ref, right_ref, const_ref, diag_ref, off_ref = refs
    panels = left_ref.shape[0]
    rows = off_ref.shape[1]
    row_at = lax.axis_index("row")
    chip = lax.axis_index("seg") // 2
    top = (1 << levels) // 2
    after = joined_cores(after_ref[...], after_other_ref[...], levels < 2)
    after = unpack(jnp.where((chip & top) == 0, after, 0.0))
    if past_refs:
        past_t = from_halves(past_refs[0][...], past_refs[1][...])
        past = unpack(from_halves(past_refs[2][...], past_refs[3][...]))
        after = jnp.where((chip & (top - 1)) != top - 1, carry(past_t, after, past), after)
    after = split(after)
    for p in range(panels):
        result = mm(mm(left_ref[p], after), right_ref[p]) + const_ref[p]
        diag_ref[p] = result[rows:]
        for s in range(rows // BLOCK):
            keep = mask_ref[p, row_at * (rows // BLOCK) + s].astype(F32)
            off_ref[p, s * BLOCK : (s + 1) * BLOCK, :] = -result[s * BLOCK : (s + 1) * BLOCK] * keep


def body(fill_blocks, fill_mask, inv_diag, factor_off):
    panels, width, _ = inv_diag.shape
    rows = factor_off.shape[1]
    seg_count = lax.axis_size("seg")
    row_count = lax.axis_size("row")
    size = rows * row_count
    own_cols = width // row_count
    slots = fill_blocks.shape[1]
    chosen_cols = slots * BLOCK
    chips = seg_count // 2
    half_cols = size // 2

    def turn(x, axis, distance):
        count = lax.axis_size(axis)
        return lax.ppermute(x, axis, [(i, (i + distance) % count) for i in range(count)])

    ups = [factor_off]
    for _ in range(row_count // 2):
        ups.append(turn(ups[-1], "row", 1))
    prior_fill = turn(fill_blocks, "seg", 1)
    pick = jax.ShapeDtypeStruct((panels, width, chosen_cols), BF16)
    token = shape(1, 1, width)
    base, own_prior, pick_high, pick_low, prior_token = call(
        prior_kernel,
        [shape(panels, chosen_cols, chosen_cols), shape(panels, own_cols, width), pick, pick, token],
        [fill_blocks, prior_fill],
        [inv_diag],
        flops=6 * panels * width * (chosen_cols * chosen_cols + own_cols * width),
        mib=24,
        name="prior",
    )
    downs = [factor_off + prior_token]
    for _ in range((row_count - 1) // 2):
        downs.append(turn(downs[-1], "row", -1))
    parts = ups + downs[:0:-1]
    last = len(ups) - 1
    early = [d for d in range(row_count) if d != last]
    (links,) = call(
        functools.partial(links_kernel, early),
        [shape(panels, size, size)],
        [fill_mask],
        [*(parts[d] for d in early), pick_high, pick_low],
        flops=6 * panels * size * size * width,
        name="links",
    )
    links_t, own_whole = call(
        functools.partial(segment_kernel, last),
        [shape(panels, size, size), shape(2 * size, size)],
        [fill_mask],
        [parts[last], pick_high, pick_low, links, base],
        scratch=[pltpu.VMEM((size, size), F32)],
        flops=6 * panels * rows * size * width + 18 * (panels - 1) * size**3,
        name="segment",
    )
    maps, maps_token = call(
        maps_kernel,
        [shape(panels, size, width), shape(1, half_cols)],
        [fill_mask],
        [inv_diag, *parts],
        scratch=[pltpu.VMEM((size, width), F32)],
        flops=6 * panels * size * width * width,
        mib=24,
        name="maps",
    )
    swap = [(i, i ^ 1) for i in range(seg_count)]
    other_whole = lax.ppermute(own_whole, "seg", swap)
    half = size // 2
    half_packed = shape(3 * half // 2, half)
    half_link = shape(half, size)
    link_t, cov, send, send_t = call(
        chip_kernel,
        [shape(size, size), shape(size, size), half_packed, half_link],
        [],
        [own_whole, other_whole],
        flops=18 * size**3,
        name="chip",
    )
    total = rows + own_cols
    left, right, const, prepare_token = call(
        prepare_kernel,
        [
            shape(panels, total, size),
            shape(panels, size, width),
            shape(panels, total, width),
            shape(1, half_cols),
        ],
        [],
        [base, own_prior, other_whole, maps, links_t],
        scratch=[pltpu.VMEM((size, width), F32)],
        flops=6 * panels * size * (total * size + size * width + total * width + 3 * size * size),
        mib=24,
        name="prepare",
    )
    past = None
    after = (jnp.zeros(half_packed.shape, F32),) * 2
    levels = (chips - 1).bit_length()
    for level in range(levels):
        bit = 1 << level
        if level > 0:
            (send,) = call(
                extend_kernel, [shape(3 * half, half)], [], [link_t, cov, *past[2:]],
                flops=12 * size**3, name="extend",
            )
            if level < levels - 1:
                (send_t,) = call(
                    extend_link_kernel, [shape(size, size)], [], [link_t, *past[:2]],
                    flops=6 * size**3, name="extend_link",
                )
        got = got_t = None
        for step in range(max(bit // 2, 1)):
            route = list(range(seg_count))
            for base_chip in range(0, chips, 2 * bit):
                for core in range(2):
                    upper_at = 2 * (base_chip + bit) + core
                    lower_at = 2 * (base_chip + (2 * step + core) % bit) + core
                    route[upper_at], route[lower_at] = lower_at, upper_at
            route = list(enumerate(route))
            here = ((lax.axis_index("seg") // 2) & (bit - 1)) // 2 == step
            piece = lax.ppermute(send, "seg", route)
            got = piece if step == 0 else jnp.where(here, piece, got)
            if level < levels - 1:
                piece_t = lax.ppermute(send_t, "seg", route)
                got_t = piece_t if step == 0 else jnp.where(here, piece_t, got_t)
        if level == levels - 1:
            got = got + prepare_token
        elif level == 0:
            got = got + maps_token
        got = (got, lax.ppermute(got, "seg", swap))
        if level == levels - 1:
            after = got
            continue
        got = (got_t, lax.ppermute(got_t, "seg", swap), *got)
        if past is None:
            past = got
        else:
            past = call(
                functools.partial(join_kernel, level),
                [half_link, half_link, half_packed, half_packed],
                [],
                [*past, *got],
                flops=18 * size**3,
                name="join",
            )
    diag, off = call(
        functools.partial(finish_kernel, levels),
        [shape(panels, own_cols, width), shape(panels, rows, width)],
        [fill_mask],
        [*after, *(past or ()), left, right, const],
        flops=6 * panels * total * size * (size + width),
        name="finish",
    )
    return diag, off


def solution(mesh):
    placed = (P("seg", None), P("seg", None), P("seg", None, None), P("seg", "row", None))
    return jax.shard_map(
        body,
        mesh=mesh,
        in_specs=placed,
        out_specs=(P("seg", "row", None), P("seg", "row", None)),
        check_vma=False,
    )
```

time: 54.9 us -> 52.2 us (0.951)
  waiting for transfers between devices: 27.9 us -> 25.1 us
  local copies, waits for them, and re-layouts: 0.01 us -> 2.28 us
  starting transfers between devices: 12.8 us -> 10.9 us
    ppermute x7 -> x4, waiting for transfers between devices: 18.5 us -> 14.8 us  [turn(): lax.ppermute(x, axis, [(i, (i + distance) % count) for i in range(count)])]
    ppermute x7 -> x4, starting transfers between devices: 8.74 us -> 5.22 us  [turn(): lax.ppermute(x, axis, [(i, (i + distance) % count) for i in range(count)])]
    ppermute x2, waiting for transfers between devices: 7.53 us -> 4.97 us  [body(): piece = lax.ppermute(send, 'seg', route)]
    ppermute x2, starting transfers between devices: 2.58 us -> 4.98 us  [body(): piece = lax.ppermute(send, 'seg', route)]
    unnamed x6 -> x10, local copies, waits for them, and re-layouts: 0.01 us -> 2.28 us
    ppermute x2, waiting for transfers between devices: 0.01 us -> 1.29 us  [body(): got = (got, lax.ppermute(got, 'seg', swap))]
    ppermute x1, starting transfers between devices: 1.28 us -> 0.07 us  [body(): piece_t = lax.ppermute(send_t, 'seg', route)]
    ppermute x1, waiting for transfers between devices: 0.08 us -> 1.13 us  [body(): piece_t = lax.ppermute(send_t, 'seg', route)]
  transfers between devices with their start and end apart: 14 -> 11, of which waited for: 8 -> 9; matrix products, arithmetic and copies ran while one was open for 0% -> 0% of each run, Pallas kernels for 16% -> 14%
where the time goes in v3:
time: 52.2 us; the launch traced here: 52.1 us
  waiting for transfers between devices  25.1 us (48%)
  Pallas kernels  13 us (25%)
  starting transfers between devices  10.9 us (21%)
  local copies, waits for them, and re-layouts  2.28 us (4%)
  between operations  0.77 us (1%)
    ppermute x4, waiting for transfers between devices, turn(): lax.ppermute(x, axis, [(i, (i + distance) % count) for i in range(count)])  14.8 us
    pallas_call x8, Pallas kernels, call(): pl.pallas_call(inner, out_shape=[*outs, *(jax.ShapeDtypeStruct(a.shape, a...  13 us
    ppermute x4, starting transfers between devices, turn(): lax.ppermute(x, axis, [(i, (i + distance) % count) for i in range(count)])  5.22 us
    ppermute x2, starting transfers between devices, body(): piece = lax.ppermute(send, 'seg', route)  4.98 us
    ppermute x2, waiting for transfers between devices, body(): piece = lax.ppermute(send, 'seg', route)  4.97 us
    unnamed x10, local copies, waits for them, and re-layouts  2.28 us
    ppermute x1, waiting for transfers between devices, body(): other_whole = lax.ppermute(own_whole, 'seg', swap)  1.9 us
    ppermute x2, waiting for transfers between devices, body(): got = (got, lax.ppermute(got, 'seg', swap))  1.29 us
  transfers between devices with their start and end apart: 11, of which 9 were waited for; matrix products, arithmetic and copies ran while one was open for 0% of the time, Pallas kernels for 14%

profile of v3, /device:TPU:0, one launch (start us, length us, event | category | flops | bytes accessed | tf_op | source)
XLA Modules:
  0.0 52.1 jit_solution(18236388037525427862)
XLA Ops:
  0.6 0.0 copy-start
  0.6 3.1 %collective-permute-start = (f32[2,64,512]{2,1,0:T(8,128)}, f32[2,64,512]{2,1,0:T(8,128)S(1)}, u32[]{:S(2)}, u32[]{:S(2)}) collective-permute-start(f32[2,64,512]{2,1,0:T(8,128)} %refs_2_.3), channel_id=1, source_target_pairs={{0,1},{1,2},{2,3},{3,0},{4,5},{5,6},{6,7},{7,4},{8,9},{9,10},{10,1... | collective-permute-start | bytes 786440 | tf_op jit(solution)/shard_map/ppermute | solution.py:349
  3.7 0.0 collective-permute-start.2
  3.7 4.1 %collective-permute-done.2.refs_1_ = s32[2,4]{1,0:T(2,128)S(1)} collective-permute-done((s32[2,4]{1,0:T(2,128)}, s32[2,4]{1,0:T(2,128)S(1)}, u32[]{:S(2)}, u32[]{:S(2)}) %collective-permute-start.2) | collective-permute-done | bytes 64 | tf_op jit(solution)/shard_map/ppermute | solution.py:349
  7.8 0.0 copy-start.1
  7.8 1.6 %copy-done.1 = f32[2,512,512]{2,1,0:T(8,128)S(1)} copy-done((f32[2,512,512]{2,1,0:T(8,128)S(1)}, f32[2,512,512]{2,1,0:T(8,128)}, u32[]{:S(2)}) %copy-start.1) | copy-done | bytes 2097176
  9.4 0.0 copy-start.4
  9.4 0.7 %copy-done.4 = s32[2,4]{1,0:T(2,128)S(1)} copy-done((s32[2,4]{1,0:T(2,128)S(1)}, s32[2,4]{1,0:T(2,128)}, u32[]{:S(2)}) %copy-start.4) | copy-done | bytes 56
  10.1 0.0 copy-start.3
  10.1 2.2 %prior.1 = (f32[2,256,256]{2,1,0:T(8,128)S(1)}, f32[2,128,512]{2,1,0:T(8,128)S(1)}, bf16[2,512,256]{2,1,0:T(8,128)(2,1)S(1)}, bf16[2,512,256]{2,1,0:T(8,128)(2,1)S(1)}, f32[1,1,512]{2,1,0:T(1,128)S(1)}) custom-call(s32[2,4]{1,0:T(2,128)S(1)} %copy-done.4, s32[2,4]{1,0:T(2,128)S(1)} %collective-permute-done.2.refs_1_, f32[2,512,512]{2,1,0:T(8,128)S(1)} %copy-done.1), custom_call_target="tpu_custom_call" | custom-call | flops 805306368 | bytes 5244928 | tf_op jit(solution)/shard_map/prior/pallas_call | solution.py:111
  12.3 0.0 copy-done
  12.3 2.1 %collective-permute-start.3 = (f32[2,64,512]{2,1,0:T(8,128)S(1)}, f32[2,64,512]{2,1,0:T(8,128)S(1)}, u32[]{:S(2)}, u32[]{:S(2)}) collective-permute-start(f32[2,64,512]{2,1,0:T(8,128)S(1)} %broadcast_add_fusion), channel_id=1, source_target_pairs={{0,3},{1,0},{2,1},{3,2},{4,7},{5,4},{6,5},{7,6},{8,11},{9,8},{10,9... | collective-permute-start | bytes 786440 | tf_op jit(solution)/shard_map/ppermute | solution.py:349
  14.5 0.0 collective-permute-done.refs_2_.refs_3_
  14.5 0.0 collective-permute-start.1
  14.5 6.8 %collective-permute-done.3.refs_3_.refs_5_ = f32[2,64,512]{2,1,0:T(8,128)S(1)} collective-permute-done((f32[2,64,512]{2,1,0:T(8,128)S(1)}, f32[2,64,512]{2,1,0:T(8,128)S(1)}, u32[]{:S(2)}, u32[]{:S(2)}) %collective-permute-start.3) | collective-permute-done | bytes 262176 | tf_op jit(solution)/shard_map/ppermute | solution.py:349
  21.2 0.0 copy-done.3
  21.2 1.5 %links.1.refs_4_ = f32[2,256,256]{2,1,0:T(8,128)S(1)} custom-call(s32[2,4]{1,0:T(2,128)S(1)} %copy-done.3, f32[2,64,512]{2,1,0:T(8,128)S(1)} %copy-done, f32[2,64,512]{2,1,0:T(8,128)S(1)} %collective-permute-done.refs_2_.refs_3_, f32[2,64,512]{2,1,0:T(8,128)S(1)} %collective-permute-done.3.refs_3_.refs_5_, ...), custom_call_target="tpu_custom_call" | custom-call | flops 402653184 | bytes 3407872 | tf_op jit(solution)/shard_map/links/pallas_call | solution.py:111
  22.7 0.0 copy-start.2
  22.7 3.9 %collective-permute-done.1.refs_1_.refs_4_ = f32[2,64,512]{2,1,0:T(8,128)S(1)} collective-permute-done((f32[2,64,512]{2,1,0:T(8,128)S(1)}, f32[2,64,512]{2,1,0:T(8,128)S(1)}, u32[]{:S(2)}, u32[]{:S(2)}) %collective-permute-start.1) | collective-permute-done | bytes 262176 | tf_op jit(solution)/shard_map/ppermute | solution.py:349
  26.7 1.6 %segment.1 = (f32[2,256,256]{2,1,0:T(8,128)S(1)}, f32[512,256]{1,0:T(8,128)S(1)}) custom-call(s32[2,4]{1,0:T(2,128)S(1)} %copy-done.3, f32[2,64,512]{2,1,0:T(8,128)S(1)} %collective-permute-done.1.refs_1_.refs_4_, bf16[2,512,256]{2,1,0:T(8,128)(2,1)S(1)} %get-tuple-element.19.refs_4_.refs_2_, bf16[2,512,256]{2,1,0:T(8,128)(2,1)S(1)} %get-tuple-element.20.refs_5_.refs_3_, ...), custom_call_target="tpu_custom_call" | custom-call | flops 402653184 | bytes 4456448 | tf_op jit(solution)/shard_map/segment/pallas_call | solution.py:111
  28.3 0.1 collective-permute-start.4
  28.3 1.9 %collective-permute-done.4.refs_1_.refs_2_ = f32[512,256]{1,0:T(8,128)S(1)} collective-permute-done((f32[512,256]{1,0:T(8,128)S(1)}, f32[512,256]{1,0:T(8,128)S(1)}, u32[]{:S(2)}, u32[]{:S(2)}) %collective-permute-start.4) | collective-permute-done | bytes 524320 | tf_op jit(solution)/shard_map/ppermute | solution.py:400
  30.2 0.6 %chip.1 = (f32[256,256]{1,0:T(8,128)S(1)}, f32[256,256]{1,0:T(8,128)S(1)}, f32[192,128]{1,0:T(8,128)S(1)}, f32[128,256]{1,0:T(8,128)S(1)}) custom-call(f32[512,256]{1,0:T(8,128)S(1)} %get-tuple-element.23.refs_0_, f32[512,256]{1,0:T(8,128)S(1)} %collective-permute-done.4.refs_1_.refs_2_), custom_call_target="tpu_custom_call" | custom-call | flops 301989888 | bytes 1802240 | tf_op jit(solution)/shard_map/chip/pallas_call | solution.py:111
  30.9 1.6 %collective-permute-start.5 = (f32[192,128]{1,0:T(8,128)S(1)}, f32[192,128]{1,0:T(8,128)S(1)}, u32[]{:S(2)}, u32[]{:S(2)}) collective-permute-start(f32[192,128]{1,0:T(8,128)S(1)} %get-tuple-element.26), channel_id=1, source_target_pairs={{0,8},{4,12},{8,0},{12,4},{16,24},{20,28},{24,16},{28,20},{1,9},{5... | collective-permute-start | bytes 294920 | tf_op jit(solution)/shard_map/ppermute | solution.py:453
  32.4 0.0 copy-done.2
  32.4 1.5 %maps.1 = (f32[2,256,512]{2,1,0:T(8,128)S(1)}, f32[1,128]{1,0:T(1,128)S(1)}) custom-call(s32[2,4]{1,0:T(2,128)S(1)} %copy-done.3, f32[2,512,512]{2,1,0:T(8,128)S(1)} %copy-done.2, f32[2,64,512]{2,1,0:T(8,128)S(1)} %copy-done, f32[2,64,512]{2,1,0:T(8,128)S(1)} %collective-permute-done.refs_2_.refs_3_, ...), custom_call_target="tpu_custom_call" | custom-call | flops 805306368 | bytes 4194816 | tf_op jit(solution)/shard_map/maps/pallas_call | solution.py:111
  33.9 1.8 %collective-permute-done.5 = f32[192,128]{1,0:T(8,128)S(1)} collective-permute-done((f32[192,128]{1,0:T(8,128)S(1)}, f32[192,128]{1,0:T(8,128)S(1)}, u32[]{:S(2)}, u32[]{:S(2)}) %collective-permute-start.5) | collective-permute-done | bytes 98336 | tf_op jit(solution)/shard_map/ppermute | solution.py:453
  35.8 0.1 collective-permute-start.6
  35.8 1.3 %collective-permute-done.6.refs_3_.refs_6_ = f32[192,128]{1,0:T(8,128)S(1)} collective-permute-done((f32[192,128]{1,0:T(8,128)S(1)}, f32[192,128]{1,0:T(8,128)S(1)}, u32[]{:S(2)}, u32[]{:S(2)}) %collective-permute-start.6) | collective-permute-done | bytes 98336 | tf_op jit(solution)/shard_map/ppermute | solution.py:462
  37.1 0.7 %extend.1 = f32[384,128]{1,0:T(8,128)S(1)} custom-call(f32[256,256]{1,0:T(8,128)S(1)} %get-tuple-element.24.refs_0_, f32[256,256]{1,0:T(8,128)S(1)} %get-tuple-element.25.refs_1_, f32[192,128]{1,0:T(8,128)S(1)} %broadcast_add_fusion.2.refs_2_.refs_5_, f32[192,128]{1,0:T(8,128)S(1)} %collective-permute-done.6.refs_3_.refs_6_), custom_call_target="tpu_custom_call" | custom-call | flops 201326592 | bytes 917504 | tf_op jit(solution)/shard_map/extend/pallas_call | solution.py:111
  37.8 3.4 %collective-permute-start.7 = (f32[384,128]{1,0:T(8,128)S(1)}, f32[384,128]{1,0:T(8,128)S(1)}, u32[]{:S(2)}, u32[]{:S(2)}) collective-permute-start(f32[384,128]{1,0:T(8,128)S(1)} %extend.1), channel_id=1, source_target_pairs={{0,16},{4,4},{8,8},{12,20},{16,0},{20,12},{24,24},{28,28},{1,17},{... | collective-permute-start | bytes 589832 | tf_op jit(solution)/shard_map/ppermute | solution.py:453
  41.2 0.1 collective-permute-start.9
  41.3 2.0 %prepare.1 = (f32[2,192,256]{2,1,0:T(8,128)S(1)}, f32[2,256,512]{2,1,0:T(8,128)S(1)}, f32[2,192,512]{2,1,0:T(8,128)S(1)}, f32[1,128]{1,0:T(1,128)S(1)}) custom-call(f32[2,256,256]{2,1,0:T(8,128)S(1)} %get-tuple-element.22.refs_5_.refs_0_, f32[2,128,512]{2,1,0:T(8,128)S(1)} %get-tuple-element.28.refs_1_, ...), custom_call_target="tpu_custom_call" | custom-call | flops 1459617792 | bytes 5374464 | tf_op jit(solution)/shard_map/prepare/pallas_call | solution.py:111
  43.4 3.2 %collective-permute-done.7 = f32[384,128]{1,0:T(8,128)S(1)} collective-permute-done((f32[384,128]{1,0:T(8,128)S(1)}, f32[384,128]{1,0:T(8,128)S(1)}, u32[]{:S(2)}, u32[]{:S(2)}) %collective-permute-start.7) | collective-permute-done | bytes 196640 | tf_op jit(solution)/shard_map/ppermute | solution.py:453
  46.5 0.1 collective-permute-start.8
  46.6 1.1 %collective-permute-done.9.refs_3_ = f32[128,256]{1,0:T(8,128)S(1)} collective-permute-done((f32[128,256]{1,0:T(8,128)S(1)}, f32[128,256]{1,0:T(8,128)S(1)}, u32[]{:S(2)}, u32[]{:S(2)}) %collective-permute-start.9) | collective-permute-done | bytes 131104 | tf_op jit(solution)/shard_map/ppermute | solution.py:456
  47.7 0.4 collective-permute-start.10
  48.2 1.0 %collective-permute-done.10.refs_4_ = f32[128,256]{1,0:T(8,128)S(1)} collective-permute-done((f32[128,256]{1,0:T(8,128)S(1)}, f32[128,256]{1,0:T(8,128)S(1)}, u32[]{:S(2)}, u32[]{:S(2)}) %collective-permute-start.10) | collective-permute-done | bytes 131104 | tf_op jit(solution)/shard_map/ppermute | solution.py:466
  49.2 0.0 collective-permute-done.8.refs_2_
  49.2 2.9 %finish.1 = (f32[2,128,512]{2,1,0:T(8,128)}, f32[2,64,512]{2,1,0:T(8,128)}) custom-call(s32[2,4]{1,0:T(2,128)S(1)} %copy-done.3, f32[384,128]{1,0:T(8,128)S(1)} %broadcast_add_fusion.1.refs_1_, f32[384,128]{1,0:T(8,128)S(1)} %collective-permute-done.8.refs_2_, f32[128,256]{1,0:T(8,128)S(1)} %collective-permute-done.9.refs_3_, ...), custom_call_target="tpu_custom_call" | custom-call | flops 452984832 | bytes 3866624 | tf_op jit(solution)/shard_map/finish/pallas_call | solution.py:111
  (3 shorter events, 0.0 us)
Async XLA Ops:
  0.6 11.7 %copy-start = (f32[2,64,512]{2,1,0:T(8,128)S(1)}, f32[2,64,512]{2,1,0:T(8,128)}, u32[]{:S(2)}) copy-start(f32[2,64,512]{2,1,0:T(8,128)} %refs_2_.3) | copy-start | bytes 786436
  0.6 13.8 %collective-permute-start = (f32[2,64,512]{2,1,0:T(8,128)}, f32[2,64,512]{2,1,0:T(8,128)S(1)}, u32[]{:S(2)}, u32[]{:S(2)}) collective-permute-start(f32[2,64,512]{2,1,0:T(8,128)} %refs_2_.3), channel_id=1, source_target_pairs={{0,1},{1,2},{2,3},{3,0},{4,5},{5,6},{6,7},{7,4},{8,9},{9,10},{10,1... | collective-permute-start | bytes 786440 | tf_op jit(solution)/shard_map/ppermute | solution.py:349
  3.7 4.1 %collective-permute-start.2 = (s32[2,4]{1,0:T(2,128)}, s32[2,4]{1,0:T(2,128)S(1)}, u32[]{:S(2)}, u32[]{:S(2)}) collective-permute-start(s32[2,4]{1,0:T(2,128)} %refs_0_.5), channel_id=1, source_target_pairs={{0,4},{4,8},{8,12},{12,16},{16,20},{20,24},{24,28},{28,0},{1,5},{5... | collective-permute-start | bytes 104 | tf_op jit(solution)/shard_map/ppermute | solution.py:349
  7.8 1.6 %copy-start.1 = (f32[2,512,512]{2,1,0:T(8,128)S(1)}, f32[2,512,512]{2,1,0:T(8,128)}, u32[]{:S(2)}) copy-start(f32[2,512,512]{2,1,0:T(8,128)} %refs_1_.3) | copy-start | bytes 6291460
  9.4 0.7 %copy-start.4 = (s32[2,4]{1,0:T(2,128)S(1)}, s32[2,4]{1,0:T(2,128)}, u32[]{:S(2)}) copy-start(s32[2,4]{1,0:T(2,128)} %refs_0_.5) | copy-start | bytes 100
  10.1 11.1 %copy-start.3 = (s32[2,4]{1,0:T(2,128)S(1)}, s32[2,4]{1,0:T(2,128)}, u32[]{:S(2)}) copy-start(s32[2,4]{1,0:T(2,128)} %refs_0_.9) | copy-start | bytes 100
  12.3 8.9 %collective-permute-start.3 = (f32[2,64,512]{2,1,0:T(8,128)S(1)}, f32[2,64,512]{2,1,0:T(8,128)S(1)}, u32[]{:S(2)}, u32[]{:S(2)}) collective-permute-start(f32[2,64,512]{2,1,0:T(8,128)S(1)} %broadcast_add_fusion), channel_id=1, source_target_pairs={{0,3},{1,0},{2,1},{3,2},{4,7},{5,4},{6,5},{7,6},{8,11},{9,8},{10,9... | collective-permute-start | bytes 786440 | tf_op jit(solution)/shard_map/ppermute | solution.py:349
  14.5 12.2 %collective-permute-start.1 = (f32[2,64,512]{2,1,0:T(8,128)S(1)}, f32[2,64,512]{2,1,0:T(8,128)S(1)}, u32[]{:S(2)}, u32[]{:S(2)}) collective-permute-start(f32[2,64,512]{2,1,0:T(8,128)S(1)} %collective-permute-done.refs_2_.refs_3_), channel_id=1, source_target_pairs={{0,1},{1,2},{2,3},{3,0},{4,5},{5,6},{6,7},{7,4},{8,9},{9,10},{10,1... | collective-permute-start | bytes 786440 | tf_op jit(solution)/shard_map/ppermute | solution.py:349
  22.7 9.7 %copy-start.2 = (f32[2,512,512]{2,1,0:T(8,128)S(1)}, f32[2,512,512]{2,1,0:T(8,128)}, u32[]{:S(2)}) copy-start(f32[2,512,512]{2,1,0:T(8,128)} %refs_1_.3) | copy-start | bytes 6291460
  28.3 2.0 %collective-permute-start.4 = (f32[512,256]{1,0:T(8,128)S(1)}, f32[512,256]{1,0:T(8,128)S(1)}, u32[]{:S(2)}, u32[]{:S(2)}) collective-permute-start(f32[512,256]{1,0:T(8,128)S(1)} %get-tuple-element.23.refs_0_), channel_id=1, source_target_pairs={{0,4},{4,0},{8,12},{12,8},{16,20},{20,16},{24,28},{28,24},{1,5},{5... | collective-permute-start | bytes 1572872 | tf_op jit(solution)/shard_map/ppermute | solution.py:400
  30.9 4.9 %collective-permute-start.5 = (f32[192,128]{1,0:T(8,128)S(1)}, f32[192,128]{1,0:T(8,128)S(1)}, u32[]{:S(2)}, u32[]{:S(2)}) collective-permute-start(f32[192,128]{1,0:T(8,128)S(1)} %get-tuple-element.26), channel_id=1, source_target_pairs={{0,8},{4,12},{8,0},{12,4},{16,24},{20,28},{24,16},{28,20},{1,9},{5... | collective-permute-start | bytes 294920 | tf_op jit(solution)/shard_map/ppermute | solution.py:453
  35.8 1.4 %collective-permute-start.6 = (f32[192,128]{1,0:T(8,128)S(1)}, f32[192,128]{1,0:T(8,128)S(1)}, u32[]{:S(2)}, u32[]{:S(2)}) collective-permute-start(f32[192,128]{1,0:T(8,128)S(1)} %broadcast_add_fusion.2.refs_2_.refs_5_), channel_id=1, source_target_pairs={{0,4},{4,0},{8,12},{12,8},{16,20},{20,16},{24,28},{28,24},{1,5},{5... | collective-permute-start | bytes 294920 | tf_op jit(solution)/shard_map/ppermute | solution.py:462
  37.8 8.7 %collective-permute-start.7 = (f32[384,128]{1,0:T(8,128)S(1)}, f32[384,128]{1,0:T(8,128)S(1)}, u32[]{:S(2)}, u32[]{:S(2)}) collective-permute-start(f32[384,128]{1,0:T(8,128)S(1)} %extend.1), channel_id=1, source_target_pairs={{0,16},{4,4},{8,8},{12,20},{16,0},{20,12},{24,24},{28,28},{1,17},{... | collective-permute-start | bytes 589832 | tf_op jit(solution)/shard_map/ppermute | solution.py:453
  41.2 6.5 %collective-permute-start.9 = (f32[128,256]{1,0:T(8,128)S(1)}, f32[128,256]{1,0:T(8,128)S(1)}, u32[]{:S(2)}, u32[]{:S(2)}) collective-permute-start(f32[128,256]{1,0:T(8,128)S(1)} %get-tuple-element.32), channel_id=1, source_target_pairs={{0,8},{4,12},{8,0},{12,4},{16,24},{20,28},{24,16},{28,20},{1,9},{5... | collective-permute-start | bytes 393224 | tf_op jit(solution)/shard_map/ppermute | solution.py:456
  46.5 2.6 %collective-permute-start.8 = (f32[384,128]{1,0:T(8,128)S(1)}, f32[384,128]{1,0:T(8,128)S(1)}, u32[]{:S(2)}, u32[]{:S(2)}) collective-permute-start(f32[384,128]{1,0:T(8,128)S(1)} %broadcast_add_fusion.1.refs_1_), channel_id=1, source_target_pairs={{0,4},{4,0},{8,12},{12,8},{16,20},{20,16},{24,28},{28,24},{1,5},{5... | collective-permute-start | bytes 589832 | tf_op jit(solution)/shard_map/ppermute | solution.py:462
  47.7 1.4 %collective-permute-start.10 = (f32[128,256]{1,0:T(8,128)S(1)}, f32[128,256]{1,0:T(8,128)S(1)}, u32[]{:S(2)}, u32[]{:S(2)}) collective-permute-start(f32[128,256]{1,0:T(8,128)S(1)} %collective-permute-done.9.refs_3_), channel_id=1, source_target_pairs={{0,4},{4,0},{8,12},{12,8},{16,20},{20,16},{24,28},{28,24},{1,5},{5... | collective-permute-start | bytes 393224 | tf_op jit(solution)/shard_map/ppermute | solution.py:466

commit v4 on v3

v4 whole, which is shorter than its diff:
```python
import functools

import jax
import jax.numpy as jnp
from jax import lax
from jax.experimental import pallas as pl
from jax.experimental.pallas import tpu as pltpu
from jax.sharding import PartitionSpec as P

BLOCK = 64
LANES = 128
F32 = jnp.float32
BF16 = jnp.bfloat16
NN = (((1,), (0,)), ((), ()))
NT = (((1,), (1,)), ((), ()))
TN = (((0,), (0,)), ((), ()))


def split(x):
    high = x.astype(BF16)
    return high, (x - high.astype(F32)).astype(BF16)


def mm(a, b, dims=NN):
    a = a if isinstance(a, tuple) else split(a)
    b = b if isinstance(b, tuple) else split(b)
    dot = functools.partial(lax.dot_general, dimension_numbers=dims, preferred_element_type=F32)
    return dot(a[0], b[0]) + (dot(a[0], b[1]) + dot(a[1], b[0]))


def carry(link_t, cov, base):
    link_t = link_t if isinstance(link_t, tuple) else split(link_t)
    return mm(mm(link_t, cov), link_t, NT) + base


def pack(cov):
    half = cov.shape[0] // 2
    return jnp.concatenate([cov[:half, :half], cov[:half, half:], cov[half:, half:]], 0)


def unpack(packed):
    half = packed.shape[0] // 3
    first, cross, second = packed[:half], packed[half : 2 * half], packed[2 * half :]
    top = jnp.concatenate([first, cross], 1)
    bottom = jnp.concatenate([cross.T, second], 1)
    return jnp.concatenate([top, bottom], 0)


def is_lower():
    return (lax.axis_index("seg") & 1) == 0


def from_halves(own, other):
    lower = is_lower()
    return jnp.concatenate([jnp.where(lower, own, other), jnp.where(lower, other, own)], 0)


def own_half(whole):
    half = whole.shape[0] // 2
    return jnp.where(is_lower(), whole[:half], whole[half:])


def two_blocks(load, left, right):
    def placed(block, half):
        slab = load(lax.shift_right_logical(block, 1))
        return jnp.where((block & 1) == half, slab, pltpu.roll(slab, BLOCK, 1))

    a, b = placed(left, 0), placed(right, 1)
    lane = lax.broadcasted_iota(jnp.int32, a.shape, 1)
    return jnp.where(lane < BLOCK, a, b)


def tile_of(ref, *lead):
    def load(tile):
        return ref[(*lead, slice(None), pl.ds(pl.multiple_of(tile * LANES, LANES), LANES))]

    return load


def chosen_of(panel, fill_ref, prior_ref=None):
    slots = fill_ref.shape[1]
    if panel > 0:
        return [fill_ref[panel - 1, j] for j in range(slots)]
    first = lax.axis_index("seg") == 0
    last = prior_ref.shape[0] - 1
    return [jnp.where(first, fill_ref[0, j], prior_ref[last, j]) for j in range(slots)]


def vmem(count):
    return [pl.BlockSpec(memory_space=pltpu.VMEM)] * count


def smem(count):
    return [pl.BlockSpec(memory_space=pltpu.SMEM)] * count


def call(kernel, outs, scalars, arrays, far=(), through=(), scratch=(), flops=0, mib=16, name=None):
    moved = sum(a.size * 4 for a in (*arrays, *far)) + sum(o.size * 4 for o in outs)
    first = len(scalars) + len(arrays) + len(far)
    count = len(through)

    def inner(*refs):
        kernel(*refs[:first], *refs[first + count : first + count + len(outs)], *refs[first + 2 * count + len(outs) :])

    return pl.pallas_call(
        inner,
        out_shape=[*outs, *(jax.ShapeDtypeStruct(a.shape, a.dtype) for a in through)],
        in_specs=smem(len(scalars))
        + vmem(len(arrays))
        + [pl.BlockSpec(memory_space=pltpu.HBM)] * len(far)
        + [pl.BlockSpec(memory_space=pl.ANY)] * count,
        out_specs=vmem(len(outs)) + [pl.BlockSpec(memory_space=pl.ANY)] * count,
        scratch_shapes=list(scratch),
        input_output_aliases={first + i: len(outs) + i for i in range(count)},
        cost_estimate=pl.CostEstimate(flops=flops, bytes_accessed=moved, transcendentals=0),
        compiler_params=pltpu.CompilerParams(vmem_limit_bytes=mib << 20),
        name=name,
    )(*scalars, *arrays, *(pltpu.with_memory_space_constraint(a, pltpu.HBM) for a in far), *through)


def shape(*dims):
    return jax.ShapeDtypeStruct(dims, F32)


def kept_rows(mask_ref, panel, slot, rows):
    alive = lax.axis_index("seg") * mask_ref.shape[0] + panel < (
        lax.axis_size("seg") * mask_ref.shape[0] - 1
    )
    return rows * (mask_ref[panel, slot].astype(F32) * alive.astype(F32))


def triangular_mm(left, lower):
    cut = left.shape[1] // 2
    first, second = split(left[:, :cut]), split(left[:, cut:])
    below = split(lower[cut:, :])
    return jnp.concatenate(
        [
            mm(second, (below[0][:, :cut], below[1][:, :cut])) + mm(first, lower[:cut, :cut]),
            mm(second, (below[0][:, cut:], below[1][:, cut:])),
        ],
        1,
    )


def prior_kernel(panel, *refs):
    *scalar_refs, inv_hbm, base_ref, own_ref, pick_high_ref, pick_low_ref = refs[:-2]
    inv_ref, sem = refs[-2:]
    copy = pltpu.make_async_copy(inv_hbm.at[panel], inv_ref, sem)
    copy.start()
    chosen = chosen_of(panel, *scalar_refs)
    own_cols = own_ref.shape[0]
    own_at = pl.ds(pl.multiple_of(lax.axis_index("row") * own_cols, own_cols), own_cols)
    copy.wait()
    picked_t = split(
        jnp.concatenate(
            [
                two_blocks(tile_of(inv_ref), chosen[2 * t], chosen[2 * t + 1]).T
                for t in range(len(chosen) // 2)
            ],
            0,
        )
    )
    pick_high_ref[...], pick_low_ref[...] = picked_t
    base_ref[...] = mm(picked_t, picked_t, NT)
    own_ref[...] = mm(inv_ref[:, own_at].T, inv_ref[...])


def put_rows(mask_ref, panel, distance, part, take):
    row_count = lax.axis_size("row")
    rows = part.shape[1]
    owner = lax.rem(lax.axis_index("row") + (row_count - distance), row_count)
    for s in range(rows // BLOCK):
        slot = owner * (rows // BLOCK) + s
        kept = kept_rows(mask_ref, panel, slot, part[panel, s * BLOCK : (s + 1) * BLOCK, :])
        take(kept, pl.ds(pl.multiple_of(slot * BLOCK, BLOCK), BLOCK))


def links_kernel(distances, missing, mask_ref, *refs):
    parts, refs = refs[: len(distances)], refs[len(distances) :]
    *pick_refs, links_t_ref, rows_ref = refs
    for p in range(links_t_ref.shape[0]):

        def take(kept, at):
            rows_ref[at, :] = kept

        for d, part in zip(distances, parts):
            put_rows(mask_ref, p, d, part, take)
        put_rows(mask_ref, p, missing, parts[0], lambda kept, at: take(jnp.zeros_like(kept), at))
        pick = (pick_refs[2 * p][...], pick_refs[2 * p + 1][...])
        links_t_ref[p] = mm(pick, rows_ref[...], NT)


def segment_kernel(distance, panels, mask_ref, part, early_ref, *refs):
    pick_refs, base_refs = refs[: 2 * panels], refs[2 * panels : 3 * panels]
    links_t_ref, whole_ref = refs[3 * panels :]
    size = links_t_ref.shape[1]
    lane = lax.broadcasted_iota(jnp.int32, (size, size), 1) // BLOCK
    cov = link_t = None
    for p in range(panels - 1, -1, -1):
        pick = (pick_refs[2 * p][...], pick_refs[2 * p + 1][...])
        pieces = [early_ref[p]]

        def take(kept, at):
            late = mm(pick, jnp.concatenate([kept] * (size // BLOCK), 0), NT)
            pieces.append(jnp.where(lane == at.start // BLOCK, late, pieces[-1]))

        put_rows(mask_ref, p, distance, part, take)
        own_t = pieces[-1]
        links_t_ref[p] = own_t
        if cov is None:
            cov, link_t = base_refs[p][...], own_t
        else:
            own_t = split(own_t)
            cov = carry(own_t, cov, base_refs[p][...])
            link_t = mm(own_t, link_t)
    whole_ref[:size] = link_t
    whole_ref[size:] = cov


def maps_kernel(mask_ref, inv_ref, *refs):
    *parts, maps_ref, token_ref, rows_ref = refs
    token_ref[...] = jnp.zeros_like(token_ref)
    for p in range(inv_ref.shape[0]):

        def take(kept, at):
            rows_ref[at, :] = kept

        for d, part in enumerate(parts):
            put_rows(mask_ref, p, d, part, take)
        maps_ref[p] = triangular_mm(rows_ref[...], inv_ref[p])


def chip_kernel(own_ref, other_ref, link_t_ref, cov_ref, packed_ref, half_t_ref):
    size = cov_ref.shape[0]
    lower = is_lower()
    own, other = own_ref[...], other_ref[...]
    down = jnp.where(lower, own, other)
    up = jnp.where(lower, other, own)
    down_t = split(down[:size])
    cov = carry(down_t, up[size:], down[size:])
    link_t = mm(down_t, up[:size])
    link_t_ref[...] = link_t
    cov_ref[...] = cov
    packed_ref[...] = own_half(pack(cov))
    half_t_ref[...] = own_half(link_t)


def merge_kernel(level, link_t_ref, cov_ref, *refs):
    got_t = from_halves(refs[0][...], refs[1][...])
    got = unpack(from_halves(refs[2][...], refs[3][...]))
    own_t, own = link_t_ref[...], cov_ref[...]
    lower = (lax.shift_right_logical(lax.axis_index("seg") // 2, level) & 1) == 0
    down_t = split(jnp.where(lower, own_t, got_t))
    cov = carry(down_t, jnp.where(lower, got, own), jnp.where(lower, own, got))
    refs[4][...] = own_half(pack(cov))
    if len(refs) > 5:
        link_t = mm(down_t, jnp.where(lower, got_t, own_t))
        refs[5][...] = own_half(link_t)
        refs[6][...] = link_t
        refs[7][...] = cov


def join_kernel(level, *refs):
    past_t, past, link_t, cov = (
        from_halves(refs[2 * i][...], refs[2 * i + 1][...]) for i in range(4)
    )
    chip = lax.axis_index("seg") // 2
    below = (lax.shift_right_logical(chip, level) & 1) == 0
    known = (chip & ((1 << level) - 1)) != (1 << level) - 1
    past_parts = split(past_t)
    joined = pack(carry(past_parts, unpack(cov), unpack(past)))
    joined_t = mm(past_parts, link_t)
    out_t = jnp.where(below, jnp.where(known, joined_t, link_t), past_t)
    out = jnp.where(below, jnp.where(known, joined, cov), past)
    for i, whole in enumerate((out_t, out)):
        half = whole.shape[0] // 2
        refs[8 + 2 * i][...] = own_half(whole)
        refs[9 + 2 * i][...] = jnp.where(is_lower(), whole[half:], whole[:half])


def prepare_kernel(levels, panels, *refs):
    base_refs, own_refs, refs = refs[:panels], refs[panels : 2 * panels], refs[2 * panels :]
    (other_ref, maps_ref, links_t_ref), refs = refs[:3], refs[3:]
    past_refs, refs = refs[: 4 * (levels > 1)], refs[4 * (levels > 1) :]
    left_high, left_low, right_high, right_low, const_ref, token_ref, scratch = refs
    token_ref[...] = jnp.zeros_like(token_ref)
    own_cols = own_refs[0].shape[0]
    size = base_refs[0].shape[0]
    row_at = lax.axis_index("row")
    rows = left_high.shape[1] - own_cols
    at_row = lax.broadcasted_iota(jnp.int32, (size, size), 0)
    at_col = lax.broadcasted_iota(jnp.int32, (size, size), 1)
    eye = (at_row == at_col).astype(F32)
    lower = is_lower()
    if past_refs:
        chip = lax.axis_index("seg") // 2
        low = (1 << (levels - 1)) - 1
        known = (chip & low) != low
        past_t = from_halves(past_refs[0][...], past_refs[1][...])
        past = unpack(from_halves(past_refs[2][...], past_refs[3][...]))
        to_t = jnp.where(known, past_t, eye)
        gain = jnp.where(known, past, 0.0)
        other_t = split(other_ref[:size, :])
        to_t = jnp.where(lower, mm(other_t, to_t), to_t)
        gain = jnp.where(lower, carry(other_t, gain, other_ref[size:, :]), gain)
    else:
        to_t = jnp.where(lower, other_ref[:size, :], eye)
        gain = jnp.where(lower, other_ref[size:, :], 0.0)
    own_at = pl.ds(pl.multiple_of(row_at * own_cols, own_cols), own_cols)
    own_rows = pl.ds(pl.multiple_of(row_at * rows, rows), rows)
    for p in range(panels - 1, -1, -1):
        whole = split(maps_ref[p])
        own_t = split(maps_ref[p, :, own_at].T)
        scratch[:, :size] = to_t
        scratch[:, size:] = gain
        to_parts = split(to_t)
        left = jnp.concatenate([scratch[own_rows, :size], mm(own_t, to_parts)], 0)
        left_high[p], left_low[p] = split(left)
        right_high[p], right_low[p] = split(mm(to_parts, whole, TN))
        gains = jnp.concatenate([scratch[own_rows, size:], mm(own_t, gain)], 0)
        const = mm(gains, whole)
        const_ref[p, :rows, :] = const[:rows]
        const_ref[p, rows:, :] = const[rows:] + own_refs[p][...]
        if p > 0:
            link_t = split(links_t_ref[p])
            to_t = mm(link_t, to_t)
            gain = carry(link_t, gain, base_refs[p][...])


def finish_kernel(levels, mask_ref, after_ref, after_other_ref, *refs):
    left_high, left_low, right_high, right_low, const_ref, diag_ref, off_ref = refs
    rows = off_ref.shape[1]
    row_at = lax.axis_index("row")
    chip = lax.axis_index("seg") // 2
    after = from_halves(after_ref[...], after_other_ref[...])
    after = split(unpack(jnp.where((chip & ((1 << levels) // 2)) == 0, after, 0.0)))
    for p in range(const_ref.shape[0]):
        left = (left_high[p], left_low[p])
        right = (right_high[p], right_low[p])
        result = mm(mm(left, after), right) + const_ref[p]
        diag_ref[p] = result[rows:]
        for s in range(rows // BLOCK):
            keep = mask_ref[p, row_at * (rows // BLOCK) + s].astype(F32)
            off_ref[p, s * BLOCK : (s + 1) * BLOCK, :] = -result[s * BLOCK : (s + 1) * BLOCK] * keep


def body(fill_blocks, fill_mask, inv_diag, factor_off):
    panels, width, _ = inv_diag.shape
    rows = factor_off.shape[1]
    seg_count = lax.axis_size("seg")
    row_count = lax.axis_size("row")
    size = rows * row_count
    own_cols = width // row_count
    slots = fill_blocks.shape[1]
    chosen_cols = slots * BLOCK
    chips = seg_count // 2
    half_cols = size // 2

    def turn(x, axis, distance):
        count = lax.axis_size(axis)
        return lax.ppermute(x, axis, [(i, (i + distance) % count) for i in range(count)])

    ups = [factor_off]
    for _ in range(row_count // 2):
        ups.append(turn(ups[-1], "row", 1))
    prior_fill = turn(fill_blocks, "seg", 1)
    pick = jax.ShapeDtypeStruct((chosen_cols, width), BF16)
    bases, priors, picks = [], [], []
    for p in range(panels):
        base, own_prior, *high_low = call(
            functools.partial(prior_kernel, p),
            [shape(chosen_cols, chosen_cols), shape(own_cols, width), pick, pick],
            [fill_blocks] if p else [fill_blocks, prior_fill],
            [],
            far=[inv_diag],
            scratch=[pltpu.VMEM((width, width), F32), pltpu.SemaphoreType.DMA],
            flops=6 * width * (chosen_cols * chosen_cols + own_cols * width),
            name="prior",
        )
        bases.append(base)
        priors.append(own_prior)
        picks += high_low
    downs = [factor_off + jnp.minimum(prior_fill[-1:, -1:], 0).astype(F32)]
    for _ in range((row_count - 1) // 2):
        downs.append(turn(downs[-1], "row", -1))
    parts = ups + downs[:0:-1]
    last = len(ups) - 1
    early = [d for d in range(row_count) if d != last]
    (links,) = call(
        functools.partial(links_kernel, early, last),
        [shape(panels, size, size)],
        [fill_mask],
        [*(parts[d] for d in early), *picks],
        scratch=[pltpu.VMEM((size, width), F32)],
        flops=6 * panels * size * size * width,
        name="links",
    )
    links_t, own_whole = call(
        functools.partial(segment_kernel, last, panels),
        [shape(panels, size, size), shape(2 * size, size)],
        [fill_mask],
        [parts[last], links, *picks, *bases],
        flops=6 * panels * size * size * width + 18 * (panels - 1) * size**3,
        name="segment",
    )
    maps, maps_token = call(
        maps_kernel,
        [shape(panels, size, width), shape(1, half_cols)],
        [fill_mask],
        [inv_diag, *parts],
        scratch=[pltpu.VMEM((size, width), F32)],
        flops=6 * panels * size * width * width,
        mib=24,
        name="maps",
    )
    swap = [(i, i ^ 1) for i in range(seg_count)]
    other_whole = lax.ppermute(own_whole, "seg", swap)
    half = size // 2
    half_packed = shape(3 * half // 2, half)
    half_link = shape(half, size)
    link_t, cov, send, send_t = call(
        chip_kernel,
        [shape(size, size), shape(size, size), half_packed, half_link],
        [],
        [own_whole, other_whole],
        flops=18 * size**3,
        name="chip",
    )
    past = None
    after = (jnp.zeros(half_packed.shape, F32),) * 2
    levels = (chips - 1).bit_length()
    prepared = None

    def prepare():
        total = rows + own_cols
        left = jax.ShapeDtypeStruct((panels, total, size), BF16)
        right = jax.ShapeDtypeStruct((panels, size, width), BF16)
        return call(
            functools.partial(prepare_kernel, levels, panels),
            [left, left, right, right, shape(panels, total, width), shape(1, half_cols)],
            [],
            [*bases, *priors, other_whole, maps, links_t, *(past or ())],
            scratch=[pltpu.VMEM((size, width), F32)],
            flops=6 * panels * size * (total * size + size * width + total * width + 3 * size * size),
            mib=24,
            name="prepare",
        )

    for level in range(levels):
        partner = [(i, i ^ (2 << level)) for i in range(seg_count)]
        got = lax.ppermute(send, "seg", partner)
        if level == levels - 1:
            *prepared, token = prepare()
            got = got + token
            after = (got, lax.ppermute(got, "seg", swap))
            break
        got_t = lax.ppermute(send_t, "seg", partner)
        if level == 0:
            got = got + maps_token
        got = (got_t, lax.ppermute(got_t, "seg", swap), got, lax.ppermute(got, "seg", swap))
        outs = [half_packed]
        if level < levels - 2:
            outs += [half_link, shape(size, size), shape(size, size)]
        send, *more = call(
            functools.partial(merge_kernel, level), outs, [], [link_t, cov, *got],
            flops=18 * size**3, name="merge",
        )
        if more:
            send_t, link_t, cov = more
        if past is None:
            past = got
        else:
            past = call(
                functools.partial(join_kernel, level),
                [half_link, half_link, half_packed, half_packed],
                [],
                [*past, *got],
                flops=18 * size**3,
                name="join",
            )
    if prepared is None:
        *prepared, _ = prepare()
    diag, off = call(
        functools.partial(finish_kernel, levels),
        [shape(panels, own_cols, width), shape(panels, rows, width)],
        [fill_mask],
        [*after, *prepared],
        flops=6 * panels * (rows + own_cols) * size * (size + width),
        name="finish",
    )
    return diag, off


def solution(mesh):
    placed = (P("seg", None), P("seg", None), P("seg", None, None), P("seg", "row", None))
    return jax.shard_map(
        body,
        mesh=mesh,
        in_specs=placed,
        out_specs=(P("seg", "row", None), P("seg", "row", None)),
        check_vma=False,
    )
```

time: 52.2 us -> 47.5 us (0.910)
  waiting for transfers between devices: 25.1 us -> 17.8 us
  Pallas kernels: 13 us -> 16.6 us
  starting transfers between devices: 10.9 us -> 9.12 us
  local copies, waits for them, and re-layouts: 2.28 us -> 1.28 us
  other arithmetic: 0.05 us -> 0.99 us
  between operations: 0.77 us -> 1.41 us
    ppermute x4, waiting for transfers between devices: 14.8 us -> 8.48 us  [turn(): lax.ppermute(x, axis, [(i, (i + distance) % count) for i in range(count)])]
    pallas_call x8 -> x9, Pallas kernels: 13 us -> 16.6 us  [call(): pl.pallas_call(inner, out_shape=[*outs, *(jax.ShapeDtypeStruct(a.shape, a...]
    ppermute x6, starting transfers between devices: 5.64 us -> 3.82 us  [the longest x2 2.13 us: body(): got = lax.ppermute(send, 'seg', partner)]
    unnamed x10 -> x8, local copies, waits for them, and re-layouts: 2.28 us -> 0.7 us
    add x2, other arithmetic: 0.04 us -> 0.98 us  [the longest x1 0.97 us: body(): downs = [factor_off + jnp.minimum(prior_fill[-1:, -1:], 0).astype(F32)]]
    ppermute x6, waiting for transfers between devices: 8.38 us -> 7.45 us  [the longest x1 2.78 us: body(): got_t = lax.ppermute(send_t, 'seg', partner)]
    slice x0 -> x1, local copies, waits for them, and re-layouts: none -> 0.58 us  [body(): downs = [factor_off + jnp.minimum(prior_fill[-1:, -1:], 0).astype(F32)]]
  transfers between devices with their start and end apart: 11 -> 11, of which waited for: 9 -> 10; matrix products, arithmetic and copies ran while one was open for 0% -> 3% of each run, Pallas kernels for 14% -> 24%
where the time goes in v4:
time: 47.5 us; the launch traced here: 47.2 us
  waiting for transfers between devices  17.8 us (37%)
  Pallas kernels  16.6 us (35%)
  starting transfers between devices  9.12 us (19%)
  between operations  1.41 us (3%)
  local copies, waits for them, and re-layouts  1.28 us (3%)
  other arithmetic  0.99 us (2%)
    pallas_call x9, Pallas kernels, call(): pl.pallas_call(inner, out_shape=[*outs, *(jax.ShapeDtypeStruct(a.shape, a...  16.6 us
    ppermute x4, waiting for transfers between devices, turn(): lax.ppermute(x, axis, [(i, (i + distance) % count) for i in range(count)])  8.48 us
    ppermute x4, starting transfers between devices, turn(): lax.ppermute(x, axis, [(i, (i + distance) % count) for i in range(count)])  5.23 us
    ppermute x1, waiting for transfers between devices, body(): got_t = lax.ppermute(send_t, 'seg', partner)  2.78 us
    ppermute x2, starting transfers between devices, body(): got = lax.ppermute(send, 'seg', partner)  2.13 us
    ppermute x2, waiting for transfers between devices, body(): got = lax.ppermute(send, 'seg', partner)  2.1 us
    ppermute x1, waiting for transfers between devices, body(): other_whole = lax.ppermute(own_whole, 'seg', swap)  1.9 us
    ppermute x1, starting transfers between devices, body(): got_t = lax.ppermute(send_t, 'seg', partner)  1.55 us
  transfers between devices with their start and end apart: 11, of which 10 were waited for; matrix products, arithmetic and copies ran while one was open for 3% of the time, Pallas kernels for 24%

profile of v4, /device:TPU:0, one launch (start us, length us, event | category | flops | bytes accessed | tf_op | source)
XLA Modules:
  0.0 47.2 jit_solution(15150078549548550042)
XLA Ops:
  0.6 3.1 %collective-permute-start = (f32[2,64,512]{2,1,0:T(8,128)}, f32[2,64,512]{2,1,0:T(8,128)S(1)}, u32[]{:S(2)}, u32[]{:S(2)}) collective-permute-start(f32[2,64,512]{2,1,0:T(8,128)} %refs_2_.3), channel_id=1, source_target_pairs={{0,1},{1,2},{2,3},{3,0},{4,5},{5,6},{6,7},{7,4},{8,9},{9,10},{10,1... | collective-permute-start | bytes 786440 | tf_op jit(solution)/shard_map/ppermute | solution.py:361
  3.7 0.0 collective-permute-start.2
  3.7 4.1 %collective-permute-done.2.refs_1_ = s32[2,4]{1,0:T(2,128)S(1)} collective-permute-done((s32[2,4]{1,0:T(2,128)}, s32[2,4]{1,0:T(2,128)S(1)}, u32[]{:S(2)}, u32[]{:S(2)}) %collective-permute-start.2) | collective-permute-done | bytes 64 | tf_op jit(solution)/shard_map/ppermute | solution.py:361
  7.8 0.6 %slice.3 = s32[1,1]{1,0:T(1,128)} slice(s32[2,4]{1,0:T(2,128)S(1)} %collective-permute-done.2.refs_1_), slice={[1:2], [3:4]} | slice | bytes 8 | tf_op jit(solution)/shard_map/slice | solution.py:383
  9.0 1.0 %broadcast_add_fusion = f32[2,64,512]{2,1,0:T(8,128)S(1)} fusion(f32[2,64,512]{2,1,0:T(8,128)} %refs_2_.3, f32[]{:T(128)} %bitcast), kind=kLoop, calls=%fused_computation | loop fusion | flops 65536 | bytes 524292 | tf_op jit(solution)/shard_map/add | solution.py:383
  10.0 0.0 copy-start.1
  10.0 0.0 copy-start.2
  10.0 2.1 %collective-permute-start.3 = (f32[2,64,512]{2,1,0:T(8,128)S(1)}, f32[2,64,512]{2,1,0:T(8,128)S(1)}, u32[]{:S(2)}, u32[]{:S(2)}) collective-permute-start(f32[2,64,512]{2,1,0:T(8,128)S(1)} %broadcast_add_fusion), channel_id=1, source_target_pairs={{0,3},{1,0},{2,1},{3,2},{4,7},{5,4},{6,5},{7,6},{8,11},{9,8},{10,9... | collective-permute-start | bytes 786440 | tf_op jit(solution)/shard_map/ppermute | solution.py:361
  12.2 0.2 collective-permute-done.refs_2_.refs_3_
  12.4 0.0 collective-permute-start.1
  12.4 0.0 copy-start.3
  12.4 0.7 %copy-done.3 = s32[2,4]{1,0:T(2,128)S(1)} copy-done((s32[2,4]{1,0:T(2,128)S(1)}, s32[2,4]{1,0:T(2,128)}, u32[]{:S(2)}) %copy-start.3) | copy-done | bytes 56
  13.0 2.9 %prior.3 = (f32[256,256]{1,0:T(8,128)S(1)}, f32[128,512]{1,0:T(8,128)S(1)}, bf16[256,512]{1,0:T(8,128)(2,1)S(1)}, bf16[256,512]{1,0:T(8,128)(2,1)S(1)}) custom-call(s32[2,4]{1,0:T(2,128)S(1)} %copy-done.3, f32[2,512,512]{2,1,0:T(8,128)} %refs_1_.5), custom_call_target="tpu_custom_call" | custom-call | flops 402653184 | bytes 3670016 | tf_op jit(solution)/shard_map/prior/pallas_call | solution.py:105
  15.9 2.9 %prior.2 = (f32[256,256]{1,0:T(8,128)S(1)}, f32[128,512]{1,0:T(8,128)S(1)}, bf16[256,512]{1,0:T(8,128)(2,1)S(1)}, bf16[256,512]{1,0:T(8,128)(2,1)S(1)}) custom-call(s32[2,4]{1,0:T(2,128)S(1)} %copy-done.3, s32[2,4]{1,0:T(2,128)S(1)} %collective-permute-done.2.refs_1_, f32[2,512,512]{2,1,0:T(8,128)} %refs_1_.5), custom_call_target="tpu_custom_call" | custom-call | flops 402653184 | bytes 3670016 | tf_op jit(solution)/shard_map/prior/pallas_call | solution.py:105
  18.8 0.8 %collective-permute-done.3.refs_3_.refs_5_ = f32[2,64,512]{2,1,0:T(8,128)S(1)} collective-permute-done((f32[2,64,512]{2,1,0:T(8,128)S(1)}, f32[2,64,512]{2,1,0:T(8,128)S(1)}, u32[]{:S(2)}, u32[]{:S(2)}) %collective-permute-start.3) | collective-permute-done | bytes 262176 | tf_op jit(solution)/shard_map/ppermute | solution.py:361
  19.6 0.0 copy-done.1
  19.6 0.0 copy-done.2
  19.6 1.4 %links.1.refs_2_ = f32[2,256,256]{2,1,0:T(8,128)S(1)} custom-call(s32[2,4]{1,0:T(2,128)S(1)} %copy-done.2, f32[2,64,512]{2,1,0:T(8,128)S(1)} %copy-done.1, f32[2,64,512]{2,1,0:T(8,128)S(1)} %collective-permute-done.refs_2_.refs_3_, f32[2,64,512]{2,1,0:T(8,128)S(1)} %collective-permute-done.3.refs_3_.refs_5_, ...), custom_call_target="tpu_custom_call" | custom-call | flops 402653184 | bytes 3407872 | tf_op jit(solution)/shard_map/links/pallas_call | solution.py:105
  20.9 0.0 copy-start
  20.9 3.5 %collective-permute-done.1.refs_1_.refs_4_ = f32[2,64,512]{2,1,0:T(8,128)S(1)} collective-permute-done((f32[2,64,512]{2,1,0:T(8,128)S(1)}, f32[2,64,512]{2,1,0:T(8,128)S(1)}, u32[]{:S(2)}, u32[]{:S(2)}) %collective-permute-start.1) | collective-permute-done | bytes 262176 | tf_op jit(solution)/shard_map/ppermute | solution.py:361
  24.4 1.8 %segment.1 = (f32[2,256,256]{2,1,0:T(8,128)S(1)}, f32[512,256]{1,0:T(8,128)S(1)}) custom-call(s32[2,4]{1,0:T(2,128)S(1)} %copy-done.2, f32[2,64,512]{2,1,0:T(8,128)S(1)} %collective-permute-done.1.refs_1_.refs_4_, f32[2,256,256]{2,1,0:T(8,128)S(1)} %links.1.refs_2_, bf16[256,512]{1,0:T(8,128)(2,1)S(1)} %get-tuple-element.24.refs_4_.refs_3_, ...), custom_call_target="tpu_custom_call" | custom-call | flops 704643072 | bytes 4456448 | tf_op jit(solution)/shard_map/segment/pallas_call | solution.py:105
  26.2 0.1 collective-permute-start.4
  26.3 1.9 %collective-permute-done.4.refs_1_.refs_4_ = f32[512,256]{1,0:T(8,128)S(1)} collective-permute-done((f32[512,256]{1,0:T(8,128)S(1)}, f32[512,256]{1,0:T(8,128)S(1)}, u32[]{:S(2)}, u32[]{:S(2)}) %collective-permute-start.4) | collective-permute-done | bytes 524320 | tf_op jit(solution)/shard_map/ppermute | solution.py:417
  28.2 0.6 %chip.1 = (f32[256,256]{1,0:T(8,128)S(1)}, f32[256,256]{1,0:T(8,128)S(1)}, f32[192,128]{1,0:T(8,128)S(1)}, f32[128,256]{1,0:T(8,128)S(1)}) custom-call(f32[512,256]{1,0:T(8,128)S(1)} %get-tuple-element.30.refs_0_, f32[512,256]{1,0:T(8,128)S(1)} %collective-permute-done.4.refs_1_.refs_4_), custom_call_target="tpu_custom_call" | custom-call | flops 301989888 | bytes 1802240 | tf_op jit(solution)/shard_map/chip/pallas_call | solution.py:105
  28.8 1.5 %collective-permute-start.5 = (f32[128,256]{1,0:T(8,128)S(1)}, f32[128,256]{1,0:T(8,128)S(1)}, u32[]{:S(2)}, u32[]{:S(2)}) collective-permute-start(f32[128,256]{1,0:T(8,128)S(1)} %get-tuple-element.33), channel_id=1, source_target_pairs={{0,8},{4,12},{8,0},{12,4},{16,24},{20,28},{24,16},{28,20},{1,9},{5... | collective-permute-start | bytes 393224 | tf_op jit(solution)/shard_map/ppermute | solution.py:457
  30.4 0.5 %collective-permute-start.7 = (f32[192,128]{1,0:T(8,128)S(1)}, f32[192,128]{1,0:T(8,128)S(1)}, u32[]{:S(2)}, u32[]{:S(2)}) collective-permute-start(f32[192,128]{1,0:T(8,128)S(1)} %get-tuple-element.34), channel_id=1, source_target_pairs={{0,8},{4,12},{8,0},{12,4},{16,24},{20,28},{24,16},{28,20},{1,9},{5... | collective-permute-start | bytes 294920 | tf_op jit(solution)/shard_map/ppermute | solution.py:451
  30.9 0.0 copy-done
  30.9 1.5 %maps.1 = (f32[2,256,512]{2,1,0:T(8,128)S(1)}, f32[1,128]{1,0:T(1,128)S(1)}) custom-call(s32[2,4]{1,0:T(2,128)S(1)} %copy-done.2, f32[2,512,512]{2,1,0:T(8,128)S(1)} %copy-done, f32[2,64,512]{2,1,0:T(8,128)S(1)} %copy-done.1, f32[2,64,512]{2,1,0:T(8,128)S(1)} %collective-permute-done.refs_2_.refs_3_, ...), custom_call_target="tpu_custom_call" | custom-call | flops 805306368 | bytes 4194816 | tf_op jit(solution)/shard_map/maps/pallas_call | solution.py:105
  32.4 2.8 %collective-permute-done.5.refs_2_.refs_7_ = f32[128,256]{1,0:T(8,128)S(1)} collective-permute-done((f32[128,256]{1,0:T(8,128)S(1)}, f32[128,256]{1,0:T(8,128)S(1)}, u32[]{:S(2)}, u32[]{:S(2)}) %collective-permute-start.5) | collective-permute-done | bytes 131104 | tf_op jit(solution)/shard_map/ppermute | solution.py:457
  35.2 0.0 collective-permute-start.6
  35.2 1.3 %collective-permute-done.7 = f32[192,128]{1,0:T(8,128)S(1)} collective-permute-done((f32[192,128]{1,0:T(8,128)S(1)}, f32[192,128]{1,0:T(8,128)S(1)}, u32[]{:S(2)}, u32[]{:S(2)}) %collective-permute-start.7) | collective-permute-done | bytes 98336 | tf_op jit(solution)/shard_map/ppermute | solution.py:451
  36.5 0.1 collective-permute-start.8
  36.6 1.3 %collective-permute-done.8.refs_5_.refs_10_ = f32[192,128]{1,0:T(8,128)S(1)} collective-permute-done((f32[192,128]{1,0:T(8,128)S(1)}, f32[192,128]{1,0:T(8,128)S(1)}, u32[]{:S(2)}, u32[]{:S(2)}) %collective-permute-start.8) | collective-permute-done | bytes 98336 | tf_op jit(solution)/shard_map/ppermute | solution.py:460
  37.9 0.0 collective-permute-done.6.refs_3_.refs_8_
  37.9 0.7 %merge.1 = f32[192,128]{1,0:T(8,128)S(1)} custom-call(f32[256,256]{1,0:T(8,128)S(1)} %get-tuple-element.31.refs_0_, f32[256,256]{1,0:T(8,128)S(1)} %get-tuple-element.32.refs_1_, f32[128,256]{1,0:T(8,128)S(1)} %collective-permute-done.5.refs_2_.refs_7_, f32[128,256]{1,0:T(8,128)S(1)} %collective-permute-done.6.refs_3_.refs_8_, ...), custom_call_target="tpu_custom_call" | custom-call | flops 301989888 | bytes 1081344 | tf_op jit(solution)/shard_map/merge/pallas_call | solution.py:105
  38.6 1.6 %collective-permute-start.9 = (f32[192,128]{1,0:T(8,128)S(1)}, f32[192,128]{1,0:T(8,128)S(1)}, u32[]{:S(2)}, u32[]{:S(2)}) collective-permute-start(f32[192,128]{1,0:T(8,128)S(1)} %merge.1), channel_id=1, source_target_pairs={{0,16},{4,20},{8,24},{12,28},{16,0},{20,4},{24,8},{28,12},{1,17},{... | collective-permute-start | bytes 294920 | tf_op jit(solution)/shard_map/ppermute | solution.py:451
  40.2 2.5 %prepare.1 = (bf16[2,192,256]{2,1,0:T(8,128)(2,1)S(1)}, bf16[2,192,256]{2,1,0:T(8,128)(2,1)S(1)}, bf16[2,256,512]{2,1,0:T(8,128)(2,1)S(1)}, bf16[2,256,512]{2,1,...) custom-call(f32[256,256]{1,0:T(8,128)S(1)} %get-tuple-element.28.refs_7_.refs_0_, ...), custom_call_target="tpu_custom_call" | custom-call | flops 1459617792 | bytes 7275008 | tf_op jit(solution)/shard_map/prepare/pallas_call | solution.py:105
  42.7 0.8 %collective-permute-done.9 = f32[192,128]{1,0:T(8,128)S(1)} collective-permute-done((f32[192,128]{1,0:T(8,128)S(1)}, f32[192,128]{1,0:T(8,128)S(1)}, u32[]{:S(2)}, u32[]{:S(2)}) %collective-permute-start.9) | collective-permute-done | bytes 98336 | tf_op jit(solution)/shard_map/ppermute | solution.py:451
  43.5 0.1 collective-permute-start.10
  43.6 1.3 %collective-permute-done.10.refs_2_ = f32[192,128]{1,0:T(8,128)S(1)} collective-permute-done((f32[192,128]{1,0:T(8,128)S(1)}, f32[192,128]{1,0:T(8,128)S(1)}, u32[]{:S(2)}, u32[]{:S(2)}) %collective-permute-start.10) | collective-permute-done | bytes 98336 | tf_op jit(solution)/shard_map/ppermute | solution.py:455
  44.9 2.3 %finish.1 = (f32[2,128,512]{2,1,0:T(8,128)}, f32[2,64,512]{2,1,0:T(8,128)}) custom-call(s32[2,4]{1,0:T(2,128)S(1)} %copy-done.2, f32[192,128]{1,0:T(8,128)S(1)} %broadcast_add_fusion.1.refs_1_, f32[192,128]{1,0:T(8,128)S(1)} %collective-permute-done.10.refs_2_, bf16[2,192,256]{2,1,0:T(8,128)(2,1)S(1)} %get-tuple-element.41.refs_3_, ...), custom_call_target="tpu_custom_call" | custom-call | flops 452984832 | bytes 4653056 | tf_op jit(solution)/shard_map/finish/pallas_call | solution.py:105
  (2 shorter events, 0.0 us)
Async XLA Ops:
  0.6 11.7 %collective-permute-start = (f32[2,64,512]{2,1,0:T(8,128)}, f32[2,64,512]{2,1,0:T(8,128)S(1)}, u32[]{:S(2)}, u32[]{:S(2)}) collective-permute-start(f32[2,64,512]{2,1,0:T(8,128)} %refs_2_.3), channel_id=1, source_target_pairs={{0,1},{1,2},{2,3},{3,0},{4,5},{5,6},{6,7},{7,4},{8,9},{9,10},{10,1... | collective-permute-start | bytes 786440 | tf_op jit(solution)/shard_map/ppermute | solution.py:361
  3.7 4.1 %collective-permute-start.2 = (s32[2,4]{1,0:T(2,128)}, s32[2,4]{1,0:T(2,128)S(1)}, u32[]{:S(2)}, u32[]{:S(2)}) collective-permute-start(s32[2,4]{1,0:T(2,128)} %refs_0_.7), channel_id=1, source_target_pairs={{0,4},{4,8},{8,12},{12,16},{16,20},{20,24},{24,28},{28,0},{1,5},{5... | collective-permute-start | bytes 104 | tf_op jit(solution)/shard_map/ppermute | solution.py:361
  10.0 9.5 %copy-start.1 = (f32[2,64,512]{2,1,0:T(8,128)S(1)}, f32[2,64,512]{2,1,0:T(8,128)}, u32[]{:S(2)}) copy-start(f32[2,64,512]{2,1,0:T(8,128)} %refs_2_.3) | copy-start | bytes 786436
  10.0 9.5 %copy-start.2 = (s32[2,4]{1,0:T(2,128)S(1)}, s32[2,4]{1,0:T(2,128)}, u32[]{:S(2)}) copy-start(s32[2,4]{1,0:T(2,128)} %refs_0_.11) | copy-start | bytes 100
  10.0 9.5 %collective-permute-start.3 = (f32[2,64,512]{2,1,0:T(8,128)S(1)}, f32[2,64,512]{2,1,0:T(8,128)S(1)}, u32[]{:S(2)}, u32[]{:S(2)}) collective-permute-start(f32[2,64,512]{2,1,0:T(8,128)S(1)} %broadcast_add_fusion), channel_id=1, source_target_pairs={{0,3},{1,0},{2,1},{3,2},{4,7},{5,4},{6,5},{7,6},{8,11},{9,8},{10,9... | collective-permute-start | bytes 786440 | tf_op jit(solution)/shard_map/ppermute | solution.py:361
  12.4 12.0 %collective-permute-start.1 = (f32[2,64,512]{2,1,0:T(8,128)S(1)}, f32[2,64,512]{2,1,0:T(8,128)S(1)}, u32[]{:S(2)}, u32[]{:S(2)}) collective-permute-start(f32[2,64,512]{2,1,0:T(8,128)S(1)} %collective-permute-done.refs_2_.refs_3_), channel_id=1, source_target_pairs={{0,1},{1,2},{2,3},{3,0},{4,5},{5,6},{6,7},{7,4},{8,9},{9,10},{10,1... | collective-permute-start | bytes 786440 | tf_op jit(solution)/shard_map/ppermute | solution.py:361
  12.4 0.7 %copy-start.3 = (s32[2,4]{1,0:T(2,128)S(1)}, s32[2,4]{1,0:T(2,128)}, u32[]{:S(2)}) copy-start(s32[2,4]{1,0:T(2,128)} %refs_0_.7) | copy-start | bytes 100
  20.9 10.0 %copy-start = (f32[2,512,512]{2,1,0:T(8,128)S(1)}, f32[2,512,512]{2,1,0:T(8,128)}, u32[]{:S(2)}) copy-start(f32[2,512,512]{2,1,0:T(8,128)} %refs_1_.5) | copy-start | bytes 6291460
  26.2 2.0 %collective-permute-start.4 = (f32[512,256]{1,0:T(8,128)S(1)}, f32[512,256]{1,0:T(8,128)S(1)}, u32[]{:S(2)}, u32[]{:S(2)}) collective-permute-start(f32[512,256]{1,0:T(8,128)S(1)} %get-tuple-element.30.refs_0_), channel_id=1, source_target_pairs={{0,4},{4,0},{8,12},{12,8},{16,20},{20,16},{24,28},{28,24},{1,5},{5... | collective-permute-start | bytes 1572872 | tf_op jit(solution)/shard_map/ppermute | solution.py:417
  28.8 6.4 %collective-permute-start.5 = (f32[128,256]{1,0:T(8,128)S(1)}, f32[128,256]{1,0:T(8,128)S(1)}, u32[]{:S(2)}, u32[]{:S(2)}) collective-permute-start(f32[128,256]{1,0:T(8,128)S(1)} %get-tuple-element.33), channel_id=1, source_target_pairs={{0,8},{4,12},{8,0},{12,4},{16,24},{20,28},{24,16},{28,20},{1,9},{5... | collective-permute-start | bytes 393224 | tf_op jit(solution)/shard_map/ppermute | solution.py:457
  30.4 6.2 %collective-permute-start.7 = (f32[192,128]{1,0:T(8,128)S(1)}, f32[192,128]{1,0:T(8,128)S(1)}, u32[]{:S(2)}, u32[]{:S(2)}) collective-permute-start(f32[192,128]{1,0:T(8,128)S(1)} %get-tuple-element.34), channel_id=1, source_target_pairs={{0,8},{4,12},{8,0},{12,4},{16,24},{20,28},{24,16},{28,20},{1,9},{5... | collective-permute-start | bytes 294920 | tf_op jit(solution)/shard_map/ppermute | solution.py:451
  35.2 2.7 %collective-permute-start.6 = (f32[128,256]{1,0:T(8,128)S(1)}, f32[128,256]{1,0:T(8,128)S(1)}, u32[]{:S(2)}, u32[]{:S(2)}) collective-permute-start(f32[128,256]{1,0:T(8,128)S(1)} %collective-permute-done.5.refs_2_.refs_7_), channel_id=1, source_target_pairs={{0,4},{4,0},{8,12},{12,8},{16,20},{20,16},{24,28},{28,24},{1,5},{5... | collective-permute-start | bytes 393224 | tf_op jit(solution)/shard_map/ppermute | solution.py:460
  36.5 1.4 %collective-permute-start.8 = (f32[192,128]{1,0:T(8,128)S(1)}, f32[192,128]{1,0:T(8,128)S(1)}, u32[]{:S(2)}, u32[]{:S(2)}) collective-permute-start(f32[192,128]{1,0:T(8,128)S(1)} %broadcast_add_fusion.2.refs_4_.refs_9_), channel_id=1, source_target_pairs={{0,4},{4,0},{8,12},{12,8},{16,20},{20,16},{24,28},{28,24},{1,5},{5... | collective-permute-start | bytes 294920 | tf_op jit(solution)/shard_map/ppermute | solution.py:460
  38.6 4.9 %collective-permute-start.9 = (f32[192,128]{1,0:T(8,128)S(1)}, f32[192,128]{1,0:T(8,128)S(1)}, u32[]{:S(2)}, u32[]{:S(2)}) collective-permute-start(f32[192,128]{1,0:T(8,128)S(1)} %merge.1), channel_id=1, source_target_pairs={{0,16},{4,20},{8,24},{12,28},{16,0},{20,4},{24,8},{28,12},{1,17},{... | collective-permute-start | bytes 294920 | tf_op jit(solution)/shard_map/ppermute | solution.py:451
  43.5 1.4 %collective-permute-start.10 = (f32[192,128]{1,0:T(8,128)S(1)}, f32[192,128]{1,0:T(8,128)S(1)}, u32[]{:S(2)}, u32[]{:S(2)}) collective-permute-start(f32[192,128]{1,0:T(8,128)S(1)} %broadcast_add_fusion.1.refs_1_), channel_id=1, source_target_pairs={{0,4},{4,0},{8,12},{12,8},{16,20},{20,16},{24,28},{28,24},{1,5},{5... | collective-permute-start | bytes 294920 | tf_op jit(solution)/shard_map/ppermute | solution.py:455

commit v5 on v4

--- a/solution.py
+++ b/solution.py
@@ -143,10 +143,11 @@
 
 
 def prior_kernel(panel, *refs):
-    *scalar_refs, inv_hbm, base_ref, own_ref, pick_high_ref, pick_low_ref = refs[:-2]
+    *scalar_refs, inv_hbm, base_ref, own_ref, pick_high_ref, pick_low_ref, token_ref = refs[:-2]
     inv_ref, sem = refs[-2:]
     copy = pltpu.make_async_copy(inv_hbm.at[panel], inv_ref, sem)
     copy.start()
+    token_ref[...] = jnp.zeros_like(token_ref)
     chosen = chosen_of(panel, *scalar_refs)
     own_cols = own_ref.shape[0]
     own_at = pl.ds(pl.multiple_of(lax.axis_index("row") * own_cols, own_cols), own_cols)
@@ -360,16 +361,16 @@
         count = lax.axis_size(axis)
         return lax.ppermute(x, axis, [(i, (i + distance) % count) for i in range(count)])
 
-    ups = [factor_off]
-    for _ in range(row_count // 2):
-        ups.append(turn(ups[-1], "row", 1))
     prior_fill = turn(fill_blocks, "seg", 1)
+    ups = [factor_off, turn(factor_off, "row", 1)]
+    for _ in range(1, row_count // 2):
+        ups.append(turn(ups[-1] + jnp.minimum(jnp.min(prior_fill), 0).astype(F32), "row", 1))
     pick = jax.ShapeDtypeStruct((chosen_cols, width), BF16)
-    bases, priors, picks = [], [], []
+    bases, priors, picks, tokens = [], [], [], []
     for p in range(panels):
-        base, own_prior, *high_low = call(
+        base, own_prior, *high_low, token = call(
             functools.partial(prior_kernel, p),
-            [shape(chosen_cols, chosen_cols), shape(own_cols, width), pick, pick],
+            [shape(chosen_cols, chosen_cols), shape(own_cols, width), pick, pick, shape(1, 1, width)],
             [fill_blocks] if p else [fill_blocks, prior_fill],
             [],
             far=[inv_diag],
@@ -380,7 +381,8 @@
         bases.append(base)
         priors.append(own_prior)
         picks += high_low
-    downs = [factor_off + jnp.minimum(prior_fill[-1:, -1:], 0).astype(F32)]
+        tokens.append(token)
+    downs = [factor_off + tokens[-1]]
     for _ in range((row_count - 1) // 2):
         downs.append(turn(downs[-1], "row", -1))
     parts = ups + downs[:0:-1]

time: 47.5 us -> 46.9 us (0.987)
  local copies, waits for them, and re-layouts: 1.28 us -> 0.7 us
  starting transfers between devices: 9.12 us -> 9.63 us
    add x1 -> x2, other arithmetic: 0.97 us -> 0.04 us  [the longest x1 0.02 us: body(): downs = [factor_off + tokens[-1]]]
    reduce_min x0 -> x1, other arithmetic: none -> 0.63 us  [body(): jnp.min(prior_fill)]
    slice x1 -> x0, local copies, waits for them, and re-layouts: 0.58 us -> none  [body(): downs = [factor_off + jnp.minimum(prior_fill[-1:, -1:], 0).astype(F32)]]
  transfers between devices with their start and end apart: 11 -> 11, of which waited for: 10 -> 9; matrix products, arithmetic and copies ran while one was open for 3% -> 1% of each run, Pallas kernels for 24% -> 24%
where the time goes in v5:
time: 46.9 us; the launch traced here: 46.7 us
  waiting for transfers between devices  17.7 us (38%)
  Pallas kernels  16.6 us (35%)
  starting transfers between devices  9.63 us (21%)
  between operations  1.44 us (3%)
  local copies, waits for them, and re-layouts  0.7 us (1%)
  other arithmetic  0.69 us (1%)
    pallas_call x9, Pallas kernels, call(): pl.pallas_call(inner, out_shape=[*outs, *(jax.ShapeDtypeStruct(a.shape, a...  16.6 us
    ppermute x4, waiting for transfers between devices, turn(): lax.ppermute(x, axis, [(i, (i + distance) % count) for i in range(count)])  8.46 us
    ppermute x4, starting transfers between devices, turn(): lax.ppermute(x, axis, [(i, (i + distance) % count) for i in range(count)])  5.29 us
    ppermute x1, waiting for transfers between devices, body(): got_t = lax.ppermute(send_t, 'seg', partner)  2.76 us
    ppermute x2, waiting for transfers between devices, body(): got = lax.ppermute(send, 'seg', partner)  2.37 us
    ppermute x2, starting transfers between devices, body(): got = lax.ppermute(send, 'seg', partner)  2.1 us
    ppermute x1, starting transfers between devices, body(): got_t = lax.ppermute(send_t, 'seg', partner)  1.58 us
    ppermute x1, waiting for transfers between devices, body(): other_whole = lax.ppermute(own_whole, 'seg', swap)  1.54 us
  transfers between devices with their start and end apart: 11, of which 9 were waited for; matrix products, arithmetic and copies ran while one was open for 1% of the time, Pallas kernels for 24%

profile of v5, /device:TPU:0, one launch (start us, length us, event | category | flops | bytes accessed | tf_op | source)
XLA Modules:
  0.0 46.7 jit_solution(11345836361562881592)
XLA Ops:
  0.6 0.0 copy-start.1
  0.6 3.1 %collective-permute-start = (f32[2,64,512]{2,1,0:T(8,128)}, f32[2,64,512]{2,1,0:T(8,128)S(1)}, u32[]{:S(2)}, u32[]{:S(2)}) collective-permute-start(f32[2,64,512]{2,1,0:T(8,128)} %refs_2_.3), channel_id=1, source_target_pairs={{0,1},{1,2},{2,3},{3,0},{4,5},{5,6},{6,7},{7,4},{8,9},{9,10},{10,1... | collective-permute-start | bytes 786440 | tf_op jit(solution)/shard_map/ppermute | solution.py:362
  3.7 0.0 collective-permute-start.1
  3.7 0.0 copy-start.3
  3.7 0.7 %copy-done.3 = s32[2,4]{1,0:T(2,128)S(1)} copy-done((s32[2,4]{1,0:T(2,128)S(1)}, s32[2,4]{1,0:T(2,128)}, u32[]{:S(2)}) %copy-start.3) | copy-done | bytes 56
  4.4 0.0 copy-start.4
  4.4 2.9 %prior.2 = (f32[256,256]{1,0:T(8,128)S(1)}, f32[128,512]{1,0:T(8,128)S(1)}, bf16[256,512]{1,0:T(8,128)(2,1)S(1)}, bf16[256,512]{1,0:T(8,128)(2,1)S(1)}, f32[1,1,512]{2,1,0:T(1,128)S(1)}) custom-call(s32[2,4]{1,0:T(2,128)S(1)} %copy-done.3, f32[2,512,512]{2,1,0:T(8,128)} %refs_1_.5), custom_call_target="tpu_custom_call" | custom-call | flops 402653184 | bytes 3672064 | tf_op jit(solution)/shard_map/prior/pallas_call | solution.py:105
  7.3 0.0 copy-start.2
  7.3 0.0 copy-done.1
  7.3 2.2 %collective-permute-start.3 = (f32[2,64,512]{2,1,0:T(8,128)S(1)}, f32[2,64,512]{2,1,0:T(8,128)S(1)}, u32[]{:S(2)}, u32[]{:S(2)}) collective-permute-start(f32[2,64,512]{2,1,0:T(8,128)S(1)} %broadcast_add_fusion), channel_id=1, source_target_pairs={{0,3},{1,0},{2,1},{3,2},{4,7},{5,4},{6,5},{7,6},{8,11},{9,8},{10,9... | collective-permute-start | bytes 786440 | tf_op jit(solution)/shard_map/ppermute | solution.py:362
  9.5 0.0 collective-permute-done.1.refs_1_
  9.5 0.6 %reduce_min.9 = s32[]{:T(128)} reduce(s32[2,4]{1,0:T(2,128)S(1)} %collective-permute-done.1.refs_1_, s32[]{:T(128)} %constant.0.clone.1), dimensions={0,1}, to_apply=%region_0.0 | reduce | flops 7 | bytes 40 | tf_op jit(solution)/shard_map/reduce_min | solution.py:367
  10.8 1.6 %collective-permute-done.refs_2_.refs_3_ = f32[2,64,512]{2,1,0:T(8,128)S(1)} collective-permute-done((f32[2,64,512]{2,1,0:T(8,128)}, f32[2,64,512]{2,1,0:T(8,128)S(1)}, u32[]{:S(2)}, u32[]{:S(2)}) %collective-permute-start) | collective-permute-done | bytes 262176 | tf_op jit(solution)/shard_map/ppermute | solution.py:362
  12.4 0.1 collective-permute-start.2
  12.5 0.0 copy-done.4
  12.5 2.9 %prior.3 = (f32[256,256]{1,0:T(8,128)S(1)}, f32[128,512]{1,0:T(8,128)S(1)}, bf16[256,512]{1,0:T(8,128)(2,1)S(1)}, bf16[256,512]{1,0:T(8,128)(2,1)S(1)}, f32[1,1,512]{2,1,0:T(1,128)}) custom-call(s32[2,4]{1,0:T(2,128)S(1)} %copy-done.4, s32[2,4]{1,0:T(2,128)S(1)} %collective-permute-done.1.refs_1_, f32[2,512,512]{2,1,0:T(8,128)} %refs_1_.5), custom_call_target="tpu_custom_call" | custom-call | flops 402653184 | bytes 3672064 | tf_op jit(solution)/shard_map/prior/pallas_call | solution.py:105
  15.4 2.5 %collective-permute-done.3.refs_3_.refs_5_ = f32[2,64,512]{2,1,0:T(8,128)S(1)} collective-permute-done((f32[2,64,512]{2,1,0:T(8,128)S(1)}, f32[2,64,512]{2,1,0:T(8,128)S(1)}, u32[]{:S(2)}, u32[]{:S(2)}) %collective-permute-start.3) | collective-permute-done | bytes 262176 | tf_op jit(solution)/shard_map/ppermute | solution.py:362
  17.8 0.0 copy-done.2
  17.8 1.3 %links.1.refs_2_ = f32[2,256,256]{2,1,0:T(8,128)S(1)} custom-call(s32[2,4]{1,0:T(2,128)S(1)} %copy-done.2, f32[2,64,512]{2,1,0:T(8,128)S(1)} %copy-done.1, f32[2,64,512]{2,1,0:T(8,128)S(1)} %collective-permute-done.refs_2_.refs_3_, f32[2,64,512]{2,1,0:T(8,128)S(1)} %collective-permute-done.3.refs_3_.refs_5_, ...), custom_call_target="tpu_custom_call" | custom-call | flops 402653184 | bytes 3407872 | tf_op jit(solution)/shard_map/links/pallas_call | solution.py:105
  19.2 0.0 copy-start
  19.2 4.4 %collective-permute-done.2.refs_1_.refs_4_ = f32[2,64,512]{2,1,0:T(8,128)S(1)} collective-permute-done((f32[2,64,512]{2,1,0:T(8,128)S(1)}, f32[2,64,512]{2,1,0:T(8,128)S(1)}, u32[]{:S(2)}, u32[]{:S(2)}) %collective-permute-start.2) | collective-permute-done | bytes 262176 | tf_op jit(solution)/shard_map/ppermute | solution.py:362
  23.6 1.8 %segment.1 = (f32[2,256,256]{2,1,0:T(8,128)S(1)}, f32[512,256]{1,0:T(8,128)S(1)}) custom-call(s32[2,4]{1,0:T(2,128)S(1)} %copy-done.2, f32[2,64,512]{2,1,0:T(8,128)S(1)} %collective-permute-done.2.refs_1_.refs_4_, f32[2,256,256]{2,1,0:T(8,128)S(1)} %links.1.refs_2_, bf16[256,512]{1,0:T(8,128)(2,1)S(1)} %get-tuple-element.26.refs_4_.refs_3_, ...), custom_call_target="tpu_custom_call" | custom-call | flops 704643072 | bytes 4456448 | tf_op jit(solution)/shard_map/segment/pallas_call | solution.py:105
  25.4 0.5 %collective-permute-start.4 = (f32[512,256]{1,0:T(8,128)S(1)}, f32[512,256]{1,0:T(8,128)S(1)}, u32[]{:S(2)}, u32[]{:S(2)}) collective-permute-start(f32[512,256]{1,0:T(8,128)S(1)} %get-tuple-element.32.refs_0_), channel_id=1, source_target_pairs={{0,4},{4,0},{8,12},{12,8},{16,20},{20,16},{24,28},{28,24},{1,5},{5... | collective-permute-start | bytes 1572872 | tf_op jit(solution)/shard_map/ppermute | solution.py:419
  25.9 1.5 %collective-permute-done.4.refs_1_.refs_4_ = f32[512,256]{1,0:T(8,128)S(1)} collective-permute-done((f32[512,256]{1,0:T(8,128)S(1)}, f32[512,256]{1,0:T(8,128)S(1)}, u32[]{:S(2)}, u32[]{:S(2)}) %collective-permute-start.4) | collective-permute-done | bytes 524320 | tf_op jit(solution)/shard_map/ppermute | solution.py:419
  27.5 0.6 %chip.1 = (f32[256,256]{1,0:T(8,128)S(1)}, f32[256,256]{1,0:T(8,128)S(1)}, f32[192,128]{1,0:T(8,128)S(1)}, f32[128,256]{1,0:T(8,128)S(1)}) custom-call(f32[512,256]{1,0:T(8,128)S(1)} %get-tuple-element.32.refs_0_, f32[512,256]{1,0:T(8,128)S(1)} %collective-permute-done.4.refs_1_.refs_4_), custom_call_target="tpu_custom_call" | custom-call | flops 301989888 | bytes 1802240 | tf_op jit(solution)/shard_map/chip/pallas_call | solution.py:105
  28.1 1.6 %collective-permute-start.5 = (f32[128,256]{1,0:T(8,128)S(1)}, f32[128,256]{1,0:T(8,128)S(1)}, u32[]{:S(2)}, u32[]{:S(2)}) collective-permute-start(f32[128,256]{1,0:T(8,128)S(1)} %get-tuple-element.35), channel_id=1, source_target_pairs={{0,8},{4,12},{8,0},{12,4},{16,24},{20,28},{24,16},{28,20},{1,9},{5... | collective-permute-start | bytes 393224 | tf_op jit(solution)/shard_map/ppermute | solution.py:459
  29.7 0.5 %collective-permute-start.7 = (f32[192,128]{1,0:T(8,128)S(1)}, f32[192,128]{1,0:T(8,128)S(1)}, u32[]{:S(2)}, u32[]{:S(2)}) collective-permute-start(f32[192,128]{1,0:T(8,128)S(1)} %get-tuple-element.36), channel_id=1, source_target_pairs={{0,8},{4,12},{8,0},{12,4},{16,24},{20,28},{24,16},{28,20},{1,9},{5... | collective-permute-start | bytes 294920 | tf_op jit(solution)/shard_map/ppermute | solution.py:453
  30.2 0.0 copy-done
  30.2 1.5 %maps.1 = (f32[2,256,512]{2,1,0:T(8,128)S(1)}, f32[1,128]{1,0:T(1,128)S(1)}) custom-call(s32[2,4]{1,0:T(2,128)S(1)} %copy-done.2, f32[2,512,512]{2,1,0:T(8,128)S(1)} %copy-done, f32[2,64,512]{2,1,0:T(8,128)S(1)} %copy-done.1, f32[2,64,512]{2,1,0:T(8,128)S(1)} %collective-permute-done.refs_2_.refs_3_, ...), custom_call_target="tpu_custom_call" | custom-call | flops 805306368 | bytes 4194816 | tf_op jit(solution)/shard_map/maps/pallas_call | solution.py:105
  31.7 2.8 %collective-permute-done.5.refs_2_.refs_7_ = f32[128,256]{1,0:T(8,128)S(1)} collective-permute-done((f32[128,256]{1,0:T(8,128)S(1)}, f32[128,256]{1,0:T(8,128)S(1)}, u32[]{:S(2)}, u32[]{:S(2)}) %collective-permute-start.5) | collective-permute-done | bytes 131104 | tf_op jit(solution)/shard_map/ppermute | solution.py:459
  34.5 0.0 collective-permute-start.6
  34.5 1.6 %collective-permute-done.7 = f32[192,128]{1,0:T(8,128)S(1)} collective-permute-done((f32[192,128]{1,0:T(8,128)S(1)}, f32[192,128]{1,0:T(8,128)S(1)}, u32[]{:S(2)}, u32[]{:S(2)}) %collective-permute-start.7) | collective-permute-done | bytes 98336 | tf_op jit(solution)/shard_map/ppermute | solution.py:453
  36.1 0.1 collective-permute-start.8
  36.1 1.3 %collective-permute-done.8.refs_5_.refs_10_ = f32[192,128]{1,0:T(8,128)S(1)} collective-permute-done((f32[192,128]{1,0:T(8,128)S(1)}, f32[192,128]{1,0:T(8,128)S(1)}, u32[]{:S(2)}, u32[]{:S(2)}) %collective-permute-start.8) | collective-permute-done | bytes 98336 | tf_op jit(solution)/shard_map/ppermute | solution.py:462
  37.4 0.0 collective-permute-done.6.refs_3_.refs_8_
  37.4 0.7 %merge.1 = f32[192,128]{1,0:T(8,128)S(1)} custom-call(f32[256,256]{1,0:T(8,128)S(1)} %get-tuple-element.33.refs_0_, f32[256,256]{1,0:T(8,128)S(1)} %get-tuple-element.34.refs_1_, f32[128,256]{1,0:T(8,128)S(1)} %collective-permute-done.5.refs_2_.refs_7_, f32[128,256]{1,0:T(8,128)S(1)} %collective-permute-done.6.refs_3_.refs_8_, ...), custom_call_target="tpu_custom_call" | custom-call | flops 301989888 | bytes 1081344 | tf_op jit(solution)/shard_map/merge/pallas_call | solution.py:105
  38.1 1.6 %collective-permute-start.9 = (f32[192,128]{1,0:T(8,128)S(1)}, f32[192,128]{1,0:T(8,128)S(1)}, u32[]{:S(2)}, u32[]{:S(2)}) collective-permute-start(f32[192,128]{1,0:T(8,128)S(1)} %merge.1), channel_id=1, source_target_pairs={{0,16},{4,20},{8,24},{12,28},{16,0},{20,4},{24,8},{28,12},{1,17},{... | collective-permute-start | bytes 294920 | tf_op jit(solution)/shard_map/ppermute | solution.py:453
  39.7 2.5 %prepare.1 = (bf16[2,192,256]{2,1,0:T(8,128)(2,1)S(1)}, bf16[2,192,256]{2,1,0:T(8,128)(2,1)S(1)}, bf16[2,256,512]{2,1,0:T(8,128)(2,1)S(1)}, bf16[2,256,512]{2,1,...) custom-call(f32[256,256]{1,0:T(8,128)S(1)} %get-tuple-element.30.refs_7_.refs_0_, ...), custom_call_target="tpu_custom_call" | custom-call | flops 1459617792 | bytes 7275008 | tf_op jit(solution)/shard_map/prepare/pallas_call | solution.py:105
  42.2 0.8 %collective-permute-done.9 = f32[192,128]{1,0:T(8,128)S(1)} collective-permute-done((f32[192,128]{1,0:T(8,128)S(1)}, f32[192,128]{1,0:T(8,128)S(1)}, u32[]{:S(2)}, u32[]{:S(2)}) %collective-permute-start.9) | collective-permute-done | bytes 98336 | tf_op jit(solution)/shard_map/ppermute | solution.py:453
  43.0 0.1 collective-permute-start.10
  43.1 1.3 %collective-permute-done.10.refs_2_ = f32[192,128]{1,0:T(8,128)S(1)} collective-permute-done((f32[192,128]{1,0:T(8,128)S(1)}, f32[192,128]{1,0:T(8,128)S(1)}, u32[]{:S(2)}, u32[]{:S(2)}) %collective-permute-start.10) | collective-permute-done | bytes 98336 | tf_op jit(solution)/shard_map/ppermute | solution.py:457
  44.4 2.3 %finish.1 = (f32[2,128,512]{2,1,0:T(8,128)}, f32[2,64,512]{2,1,0:T(8,128)}) custom-call(s32[2,4]{1,0:T(2,128)S(1)} %copy-done.2, f32[192,128]{1,0:T(8,128)S(1)} %broadcast_add_fusion.2.refs_1_, f32[192,128]{1,0:T(8,128)S(1)} %collective-permute-done.10.refs_2_, bf16[2,192,256]{2,1,0:T(8,128)(2,1)S(1)} %get-tuple-element.43.refs_3_, ...), custom_call_target="tpu_custom_call" | custom-call | flops 452984832 | bytes 4653056 | tf_op jit(solution)/shard_map/finish/pallas_call | solution.py:105
  (4 shorter events, 0.1 us)
Async XLA Ops:
  0.6 6.7 %copy-start.1 = (f32[2,64,512]{2,1,0:T(8,128)S(1)}, f32[2,64,512]{2,1,0:T(8,128)}, u32[]{:S(2)}) copy-start(f32[2,64,512]{2,1,0:T(8,128)} %refs_2_.3) | copy-start | bytes 786436
  0.6 11.7 %collective-permute-start = (f32[2,64,512]{2,1,0:T(8,128)}, f32[2,64,512]{2,1,0:T(8,128)S(1)}, u32[]{:S(2)}, u32[]{:S(2)}) collective-permute-start(f32[2,64,512]{2,1,0:T(8,128)} %refs_2_.3), channel_id=1, source_target_pairs={{0,1},{1,2},{2,3},{3,0},{4,5},{5,6},{6,7},{7,4},{8,9},{9,10},{10,1... | collective-permute-start | bytes 786440 | tf_op jit(solution)/shard_map/ppermute | solution.py:362
  3.7 5.8 %collective-permute-start.1 = (s32[2,4]{1,0:T(2,128)}, s32[2,4]{1,0:T(2,128)S(1)}, u32[]{:S(2)}, u32[]{:S(2)}) collective-permute-start(s32[2,4]{1,0:T(2,128)} %refs_0_.7), channel_id=1, source_target_pairs={{0,4},{4,8},{8,12},{12,16},{16,20},{20,24},{24,28},{28,0},{1,5},{5... | collective-permute-start | bytes 104 | tf_op jit(solution)/shard_map/ppermute | solution.py:362
  3.7 0.7 %copy-start.3 = (s32[2,4]{1,0:T(2,128)S(1)}, s32[2,4]{1,0:T(2,128)}, u32[]{:S(2)}) copy-start(s32[2,4]{1,0:T(2,128)} %refs_0_.7) | copy-start | bytes 100
  4.4 8.1 %copy-start.4 = (s32[2,4]{1,0:T(2,128)S(1)}, s32[2,4]{1,0:T(2,128)}, u32[]{:S(2)}) copy-start(s32[2,4]{1,0:T(2,128)} %refs_0_.7) | copy-start | bytes 100
  7.3 10.5 %copy-start.2 = (s32[2,4]{1,0:T(2,128)S(1)}, s32[2,4]{1,0:T(2,128)}, u32[]{:S(2)}) copy-start(s32[2,4]{1,0:T(2,128)} %refs_0_.11) | copy-start | bytes 100
  7.3 10.5 %collective-permute-start.3 = (f32[2,64,512]{2,1,0:T(8,128)S(1)}, f32[2,64,512]{2,1,0:T(8,128)S(1)}, u32[]{:S(2)}, u32[]{:S(2)}) collective-permute-start(f32[2,64,512]{2,1,0:T(8,128)S(1)} %broadcast_add_fusion), channel_id=1, source_target_pairs={{0,3},{1,0},{2,1},{3,2},{4,7},{5,4},{6,5},{7,6},{8,11},{9,8},{10,9... | collective-permute-start | bytes 786440 | tf_op jit(solution)/shard_map/ppermute | solution.py:362
  12.4 11.2 %collective-permute-start.2 = (f32[2,64,512]{2,1,0:T(8,128)S(1)}, f32[2,64,512]{2,1,0:T(8,128)S(1)}, u32[]{:S(2)}, u32[]{:S(2)}) collective-permute-start(f32[2,64,512]{2,1,0:T(8,128)S(1)} %broadcast_add_fusion.1), channel_id=1, source_target_pairs={{0,1},{1,2},{2,3},{3,0},{4,5},{5,6},{6,7},{7,4},{8,9},{9,10},{10,1... | collective-permute-start | bytes 786440 | tf_op jit(solution)/shard_map/ppermute | solution.py:362
  19.2 11.0 %copy-start = (f32[2,512,512]{2,1,0:T(8,128)S(1)}, f32[2,512,512]{2,1,0:T(8,128)}, u32[]{:S(2)}) copy-start(f32[2,512,512]{2,1,0:T(8,128)} %refs_1_.5) | copy-start | bytes 6291460
  25.4 2.0 %collective-permute-start.4 = (f32[512,256]{1,0:T(8,128)S(1)}, f32[512,256]{1,0:T(8,128)S(1)}, u32[]{:S(2)}, u32[]{:S(2)}) collective-permute-start(f32[512,256]{1,0:T(8,128)S(1)} %get-tuple-element.32.refs_0_), channel_id=1, source_target_pairs={{0,4},{4,0},{8,12},{12,8},{16,20},{20,16},{24,28},{28,24},{1,5},{5... | collective-permute-start | bytes 1572872 | tf_op jit(solution)/shard_map/ppermute | solution.py:419
  28.1 6.4 %collective-permute-start.5 = (f32[128,256]{1,0:T(8,128)S(1)}, f32[128,256]{1,0:T(8,128)S(1)}, u32[]{:S(2)}, u32[]{:S(2)}) collective-permute-start(f32[128,256]{1,0:T(8,128)S(1)} %get-tuple-element.35), channel_id=1, source_target_pairs={{0,8},{4,12},{8,0},{12,4},{16,24},{20,28},{24,16},{28,20},{1,9},{5... | collective-permute-start | bytes 393224 | tf_op jit(solution)/shard_map/ppermute | solution.py:459
  29.7 6.4 %collective-permute-start.7 = (f32[192,128]{1,0:T(8,128)S(1)}, f32[192,128]{1,0:T(8,128)S(1)}, u32[]{:S(2)}, u32[]{:S(2)}) collective-permute-start(f32[192,128]{1,0:T(8,128)S(1)} %get-tuple-element.36), channel_id=1, source_target_pairs={{0,8},{4,12},{8,0},{12,4},{16,24},{20,28},{24,16},{28,20},{1,9},{5... | collective-permute-start | bytes 294920 | tf_op jit(solution)/shard_map/ppermute | solution.py:453
  34.5 2.9 %collective-permute-start.6 = (f32[128,256]{1,0:T(8,128)S(1)}, f32[128,256]{1,0:T(8,128)S(1)}, u32[]{:S(2)}, u32[]{:S(2)}) collective-permute-start(f32[128,256]{1,0:T(8,128)S(1)} %collective-permute-done.5.refs_2_.refs_7_), channel_id=1, source_target_pairs={{0,4},{4,0},{8,12},{12,8},{16,20},{20,16},{24,28},{28,24},{1,5},{5... | collective-permute-start | bytes 393224 | tf_op jit(solution)/shard_map/ppermute | solution.py:462
  36.1 1.4 %collective-permute-start.8 = (f32[192,128]{1,0:T(8,128)S(1)}, f32[192,128]{1,0:T(8,128)S(1)}, u32[]{:S(2)}, u32[]{:S(2)}) collective-permute-start(f32[192,128]{1,0:T(8,128)S(1)} %broadcast_add_fusion.3.refs_4_.refs_9_), channel_id=1, source_target_pairs={{0,4},{4,0},{8,12},{12,8},{16,20},{20,16},{24,28},{28,24},{1,5},{5... | collective-permute-start | bytes 294920 | tf_op jit(solution)/shard_map/ppermute | solution.py:462
  38.1 4.9 %collective-permute-start.9 = (f32[192,128]{1,0:T(8,128)S(1)}, f32[192,128]{1,0:T(8,128)S(1)}, u32[]{:S(2)}, u32[]{:S(2)}) collective-permute-start(f32[192,128]{1,0:T(8,128)S(1)} %merge.1), channel_id=1, source_target_pairs={{0,16},{4,20},{8,24},{12,28},{16,0},{20,4},{24,8},{28,12},{1,17},{... | collective-permute-start | bytes 294920 | tf_op jit(solution)/shard_map/ppermute | solution.py:453
  43.0 1.4 %collective-permute-start.10 = (f32[192,128]{1,0:T(8,128)S(1)}, f32[192,128]{1,0:T(8,128)S(1)}, u32[]{:S(2)}, u32[]{:S(2)}) collective-permute-start(f32[192,128]{1,0:T(8,128)S(1)} %broadcast_add_fusion.2.refs_1_), channel_id=1, source_target_pairs={{0,4},{4,0},{8,12},{12,8},{16,20},{20,16},{24,28},{28,24},{1,5},{5... | collective-permute-start | bytes 294920 | tf_op jit(solution)/shard_map/ppermute | solution.py:457

commit v6 on v4

v6 whole, which is shorter than its diff:
```python
import functools

import jax
import jax.numpy as jnp
from jax import lax
from jax.experimental import pallas as pl
from jax.experimental.pallas import tpu as pltpu
from jax.sharding import PartitionSpec as P

BLOCK = 64
LANES = 128
F32 = jnp.float32
BF16 = jnp.bfloat16
NN = (((1,), (0,)), ((), ()))
NT = (((1,), (1,)), ((), ()))
TN = (((0,), (0,)), ((), ()))


def split(x):
    high = x.astype(BF16)
    return high, (x - high.astype(F32)).astype(BF16)


def mm(a, b, dims=NN):
    a = a if isinstance(a, tuple) else split(a)
    b = b if isinstance(b, tuple) else split(b)
    dot = functools.partial(lax.dot_general, dimension_numbers=dims, preferred_element_type=F32)
    return dot(a[0], b[0]) + (dot(a[0], b[1]) + dot(a[1], b[0]))


def carry(link_t, cov, base):
    link_t = link_t if isinstance(link_t, tuple) else split(link_t)
    return mm(mm(link_t, cov), link_t, NT) + base


def pack(cov):
    half = cov.shape[0] // 2
    return jnp.concatenate([cov[:half, :half], cov[:half, half:], cov[half:, half:]], 0)


def unpack(packed):
    half = packed.shape[0] // 3
    first, cross, second = packed[:half], packed[half : 2 * half], packed[2 * half :]
    top = jnp.concatenate([first, cross], 1)
    bottom = jnp.concatenate([cross.T, second], 1)
    return jnp.concatenate([top, bottom], 0)


def is_lower():
    return (lax.axis_index("seg") & 1) == 0


def from_halves(own, other):
    lower = is_lower()
    return jnp.concatenate([jnp.where(lower, own, other), jnp.where(lower, other, own)], 0)


def joined_cores(own, other, halves):
    if halves:
        return from_halves(own, other)
    seg_at = lax.axis_index("seg")
    return jnp.where(((seg_at // 2) & 1) == (seg_at & 1), own, other)


def own_half(whole):
    half = whole.shape[0] // 2
    return jnp.where(is_lower(), whole[:half], whole[half:])


def two_blocks(load, left, right):
    def placed(block, half):
        slab = load(lax.shift_right_logical(block, 1))
        return jnp.where((block & 1) == half, slab, pltpu.roll(slab, BLOCK, 1))

    a, b = placed(left, 0), placed(right, 1)
    lane = lax.broadcasted_iota(jnp.int32, a.shape, 1)
    return jnp.where(lane < BLOCK, a, b)


def tile_of(ref, *lead):
    def load(tile):
        return ref[(*lead, slice(None), pl.ds(pl.multiple_of(tile * LANES, LANES), LANES))]

    return load


def chosen_of(panel, fill_ref, prior_ref=None):
    slots = fill_ref.shape[1]
    if panel > 0:
        return [fill_ref[panel - 1, j] for j in range(slots)]
    first = lax.axis_index("seg") == 0
    last = prior_ref.shape[0] - 1
    return [jnp.where(first, fill_ref[0, j], prior_ref[last, j]) for j in range(slots)]


def vmem(count):
    return [pl.BlockSpec(memory_space=pltpu.VMEM)] * count


def smem(count):
    return [pl.BlockSpec(memory_space=pltpu.SMEM)] * count


def call(kernel, outs, scalars, arrays, far=(), through=(), scratch=(), flops=0, mib=16, name=None):
    moved = sum(a.size * 4 for a in (*arrays, *far)) + sum(o.size * 4 for o in outs)
    first = len(scalars) + len(arrays) + len(far)
    count = len(through)

    def inner(*refs):
        kernel(*refs[:first], *refs[first + count : first + count + len(outs)], *refs[first + 2 * count + len(outs) :])

    return pl.pallas_call(
        inner,
        out_shape=[*outs, *(jax.ShapeDtypeStruct(a.shape, a.dtype) for a in through)],
        in_specs=smem(len(scalars))
        + vmem(len(arrays))
        + [pl.BlockSpec(memory_space=pltpu.HBM)] * len(far)
        + [pl.BlockSpec(memory_space=pl.ANY)] * count,
        out_specs=vmem(len(outs)) + [pl.BlockSpec(memory_space=pl.ANY)] * count,
        scratch_shapes=list(scratch),
        input_output_aliases={first + i: len(outs) + i for i in range(count)},
        cost_estimate=pl.CostEstimate(flops=flops, bytes_accessed=moved, transcendentals=0),
        compiler_params=pltpu.CompilerParams(vmem_limit_bytes=mib << 20),
        name=name,
    )(*scalars, *arrays, *(pltpu.with_memory_space_constraint(a, pltpu.HBM) for a in far), *through)


def shape(*dims):
    return jax.ShapeDtypeStruct(dims, F32)


def kept_rows(mask_ref, panel, slot, rows):
    alive = lax.axis_index("seg") * mask_ref.shape[0] + panel < (
        lax.axis_size("seg") * mask_ref.shape[0] - 1
    )
    return rows * (mask_ref[panel, slot].astype(F32) * alive.astype(F32))


def triangular_mm(left, lower):
    cut = left.shape[1] // 2
    first, second = split(left[:, :cut]), split(left[:, cut:])
    below = split(lower[cut:, :])
    return jnp.concatenate(
        [
            mm(second, (below[0][:, :cut], below[1][:, :cut])) + mm(first, lower[:cut, :cut]),
            mm(second, (below[0][:, cut:], below[1][:, cut:])),
        ],
        1,
    )


def raw_kernel(factor_hbm, first_ref, upper_ref, sems):
    copies = [
        pltpu.make_async_copy(factor_hbm.at[1:], upper_ref, sems.at[0]),
        pltpu.make_async_copy(factor_hbm.at[:1], first_ref, sems.at[1]),
    ]
    for copy in copies:
        copy.start()
    for copy in copies:
        copy.wait()


def prior_kernel(panel, *refs):
    *scalar_refs, inv_hbm, factor_hbm, base_ref, own_ref, pick_high_ref, pick_low_ref = refs[:-5]
    first_ref, upper_ref, inv_ref, sem, raw_sems = refs[-5:]
    copy = pltpu.make_async_copy(inv_hbm.at[panel], inv_ref, sem)
    copy.start()
    raw_copies = (
        pltpu.make_async_copy(factor_hbm.at[1:], upper_ref, raw_sems.at[0]),
        pltpu.make_async_copy(factor_hbm.at[:1], first_ref, raw_sems.at[1]),
    )
    for raw_copy in raw_copies:
        raw_copy.start()
    chosen = chosen_of(panel, *scalar_refs)
    own_cols = own_ref.shape[0]
    own_at = pl.ds(pl.multiple_of(lax.axis_index("row") * own_cols, own_cols), own_cols)
    copy.wait()
    picked = split(
        jnp.concatenate(
            [
                two_blocks(tile_of(inv_ref), chosen[2 * t], chosen[2 * t + 1])
                for t in range(len(chosen) // 2)
            ],
            1,
        )
    )
    pick_high_ref[...], pick_low_ref[...] = picked
    base_ref[...] = mm(picked, picked, TN)
    own_ref[...] = mm(inv_ref[:, own_at], inv_ref[...], TN)
    for raw_copy in raw_copies:
        raw_copy.wait()


def put_rows(mask_ref, panel, distance, part, take):
    row_count = lax.axis_size("row")
    rows = part.shape[0]
    owner = lax.rem(lax.axis_index("row") + (row_count - distance), row_count)
    for s in range(rows // BLOCK):
        slot = owner * (rows // BLOCK) + s
        kept = kept_rows(mask_ref, panel, slot, part[s * BLOCK : (s + 1) * BLOCK, :])
        take(kept, pl.ds(pl.multiple_of(slot * BLOCK, BLOCK), BLOCK))


def links_kernel(first, distances, mask_ref, *refs):
    parts, refs = refs[: len(distances)], refs[len(distances) :]
    *pick_refs, links_t_ref, rows_ref = refs
    rows_ref[...] = jnp.zeros_like(rows_ref)
    for p in range(links_t_ref.shape[0]):
        pick = (pick_refs[2 * p][...], pick_refs[2 * p + 1][...])

        def take(kept, at):
            rows_ref[at, :] = mm(kept, pick)

        for d, part in zip(distances, parts):
            put_rows(mask_ref, first + p, d, part[p], take)
        links_t_ref[p] = rows_ref[...].T


def early_kernel(distances, mask_ref, raw_ref, *refs):
    *refs, raw_out_ref, rows_ref = refs
    raw_out_ref[...] = raw_ref[...]
    links_kernel(0, distances, mask_ref, *refs, rows_ref)


def late_kernel(distances, mask_ref, first_t_ref, *refs):
    *in_refs, _, links_t_ref, top_ref, bottom_ref, rows_ref = refs
    links_kernel(1, distances, mask_ref, *in_refs, links_t_ref, rows_ref)
    link_t = links_t_ref[links_t_ref.shape[0] - 1]
    for p in range(links_t_ref.shape[0] - 2, -1, -1):
        link_t = mm(links_t_ref[p], link_t)
    whole = mm(first_t_ref[0], link_t)
    top_ref[...] = whole[: top_ref.shape[0]]
    bottom_ref[...] = whole[top_ref.shape[0] :]


def segment_kernel(distance, panels, mask_ref, *refs):
    first_part, first_early, upper_part, upper_early = refs[:4]
    pick_refs, base_refs = refs[4 : 4 + 2 * panels], refs[4 + 2 * panels : 4 + 3 * panels]
    first_t_ref, upper_t_ref, whole_ref = refs[4 + 3 * panels :]
    size = base_refs[0].shape[0]
    lane = lax.broadcasted_iota(jnp.int32, (size, size), 1) // BLOCK
    cov = link_t = None
    for p in range(panels - 1, -1, -1):
        pick = (pick_refs[2 * p][...], pick_refs[2 * p + 1][...])
        part, early = (upper_part[p - 1], upper_early[p - 1]) if p else (first_part[0], first_early[0])
        pieces = [early]

        def take(kept, at):
            late = jnp.concatenate([mm(kept, pick)] * (size // BLOCK), 0).T
            pieces.append(jnp.where(lane == at.start // BLOCK, late, pieces[-1]))

        put_rows(mask_ref, p, distance, part, take)
        own_t = pieces[-1]
        if p:
            upper_t_ref[p - 1] = own_t
        else:
            first_t_ref[0] = own_t
        if cov is None:
            cov, link_t = base_refs[p][...], own_t
        else:
            own_t = split(own_t)
            cov = carry(own_t, cov, base_refs[p][...])
            link_t = mm(own_t, link_t)
    whole_ref[:size] = link_t
    whole_ref[size:] = cov


def maps_kernel(row_count, mask_ref, inv_ref, *refs):
    firsts, lowers, uppers = (refs[i * row_count : (i + 1) * row_count] for i in range(3))
    maps_ref, rows_ref = refs[3 * row_count :]
    lower = is_lower()

    def take(kept, at):
        rows_ref[at, :] = kept

    for p in range(inv_ref.shape[0]):
        for d in range(row_count):
            part = jnp.where(lower, lowers[d][p - 1], uppers[d][p - 1]) if p else firsts[d][0]
            put_rows(mask_ref, p, d, part, take)
        maps_ref[p] = triangular_mm(rows_ref[...], inv_ref[p])


def chip_kernel(own_ref, other_ref, cov_ref, packed_ref):
    size = cov_ref.shape[0]
    lower = is_lower()
    own, other = own_ref[...], other_ref[...]
    down_t = jnp.where(lower, own[:size], other[:size])
    up = jnp.where(lower, other[size:], own[size:])
    cov = carry(down_t, up, jnp.where(lower, own[size:], other[size:]))
    cov_ref[...] = cov
    packed_ref[...] = own_half(pack(cov))


def chip_link_kernel(own_ref, other_ref, *refs):
    link_t_ref, half_t_ref = refs[5:]
    size = link_t_ref.shape[0]
    lower = is_lower()
    down_t = jnp.where(lower, own_ref[:size, :], other_ref[:size, :])
    late_t, other_late_t = (jnp.concatenate([a[...], b[...]], 0) for a, b in (refs[:2], refs[2:4]))
    link_t = mm(down_t, jnp.where(lower, other_late_t, late_t))
    link_t_ref[...] = link_t
    half_t_ref[...] = own_half(link_t)


def extend_kernel(link_t_ref, cov_ref, own_ref, other_ref, packed_ref):
    after = unpack(from_halves(own_ref[...], other_ref[...]))
    packed_ref[...] = pack(carry(link_t_ref[...], after, cov_ref[...]))


def extend_link_kernel(link_t_ref, own_t_ref, other_t_ref, out_ref):
    out_ref[...] = mm(link_t_ref[...], from_halves(own_t_ref[...], other_t_ref[...]))


def join_kernel(level, *refs):
    past_t, past, link_t, cov = (
        joined_cores(refs[2 * i][...], refs[2 * i + 1][...], i < 2) for i in range(4)
    )
    chip = lax.axis_index("seg") // 2
    below = (lax.shift_right_logical(chip, level) & 1) == 0
    known = (chip & ((1 << level) - 1)) != (1 << level) - 1
    past_parts = split(past_t)
    joined = pack(carry(past_parts, unpack(cov), unpack(past)))
    joined_t = mm(past_parts, link_t)
    out_t = jnp.where(below, jnp.where(known, joined_t, link_t), past_t)
    out = jnp.where(below, jnp.where(known, joined, cov), past)
    for ref, whole in zip(refs[8:], (out_t, out_t, out, out)):
        ref[...] = own_half(whole)
    for ref, whole in ((refs[9], out_t), (refs[11], out)):
        half = whole.shape[0] // 2
        ref[...] = jnp.where(is_lower(), whole[half:], whole[:half])


def prepare_kernel(panels, *refs):
    base_refs, own_refs, refs = refs[:panels], refs[panels : 2 * panels], refs[2 * panels :]
    (other_ref, top_ref, bottom_ref, maps_ref, lower_t_ref, upper_t_ref), refs = refs[:6], refs[6:]
    left_high, left_low, right_high, right_low, const_ref, token_ref, scratch = refs
    token_ref[...] = jnp.zeros_like(token_ref)
    own_cols = own_refs[0].shape[0]
    size = base_refs[0].shape[0]
    row_at = lax.axis_index("row")
    rows = left_high.shape[1] - own_cols
    at_row = lax.broadcasted_iota(jnp.int32, (size, size), 0)
    at_col = lax.broadcasted_iota(jnp.int32, (size, size), 1)
    eye = (at_row == at_col).astype(F32)
    lower = is_lower()
    to_t = jnp.where(lower, jnp.concatenate([top_ref[...], bottom_ref[...]], 0), eye)
    gain = jnp.where(lower, other_ref[size:, :], 0.0)
    own_at = pl.ds(pl.multiple_of(row_at * own_cols, own_cols), own_cols)
    own_rows = pl.ds(pl.multiple_of(row_at * rows, rows), rows)
    for p in range(panels - 1, -1, -1):
        whole = split(maps_ref[p])
        own_t = split(maps_ref[p, :, own_at].T)
        scratch[:, :size] = to_t
        scratch[:, size:] = gain
        to_parts = split(to_t)
        left = jnp.concatenate([scratch[own_rows, :size], mm(own_t, to_parts)], 0)
        left_high[p], left_low[p] = split(left)
        right_high[p], right_low[p] = split(mm(to_parts, whole, TN))
        gains = jnp.concatenate([scratch[own_rows, size:], mm(own_t, gain)], 0)
        const = mm(gains, whole)
        const_ref[p, :rows, :] = const[:rows]
        const_ref[p, rows:, :] = const[rows:] + own_refs[p][...]
        if p > 0:
            link_t = split(jnp.where(lower, lower_t_ref[p - 1], upper_t_ref[p - 1]))
            to_t = mm(link_t, to_t)
            gain = carry(link_t, gain, base_refs[p][...])


def finish_kernel(levels, mask_ref, after_ref, after_other_ref, *refs):
    past_refs, refs = refs[: 4 * (levels > 1)], refs[4 * (levels > 1) :]
    left_high, left_low, right_high, right_low, const_ref, diag_ref, off_ref = refs
    rows = off_ref.shape[1]
    row_at = lax.axis_index("row")
    chip = lax.axis_index("seg") // 2
    after = joined_cores(after_ref[...], after_other_ref[...], levels < 2)
    top = (1 << levels) // 2
    after = unpack(jnp.where((chip & top) == 0, after, 0.0))
    if past_refs:
        past_t = from_halves(past_refs[0][...], past_refs[1][...])
        past = unpack(from_halves(past_refs[2][...], past_refs[3][...]))
        after = jnp.where((chip & (top - 1)) != top - 1, carry(past_t, after, past), after)
    after = split(after)
    for p in range(const_ref.shape[0]):
        left = (left_high[p], left_low[p])
        right = (right_high[p], right_low[p])
        result = mm(mm(left, after), right) + const_ref[p]
        diag_ref[p] = result[rows:]
        for s in range(rows // BLOCK):
            keep = mask_ref[p, row_at * (rows // BLOCK) + s].astype(F32)
            off_ref[p, s * BLOCK : (s + 1) * BLOCK, :] = -result[s * BLOCK : (s + 1) * BLOCK] * keep


def body(fill_blocks, fill_mask, inv_diag, factor_off):
    panels, width, _ = inv_diag.shape
    rows = factor_off.shape[1]
    seg_count = lax.axis_size("seg")
    row_count = lax.axis_size("row")
    size = rows * row_count
    own_cols = width // row_count
    slots = fill_blocks.shape[1]
    chosen_cols = slots * BLOCK
    chips = seg_count // 2
    half_cols = size // 2

    def turn_seg(x):
        return lax.ppermute(x, "seg", [(i, (i + 1) % seg_count) for i in range(seg_count)])

    def turn(x, distance, core=None):
        route = []
        for i in range(seg_count):
            for j in range(row_count):
                moves = distance if core is None or i % 2 == core else 0
                route.append((i * row_count + j, i * row_count + (j + moves) % row_count))
        return lax.ppermute(x, ("seg", "row"), route)

    def gather(x, x_down, core, gate):
        ups, downs = [x, turn(x, 1, core)], [x_down]
        for _ in range(1, row_count // 2):
            ups.append(turn(ups[-1] + gate, 1, core))
        for _ in range((row_count - 1) // 2):
            downs.append(turn(downs[-1], -1, core))
        return ups + downs[:0:-1]

    prior_fill = turn_seg(fill_blocks)
    pick = jax.ShapeDtypeStruct((width, chosen_cols), BF16)
    raw_shapes = [shape(1, rows, width), shape(panels - 1, rows, width)]
    bases, priors, picks, raws = [], [], [], []
    for p in range(panels):
        base, own_prior, *high_low, raw_first, raw_upper = call(
            functools.partial(prior_kernel, p),
            [shape(chosen_cols, chosen_cols), shape(own_cols, width), pick, pick, *raw_shapes],
            [fill_blocks] if p else [fill_blocks, prior_fill],
            [],
            far=[inv_diag, factor_off],
            scratch=[
                pltpu.VMEM((width, width), F32),
                pltpu.SemaphoreType.DMA,
                pltpu.SemaphoreType.DMA((2,)),
            ],
            flops=6 * width * (chosen_cols * chosen_cols + own_cols * width),
            name="prior",
        )
        bases.append(base)
        priors.append(own_prior)
        picks += high_low
        raws.append((raw_first, raw_upper))
    index_gate = jnp.minimum(jnp.min(prior_fill), 0).astype(F32)
    raw_first, raw_upper = call(
        raw_kernel,
        raw_shapes,
        [],
        [],
        far=[factor_off],
        scratch=[pltpu.SemaphoreType.DMA((2,))],
        name="raw",
    )
    firsts = gather(raw_first, raws[-1][0], None, index_gate)
    lowers = gather(raw_upper, raws[-1][1], 0, index_gate)
    last = row_count // 2
    early = [d for d in range(row_count) if d != last]
    first_early, raw_late = call(
        functools.partial(early_kernel, early),
        [shape(1, size, size), raw_shapes[1]],
        [fill_mask],
        [raws[-1][1], *(firsts[d] for d in early), *picks[:2]],
        scratch=[pltpu.VMEM((size, chosen_cols), F32)],
        flops=6 * size * size * width,
        name="early",
    )
    uppers = gather(raw_late, raw_late, 1, index_gate)
    (upper_early,) = call(
        functools.partial(links_kernel, 1, early),
        [shape(panels - 1, size, size)],
        [fill_mask],
        [*(lowers[d] for d in early), *picks[2:]],
        scratch=[pltpu.VMEM((size, chosen_cols), F32)],
        flops=6 * (panels - 1) * size * size * width,
        name="links",
    )
    first_t, lower_t, own_whole = call(
        functools.partial(segment_kernel, last, panels),
        [shape(1, size, size), shape(panels - 1, size, size), shape(2 * size, size)],
        [fill_mask],
        [firsts[last], first_early, lowers[last], upper_early, *picks, *bases],
        flops=6 * panels * rows * size * width + 18 * (panels - 1) * size**3,
        name="segment",
    )
    (maps,) = call(
        functools.partial(maps_kernel, row_count),
        [shape(panels, size, width)],
        [fill_mask],
        [inv_diag, *firsts, *lowers, *uppers],
        scratch=[pltpu.VMEM((size, width), F32)],
        flops=6 * panels * size * width * width,
        mib=24,
        name="maps",
    )
    swap = [(i, i ^ 1) for i in range(seg_count)]
    late_gate = uppers[1][0, :1, :size] * 0.0
    other_whole = lax.ppermute(own_whole + late_gate, "seg", swap)
    half = size // 2
    half_packed = shape(3 * half // 2, half)
    half_link = shape(half, size)
    cov, send = call(
        chip_kernel, [shape(size, size), half_packed], [], [own_whole, other_whole],
        flops=12 * size**3, name="chip",
    )
    upper_t, *own_late = call(
        functools.partial(late_kernel, list(range(row_count))),
        [shape(panels - 1, size, size), half_link, half_link],
        [fill_mask],
        [first_t, *uppers, *picks[2:], send],
        scratch=[pltpu.VMEM((size, chosen_cols), F32)],
        flops=6 * (panels - 1) * size * size * width + 6 * (panels - 1) * size**3,
        name="late",
    )
    other_late = [lax.ppermute(x, "seg", swap) for x in own_late]
    past = None
    after = (jnp.zeros(half_packed.shape, F32),) * 2
    levels = (chips - 1).bit_length()
    prepared = None

    def prepare():
        total = rows + own_cols
        left = jax.ShapeDtypeStruct((panels, total, size), BF16)
        right = jax.ShapeDtypeStruct((panels, size, width), BF16)
        return call(
            functools.partial(prepare_kernel, panels),
            [left, left, right, right, shape(panels, total, width), shape(1, half_cols)],
            [],
            [*bases, *priors, other_whole, *other_late, maps, lower_t, upper_t],
            scratch=[pltpu.VMEM((size, width), F32)],
            flops=6 * panels * size * (total * size + size * width + total * width + 3 * size * size),
            mib=24,
            name="prepare",
        )

    for level in range(levels):
        bit = 1 << level
        if level > 0:
            (send,) = call(
                extend_kernel, [shape(3 * half, half)], [], [link_t, cov, *past[2:]],
                flops=12 * size**3, name="extend",
            )
            if level < levels - 1:
                (send_t,) = call(
                    extend_link_kernel, [shape(size, size)], [], [link_t, *past[:2]],
                    flops=6 * size**3, name="extend_link",
                )
        got = got_t = None
        for step in range(max(bit // 2, 1)):
            route = list(range(seg_count))
            for base_chip in range(0, chips, 2 * bit):
                for core in range(2):
                    upper_at = 2 * (base_chip + bit) + core
                    lower_at = 2 * (base_chip + (2 * step + core) % bit) + core
                    route[upper_at], route[lower_at] = lower_at, upper_at
            route = list(enumerate(route))
            here = ((lax.axis_index("seg") // 2) & (bit - 1)) // 2 == step
            piece = lax.ppermute(send, "seg", route)
            got = piece if step == 0 else jnp.where(here, piece, got)
            if level == 0 and levels > 1:
                link_t, send_t = call(
                    chip_link_kernel, [shape(size, size), half_link], [],
                    [own_whole, other_whole, *own_late, *other_late, piece],
                    flops=6 * size**3, name="chip_link",
                )
            if level < levels - 1:
                piece_t = lax.ppermute(send_t, "seg", route)
                got_t = piece_t if step == 0 else jnp.where(here, piece_t, got_t)
        if level == levels - 1:
            *prepared, token = prepare()
            got = got + token
            after = (got, lax.ppermute(got, "seg", swap))
            break
        got = (got_t, lax.ppermute(got_t, "seg", swap), got, lax.ppermute(got, "seg", swap))
        if past is None:
            past = got
        else:
            past = call(
                functools.partial(join_kernel, level),
                [half_link, half_link, half_packed, half_packed],
                [],
                [*past, *got],
                flops=18 * size**3,
                name="join",
            )
    if prepared is None:
        *prepared, _ = prepare()
    diag, off = call(
        functools.partial(finish_kernel, levels),
        [shape(panels, own_cols, width), shape(panels, rows, width)],
        [fill_mask],
        [*after, *(past or ()), *prepared],
        flops=6 * panels * (rows + own_cols) * size * (size + width),
        name="finish",
    )
    return diag, off


def solution(mesh):
    placed = (P("seg", None), P("seg", None), P("seg", None, None), P("seg", "row", None))
    return jax.shard_map(
        body,
        mesh=mesh,
        in_specs=placed,
        out_specs=(P("seg", "row", None), P("seg", "row", None)),
        check_vma=False,
    )
```

time: 47.5 us -> 66.4 us (1.40)
  starting transfers between devices: 9.12 us -> 30.3 us
  waiting for transfers between devices: 17.8 us -> 11.6 us
  Pallas kernels: 16.6 us -> 21.1 us
    ppermute x8 -> x16, starting transfers between devices: 8.97 us -> 29.8 us  [the longest x9 16.8 us: turn(): return lax.ppermute(x, ('seg', 'row'), route)]
    ppermute x8 -> x16, waiting for transfers between devices: 15.3 us -> 10.2 us  [the longest x9 5.5 us: turn(): return lax.ppermute(x, ('seg', 'row'), route)]
    pallas_call x9 -> x13, Pallas kernels: 16.6 us -> 21.1 us  [call(): pl.pallas_call(inner, out_shape=[*outs, *(jax.ShapeDtypeStruct(a.shape, a...]
    ppermute x1, waiting for transfers between devices: 0.01 us -> 1.35 us  [body(): lax.ppermute(got_t, 'seg', swap)]
    ppermute x1, waiting for transfers between devices: 1.29 us -> 0.01 us  [body(): after = (got, lax.ppermute(got, 'seg', swap))]
    ppermute x1, waiting for transfers between devices: 1.29 us -> 0.01 us  [body(): lax.ppermute(got, 'seg', swap)]
    add x2 -> x4, other arithmetic: 0.98 us -> 0.08 us  [the longest x3 0.04 us: gather(): ups.append(turn(ups[-1] + gate, 1, core))]
  transfers between devices with their start and end apart: 11 -> 19, of which waited for: 10 -> 8; matrix products, arithmetic and copies ran while one was open for 3% -> 1% of each run, Pallas kernels for 24% -> 23%
where the time goes in v6:
time: 66.4 us; the launch traced here: 66.1 us
  starting transfers between devices  30.3 us (46%)
  Pallas kernels  21.1 us (32%)
  waiting for transfers between devices  11.6 us (17%)
  between operations  1.62 us (2%)
  other arithmetic  0.73 us (1%)
  local copies, waits for them, and re-layouts  0.7 us (1%)
    pallas_call x13, Pallas kernels, call(): pl.pallas_call(inner, out_shape=[*outs, *(jax.ShapeDtypeStruct(a.shape, a...  21.1 us
    ppermute x9, starting transfers between devices, turn(): return lax.ppermute(x, ('seg', 'row'), route)  16.8 us
    ppermute x2, starting transfers between devices, body(): other_late = [lax.ppermute(x, 'seg', swap) for x in own_late]  7.55 us
    ppermute x9, waiting for transfers between devices, turn(): return lax.ppermute(x, ('seg', 'row'), route)  5.5 us
    ppermute x2, starting transfers between devices, body(): piece = lax.ppermute(send, 'seg', route)  5.29 us
    ppermute x1, waiting for transfers between devices, body(): piece_t = lax.ppermute(send_t, 'seg', route)  1.79 us
    ppermute x2, waiting for transfers between devices, body(): piece = lax.ppermute(send, 'seg', route)  1.58 us
    ppermute x1, waiting for transfers between devices, body(): lax.ppermute(got_t, 'seg', swap)  1.35 us
  transfers between devices with their start and end apart: 19, of which 8 were waited for; matrix products, arithmetic and copies ran while one was open for 1% of the time, Pallas kernels for 23%

profile of v6, /device:TPU:0, one launch (start us, length us, event | category | flops | bytes accessed | tf_op | source)
XLA Modules:
  0.0 66.1 jit_solution(3663680230701292657)
XLA Ops:
  0.6 0.0 copy-start.3
  0.6 1.0 %raw.1 = (f32[1,64,512]{2,1,0:T(8,128)S(1)}, f32[1,64,512]{2,1,0:T(8,128)S(1)}) custom-call(f32[2,64,512]{2,1,0:T(8,128)} %refs_3_.1), custom_call_target="tpu_custom_call" | custom-call | bytes 524288 | tf_op jit(solution)/shard_map/raw/pallas_call | solution.py:112
  1.6 0.0 copy-start.1
  1.7 3.1 %collective-permute-start = (f32[1,64,512]{2,1,0:T(8,128)S(1)}, f32[1,64,512]{2,1,0:T(8,128)S(1)}, u32[]{:S(2)}, u32[]{:S(2)}) collective-permute-start(f32[1,64,512]{2,1,0:T(8,128)S(1)} %get-tuple-element.32.refs_2_), channel_id=1, source_target_pairs={{0,1},{1,2},{2,3},{3,0},{4,5},{5,6},{6,7},{7,4},{8,9},{9,10},{10,1... | collective-permute-start | bytes 393224 | tf_op jit(solution)/shard_map/ppermute | solution.py:414
  4.7 0.0 collective-permute-start.1
  4.7 0.0 copy-start.2
  4.7 0.7 %copy-done.2 = s32[2,4]{1,0:T(2,128)S(1)} copy-done((s32[2,4]{1,0:T(2,128)S(1)}, s32[2,4]{1,0:T(2,128)}, u32[]{:S(2)}) %copy-start.2) | copy-done | bytes 56
  5.4 2.9 %prior.2 = (f32[256,256]{1,0:T(8,128)S(1)}, f32[128,512]{1,0:T(8,128)S(1)}, bf16[512,256]{1,0:T(8,128)(2,1)S(1)}, bf16[512,256]{1,0:T(8,128)(2,1)S(1)}, f32[1,64...) custom-call(s32[2,4]{1,0:T(2,128)S(1)} %copy-done.2, f32[2,512,512]{2,1,0:T(8,128)} %refs_1_.3, f32[2,64,512]{2,1,0:T(8,128)} %refs_3_.1), custom_call_target="tpu_custom_call" | custom-call | flops 402653184 | bytes 4194304 | tf_op jit(solution)/shard_map/prior/pallas_call | solution.py:112
  8.3 2.2 %collective-permute-start.3 = (f32[1,64,512]{2,1,0:T(8,128)S(1)}, f32[1,64,512]{2,1,0:T(8,128)S(1)}, u32[]{:S(2)}, u32[]{:S(2)}) collective-permute-start(f32[1,64,512]{2,1,0:T(8,128)S(1)} %get-tuple-element.34), channel_id=1, source_target_pairs={{0,3},{1,0},{2,1},{3,2},{4,7},{5,4},{6,5},{7,6},{8,11},{9,8},{10,9... | collective-permute-start | bytes 393224 | tf_op jit(solution)/shard_map/ppermute | solution.py:414
  10.4 1.9 %collective-permute-start.4 = (f32[1,64,512]{2,1,0:T(8,128)S(1)}, f32[1,64,512]{2,1,0:T(8,128)S(1)}, u32[]{:S(2)}, u32[]{:S(2)}) collective-permute-start(f32[1,64,512]{2,1,0:T(8,128)S(1)} %get-tuple-element.38.refs_1_.refs_6_), channel_id=1, source_target_pairs={{0,1},{1,2},{2,3},{3,0},{4,4},{5,5},{6,6},{7,7},{8,9},{9,10},{10,1... | collective-permute-start | bytes 393224 | tf_op jit(solution)/shard_map/ppermute | solution.py:414
  12.3 5.7 %collective-permute-start.6 = (f32[1,64,512]{2,1,0:T(8,128)S(1)}, f32[1,64,512]{2,1,0:T(8,128)S(1)}, u32[]{:S(2)}, u32[]{:S(2)}) collective-permute-start(f32[1,64,512]{2,1,0:T(8,128)S(1)} %get-tuple-element.33.refs_1_), channel_id=1, source_target_pairs={{0,3},{1,0},{2,1},{3,2},{4,4},{5,5},{6,6},{7,7},{8,11},{9,8},{10,9... | collective-permute-start | bytes 393224 | tf_op jit(solution)/shard_map/ppermute | solution.py:414
  18.1 0.0 collective-permute-done.1.refs_1_
  18.1 0.6 reduce_min.9
  19.4 0.0 copy-done.3
  19.4 3.6 %prior.3 = (f32[256,256]{1,0:T(8,128)S(1)}, f32[128,512]{1,0:T(8,128)S(1)}, bf16[512,256]{1,0:T(8,128)(2,1)S(1)}, bf16[512,256]{1,0:T(8,128)(2,1)S(1)}, f32[1,64,512]{2,1,0:T(8,128)}, /*index=5*/f32[1,64,512]{2,1,0:T(8,128)}) custom-call(s32[2,4]{1,0:T(2,128)S(1)} %copy-done.3, s32[2,4]{1,0:T(2,128)S(1)} %collective-permute-done.1.refs_1_, ...), custom_call_target="tpu_custom_call" | custom-call | flops 402653184 | bytes 4194304 | tf_op jit(solution)/shard_map/prior/pallas_call | solution.py:112
  23.0 0.0 collective-permute-done.refs_3_
  23.0 0.1 collective-permute-start.2
  23.1 0.0 collective-permute-done.3.refs_4_.refs_5_
  23.1 0.0 copy-done.1
  23.1 1.2 %early.1 = (f32[1,256,256]{2,1,0:T(8,128)S(1)}, f32[1,64,512]{2,1,0:T(8,128)S(1)}) custom-call(s32[2,4]{1,0:T(2,128)S(1)} %copy-done.1, f32[1,64,512]{2,1,0:T(8,128)S(1)} %get-tuple-element.33.refs_1_, f32[1,64,512]{2,1,0:T(8,128)S(1)} %get-tuple-element.32.refs_2_, f32[1,64,512]{2,1,0:T(8,128)S(1)} %collective-permute-done.refs_3_, ...), custom_call_target="tpu_custom_call" | custom-call | flops 201326592 | bytes 1966080 | tf_op jit(solution)/shard_map/early/pallas_call | solution.py:112
  24.3 0.7 %collective-permute-start.7 = (f32[1,64,512]{2,1,0:T(8,128)S(1)}, f32[1,64,512]{2,1,0:T(8,128)S(1)}, u32[]{:S(2)}, u32[]{:S(2)}) collective-permute-start(f32[1,64,512]{2,1,0:T(8,128)S(1)} %get-tuple-element.44.refs_2_.refs_10_), channel_id=1, source_target_pairs={{0,0},{1,1},{2,2},{3,3},{4,5},{5,6},{6,7},{7,4},{8,8},{9,9},{10,10... | collective-permute-start | bytes 393224 | tf_op jit(solution)/shard_map/ppermute | solution.py:414
  25.0 0.0 collective-permute-done.4.refs_2_.refs_7_
  25.0 1.9 %collective-permute-start.5 = (f32[1,64,512]{2,1,0:T(8,128)S(1)}, f32[1,64,512]{2,1,0:T(8,128)S(1)}, u32[]{:S(2)}, u32[]{:S(2)}) collective-permute-start(f32[1,64,512]{2,1,0:T(8,128)S(1)} %broadcast_add_fusion.3), channel_id=1, source_target_pairs={{0,1},{1,2},{2,3},{3,0},{4,4},{5,5},{6,6},{7,7},{8,9},{9,10},{10,1... | collective-permute-start | bytes 393224 | tf_op jit(solution)/shard_map/ppermute | solution.py:414
  26.9 0.0 collective-permute-done.6.refs_3_.refs_9_
  27.0 1.2 %links.1.refs_4_ = f32[1,256,256]{2,1,0:T(8,128)S(1)} custom-call(s32[2,4]{1,0:T(2,128)S(1)} %copy-done.1, f32[1,64,512]{2,1,0:T(8,128)S(1)} %get-tuple-element.38.refs_1_.refs_6_, f32[1,64,512]{2,1,0:T(8,128)S(1)} %collective-permute-done.4.refs_2_.refs_7_, f32[1,64,512]{2,1,0:T(8,128)S(1)} %collective-permute-done.6.refs_3_.refs_9_, ...), custom_call_target="tpu_custom_call" | custom-call | flops 201326592 | bytes 1703936 | tf_op jit(solution)/shard_map/links/pallas_call | solution.py:112
  28.2 0.0 collective-permute-done.7.refs_3_.refs_11_
  28.2 1.6 %collective-permute-done.2.refs_1_.refs_4_ = f32[1,64,512]{2,1,0:T(8,128)S(1)} collective-permute-done((f32[1,64,512]{2,1,0:T(8,128)S(1)}, f32[1,64,512]{2,1,0:T(8,128)S(1)}, u32[]{:S(2)}, u32[]{:S(2)}) %collective-permute-start.2) | collective-permute-done | bytes 131104 | tf_op jit(solution)/shard_map/ppermute | solution.py:414
  29.8 3.9 %collective-permute-done.5.refs_3_.refs_8_ = f32[1,64,512]{2,1,0:T(8,128)S(1)} collective-permute-done((f32[1,64,512]{2,1,0:T(8,128)S(1)}, f32[1,64,512]{2,1,0:T(8,128)S(1)}, u32[]{:S(2)}, u32[]{:S(2)}) %collective-permute-start.5) | collective-permute-done | bytes 131104 | tf_op jit(solution)/shard_map/ppermute | solution.py:414
  33.7 1.6 %segment.1 = (f32[1,256,256]{2,1,0:T(8,128)S(1)}, f32[1,256,256]{2,1,0:T(8,128)S(1)}, f32[512,256]{1,0:T(8,128)S(1)}) custom-call(s32[2,4]{1,0:T(2,128)S(1)} %copy-done.1, f32[1,64,512]{2,1,0:T(8,128)S(1)} %collective-permute-done.2.refs_1_.refs_4_, f32[1,256,256]{2,1,0:T(8,128)S(1)} %get-tuple-element.37.refs_2_, ...), custom_call_target="tpu_custom_call" | custom-call | flops 402653184 | bytes 4456448 | tf_op jit(solution)/shard_map/segment/pallas_call | solution.py:112
  35.3 0.1 collective-permute-start.8
  35.4 0.7 %collective-permute-start.10 = (f32[1,64,512]{2,1,0:T(8,128)S(1)}, f32[1,64,512]{2,1,0:T(8,128)S(1)}, u32[]{:S(2)}, u32[]{:S(2)}) collective-permute-start(f32[1,64,512]{2,1,0:T(8,128)S(1)} %get-tuple-element.44.refs_2_.refs_10_), channel_id=1, source_target_pairs={{0,0},{1,1},{2,2},{3,3},{4,7},{5,4},{6,5},{7,6},{8,8},{9,9},{10,10... | collective-permute-start | bytes 393224 | tf_op jit(solution)/shard_map/ppermute | solution.py:414
  36.1 0.7 %collective-permute-start.9 = (f32[1,64,512]{2,1,0:T(8,128)S(1)}, f32[1,64,512]{2,1,0:T(8,128)S(1)}, u32[]{:S(2)}, u32[]{:S(2)}) collective-permute-start(f32[1,64,512]{2,1,0:T(8,128)S(1)} %broadcast_add_fusion.2), channel_id=1, source_target_pairs={{0,0},{1,1},{2,2},{3,3},{4,5},{5,6},{6,7},{7,4},{8,8},{9,9},{10,10... | collective-permute-start | bytes 393224 | tf_op jit(solution)/shard_map/ppermute | solution.py:414
  36.8 0.5 collective-permute-done.8.refs_1_.refs_4_
  37.3 0.6 chip.1
  37.9 0.0 copy-start
  37.9 1.7 %collective-permute-start.13 = (f32[192,128]{1,0:T(8,128)S(1)}, f32[192,128]{1,0:T(8,128)S(1)}, u32[]{:S(2)}, u32[]{:S(2)}) collective-permute-start(f32[192,128]{1,0:T(8,128)S(1)} %get-tuple-element.46.refs_8_), channel_id=1, source_target_pairs={{0,8},{4,12},{8,0},{12,4},{16,24},{20,28},{24,16},{28,20},{1,9},{5... | collective-permute-start | bytes 294920 | tf_op jit(solution)/shard_map/ppermute | solution.py:560
  39.6 0.0 collective-permute-done.10.refs_5_.refs_13_
  39.6 0.0 collective-permute-done.9.refs_4_.refs_12_
  39.6 1.7 %late.1 = (f32[1,256,256]{2,1,0:T(8,128)S(1)}, f32[128,256]{1,0:T(8,128)S(1)}, f32[128,256]{1,0:T(8,128)S(1)}) custom-call(s32[2,4]{1,0:T(2,128)S(1)} %copy-done.1, f32[1,256,256]{2,1,0:T(8,128)S(1)} %get-tuple-element.45.refs_1_, f32[1,64,512]{2,1,0:T(8,128)S(1)} %get-tuple-element.44.refs_2_.refs_10_, ...), custom_call_target="tpu_custom_call" | custom-call | flops 301989888 | bytes 2457600 | tf_op jit(solution)/shard_map/late/pallas_call | solution.py:112
  41.3 7.5 %collective-permute-start.11 = (f32[128,256]{1,0:T(8,128)S(1)}, f32[128,256]{1,0:T(8,128)S(1)}, u32[]{:S(2)}, u32[]{:S(2)}) collective-permute-start(f32[128,256]{1,0:T(8,128)S(1)} %get-tuple-element.47.refs_2_), channel_id=1, source_target_pairs={{0,4},{4,0},{8,12},{12,8},{16,20},{20,16},{24,28},{28,24},{1,5},{5... | collective-permute-start | bytes 393224 | tf_op jit(solution)/shard_map/ppermute | solution.py:517
  48.8 0.1 collective-permute-start.12
  48.8 0.0 collective-permute-done.13.refs_6_.refs_2_.refs_5_
  48.8 0.4 collective-permute-start.14
  49.3 0.5 collective-permute-done.11.refs_4_.refs_5_
  49.7 0.4 collective-permute-done.12.refs_5_.refs_6_
  50.1 0.3 chip_link.1
  50.4 0.0 collective-permute-done.14.refs_3_.refs_6_
  50.4 0.7 %extend.1 = f32[384,128]{1,0:T(8,128)S(1)} custom-call(f32[256,256]{1,0:T(8,128)S(1)} %get-tuple-element.49.refs_0_, f32[256,256]{1,0:T(8,128)S(1)} %get-tuple-element.50.refs_1_, f32[192,128]{1,0:T(8,128)S(1)} %collective-permute-done.13.refs_6_.refs_2_.refs_5_, f32[192,128]{1,0:T(8,128)S(1)} %collective-permute-done.14.refs_3_.refs_6_), custom_call_target="tpu_custom_call" | custom-call | flops 201326592 | bytes 917504 | tf_op jit(solution)/shard_map/extend/pallas_call | solution.py:112
  51.1 3.6 %collective-permute-start.15 = (f32[384,128]{1,0:T(8,128)S(1)}, f32[384,128]{1,0:T(8,128)S(1)}, u32[]{:S(2)}, u32[]{:S(2)}) collective-permute-start(f32[384,128]{1,0:T(8,128)S(1)} %extend.1), channel_id=1, source_target_pairs={{0,16},{4,4},{8,8},{12,20},{16,0},{20,12},{24,24},{28,28},{1,17},{... | collective-permute-start | bytes 589832 | tf_op jit(solution)/shard_map/ppermute | solution.py:560
  54.7 0.0 copy-done
  54.7 1.5 %maps.1.refs_7_ = f32[2,256,512]{2,1,0:T(8,128)S(1)} custom-call(s32[2,4]{1,0:T(2,128)S(1)} %copy-done.1, f32[2,512,512]{2,1,0:T(8,128)S(1)} %copy-done, f32[1,64,512]{2,1,0:T(8,128)S(1)} %get-tuple-element.32.refs_2_, f32[1,64,512]{2,1,0:T(8,128)S(1)} %collective-permute-done.refs_3_, f32[1,64,512]{2,1,0:T(8,128)S(1)} %collective-permute-done.2.refs_1_.refs_4_, ...), custom_call_target="tpu_custom_call" | custom-call | flops 805306368 | bytes 4718592 | tf_op jit(solution)/shard_map/maps/pallas_call | solution.py:112
  56.2 0.1 collective-permute-start.17
  56.3 2.1 %prepare.1 = (bf16[2,192,256]{2,1,0:T(8,128)(2,1)S(1)}, bf16[2,192,256]{2,1,0:T(8,128)(2,1)S(1)}, bf16[2,256,512]{2,1,0:T(8,128)(2,1)S(1)}, bf16[2,256,512]{2,1,...) custom-call(f32[256,256]{1,0:T(8,128)S(1)} %get-tuple-element.41.refs_9_.refs_0_, ...), custom_call_target="tpu_custom_call" | custom-call | flops 1459617792 | bytes 7078400 | tf_op jit(solution)/shard_map/prepare/pallas_call | solution.py:112
  58.4 1.6 %collective-permute-done.15 = f32[384,128]{1,0:T(8,128)S(1)} collective-permute-done((f32[384,128]{1,0:T(8,128)S(1)}, f32[384,128]{1,0:T(8,128)S(1)}, u32[]{:S(2)}, u32[]{:S(2)}) %collective-permute-start.15) | collective-permute-done | bytes 196640 | tf_op jit(solution)/shard_map/ppermute | solution.py:560
  60.0 0.1 collective-permute-start.16
  60.0 1.8 %collective-permute-done.17.refs_3_ = f32[128,256]{1,0:T(8,128)S(1)} collective-permute-done((f32[128,256]{1,0:T(8,128)S(1)}, f32[128,256]{1,0:T(8,128)S(1)}, u32[]{:S(2)}, u32[]{:S(2)}) %collective-permute-start.17) | collective-permute-done | bytes 131104 | tf_op jit(solution)/shard_map/ppermute | solution.py:569
  61.8 0.0 collective-permute-start.18
  61.8 1.3 %collective-permute-done.18.refs_4_ = f32[128,256]{1,0:T(8,128)S(1)} collective-permute-done((f32[128,256]{1,0:T(8,128)S(1)}, f32[128,256]{1,0:T(8,128)S(1)}, u32[]{:S(2)}, u32[]{:S(2)}) %collective-permute-start.18) | collective-permute-done | bytes 131104 | tf_op jit(solution)/shard_map/ppermute | solution.py:576
  63.2 0.0 collective-permute-done.16.refs_2_
  63.2 2.9 %finish.1 = (f32[2,128,512]{2,1,0:T(8,128)}, f32[2,64,512]{2,1,0:T(8,128)}) custom-call(s32[2,4]{1,0:T(2,128)S(1)} %copy-done.1, f32[384,128]{1,0:T(8,128)S(1)} %broadcast_add_fusion.1.refs_1_, f32[384,128]{1,0:T(8,128)S(1)} %collective-permute-done.16.refs_2_, f32[128,256]{1,0:T(8,128)S(1)} %collective-permute-done.17.refs_3_, ...), custom_call_target="tpu_custom_call" | custom-call | flops 452984832 | bytes 5308416 | tf_op jit(solution)/shard_map/finish/pallas_call | solution.py:112
  (6 shorter events, 0.1 us)
Async XLA Ops:
  0.6 18.7 %copy-start.3 = (s32[2,4]{1,0:T(2,128)S(1)}, s32[2,4]{1,0:T(2,128)}, u32[]{:S(2)}) copy-start(s32[2,4]{1,0:T(2,128)} %refs_0_.11) | copy-start | bytes 100
  1.6 21.4 %copy-start.1 = (s32[2,4]{1,0:T(2,128)S(1)}, s32[2,4]{1,0:T(2,128)}, u32[]{:S(2)}) copy-start(s32[2,4]{1,0:T(2,128)} %refs_0_.17) | copy-start | bytes 100
  1.7 21.3 %collective-permute-start = (f32[1,64,512]{2,1,0:T(8,128)S(1)}, f32[1,64,512]{2,1,0:T(8,128)S(1)}, u32[]{:S(2)}, u32[]{:S(2)}) collective-permute-start(f32[1,64,512]{2,1,0:T(8,128)S(1)} %get-tuple-element.32.refs_2_), channel_id=1, source_target_pairs={{0,1},{1,2},{2,3},{3,0},{4,5},{5,6},{6,7},{7,4},{8,9},{9,10},{10,1... | collective-permute-start | bytes 393224 | tf_op jit(solution)/shard_map/ppermute | solution.py:414
  4.7 13.3 %collective-permute-start.1 = (s32[2,4]{1,0:T(2,128)}, s32[2,4]{1,0:T(2,128)S(1)}, u32[]{:S(2)}, u32[]{:S(2)}) collective-permute-start(s32[2,4]{1,0:T(2,128)} %refs_0_.11), channel_id=1, source_target_pairs={{0,4},{4,8},{8,12},{12,16},{16,20},{20,24},{24,28},{28,0},{1,5},{5... | collective-permute-start | bytes 104 | tf_op jit(solution)/shard_map/ppermute | solution.py:406
  4.7 0.7 %copy-start.2 = (s32[2,4]{1,0:T(2,128)S(1)}, s32[2,4]{1,0:T(2,128)}, u32[]{:S(2)}) copy-start(s32[2,4]{1,0:T(2,128)} %refs_0_.11) | copy-start | bytes 100
  8.3 14.8 %collective-permute-start.3 = (f32[1,64,512]{2,1,0:T(8,128)S(1)}, f32[1,64,512]{2,1,0:T(8,128)S(1)}, u32[]{:S(2)}, u32[]{:S(2)}) collective-permute-start(f32[1,64,512]{2,1,0:T(8,128)S(1)} %get-tuple-element.34), channel_id=1, source_target_pairs={{0,3},{1,0},{2,1},{3,2},{4,7},{5,4},{6,5},{7,6},{8,11},{9,8},{10,9... | collective-permute-start | bytes 393224 | tf_op jit(solution)/shard_map/ppermute | solution.py:414
  10.4 14.6 %collective-permute-start.4 = (f32[1,64,512]{2,1,0:T(8,128)S(1)}, f32[1,64,512]{2,1,0:T(8,128)S(1)}, u32[]{:S(2)}, u32[]{:S(2)}) collective-permute-start(f32[1,64,512]{2,1,0:T(8,128)S(1)} %get-tuple-element.38.refs_1_.refs_6_), channel_id=1, source_target_pairs={{0,1},{1,2},{2,3},{3,0},{4,4},{5,5},{6,6},{7,7},{8,9},{9,10},{10,1... | collective-permute-start | bytes 393224 | tf_op jit(solution)/shard_map/ppermute | solution.py:414
  12.3 14.6 %collective-permute-start.6 = (f32[1,64,512]{2,1,0:T(8,128)S(1)}, f32[1,64,512]{2,1,0:T(8,128)S(1)}, u32[]{:S(2)}, u32[]{:S(2)}) collective-permute-start(f32[1,64,512]{2,1,0:T(8,128)S(1)} %get-tuple-element.33.refs_1_), channel_id=1, source_target_pairs={{0,3},{1,0},{2,1},{3,2},{4,4},{5,5},{6,6},{7,7},{8,11},{9,8},{10,9... | collective-permute-start | bytes 393224 | tf_op jit(solution)/shard_map/ppermute | solution.py:414
  23.0 6.8 %collective-permute-start.2 = (f32[1,64,512]{2,1,0:T(8,128)S(1)}, f32[1,64,512]{2,1,0:T(8,128)S(1)}, u32[]{:S(2)}, u32[]{:S(2)}) collective-permute-start(f32[1,64,512]{2,1,0:T(8,128)S(1)} %broadcast_add_fusion.4), channel_id=1, source_target_pairs={{0,1},{1,2},{2,3},{3,0},{4,5},{5,6},{6,7},{7,4},{8,9},{9,10},{10,1... | collective-permute-start | bytes 393224 | tf_op jit(solution)/shard_map/ppermute | solution.py:414
  24.3 3.9 %collective-permute-start.7 = (f32[1,64,512]{2,1,0:T(8,128)S(1)}, f32[1,64,512]{2,1,0:T(8,128)S(1)}, u32[]{:S(2)}, u32[]{:S(2)}) collective-permute-start(f32[1,64,512]{2,1,0:T(8,128)S(1)} %get-tuple-element.44.refs_2_.refs_10_), channel_id=1, source_target_pairs={{0,0},{1,1},{2,2},{3,3},{4,5},{5,6},{6,7},{7,4},{8,8},{9,9},{10,10... | collective-permute-start | bytes 393224 | tf_op jit(solution)/shard_map/ppermute | solution.py:414
  25.0 8.7 %collective-permute-start.5 = (f32[1,64,512]{2,1,0:T(8,128)S(1)}, f32[1,64,512]{2,1,0:T(8,128)S(1)}, u32[]{:S(2)}, u32[]{:S(2)}) collective-permute-start(f32[1,64,512]{2,1,0:T(8,128)S(1)} %broadcast_add_fusion.3), channel_id=1, source_target_pairs={{0,1},{1,2},{2,3},{3,0},{4,4},{5,5},{6,6},{7,7},{8,9},{9,10},{10,1... | collective-permute-start | bytes 393224 | tf_op jit(solution)/shard_map/ppermute | solution.py:414
  35.3 2.0 %collective-permute-start.8 = (f32[512,256]{1,0:T(8,128)S(1)}, f32[512,256]{1,0:T(8,128)S(1)}, u32[]{:S(2)}, u32[]{:S(2)}) collective-permute-start(f32[512,256]{1,0:T(8,128)S(1)} %broadcast_add_fusion), channel_id=1, source_target_pairs={{0,4},{4,0},{8,12},{12,8},{16,20},{20,16},{24,28},{28,24},{1,5},{5... | collective-permute-start | bytes 1572872 | tf_op jit(solution)/shard_map/ppermute | solution.py:500
  35.4 4.2 %collective-permute-start.10 = (f32[1,64,512]{2,1,0:T(8,128)S(1)}, f32[1,64,512]{2,1,0:T(8,128)S(1)}, u32[]{:S(2)}, u32[]{:S(2)}) collective-permute-start(f32[1,64,512]{2,1,0:T(8,128)S(1)} %get-tuple-element.44.refs_2_.refs_10_), channel_id=1, source_target_pairs={{0,0},{1,1},{2,2},{3,3},{4,7},{5,4},{6,5},{7,6},{8,8},{9,9},{10,10... | collective-permute-start | bytes 393224 | tf_op jit(solution)/shard_map/ppermute | solution.py:414
  36.1 3.5 %collective-permute-start.9 = (f32[1,64,512]{2,1,0:T(8,128)S(1)}, f32[1,64,512]{2,1,0:T(8,128)S(1)}, u32[]{:S(2)}, u32[]{:S(2)}) collective-permute-start(f32[1,64,512]{2,1,0:T(8,128)S(1)} %broadcast_add_fusion.2), channel_id=1, source_target_pairs={{0,0},{1,1},{2,2},{3,3},{4,5},{5,6},{6,7},{7,4},{8,8},{9,9},{10,10... | collective-permute-start | bytes 393224 | tf_op jit(solution)/shard_map/ppermute | solution.py:414
  37.9 16.8 %copy-start = (f32[2,512,512]{2,1,0:T(8,128)S(1)}, f32[2,512,512]{2,1,0:T(8,128)}, u32[]{:S(2)}) copy-start(f32[2,512,512]{2,1,0:T(8,128)} %refs_1_.3) | copy-start | bytes 6291460
  37.9 10.9 %collective-permute-start.13 = (f32[192,128]{1,0:T(8,128)S(1)}, f32[192,128]{1,0:T(8,128)S(1)}, u32[]{:S(2)}, u32[]{:S(2)}) collective-permute-start(f32[192,128]{1,0:T(8,128)S(1)} %get-tuple-element.46.refs_8_), channel_id=1, source_target_pairs={{0,8},{4,12},{8,0},{12,4},{16,24},{20,28},{24,16},{28,20},{1,9},{5... | collective-permute-start | bytes 294920 | tf_op jit(solution)/shard_map/ppermute | solution.py:560
  41.3 8.5 %collective-permute-start.11 = (f32[128,256]{1,0:T(8,128)S(1)}, f32[128,256]{1,0:T(8,128)S(1)}, u32[]{:S(2)}, u32[]{:S(2)}) collective-permute-start(f32[128,256]{1,0:T(8,128)S(1)} %get-tuple-element.47.refs_2_), channel_id=1, source_target_pairs={{0,4},{4,0},{8,12},{12,8},{16,20},{20,16},{24,28},{28,24},{1,5},{5... | collective-permute-start | bytes 393224 | tf_op jit(solution)/shard_map/ppermute | solution.py:517
  48.8 1.3 %collective-permute-start.12 = (f32[128,256]{1,0:T(8,128)S(1)}, f32[128,256]{1,0:T(8,128)S(1)}, u32[]{:S(2)}, u32[]{:S(2)}) collective-permute-start(f32[128,256]{1,0:T(8,128)S(1)} %get-tuple-element.48.refs_3_), channel_id=1, source_target_pairs={{0,4},{4,0},{8,12},{12,8},{16,20},{20,16},{24,28},{28,24},{1,5},{5... | collective-permute-start | bytes 393224 | tf_op jit(solution)/shard_map/ppermute | solution.py:517
  48.8 1.6 %collective-permute-start.14 = (f32[192,128]{1,0:T(8,128)S(1)}, f32[192,128]{1,0:T(8,128)S(1)}, u32[]{:S(2)}, u32[]{:S(2)}) collective-permute-start(f32[192,128]{1,0:T(8,128)S(1)} %collective-permute-done.13.refs_6_.refs_2_.refs_5_), channel_id=1, source_target_pairs={{0,4},{4,0},{8,12},{12,8},{16,20},{20,16},{24,28},{28,24},{1,5},{5... | collective-permute-start | bytes 294920 | tf_op jit(solution)/shard_map/ppermute | solution.py:576
  51.1 8.9 %collective-permute-start.15 = (f32[384,128]{1,0:T(8,128)S(1)}, f32[384,128]{1,0:T(8,128)S(1)}, u32[]{:S(2)}, u32[]{:S(2)}) collective-permute-start(f32[384,128]{1,0:T(8,128)S(1)} %extend.1), channel_id=1, source_target_pairs={{0,16},{4,4},{8,8},{12,20},{16,0},{20,12},{24,24},{28,28},{1,17},{... | collective-permute-start | bytes 589832 | tf_op jit(solution)/shard_map/ppermute | solution.py:560
  56.2 5.6 %collective-permute-start.17 = (f32[128,256]{1,0:T(8,128)S(1)}, f32[128,256]{1,0:T(8,128)S(1)}, u32[]{:S(2)}, u32[]{:S(2)}) collective-permute-start(f32[128,256]{1,0:T(8,128)S(1)} %get-tuple-element.56), channel_id=1, source_target_pairs={{0,8},{4,12},{8,0},{12,4},{16,24},{20,28},{24,16},{28,20},{1,9},{5... | collective-permute-start | bytes 393224 | tf_op jit(solution)/shard_map/ppermute | solution.py:569
  60.0 3.2 %collective-permute-start.16 = (f32[384,128]{1,0:T(8,128)S(1)}, f32[384,128]{1,0:T(8,128)S(1)}, u32[]{:S(2)}, u32[]{:S(2)}) collective-permute-start(f32[384,128]{1,0:T(8,128)S(1)} %broadcast_add_fusion.1.refs_1_), channel_id=1, source_target_pairs={{0,4},{4,0},{8,12},{12,8},{16,20},{20,16},{24,28},{28,24},{1,5},{5... | collective-permute-start | bytes 589832 | tf_op jit(solution)/shard_map/ppermute | solution.py:574
  61.8 1.3 %collective-permute-start.18 = (f32[128,256]{1,0:T(8,128)S(1)}, f32[128,256]{1,0:T(8,128)S(1)}, u32[]{:S(2)}, u32[]{:S(2)}) collective-permute-start(f32[128,256]{1,0:T(8,128)S(1)} %collective-permute-done.17.refs_3_), channel_id=1, source_target_pairs={{0,4},{4,0},{8,12},{12,8},{16,20},{20,16},{24,28},{28,24},{1,5},{5... | collective-permute-start | bytes 393224 | tf_op jit(solution)/shard_map/ppermute | solution.py:576

commit v7 on v5

--- a/solution.py
+++ b/solution.py
@@ -35,12 +35,26 @@
 
 def pack(cov):
     half = cov.shape[0] // 2
-    return jnp.concatenate([cov[:half, :half], cov[:half, half:], cov[half:, half:]], 0)
+    part = half // 2
+    first, second = cov[:half, :half], cov[half:, half:]
+    lane = lax.broadcasted_iota(jnp.int32, (part, half), 1)
+    last = jnp.where(lane < part, pltpu.roll(first[part:], part, 1), second[part:])
+    return jnp.concatenate([cov[:half, half:], first[:part], second[:part], last], 0)
 
 
 def unpack(packed):
-    half = packed.shape[0] // 3
-    first, cross, second = packed[:half], packed[half : 2 * half], packed[2 * half :]
+    half = packed.shape[1]
+    part = half // 2
+    cross, last = packed[:half], packed[2 * half :]
+    row = lax.broadcasted_iota(jnp.int32, (half, half), 0)
+    lane = lax.broadcasted_iota(jnp.int32, (half, half), 1)
+
+    def symmetric(top, bottom):
+        upper = jnp.concatenate([top, bottom], 0)
+        return jnp.where((row < part) | (lane >= part), upper, upper.T)
+
+    first = symmetric(packed[half : half + part], pltpu.roll(last, part, 1))
+    second = symmetric(packed[half + part : 2 * half], last)
     top = jnp.concatenate([first, cross], 1)
     bottom = jnp.concatenate([cross.T, second], 1)
     return jnp.concatenate([top, bottom], 0)
@@ -84,6 +98,26 @@
     first = lax.axis_index("seg") == 0
     last = prior_ref.shape[0] - 1
     return [jnp.where(first, fill_ref[0, j], prior_ref[last, j]) for j in range(slots)]
+
+
+def order_of(chosen, blocks):
+    slots = len(chosen)
+    rest = [jnp.int32(0)] * (blocks - slots)
+    place = []
+    seen = jnp.int32(0)
+    for b in range(blocks):
+        hit = jnp.int32(0)
+        where = jnp.int32(0)
+        for j in range(slots):
+            same = (chosen[j] == b).astype(jnp.int32)
+            hit = hit + same
+            where = where + same * j
+        free = 1 - hit
+        for q in range(blocks - slots):
+            rest[q] = rest[q] + jnp.where(seen == q, free * b, 0)
+        place.append(jnp.where(hit > 0, where, slots + seen))
+        seen = seen + free
+    return rest, place
 
 
 def vmem(count):
@@ -152,61 +186,112 @@
     own_cols = own_ref.shape[0]
     own_at = pl.ds(pl.multiple_of(lax.axis_index("row") * own_cols, own_cols), own_cols)
     copy.wait()
-    picked_t = split(
+    picked = split(
         jnp.concatenate(
             [
-                two_blocks(tile_of(inv_ref), chosen[2 * t], chosen[2 * t + 1]).T
+                two_blocks(tile_of(inv_ref), chosen[2 * t], chosen[2 * t + 1])
                 for t in range(len(chosen) // 2)
+            ],
+            1,
+        )
+    )
+    pick_high_ref[...], pick_low_ref[...] = picked
+    base_ref[...] = mm(picked, picked, TN)
+    own_ref[...] = mm(inv_ref[:, own_at], inv_ref[...], TN)
+
+
+def send_kernel(
+    mask_hbm, fill_hbm, factor_hbm, inv_hbm, sent_ref, rest_ref,
+    mask_ref, fill_ref, factor_ref, inv_ref, map_ref, sems
+):
+    panels, rows, width = factor_ref.shape
+    cut = width // 2
+    row_at = lax.axis_index("row")
+    small = [
+        pltpu.make_async_copy(mask_hbm, mask_ref, sems.at[0, 0]),
+        pltpu.make_async_copy(fill_hbm, fill_ref, sems.at[0, 1]),
+        pltpu.make_async_copy(factor_hbm, factor_ref, sems.at[0, 2]),
+    ]
+    large = [
+        (
+            pltpu.make_async_copy(inv_hbm.at[p, cut:, :], inv_ref.at[p - 1, cut:, :], sems.at[p, 0]),
+            pltpu.make_async_copy(
+                inv_hbm.at[p, :cut, :cut], inv_ref.at[p - 1, :cut, :cut], sems.at[p, 1]
+            ),
+        )
+        for p in range(1, panels)
+    ]
+    for copy in (*small, *(copy for pair in large for copy in pair)):
+        copy.start()
+    for copy in small:
+        copy.wait()
+
+    def kept_own(p):
+        return jnp.concatenate(
+            [
+                kept_rows(
+                    mask_ref, p, row_at * (rows // BLOCK) + s,
+                    factor_ref[p, s * BLOCK : (s + 1) * BLOCK, :],
+                )
+                for s in range(rows // BLOCK)
             ],
             0,
         )
-    )
-    pick_high_ref[...], pick_low_ref[...] = picked_t
-    base_ref[...] = mm(picked_t, picked_t, NT)
-    own_ref[...] = mm(inv_ref[:, own_at].T, inv_ref[...])
-
-
-def put_rows(mask_ref, panel, distance, part, take):
+
+    sent_ref[:, :width] = kept_own(0)
+    for p in range(1, panels):
+        chosen = chosen_of(p, fill_ref)
+        rest, _ = order_of(chosen, width // BLOCK)
+        kept = kept_own(p)
+        for copy in large[p - 1]:
+            copy.wait()
+        map_ref[...] = triangular_mm(kept, inv_ref[p - 1])
+        for ref, wanted, at in (
+            (sent_ref, chosen, width + (p - 1) * len(chosen) * BLOCK),
+            (rest_ref, rest, (p - 1) * len(rest) * BLOCK),
+        ):
+            for t in range(len(wanted) // 2):
+                ref[:, at + t * LANES : at + (t + 1) * LANES] = two_blocks(
+                    tile_of(map_ref), wanted[2 * t], wanted[2 * t + 1]
+                )
+
+
+def rows_from(distance, rows):
     row_count = lax.axis_size("row")
-    rows = part.shape[1]
     owner = lax.rem(lax.axis_index("row") + (row_count - distance), row_count)
-    for s in range(rows // BLOCK):
-        slot = owner * (rows // BLOCK) + s
-        kept = kept_rows(mask_ref, panel, slot, part[panel, s * BLOCK : (s + 1) * BLOCK, :])
-        take(kept, pl.ds(pl.multiple_of(slot * BLOCK, BLOCK), BLOCK))
-
-
-def links_kernel(distances, missing, mask_ref, *refs):
-    parts, refs = refs[: len(distances)], refs[len(distances) :]
-    *pick_refs, links_t_ref, rows_ref = refs
-    for p in range(links_t_ref.shape[0]):
-
-        def take(kept, at):
-            rows_ref[at, :] = kept
-
+    return pl.ds(pl.multiple_of(owner * rows, rows), rows)
+
+
+def links_kernel(distances, panels, *refs):
+    parts, (high_ref, low_ref, links_t_ref, rows_ref) = refs[: len(distances)], refs[len(distances) :]
+    width = high_ref.shape[0]
+    size = rows_ref.shape[0]
+    pick = (high_ref[...], low_ref[...])
+    rows_ref[...] = jnp.zeros_like(rows_ref)
+    for p in range(panels):
         for d, part in zip(distances, parts):
-            put_rows(mask_ref, p, d, part, take)
-        put_rows(mask_ref, p, missing, parts[0], lambda kept, at: take(jnp.zeros_like(kept), at))
-        pick = (pick_refs[2 * p][...], pick_refs[2 * p + 1][...])
-        links_t_ref[p] = mm(pick, rows_ref[...], NT)
-
-
-def segment_kernel(distance, panels, mask_ref, part, early_ref, *refs):
-    pick_refs, base_refs = refs[: 2 * panels], refs[2 * panels : 3 * panels]
-    links_t_ref, whole_ref = refs[3 * panels :]
-    size = links_t_ref.shape[1]
-    lane = lax.broadcasted_iota(jnp.int32, (size, size), 1) // BLOCK
-    cov = link_t = None
+            at = rows_from(d, part.shape[0])
+            if p == 0:
+                rows_ref[at, :] = mm(part[:, :width], pick)
+            else:
+                rows_ref[at, :] = part[:, width + (p - 1) * size : width + p * size]
+        links_t_ref[p] = rows_ref[...].T
+
+
+def segment_kernel(distance, panels, part, high_ref, low_ref, early_ref, *refs):
+    base_refs, (links_t_ref, whole_ref) = refs[:panels], refs[panels:]
+    rows = part.shape[0]
+    width, size = high_ref.shape
+    lane = lax.broadcasted_iota(jnp.int32, (size, size), 1) // rows
+    here = lane == rows_from(distance, rows).start // rows
+    link_t = cov = None
     for p in range(panels - 1, -1, -1):
-        pick = (pick_refs[2 * p][...], pick_refs[2 * p + 1][...])
-        pieces = [early_ref[p]]
-
-        def take(kept, at):
-            late = mm(pick, jnp.concatenate([kept] * (size // BLOCK), 0), NT)
-            pieces.append(jnp.where(lane == at.start // BLOCK, late, pieces[-1]))
-
-        put_rows(mask_ref, p, distance, part, take)
-        own_t = pieces[-1]
+        if p == 0:
+            late = mm(part[:, :width], (high_ref[...], low_ref[...]))
+        else:
+            late = part[:, width + (p - 1) * size : width + p * size]
+        late_t = jnp.concatenate([late] * (size // rows), 0).T
+        own_t = jnp.where(here, late_t, early_ref[p])
         links_t_ref[p] = own_t
         if cov is None:
             cov, link_t = base_refs[p][...], own_t
@@ -218,17 +303,13 @@
     whole_ref[size:] = cov
 
 
-def maps_kernel(mask_ref, inv_ref, *refs):
-    *parts, maps_ref, token_ref, rows_ref = refs
+def first_map_kernel(inv_ref, *refs):
+    *parts, _, map_ref, token_ref, rows_ref = refs
+    width = map_ref.shape[1]
     token_ref[...] = jnp.zeros_like(token_ref)
-    for p in range(inv_ref.shape[0]):
-
-        def take(kept, at):
-            rows_ref[at, :] = kept
-
-        for d, part in enumerate(parts):
-            put_rows(mask_ref, p, d, part, take)
-        maps_ref[p] = triangular_mm(rows_ref[...], inv_ref[p])
+    for d, part in enumerate(parts):
+        rows_ref[rows_from(d, part.shape[0]), :] = part[:, :width]
+    map_ref[...] = triangular_mm(rows_ref[...], inv_ref[0])
 
 
 def chip_kernel(own_ref, other_ref, link_t_ref, cov_ref, packed_ref, half_t_ref):
@@ -279,13 +360,14 @@
         refs[9 + 2 * i][...] = jnp.where(is_lower(), whole[half:], whole[:half])
 
 
-def prepare_kernel(levels, panels, *refs):
+def prepare_kernel(levels, panels, row_count, fill_ref, *refs):
     base_refs, own_refs, refs = refs[:panels], refs[panels : 2 * panels], refs[2 * panels :]
-    (other_ref, maps_ref, links_t_ref), refs = refs[:3], refs[3:]
+    (other_ref, first_map_ref, links_t_ref), refs = refs[:3], refs[3:]
+    parts, rests, refs = refs[:row_count], refs[row_count : 2 * row_count], refs[2 * row_count :]
     past_refs, refs = refs[: 4 * (levels > 1)], refs[4 * (levels > 1) :]
-    left_high, left_low, right_high, right_low, const_ref, token_ref, scratch = refs
+    left_high, left_low, right_high, right_low, const_ref, token_ref, scratch, order_ref = refs
     token_ref[...] = jnp.zeros_like(token_ref)
-    own_cols = own_refs[0].shape[0]
+    own_cols, width = own_refs[0].shape
     size = base_refs[0].shape[0]
     row_at = lax.axis_index("row")
     rows = left_high.shape[1] - own_cols
@@ -310,8 +392,25 @@
     own_at = pl.ds(pl.multiple_of(row_at * own_cols, own_cols), own_cols)
     own_rows = pl.ds(pl.multiple_of(row_at * rows, rows), rows)
     for p in range(panels - 1, -1, -1):
-        whole = split(maps_ref[p])
-        own_t = split(maps_ref[p, :, own_at].T)
+        if p == 0:
+            whole, own_map = first_map_ref[...], first_map_ref[:, own_at]
+        else:
+            _, place = order_of(chosen_of(p, fill_ref), width // BLOCK)
+            chosen_at, rest_at = width + (p - 1) * size, (p - 1) * (width - size)
+            for d in range(row_count):
+                at = rows_from(d, rows)
+                order_ref[at, :size] = parts[d][:, chosen_at : chosen_at + size]
+                order_ref[at, size:] = rests[d][:, rest_at : rest_at + width - size]
+            whole = jnp.concatenate(
+                [
+                    two_blocks(tile_of(order_ref), place[2 * t], place[2 * t + 1])
+                    for t in range(len(place) // 2)
+                ],
+                1,
+            )
+            order_ref[...] = whole
+            own_map = order_ref[:, own_at]
+        whole, own_t = split(whole), split(own_map.T)
         scratch[:, :size] = to_t
         scratch[:, size:] = gain
         to_parts = split(to_t)
@@ -354,6 +453,7 @@
     own_cols = width // row_count
     slots = fill_blocks.shape[1]
     chosen_cols = slots * BLOCK
+    rest_cols = width - chosen_cols
     chips = seg_count // 2
     half_cols = size // 2
 
@@ -361,16 +461,37 @@
         count = lax.axis_size(axis)
         return lax.ppermute(x, axis, [(i, (i + distance) % count) for i in range(count)])
 
+    sent, rest = call(
+        send_kernel,
+        [shape(rows, width + (panels - 1) * chosen_cols), shape(rows, (panels - 1) * rest_cols)],
+        [],
+        [],
+        far=[fill_mask, fill_blocks, factor_off, inv_diag],
+        scratch=[
+            pltpu.SMEM(fill_mask.shape, jnp.int32),
+            pltpu.SMEM(fill_blocks.shape, jnp.int32),
+            pltpu.VMEM(factor_off.shape, F32),
+            pltpu.VMEM((panels - 1, width, width), F32),
+            pltpu.VMEM((rows, width), F32),
+            pltpu.SemaphoreType.DMA((panels, 3)),
+        ],
+        flops=6 * (panels - 1) * rows * width * width,
+        name="send",
+    )
+
+    def zero_of(x):
+        return jnp.minimum(jnp.abs(x), 0.0)
+
     prior_fill = turn(fill_blocks, "seg", 1)
-    ups = [factor_off, turn(factor_off, "row", 1)]
+    ups = [sent, turn(sent, "row", 1)]
     for _ in range(1, row_count // 2):
         ups.append(turn(ups[-1] + jnp.minimum(jnp.min(prior_fill), 0).astype(F32), "row", 1))
-    pick = jax.ShapeDtypeStruct((chosen_cols, width), BF16)
+    pick = jax.ShapeDtypeStruct((width, chosen_cols), BF16)
     bases, priors, picks, tokens = [], [], [], []
     for p in range(panels):
         base, own_prior, *high_low, token = call(
             functools.partial(prior_kernel, p),
-            [shape(chosen_cols, chosen_cols), shape(own_cols, width), pick, pick, shape(1, 1, width)],
+            [shape(chosen_cols, chosen_cols), shape(own_cols, width), pick, pick, shape(1, sent.shape[1])],
             [fill_blocks] if p else [fill_blocks, prior_fill],
             [],
             far=[inv_diag],
@@ -382,43 +503,41 @@
         priors.append(own_prior)
         picks += high_low
         tokens.append(token)
-    downs = [factor_off + tokens[-1]]
+    downs = [sent + tokens[-1]]
     for _ in range((row_count - 1) // 2):
         downs.append(turn(downs[-1], "row", -1))
     parts = ups + downs[:0:-1]
     last = len(ups) - 1
     early = [d for d in range(row_count) if d != last]
     (links,) = call(
-        functools.partial(links_kernel, early, last),
+        functools.partial(links_kernel, early, panels),
         [shape(panels, size, size)],
-        [fill_mask],
-        [*(parts[d] for d in early), *picks],
-        scratch=[pltpu.VMEM((size, width), F32)],
-        flops=6 * panels * size * size * width,
+        [],
+        [*(parts[d] for d in early), *picks[:2]],
+        scratch=[pltpu.VMEM((size, size), F32)],
+        flops=6 * size * size * width,
         name="links",
     )
     links_t, own_whole = call(
         functools.partial(segment_kernel, last, panels),
         [shape(panels, size, size), shape(2 * size, size)],
-        [fill_mask],
-        [parts[last], links, *picks, *bases],
-        flops=6 * panels * size * size * width + 18 * (panels - 1) * size**3,
+        [],
+        [parts[last], *picks[:2], links, *bases],
+        flops=6 * rows * size * width + 18 * (panels - 1) * size**3,
         name="segment",
     )
-    maps, maps_token = call(
-        maps_kernel,
-        [shape(panels, size, width), shape(1, half_cols)],
-        [fill_mask],
-        [inv_diag, *parts],
-        scratch=[pltpu.VMEM((size, width), F32)],
-        flops=6 * panels * size * width * width,
-        mib=24,
-        name="maps",
-    )
+    rest = rest + zero_of(ups[1][:1, : rest.shape[1]])
+    rest_ups, rest_downs = [rest, turn(rest, "row", 1)], [rest]
+    for _ in range(1, row_count // 2):
+        rest_ups.append(turn(rest_ups[-1], "row", 1))
+    for _ in range((row_count - 1) // 2):
+        rest_downs.append(turn(rest_downs[-1], "row", -1))
+    rests = rest_ups + rest_downs[:0:-1]
+    swap_gate = zero_of(rest_ups[1][:1, :size] + own_whole[:1])
     swap = [(i, i ^ 1) for i in range(seg_count)]
-    other_whole = lax.ppermute(own_whole, "seg", swap)
+    other_whole = lax.ppermute(own_whole + swap_gate, "seg", swap)
     half = size // 2
-    half_packed = shape(3 * half // 2, half)
+    half_packed = shape(5 * half // 4, half)
     half_link = shape(half, size)
     link_t, cov, send, send_t = call(
         chip_kernel,
@@ -428,6 +547,16 @@
         flops=18 * size**3,
         name="chip",
     )
+    first_map, map_token = call(
+        first_map_kernel,
+        [shape(size, width), shape(1, half_cols)],
+        [],
+        [inv_diag, *parts, send],
+        scratch=[pltpu.VMEM((size, width), F32)],
+        flops=6 * size * width * width,
+        name="first_map",
+    )
+    level_gate = map_token + zero_of(rest_ups[-1][:1, :half_cols] + rest_downs[-1][:1, :half_cols])
     past = None
     after = (jnp.zeros(half_packed.shape, F32),) * 2
     levels = (chips - 1).bit_length()
@@ -438,11 +567,11 @@
         left = jax.ShapeDtypeStruct((panels, total, size), BF16)
         right = jax.ShapeDtypeStruct((panels, size, width), BF16)
         return call(
-            functools.partial(prepare_kernel, levels, panels),
+            functools.partial(prepare_kernel, levels, panels, row_count),
             [left, left, right, right, shape(panels, total, width), shape(1, half_cols)],
-            [],
-            [*bases, *priors, other_whole, maps, links_t, *(past or ())],
-            scratch=[pltpu.VMEM((size, width), F32)],
+            [fill_blocks],
+            [*bases, *priors, other_whole, first_map, links_t, *parts, *rests, *(past or ())],
+            scratch=[pltpu.VMEM((size, width), F32), pltpu.VMEM((size, width), F32)],
             flops=6 * panels * size * (total * size + size * width + total * width + 3 * size * size),
             mib=24,
             name="prepare",
@@ -458,7 +587,7 @@
             break
         got_t = lax.ppermute(send_t, "seg", partner)
         if level == 0:
-            got = got + maps_token
+            got = got + level_gate
         got = (got_t, lax.ppermute(got_t, "seg", swap), got, lax.ppermute(got, "seg", swap))
         outs = [half_packed]
         if level < levels - 2:

time: 46.9 us -> 45.4 us (0.968)
  waiting for transfers between devices: 17.7 us -> 12.2 us
  starting transfers between devices: 9.63 us -> 13.7 us
  local copies, waits for them, and re-layouts: 0.7 us -> 0.01 us
    ppermute x4 -> x7, starting transfers between devices: 5.29 us -> 9.29 us  [turn(): lax.ppermute(x, axis, [(i, (i + distance) % count) for i in range(count)])]
    ppermute x1, waiting for transfers between devices: 2.76 us -> 1.07 us  [body(): got_t = lax.ppermute(send_t, 'seg', partner)]
    ppermute x1, waiting for transfers between devices: 1.54 us -> 0.01 us  [body(): other_whole = lax.ppermute(own_whole + swap_gate, 'seg', swap)]
    ppermute x2, waiting for transfers between devices: 2.37 us -> 0.88 us  [body(): got = lax.ppermute(send, 'seg', partner)]
    ppermute x4 -> x7, waiting for transfers between devices: 8.46 us -> 7.76 us  [turn(): lax.ppermute(x, axis, [(i, (i + distance) % count) for i in range(count)])]
    unnamed x10 -> x6, local copies, waits for them, and re-layouts: 0.7 us -> 0.01 us
    pallas_call x9 -> x10, Pallas kernels: 16.6 us -> 17 us  [call(): pl.pallas_call(inner, out_shape=[*outs, *(jax.ShapeDtypeStruct(a.shape, a...]
  transfers between devices with their start and end apart: 11 -> 14, of which waited for: 9 -> 9; matrix products, arithmetic and copies ran while one was open for 1% -> 2% of each run, Pallas kernels for 24% -> 27%
where the time goes in v7:
time: 45.4 us; the launch traced here: 45.2 us
  Pallas kernels  17 us (37%)
  starting transfers between devices  13.7 us (30%)
  waiting for transfers between devices  12.2 us (27%)
  between operations  1.45 us (3%)
  other arithmetic  0.77 us (2%)
    pallas_call x10, Pallas kernels, call(): pl.pallas_call(inner, out_shape=[*outs, *(jax.ShapeDtypeStruct(a.shape, a...  17 us
    ppermute x7, starting transfers between devices, turn(): lax.ppermute(x, axis, [(i, (i + distance) % count) for i in range(count)])  9.29 us
    ppermute x7, waiting for transfers between devices, turn(): lax.ppermute(x, axis, [(i, (i + distance) % count) for i in range(count)])  7.76 us
    ppermute x2, starting transfers between devices, body(): got = lax.ppermute(send, 'seg', partner)  2.28 us
    ppermute x1, starting transfers between devices, body(): got_t = lax.ppermute(send_t, 'seg', partner)  1.58 us
    ppermute x1, waiting for transfers between devices, body(): lax.ppermute(got, 'seg', swap)  1.26 us
    ppermute x1, waiting for transfers between devices, body(): after = (got, lax.ppermute(got, 'seg', swap))  1.26 us
    ppermute x1, waiting for transfers between devices, body(): got_t = lax.ppermute(send_t, 'seg', partner)  1.07 us
  transfers between devices with their start and end apart: 14, of which 9 were waited for; matrix products, arithmetic and copies ran while one was open for 2% of the time, Pallas kernels for 27%

profile of v7, /device:TPU:0, one launch (start us, length us, event | category | flops | bytes accessed | tf_op | source)
XLA Modules:
  0.0 45.2 jit_solution(7071947222564214444)
XLA Ops:
  0.6 0.0 copy-start.1
  0.6 0.5 %collective-permute-start.1 = (s32[2,4]{1,0:T(2,128)}, s32[2,4]{1,0:T(2,128)S(1)}, u32[]{:S(2)}, u32[]{:S(2)}) collective-permute-start(s32[2,4]{1,0:T(2,128)} %refs_0_.10), channel_id=1, source_target_pairs={{0,4},{4,8},{8,12},{12,16},{16,20},{20,24},{24,28},{28,0},{1,5},{5... | collective-permute-start | bytes 104 | tf_op jit(solution)/shard_map/ppermute | solution.py:462
  1.1 1.7 %send.1 = (f32[64,768]{1,0:T(8,128)S(1)}, f32[64,256]{1,0:T(8,128)S(1)}) custom-call(s32[2,4]{1,0:T(2,128)} %refs_0_.11, s32[2,4]{1,0:T(2,128)} %refs_0_.10, f32[2,64,512]{2,1,0:T(8,128)} %refs_2_.2, f32[2,512,512]{2,1,0:T(8,128)} %refs_0_.9), custom_call_target="tpu_custom_call" | custom-call | flops 100663296 | bytes 2621504 | tf_op jit(solution)/shard_map/send/pallas_call | solution.py:139
  2.9 2.6 %collective-permute-start = (f32[64,768]{1,0:T(8,128)S(1)}, f32[64,768]{1,0:T(8,128)S(1)}, u32[]{:S(2)}, u32[]{:S(2)}) collective-permute-start(f32[64,768]{1,0:T(8,128)S(1)} %get-tuple-element.25.refs_0_.refs_1_.refs_8_), channel_id=1, source_target_pairs={{0,1},{1,2},{2,3},{3,0},{4,5},{5,6},{6,7},{7,4},{8,9},{9,10},{10,1... | collective-permute-start | bytes 589832 | tf_op jit(solution)/shard_map/ppermute | solution.py:462
  5.5 0.0 copy-done.1
  5.5 3.1 %prior.3 = (f32[256,256]{1,0:T(8,128)S(1)}, f32[128,512]{1,0:T(8,128)S(1)}, bf16[512,256]{1,0:T(8,128)(2,1)}, bf16[512,256]{1,0:T(8,128)(2,1)}, f32[1,768]{1,0:T(1,128)S(1)}) custom-call(s32[2,4]{1,0:T(2,128)S(1)} %copy-done.1, f32[2,512,512]{2,1,0:T(8,128)} %refs_0_.9), custom_call_target="tpu_custom_call" | custom-call | flops 402653184 | bytes 3673088 | tf_op jit(solution)/shard_map/prior/pallas_call | solution.py:139
  8.7 2.1 %collective-permute-start.3 = (f32[64,768]{1,0:T(8,128)S(1)}, f32[64,768]{1,0:T(8,128)S(1)}, u32[]{:S(2)}, u32[]{:S(2)}) collective-permute-start(f32[64,768]{1,0:T(8,128)S(1)} %broadcast_add_fusion.1), channel_id=1, source_target_pairs={{0,3},{1,0},{2,1},{3,2},{4,7},{5,4},{6,5},{7,6},{8,11},{9,8},{10,9... | collective-permute-start | bytes 589832 | tf_op jit(solution)/shard_map/ppermute | solution.py:462
  10.8 0.0 collective-permute-done.1.refs_1_
  10.8 0.6 %reduce_min.9 = s32[]{:T(128)} reduce(s32[2,4]{1,0:T(2,128)S(1)} %collective-permute-done.1.refs_1_, s32[]{:T(128)} %constant.3.clone.1), dimensions={0,1}, to_apply=%region_0.0 | reduce | flops 7 | bytes 40 | tf_op jit(solution)/shard_map/reduce_min | solution.py:488
  12.1 0.3 collective-permute-done.refs_1_.refs_2_.refs_9_
  12.4 0.4 collective-permute-start.2
  12.8 1.6 %collective-permute-start.4 = (f32[64,256]{1,0:T(8,128)S(1)}, f32[64,256]{1,0:T(8,128)S(1)}, u32[]{:S(2)}, u32[]{:S(2)}) collective-permute-start(f32[64,256]{1,0:T(8,128)S(1)} %broadcast_add_fusion.5.refs_12_), channel_id=1, source_target_pairs={{0,1},{1,2},{2,3},{3,0},{4,5},{5,6},{6,7},{7,4},{8,9},{9,10},{10,1... | collective-permute-start | bytes 196616 | tf_op jit(solution)/shard_map/ppermute | solution.py:462
  14.5 2.8 %prior.2 = (f32[256,256]{1,0:T(8,128)S(1)}, f32[128,512]{1,0:T(8,128)S(1)}, bf16[512,256]{1,0:T(8,128)(2,1)S(1)}, bf16[512,256]{1,0:T(8,128)(2,1)S(1)}, f32[1,768]{1,0:T(1,128)}) custom-call(s32[2,4]{1,0:T(2,128)S(1)} %copy-done.1, s32[2,4]{1,0:T(2,128)S(1)} %collective-permute-done.1.refs_1_, f32[2,512,512]{2,1,0:T(8,128)} %refs_0_.9), custom_call_target="tpu_custom_call" | custom-call | flops 402653184 | bytes 3673088 | tf_op jit(solution)/shard_map/prior/pallas_call | solution.py:139
  17.3 0.2 collective-permute-done.3.refs_2_.refs_4_.refs_11_
  17.5 0.7 %links.1.refs_3_ = f32[2,256,256]{2,1,0:T(8,128)S(1)} custom-call(f32[64,768]{1,0:T(8,128)S(1)} %get-tuple-element.25.refs_0_.refs_1_.refs_8_, f32[64,768]{1,0:T(8,128)S(1)} %collective-permute-done.refs_1_.refs_2_.refs_9_, f32[64,768]{1,0:T(8,128)S(1)} %collective-permute-done.3.refs_2_.refs_4_.refs_11_, ...), custom_call_target="tpu_custom_call" | custom-call | flops 201326592 | bytes 2162688 | tf_op jit(solution)/shard_map/links/pallas_call | solution.py:139
  18.2 0.0 copy-start
  18.3 4.2 %collective-permute-done.2.refs_0_.refs_3_.refs_10_ = f32[64,768]{1,0:T(8,128)S(1)} collective-permute-done((f32[64,768]{1,0:T(8,128)S(1)}, f32[64,768]{1,0:T(8,128)S(1)}, u32[]{:S(2)}, u32[]{:S(2)}) %collective-permute-start.2) | collective-permute-done | bytes 196640 | tf_op jit(solution)/shard_map/ppermute | solution.py:462
  22.4 1.0 %segment.1 = (f32[2,256,256]{2,1,0:T(8,128)S(1)}, f32[512,256]{1,0:T(8,128)S(1)}) custom-call(f32[64,768]{1,0:T(8,128)S(1)} %collective-permute-done.2.refs_0_.refs_3_.refs_10_, bf16[512,256]{1,0:T(8,128)(2,1)S(1)} %get-tuple-element.26.refs_3_.refs_1_, bf16[512,256]{1,0:T(8,128)(2,1)S(1)} %get-tuple-element.27.refs_4_.refs_2_, ...), custom_call_target="tpu_custom_call" | custom-call | flops 352321536 | bytes 3342336 | tf_op jit(solution)/shard_map/segment/pallas_call | solution.py:139
  23.4 0.4 collective-permute-done.4.refs_13_
  23.9 0.4 collective-permute-start.5
  24.3 1.9 %collective-permute-start.10 = (f32[64,256]{1,0:T(8,128)S(1)}, f32[64,256]{1,0:T(8,128)S(1)}, u32[]{:S(2)}, u32[]{:S(2)}) collective-permute-start(f32[64,256]{1,0:T(8,128)S(1)} %broadcast_add_fusion.5.refs_12_), channel_id=1, source_target_pairs={{0,3},{1,0},{2,1},{3,2},{4,7},{5,4},{6,5},{7,6},{8,11},{9,8},{10,9... | collective-permute-start | bytes 196616 | tf_op jit(solution)/shard_map/ppermute | solution.py:462
  26.2 0.2 collective-permute-start.9
  26.3 0.0 collective-permute-done.5.refs_1_.refs_5_
  26.3 0.6 %chip.1 = (f32[256,256]{1,0:T(8,128)S(1)}, f32[256,256]{1,0:T(8,128)S(1)}, f32[160,128]{1,0:T(8,128)S(1)}, f32[128,256]{1,0:T(8,128)S(1)}) custom-call(f32[512,256]{1,0:T(8,128)S(1)} %get-tuple-element.31.refs_0_, f32[512,256]{1,0:T(8,128)S(1)} %collective-permute-done.5.refs_1_.refs_5_), custom_call_target="tpu_custom_call" | custom-call | flops 301989888 | bytes 1785856 | tf_op jit(solution)/shard_map/chip/pallas_call | solution.py:139
  27.0 1.6 %collective-permute-start.6 = (f32[128,256]{1,0:T(8,128)S(1)}, f32[128,256]{1,0:T(8,128)S(1)}, u32[]{:S(2)}, u32[]{:S(2)}) collective-permute-start(f32[128,256]{1,0:T(8,128)S(1)} %get-tuple-element.35), channel_id=1, source_target_pairs={{0,8},{4,12},{8,0},{12,4},{16,24},{20,28},{24,16},{28,20},{1,9},{5... | collective-permute-start | bytes 393224 | tf_op jit(solution)/shard_map/ppermute | solution.py:588
  28.6 0.5 %collective-permute-start.8 = (f32[160,128]{1,0:T(8,128)S(1)}, f32[160,128]{1,0:T(8,128)S(1)}, u32[]{:S(2)}, u32[]{:S(2)}) collective-permute-start(f32[160,128]{1,0:T(8,128)S(1)} %get-tuple-element.36.refs_5_), channel_id=1, source_target_pairs={{0,8},{4,12},{8,0},{12,4},{16,24},{20,28},{24,16},{28,20},{1,9},{5... | collective-permute-start | bytes 245768 | tf_op jit(solution)/shard_map/ppermute | solution.py:582
  29.1 0.0 copy-done
  29.1 0.6 %first_map.1 = (f32[256,512]{1,0:T(8,128)S(1)}, f32[1,128]{1,0:T(1,128)S(1)}) custom-call(f32[2,512,512]{2,1,0:T(8,128)S(1)} %copy-done, f32[64,768]{1,0:T(8,128)S(1)} %get-tuple-element.25.refs_0_.refs_1_.refs_8_, f32[64,768]{1,0:T(8,128)S(1)} %collective-permute-done.refs_1_.refs_2_.refs_9_, f32[64,768]{1,0:T(8,128)S(1)} %collective-permute-done.2.refs_0_.refs_3_.refs_10_, ...), custom_call_target="tpu_custom_call" | custom-call | flops 402653184 | bytes 3490304 | tf_op jit(solution)/shard_map/first_map/pallas_call | solution.py:139
  29.6 0.0 collective-permute-done.10.refs_15_
  29.6 2.6 %collective-permute-done.9.refs_14_ = f32[64,256]{1,0:T(8,128)S(1)} collective-permute-done((f32[64,256]{1,0:T(8,128)S(1)}, f32[64,256]{1,0:T(8,128)S(1)}, u32[]{:S(2)}, u32[]{:S(2)}) %collective-permute-start.9) | collective-permute-done | bytes 65568 | tf_op jit(solution)/shard_map/ppermute | solution.py:462
  32.2 1.1 %collective-permute-done.6.refs_2_.refs_16_ = f32[128,256]{1,0:T(8,128)S(1)} collective-permute-done((f32[128,256]{1,0:T(8,128)S(1)}, f32[128,256]{1,0:T(8,128)S(1)}, u32[]{:S(2)}, u32[]{:S(2)}) %collective-permute-start.6) | collective-permute-done | bytes 131104 | tf_op jit(solution)/shard_map/ppermute | solution.py:588
  33.3 0.0 collective-permute-start.7
  33.3 0.9 %collective-permute-done.8 = f32[160,128]{1,0:T(8,128)S(1)} collective-permute-done((f32[160,128]{1,0:T(8,128)S(1)}, f32[160,128]{1,0:T(8,128)S(1)}, u32[]{:S(2)}, u32[]{:S(2)}) %collective-permute-start.8) | collective-permute-done | bytes 81952 | tf_op jit(solution)/shard_map/ppermute | solution.py:582
  34.2 0.1 collective-permute-start.11
  34.3 1.3 %collective-permute-done.11.refs_5_.refs_19_ = f32[160,128]{1,0:T(8,128)S(1)} collective-permute-done((f32[160,128]{1,0:T(8,128)S(1)}, f32[160,128]{1,0:T(8,128)S(1)}, u32[]{:S(2)}, u32[]{:S(2)}) %collective-permute-start.11) | collective-permute-done | bytes 81952 | tf_op jit(solution)/shard_map/ppermute | solution.py:591
  35.5 0.0 collective-permute-done.7.refs_3_.refs_17_
  35.5 0.8 %merge.1 = f32[160,128]{1,0:T(8,128)S(1)} custom-call(f32[256,256]{1,0:T(8,128)S(1)} %get-tuple-element.33.refs_0_, f32[256,256]{1,0:T(8,128)S(1)} %get-tuple-element.34.refs_1_, f32[128,256]{1,0:T(8,128)S(1)} %collective-permute-done.6.refs_2_.refs_16_, f32[128,256]{1,0:T(8,128)S(1)} %collective-permute-done.7.refs_3_.refs_17_, ...), custom_call_target="tpu_custom_call" | custom-call | flops 301989888 | bytes 1032192 | tf_op jit(solution)/shard_map/merge/pallas_call | solution.py:139
  36.4 1.8 %collective-permute-start.12 = (f32[160,128]{1,0:T(8,128)S(1)}, f32[160,128]{1,0:T(8,128)S(1)}, u32[]{:S(2)}, u32[]{:S(2)}) collective-permute-start(f32[160,128]{1,0:T(8,128)S(1)} %merge.1), channel_id=1, source_target_pairs={{0,16},{4,20},{8,24},{12,28},{16,0},{20,4},{24,8},{28,12},{1,17},{... | collective-permute-start | bytes 245768 | tf_op jit(solution)/shard_map/ppermute | solution.py:582
  38.1 0.0 copy-start.2
  38.1 3.3 %prepare.1 = (bf16[2,192,256]{2,1,0:T(8,128)(2,1)S(1)}, bf16[2,192,256]{2,1,0:T(8,128)(2,1)S(1)}, bf16[2,256,512]{2,1,0:T(8,128)(2,1)S(1)}, bf16[2,256,512]{2,1,...) custom-call(s32[2,4]{1,0:T(2,128)S(1)} %copy-done.1, ...), custom_call_target="tpu_custom_call" | custom-call | flops 1459617792 | bytes 7766528 | tf_op jit(solution)/shard_map/prepare/pallas_call | solution.py:139
  41.4 0.0 collective-permute-done.12
  41.4 0.1 collective-permute-start.13
  41.5 1.3 %collective-permute-done.13.refs_2_ = f32[160,128]{1,0:T(8,128)S(1)} collective-permute-done((f32[160,128]{1,0:T(8,128)S(1)}, f32[160,128]{1,0:T(8,128)S(1)}, u32[]{:S(2)}, u32[]{:S(2)}) %collective-permute-start.13) | collective-permute-done | bytes 81952 | tf_op jit(solution)/shard_map/ppermute | solution.py:586
  42.8 0.0 copy-done.2
  42.8 2.4 %finish.1 = (f32[2,128,512]{2,1,0:T(8,128)}, f32[2,64,512]{2,1,0:T(8,128)}) custom-call(s32[2,4]{1,0:T(2,128)S(1)} %copy-done.2, f32[160,128]{1,0:T(8,128)S(1)} %broadcast_add_fusion.3.refs_1_, f32[160,128]{1,0:T(8,128)S(1)} %collective-permute-done.13.refs_2_, bf16[2,192,256]{2,1,0:T(8,128)(2,1)S(1)} %get-tuple-element.43.refs_3_, ...), custom_call_target="tpu_custom_call" | custom-call | flops 452984832 | bytes 4620288 | tf_op jit(solution)/shard_map/finish/pallas_call | solution.py:139
  (10 shorter events, 0.1 us)
Async XLA Ops:
  0.6 4.9 %copy-start.1 = (s32[2,4]{1,0:T(2,128)S(1)}, s32[2,4]{1,0:T(2,128)}, u32[]{:S(2)}) copy-start(s32[2,4]{1,0:T(2,128)} %refs_0_.10) | copy-start | bytes 100
  0.6 10.2 %collective-permute-start.1 = (s32[2,4]{1,0:T(2,128)}, s32[2,4]{1,0:T(2,128)S(1)}, u32[]{:S(2)}, u32[]{:S(2)}) collective-permute-start(s32[2,4]{1,0:T(2,128)} %refs_0_.10), channel_id=1, source_target_pairs={{0,4},{4,8},{8,12},{12,16},{16,20},{20,24},{24,28},{28,0},{1,5},{5... | collective-permute-start | bytes 104 | tf_op jit(solution)/shard_map/ppermute | solution.py:462
  2.9 9.6 %collective-permute-start = (f32[64,768]{1,0:T(8,128)S(1)}, f32[64,768]{1,0:T(8,128)S(1)}, u32[]{:S(2)}, u32[]{:S(2)}) collective-permute-start(f32[64,768]{1,0:T(8,128)S(1)} %get-tuple-element.25.refs_0_.refs_1_.refs_8_), channel_id=1, source_target_pairs={{0,1},{1,2},{2,3},{3,0},{4,5},{5,6},{6,7},{7,4},{8,9},{9,10},{10,1... | collective-permute-start | bytes 589832 | tf_op jit(solution)/shard_map/ppermute | solution.py:462
  8.7 8.8 %collective-permute-start.3 = (f32[64,768]{1,0:T(8,128)S(1)}, f32[64,768]{1,0:T(8,128)S(1)}, u32[]{:S(2)}, u32[]{:S(2)}) collective-permute-start(f32[64,768]{1,0:T(8,128)S(1)} %broadcast_add_fusion.1), channel_id=1, source_target_pairs={{0,3},{1,0},{2,1},{3,2},{4,7},{5,4},{6,5},{7,6},{8,11},{9,8},{10,9... | collective-permute-start | bytes 589832 | tf_op jit(solution)/shard_map/ppermute | solution.py:462
  12.4 10.0 %collective-permute-start.2 = (f32[64,768]{1,0:T(8,128)S(1)}, f32[64,768]{1,0:T(8,128)S(1)}, u32[]{:S(2)}, u32[]{:S(2)}) collective-permute-start(f32[64,768]{1,0:T(8,128)S(1)} %broadcast_add_fusion.2), channel_id=1, source_target_pairs={{0,1},{1,2},{2,3},{3,0},{4,5},{5,6},{6,7},{7,4},{8,9},{9,10},{10,1... | collective-permute-start | bytes 589832 | tf_op jit(solution)/shard_map/ppermute | solution.py:462
  12.8 11.0 %collective-permute-start.4 = (f32[64,256]{1,0:T(8,128)S(1)}, f32[64,256]{1,0:T(8,128)S(1)}, u32[]{:S(2)}, u32[]{:S(2)}) collective-permute-start(f32[64,256]{1,0:T(8,128)S(1)} %broadcast_add_fusion.5.refs_12_), channel_id=1, source_target_pairs={{0,1},{1,2},{2,3},{3,0},{4,5},{5,6},{6,7},{7,4},{8,9},{9,10},{10,1... | collective-permute-start | bytes 196616 | tf_op jit(solution)/shard_map/ppermute | solution.py:462
  18.2 10.8 %copy-start = (f32[2,512,512]{2,1,0:T(8,128)S(1)}, f32[2,512,512]{2,1,0:T(8,128)}, u32[]{:S(2)}) copy-start(f32[2,512,512]{2,1,0:T(8,128)} %refs_0_.9) | copy-start | bytes 6291460
  23.9 2.5 %collective-permute-start.5 = (f32[512,256]{1,0:T(8,128)S(1)}, f32[512,256]{1,0:T(8,128)S(1)}, u32[]{:S(2)}, u32[]{:S(2)}) collective-permute-start(f32[512,256]{1,0:T(8,128)S(1)} %broadcast_add_fusion), channel_id=1, source_target_pairs={{0,4},{4,0},{8,12},{12,8},{16,20},{20,16},{24,28},{28,24},{1,5},{5... | collective-permute-start | bytes 1572872 | tf_op jit(solution)/shard_map/ppermute | solution.py:538
  24.3 5.3 %collective-permute-start.10 = (f32[64,256]{1,0:T(8,128)S(1)}, f32[64,256]{1,0:T(8,128)S(1)}, u32[]{:S(2)}, u32[]{:S(2)}) collective-permute-start(f32[64,256]{1,0:T(8,128)S(1)} %broadcast_add_fusion.5.refs_12_), channel_id=1, source_target_pairs={{0,3},{1,0},{2,1},{3,2},{4,7},{5,4},{6,5},{7,6},{8,11},{9,8},{10,9... | collective-permute-start | bytes 196616 | tf_op jit(solution)/shard_map/ppermute | solution.py:462
  26.2 6.1 %collective-permute-start.9 = (f32[64,256]{1,0:T(8,128)S(1)}, f32[64,256]{1,0:T(8,128)S(1)}, u32[]{:S(2)}, u32[]{:S(2)}) collective-permute-start(f32[64,256]{1,0:T(8,128)S(1)} %collective-permute-done.4.refs_13_), channel_id=1, source_target_pairs={{0,1},{1,2},{2,3},{3,0},{4,5},{5,6},{6,7},{7,4},{8,9},{9,10},{10,1... | collective-permute-start | bytes 196616 | tf_op jit(solution)/shard_map/ppermute | solution.py:462
  27.0 6.3 %collective-permute-start.6 = (f32[128,256]{1,0:T(8,128)S(1)}, f32[128,256]{1,0:T(8,128)S(1)}, u32[]{:S(2)}, u32[]{:S(2)}) collective-permute-start(f32[128,256]{1,0:T(8,128)S(1)} %get-tuple-element.35), channel_id=1, source_target_pairs={{0,8},{4,12},{8,0},{12,4},{16,24},{20,28},{24,16},{28,20},{1,9},{5... | collective-permute-start | bytes 393224 | tf_op jit(solution)/shard_map/ppermute | solution.py:588
  28.6 5.6 %collective-permute-start.8 = (f32[160,128]{1,0:T(8,128)S(1)}, f32[160,128]{1,0:T(8,128)S(1)}, u32[]{:S(2)}, u32[]{:S(2)}) collective-permute-start(f32[160,128]{1,0:T(8,128)S(1)} %get-tuple-element.36.refs_5_), channel_id=1, source_target_pairs={{0,8},{4,12},{8,0},{12,4},{16,24},{20,28},{24,16},{28,20},{1,9},{5... | collective-permute-start | bytes 245768 | tf_op jit(solution)/shard_map/ppermute | solution.py:582
  33.3 2.2 %collective-permute-start.7 = (f32[128,256]{1,0:T(8,128)S(1)}, f32[128,256]{1,0:T(8,128)S(1)}, u32[]{:S(2)}, u32[]{:S(2)}) collective-permute-start(f32[128,256]{1,0:T(8,128)S(1)} %collective-permute-done.6.refs_2_.refs_16_), channel_id=1, source_target_pairs={{0,4},{4,0},{8,12},{12,8},{16,20},{20,16},{24,28},{28,24},{1,5},{5... | collective-permute-start | bytes 393224 | tf_op jit(solution)/shard_map/ppermute | solution.py:591
  34.2 1.3 %collective-permute-start.11 = (f32[160,128]{1,0:T(8,128)S(1)}, f32[160,128]{1,0:T(8,128)S(1)}, u32[]{:S(2)}, u32[]{:S(2)}) collective-permute-start(f32[160,128]{1,0:T(8,128)S(1)} %broadcast_add_fusion.4.refs_4_.refs_18_), channel_id=1, source_target_pairs={{0,4},{4,0},{8,12},{12,8},{16,20},{20,16},{24,28},{28,24},{1,5},{5... | collective-permute-start | bytes 245768 | tf_op jit(solution)/shard_map/ppermute | solution.py:591
  36.4 5.0 %collective-permute-start.12 = (f32[160,128]{1,0:T(8,128)S(1)}, f32[160,128]{1,0:T(8,128)S(1)}, u32[]{:S(2)}, u32[]{:S(2)}) collective-permute-start(f32[160,128]{1,0:T(8,128)S(1)} %merge.1), channel_id=1, source_target_pairs={{0,16},{4,20},{8,24},{12,28},{16,0},{20,4},{24,8},{28,12},{1,17},{... | collective-permute-start | bytes 245768 | tf_op jit(solution)/shard_map/ppermute | solution.py:582
  38.1 4.6 %copy-start.2 = (s32[2,4]{1,0:T(2,128)S(1)}, s32[2,4]{1,0:T(2,128)}, u32[]{:S(2)}) copy-start(s32[2,4]{1,0:T(2,128)} %refs_0_.11) | copy-start | bytes 100
  41.4 1.3 %collective-permute-start.13 = (f32[160,128]{1,0:T(8,128)S(1)}, f32[160,128]{1,0:T(8,128)S(1)}, u32[]{:S(2)}, u32[]{:S(2)}) collective-permute-start(f32[160,128]{1,0:T(8,128)S(1)} %broadcast_add_fusion.3.refs_1_), channel_id=1, source_target_pairs={{0,4},{4,0},{8,12},{12,8},{16,20},{20,16},{24,28},{28,24},{1,5},{5... | collective-permute-start | bytes 245768 | tf_op jit(solution)/shard_map/ppermute | solution.py:586

commit v8 on v5

--- a/solution.py
+++ b/solution.py
@@ -35,12 +35,26 @@
 
 def pack(cov):
     half = cov.shape[0] // 2
-    return jnp.concatenate([cov[:half, :half], cov[:half, half:], cov[half:, half:]], 0)
+    part = half // 2
+    first, second = cov[:half, :half], cov[half:, half:]
+    lane = lax.broadcasted_iota(jnp.int32, (part, half), 1)
+    last = jnp.where(lane < part, pltpu.roll(first[part:], part, 1), second[part:])
+    return jnp.concatenate([cov[:half, half:], first[:part], second[:part], last], 0)
 
 
 def unpack(packed):
-    half = packed.shape[0] // 3
-    first, cross, second = packed[:half], packed[half : 2 * half], packed[2 * half :]
+    half = packed.shape[1]
+    part = half // 2
+    cross, last = packed[:half], packed[2 * half :]
+    row = lax.broadcasted_iota(jnp.int32, (half, half), 0)
+    lane = lax.broadcasted_iota(jnp.int32, (half, half), 1)
+
+    def symmetric(top, bottom):
+        upper = jnp.concatenate([top, bottom], 0)
+        return jnp.where((row < part) | (lane >= part), upper, upper.T)
+
+    first = symmetric(packed[half : half + part], pltpu.roll(last, part, 1))
+    second = symmetric(packed[half + part : 2 * half], last)
     top = jnp.concatenate([first, cross], 1)
     bottom = jnp.concatenate([cross.T, second], 1)
     return jnp.concatenate([top, bottom], 0)
@@ -94,7 +108,9 @@
     return [pl.BlockSpec(memory_space=pltpu.SMEM)] * count
 
 
-def call(kernel, outs, scalars, arrays, far=(), through=(), scratch=(), flops=0, mib=16, name=None):
+def call(
+    kernel, outs, scalars, arrays, far=(), out_far=False, through=(), scratch=(), flops=0, mib=16, name=None
+):
     moved = sum(a.size * 4 for a in (*arrays, *far)) + sum(o.size * 4 for o in outs)
     first = len(scalars) + len(arrays) + len(far)
     count = len(through)
@@ -109,7 +125,8 @@
         + vmem(len(arrays))
         + [pl.BlockSpec(memory_space=pltpu.HBM)] * len(far)
         + [pl.BlockSpec(memory_space=pl.ANY)] * count,
-        out_specs=vmem(len(outs)) + [pl.BlockSpec(memory_space=pl.ANY)] * count,
+        out_specs=([pl.BlockSpec(memory_space=pltpu.HBM)] * len(outs) if out_far else vmem(len(outs)))
+        + [pl.BlockSpec(memory_space=pl.ANY)] * count,
         scratch_shapes=list(scratch),
         input_output_aliases={first + i: len(outs) + i for i in range(count)},
         cost_estimate=pl.CostEstimate(flops=flops, bytes_accessed=moved, transcendentals=0),
@@ -152,18 +169,18 @@
     own_cols = own_ref.shape[0]
     own_at = pl.ds(pl.multiple_of(lax.axis_index("row") * own_cols, own_cols), own_cols)
     copy.wait()
-    picked_t = split(
+    picked = split(
         jnp.concatenate(
             [
-                two_blocks(tile_of(inv_ref), chosen[2 * t], chosen[2 * t + 1]).T
+                two_blocks(tile_of(inv_ref), chosen[2 * t], chosen[2 * t + 1])
                 for t in range(len(chosen) // 2)
             ],
-            0,
+            1,
         )
     )
-    pick_high_ref[...], pick_low_ref[...] = picked_t
-    base_ref[...] = mm(picked_t, picked_t, NT)
-    own_ref[...] = mm(inv_ref[:, own_at].T, inv_ref[...])
+    pick_high_ref[...], pick_low_ref[...] = picked
+    base_ref[...] = mm(picked, picked, TN)
+    own_ref[...] = mm(inv_ref[:, own_at], inv_ref[...], TN)
 
 
 def put_rows(mask_ref, panel, distance, part, take):
@@ -176,19 +193,19 @@
         take(kept, pl.ds(pl.multiple_of(slot * BLOCK, BLOCK), BLOCK))
 
 
-def links_kernel(distances, missing, mask_ref, *refs):
+def links_kernel(distances, mask_ref, *refs):
     parts, refs = refs[: len(distances)], refs[len(distances) :]
     *pick_refs, links_t_ref, rows_ref = refs
+    rows_ref[...] = jnp.zeros_like(rows_ref)
     for p in range(links_t_ref.shape[0]):
+        pick = (pick_refs[2 * p][...], pick_refs[2 * p + 1][...])
 
         def take(kept, at):
-            rows_ref[at, :] = kept
+            rows_ref[at, :] = mm(kept, pick)
 
         for d, part in zip(distances, parts):
             put_rows(mask_ref, p, d, part, take)
-        put_rows(mask_ref, p, missing, parts[0], lambda kept, at: take(jnp.zeros_like(kept), at))
-        pick = (pick_refs[2 * p][...], pick_refs[2 * p + 1][...])
-        links_t_ref[p] = mm(pick, rows_ref[...], NT)
+        links_t_ref[p] = rows_ref[...].T
 
 
 def segment_kernel(distance, panels, mask_ref, part, early_ref, *refs):
@@ -202,8 +219,8 @@
         pieces = [early_ref[p]]
 
         def take(kept, at):
-            late = mm(pick, jnp.concatenate([kept] * (size // BLOCK), 0), NT)
-            pieces.append(jnp.where(lane == at.start // BLOCK, late, pieces[-1]))
+            late_t = jnp.concatenate([mm(kept, pick)] * (size // BLOCK), 0).T
+            pieces.append(jnp.where(lane == at.start // BLOCK, late_t, pieces[-1]))
 
         put_rows(mask_ref, p, distance, part, take)
         own_t = pieces[-1]
@@ -288,7 +305,7 @@
     own_cols = own_refs[0].shape[0]
     size = base_refs[0].shape[0]
     row_at = lax.axis_index("row")
-    rows = left_high.shape[1] - own_cols
+    rows = left_high.shape[0] // panels - own_cols
     at_row = lax.broadcasted_iota(jnp.int32, (size, size), 0)
     at_col = lax.broadcasted_iota(jnp.int32, (size, size), 1)
     eye = (at_row == at_col).astype(F32)
@@ -316,7 +333,8 @@
         scratch[:, size:] = gain
         to_parts = split(to_t)
         left = jnp.concatenate([scratch[own_rows, :size], mm(own_t, to_parts)], 0)
-        left_high[p], left_low[p] = split(left)
+        part = slice(p * left.shape[0], (p + 1) * left.shape[0])
+        left_high[part, :], left_low[part, :] = split(left)
         right_high[p], right_low[p] = split(mm(to_parts, whole, TN))
         gains = jnp.concatenate([scratch[own_rows, size:], mm(own_t, gain)], 0)
         const = mm(gains, whole)
@@ -329,20 +347,30 @@
 
 
 def finish_kernel(levels, mask_ref, after_ref, after_other_ref, *refs):
-    left_high, left_low, right_high, right_low, const_ref, diag_ref, off_ref = refs
+    left_high, left_low, right_high, right_low, const_ref, diag_hbm, off_hbm = refs[:7]
+    diag_ref, off_ref, sems = refs[7:]
+    panels, total, _ = const_ref.shape
     rows = off_ref.shape[1]
     row_at = lax.axis_index("row")
     chip = lax.axis_index("seg") // 2
     after = from_halves(after_ref[...], after_other_ref[...])
-    after = split(unpack(jnp.where((chip & ((1 << levels) // 2)) == 0, after, 0.0)))
-    for p in range(const_ref.shape[0]):
-        left = (left_high[p], left_low[p])
+    after = unpack(jnp.where((chip & ((1 << levels) // 2)) == 0, after, 0.0))
+    inner = split(mm((left_high[...], left_low[...]), after))
+    copies = []
+    for p in range(panels):
+        part = slice(p * total, (p + 1) * total)
         right = (right_high[p], right_low[p])
-        result = mm(mm(left, after), right) + const_ref[p]
+        result = mm((inner[0][part], inner[1][part]), right) + const_ref[p]
         diag_ref[p] = result[rows:]
         for s in range(rows // BLOCK):
             keep = mask_ref[p, row_at * (rows // BLOCK) + s].astype(F32)
             off_ref[p, s * BLOCK : (s + 1) * BLOCK, :] = -result[s * BLOCK : (s + 1) * BLOCK] * keep
+        copies.append(pltpu.make_async_copy(diag_ref.at[p], diag_hbm.at[p], sems.at[p, 0]))
+        copies.append(pltpu.make_async_copy(off_ref.at[p], off_hbm.at[p], sems.at[p, 1]))
+        copies[-2].start()
+        copies[-1].start()
+    for copy in copies:
+        copy.wait()
 
 
 def body(fill_blocks, fill_mask, inv_diag, factor_off):
@@ -365,7 +393,7 @@
     ups = [factor_off, turn(factor_off, "row", 1)]
     for _ in range(1, row_count // 2):
         ups.append(turn(ups[-1] + jnp.minimum(jnp.min(prior_fill), 0).astype(F32), "row", 1))
-    pick = jax.ShapeDtypeStruct((chosen_cols, width), BF16)
+    pick = jax.ShapeDtypeStruct((width, chosen_cols), BF16)
     bases, priors, picks, tokens = [], [], [], []
     for p in range(panels):
         base, own_prior, *high_low, token = call(
@@ -389,11 +417,11 @@
     last = len(ups) - 1
     early = [d for d in range(row_count) if d != last]
     (links,) = call(
-        functools.partial(links_kernel, early, last),
+        functools.partial(links_kernel, early),
         [shape(panels, size, size)],
         [fill_mask],
         [*(parts[d] for d in early), *picks],
-        scratch=[pltpu.VMEM((size, width), F32)],
+        scratch=[pltpu.VMEM((size, chosen_cols), F32)],
         flops=6 * panels * size * size * width,
         name="links",
     )
@@ -402,7 +430,7 @@
         [shape(panels, size, size), shape(2 * size, size)],
         [fill_mask],
         [parts[last], links, *picks, *bases],
-        flops=6 * panels * size * size * width + 18 * (panels - 1) * size**3,
+        flops=6 * panels * rows * size * width + 18 * (panels - 1) * size**3,
         name="segment",
     )
     maps, maps_token = call(
@@ -418,7 +446,7 @@
     swap = [(i, i ^ 1) for i in range(seg_count)]
     other_whole = lax.ppermute(own_whole, "seg", swap)
     half = size // 2
-    half_packed = shape(3 * half // 2, half)
+    half_packed = shape(5 * half // 4, half)
     half_link = shape(half, size)
     link_t, cov, send, send_t = call(
         chip_kernel,
@@ -435,7 +463,7 @@
 
     def prepare():
         total = rows + own_cols
-        left = jax.ShapeDtypeStruct((panels, total, size), BF16)
+        left = jax.ShapeDtypeStruct((panels * total, size), BF16)
         right = jax.ShapeDtypeStruct((panels, size, width), BF16)
         return call(
             functools.partial(prepare_kernel, levels, panels),
@@ -487,6 +515,12 @@
         [shape(panels, own_cols, width), shape(panels, rows, width)],
         [fill_mask],
         [*after, *prepared],
+        out_far=True,
+        scratch=[
+            pltpu.VMEM((panels, own_cols, width), F32),
+            pltpu.VMEM((panels, rows, width), F32),
+            pltpu.SemaphoreType.DMA((panels, 2)),
+        ],
         flops=6 * panels * (rows + own_cols) * size * (size + width),
         name="finish",
     )

time: 46.9 us -> 46.1 us (0.983)
  waiting for transfers between devices: 17.7 us -> 16.8 us
    ppermute x2, waiting for transfers between devices: 2.37 us -> 1.69 us  [body(): got = lax.ppermute(send, 'seg', partner)]
where the time goes in v8:
time: 46.1 us; the launch traced here: 45.9 us
  waiting for transfers between devices  16.8 us (36%)
  Pallas kernels  16.6 us (36%)
  starting transfers between devices  9.64 us (21%)
  between operations  1.44 us (3%)
  local copies, waits for them, and re-layouts  0.7 us (2%)
  other arithmetic  0.69 us (1%)
    pallas_call x9, Pallas kernels, call(): pl.pallas_call(inner, out_shape=[*outs, *(jax.ShapeDtypeStruct(a.shape, a...  16.6 us
    ppermute x4, waiting for transfers between devices, turn(): lax.ppermute(x, axis, [(i, (i + distance) % count) for i in range(count)])  8.25 us
    ppermute x4, starting transfers between devices, turn(): lax.ppermute(x, axis, [(i, (i + distance) % count) for i in range(count)])  5.3 us
    ppermute x1, waiting for transfers between devices, body(): got_t = lax.ppermute(send_t, 'seg', partner)  2.77 us
    ppermute x2, starting transfers between devices, body(): got = lax.ppermute(send, 'seg', partner)  2.12 us
    ppermute x2, waiting for transfers between devices, body(): got = lax.ppermute(send, 'seg', partner)  1.69 us
    ppermute x1, starting transfers between devices, body(): got_t = lax.ppermute(send_t, 'seg', partner)  1.58 us
    ppermute x1, waiting for transfers between devices, body(): other_whole = lax.ppermute(own_whole, 'seg', swap)  1.54 us
  transfers between devices with their start and end apart: 11, of which 9 were waited for; matrix products, arithmetic and copies ran while one was open for 1% of the time, Pallas kernels for 24%

profile of v8, /device:TPU:0, one launch (start us, length us, event | category | flops | bytes accessed | tf_op | source)
XLA Modules:
  0.0 45.9 jit_solution(8957836018755862898)
XLA Ops:
  0.6 0.0 copy-start.1
  0.6 3.1 %collective-permute-start = (f32[2,64,512]{2,1,0:T(8,128)}, f32[2,64,512]{2,1,0:T(8,128)S(1)}, u32[]{:S(2)}, u32[]{:S(2)}) collective-permute-start(f32[2,64,512]{2,1,0:T(8,128)} %refs_2_.3), channel_id=1, source_target_pairs={{0,1},{1,2},{2,3},{3,0},{4,5},{5,6},{6,7},{7,4},{8,9},{9,10},{10,1... | collective-permute-start | bytes 786440 | tf_op jit(solution)/shard_map/ppermute | solution.py:390
  3.7 0.0 collective-permute-start.1
  3.7 0.0 copy-start.3
  3.7 0.7 %copy-done.3 = s32[2,4]{1,0:T(2,128)S(1)} copy-done((s32[2,4]{1,0:T(2,128)S(1)}, s32[2,4]{1,0:T(2,128)}, u32[]{:S(2)}) %copy-start.3) | copy-done | bytes 56
  4.4 0.0 copy-start.4
  4.4 2.8 %prior.2 = (f32[256,256]{1,0:T(8,128)S(1)}, f32[128,512]{1,0:T(8,128)S(1)}, bf16[512,256]{1,0:T(8,128)(2,1)S(1)}, bf16[512,256]{1,0:T(8,128)(2,1)S(1)}, f32[1,1,512]{2,1,0:T(1,128)S(1)}) custom-call(s32[2,4]{1,0:T(2,128)S(1)} %copy-done.3, f32[2,512,512]{2,1,0:T(8,128)} %refs_1_.5), custom_call_target="tpu_custom_call" | custom-call | flops 402653184 | bytes 3672064 | tf_op jit(solution)/shard_map/prior/pallas_call | solution.py:121
  7.2 0.0 copy-start.2
  7.2 0.0 copy-done.1
  7.2 2.2 %collective-permute-start.3 = (f32[2,64,512]{2,1,0:T(8,128)S(1)}, f32[2,64,512]{2,1,0:T(8,128)S(1)}, u32[]{:S(2)}, u32[]{:S(2)}) collective-permute-start(f32[2,64,512]{2,1,0:T(8,128)S(1)} %broadcast_add_fusion), channel_id=1, source_target_pairs={{0,3},{1,0},{2,1},{3,2},{4,7},{5,4},{6,5},{7,6},{8,11},{9,8},{10,9... | collective-permute-start | bytes 786440 | tf_op jit(solution)/shard_map/ppermute | solution.py:390
  9.4 0.0 collective-permute-done.1.refs_1_
  9.4 0.6 %reduce_min.9 = s32[]{:T(128)} reduce(s32[2,4]{1,0:T(2,128)S(1)} %collective-permute-done.1.refs_1_, s32[]{:T(128)} %constant.0.clone.1), dimensions={0,1}, to_apply=%region_0.0 | reduce | flops 7 | bytes 40 | tf_op jit(solution)/shard_map/reduce_min | solution.py:395
  10.7 1.7 %collective-permute-done.refs_2_.refs_3_ = f32[2,64,512]{2,1,0:T(8,128)S(1)} collective-permute-done((f32[2,64,512]{2,1,0:T(8,128)}, f32[2,64,512]{2,1,0:T(8,128)S(1)}, u32[]{:S(2)}, u32[]{:S(2)}) %collective-permute-start) | collective-permute-done | bytes 262176 | tf_op jit(solution)/shard_map/ppermute | solution.py:390
  12.4 0.1 collective-permute-start.2
  12.5 0.0 copy-done.4
  12.5 2.8 %prior.3 = (f32[256,256]{1,0:T(8,128)S(1)}, f32[128,512]{1,0:T(8,128)S(1)}, bf16[512,256]{1,0:T(8,128)(2,1)S(1)}, bf16[512,256]{1,0:T(8,128)(2,1)S(1)}, f32[1,1,512]{2,1,0:T(1,128)}) custom-call(s32[2,4]{1,0:T(2,128)S(1)} %copy-done.4, s32[2,4]{1,0:T(2,128)S(1)} %collective-permute-done.1.refs_1_, f32[2,512,512]{2,1,0:T(8,128)} %refs_1_.5), custom_call_target="tpu_custom_call" | custom-call | flops 402653184 | bytes 3672064 | tf_op jit(solution)/shard_map/prior/pallas_call | solution.py:121
  15.3 2.6 %collective-permute-done.3.refs_3_.refs_5_ = f32[2,64,512]{2,1,0:T(8,128)S(1)} collective-permute-done((f32[2,64,512]{2,1,0:T(8,128)S(1)}, f32[2,64,512]{2,1,0:T(8,128)S(1)}, u32[]{:S(2)}, u32[]{:S(2)}) %collective-permute-start.3) | collective-permute-done | bytes 262176 | tf_op jit(solution)/shard_map/ppermute | solution.py:390
  17.8 0.0 copy-done.2
  17.8 1.7 %links.1.refs_2_ = f32[2,256,256]{2,1,0:T(8,128)S(1)} custom-call(s32[2,4]{1,0:T(2,128)S(1)} %copy-done.2, f32[2,64,512]{2,1,0:T(8,128)S(1)} %copy-done.1, f32[2,64,512]{2,1,0:T(8,128)S(1)} %collective-permute-done.refs_2_.refs_3_, f32[2,64,512]{2,1,0:T(8,128)S(1)} %collective-permute-done.3.refs_3_.refs_5_, ...), custom_call_target="tpu_custom_call" | custom-call | flops 402653184 | bytes 3407872 | tf_op jit(solution)/shard_map/links/pallas_call | solution.py:121
  19.5 0.0 copy-start
  19.5 4.0 %collective-permute-done.2.refs_1_.refs_4_ = f32[2,64,512]{2,1,0:T(8,128)S(1)} collective-permute-done((f32[2,64,512]{2,1,0:T(8,128)S(1)}, f32[2,64,512]{2,1,0:T(8,128)S(1)}, u32[]{:S(2)}, u32[]{:S(2)}) %collective-permute-start.2) | collective-permute-done | bytes 262176 | tf_op jit(solution)/shard_map/ppermute | solution.py:390
  23.5 1.6 %segment.1 = (f32[2,256,256]{2,1,0:T(8,128)S(1)}, f32[512,256]{1,0:T(8,128)S(1)}) custom-call(s32[2,4]{1,0:T(2,128)S(1)} %copy-done.2, f32[2,64,512]{2,1,0:T(8,128)S(1)} %collective-permute-done.2.refs_1_.refs_4_, f32[2,256,256]{2,1,0:T(8,128)S(1)} %links.1.refs_2_, bf16[512,256]{1,0:T(8,128)(2,1)S(1)} %get-tuple-element.26.refs_4_.refs_3_, ...), custom_call_target="tpu_custom_call" | custom-call | flops 402653184 | bytes 4456448 | tf_op jit(solution)/shard_map/segment/pallas_call | solution.py:121
  25.1 0.5 %collective-permute-start.4 = (f32[512,256]{1,0:T(8,128)S(1)}, f32[512,256]{1,0:T(8,128)S(1)}, u32[]{:S(2)}, u32[]{:S(2)}) collective-permute-start(f32[512,256]{1,0:T(8,128)S(1)} %get-tuple-element.32.refs_0_), channel_id=1, source_target_pairs={{0,4},{4,0},{8,12},{12,8},{16,20},{20,16},{24,28},{28,24},{1,5},{5... | collective-permute-start | bytes 1572872 | tf_op jit(solution)/shard_map/ppermute | solution.py:447
  25.6 1.5 %collective-permute-done.4.refs_1_.refs_4_ = f32[512,256]{1,0:T(8,128)S(1)} collective-permute-done((f32[512,256]{1,0:T(8,128)S(1)}, f32[512,256]{1,0:T(8,128)S(1)}, u32[]{:S(2)}, u32[]{:S(2)}) %collective-permute-start.4) | collective-permute-done | bytes 524320 | tf_op jit(solution)/shard_map/ppermute | solution.py:447
  27.1 0.6 %chip.1 = (f32[256,256]{1,0:T(8,128)S(1)}, f32[256,256]{1,0:T(8,128)S(1)}, f32[160,128]{1,0:T(8,128)S(1)}, f32[128,256]{1,0:T(8,128)S(1)}) custom-call(f32[512,256]{1,0:T(8,128)S(1)} %get-tuple-element.32.refs_0_, f32[512,256]{1,0:T(8,128)S(1)} %collective-permute-done.4.refs_1_.refs_4_), custom_call_target="tpu_custom_call" | custom-call | flops 301989888 | bytes 1785856 | tf_op jit(solution)/shard_map/chip/pallas_call | solution.py:121
  27.7 1.6 %collective-permute-start.5 = (f32[128,256]{1,0:T(8,128)S(1)}, f32[128,256]{1,0:T(8,128)S(1)}, u32[]{:S(2)}, u32[]{:S(2)}) collective-permute-start(f32[128,256]{1,0:T(8,128)S(1)} %get-tuple-element.35), channel_id=1, source_target_pairs={{0,8},{4,12},{8,0},{12,4},{16,24},{20,28},{24,16},{28,20},{1,9},{5... | collective-permute-start | bytes 393224 | tf_op jit(solution)/shard_map/ppermute | solution.py:487
  29.3 0.5 %collective-permute-start.7 = (f32[160,128]{1,0:T(8,128)S(1)}, f32[160,128]{1,0:T(8,128)S(1)}, u32[]{:S(2)}, u32[]{:S(2)}) collective-permute-start(f32[160,128]{1,0:T(8,128)S(1)} %get-tuple-element.36), channel_id=1, source_target_pairs={{0,8},{4,12},{8,0},{12,4},{16,24},{20,28},{24,16},{28,20},{1,9},{5... | collective-permute-start | bytes 245768 | tf_op jit(solution)/shard_map/ppermute | solution.py:481
  29.8 0.0 copy-done
  29.8 1.5 %maps.1 = (f32[2,256,512]{2,1,0:T(8,128)S(1)}, f32[1,128]{1,0:T(1,128)S(1)}) custom-call(s32[2,4]{1,0:T(2,128)S(1)} %copy-done.2, f32[2,512,512]{2,1,0:T(8,128)S(1)} %copy-done, f32[2,64,512]{2,1,0:T(8,128)S(1)} %copy-done.1, f32[2,64,512]{2,1,0:T(8,128)S(1)} %collective-permute-done.refs_2_.refs_3_, ...), custom_call_target="tpu_custom_call" | custom-call | flops 805306368 | bytes 4194816 | tf_op jit(solution)/shard_map/maps/pallas_call | solution.py:121
  31.4 2.8 %collective-permute-done.5.refs_2_.refs_7_ = f32[128,256]{1,0:T(8,128)S(1)} collective-permute-done((f32[128,256]{1,0:T(8,128)S(1)}, f32[128,256]{1,0:T(8,128)S(1)}, u32[]{:S(2)}, u32[]{:S(2)}) %collective-permute-start.5) | collective-permute-done | bytes 131104 | tf_op jit(solution)/shard_map/ppermute | solution.py:487
  34.1 0.0 collective-permute-start.6
  34.1 1.2 %collective-permute-done.7 = f32[160,128]{1,0:T(8,128)S(1)} collective-permute-done((f32[160,128]{1,0:T(8,128)S(1)}, f32[160,128]{1,0:T(8,128)S(1)}, u32[]{:S(2)}, u32[]{:S(2)}) %collective-permute-start.7) | collective-permute-done | bytes 81952 | tf_op jit(solution)/shard_map/ppermute | solution.py:481
  35.3 0.1 collective-permute-start.8
  35.4 1.3 %collective-permute-done.8.refs_5_.refs_10_ = f32[160,128]{1,0:T(8,128)S(1)} collective-permute-done((f32[160,128]{1,0:T(8,128)S(1)}, f32[160,128]{1,0:T(8,128)S(1)}, u32[]{:S(2)}, u32[]{:S(2)}) %collective-permute-start.8) | collective-permute-done | bytes 81952 | tf_op jit(solution)/shard_map/ppermute | solution.py:490
  36.7 0.0 collective-permute-done.6.refs_3_.refs_8_
  36.7 0.8 %merge.1 = f32[160,128]{1,0:T(8,128)S(1)} custom-call(f32[256,256]{1,0:T(8,128)S(1)} %get-tuple-element.33.refs_0_, f32[256,256]{1,0:T(8,128)S(1)} %get-tuple-element.34.refs_1_, f32[128,256]{1,0:T(8,128)S(1)} %collective-permute-done.5.refs_2_.refs_7_, f32[128,256]{1,0:T(8,128)S(1)} %collective-permute-done.6.refs_3_.refs_8_, ...), custom_call_target="tpu_custom_call" | custom-call | flops 301989888 | bytes 1032192 | tf_op jit(solution)/shard_map/merge/pallas_call | solution.py:121
  37.5 1.6 %collective-permute-start.9 = (f32[160,128]{1,0:T(8,128)S(1)}, f32[160,128]{1,0:T(8,128)S(1)}, u32[]{:S(2)}, u32[]{:S(2)}) collective-permute-start(f32[160,128]{1,0:T(8,128)S(1)} %merge.1), channel_id=1, source_target_pairs={{0,16},{4,20},{8,24},{12,28},{16,0},{20,4},{24,8},{28,12},{1,17},{... | collective-permute-start | bytes 245768 | tf_op jit(solution)/shard_map/ppermute | solution.py:481
  39.1 2.5 %prepare.1 = (bf16[384,256]{1,0:T(8,128)(2,1)S(1)}, bf16[384,256]{1,0:T(8,128)(2,1)S(1)}, bf16[2,256,512]{2,1,0:T(8,128)(2,1)S(1)}, bf16[2,256,512]{2,1,0:T(8,12...) custom-call(f32[256,256]{1,0:T(8,128)S(1)} %get-tuple-element.30.refs_7_.refs_0_, ...), custom_call_target="tpu_custom_call" | custom-call | flops 1459617792 | bytes 7242240 | tf_op jit(solution)/shard_map/prepare/pallas_call | solution.py:121
  41.6 0.5 %collective-permute-done.9 = f32[160,128]{1,0:T(8,128)S(1)} collective-permute-done((f32[160,128]{1,0:T(8,128)S(1)}, f32[160,128]{1,0:T(8,128)S(1)}, u32[]{:S(2)}, u32[]{:S(2)}) %collective-permute-start.9) | collective-permute-done | bytes 81952 | tf_op jit(solution)/shard_map/ppermute | solution.py:481
  42.1 0.1 collective-permute-start.10
  42.1 1.3 %collective-permute-done.10.refs_2_ = f32[160,128]{1,0:T(8,128)S(1)} collective-permute-done((f32[160,128]{1,0:T(8,128)S(1)}, f32[160,128]{1,0:T(8,128)S(1)}, u32[]{:S(2)}, u32[]{:S(2)}) %collective-permute-start.10) | collective-permute-done | bytes 81952 | tf_op jit(solution)/shard_map/ppermute | solution.py:485
  43.4 2.4 %finish.1 = (f32[2,128,512]{2,1,0:T(8,128)}, f32[2,64,512]{2,1,0:T(8,128)}) custom-call(s32[2,4]{1,0:T(2,128)S(1)} %copy-done.2, f32[160,128]{1,0:T(8,128)S(1)} %broadcast_add_fusion.2.refs_1_, f32[160,128]{1,0:T(8,128)S(1)} %collective-permute-done.10.refs_2_, bf16[384,256]{1,0:T(8,128)(2,1)S(1)} %get-tuple-element.43.refs_3_, ...), custom_call_target="tpu_custom_call" | custom-call | flops 452984832 | bytes 4620288 | tf_op jit(solution)/shard_map/finish/pallas_call | solution.py:121
  (4 shorter events, 0.1 us)
Async XLA Ops:
  0.6 6.6 %copy-start.1 = (f32[2,64,512]{2,1,0:T(8,128)S(1)}, f32[2,64,512]{2,1,0:T(8,128)}, u32[]{:S(2)}) copy-start(f32[2,64,512]{2,1,0:T(8,128)} %refs_2_.3) | copy-start | bytes 786436
  0.6 11.7 %collective-permute-start = (f32[2,64,512]{2,1,0:T(8,128)}, f32[2,64,512]{2,1,0:T(8,128)S(1)}, u32[]{:S(2)}, u32[]{:S(2)}) collective-permute-start(f32[2,64,512]{2,1,0:T(8,128)} %refs_2_.3), channel_id=1, source_target_pairs={{0,1},{1,2},{2,3},{3,0},{4,5},{5,6},{6,7},{7,4},{8,9},{9,10},{10,1... | collective-permute-start | bytes 786440 | tf_op jit(solution)/shard_map/ppermute | solution.py:390
  3.7 5.7 %collective-permute-start.1 = (s32[2,4]{1,0:T(2,128)}, s32[2,4]{1,0:T(2,128)S(1)}, u32[]{:S(2)}, u32[]{:S(2)}) collective-permute-start(s32[2,4]{1,0:T(2,128)} %refs_0_.7), channel_id=1, source_target_pairs={{0,4},{4,8},{8,12},{12,16},{16,20},{20,24},{24,28},{28,0},{1,5},{5... | collective-permute-start | bytes 104 | tf_op jit(solution)/shard_map/ppermute | solution.py:390
  3.7 0.7 %copy-start.3 = (s32[2,4]{1,0:T(2,128)S(1)}, s32[2,4]{1,0:T(2,128)}, u32[]{:S(2)}) copy-start(s32[2,4]{1,0:T(2,128)} %refs_0_.7) | copy-start | bytes 100
  4.4 8.1 %copy-start.4 = (s32[2,4]{1,0:T(2,128)S(1)}, s32[2,4]{1,0:T(2,128)}, u32[]{:S(2)}) copy-start(s32[2,4]{1,0:T(2,128)} %refs_0_.7) | copy-start | bytes 100
  7.2 10.7 %copy-start.2 = (s32[2,4]{1,0:T(2,128)S(1)}, s32[2,4]{1,0:T(2,128)}, u32[]{:S(2)}) copy-start(s32[2,4]{1,0:T(2,128)} %refs_0_.11) | copy-start | bytes 100
  7.2 10.6 %collective-permute-start.3 = (f32[2,64,512]{2,1,0:T(8,128)S(1)}, f32[2,64,512]{2,1,0:T(8,128)S(1)}, u32[]{:S(2)}, u32[]{:S(2)}) collective-permute-start(f32[2,64,512]{2,1,0:T(8,128)S(1)} %broadcast_add_fusion), channel_id=1, source_target_pairs={{0,3},{1,0},{2,1},{3,2},{4,7},{5,4},{6,5},{7,6},{8,11},{9,8},{10,9... | collective-permute-start | bytes 786440 | tf_op jit(solution)/shard_map/ppermute | solution.py:390
  12.4 11.1 %collective-permute-start.2 = (f32[2,64,512]{2,1,0:T(8,128)S(1)}, f32[2,64,512]{2,1,0:T(8,128)S(1)}, u32[]{:S(2)}, u32[]{:S(2)}) collective-permute-start(f32[2,64,512]{2,1,0:T(8,128)S(1)} %broadcast_add_fusion.1), channel_id=1, source_target_pairs={{0,1},{1,2},{2,3},{3,0},{4,5},{5,6},{6,7},{7,4},{8,9},{9,10},{10,1... | collective-permute-start | bytes 786440 | tf_op jit(solution)/shard_map/ppermute | solution.py:390
  19.5 10.3 %copy-start = (f32[2,512,512]{2,1,0:T(8,128)S(1)}, f32[2,512,512]{2,1,0:T(8,128)}, u32[]{:S(2)}) copy-start(f32[2,512,512]{2,1,0:T(8,128)} %refs_1_.5) | copy-start | bytes 6291460
  25.1 2.0 %collective-permute-start.4 = (f32[512,256]{1,0:T(8,128)S(1)}, f32[512,256]{1,0:T(8,128)S(1)}, u32[]{:S(2)}, u32[]{:S(2)}) collective-permute-start(f32[512,256]{1,0:T(8,128)S(1)} %get-tuple-element.32.refs_0_), channel_id=1, source_target_pairs={{0,4},{4,0},{8,12},{12,8},{16,20},{20,16},{24,28},{28,24},{1,5},{5... | collective-permute-start | bytes 1572872 | tf_op jit(solution)/shard_map/ppermute | solution.py:447
  27.7 6.4 %collective-permute-start.5 = (f32[128,256]{1,0:T(8,128)S(1)}, f32[128,256]{1,0:T(8,128)S(1)}, u32[]{:S(2)}, u32[]{:S(2)}) collective-permute-start(f32[128,256]{1,0:T(8,128)S(1)} %get-tuple-element.35), channel_id=1, source_target_pairs={{0,8},{4,12},{8,0},{12,4},{16,24},{20,28},{24,16},{28,20},{1,9},{5... | collective-permute-start | bytes 393224 | tf_op jit(solution)/shard_map/ppermute | solution.py:487
  29.3 6.0 %collective-permute-start.7 = (f32[160,128]{1,0:T(8,128)S(1)}, f32[160,128]{1,0:T(8,128)S(1)}, u32[]{:S(2)}, u32[]{:S(2)}) collective-permute-start(f32[160,128]{1,0:T(8,128)S(1)} %get-tuple-element.36), channel_id=1, source_target_pairs={{0,8},{4,12},{8,0},{12,4},{16,24},{20,28},{24,16},{28,20},{1,9},{5... | collective-permute-start | bytes 245768 | tf_op jit(solution)/shard_map/ppermute | solution.py:481
  34.1 2.6 %collective-permute-start.6 = (f32[128,256]{1,0:T(8,128)S(1)}, f32[128,256]{1,0:T(8,128)S(1)}, u32[]{:S(2)}, u32[]{:S(2)}) collective-permute-start(f32[128,256]{1,0:T(8,128)S(1)} %collective-permute-done.5.refs_2_.refs_7_), channel_id=1, source_target_pairs={{0,4},{4,0},{8,12},{12,8},{16,20},{20,16},{24,28},{28,24},{1,5},{5... | collective-permute-start | bytes 393224 | tf_op jit(solution)/shard_map/ppermute | solution.py:490
  35.3 1.3 %collective-permute-start.8 = (f32[160,128]{1,0:T(8,128)S(1)}, f32[160,128]{1,0:T(8,128)S(1)}, u32[]{:S(2)}, u32[]{:S(2)}) collective-permute-start(f32[160,128]{1,0:T(8,128)S(1)} %broadcast_add_fusion.3.refs_4_.refs_9_), channel_id=1, source_target_pairs={{0,4},{4,0},{8,12},{12,8},{16,20},{20,16},{24,28},{28,24},{1,5},{5... | collective-permute-start | bytes 245768 | tf_op jit(solution)/shard_map/ppermute | solution.py:490
  37.5 4.6 %collective-permute-start.9 = (f32[160,128]{1,0:T(8,128)S(1)}, f32[160,128]{1,0:T(8,128)S(1)}, u32[]{:S(2)}, u32[]{:S(2)}) collective-permute-start(f32[160,128]{1,0:T(8,128)S(1)} %merge.1), channel_id=1, source_target_pairs={{0,16},{4,20},{8,24},{12,28},{16,0},{20,4},{24,8},{28,12},{1,17},{... | collective-permute-start | bytes 245768 | tf_op jit(solution)/shard_map/ppermute | solution.py:481
  42.1 1.3 %collective-permute-start.10 = (f32[160,128]{1,0:T(8,128)S(1)}, f32[160,128]{1,0:T(8,128)S(1)}, u32[]{:S(2)}, u32[]{:S(2)}) collective-permute-start(f32[160,128]{1,0:T(8,128)S(1)} %broadcast_add_fusion.2.refs_1_), channel_id=1, source_target_pairs={{0,4},{4,0},{8,12},{12,8},{16,20},{20,16},{24,28},{28,24},{1,5},{5... | collective-permute-start | bytes 245768 | tf_op jit(solution)/shard_map/ppermute | solution.py:485

commit v9 on v8

--- a/solution.py
+++ b/solution.py
@@ -1,4 +1,5 @@
 import functools
+from typing import NamedTuple
 
 import jax
 import jax.numpy as jnp
@@ -183,47 +184,67 @@
     own_ref[...] = mm(inv_ref[:, own_at], inv_ref[...], TN)
 
 
-def put_rows(mask_ref, panel, distance, part, take):
-    row_count = lax.axis_size("row")
-    rows = part.shape[1]
-    owner = lax.rem(lax.axis_index("row") + (row_count - distance), row_count)
-    for s in range(rows // BLOCK):
-        slot = owner * (rows // BLOCK) + s
-        kept = kept_rows(mask_ref, panel, slot, part[panel, s * BLOCK : (s + 1) * BLOCK, :])
-        take(kept, pl.ds(pl.multiple_of(slot * BLOCK, BLOCK), BLOCK))
-
-
-def links_kernel(distances, mask_ref, *refs):
-    parts, refs = refs[: len(distances)], refs[len(distances) :]
-    *pick_refs, links_t_ref, rows_ref = refs
+class Plan(NamedTuple):
+    early: tuple
+    late: tuple
+    late_from: tuple
+
+
+def at_row(table):
+    value = jnp.int32(table[0])
+    for i, entry in enumerate(table[1:], 1):
+        value = jnp.where(lax.axis_index("row") == i, entry, value)
+    return value
+
+
+def slots_of(owners, rows):
+    first = at_row(owners) * (rows // BLOCK)
+    return [first + s for s in range(rows // BLOCK)]
+
+
+def put_rows(mask_ref, panel, owners, part, out_ref, take):
+    for s, slot in enumerate(slots_of(owners, part.shape[0])):
+        kept = kept_rows(mask_ref, panel, slot, part[s * BLOCK : (s + 1) * BLOCK, :])
+        out_ref[pl.ds(pl.multiple_of(slot * BLOCK, BLOCK), BLOCK), :] = take(kept)
+
+
+def late_part(plan, refs, panel):
+    part = refs[0][panel]
+    for i, ref in enumerate(refs[1:], 1):
+        part = jnp.where(at_row(plan.late_from) == i, ref[panel], part)
+    return part
+
+
+def links_kernel(plan, mask_ref, *refs):
+    count = len(plan.early)
+    parts, refs = refs[:count], refs[count:]
+    *pick_refs, links_t_ref, late_keep_ref, rows_ref = refs
     rows_ref[...] = jnp.zeros_like(rows_ref)
     for p in range(links_t_ref.shape[0]):
         pick = (pick_refs[2 * p][...], pick_refs[2 * p + 1][...])
-
-        def take(kept, at):
-            rows_ref[at, :] = mm(kept, pick)
-
-        for d, part in zip(distances, parts):
-            put_rows(mask_ref, p, d, part, take)
+        for owners, part in zip(plan.early, parts):
+            put_rows(mask_ref, p, owners, part[p], rows_ref, lambda kept: mm(kept, pick))
         links_t_ref[p] = rows_ref[...].T
-
-
-def segment_kernel(distance, panels, mask_ref, part, early_ref, *refs):
+        for s, slot in enumerate(slots_of(plan.late, late_keep_ref.shape[1])):
+            block = slice(s * BLOCK, (s + 1) * BLOCK)
+            ones = jnp.ones((BLOCK, late_keep_ref.shape[2]), F32)
+            late_keep_ref[p, block, :] = kept_rows(mask_ref, p, slot, ones)
+
+
+def segment_kernel(plan, panels, *refs):
+    count = max(plan.late_from) + 1
+    late_refs, (early_ref, keep_ref), refs = refs[:count], refs[count : count + 2], refs[count + 2 :]
     pick_refs, base_refs = refs[: 2 * panels], refs[2 * panels : 3 * panels]
     links_t_ref, whole_ref = refs[3 * panels :]
     size = links_t_ref.shape[1]
-    lane = lax.broadcasted_iota(jnp.int32, (size, size), 1) // BLOCK
+    rows = keep_ref.shape[1]
+    here = lax.broadcasted_iota(jnp.int32, (size, size), 1) // rows == at_row(plan.late)
     cov = link_t = None
     for p in range(panels - 1, -1, -1):
         pick = (pick_refs[2 * p][...], pick_refs[2 * p + 1][...])
-        pieces = [early_ref[p]]
-
-        def take(kept, at):
-            late_t = jnp.concatenate([mm(kept, pick)] * (size // BLOCK), 0).T
-            pieces.append(jnp.where(lane == at.start // BLOCK, late_t, pieces[-1]))
-
-        put_rows(mask_ref, p, distance, part, take)
-        own_t = pieces[-1]
+        late = mm(late_part(plan, late_refs, p), pick) * keep_ref[p]
+        late_t = jnp.concatenate([late] * (size // rows), 0).T
+        own_t = jnp.where(here, late_t, early_ref[p])
         links_t_ref[p] = own_t
         if cov is None:
             cov, link_t = base_refs[p][...], own_t
@@ -235,16 +256,15 @@
     whole_ref[size:] = cov
 
 
-def maps_kernel(mask_ref, inv_ref, *refs):
-    *parts, maps_ref, token_ref, rows_ref = refs
+def maps_kernel(plan, mask_ref, inv_ref, *refs):
+    count = len(plan.early)
+    parts, late_refs = refs[:count], refs[count:-3]
+    maps_ref, token_ref, rows_ref = refs[-3:]
     token_ref[...] = jnp.zeros_like(token_ref)
     for p in range(inv_ref.shape[0]):
-
-        def take(kept, at):
-            rows_ref[at, :] = kept
-
-        for d, part in enumerate(parts):
-            put_rows(mask_ref, p, d, part, take)
+        for owners, part in zip(plan.early, parts):
+            put_rows(mask_ref, p, owners, part[p], rows_ref, lambda kept: kept)
+        put_rows(mask_ref, p, plan.late, late_part(plan, late_refs, p), rows_ref, lambda kept: kept)
         maps_ref[p] = triangular_mm(rows_ref[...], inv_ref[p])
 
 
@@ -296,7 +316,7 @@
         refs[9 + 2 * i][...] = jnp.where(is_lower(), whole[half:], whole[:half])
 
 
-def prepare_kernel(levels, panels, *refs):
+def prepare_kernel(levels, panels, mask_ref, *refs):
     base_refs, own_refs, refs = refs[:panels], refs[panels : 2 * panels], refs[2 * panels :]
     (other_ref, maps_ref, links_t_ref), refs = refs[:3], refs[3:]
     past_refs, refs = refs[: 4 * (levels > 1)], refs[4 * (levels > 1) :]
@@ -332,11 +352,18 @@
         scratch[:, :size] = to_t
         scratch[:, size:] = gain
         to_parts = split(to_t)
-        left = jnp.concatenate([scratch[own_rows, :size], mm(own_t, to_parts)], 0)
+        cross = jnp.concatenate(
+            [
+                jnp.full((BLOCK, size), -mask_ref[p, slot].astype(F32))
+                for slot in slots_of(tuple(range(size // rows)), rows)
+            ],
+            0,
+        )
+        left = jnp.concatenate([scratch[own_rows, :size] * cross, mm(own_t, to_parts)], 0)
         part = slice(p * left.shape[0], (p + 1) * left.shape[0])
         left_high[part, :], left_low[part, :] = split(left)
         right_high[p], right_low[p] = split(mm(to_parts, whole, TN))
-        gains = jnp.concatenate([scratch[own_rows, size:], mm(own_t, gain)], 0)
+        gains = jnp.concatenate([scratch[own_rows, size:] * cross, mm(own_t, gain)], 0)
         const = mm(gains, whole)
         const_ref[p, :rows, :] = const[:rows]
         const_ref[p, rows:, :] = const[rows:] + own_refs[p][...]
@@ -346,12 +373,11 @@
             gain = carry(link_t, gain, base_refs[p][...])
 
 
-def finish_kernel(levels, mask_ref, after_ref, after_other_ref, *refs):
+def finish_kernel(levels, after_ref, after_other_ref, *refs):
     left_high, left_low, right_high, right_low, const_ref, diag_hbm, off_hbm = refs[:7]
     diag_ref, off_ref, sems = refs[7:]
     panels, total, _ = const_ref.shape
     rows = off_ref.shape[1]
-    row_at = lax.axis_index("row")
     chip = lax.axis_index("seg") // 2
     after = from_halves(after_ref[...], after_other_ref[...])
     after = unpack(jnp.where((chip & ((1 << levels) // 2)) == 0, after, 0.0))
@@ -362,9 +388,7 @@
         right = (right_high[p], right_low[p])
         result = mm((inner[0][part], inner[1][part]), right) + const_ref[p]
         diag_ref[p] = result[rows:]
-        for s in range(rows // BLOCK):
-            keep = mask_ref[p, row_at * (rows // BLOCK) + s].astype(F32)
-            off_ref[p, s * BLOCK : (s + 1) * BLOCK, :] = -result[s * BLOCK : (s + 1) * BLOCK] * keep
+        off_ref[p] = result[:rows]
         copies.append(pltpu.make_async_copy(diag_ref.at[p], diag_hbm.at[p], sems.at[p, 0]))
         copies.append(pltpu.make_async_copy(off_ref.at[p], off_hbm.at[p], sems.at[p, 1]))
         copies[-2].start()
@@ -390,9 +414,6 @@
         return lax.ppermute(x, axis, [(i, (i + distance) % count) for i in range(count)])
 
     prior_fill = turn(fill_blocks, "seg", 1)
-    ups = [factor_off, turn(factor_off, "row", 1)]
-    for _ in range(1, row_count // 2):
-        ups.append(turn(ups[-1] + jnp.minimum(jnp.min(prior_fill), 0).astype(F32), "row", 1))
     pick = jax.ShapeDtypeStruct((width, chosen_cols), BF16)
     bases, priors, picks, tokens = [], [], [], []
     for p in range(panels):
@@ -410,34 +431,51 @@
         priors.append(own_prior)
         picks += high_low
         tokens.append(token)
-    downs = [factor_off + tokens[-1]]
-    for _ in range((row_count - 1) // 2):
-        downs.append(turn(downs[-1], "row", -1))
-    parts = ups + downs[:0:-1]
-    last = len(ups) - 1
-    early = [d for d in range(row_count) if d != last]
-    (links,) = call(
-        functools.partial(links_kernel, early),
-        [shape(panels, size, size)],
+    second = factor_off + tokens[-1]
+    index_gate = jnp.minimum(jnp.min(prior_fill), 0).astype(F32)
+
+    def step(x, targets):
+        return lax.ppermute(x, "row", list(enumerate(targets)))
+
+    if row_count == 4:
+        near = step(factor_off, (2, 0, 3, 1))
+        far = step(second, (1, 3, 0, 2))
+        lates = [step(second, (0, 2, 1, 3)), step(near + index_gate, (1, 0, 3, 2))]
+        parts = [factor_off, near, far]
+        plan = Plan(((0, 1, 2, 3), (1, 3, 0, 2), (2, 0, 3, 1)), (3, 2, 1, 0), (1, 0, 0, 1))
+    else:
+        ups, downs = [factor_off], [second]
+        for i in range(row_count // 2):
+            ups.append(turn(ups[-1] + index_gate if i else ups[-1], "row", 1))
+        for _ in range((row_count - 1) // 2):
+            downs.append(turn(downs[-1], "row", -1))
+        parts, lates = ups[:-1] + downs[:0:-1], ups[-1:]
+        far_off = len(ups) - 1
+        came = [d for d in range(row_count) if d != far_off]
+        whose = [tuple((i - d) % row_count for i in range(row_count)) for d in (*came, far_off)]
+        plan = Plan(tuple(whose[:-1]), whose[-1], (0,) * row_count)
+    links, late_keep = call(
+        functools.partial(links_kernel, plan),
+        [shape(panels, size, size), shape(panels, rows, size)],
         [fill_mask],
-        [*(parts[d] for d in early), *picks],
+        [*parts, *picks],
         scratch=[pltpu.VMEM((size, chosen_cols), F32)],
         flops=6 * panels * size * size * width,
         name="links",
     )
     links_t, own_whole = call(
-        functools.partial(segment_kernel, last, panels),
+        functools.partial(segment_kernel, plan, panels),
         [shape(panels, size, size), shape(2 * size, size)],
-        [fill_mask],
-        [parts[last], links, *picks, *bases],
+        [],
+        [*lates, links, late_keep, *picks, *bases],
         flops=6 * panels * rows * size * width + 18 * (panels - 1) * size**3,
         name="segment",
     )
     maps, maps_token = call(
-        maps_kernel,
+        functools.partial(maps_kernel, plan),
         [shape(panels, size, width), shape(1, half_cols)],
         [fill_mask],
-        [inv_diag, *parts],
+        [inv_diag, *parts, *lates],
         scratch=[pltpu.VMEM((size, width), F32)],
         flops=6 * panels * size * width * width,
         mib=24,
@@ -468,7 +506,7 @@
         return call(
             functools.partial(prepare_kernel, levels, panels),
             [left, left, right, right, shape(panels, total, width), shape(1, half_cols)],
-            [],
+            [fill_mask],
             [*bases, *priors, other_whole, maps, links_t, *(past or ())],
             scratch=[pltpu.VMEM((size, width), F32)],
             flops=6 * panels * size * (total * size + size * width + total * width + 3 * size * size),
@@ -513,7 +551,7 @@
     diag, off = call(
         functools.partial(finish_kernel, levels),
         [shape(panels, own_cols, width), shape(panels, rows, width)],
-        [fill_mask],
+        [],
         [*after, *prepared],
         out_far=True,
         scratch=[

time: 46.1 us -> 49.7 us (1.078)
  starting transfers between devices: 9.64 us -> 12.3 us
  waiting for transfers between devices: 16.8 us -> 18.3 us
  Pallas kernels: 16.6 us -> 16 us
    ppermute x0 -> x4, waiting for transfers between devices: none -> 10.2 us  [step(): return lax.ppermute(x, 'row', list(enumerate(targets)))]
    ppermute x0 -> x4, starting transfers between devices: none -> 8.28 us  [step(): return lax.ppermute(x, 'row', list(enumerate(targets)))]
    ppermute x4 -> x1, waiting for transfers between devices: 8.25 us -> 0.01 us  [turn(): lax.ppermute(x, axis, [(i, (i + distance) % count) for i in range(count)])]
    ppermute x4 -> x1, starting transfers between devices: 5.3 us -> 0.01 us  [turn(): lax.ppermute(x, axis, [(i, (i + distance) % count) for i in range(count)])]
    ppermute x2, waiting for transfers between devices: 1.69 us -> 0.95 us  [body(): got = lax.ppermute(send, 'seg', partner)]
    pallas_call x9, Pallas kernels: 16.6 us -> 16 us  [call(): pl.pallas_call(inner, out_shape=[*outs, *(jax.ShapeDtypeStruct(a.shape, a...]
  transfers between devices with their start and end apart: 11 -> 12, of which waited for: 9 -> 7; matrix products, arithmetic and copies ran while one was open for 1% -> 1% of each run, Pallas kernels for 24% -> 24%
where the time goes in v9:
time: 49.7 us; the launch traced here: 49.4 us
  waiting for transfers between devices  18.3 us (37%)
  Pallas kernels  16 us (32%)
  starting transfers between devices  12.3 us (25%)
  between operations  1.46 us (3%)
  local copies, waits for them, and re-layouts  0.7 us (1%)
  other arithmetic  0.69 us (1%)
    pallas_call x9, Pallas kernels, call(): pl.pallas_call(inner, out_shape=[*outs, *(jax.ShapeDtypeStruct(a.shape, a...  16 us
    ppermute x4, waiting for transfers between devices, step(): return lax.ppermute(x, 'row', list(enumerate(targets)))  10.2 us
    ppermute x4, starting transfers between devices, step(): return lax.ppermute(x, 'row', list(enumerate(targets)))  8.28 us
    ppermute x1, waiting for transfers between devices, body(): got_t = lax.ppermute(send_t, 'seg', partner)  2.8 us
    ppermute x2, starting transfers between devices, body(): got = lax.ppermute(send, 'seg', partner)  2.09 us
    ppermute x1, waiting for transfers between devices, body(): other_whole = lax.ppermute(own_whole, 'seg', swap)  1.79 us
    ppermute x1, starting transfers between devices, body(): got_t = lax.ppermute(send_t, 'seg', partner)  1.58 us
    ppermute x1, waiting for transfers between devices, body(): after = (got, lax.ppermute(got, 'seg', swap))  1.26 us
  transfers between devices with their start and end apart: 12, of which 7 were waited for; matrix products, arithmetic and copies ran while one was open for 1% of the time, Pallas kernels for 24%

profile of v9, /device:TPU:0, one launch (start us, length us, event | category | flops | bytes accessed | tf_op | source)
XLA Modules:
  0.0 49.4 jit_solution(6041503700545040821)
XLA Ops:
  0.6 0.0 copy-start.1
  0.6 4.1 %collective-permute-start.1 = (f32[2,64,512]{2,1,0:T(8,128)}, f32[2,64,512]{2,1,0:T(8,128)S(1)}, u32[]{:S(2)}, u32[]{:S(2)}) collective-permute-start(f32[2,64,512]{2,1,0:T(8,128)} %refs_2_.3), channel_id=1, source_target_pairs={{0,2},{1,0},{2,3},{3,1},{4,6},{5,4},{6,7},{7,5},{8,10},{9,8},{10,1... | collective-permute-start | bytes 786440 | tf_op jit(solution)/shard_map/ppermute | solution.py:438
  4.7 0.0 collective-permute-start.2
  4.7 0.0 copy-start.2
  4.7 0.7 %copy-done.2 = s32[2,4]{1,0:T(2,128)S(1)} copy-done((s32[2,4]{1,0:T(2,128)S(1)}, s32[2,4]{1,0:T(2,128)}, u32[]{:S(2)}) %copy-start.2) | copy-done | bytes 56
  5.4 0.0 copy-start.3
  5.4 2.8 %prior.2 = (f32[256,256]{1,0:T(8,128)S(1)}, f32[128,512]{1,0:T(8,128)S(1)}, bf16[512,256]{1,0:T(8,128)(2,1)S(1)}, bf16[512,256]{1,0:T(8,128)(2,1)S(1)}, f32[1,1,512]{2,1,0:T(1,128)S(1)}) custom-call(s32[2,4]{1,0:T(2,128)S(1)} %copy-done.2, f32[2,512,512]{2,1,0:T(8,128)} %refs_1_.5), custom_call_target="tpu_custom_call" | custom-call | flops 402653184 | bytes 3672064 | tf_op jit(solution)/shard_map/prior/pallas_call | solution.py:122
  8.2 0.0 copy-start.4
  8.2 0.0 copy-done.1
  8.2 0.7 %collective-permute-start = (f32[2,64,512]{2,1,0:T(8,128)S(1)}, f32[2,64,512]{2,1,0:T(8,128)S(1)}, u32[]{:S(2)}, u32[]{:S(2)}) collective-permute-start(f32[2,64,512]{2,1,0:T(8,128)S(1)} %broadcast_add_fusion.1), channel_id=1, source_target_pairs={{0,0},{1,2},{2,1},{3,3},{4,4},{5,6},{6,5},{7,7},{8,8},{9,10},{10,9... | collective-permute-start | bytes 786440 | tf_op jit(solution)/shard_map/ppermute | solution.py:438
  8.9 3.4 %collective-permute-start.4 = (f32[2,64,512]{2,1,0:T(8,128)S(1)}, f32[2,64,512]{2,1,0:T(8,128)S(1)}, u32[]{:S(2)}, u32[]{:S(2)}) collective-permute-start(f32[2,64,512]{2,1,0:T(8,128)S(1)} %broadcast_add_fusion.1), channel_id=1, source_target_pairs={{0,1},{1,3},{2,0},{3,2},{4,5},{5,7},{6,4},{7,6},{8,9},{9,11},{10,8... | collective-permute-start | bytes 786440 | tf_op jit(solution)/shard_map/ppermute | solution.py:438
  12.3 0.0 collective-permute-done.2.refs_1_
  12.4 0.6 %reduce_min.9 = s32[]{:T(128)} reduce(s32[2,4]{1,0:T(2,128)S(1)} %collective-permute-done.2.refs_1_, s32[]{:T(128)} %constant.0.clone.1), dimensions={0,1}, to_apply=%region_0.0 | reduce | flops 7 | bytes 40 | tf_op jit(solution)/shard_map/reduce_min | solution.py:435
  13.6 0.0 collective-permute-done.1.refs_2_.refs_3_
  13.7 0.1 collective-permute-start.3
  13.8 0.0 copy-done.3
  13.8 2.8 %prior.3 = (f32[256,256]{1,0:T(8,128)S(1)}, f32[128,512]{1,0:T(8,128)S(1)}, bf16[512,256]{1,0:T(8,128)(2,1)S(1)}, bf16[512,256]{1,0:T(8,128)(2,1)S(1)}, f32[1,1,512]{2,1,0:T(1,128)}) custom-call(s32[2,4]{1,0:T(2,128)S(1)} %copy-done.3, s32[2,4]{1,0:T(2,128)S(1)} %collective-permute-done.2.refs_1_, f32[2,512,512]{2,1,0:T(8,128)} %refs_1_.5), custom_call_target="tpu_custom_call" | custom-call | flops 402653184 | bytes 3672064 | tf_op jit(solution)/shard_map/prior/pallas_call | solution.py:122
  16.6 7.1 %collective-permute-done.4.refs_3_.refs_4_ = f32[2,64,512]{2,1,0:T(8,128)S(1)} collective-permute-done((f32[2,64,512]{2,1,0:T(8,128)S(1)}, f32[2,64,512]{2,1,0:T(8,128)S(1)}, u32[]{:S(2)}, u32[]{:S(2)}) %collective-permute-start.4) | collective-permute-done | bytes 262176 | tf_op jit(solution)/shard_map/ppermute | solution.py:438
  23.7 0.0 copy-done.4
  23.7 1.6 %links.1 = (f32[2,256,256]{2,1,0:T(8,128)S(1)}, f32[2,64,256]{2,1,0:T(8,128)S(1)}) custom-call(s32[2,4]{1,0:T(2,128)S(1)} %copy-done.4, f32[2,64,512]{2,1,0:T(8,128)S(1)} %copy-done.1, f32[2,64,512]{2,1,0:T(8,128)S(1)} %collective-permute-done.1.refs_2_.refs_3_, f32[2,64,512]{2,1,0:T(8,128)S(1)} %collective-permute-done.4.refs_3_.refs_4_, ...), custom_call_target="tpu_custom_call" | custom-call | flops 402653184 | bytes 3538944 | tf_op jit(solution)/shard_map/links/pallas_call | solution.py:122
  25.3 0.0 copy-start
  25.3 0.0 collective-permute-done.refs_0_.refs_5_
  25.3 3.1 %collective-permute-done.3.refs_1_.refs_6_ = f32[2,64,512]{2,1,0:T(8,128)S(1)} collective-permute-done((f32[2,64,512]{2,1,0:T(8,128)S(1)}, f32[2,64,512]{2,1,0:T(8,128)S(1)}, u32[]{:S(2)}, u32[]{:S(2)}) %collective-permute-start.3) | collective-permute-done | bytes 262176 | tf_op jit(solution)/shard_map/ppermute | solution.py:438
  28.4 1.0 %segment.1 = (f32[2,256,256]{2,1,0:T(8,128)S(1)}, f32[512,256]{1,0:T(8,128)S(1)}) custom-call(f32[2,64,512]{2,1,0:T(8,128)S(1)} %collective-permute-done.refs_0_.refs_5_, f32[2,64,512]{2,1,0:T(8,128)S(1)} %collective-permute-done.3.refs_1_.refs_6_, f32[2,256,256]{2,1,0:T(8,128)S(1)} %get-tuple-element.32.refs_2_, ...), custom_call_target="tpu_custom_call" | custom-call | flops 402653184 | bytes 4849664 | tf_op jit(solution)/shard_map/segment/pallas_call | solution.py:122
  29.4 0.2 collective-permute-start.5
  29.6 1.8 %collective-permute-done.5.refs_1_.refs_5_ = f32[512,256]{1,0:T(8,128)S(1)} collective-permute-done((f32[512,256]{1,0:T(8,128)S(1)}, f32[512,256]{1,0:T(8,128)S(1)}, u32[]{:S(2)}, u32[]{:S(2)}) %collective-permute-start.5) | collective-permute-done | bytes 524320 | tf_op jit(solution)/shard_map/ppermute | solution.py:485
  31.4 0.6 %chip.1 = (f32[256,256]{1,0:T(8,128)S(1)}, f32[256,256]{1,0:T(8,128)S(1)}, f32[160,128]{1,0:T(8,128)S(1)}, f32[128,256]{1,0:T(8,128)S(1)}) custom-call(f32[512,256]{1,0:T(8,128)S(1)} %get-tuple-element.36.refs_0_, f32[512,256]{1,0:T(8,128)S(1)} %collective-permute-done.5.refs_1_.refs_5_), custom_call_target="tpu_custom_call" | custom-call | flops 301989888 | bytes 1785856 | tf_op jit(solution)/shard_map/chip/pallas_call | solution.py:122
  32.0 1.6 %collective-permute-start.6 = (f32[128,256]{1,0:T(8,128)S(1)}, f32[128,256]{1,0:T(8,128)S(1)}, u32[]{:S(2)}, u32[]{:S(2)}) collective-permute-start(f32[128,256]{1,0:T(8,128)S(1)} %get-tuple-element.39), channel_id=1, source_target_pairs={{0,8},{4,12},{8,0},{12,4},{16,24},{20,28},{24,16},{28,20},{1,9},{5... | collective-permute-start | bytes 393224 | tf_op jit(solution)/shard_map/ppermute | solution.py:525
  33.6 0.5 %collective-permute-start.8 = (f32[160,128]{1,0:T(8,128)S(1)}, f32[160,128]{1,0:T(8,128)S(1)}, u32[]{:S(2)}, u32[]{:S(2)}) collective-permute-start(f32[160,128]{1,0:T(8,128)S(1)} %get-tuple-element.40), channel_id=1, source_target_pairs={{0,8},{4,12},{8,0},{12,4},{16,24},{20,28},{24,16},{28,20},{1,9},{5... | collective-permute-start | bytes 245768 | tf_op jit(solution)/shard_map/ppermute | solution.py:519
  34.1 0.0 copy-done
  34.1 1.5 %maps.1 = (f32[2,256,512]{2,1,0:T(8,128)S(1)}, f32[1,128]{1,0:T(1,128)S(1)}) custom-call(s32[2,4]{1,0:T(2,128)S(1)} %copy-done.4, f32[2,512,512]{2,1,0:T(8,128)S(1)} %copy-done, f32[2,64,512]{2,1,0:T(8,128)S(1)} %copy-done.1, f32[2,64,512]{2,1,0:T(8,128)S(1)} %collective-permute-done.1.refs_2_.refs_3_, ...), custom_call_target="tpu_custom_call" | custom-call | flops 805306368 | bytes 4456960 | tf_op jit(solution)/shard_map/maps/pallas_call | solution.py:122
  35.7 2.8 %collective-permute-done.6.refs_2_.refs_8_ = f32[128,256]{1,0:T(8,128)S(1)} collective-permute-done((f32[128,256]{1,0:T(8,128)S(1)}, f32[128,256]{1,0:T(8,128)S(1)}, u32[]{:S(2)}, u32[]{:S(2)}) %collective-permute-start.6) | collective-permute-done | bytes 131104 | tf_op jit(solution)/shard_map/ppermute | solution.py:525
  38.5 0.0 collective-permute-start.7
  38.5 0.9 %collective-permute-done.8 = f32[160,128]{1,0:T(8,128)S(1)} collective-permute-done((f32[160,128]{1,0:T(8,128)S(1)}, f32[160,128]{1,0:T(8,128)S(1)}, u32[]{:S(2)}, u32[]{:S(2)}) %collective-permute-start.8) | collective-permute-done | bytes 81952 | tf_op jit(solution)/shard_map/ppermute | solution.py:519
  39.4 0.1 collective-permute-start.9
  39.5 1.3 %collective-permute-done.9.refs_5_.refs_11_ = f32[160,128]{1,0:T(8,128)S(1)} collective-permute-done((f32[160,128]{1,0:T(8,128)S(1)}, f32[160,128]{1,0:T(8,128)S(1)}, u32[]{:S(2)}, u32[]{:S(2)}) %collective-permute-start.9) | collective-permute-done | bytes 81952 | tf_op jit(solution)/shard_map/ppermute | solution.py:528
  40.8 0.0 collective-permute-done.7.refs_3_.refs_9_
  40.8 0.8 %merge.1 = f32[160,128]{1,0:T(8,128)S(1)} custom-call(f32[256,256]{1,0:T(8,128)S(1)} %get-tuple-element.37.refs_0_, f32[256,256]{1,0:T(8,128)S(1)} %get-tuple-element.38.refs_1_, f32[128,256]{1,0:T(8,128)S(1)} %collective-permute-done.6.refs_2_.refs_8_, f32[128,256]{1,0:T(8,128)S(1)} %collective-permute-done.7.refs_3_.refs_9_, ...), custom_call_target="tpu_custom_call" | custom-call | flops 301989888 | bytes 1032192 | tf_op jit(solution)/shard_map/merge/pallas_call | solution.py:122
  41.6 1.6 %collective-permute-start.10 = (f32[160,128]{1,0:T(8,128)S(1)}, f32[160,128]{1,0:T(8,128)S(1)}, u32[]{:S(2)}, u32[]{:S(2)}) collective-permute-start(f32[160,128]{1,0:T(8,128)S(1)} %merge.1), channel_id=1, source_target_pairs={{0,16},{4,20},{8,24},{12,28},{16,0},{20,4},{24,8},{28,12},{1,17},{... | collective-permute-start | bytes 245768 | tf_op jit(solution)/shard_map/ppermute | solution.py:519
  43.2 3.0 %prepare.1 = (bf16[384,256]{1,0:T(8,128)(2,1)S(1)}, bf16[384,256]{1,0:T(8,128)(2,1)S(1)}, bf16[2,256,512]{2,1,0:T(8,128)(2,1)S(1)}, bf16[2,256,512]{2,1,0:T(8,12...) custom-call(s32[2,4]{1,0:T(2,128)S(1)} %copy-done.4, f32[256,256]{1,0:T(8,128)S(1)} %get-tuple-element.34.refs_8_.refs_1_, ...), custom_call_target="tpu_custom_call" | custom-call | flops 1459617792 | bytes 7242240 | tf_op jit(solution)/shard_map/prepare/pallas_call | solution.py:122
  46.2 0.0 collective-permute-done.10
  46.2 0.1 collective-permute-start.11
  46.3 1.3 %collective-permute-done.11.refs_1_ = f32[160,128]{1,0:T(8,128)S(1)} collective-permute-done((f32[160,128]{1,0:T(8,128)S(1)}, f32[160,128]{1,0:T(8,128)S(1)}, u32[]{:S(2)}, u32[]{:S(2)}) %collective-permute-start.11) | collective-permute-done | bytes 81952 | tf_op jit(solution)/shard_map/ppermute | solution.py:523
  47.6 1.9 %finish.1 = (f32[2,128,512]{2,1,0:T(8,128)}, f32[2,64,512]{2,1,0:T(8,128)}) custom-call(f32[160,128]{1,0:T(8,128)S(1)} %broadcast_add_fusion.2.refs_0_, f32[160,128]{1,0:T(8,128)S(1)} %collective-permute-done.11.refs_1_, bf16[384,256]{1,0:T(8,128)(2,1)S(1)} %get-tuple-element.47.refs_2_, bf16[384,256]{1,0:T(8,128)(2,1)S(1)} %get-tuple-element.48.refs_3_, ...), custom_call_target="tpu_custom_call" | custom-call | flops 452984832 | bytes 4620288 | tf_op jit(solution)/shard_map/finish/pallas_call | solution.py:122
  (4 shorter events, 0.1 us)
Async XLA Ops:
  0.6 7.6 %copy-start.1 = (f32[2,64,512]{2,1,0:T(8,128)S(1)}, f32[2,64,512]{2,1,0:T(8,128)}, u32[]{:S(2)}) copy-start(f32[2,64,512]{2,1,0:T(8,128)} %refs_2_.3) | copy-start | bytes 786436
  0.6 13.0 %collective-permute-start.1 = (f32[2,64,512]{2,1,0:T(8,128)}, f32[2,64,512]{2,1,0:T(8,128)S(1)}, u32[]{:S(2)}, u32[]{:S(2)}) collective-permute-start(f32[2,64,512]{2,1,0:T(8,128)} %refs_2_.3), channel_id=1, source_target_pairs={{0,2},{1,0},{2,3},{3,1},{4,6},{5,4},{6,7},{7,5},{8,10},{9,8},{10,1... | collective-permute-start | bytes 786440 | tf_op jit(solution)/shard_map/ppermute | solution.py:438
  4.7 7.6 %collective-permute-start.2 = (s32[2,4]{1,0:T(2,128)}, s32[2,4]{1,0:T(2,128)S(1)}, u32[]{:S(2)}, u32[]{:S(2)}) collective-permute-start(s32[2,4]{1,0:T(2,128)} %refs_0_.6), channel_id=1, source_target_pairs={{0,4},{4,8},{8,12},{12,16},{16,20},{20,24},{24,28},{28,0},{1,5},{5... | collective-permute-start | bytes 104 | tf_op jit(solution)/shard_map/ppermute | solution.py:414
  4.7 0.7 %copy-start.2 = (s32[2,4]{1,0:T(2,128)S(1)}, s32[2,4]{1,0:T(2,128)}, u32[]{:S(2)}) copy-start(s32[2,4]{1,0:T(2,128)} %refs_0_.6) | copy-start | bytes 100
  5.4 8.4 %copy-start.3 = (s32[2,4]{1,0:T(2,128)S(1)}, s32[2,4]{1,0:T(2,128)}, u32[]{:S(2)}) copy-start(s32[2,4]{1,0:T(2,128)} %refs_0_.6) | copy-start | bytes 100
  8.2 15.5 %copy-start.4 = (s32[2,4]{1,0:T(2,128)S(1)}, s32[2,4]{1,0:T(2,128)}, u32[]{:S(2)}) copy-start(s32[2,4]{1,0:T(2,128)} %refs_0_.9) | copy-start | bytes 100
  8.2 17.1 %collective-permute-start = (f32[2,64,512]{2,1,0:T(8,128)S(1)}, f32[2,64,512]{2,1,0:T(8,128)S(1)}, u32[]{:S(2)}, u32[]{:S(2)}) collective-permute-start(f32[2,64,512]{2,1,0:T(8,128)S(1)} %broadcast_add_fusion.1), channel_id=1, source_target_pairs={{0,0},{1,2},{2,1},{3,3},{4,4},{5,6},{6,5},{7,7},{8,8},{9,10},{10,9... | collective-permute-start | bytes 786440 | tf_op jit(solution)/shard_map/ppermute | solution.py:438
  8.9 14.7 %collective-permute-start.4 = (f32[2,64,512]{2,1,0:T(8,128)S(1)}, f32[2,64,512]{2,1,0:T(8,128)S(1)}, u32[]{:S(2)}, u32[]{:S(2)}) collective-permute-start(f32[2,64,512]{2,1,0:T(8,128)S(1)} %broadcast_add_fusion.1), channel_id=1, source_target_pairs={{0,1},{1,3},{2,0},{3,2},{4,5},{5,7},{6,4},{7,6},{8,9},{9,11},{10,8... | collective-permute-start | bytes 786440 | tf_op jit(solution)/shard_map/ppermute | solution.py:438
  13.7 14.8 %collective-permute-start.3 = (f32[2,64,512]{2,1,0:T(8,128)S(1)}, f32[2,64,512]{2,1,0:T(8,128)S(1)}, u32[]{:S(2)}, u32[]{:S(2)}) collective-permute-start(f32[2,64,512]{2,1,0:T(8,128)S(1)} %broadcast_add_fusion), channel_id=1, source_target_pairs={{0,1},{1,0},{2,3},{3,2},{4,5},{5,4},{6,7},{7,6},{8,9},{9,8},{10,11... | collective-permute-start | bytes 786440 | tf_op jit(solution)/shard_map/ppermute | solution.py:438
  25.3 8.8 %copy-start = (f32[2,512,512]{2,1,0:T(8,128)S(1)}, f32[2,512,512]{2,1,0:T(8,128)}, u32[]{:S(2)}) copy-start(f32[2,512,512]{2,1,0:T(8,128)} %refs_1_.5) | copy-start | bytes 6291460
  29.4 2.0 %collective-permute-start.5 = (f32[512,256]{1,0:T(8,128)S(1)}, f32[512,256]{1,0:T(8,128)S(1)}, u32[]{:S(2)}, u32[]{:S(2)}) collective-permute-start(f32[512,256]{1,0:T(8,128)S(1)} %get-tuple-element.36.refs_0_), channel_id=1, source_target_pairs={{0,4},{4,0},{8,12},{12,8},{16,20},{20,16},{24,28},{28,24},{1,5},{5... | collective-permute-start | bytes 1572872 | tf_op jit(solution)/shard_map/ppermute | solution.py:485
  32.0 6.4 %collective-permute-start.6 = (f32[128,256]{1,0:T(8,128)S(1)}, f32[128,256]{1,0:T(8,128)S(1)}, u32[]{:S(2)}, u32[]{:S(2)}) collective-permute-start(f32[128,256]{1,0:T(8,128)S(1)} %get-tuple-element.39), channel_id=1, source_target_pairs={{0,8},{4,12},{8,0},{12,4},{16,24},{20,28},{24,16},{28,20},{1,9},{5... | collective-permute-start | bytes 393224 | tf_op jit(solution)/shard_map/ppermute | solution.py:525
  33.6 5.8 %collective-permute-start.8 = (f32[160,128]{1,0:T(8,128)S(1)}, f32[160,128]{1,0:T(8,128)S(1)}, u32[]{:S(2)}, u32[]{:S(2)}) collective-permute-start(f32[160,128]{1,0:T(8,128)S(1)} %get-tuple-element.40), channel_id=1, source_target_pairs={{0,8},{4,12},{8,0},{12,4},{16,24},{20,28},{24,16},{28,20},{1,9},{5... | collective-permute-start | bytes 245768 | tf_op jit(solution)/shard_map/ppermute | solution.py:519
  38.5 2.3 %collective-permute-start.7 = (f32[128,256]{1,0:T(8,128)S(1)}, f32[128,256]{1,0:T(8,128)S(1)}, u32[]{:S(2)}, u32[]{:S(2)}) collective-permute-start(f32[128,256]{1,0:T(8,128)S(1)} %collective-permute-done.6.refs_2_.refs_8_), channel_id=1, source_target_pairs={{0,4},{4,0},{8,12},{12,8},{16,20},{20,16},{24,28},{28,24},{1,5},{5... | collective-permute-start | bytes 393224 | tf_op jit(solution)/shard_map/ppermute | solution.py:528
  39.4 1.3 %collective-permute-start.9 = (f32[160,128]{1,0:T(8,128)S(1)}, f32[160,128]{1,0:T(8,128)S(1)}, u32[]{:S(2)}, u32[]{:S(2)}) collective-permute-start(f32[160,128]{1,0:T(8,128)S(1)} %broadcast_add_fusion.3.refs_4_.refs_10_), channel_id=1, source_target_pairs={{0,4},{4,0},{8,12},{12,8},{16,20},{20,16},{24,28},{28,24},{1,5},{5... | collective-permute-start | bytes 245768 | tf_op jit(solution)/shard_map/ppermute | solution.py:528
  41.6 4.6 %collective-permute-start.10 = (f32[160,128]{1,0:T(8,128)S(1)}, f32[160,128]{1,0:T(8,128)S(1)}, u32[]{:S(2)}, u32[]{:S(2)}) collective-permute-start(f32[160,128]{1,0:T(8,128)S(1)} %merge.1), channel_id=1, source_target_pairs={{0,16},{4,20},{8,24},{12,28},{16,0},{20,4},{24,8},{28,12},{1,17},{... | collective-permute-start | bytes 245768 | tf_op jit(solution)/shard_map/ppermute | solution.py:519
  46.2 1.3 %collective-permute-start.11 = (f32[160,128]{1,0:T(8,128)S(1)}, f32[160,128]{1,0:T(8,128)S(1)}, u32[]{:S(2)}, u32[]{:S(2)}) collective-permute-start(f32[160,128]{1,0:T(8,128)S(1)} %broadcast_add_fusion.2.refs_0_), channel_id=1, source_target_pairs={{0,4},{4,0},{8,12},{12,8},{16,20},{20,16},{24,28},{28,24},{1,5},{5... | collective-permute-start | bytes 245768 | tf_op jit(solution)/shard_map/ppermute | solution.py:523

commit v10 on v9

--- a/solution.py
+++ b/solution.py
@@ -59,6 +59,16 @@
     top = jnp.concatenate([first, cross], 1)
     bottom = jnp.concatenate([cross.T, second], 1)
     return jnp.concatenate([top, bottom], 0)
+
+
+def widen(packed):
+    rows = packed.shape[0] // 2
+    return jnp.concatenate([packed[:rows], packed[rows:]], 1)
+
+
+def narrow(wide):
+    columns = wide.shape[1] // 2
+    return jnp.concatenate([wide[:, :columns], wide[:, columns:]], 0)
 
 
 def is_lower():
@@ -187,7 +197,6 @@
 class Plan(NamedTuple):
     early: tuple
     late: tuple
-    late_from: tuple
 
 
 def at_row(table):
@@ -206,13 +215,6 @@
     for s, slot in enumerate(slots_of(owners, part.shape[0])):
         kept = kept_rows(mask_ref, panel, slot, part[s * BLOCK : (s + 1) * BLOCK, :])
         out_ref[pl.ds(pl.multiple_of(slot * BLOCK, BLOCK), BLOCK), :] = take(kept)
-
-
-def late_part(plan, refs, panel):
-    part = refs[0][panel]
-    for i, ref in enumerate(refs[1:], 1):
-        part = jnp.where(at_row(plan.late_from) == i, ref[panel], part)
-    return part
 
 
 def links_kernel(plan, mask_ref, *refs):
@@ -232,17 +234,16 @@
 
 
 def segment_kernel(plan, panels, *refs):
-    count = max(plan.late_from) + 1
-    late_refs, (early_ref, keep_ref), refs = refs[:count], refs[count : count + 2], refs[count + 2 :]
+    late_ref, early_ref, keep_ref, *refs = refs
     pick_refs, base_refs = refs[: 2 * panels], refs[2 * panels : 3 * panels]
-    links_t_ref, whole_ref = refs[3 * panels :]
+    links_t_ref, whole_ref, cov_ref = refs[3 * panels :]
     size = links_t_ref.shape[1]
     rows = keep_ref.shape[1]
     here = lax.broadcasted_iota(jnp.int32, (size, size), 1) // rows == at_row(plan.late)
     cov = link_t = None
     for p in range(panels - 1, -1, -1):
         pick = (pick_refs[2 * p][...], pick_refs[2 * p + 1][...])
-        late = mm(late_part(plan, late_refs, p), pick) * keep_ref[p]
+        late = mm(late_ref[p], pick) * keep_ref[p]
         late_t = jnp.concatenate([late] * (size // rows), 0).T
         own_t = jnp.where(here, late_t, early_ref[p])
         links_t_ref[p] = own_t
@@ -253,30 +254,29 @@
             cov = carry(own_t, cov, base_refs[p][...])
             link_t = mm(own_t, link_t)
     whole_ref[:size] = link_t
-    whole_ref[size:] = cov
+    whole_ref[size:] = widen(pack(cov))
+    cov_ref[...] = cov
 
 
 def maps_kernel(plan, mask_ref, inv_ref, *refs):
     count = len(plan.early)
-    parts, late_refs = refs[:count], refs[count:-3]
-    maps_ref, token_ref, rows_ref = refs[-3:]
+    parts, (late_ref, maps_ref, token_ref, rows_ref) = refs[:count], refs[count:]
     token_ref[...] = jnp.zeros_like(token_ref)
     for p in range(inv_ref.shape[0]):
         for owners, part in zip(plan.early, parts):
             put_rows(mask_ref, p, owners, part[p], rows_ref, lambda kept: kept)
-        put_rows(mask_ref, p, plan.late, late_part(plan, late_refs, p), rows_ref, lambda kept: kept)
+        put_rows(mask_ref, p, plan.late, late_ref[p], rows_ref, lambda kept: kept)
         maps_ref[p] = triangular_mm(rows_ref[...], inv_ref[p])
 
 
-def chip_kernel(own_ref, other_ref, link_t_ref, cov_ref, packed_ref, half_t_ref):
+def chip_kernel(own_ref, own_cov_ref, other_ref, link_t_ref, cov_ref, packed_ref, half_t_ref):
     size = cov_ref.shape[0]
     lower = is_lower()
-    own, other = own_ref[...], other_ref[...]
-    down = jnp.where(lower, own, other)
-    up = jnp.where(lower, other, own)
-    down_t = split(down[:size])
-    cov = carry(down_t, up[size:], down[size:])
-    link_t = mm(down_t, up[:size])
+    own_t, other_t = own_ref[:size, :], other_ref[:size, :]
+    own, other = own_cov_ref[...], unpack(narrow(other_ref[size:, :]))
+    down_t = split(jnp.where(lower, own_t, other_t))
+    cov = carry(down_t, jnp.where(lower, other, own), jnp.where(lower, own, other))
+    link_t = mm(down_t, jnp.where(lower, other_t, own_t))
     link_t_ref[...] = link_t
     cov_ref[...] = cov
     packed_ref[...] = own_half(pack(cov))
@@ -329,6 +329,7 @@
     at_row = lax.broadcasted_iota(jnp.int32, (size, size), 0)
     at_col = lax.broadcasted_iota(jnp.int32, (size, size), 1)
     eye = (at_row == at_col).astype(F32)
+    other = unpack(narrow(other_ref[size:, :]))
     lower = is_lower()
     if past_refs:
         chip = lax.axis_index("seg") // 2
@@ -340,10 +341,10 @@
         gain = jnp.where(known, past, 0.0)
         other_t = split(other_ref[:size, :])
         to_t = jnp.where(lower, mm(other_t, to_t), to_t)
-        gain = jnp.where(lower, carry(other_t, gain, other_ref[size:, :]), gain)
+        gain = jnp.where(lower, carry(other_t, gain, other), gain)
     else:
         to_t = jnp.where(lower, other_ref[:size, :], eye)
-        gain = jnp.where(lower, other_ref[size:, :], 0.0)
+        gain = jnp.where(lower, other, 0.0)
     own_at = pl.ds(pl.multiple_of(row_at * own_cols, own_cols), own_cols)
     own_rows = pl.ds(pl.multiple_of(row_at * rows, rows), rows)
     for p in range(panels - 1, -1, -1):
@@ -407,7 +408,7 @@
     slots = fill_blocks.shape[1]
     chosen_cols = slots * BLOCK
     chips = seg_count // 2
-    half_cols = size // 2
+    half = size // 2
 
     def turn(x, axis, distance):
         count = lax.axis_size(axis)
@@ -434,26 +435,17 @@
     second = factor_off + tokens[-1]
     index_gate = jnp.minimum(jnp.min(prior_fill), 0).astype(F32)
 
-    def step(x, targets):
-        return lax.ppermute(x, "row", list(enumerate(targets)))
-
-    if row_count == 4:
-        near = step(factor_off, (2, 0, 3, 1))
-        far = step(second, (1, 3, 0, 2))
-        lates = [step(second, (0, 2, 1, 3)), step(near + index_gate, (1, 0, 3, 2))]
-        parts = [factor_off, near, far]
-        plan = Plan(((0, 1, 2, 3), (1, 3, 0, 2), (2, 0, 3, 1)), (3, 2, 1, 0), (1, 0, 0, 1))
-    else:
-        ups, downs = [factor_off], [second]
-        for i in range(row_count // 2):
-            ups.append(turn(ups[-1] + index_gate if i else ups[-1], "row", 1))
-        for _ in range((row_count - 1) // 2):
-            downs.append(turn(downs[-1], "row", -1))
-        parts, lates = ups[:-1] + downs[:0:-1], ups[-1:]
-        far_off = len(ups) - 1
-        came = [d for d in range(row_count) if d != far_off]
-        whose = [tuple((i - d) % row_count for i in range(row_count)) for d in (*came, far_off)]
-        plan = Plan(tuple(whose[:-1]), whose[-1], (0,) * row_count)
+    downs, ups = [factor_off], [second]
+    for i in range(row_count // 2):
+        downs.append(turn(downs[-1] + index_gate if i else downs[-1], "row", -1))
+    for _ in range((row_count - 1) // 2):
+        ups.append(turn(ups[-1], "row", 1))
+    parts, late = downs[:-1] + ups[:0:-1], downs[-1]
+    far = len(downs) - 1
+    came = [d for d in range(row_count) if d != far]
+    whose = [tuple((i + d) % row_count for i in range(row_count)) for d in (*came, far)]
+    plan = Plan(tuple(whose[:-1]), whose[-1])
+
     links, late_keep = call(
         functools.partial(links_kernel, plan),
         [shape(panels, size, size), shape(panels, rows, size)],
@@ -463,19 +455,19 @@
         flops=6 * panels * size * size * width,
         name="links",
     )
-    links_t, own_whole = call(
+    links_t, own_whole, own_cov = call(
         functools.partial(segment_kernel, plan, panels),
-        [shape(panels, size, size), shape(2 * size, size)],
+        [shape(panels, size, size), shape(size + 5 * half // 4, size), shape(size, size)],
         [],
-        [*lates, links, late_keep, *picks, *bases],
+        [late, links, late_keep, *picks, *bases],
         flops=6 * panels * rows * size * width + 18 * (panels - 1) * size**3,
         name="segment",
     )
     maps, maps_token = call(
         functools.partial(maps_kernel, plan),
-        [shape(panels, size, width), shape(1, half_cols)],
+        [shape(panels, size, width), shape(1, half)],
         [fill_mask],
-        [inv_diag, *parts, *lates],
+        [inv_diag, *parts, late],
         scratch=[pltpu.VMEM((size, width), F32)],
         flops=6 * panels * size * width * width,
         mib=24,
@@ -483,14 +475,13 @@
     )
     swap = [(i, i ^ 1) for i in range(seg_count)]
     other_whole = lax.ppermute(own_whole, "seg", swap)
-    half = size // 2
     half_packed = shape(5 * half // 4, half)
     half_link = shape(half, size)
     link_t, cov, send, send_t = call(
         chip_kernel,
         [shape(size, size), shape(size, size), half_packed, half_link],
         [],
-        [own_whole, other_whole],
+        [own_whole, own_cov, other_whole],
         flops=18 * size**3,
         name="chip",
     )
@@ -505,7 +496,7 @@
         right = jax.ShapeDtypeStruct((panels, size, width), BF16)
         return call(
             functools.partial(prepare_kernel, levels, panels),
-            [left, left, right, right, shape(panels, total, width), shape(1, half_cols)],
+            [left, left, right, right, shape(panels, total, width), shape(1, half)],
             [fill_mask],
             [*bases, *priors, other_whole, maps, links_t, *(past or ())],
             scratch=[pltpu.VMEM((size, width), F32)],

time: 49.7 us -> 47.2 us (0.950)
  waiting for transfers between devices: 18.3 us -> 14.7 us
  starting transfers between devices: 12.3 us -> 13.3 us
    ppermute x4 -> x0, waiting for transfers between devices: 10.2 us -> none  [step(): return lax.ppermute(x, 'row', list(enumerate(targets)))]
    ppermute x1 -> x4, starting transfers between devices: 0.01 us -> 9.39 us  [turn(): lax.ppermute(x, axis, [(i, (i + distance) % count) for i in range(count)])]
    ppermute x4 -> x0, starting transfers between devices: 8.28 us -> none  [step(): return lax.ppermute(x, 'row', list(enumerate(targets)))]
    ppermute x1 -> x4, waiting for transfers between devices: 0.01 us -> 6.68 us  [turn(): lax.ppermute(x, axis, [(i, (i + distance) % count) for i in range(count)])]
  transfers between devices with their start and end apart: 12 -> 11, of which waited for: 7 -> 9; matrix products, arithmetic and copies ran while one was open for 1% -> 1% of each run, Pallas kernels for 24% -> 25%
where the time goes in v10:
time: 47.2 us; the launch traced here: 47 us
  Pallas kernels  16.2 us (34%)
  waiting for transfers between devices  14.7 us (31%)
  starting transfers between devices  13.3 us (28%)
  between operations  1.44 us (3%)
  local copies, waits for them, and re-layouts  0.7 us (1%)
  other arithmetic  0.69 us (1%)
    pallas_call x9, Pallas kernels, call(): pl.pallas_call(inner, out_shape=[*outs, *(jax.ShapeDtypeStruct(a.shape, a...  16.2 us
    ppermute x4, starting transfers between devices, turn(): lax.ppermute(x, axis, [(i, (i + distance) % count) for i in range(count)])  9.39 us
    ppermute x4, waiting for transfers between devices, turn(): lax.ppermute(x, axis, [(i, (i + distance) % count) for i in range(count)])  6.68 us
    ppermute x1, waiting for transfers between devices, body(): got_t = lax.ppermute(send_t, 'seg', partner)  2.8 us
    ppermute x2, starting transfers between devices, body(): got = lax.ppermute(send, 'seg', partner)  2.09 us
    ppermute x1, waiting for transfers between devices, body(): other_whole = lax.ppermute(own_whole, 'seg', swap)  1.7 us
    ppermute x1, starting transfers between devices, body(): got_t = lax.ppermute(send_t, 'seg', partner)  1.59 us
    ppermute x1, waiting for transfers between devices, body(): lax.ppermute(got, 'seg', swap)  1.26 us
  transfers between devices with their start and end apart: 11, of which 9 were waited for; matrix products, arithmetic and copies ran while one was open for 1% of the time, Pallas kernels for 25%

profile of v10, /device:TPU:0, one launch (start us, length us, event | category | flops | bytes accessed | tf_op | source)
XLA Modules:
  0.0 47.0 jit_solution(1606572327603987143)
XLA Ops:
  0.6 0.0 copy-start.1
  0.6 5.1 %collective-permute-start = (f32[2,64,512]{2,1,0:T(8,128)}, f32[2,64,512]{2,1,0:T(8,128)S(1)}, u32[]{:S(2)}, u32[]{:S(2)}) collective-permute-start(f32[2,64,512]{2,1,0:T(8,128)} %refs_2_.3), channel_id=1, source_target_pairs={{0,3},{1,0},{2,1},{3,2},{4,7},{5,4},{6,5},{7,6},{8,11},{9,8},{10,9... | collective-permute-start | bytes 786440 | tf_op jit(solution)/shard_map/ppermute | solution.py:415
  5.7 0.0 collective-permute-start.1
  5.7 0.0 copy-start.2
  5.7 0.7 %copy-done.2 = s32[2,4]{1,0:T(2,128)S(1)} copy-done((s32[2,4]{1,0:T(2,128)S(1)}, s32[2,4]{1,0:T(2,128)}, u32[]{:S(2)}) %copy-start.2) | copy-done | bytes 56
  6.4 0.0 copy-start.3
  6.4 2.8 %prior.2 = (f32[256,256]{1,0:T(8,128)S(1)}, f32[128,512]{1,0:T(8,128)S(1)}, bf16[512,256]{1,0:T(8,128)(2,1)S(1)}, bf16[512,256]{1,0:T(8,128)(2,1)S(1)}, f32[1,1,512]{2,1,0:T(1,128)S(1)}) custom-call(s32[2,4]{1,0:T(2,128)S(1)} %copy-done.2, f32[2,512,512]{2,1,0:T(8,128)} %refs_1_.5), custom_call_target="tpu_custom_call" | custom-call | flops 402653184 | bytes 3672064 | tf_op jit(solution)/shard_map/prior/pallas_call | solution.py:132
  9.2 0.0 copy-start.4
  9.2 0.0 copy-done.1
  9.2 0.1 collective-permute-start.3
  9.3 0.5 %collective-permute-done.1.refs_1_ = s32[2,4]{1,0:T(2,128)S(1)} collective-permute-done((s32[2,4]{1,0:T(2,128)}, s32[2,4]{1,0:T(2,128)S(1)}, u32[]{:S(2)}, u32[]{:S(2)}) %collective-permute-start.1) | collective-permute-done | bytes 64 | tf_op jit(solution)/shard_map/ppermute | solution.py:415
  9.8 0.6 %reduce_min.9 = s32[]{:T(128)} reduce(s32[2,4]{1,0:T(2,128)S(1)} %collective-permute-done.1.refs_1_, s32[]{:T(128)} %constant.0.clone.1), dimensions={0,1}, to_apply=%region_0.0 | reduce | flops 7 | bytes 40 | tf_op jit(solution)/shard_map/reduce_min | solution.py:436
  11.1 0.7 %collective-permute-done.refs_2_.refs_3_ = f32[2,64,512]{2,1,0:T(8,128)S(1)} collective-permute-done((f32[2,64,512]{2,1,0:T(8,128)}, f32[2,64,512]{2,1,0:T(8,128)S(1)}, u32[]{:S(2)}, u32[]{:S(2)}) %collective-permute-start) | collective-permute-done | bytes 262176 | tf_op jit(solution)/shard_map/ppermute | solution.py:415
  11.9 4.2 %collective-permute-start.2 = (f32[2,64,512]{2,1,0:T(8,128)S(1)}, f32[2,64,512]{2,1,0:T(8,128)S(1)}, u32[]{:S(2)}, u32[]{:S(2)}) collective-permute-start(f32[2,64,512]{2,1,0:T(8,128)S(1)} %broadcast_add_fusion.1), channel_id=1, source_target_pairs={{0,3},{1,0},{2,1},{3,2},{4,7},{5,4},{6,5},{7,6},{8,11},{9,8},{10,9... | collective-permute-start | bytes 786440 | tf_op jit(solution)/shard_map/ppermute | solution.py:415
  16.1 0.0 copy-done.3
  16.1 2.8 %prior.3 = (f32[256,256]{1,0:T(8,128)S(1)}, f32[128,512]{1,0:T(8,128)S(1)}, bf16[512,256]{1,0:T(8,128)(2,1)S(1)}, bf16[512,256]{1,0:T(8,128)(2,1)S(1)}, f32[1,1,512]{2,1,0:T(1,128)}) custom-call(s32[2,4]{1,0:T(2,128)S(1)} %copy-done.3, s32[2,4]{1,0:T(2,128)S(1)} %collective-permute-done.1.refs_1_, f32[2,512,512]{2,1,0:T(8,128)} %refs_1_.5), custom_call_target="tpu_custom_call" | custom-call | flops 402653184 | bytes 3672064 | tf_op jit(solution)/shard_map/prior/pallas_call | solution.py:132
  18.9 1.0 %collective-permute-done.3.refs_3_.refs_4_ = f32[2,64,512]{2,1,0:T(8,128)S(1)} collective-permute-done((f32[2,64,512]{2,1,0:T(8,128)S(1)}, f32[2,64,512]{2,1,0:T(8,128)S(1)}, u32[]{:S(2)}, u32[]{:S(2)}) %collective-permute-start.3) | collective-permute-done | bytes 262176 | tf_op jit(solution)/shard_map/ppermute | solution.py:415
  19.9 0.0 copy-done.4
  19.9 1.6 %links.1 = (f32[2,256,256]{2,1,0:T(8,128)S(1)}, f32[2,64,256]{2,1,0:T(8,128)S(1)}) custom-call(s32[2,4]{1,0:T(2,128)S(1)} %copy-done.4, f32[2,64,512]{2,1,0:T(8,128)S(1)} %copy-done.1, f32[2,64,512]{2,1,0:T(8,128)S(1)} %collective-permute-done.refs_2_.refs_3_, f32[2,64,512]{2,1,0:T(8,128)S(1)} %collective-permute-done.3.refs_3_.refs_4_, ...), custom_call_target="tpu_custom_call" | custom-call | flops 402653184 | bytes 3538944 | tf_op jit(solution)/shard_map/links/pallas_call | solution.py:132
  21.5 0.0 copy-start
  21.5 4.5 %collective-permute-done.2.refs_0_.refs_5_ = f32[2,64,512]{2,1,0:T(8,128)S(1)} collective-permute-done((f32[2,64,512]{2,1,0:T(8,128)S(1)}, f32[2,64,512]{2,1,0:T(8,128)S(1)}, u32[]{:S(2)}, u32[]{:S(2)}) %collective-permute-start.2) | collective-permute-done | bytes 262176 | tf_op jit(solution)/shard_map/ppermute | solution.py:415
  26.0 1.1 %segment.1 = (f32[2,256,256]{2,1,0:T(8,128)S(1)}, f32[416,256]{1,0:T(8,128)S(1)}, f32[256,256]{1,0:T(8,128)S(1)}) custom-call(f32[2,64,512]{2,1,0:T(8,128)S(1)} %collective-permute-done.2.refs_0_.refs_5_, f32[2,256,256]{2,1,0:T(8,128)S(1)} %get-tuple-element.33.refs_1_, f32[2,64,256]{2,1,0:T(8,128)S(1)} %get-tuple-element.34.refs_2_, ...), custom_call_target="tpu_custom_call" | custom-call | flops 402653184 | bytes 4751360 | tf_op jit(solution)/shard_map/segment/pallas_call | solution.py:132
  27.1 0.1 collective-permute-start.4
  27.2 1.7 %collective-permute-done.4.refs_2_.refs_5_ = f32[416,256]{1,0:T(8,128)S(1)} collective-permute-done((f32[416,256]{1,0:T(8,128)S(1)}, f32[416,256]{1,0:T(8,128)S(1)}, u32[]{:S(2)}, u32[]{:S(2)}) %collective-permute-start.4) | collective-permute-done | bytes 426016 | tf_op jit(solution)/shard_map/ppermute | solution.py:477
  28.9 0.8 %chip.1 = (f32[256,256]{1,0:T(8,128)S(1)}, f32[256,256]{1,0:T(8,128)S(1)}, f32[160,128]{1,0:T(8,128)S(1)}, f32[128,256]{1,0:T(8,128)S(1)}) custom-call(f32[416,256]{1,0:T(8,128)S(1)} %get-tuple-element.37.refs_0_, f32[256,256]{1,0:T(8,128)S(1)} %get-tuple-element.38.refs_1_, f32[416,256]{1,0:T(8,128)S(1)} %collective-permute-done.4.refs_2_.refs_5_), custom_call_target="tpu_custom_call" | custom-call | flops 301989888 | bytes 1851392 | tf_op jit(solution)/shard_map/chip/pallas_call | solution.py:132
  29.7 1.6 %collective-permute-start.5 = (f32[128,256]{1,0:T(8,128)S(1)}, f32[128,256]{1,0:T(8,128)S(1)}, u32[]{:S(2)}, u32[]{:S(2)}) collective-permute-start(f32[128,256]{1,0:T(8,128)S(1)} %get-tuple-element.41), channel_id=1, source_target_pairs={{0,8},{4,12},{8,0},{12,4},{16,24},{20,28},{24,16},{28,20},{1,9},{5... | collective-permute-start | bytes 393224 | tf_op jit(solution)/shard_map/ppermute | solution.py:516
  31.2 0.5 %collective-permute-start.7 = (f32[160,128]{1,0:T(8,128)S(1)}, f32[160,128]{1,0:T(8,128)S(1)}, u32[]{:S(2)}, u32[]{:S(2)}) collective-permute-start(f32[160,128]{1,0:T(8,128)S(1)} %get-tuple-element.42), channel_id=1, source_target_pairs={{0,8},{4,12},{8,0},{12,4},{16,24},{20,28},{24,16},{28,20},{1,9},{5... | collective-permute-start | bytes 245768 | tf_op jit(solution)/shard_map/ppermute | solution.py:510
  31.7 0.0 copy-done
  31.8 1.5 %maps.1 = (f32[2,256,512]{2,1,0:T(8,128)S(1)}, f32[1,128]{1,0:T(1,128)S(1)}) custom-call(s32[2,4]{1,0:T(2,128)S(1)} %copy-done.4, f32[2,512,512]{2,1,0:T(8,128)S(1)} %copy-done, f32[2,64,512]{2,1,0:T(8,128)S(1)} %copy-done.1, f32[2,64,512]{2,1,0:T(8,128)S(1)} %collective-permute-done.refs_2_.refs_3_, ...), custom_call_target="tpu_custom_call" | custom-call | flops 805306368 | bytes 4194816 | tf_op jit(solution)/shard_map/maps/pallas_call | solution.py:132
  33.3 2.8 %collective-permute-done.5.refs_2_.refs_8_ = f32[128,256]{1,0:T(8,128)S(1)} collective-permute-done((f32[128,256]{1,0:T(8,128)S(1)}, f32[128,256]{1,0:T(8,128)S(1)}, u32[]{:S(2)}, u32[]{:S(2)}) %collective-permute-start.5) | collective-permute-done | bytes 131104 | tf_op jit(solution)/shard_map/ppermute | solution.py:516
  36.1 0.0 collective-permute-start.6
  36.1 1.0 %collective-permute-done.7 = f32[160,128]{1,0:T(8,128)S(1)} collective-permute-done((f32[160,128]{1,0:T(8,128)S(1)}, f32[160,128]{1,0:T(8,128)S(1)}, u32[]{:S(2)}, u32[]{:S(2)}) %collective-permute-start.7) | collective-permute-done | bytes 81952 | tf_op jit(solution)/shard_map/ppermute | solution.py:510
  37.0 0.1 collective-permute-start.8
  37.1 1.3 %collective-permute-done.8.refs_5_.refs_11_ = f32[160,128]{1,0:T(8,128)S(1)} collective-permute-done((f32[160,128]{1,0:T(8,128)S(1)}, f32[160,128]{1,0:T(8,128)S(1)}, u32[]{:S(2)}, u32[]{:S(2)}) %collective-permute-start.8) | collective-permute-done | bytes 81952 | tf_op jit(solution)/shard_map/ppermute | solution.py:519
  38.4 0.0 collective-permute-done.6.refs_3_.refs_9_
  38.4 0.8 %merge.1 = f32[160,128]{1,0:T(8,128)S(1)} custom-call(f32[256,256]{1,0:T(8,128)S(1)} %get-tuple-element.39.refs_0_, f32[256,256]{1,0:T(8,128)S(1)} %get-tuple-element.40.refs_1_, f32[128,256]{1,0:T(8,128)S(1)} %collective-permute-done.5.refs_2_.refs_8_, f32[128,256]{1,0:T(8,128)S(1)} %collective-permute-done.6.refs_3_.refs_9_, ...), custom_call_target="tpu_custom_call" | custom-call | flops 301989888 | bytes 1032192 | tf_op jit(solution)/shard_map/merge/pallas_call | solution.py:132
  39.2 1.6 %collective-permute-start.9 = (f32[160,128]{1,0:T(8,128)S(1)}, f32[160,128]{1,0:T(8,128)S(1)}, u32[]{:S(2)}, u32[]{:S(2)}) collective-permute-start(f32[160,128]{1,0:T(8,128)S(1)} %merge.1), channel_id=1, source_target_pairs={{0,16},{4,20},{8,24},{12,28},{16,0},{20,4},{24,8},{28,12},{1,17},{... | collective-permute-start | bytes 245768 | tf_op jit(solution)/shard_map/ppermute | solution.py:510
  40.8 3.0 %prepare.1 = (bf16[384,256]{1,0:T(8,128)(2,1)S(1)}, bf16[384,256]{1,0:T(8,128)(2,1)S(1)}, bf16[2,256,512]{2,1,0:T(8,128)(2,1)S(1)}, bf16[2,256,512]{2,1,0:T(8,12...) custom-call(s32[2,4]{1,0:T(2,128)S(1)} %copy-done.4, f32[256,256]{1,0:T(8,128)S(1)} %get-tuple-element.35.refs_7_.refs_1_, ...), custom_call_target="tpu_custom_call" | custom-call | flops 1459617792 | bytes 7143936 | tf_op jit(solution)/shard_map/prepare/pallas_call | solution.py:132
  43.8 0.0 collective-permute-done.9
  43.8 0.1 collective-permute-start.10
  43.9 1.3 %collective-permute-done.10.refs_1_ = f32[160,128]{1,0:T(8,128)S(1)} collective-permute-done((f32[160,128]{1,0:T(8,128)S(1)}, f32[160,128]{1,0:T(8,128)S(1)}, u32[]{:S(2)}, u32[]{:S(2)}) %collective-permute-start.10) | collective-permute-done | bytes 81952 | tf_op jit(solution)/shard_map/ppermute | solution.py:514
  45.1 1.9 %finish.1 = (f32[2,128,512]{2,1,0:T(8,128)}, f32[2,64,512]{2,1,0:T(8,128)}) custom-call(f32[160,128]{1,0:T(8,128)S(1)} %broadcast_add_fusion.2.refs_0_, f32[160,128]{1,0:T(8,128)S(1)} %collective-permute-done.10.refs_1_, bf16[384,256]{1,0:T(8,128)(2,1)S(1)} %get-tuple-element.49.refs_2_, bf16[384,256]{1,0:T(8,128)(2,1)S(1)} %get-tuple-element.50.refs_3_, ...), custom_call_target="tpu_custom_call" | custom-call | flops 452984832 | bytes 4620288 | tf_op jit(solution)/shard_map/finish/pallas_call | solution.py:132
  (4 shorter events, 0.1 us)
Async XLA Ops:
  0.6 8.6 %copy-start.1 = (f32[2,64,512]{2,1,0:T(8,128)S(1)}, f32[2,64,512]{2,1,0:T(8,128)}, u32[]{:S(2)}) copy-start(f32[2,64,512]{2,1,0:T(8,128)} %refs_2_.3) | copy-start | bytes 786436
  0.6 11.2 %collective-permute-start = (f32[2,64,512]{2,1,0:T(8,128)}, f32[2,64,512]{2,1,0:T(8,128)S(1)}, u32[]{:S(2)}, u32[]{:S(2)}) collective-permute-start(f32[2,64,512]{2,1,0:T(8,128)} %refs_2_.3), channel_id=1, source_target_pairs={{0,3},{1,0},{2,1},{3,2},{4,7},{5,4},{6,5},{7,6},{8,11},{9,8},{10,9... | collective-permute-start | bytes 786440 | tf_op jit(solution)/shard_map/ppermute | solution.py:415
  5.7 4.1 %collective-permute-start.1 = (s32[2,4]{1,0:T(2,128)}, s32[2,4]{1,0:T(2,128)S(1)}, u32[]{:S(2)}, u32[]{:S(2)}) collective-permute-start(s32[2,4]{1,0:T(2,128)} %refs_0_.6), channel_id=1, source_target_pairs={{0,4},{4,8},{8,12},{12,16},{16,20},{20,24},{24,28},{28,0},{1,5},{5... | collective-permute-start | bytes 104 | tf_op jit(solution)/shard_map/ppermute | solution.py:415
  5.7 0.7 %copy-start.2 = (s32[2,4]{1,0:T(2,128)S(1)}, s32[2,4]{1,0:T(2,128)}, u32[]{:S(2)}) copy-start(s32[2,4]{1,0:T(2,128)} %refs_0_.6) | copy-start | bytes 100
  6.4 9.7 %copy-start.3 = (s32[2,4]{1,0:T(2,128)S(1)}, s32[2,4]{1,0:T(2,128)}, u32[]{:S(2)}) copy-start(s32[2,4]{1,0:T(2,128)} %refs_0_.6) | copy-start | bytes 100
  9.2 10.7 %copy-start.4 = (s32[2,4]{1,0:T(2,128)S(1)}, s32[2,4]{1,0:T(2,128)}, u32[]{:S(2)}) copy-start(s32[2,4]{1,0:T(2,128)} %refs_0_.9) | copy-start | bytes 100
  9.2 10.6 %collective-permute-start.3 = (f32[2,64,512]{2,1,0:T(8,128)S(1)}, f32[2,64,512]{2,1,0:T(8,128)S(1)}, u32[]{:S(2)}, u32[]{:S(2)}) collective-permute-start(f32[2,64,512]{2,1,0:T(8,128)S(1)} %broadcast_add_fusion), channel_id=1, source_target_pairs={{0,1},{1,2},{2,3},{3,0},{4,5},{5,6},{6,7},{7,4},{8,9},{9,10},{10,1... | collective-permute-start | bytes 786440 | tf_op jit(solution)/shard_map/ppermute | solution.py:415
  11.9 14.1 %collective-permute-start.2 = (f32[2,64,512]{2,1,0:T(8,128)S(1)}, f32[2,64,512]{2,1,0:T(8,128)S(1)}, u32[]{:S(2)}, u32[]{:S(2)}) collective-permute-start(f32[2,64,512]{2,1,0:T(8,128)S(1)} %broadcast_add_fusion.1), channel_id=1, source_target_pairs={{0,3},{1,0},{2,1},{3,2},{4,7},{5,4},{6,5},{7,6},{8,11},{9,8},{10,9... | collective-permute-start | bytes 786440 | tf_op jit(solution)/shard_map/ppermute | solution.py:415
  21.5 10.2 %copy-start = (f32[2,512,512]{2,1,0:T(8,128)S(1)}, f32[2,512,512]{2,1,0:T(8,128)}, u32[]{:S(2)}) copy-start(f32[2,512,512]{2,1,0:T(8,128)} %refs_1_.5) | copy-start | bytes 6291460
  27.1 1.8 %collective-permute-start.4 = (f32[416,256]{1,0:T(8,128)S(1)}, f32[416,256]{1,0:T(8,128)S(1)}, u32[]{:S(2)}, u32[]{:S(2)}) collective-permute-start(f32[416,256]{1,0:T(8,128)S(1)} %get-tuple-element.37.refs_0_), channel_id=1, source_target_pairs={{0,4},{4,0},{8,12},{12,8},{16,20},{20,16},{24,28},{28,24},{1,5},{5... | collective-permute-start | bytes 1277960 | tf_op jit(solution)/shard_map/ppermute | solution.py:477
  29.7 6.4 %collective-permute-start.5 = (f32[128,256]{1,0:T(8,128)S(1)}, f32[128,256]{1,0:T(8,128)S(1)}, u32[]{:S(2)}, u32[]{:S(2)}) collective-permute-start(f32[128,256]{1,0:T(8,128)S(1)} %get-tuple-element.41), channel_id=1, source_target_pairs={{0,8},{4,12},{8,0},{12,4},{16,24},{20,28},{24,16},{28,20},{1,9},{5... | collective-permute-start | bytes 393224 | tf_op jit(solution)/shard_map/ppermute | solution.py:516
  31.2 5.8 %collective-permute-start.7 = (f32[160,128]{1,0:T(8,128)S(1)}, f32[160,128]{1,0:T(8,128)S(1)}, u32[]{:S(2)}, u32[]{:S(2)}) collective-permute-start(f32[160,128]{1,0:T(8,128)S(1)} %get-tuple-element.42), channel_id=1, source_target_pairs={{0,8},{4,12},{8,0},{12,4},{16,24},{20,28},{24,16},{28,20},{1,9},{5... | collective-permute-start | bytes 245768 | tf_op jit(solution)/shard_map/ppermute | solution.py:510
  36.1 2.3 %collective-permute-start.6 = (f32[128,256]{1,0:T(8,128)S(1)}, f32[128,256]{1,0:T(8,128)S(1)}, u32[]{:S(2)}, u32[]{:S(2)}) collective-permute-start(f32[128,256]{1,0:T(8,128)S(1)} %collective-permute-done.5.refs_2_.refs_8_), channel_id=1, source_target_pairs={{0,4},{4,0},{8,12},{12,8},{16,20},{20,16},{24,28},{28,24},{1,5},{5... | collective-permute-start | bytes 393224 | tf_op jit(solution)/shard_map/ppermute | solution.py:519
  37.0 1.3 %collective-permute-start.8 = (f32[160,128]{1,0:T(8,128)S(1)}, f32[160,128]{1,0:T(8,128)S(1)}, u32[]{:S(2)}, u32[]{:S(2)}) collective-permute-start(f32[160,128]{1,0:T(8,128)S(1)} %broadcast_add_fusion.3.refs_4_.refs_10_), channel_id=1, source_target_pairs={{0,4},{4,0},{8,12},{12,8},{16,20},{20,16},{24,28},{28,24},{1,5},{5... | collective-permute-start | bytes 245768 | tf_op jit(solution)/shard_map/ppermute | solution.py:519
  39.2 4.6 %collective-permute-start.9 = (f32[160,128]{1,0:T(8,128)S(1)}, f32[160,128]{1,0:T(8,128)S(1)}, u32[]{:S(2)}, u32[]{:S(2)}) collective-permute-start(f32[160,128]{1,0:T(8,128)S(1)} %merge.1), channel_id=1, source_target_pairs={{0,16},{4,20},{8,24},{12,28},{16,0},{20,4},{24,8},{28,12},{1,17},{... | collective-permute-start | bytes 245768 | tf_op jit(solution)/shard_map/ppermute | solution.py:510
  43.8 1.3 %collective-permute-start.10 = (f32[160,128]{1,0:T(8,128)S(1)}, f32[160,128]{1,0:T(8,128)S(1)}, u32[]{:S(2)}, u32[]{:S(2)}) collective-permute-start(f32[160,128]{1,0:T(8,128)S(1)} %broadcast_add_fusion.2.refs_0_), channel_id=1, source_target_pairs={{0,4},{4,0},{8,12},{12,8},{16,20},{20,16},{24,28},{28,24},{1,5},{5... | collective-permute-start | bytes 245768 | tf_op jit(solution)/shard_map/ppermute | solution.py:514

commit v11 on v10

--- a/solution.py
+++ b/solution.py
@@ -59,16 +59,6 @@
     top = jnp.concatenate([first, cross], 1)
     bottom = jnp.concatenate([cross.T, second], 1)
     return jnp.concatenate([top, bottom], 0)
-
-
-def widen(packed):
-    rows = packed.shape[0] // 2
-    return jnp.concatenate([packed[:rows], packed[rows:]], 1)
-
-
-def narrow(wide):
-    columns = wide.shape[1] // 2
-    return jnp.concatenate([wide[:, :columns], wide[:, columns:]], 0)
 
 
 def is_lower():
@@ -236,7 +226,7 @@
 def segment_kernel(plan, panels, *refs):
     late_ref, early_ref, keep_ref, *refs = refs
     pick_refs, base_refs = refs[: 2 * panels], refs[2 * panels : 3 * panels]
-    links_t_ref, whole_ref, cov_ref = refs[3 * panels :]
+    links_t_ref, whole_ref = refs[3 * panels :]
     size = links_t_ref.shape[1]
     rows = keep_ref.shape[1]
     here = lax.broadcasted_iota(jnp.int32, (size, size), 1) // rows == at_row(plan.late)
@@ -254,8 +244,7 @@
             cov = carry(own_t, cov, base_refs[p][...])
             link_t = mm(own_t, link_t)
     whole_ref[:size] = link_t
-    whole_ref[size:] = widen(pack(cov))
-    cov_ref[...] = cov
+    whole_ref[size:] = cov
 
 
 def maps_kernel(plan, mask_ref, inv_ref, *refs):
@@ -269,11 +258,11 @@
         maps_ref[p] = triangular_mm(rows_ref[...], inv_ref[p])
 
 
-def chip_kernel(own_ref, own_cov_ref, other_ref, link_t_ref, cov_ref, packed_ref, half_t_ref):
+def chip_kernel(own_ref, other_ref, link_t_ref, cov_ref, packed_ref, half_t_ref):
     size = cov_ref.shape[0]
     lower = is_lower()
     own_t, other_t = own_ref[:size, :], other_ref[:size, :]
-    own, other = own_cov_ref[...], unpack(narrow(other_ref[size:, :]))
+    own, other = own_ref[size:, :], other_ref[size:, :]
     down_t = split(jnp.where(lower, own_t, other_t))
     cov = carry(down_t, jnp.where(lower, other, own), jnp.where(lower, own, other))
     link_t = mm(down_t, jnp.where(lower, other_t, own_t))
@@ -329,7 +318,7 @@
     at_row = lax.broadcasted_iota(jnp.int32, (size, size), 0)
     at_col = lax.broadcasted_iota(jnp.int32, (size, size), 1)
     eye = (at_row == at_col).astype(F32)
-    other = unpack(narrow(other_ref[size:, :]))
+    other = other_ref[size:, :]
     lower = is_lower()
     if past_refs:
         chip = lax.axis_index("seg") // 2
@@ -435,15 +424,15 @@
     second = factor_off + tokens[-1]
     index_gate = jnp.minimum(jnp.min(prior_fill), 0).astype(F32)
 
-    downs, ups = [factor_off], [second]
+    ups, downs = [factor_off], [second]
     for i in range(row_count // 2):
-        downs.append(turn(downs[-1] + index_gate if i else downs[-1], "row", -1))
+        ups.append(turn(ups[-1] + index_gate if i else ups[-1], "row", 1))
     for _ in range((row_count - 1) // 2):
-        ups.append(turn(ups[-1], "row", 1))
-    parts, late = downs[:-1] + ups[:0:-1], downs[-1]
-    far = len(downs) - 1
+        downs.append(turn(downs[-1], "row", -1))
+    parts, late = ups[:-1] + downs[:0:-1], ups[-1]
+    far = len(ups) - 1
     came = [d for d in range(row_count) if d != far]
-    whose = [tuple((i + d) % row_count for i in range(row_count)) for d in (*came, far)]
+    whose = [tuple((i - d) % row_count for i in range(row_count)) for d in (*came, far)]
     plan = Plan(tuple(whose[:-1]), whose[-1])
 
     links, late_keep = call(
@@ -455,9 +444,9 @@
         flops=6 * panels * size * size * width,
         name="links",
     )
-    links_t, own_whole, own_cov = call(
+    links_t, own_whole = call(
         functools.partial(segment_kernel, plan, panels),
-        [shape(panels, size, size), shape(size + 5 * half // 4, size), shape(size, size)],
+        [shape(panels, size, size), shape(2 * size, size)],
         [],
         [late, links, late_keep, *picks, *bases],
         flops=6 * panels * rows * size * width + 18 * (panels - 1) * size**3,
@@ -481,7 +470,7 @@
         chip_kernel,
         [shape(size, size), shape(size, size), half_packed, half_link],
         [],
-        [own_whole, own_cov, other_whole],
+        [own_whole, other_whole],
         flops=18 * size**3,
         name="chip",
     )

time: 47.2 us -> 45 us (0.953)
  starting transfers between devices: 13.3 us -> 9.65 us
  waiting for transfers between devices: 14.7 us -> 16.3 us
    ppermute x4, starting transfers between devices: 9.39 us -> 5.3 us  [turn(): lax.ppermute(x, axis, [(i, (i + distance) % count) for i in range(count)])]
    ppermute x4, waiting for transfers between devices: 6.68 us -> 8.25 us  [turn(): lax.ppermute(x, axis, [(i, (i + distance) % count) for i in range(count)])]
  transfers between devices with their start and end apart: 11 -> 11, of which waited for: 9 -> 8; matrix products, arithmetic and copies ran while one was open for 1% -> 2% of each run, Pallas kernels for 25% -> 26%
where the time goes in v11:
time: 45 us; the launch traced here: 44.8 us
  waiting for transfers between devices  16.3 us (36%)
  Pallas kernels  16 us (36%)
  starting transfers between devices  9.65 us (21%)
  between operations  1.45 us (3%)
  local copies, waits for them, and re-layouts  0.7 us (2%)
  other arithmetic  0.69 us (2%)
    pallas_call x9, Pallas kernels, call(): pl.pallas_call(inner, out_shape=[*outs, *(jax.ShapeDtypeStruct(a.shape, a...  16 us
    ppermute x4, waiting for transfers between devices, turn(): lax.ppermute(x, axis, [(i, (i + distance) % count) for i in range(count)])  8.25 us
    ppermute x4, starting transfers between devices, turn(): lax.ppermute(x, axis, [(i, (i + distance) % count) for i in range(count)])  5.3 us
    ppermute x1, waiting for transfers between devices, body(): got_t = lax.ppermute(send_t, 'seg', partner)  2.78 us
    ppermute x2, starting transfers between devices, body(): got = lax.ppermute(send, 'seg', partner)  2.13 us
    ppermute x1, starting transfers between devices, body(): got_t = lax.ppermute(send_t, 'seg', partner)  1.57 us
    ppermute x1, waiting for transfers between devices, body(): other_whole = lax.ppermute(own_whole, 'seg', swap)  1.54 us
    ppermute x1, waiting for transfers between devices, body(): lax.ppermute(got, 'seg', swap)  1.26 us
  transfers between devices with their start and end apart: 11, of which 8 were waited for; matrix products, arithmetic and copies ran while one was open for 2% of the time, Pallas kernels for 26%

profile of v11, /device:TPU:0, one launch (start us, length us, event | category | flops | bytes accessed | tf_op | source)
XLA Modules:
  0.0 44.8 jit_solution(16353446273333681218)
XLA Ops:
  0.6 0.0 copy-start.1
  0.6 3.1 %collective-permute-start = (f32[2,64,512]{2,1,0:T(8,128)}, f32[2,64,512]{2,1,0:T(8,128)S(1)}, u32[]{:S(2)}, u32[]{:S(2)}) collective-permute-start(f32[2,64,512]{2,1,0:T(8,128)} %refs_2_.3), channel_id=1, source_target_pairs={{0,1},{1,2},{2,3},{3,0},{4,5},{5,6},{6,7},{7,4},{8,9},{9,10},{10,1... | collective-permute-start | bytes 786440 | tf_op jit(solution)/shard_map/ppermute | solution.py:404
  3.7 0.0 collective-permute-start.1
  3.7 0.0 copy-start.2
  3.7 0.7 %copy-done.2 = s32[2,4]{1,0:T(2,128)S(1)} copy-done((s32[2,4]{1,0:T(2,128)S(1)}, s32[2,4]{1,0:T(2,128)}, u32[]{:S(2)}) %copy-start.2) | copy-done | bytes 56
  4.4 0.0 copy-start.3
  4.4 2.8 %prior.2 = (f32[256,256]{1,0:T(8,128)S(1)}, f32[128,512]{1,0:T(8,128)S(1)}, bf16[512,256]{1,0:T(8,128)(2,1)S(1)}, bf16[512,256]{1,0:T(8,128)(2,1)S(1)}, f32[1,1,512]{2,1,0:T(1,128)S(1)}) custom-call(s32[2,4]{1,0:T(2,128)S(1)} %copy-done.2, f32[2,512,512]{2,1,0:T(8,128)} %refs_1_.5), custom_call_target="tpu_custom_call" | custom-call | flops 402653184 | bytes 3672064 | tf_op jit(solution)/shard_map/prior/pallas_call | solution.py:122
  7.2 0.0 copy-start.4
  7.2 0.0 copy-done.1
  7.2 2.2 %collective-permute-start.3 = (f32[2,64,512]{2,1,0:T(8,128)S(1)}, f32[2,64,512]{2,1,0:T(8,128)S(1)}, u32[]{:S(2)}, u32[]{:S(2)}) collective-permute-start(f32[2,64,512]{2,1,0:T(8,128)S(1)} %broadcast_add_fusion), channel_id=1, source_target_pairs={{0,3},{1,0},{2,1},{3,2},{4,7},{5,4},{6,5},{7,6},{8,11},{9,8},{10,9... | collective-permute-start | bytes 786440 | tf_op jit(solution)/shard_map/ppermute | solution.py:404
  9.4 0.0 collective-permute-done.1.refs_1_
  9.4 0.6 %reduce_min.9 = s32[]{:T(128)} reduce(s32[2,4]{1,0:T(2,128)S(1)} %collective-permute-done.1.refs_1_, s32[]{:T(128)} %constant.0.clone.1), dimensions={0,1}, to_apply=%region_0.0 | reduce | flops 7 | bytes 40 | tf_op jit(solution)/shard_map/reduce_min | solution.py:425
  10.7 1.7 %collective-permute-done.refs_2_.refs_3_ = f32[2,64,512]{2,1,0:T(8,128)S(1)} collective-permute-done((f32[2,64,512]{2,1,0:T(8,128)}, f32[2,64,512]{2,1,0:T(8,128)S(1)}, u32[]{:S(2)}, u32[]{:S(2)}) %collective-permute-start) | collective-permute-done | bytes 262176 | tf_op jit(solution)/shard_map/ppermute | solution.py:404
  12.4 0.1 collective-permute-start.2
  12.5 0.0 copy-done.3
  12.5 2.8 %prior.3 = (f32[256,256]{1,0:T(8,128)S(1)}, f32[128,512]{1,0:T(8,128)S(1)}, bf16[512,256]{1,0:T(8,128)(2,1)S(1)}, bf16[512,256]{1,0:T(8,128)(2,1)S(1)}, f32[1,1,512]{2,1,0:T(1,128)}) custom-call(s32[2,4]{1,0:T(2,128)S(1)} %copy-done.3, s32[2,4]{1,0:T(2,128)S(1)} %collective-permute-done.1.refs_1_, f32[2,512,512]{2,1,0:T(8,128)} %refs_1_.5), custom_call_target="tpu_custom_call" | custom-call | flops 402653184 | bytes 3672064 | tf_op jit(solution)/shard_map/prior/pallas_call | solution.py:122
  15.3 2.6 %collective-permute-done.3.refs_3_.refs_4_ = f32[2,64,512]{2,1,0:T(8,128)S(1)} collective-permute-done((f32[2,64,512]{2,1,0:T(8,128)S(1)}, f32[2,64,512]{2,1,0:T(8,128)S(1)}, u32[]{:S(2)}, u32[]{:S(2)}) %collective-permute-start.3) | collective-permute-done | bytes 262176 | tf_op jit(solution)/shard_map/ppermute | solution.py:404
  17.8 0.0 copy-done.4
  17.8 1.6 %links.1 = (f32[2,256,256]{2,1,0:T(8,128)S(1)}, f32[2,64,256]{2,1,0:T(8,128)S(1)}) custom-call(s32[2,4]{1,0:T(2,128)S(1)} %copy-done.4, f32[2,64,512]{2,1,0:T(8,128)S(1)} %copy-done.1, f32[2,64,512]{2,1,0:T(8,128)S(1)} %collective-permute-done.refs_2_.refs_3_, f32[2,64,512]{2,1,0:T(8,128)S(1)} %collective-permute-done.3.refs_3_.refs_4_, ...), custom_call_target="tpu_custom_call" | custom-call | flops 402653184 | bytes 3538944 | tf_op jit(solution)/shard_map/links/pallas_call | solution.py:122
  19.5 0.0 copy-start
  19.5 4.0 %collective-permute-done.2.refs_0_.refs_5_ = f32[2,64,512]{2,1,0:T(8,128)S(1)} collective-permute-done((f32[2,64,512]{2,1,0:T(8,128)S(1)}, f32[2,64,512]{2,1,0:T(8,128)S(1)}, u32[]{:S(2)}, u32[]{:S(2)}) %collective-permute-start.2) | collective-permute-done | bytes 262176 | tf_op jit(solution)/shard_map/ppermute | solution.py:404
  23.5 1.0 %segment.1 = (f32[2,256,256]{2,1,0:T(8,128)S(1)}, f32[512,256]{1,0:T(8,128)S(1)}) custom-call(f32[2,64,512]{2,1,0:T(8,128)S(1)} %collective-permute-done.2.refs_0_.refs_5_, f32[2,256,256]{2,1,0:T(8,128)S(1)} %get-tuple-element.32.refs_1_, f32[2,64,256]{2,1,0:T(8,128)S(1)} %get-tuple-element.33.refs_2_, ...), custom_call_target="tpu_custom_call" | custom-call | flops 402653184 | bytes 4587520 | tf_op jit(solution)/shard_map/segment/pallas_call | solution.py:122
  24.5 0.5 %collective-permute-start.4 = (f32[512,256]{1,0:T(8,128)S(1)}, f32[512,256]{1,0:T(8,128)S(1)}, u32[]{:S(2)}, u32[]{:S(2)}) collective-permute-start(f32[512,256]{1,0:T(8,128)S(1)} %get-tuple-element.36.refs_0_), channel_id=1, source_target_pairs={{0,4},{4,0},{8,12},{12,8},{16,20},{20,16},{24,28},{28,24},{1,5},{5... | collective-permute-start | bytes 1572872 | tf_op jit(solution)/shard_map/ppermute | solution.py:466
  25.0 1.5 %collective-permute-done.4.refs_1_.refs_5_ = f32[512,256]{1,0:T(8,128)S(1)} collective-permute-done((f32[512,256]{1,0:T(8,128)S(1)}, f32[512,256]{1,0:T(8,128)S(1)}, u32[]{:S(2)}, u32[]{:S(2)}) %collective-permute-start.4) | collective-permute-done | bytes 524320 | tf_op jit(solution)/shard_map/ppermute | solution.py:466
  26.6 0.6 %chip.1 = (f32[256,256]{1,0:T(8,128)S(1)}, f32[256,256]{1,0:T(8,128)S(1)}, f32[160,128]{1,0:T(8,128)S(1)}, f32[128,256]{1,0:T(8,128)S(1)}) custom-call(f32[512,256]{1,0:T(8,128)S(1)} %get-tuple-element.36.refs_0_, f32[512,256]{1,0:T(8,128)S(1)} %collective-permute-done.4.refs_1_.refs_5_), custom_call_target="tpu_custom_call" | custom-call | flops 301989888 | bytes 1785856 | tf_op jit(solution)/shard_map/chip/pallas_call | solution.py:122
  27.2 1.6 %collective-permute-start.5 = (f32[128,256]{1,0:T(8,128)S(1)}, f32[128,256]{1,0:T(8,128)S(1)}, u32[]{:S(2)}, u32[]{:S(2)}) collective-permute-start(f32[128,256]{1,0:T(8,128)S(1)} %get-tuple-element.39), channel_id=1, source_target_pairs={{0,8},{4,12},{8,0},{12,4},{16,24},{20,28},{24,16},{28,20},{1,9},{5... | collective-permute-start | bytes 393224 | tf_op jit(solution)/shard_map/ppermute | solution.py:505
  28.7 0.5 %collective-permute-start.7 = (f32[160,128]{1,0:T(8,128)S(1)}, f32[160,128]{1,0:T(8,128)S(1)}, u32[]{:S(2)}, u32[]{:S(2)}) collective-permute-start(f32[160,128]{1,0:T(8,128)S(1)} %get-tuple-element.40), channel_id=1, source_target_pairs={{0,8},{4,12},{8,0},{12,4},{16,24},{20,28},{24,16},{28,20},{1,9},{5... | collective-permute-start | bytes 245768 | tf_op jit(solution)/shard_map/ppermute | solution.py:499
  29.3 0.0 copy-done
  29.3 1.5 %maps.1 = (f32[2,256,512]{2,1,0:T(8,128)S(1)}, f32[1,128]{1,0:T(1,128)S(1)}) custom-call(s32[2,4]{1,0:T(2,128)S(1)} %copy-done.4, f32[2,512,512]{2,1,0:T(8,128)S(1)} %copy-done, f32[2,64,512]{2,1,0:T(8,128)S(1)} %copy-done.1, f32[2,64,512]{2,1,0:T(8,128)S(1)} %collective-permute-done.refs_2_.refs_3_, ...), custom_call_target="tpu_custom_call" | custom-call | flops 805306368 | bytes 4194816 | tf_op jit(solution)/shard_map/maps/pallas_call | solution.py:122
  30.8 2.8 %collective-permute-done.5.refs_2_.refs_8_ = f32[128,256]{1,0:T(8,128)S(1)} collective-permute-done((f32[128,256]{1,0:T(8,128)S(1)}, f32[128,256]{1,0:T(8,128)S(1)}, u32[]{:S(2)}, u32[]{:S(2)}) %collective-permute-start.5) | collective-permute-done | bytes 131104 | tf_op jit(solution)/shard_map/ppermute | solution.py:505
  33.6 0.0 collective-permute-start.6
  33.6 1.2 %collective-permute-done.7 = f32[160,128]{1,0:T(8,128)S(1)} collective-permute-done((f32[160,128]{1,0:T(8,128)S(1)}, f32[160,128]{1,0:T(8,128)S(1)}, u32[]{:S(2)}, u32[]{:S(2)}) %collective-permute-start.7) | collective-permute-done | bytes 81952 | tf_op jit(solution)/shard_map/ppermute | solution.py:499
  34.8 0.1 collective-permute-start.8
  34.9 1.3 %collective-permute-done.8.refs_5_.refs_11_ = f32[160,128]{1,0:T(8,128)S(1)} collective-permute-done((f32[160,128]{1,0:T(8,128)S(1)}, f32[160,128]{1,0:T(8,128)S(1)}, u32[]{:S(2)}, u32[]{:S(2)}) %collective-permute-start.8) | collective-permute-done | bytes 81952 | tf_op jit(solution)/shard_map/ppermute | solution.py:508
  36.1 0.0 collective-permute-done.6.refs_3_.refs_9_
  36.1 0.8 %merge.1 = f32[160,128]{1,0:T(8,128)S(1)} custom-call(f32[256,256]{1,0:T(8,128)S(1)} %get-tuple-element.37.refs_0_, f32[256,256]{1,0:T(8,128)S(1)} %get-tuple-element.38.refs_1_, f32[128,256]{1,0:T(8,128)S(1)} %collective-permute-done.5.refs_2_.refs_8_, f32[128,256]{1,0:T(8,128)S(1)} %collective-permute-done.6.refs_3_.refs_9_, ...), custom_call_target="tpu_custom_call" | custom-call | flops 301989888 | bytes 1032192 | tf_op jit(solution)/shard_map/merge/pallas_call | solution.py:122
  36.9 1.6 %collective-permute-start.9 = (f32[160,128]{1,0:T(8,128)S(1)}, f32[160,128]{1,0:T(8,128)S(1)}, u32[]{:S(2)}, u32[]{:S(2)}) collective-permute-start(f32[160,128]{1,0:T(8,128)S(1)} %merge.1), channel_id=1, source_target_pairs={{0,16},{4,20},{8,24},{12,28},{16,0},{20,4},{24,8},{28,12},{1,17},{... | collective-permute-start | bytes 245768 | tf_op jit(solution)/shard_map/ppermute | solution.py:499
  38.5 3.0 %prepare.1 = (bf16[384,256]{1,0:T(8,128)(2,1)S(1)}, bf16[384,256]{1,0:T(8,128)(2,1)S(1)}, bf16[2,256,512]{2,1,0:T(8,128)(2,1)S(1)}, bf16[2,256,512]{2,1,0:T(8,12...) custom-call(s32[2,4]{1,0:T(2,128)S(1)} %copy-done.4, f32[256,256]{1,0:T(8,128)S(1)} %get-tuple-element.34.refs_7_.refs_1_, ...), custom_call_target="tpu_custom_call" | custom-call | flops 1459617792 | bytes 7242240 | tf_op jit(solution)/shard_map/prepare/pallas_call | solution.py:122
  41.6 0.0 collective-permute-done.9
  41.6 0.1 collective-permute-start.10
  41.7 1.3 %collective-permute-done.10.refs_1_ = f32[160,128]{1,0:T(8,128)S(1)} collective-permute-done((f32[160,128]{1,0:T(8,128)S(1)}, f32[160,128]{1,0:T(8,128)S(1)}, u32[]{:S(2)}, u32[]{:S(2)}) %collective-permute-start.10) | collective-permute-done | bytes 81952 | tf_op jit(solution)/shard_map/ppermute | solution.py:503
  42.9 1.9 %finish.1 = (f32[2,128,512]{2,1,0:T(8,128)}, f32[2,64,512]{2,1,0:T(8,128)}) custom-call(f32[160,128]{1,0:T(8,128)S(1)} %broadcast_add_fusion.2.refs_0_, f32[160,128]{1,0:T(8,128)S(1)} %collective-permute-done.10.refs_1_, bf16[384,256]{1,0:T(8,128)(2,1)S(1)} %get-tuple-element.47.refs_2_, bf16[384,256]{1,0:T(8,128)(2,1)S(1)} %get-tuple-element.48.refs_3_, ...), custom_call_target="tpu_custom_call" | custom-call | flops 452984832 | bytes 4620288 | tf_op jit(solution)/shard_map/finish/pallas_call | solution.py:122
  (4 shorter events, 0.1 us)
Async XLA Ops:
  0.6 6.6 %copy-start.1 = (f32[2,64,512]{2,1,0:T(8,128)S(1)}, f32[2,64,512]{2,1,0:T(8,128)}, u32[]{:S(2)}) copy-start(f32[2,64,512]{2,1,0:T(8,128)} %refs_2_.3) | copy-start | bytes 786436
  0.6 11.7 %collective-permute-start = (f32[2,64,512]{2,1,0:T(8,128)}, f32[2,64,512]{2,1,0:T(8,128)S(1)}, u32[]{:S(2)}, u32[]{:S(2)}) collective-permute-start(f32[2,64,512]{2,1,0:T(8,128)} %refs_2_.3), channel_id=1, source_target_pairs={{0,1},{1,2},{2,3},{3,0},{4,5},{5,6},{6,7},{7,4},{8,9},{9,10},{10,1... | collective-permute-start | bytes 786440 | tf_op jit(solution)/shard_map/ppermute | solution.py:404
  3.7 5.7 %collective-permute-start.1 = (s32[2,4]{1,0:T(2,128)}, s32[2,4]{1,0:T(2,128)S(1)}, u32[]{:S(2)}, u32[]{:S(2)}) collective-permute-start(s32[2,4]{1,0:T(2,128)} %refs_0_.6), channel_id=1, source_target_pairs={{0,4},{4,8},{8,12},{12,16},{16,20},{20,24},{24,28},{28,0},{1,5},{5... | collective-permute-start | bytes 104 | tf_op jit(solution)/shard_map/ppermute | solution.py:404
  3.7 0.7 %copy-start.2 = (s32[2,4]{1,0:T(2,128)S(1)}, s32[2,4]{1,0:T(2,128)}, u32[]{:S(2)}) copy-start(s32[2,4]{1,0:T(2,128)} %refs_0_.6) | copy-start | bytes 100
  4.4 8.1 %copy-start.3 = (s32[2,4]{1,0:T(2,128)S(1)}, s32[2,4]{1,0:T(2,128)}, u32[]{:S(2)}) copy-start(s32[2,4]{1,0:T(2,128)} %refs_0_.6) | copy-start | bytes 100
  7.2 10.6 %copy-start.4 = (s32[2,4]{1,0:T(2,128)S(1)}, s32[2,4]{1,0:T(2,128)}, u32[]{:S(2)}) copy-start(s32[2,4]{1,0:T(2,128)} %refs_0_.9) | copy-start | bytes 100
  7.2 10.6 %collective-permute-start.3 = (f32[2,64,512]{2,1,0:T(8,128)S(1)}, f32[2,64,512]{2,1,0:T(8,128)S(1)}, u32[]{:S(2)}, u32[]{:S(2)}) collective-permute-start(f32[2,64,512]{2,1,0:T(8,128)S(1)} %broadcast_add_fusion), channel_id=1, source_target_pairs={{0,3},{1,0},{2,1},{3,2},{4,7},{5,4},{6,5},{7,6},{8,11},{9,8},{10,9... | collective-permute-start | bytes 786440 | tf_op jit(solution)/shard_map/ppermute | solution.py:404
  12.4 11.1 %collective-permute-start.2 = (f32[2,64,512]{2,1,0:T(8,128)S(1)}, f32[2,64,512]{2,1,0:T(8,128)S(1)}, u32[]{:S(2)}, u32[]{:S(2)}) collective-permute-start(f32[2,64,512]{2,1,0:T(8,128)S(1)} %broadcast_add_fusion.1), channel_id=1, source_target_pairs={{0,1},{1,2},{2,3},{3,0},{4,5},{5,6},{6,7},{7,4},{8,9},{9,10},{10,1... | collective-permute-start | bytes 786440 | tf_op jit(solution)/shard_map/ppermute | solution.py:404
  19.5 9.8 %copy-start = (f32[2,512,512]{2,1,0:T(8,128)S(1)}, f32[2,512,512]{2,1,0:T(8,128)}, u32[]{:S(2)}) copy-start(f32[2,512,512]{2,1,0:T(8,128)} %refs_1_.5) | copy-start | bytes 6291460
  24.5 2.0 %collective-permute-start.4 = (f32[512,256]{1,0:T(8,128)S(1)}, f32[512,256]{1,0:T(8,128)S(1)}, u32[]{:S(2)}, u32[]{:S(2)}) collective-permute-start(f32[512,256]{1,0:T(8,128)S(1)} %get-tuple-element.36.refs_0_), channel_id=1, source_target_pairs={{0,4},{4,0},{8,12},{12,8},{16,20},{20,16},{24,28},{28,24},{1,5},{5... | collective-permute-start | bytes 1572872 | tf_op jit(solution)/shard_map/ppermute | solution.py:466
  27.2 6.4 %collective-permute-start.5 = (f32[128,256]{1,0:T(8,128)S(1)}, f32[128,256]{1,0:T(8,128)S(1)}, u32[]{:S(2)}, u32[]{:S(2)}) collective-permute-start(f32[128,256]{1,0:T(8,128)S(1)} %get-tuple-element.39), channel_id=1, source_target_pairs={{0,8},{4,12},{8,0},{12,4},{16,24},{20,28},{24,16},{28,20},{1,9},{5... | collective-permute-start | bytes 393224 | tf_op jit(solution)/shard_map/ppermute | solution.py:505
  28.7 6.0 %collective-permute-start.7 = (f32[160,128]{1,0:T(8,128)S(1)}, f32[160,128]{1,0:T(8,128)S(1)}, u32[]{:S(2)}, u32[]{:S(2)}) collective-permute-start(f32[160,128]{1,0:T(8,128)S(1)} %get-tuple-element.40), channel_id=1, source_target_pairs={{0,8},{4,12},{8,0},{12,4},{16,24},{20,28},{24,16},{28,20},{1,9},{5... | collective-permute-start | bytes 245768 | tf_op jit(solution)/shard_map/ppermute | solution.py:499
  33.6 2.6 %collective-permute-start.6 = (f32[128,256]{1,0:T(8,128)S(1)}, f32[128,256]{1,0:T(8,128)S(1)}, u32[]{:S(2)}, u32[]{:S(2)}) collective-permute-start(f32[128,256]{1,0:T(8,128)S(1)} %collective-permute-done.5.refs_2_.refs_8_), channel_id=1, source_target_pairs={{0,4},{4,0},{8,12},{12,8},{16,20},{20,16},{24,28},{28,24},{1,5},{5... | collective-permute-start | bytes 393224 | tf_op jit(solution)/shard_map/ppermute | solution.py:508
  34.8 1.3 %collective-permute-start.8 = (f32[160,128]{1,0:T(8,128)S(1)}, f32[160,128]{1,0:T(8,128)S(1)}, u32[]{:S(2)}, u32[]{:S(2)}) collective-permute-start(f32[160,128]{1,0:T(8,128)S(1)} %broadcast_add_fusion.3.refs_4_.refs_10_), channel_id=1, source_target_pairs={{0,4},{4,0},{8,12},{12,8},{16,20},{20,16},{24,28},{28,24},{1,5},{5... | collective-permute-start | bytes 245768 | tf_op jit(solution)/shard_map/ppermute | solution.py:508
  36.9 4.6 %collective-permute-start.9 = (f32[160,128]{1,0:T(8,128)S(1)}, f32[160,128]{1,0:T(8,128)S(1)}, u32[]{:S(2)}, u32[]{:S(2)}) collective-permute-start(f32[160,128]{1,0:T(8,128)S(1)} %merge.1), channel_id=1, source_target_pairs={{0,16},{4,20},{8,24},{12,28},{16,0},{20,4},{24,8},{28,12},{1,17},{... | collective-permute-start | bytes 245768 | tf_op jit(solution)/shard_map/ppermute | solution.py:499
  41.6 1.3 %collective-permute-start.10 = (f32[160,128]{1,0:T(8,128)S(1)}, f32[160,128]{1,0:T(8,128)S(1)}, u32[]{:S(2)}, u32[]{:S(2)}) collective-permute-start(f32[160,128]{1,0:T(8,128)S(1)} %broadcast_add_fusion.2.refs_0_), channel_id=1, source_target_pairs={{0,4},{4,0},{8,12},{12,8},{16,20},{20,16},{24,28},{28,24},{1,5},{5... | collective-permute-start | bytes 245768 | tf_op jit(solution)/shard_map/ppermute | solution.py:503

commit v12 on v11

--- a/solution.py
+++ b/solution.py
@@ -99,6 +99,26 @@
     first = lax.axis_index("seg") == 0
     last = prior_ref.shape[0] - 1
     return [jnp.where(first, fill_ref[0, j], prior_ref[last, j]) for j in range(slots)]
+
+
+def order_of(chosen, blocks):
+    slots = len(chosen)
+    rest = [jnp.int32(0)] * (blocks - slots)
+    place = []
+    seen = jnp.int32(0)
+    for b in range(blocks):
+        hit = jnp.int32(0)
+        where = jnp.int32(0)
+        for j in range(slots):
+            same = (chosen[j] == b).astype(jnp.int32)
+            hit = hit + same
+            where = where + same * j
+        free = 1 - hit
+        for q in range(blocks - slots):
+            rest[q] = rest[q] + jnp.where(seen == q, free * b, 0)
+        place.append(jnp.where(hit > 0, where, slots + seen))
+        seen = seen + free
+    return rest, place
 
 
 def vmem(count):
@@ -208,33 +228,54 @@
 
 
 def links_kernel(plan, mask_ref, *refs):
-    count = len(plan.early)
-    parts, refs = refs[:count], refs[count:]
-    *pick_refs, links_t_ref, late_keep_ref, rows_ref = refs
+    parts, refs = refs[: len(plan.early)], refs[len(plan.early) :]
+    *pick_refs, links_t_ref, rows_ref = refs
     rows_ref[...] = jnp.zeros_like(rows_ref)
     for p in range(links_t_ref.shape[0]):
         pick = (pick_refs[2 * p][...], pick_refs[2 * p + 1][...])
         for owners, part in zip(plan.early, parts):
             put_rows(mask_ref, p, owners, part[p], rows_ref, lambda kept: mm(kept, pick))
         links_t_ref[p] = rows_ref[...].T
-        for s, slot in enumerate(slots_of(plan.late, late_keep_ref.shape[1])):
-            block = slice(s * BLOCK, (s + 1) * BLOCK)
-            ones = jnp.ones((BLOCK, late_keep_ref.shape[2]), F32)
-            late_keep_ref[p, block, :] = kept_rows(mask_ref, p, slot, ones)
-
-
-def segment_kernel(plan, panels, *refs):
-    late_ref, early_ref, keep_ref, *refs = refs
-    pick_refs, base_refs = refs[: 2 * panels], refs[2 * panels : 3 * panels]
-    links_t_ref, whole_ref = refs[3 * panels :]
+
+
+def kept_block(mask_ref, panel, owners, part):
+    return jnp.concatenate(
+        [
+            kept_rows(mask_ref, panel, slot, part[s * BLOCK : (s + 1) * BLOCK, :])
+            for s, slot in enumerate(slots_of(owners, part.shape[0]))
+        ],
+        0,
+    )
+
+
+def chosen_kernel(owners, mask_ref, part, *refs):
+    *pick_refs, out_ref = refs
+    for p in range(out_ref.shape[0]):
+        pick = (pick_refs[2 * p][...], pick_refs[2 * p + 1][...])
+        out_ref[p] = mm(kept_block(mask_ref, p, owners, part[p]), pick)
+
+
+def rest_kernel(owners, mask_ref, fill_ref, prior_ref, inv_ref, *refs):
+    *parts, _, out_ref, map_ref = refs
+    odd = (lax.axis_index("row") & 1) == 1
+    for p in range(out_ref.shape[0]):
+        part = parts[0][p] if len(parts) == 1 else jnp.where(odd, parts[1][p], parts[0][p])
+        map_ref[...] = triangular_mm(kept_block(mask_ref, p, owners, part), inv_ref[p])
+        rest, _ = order_of(chosen_of(p, fill_ref, prior_ref), map_ref.shape[1] // BLOCK)
+        for t in range(len(rest) // 2):
+            out_ref[p, :, t * LANES : (t + 1) * LANES] = two_blocks(
+                tile_of(map_ref), rest[2 * t], rest[2 * t + 1]
+            )
+
+
+def segment_kernel(plan, panels, late_ref, early_ref, *refs):
+    base_refs, (links_t_ref, whole_ref) = refs[:panels], refs[panels:]
     size = links_t_ref.shape[1]
-    rows = keep_ref.shape[1]
+    rows = late_ref.shape[1]
     here = lax.broadcasted_iota(jnp.int32, (size, size), 1) // rows == at_row(plan.late)
     cov = link_t = None
     for p in range(panels - 1, -1, -1):
-        pick = (pick_refs[2 * p][...], pick_refs[2 * p + 1][...])
-        late = mm(late_ref[p], pick) * keep_ref[p]
-        late_t = jnp.concatenate([late] * (size // rows), 0).T
+        late_t = jnp.concatenate([late_ref[p]] * (size // rows), 0).T
         own_t = jnp.where(here, late_t, early_ref[p])
         links_t_ref[p] = own_t
         if cov is None:
@@ -248,13 +289,12 @@
 
 
 def maps_kernel(plan, mask_ref, inv_ref, *refs):
-    count = len(plan.early)
-    parts, (late_ref, maps_ref, token_ref, rows_ref) = refs[:count], refs[count:]
+    *parts, maps_ref, token_ref, rows_ref = refs
     token_ref[...] = jnp.zeros_like(token_ref)
+    rows_ref[...] = jnp.zeros_like(rows_ref)
     for p in range(inv_ref.shape[0]):
         for owners, part in zip(plan.early, parts):
             put_rows(mask_ref, p, owners, part[p], rows_ref, lambda kept: kept)
-        put_rows(mask_ref, p, plan.late, late_ref[p], rows_ref, lambda kept: kept)
         maps_ref[p] = triangular_mm(rows_ref[...], inv_ref[p])
 
 
@@ -305,19 +345,20 @@
         refs[9 + 2 * i][...] = jnp.where(is_lower(), whole[half:], whole[:half])
 
 
-def prepare_kernel(levels, panels, mask_ref, *refs):
+def prepare_kernel(plan, levels, panels, mask_ref, fill_ref, prior_ref, *refs):
     base_refs, own_refs, refs = refs[:panels], refs[panels : 2 * panels], refs[2 * panels :]
-    (other_ref, maps_ref, links_t_ref), refs = refs[:3], refs[3:]
+    (other_ref, maps_ref, links_t_ref, late_ref, rest_ref), refs = refs[:5], refs[5:]
     past_refs, refs = refs[: 4 * (levels > 1)], refs[4 * (levels > 1) :]
-    left_high, left_low, right_high, right_low, const_ref, token_ref, scratch = refs
+    left_high, left_low, right_high, right_low, const_ref, token_ref, scratch, map_ref, late_map_ref = refs
     token_ref[...] = jnp.zeros_like(token_ref)
-    own_cols = own_refs[0].shape[0]
+    own_cols, width = own_refs[0].shape
+    late_at = at_row(plan.late)
     size = base_refs[0].shape[0]
     row_at = lax.axis_index("row")
     rows = left_high.shape[0] // panels - own_cols
-    at_row = lax.broadcasted_iota(jnp.int32, (size, size), 0)
-    at_col = lax.broadcasted_iota(jnp.int32, (size, size), 1)
-    eye = (at_row == at_col).astype(F32)
+    row = lax.broadcasted_iota(jnp.int32, (size, size), 0)
+    column = lax.broadcasted_iota(jnp.int32, (size, size), 1)
+    eye = (row == column).astype(F32)
     other = other_ref[size:, :]
     lower = is_lower()
     if past_refs:
@@ -336,9 +377,18 @@
         gain = jnp.where(lower, other, 0.0)
     own_at = pl.ds(pl.multiple_of(row_at * own_cols, own_cols), own_cols)
     own_rows = pl.ds(pl.multiple_of(row_at * rows, rows), rows)
+    late_rows = pl.ds(pl.multiple_of(late_at * rows, rows), rows)
     for p in range(panels - 1, -1, -1):
-        whole = split(maps_ref[p])
-        own_t = split(maps_ref[p, :, own_at].T)
+        late_map_ref[:, :size] = late_ref[p]
+        late_map_ref[:, size:] = rest_ref[p]
+        _, place = order_of(chosen_of(p, fill_ref, prior_ref), width // BLOCK)
+        map_ref[...] = maps_ref[p]
+        for t in range(len(place) // 2):
+            map_ref[late_rows, t * LANES : (t + 1) * LANES] = two_blocks(
+                tile_of(late_map_ref), place[2 * t], place[2 * t + 1]
+            )
+        whole = split(map_ref[...])
+        own_t = split(map_ref[:, own_at].T)
         scratch[:, :size] = to_t
         scratch[:, size:] = gain
         to_parts = split(to_t)
@@ -421,23 +471,31 @@
         priors.append(own_prior)
         picks += high_low
         tokens.append(token)
-    second = factor_off + tokens[-1]
-    index_gate = jnp.minimum(jnp.min(prior_fill), 0).astype(F32)
-
-    ups, downs = [factor_off], [second]
-    for i in range(row_count // 2):
-        ups.append(turn(ups[-1] + index_gate if i else ups[-1], "row", 1))
+    short = row_count == 4
+    ups, downs = [factor_off], [factor_off + tokens[-1]]
+    for _ in range(row_count // 2 - short):
+        ups.append(turn(ups[-1], "row", 1))
     for _ in range((row_count - 1) // 2):
         downs.append(turn(downs[-1], "row", -1))
-    parts, late = ups[:-1] + downs[:0:-1], ups[-1]
-    far = len(ups) - 1
+    far = row_count // 2
     came = [d for d in range(row_count) if d != far]
-    whose = [tuple((i - d) % row_count for i in range(row_count)) for d in (*came, far)]
-    plan = Plan(tuple(whose[:-1]), whose[-1])
-
-    links, late_keep = call(
+    whose = [tuple((i - d) % row_count for i in range(row_count)) for d in range(row_count)]
+    plan = Plan(tuple(whose[d] for d in came), whose[far])
+    parts = ups[:far] + downs[:0:-1]
+    index_gate = jnp.minimum(jnp.min(prior_fill), 0).astype(F32)
+    (late,) = call(
+        functools.partial(chosen_kernel, whose[1] if short else whose[far]),
+        [shape(panels, rows, chosen_cols)],
+        [fill_mask],
+        [ups[-1] + index_gate, *picks],
+        flops=6 * panels * rows * chosen_cols * width,
+        name="chosen",
+    )
+    if short:
+        late = turn(late, "row", 1)
+    (links,) = call(
         functools.partial(links_kernel, plan),
-        [shape(panels, size, size), shape(panels, rows, size)],
+        [shape(panels, size, size)],
         [fill_mask],
         [*parts, *picks],
         scratch=[pltpu.VMEM((size, chosen_cols), F32)],
@@ -448,15 +506,15 @@
         functools.partial(segment_kernel, plan, panels),
         [shape(panels, size, size), shape(2 * size, size)],
         [],
-        [late, links, late_keep, *picks, *bases],
-        flops=6 * panels * rows * size * width + 18 * (panels - 1) * size**3,
+        [late, links, *bases],
+        flops=18 * (panels - 1) * size**3,
         name="segment",
     )
     maps, maps_token = call(
         functools.partial(maps_kernel, plan),
         [shape(panels, size, width), shape(1, half)],
         [fill_mask],
-        [inv_diag, *parts, late],
+        [inv_diag, *parts],
         scratch=[pltpu.VMEM((size, width), F32)],
         flops=6 * panels * size * width * width,
         mib=24,
@@ -474,6 +532,22 @@
         flops=18 * size**3,
         name="chip",
     )
+    held = [ups[-1], downs[-1]] if short else [ups[-1]]
+    held_by = whose[far]
+    if short:
+        held_by = tuple(whose[-1][i] if i % 2 else whose[1][i] for i in range(row_count))
+    (rest,) = call(
+        functools.partial(rest_kernel, held_by),
+        [shape(panels, rows, width - chosen_cols)],
+        [fill_mask, fill_blocks, prior_fill],
+        [inv_diag, *held, send],
+        scratch=[pltpu.VMEM((rows, width), F32)],
+        flops=6 * panels * rows * width * width,
+        mib=24,
+        name="rest",
+    )
+    if short:
+        rest = lax.ppermute(rest, "row", [(i, i ^ 1) for i in range(row_count)])
     past = None
     after = (jnp.zeros(half_packed.shape, F32),) * 2
     levels = (chips - 1).bit_length()
@@ -484,11 +558,15 @@
         left = jax.ShapeDtypeStruct((panels * total, size), BF16)
         right = jax.ShapeDtypeStruct((panels, size, width), BF16)
         return call(
-            functools.partial(prepare_kernel, levels, panels),
+            functools.partial(prepare_kernel, plan, levels, panels),
             [left, left, right, right, shape(panels, total, width), shape(1, half)],
-            [fill_mask],
-            [*bases, *priors, other_whole, maps, links_t, *(past or ())],
-            scratch=[pltpu.VMEM((size, width), F32)],
+            [fill_mask, fill_blocks, prior_fill],
+            [*bases, *priors, other_whole, maps, links_t, late, rest, *(past or ())],
+            scratch=[
+                pltpu.VMEM((size, width), F32),
+                pltpu.VMEM((size, width), F32),
+                pltpu.VMEM((rows, width), F32),
+            ],
             flops=6 * panels * size * (total * size + size * width + total * width + 3 * size * size),
             mib=24,
             name="prepare",

time: 45 us -> 44.9 us (level)
  waiting for transfers between devices: 16.3 us -> 11.8 us
  starting transfers between devices: 9.65 us -> 12 us
  Pallas kernels: 16 us -> 18 us
    ppermute x4, waiting for transfers between devices: 8.25 us -> 5.09 us  [turn(): lax.ppermute(x, axis, [(i, (i + distance) % count) for i in range(count)])]
    ppermute x1, starting transfers between devices: 0.51 us -> 2.7 us  [body(): other_whole = lax.ppermute(own_whole, 'seg', swap)]
    pallas_call x9 -> x11, Pallas kernels: 16 us -> 18 us  [call(): pl.pallas_call(inner, out_shape=[*outs, *(jax.ShapeDtypeStruct(a.shape, a...]
    ppermute x1, waiting for transfers between devices: 2.78 us -> 1.4 us  [body(): got_t = lax.ppermute(send_t, 'seg', partner)]
  transfers between devices with their start and end apart: 11 -> 12, of which waited for: 8 -> 7; matrix products, arithmetic and copies ran while one was open for 2% -> 2% of each run, Pallas kernels for 26% -> 33%
where the time goes in v12:
time: 44.9 us; the launch traced here: 44.7 us
  Pallas kernels  18 us (40%)
  starting transfers between devices  12 us (27%)
  waiting for transfers between devices  11.8 us (26%)
  between operations  1.48 us (3%)
  local copies, waits for them, and re-layouts  0.7 us (2%)
  other arithmetic  0.7 us (2%)
    pallas_call x11, Pallas kernels, call(): pl.pallas_call(inner, out_shape=[*outs, *(jax.ShapeDtypeStruct(a.shape, a...  18 us
    ppermute x4, starting transfers between devices, turn(): lax.ppermute(x, axis, [(i, (i + distance) % count) for i in range(count)])  5.3 us
    ppermute x4, waiting for transfers between devices, turn(): lax.ppermute(x, axis, [(i, (i + distance) % count) for i in range(count)])  5.09 us
    ppermute x1, starting transfers between devices, body(): other_whole = lax.ppermute(own_whole, 'seg', swap)  2.7 us
    ppermute x2, starting transfers between devices, body(): got = lax.ppermute(send, 'seg', partner)  2.22 us
    ppermute x1, starting transfers between devices, body(): got_t = lax.ppermute(send_t, 'seg', partner)  1.59 us
    ppermute x1, waiting for transfers between devices, body(): other_whole = lax.ppermute(own_whole, 'seg', swap)  1.54 us
    ppermute x1, waiting for transfers between devices, body(): got_t = lax.ppermute(send_t, 'seg', partner)  1.4 us
  transfers between devices with their start and end apart: 12, of which 7 were waited for; matrix products, arithmetic and copies ran while one was open for 2% of the time, Pallas kernels for 33%

profile of v12, /device:TPU:0, one launch (start us, length us, event | category | flops | bytes accessed | tf_op | source)
XLA Modules:
  0.0 44.7 jit_solution(9312370967067389182)
XLA Ops:
  0.6 0.0 copy-start.1
  0.6 0.5 %collective-permute-start.1 = (s32[2,4]{1,0:T(2,128)}, s32[2,4]{1,0:T(2,128)S(1)}, u32[]{:S(2)}, u32[]{:S(2)}) collective-permute-start(s32[2,4]{1,0:T(2,128)} %refs_1_.9), channel_id=1, source_target_pairs={{0,4},{4,8},{8,12},{12,16},{16,20},{20,24},{24,28},{28,0},{1,5},{5... | collective-permute-start | bytes 104 | tf_op jit(solution)/shard_map/ppermute | solution.py:454
  1.1 2.6 %collective-permute-start = (f32[2,64,512]{2,1,0:T(8,128)}, f32[2,64,512]{2,1,0:T(8,128)S(1)}, u32[]{:S(2)}, u32[]{:S(2)}) collective-permute-start(f32[2,64,512]{2,1,0:T(8,128)} %refs_2_.3), channel_id=1, source_target_pairs={{0,1},{1,2},{2,3},{3,0},{4,5},{5,6},{6,7},{7,4},{8,9},{9,10},{10,1... | collective-permute-start | bytes 786440 | tf_op jit(solution)/shard_map/ppermute | solution.py:454
  3.8 0.0 copy-start.2
  3.8 0.7 %copy-done.2 = s32[2,4]{1,0:T(2,128)S(1)} copy-done((s32[2,4]{1,0:T(2,128)S(1)}, s32[2,4]{1,0:T(2,128)}, u32[]{:S(2)}) %copy-start.2) | copy-done | bytes 56
  4.5 0.0 copy-start.3
  4.5 2.8 %prior.3 = (f32[256,256]{1,0:T(8,128)S(1)}, f32[128,512]{1,0:T(8,128)S(1)}, bf16[512,256]{1,0:T(8,128)(2,1)S(1)}, bf16[512,256]{1,0:T(8,128)(2,1)S(1)}, f32[1,1,512]{2,1,0:T(1,128)S(1)}) custom-call(s32[2,4]{1,0:T(2,128)S(1)} %copy-done.2, f32[2,512,512]{2,1,0:T(8,128)} %refs_3_.1), custom_call_target="tpu_custom_call" | custom-call | flops 402653184 | bytes 3672064 | tf_op jit(solution)/shard_map/prior/pallas_call | solution.py:142
  7.2 0.0 copy-start.4
  7.2 0.0 copy-done.1
  7.3 2.1 %collective-permute-start.3 = (f32[2,64,512]{2,1,0:T(8,128)S(1)}, f32[2,64,512]{2,1,0:T(8,128)S(1)}, u32[]{:S(2)}, u32[]{:S(2)}) collective-permute-start(f32[2,64,512]{2,1,0:T(8,128)S(1)} %broadcast_add_fusion), channel_id=1, source_target_pairs={{0,3},{1,0},{2,1},{3,2},{4,7},{5,4},{6,5},{7,6},{8,11},{9,8},{10,9... | collective-permute-start | bytes 786440 | tf_op jit(solution)/shard_map/ppermute | solution.py:454
  9.4 0.0 collective-permute-done.1.refs_1_.refs_2_
  9.4 0.6 %reduce_min.9 = s32[]{:T(128)} reduce(s32[2,4]{1,0:T(2,128)S(1)} %collective-permute-done.1.refs_1_.refs_2_, s32[]{:T(128)} %constant.0.clone.1), dimensions={0,1}, to_apply=%region_0.0 | reduce | flops 7 | bytes 40 | tf_op jit(solution)/shard_map/reduce_min | solution.py:485
  10.7 0.0 copy-done.3
  10.7 2.8 %prior.2 = (f32[256,256]{1,0:T(8,128)S(1)}, f32[128,512]{1,0:T(8,128)S(1)}, bf16[512,256]{1,0:T(8,128)(2,1)S(1)}, bf16[512,256]{1,0:T(8,128)(2,1)S(1)}, f32[1,1,512]{2,1,0:T(1,128)}) custom-call(s32[2,4]{1,0:T(2,128)S(1)} %copy-done.3, s32[2,4]{1,0:T(2,128)S(1)} %collective-permute-done.1.refs_1_.refs_2_, f32[2,512,512]{2,1,0:T(8,128)} %refs_3_.1), custom_call_target="tpu_custom_call" | custom-call | flops 402653184 | bytes 3672064 | tf_op jit(solution)/shard_map/prior/pallas_call | solution.py:142
  13.5 0.0 collective-permute-done.refs_2_.refs_3_.refs_4_
  13.5 0.0 copy-done.4
  13.5 0.9 %chosen.1 = f32[2,64,256]{2,1,0:T(8,128)S(1)} custom-call(s32[2,4]{1,0:T(2,128)S(1)} %copy-done.4, f32[2,64,512]{2,1,0:T(8,128)S(1)} %broadcast_add_fusion.1.refs_1_, bf16[512,256]{1,0:T(8,128)(2,1)S(1)} %get-tuple-element.25.refs_2_.refs_4_, bf16[512,256]{1,0:T(8,128)(2,1)S(1)} %get-tuple-element.26.refs_3_.refs_5_, ...), custom_call_target="tpu_custom_call" | custom-call | flops 100663296 | bytes 2490368 | tf_op jit(solution)/shard_map/chosen/pallas_call | solution.py:142
  14.5 0.0 copy-start
  14.5 0.1 collective-permute-start.2
  14.6 4.2 %collective-permute-done.3.refs_3_.refs_4_.refs_5_ = f32[2,64,512]{2,1,0:T(8,128)S(1)} collective-permute-done((f32[2,64,512]{2,1,0:T(8,128)S(1)}, f32[2,64,512]{2,1,0:T(8,128)S(1)}, u32[]{:S(2)}, u32[]{:S(2)}) %collective-permute-start.3) | collective-permute-done | bytes 262176 | tf_op jit(solution)/shard_map/ppermute | solution.py:454
  18.8 1.7 %links.1.refs_1_ = f32[2,256,256]{2,1,0:T(8,128)S(1)} custom-call(s32[2,4]{1,0:T(2,128)S(1)} %copy-done.4, f32[2,64,512]{2,1,0:T(8,128)S(1)} %copy-done.1, f32[2,64,512]{2,1,0:T(8,128)S(1)} %collective-permute-done.refs_2_.refs_3_.refs_4_, f32[2,64,512]{2,1,0:T(8,128)S(1)} %collective-permute-done.3.refs_3_.refs_4_.refs_5_, ...), custom_call_target="tpu_custom_call" | custom-call | flops 402653184 | bytes 3407872 | tf_op jit(solution)/shard_map/links/pallas_call | solution.py:142
  20.4 0.9 %collective-permute-done.2.refs_0_.refs_10_ = f32[2,64,256]{2,1,0:T(8,128)S(1)} collective-permute-done((f32[2,64,256]{2,1,0:T(8,128)S(1)}, f32[2,64,256]{2,1,0:T(8,128)S(1)}, u32[]{:S(2)}, u32[]{:S(2)}) %collective-permute-start.2) | collective-permute-done | bytes 131104 | tf_op jit(solution)/shard_map/ppermute | solution.py:454
  21.3 0.6 %segment.1 = (f32[2,256,256]{2,1,0:T(8,128)S(1)}, f32[512,256]{1,0:T(8,128)S(1)}) custom-call(f32[2,64,256]{2,1,0:T(8,128)S(1)} %collective-permute-done.2.refs_0_.refs_10_, f32[2,256,256]{2,1,0:T(8,128)S(1)} %links.1.refs_1_, f32[256,256]{1,0:T(8,128)S(1)} %get-tuple-element.30.refs_2_.refs_3_, f32[256,256]{1,0:T(8,128)S(1)} %get-tuple-element.31.refs_3_.refs_4_), custom_call_target="tpu_custom_call" | custom-call | flops 301989888 | bytes 2228224 | tf_op jit(solution)/shard_map/segment/pallas_call | solution.py:142
  22.0 2.7 %collective-permute-start.4 = (f32[512,256]{1,0:T(8,128)S(1)}, f32[512,256]{1,0:T(8,128)S(1)}, u32[]{:S(2)}, u32[]{:S(2)}) collective-permute-start(f32[512,256]{1,0:T(8,128)S(1)} %get-tuple-element.32.refs_0_), channel_id=1, source_target_pairs={{0,4},{4,0},{8,12},{12,8},{16,20},{20,16},{24,28},{28,24},{1,5},{5... | collective-permute-start | bytes 1572872 | tf_op jit(solution)/shard_map/ppermute | solution.py:524
  24.7 1.5 %collective-permute-done.4.refs_1_.refs_7_ = f32[512,256]{1,0:T(8,128)S(1)} collective-permute-done((f32[512,256]{1,0:T(8,128)S(1)}, f32[512,256]{1,0:T(8,128)S(1)}, u32[]{:S(2)}, u32[]{:S(2)}) %collective-permute-start.4) | collective-permute-done | bytes 524320 | tf_op jit(solution)/shard_map/ppermute | solution.py:524
  26.2 0.6 %chip.1 = (f32[256,256]{1,0:T(8,128)S(1)}, f32[256,256]{1,0:T(8,128)S(1)}, f32[160,128]{1,0:T(8,128)S(1)}, f32[128,256]{1,0:T(8,128)S(1)}) custom-call(f32[512,256]{1,0:T(8,128)S(1)} %get-tuple-element.32.refs_0_, f32[512,256]{1,0:T(8,128)S(1)} %collective-permute-done.4.refs_1_.refs_7_), custom_call_target="tpu_custom_call" | custom-call | flops 301989888 | bytes 1785856 | tf_op jit(solution)/shard_map/chip/pallas_call | solution.py:142
  26.8 1.6 %collective-permute-start.5 = (f32[128,256]{1,0:T(8,128)S(1)}, f32[128,256]{1,0:T(8,128)S(1)}, u32[]{:S(2)}, u32[]{:S(2)}) collective-permute-start(f32[128,256]{1,0:T(8,128)S(1)} %get-tuple-element.35), channel_id=1, source_target_pairs={{0,8},{4,12},{8,0},{12,4},{16,24},{20,28},{24,16},{28,20},{1,9},{5... | collective-permute-start | bytes 393224 | tf_op jit(solution)/shard_map/ppermute | solution.py:583
  28.4 0.5 %collective-permute-start.7 = (f32[160,128]{1,0:T(8,128)S(1)}, f32[160,128]{1,0:T(8,128)S(1)}, u32[]{:S(2)}, u32[]{:S(2)}) collective-permute-start(f32[160,128]{1,0:T(8,128)S(1)} %get-tuple-element.36.refs_6_), channel_id=1, source_target_pairs={{0,8},{4,12},{8,0},{12,4},{16,24},{20,28},{24,16},{28,20},{1,9},{5... | collective-permute-start | bytes 245768 | tf_op jit(solution)/shard_map/ppermute | solution.py:577
  28.9 0.0 copy-done
  28.9 1.5 %maps.1 = (f32[2,256,512]{2,1,0:T(8,128)S(1)}, f32[1,128]{1,0:T(1,128)S(1)}) custom-call(s32[2,4]{1,0:T(2,128)S(1)} %copy-done.4, f32[2,512,512]{2,1,0:T(8,128)S(1)} %copy-done, f32[2,64,512]{2,1,0:T(8,128)S(1)} %copy-done.1, f32[2,64,512]{2,1,0:T(8,128)S(1)} %collective-permute-done.refs_2_.refs_3_.refs_4_, ...), custom_call_target="tpu_custom_call" | custom-call | flops 805306368 | bytes 3932672 | tf_op jit(solution)/shard_map/maps/pallas_call | solution.py:142
  30.5 1.3 %rest.1 = f32[2,64,256]{2,1,0:T(8,128)S(1)} custom-call(s32[2,4]{1,0:T(2,128)S(1)} %copy-done.4, s32[2,4]{1,0:T(2,128)S(1)} %copy-done.3, s32[2,4]{1,0:T(2,128)S(1)} %collective-permute-done.1.refs_1_.refs_2_, f32[2,512,512]{2,1,0:T(8,128)S(1)} %copy-done, f32[2,64,512]{2,1,0:T(8,128)S(1)} %collective-permute-done.refs_2_.refs_3_.refs_4_, ...), custom_call_target="tpu_custom_call" | custom-call | flops 201326592 | bytes 2834432 | tf_op jit(solution)/shard_map/rest/pallas_call | solution.py:142
  31.7 0.1 collective-permute-start.10
  31.8 1.4 %collective-permute-done.5.refs_2_.refs_12_ = f32[128,256]{1,0:T(8,128)S(1)} collective-permute-done((f32[128,256]{1,0:T(8,128)S(1)}, f32[128,256]{1,0:T(8,128)S(1)}, u32[]{:S(2)}, u32[]{:S(2)}) %collective-permute-start.5) | collective-permute-done | bytes 131104 | tf_op jit(solution)/shard_map/ppermute | solution.py:583
  33.2 0.0 collective-permute-start.6
  33.2 1.2 %collective-permute-done.7 = f32[160,128]{1,0:T(8,128)S(1)} collective-permute-done((f32[160,128]{1,0:T(8,128)S(1)}, f32[160,128]{1,0:T(8,128)S(1)}, u32[]{:S(2)}, u32[]{:S(2)}) %collective-permute-start.7) | collective-permute-done | bytes 81952 | tf_op jit(solution)/shard_map/ppermute | solution.py:577
  34.4 0.1 collective-permute-start.8
  34.5 1.3 %collective-permute-done.8.refs_5_.refs_15_ = f32[160,128]{1,0:T(8,128)S(1)} collective-permute-done((f32[160,128]{1,0:T(8,128)S(1)}, f32[160,128]{1,0:T(8,128)S(1)}, u32[]{:S(2)}, u32[]{:S(2)}) %collective-permute-start.8) | collective-permute-done | bytes 81952 | tf_op jit(solution)/shard_map/ppermute | solution.py:586
  35.8 0.0 collective-permute-done.6.refs_3_.refs_13_
  35.8 0.8 %merge.1 = f32[160,128]{1,0:T(8,128)S(1)} custom-call(f32[256,256]{1,0:T(8,128)S(1)} %get-tuple-element.33.refs_0_, f32[256,256]{1,0:T(8,128)S(1)} %get-tuple-element.34.refs_1_, f32[128,256]{1,0:T(8,128)S(1)} %collective-permute-done.5.refs_2_.refs_12_, f32[128,256]{1,0:T(8,128)S(1)} %collective-permute-done.6.refs_3_.refs_13_, ...), custom_call_target="tpu_custom_call" | custom-call | flops 301989888 | bytes 1032192 | tf_op jit(solution)/shard_map/merge/pallas_call | solution.py:142
  36.6 1.7 %collective-permute-start.9 = (f32[160,128]{1,0:T(8,128)S(1)}, f32[160,128]{1,0:T(8,128)S(1)}, u32[]{:S(2)}, u32[]{:S(2)}) collective-permute-start(f32[160,128]{1,0:T(8,128)S(1)} %merge.1), channel_id=1, source_target_pairs={{0,16},{4,20},{8,24},{12,28},{16,0},{20,4},{24,8},{28,12},{1,17},{... | collective-permute-start | bytes 245768 | tf_op jit(solution)/shard_map/ppermute | solution.py:577
  38.3 0.0 collective-permute-done.10.refs_11_
  38.3 3.1 %prepare.1 = (bf16[384,256]{1,0:T(8,128)(2,1)S(1)}, bf16[384,256]{1,0:T(8,128)(2,1)S(1)}, bf16[2,256,512]{2,1,0:T(8,128)(2,1)S(1)}, bf16[2,256,512]{2,1,0:T(8,12...) custom-call(s32[2,4]{1,0:T(2,128)S(1)} %copy-done.4, s32[2,4]{1,0:T(2,128)S(1)} %copy-done.3, ...), custom_call_target="tpu_custom_call" | custom-call | flops 1459617792 | bytes 7504384 | tf_op jit(solution)/shard_map/prepare/pallas_call | solution.py:142
  41.4 0.0 collective-permute-done.9
  41.4 0.1 collective-permute-start.11
  41.5 1.3 %collective-permute-done.11.refs_1_ = f32[160,128]{1,0:T(8,128)S(1)} collective-permute-done((f32[160,128]{1,0:T(8,128)S(1)}, f32[160,128]{1,0:T(8,128)S(1)}, u32[]{:S(2)}, u32[]{:S(2)}) %collective-permute-start.11) | collective-permute-done | bytes 81952 | tf_op jit(solution)/shard_map/ppermute | solution.py:581
  42.8 1.9 %finish.1 = (f32[2,128,512]{2,1,0:T(8,128)}, f32[2,64,512]{2,1,0:T(8,128)}) custom-call(f32[160,128]{1,0:T(8,128)S(1)} %broadcast_add_fusion.2.refs_0_, f32[160,128]{1,0:T(8,128)S(1)} %collective-permute-done.11.refs_1_, bf16[384,256]{1,0:T(8,128)(2,1)S(1)} %get-tuple-element.43.refs_2_, bf16[384,256]{1,0:T(8,128)(2,1)S(1)} %get-tuple-element.44.refs_3_, ...), custom_call_target="tpu_custom_call" | custom-call | flops 452984832 | bytes 4620288 | tf_op jit(solution)/shard_map/finish/pallas_call | solution.py:142
  (4 shorter events, 0.1 us)
Async XLA Ops:
  0.6 6.6 %copy-start.1 = (f32[2,64,512]{2,1,0:T(8,128)S(1)}, f32[2,64,512]{2,1,0:T(8,128)}, u32[]{:S(2)}) copy-start(f32[2,64,512]{2,1,0:T(8,128)} %refs_2_.3) | copy-start | bytes 786436
  0.6 8.7 %collective-permute-start.1 = (s32[2,4]{1,0:T(2,128)}, s32[2,4]{1,0:T(2,128)S(1)}, u32[]{:S(2)}, u32[]{:S(2)}) collective-permute-start(s32[2,4]{1,0:T(2,128)} %refs_1_.9), channel_id=1, source_target_pairs={{0,4},{4,8},{8,12},{12,16},{16,20},{20,24},{24,28},{28,0},{1,5},{5... | collective-permute-start | bytes 104 | tf_op jit(solution)/shard_map/ppermute | solution.py:454
  1.1 12.3 %collective-permute-start = (f32[2,64,512]{2,1,0:T(8,128)}, f32[2,64,512]{2,1,0:T(8,128)S(1)}, u32[]{:S(2)}, u32[]{:S(2)}) collective-permute-start(f32[2,64,512]{2,1,0:T(8,128)} %refs_2_.3), channel_id=1, source_target_pairs={{0,1},{1,2},{2,3},{3,0},{4,5},{5,6},{6,7},{7,4},{8,9},{9,10},{10,1... | collective-permute-start | bytes 786440 | tf_op jit(solution)/shard_map/ppermute | solution.py:454
  3.8 0.7 %copy-start.2 = (s32[2,4]{1,0:T(2,128)S(1)}, s32[2,4]{1,0:T(2,128)}, u32[]{:S(2)}) copy-start(s32[2,4]{1,0:T(2,128)} %refs_1_.9) | copy-start | bytes 100
  4.5 6.2 %copy-start.3 = (s32[2,4]{1,0:T(2,128)S(1)}, s32[2,4]{1,0:T(2,128)}, u32[]{:S(2)}) copy-start(s32[2,4]{1,0:T(2,128)} %refs_1_.9) | copy-start | bytes 100
  7.2 6.3 %copy-start.4 = (s32[2,4]{1,0:T(2,128)S(1)}, s32[2,4]{1,0:T(2,128)}, u32[]{:S(2)}) copy-start(s32[2,4]{1,0:T(2,128)} %refs_0_.13) | copy-start | bytes 100
  7.3 11.5 %collective-permute-start.3 = (f32[2,64,512]{2,1,0:T(8,128)S(1)}, f32[2,64,512]{2,1,0:T(8,128)S(1)}, u32[]{:S(2)}, u32[]{:S(2)}) collective-permute-start(f32[2,64,512]{2,1,0:T(8,128)S(1)} %broadcast_add_fusion), channel_id=1, source_target_pairs={{0,3},{1,0},{2,1},{3,2},{4,7},{5,4},{6,5},{7,6},{8,11},{9,8},{10,9... | collective-permute-start | bytes 786440 | tf_op jit(solution)/shard_map/ppermute | solution.py:454
  14.5 14.5 %copy-start = (f32[2,512,512]{2,1,0:T(8,128)S(1)}, f32[2,512,512]{2,1,0:T(8,128)}, u32[]{:S(2)}) copy-start(f32[2,512,512]{2,1,0:T(8,128)} %refs_3_.1) | copy-start | bytes 6291460
  14.5 6.8 %collective-permute-start.2 = (f32[2,64,256]{2,1,0:T(8,128)S(1)}, f32[2,64,256]{2,1,0:T(8,128)S(1)}, u32[]{:S(2)}, u32[]{:S(2)}) collective-permute-start(f32[2,64,256]{2,1,0:T(8,128)S(1)} %chosen.1), channel_id=1, source_target_pairs={{0,1},{1,2},{2,3},{3,0},{4,5},{5,6},{6,7},{7,4},{8,9},{9,10},{10,1... | collective-permute-start | bytes 393224 | tf_op jit(solution)/shard_map/ppermute | solution.py:454
  22.0 4.2 %collective-permute-start.4 = (f32[512,256]{1,0:T(8,128)S(1)}, f32[512,256]{1,0:T(8,128)S(1)}, u32[]{:S(2)}, u32[]{:S(2)}) collective-permute-start(f32[512,256]{1,0:T(8,128)S(1)} %get-tuple-element.32.refs_0_), channel_id=1, source_target_pairs={{0,4},{4,0},{8,12},{12,8},{16,20},{20,16},{24,28},{28,24},{1,5},{5... | collective-permute-start | bytes 1572872 | tf_op jit(solution)/shard_map/ppermute | solution.py:524
  26.8 6.4 %collective-permute-start.5 = (f32[128,256]{1,0:T(8,128)S(1)}, f32[128,256]{1,0:T(8,128)S(1)}, u32[]{:S(2)}, u32[]{:S(2)}) collective-permute-start(f32[128,256]{1,0:T(8,128)S(1)} %get-tuple-element.35), channel_id=1, source_target_pairs={{0,8},{4,12},{8,0},{12,4},{16,24},{20,28},{24,16},{28,20},{1,9},{5... | collective-permute-start | bytes 393224 | tf_op jit(solution)/shard_map/ppermute | solution.py:583
  28.4 6.0 %collective-permute-start.7 = (f32[160,128]{1,0:T(8,128)S(1)}, f32[160,128]{1,0:T(8,128)S(1)}, u32[]{:S(2)}, u32[]{:S(2)}) collective-permute-start(f32[160,128]{1,0:T(8,128)S(1)} %get-tuple-element.36.refs_6_), channel_id=1, source_target_pairs={{0,8},{4,12},{8,0},{12,4},{16,24},{20,28},{24,16},{28,20},{1,9},{5... | collective-permute-start | bytes 245768 | tf_op jit(solution)/shard_map/ppermute | solution.py:577
  31.7 6.6 %collective-permute-start.10 = (f32[2,64,256]{2,1,0:T(8,128)S(1)}, f32[2,64,256]{2,1,0:T(8,128)S(1)}, u32[]{:S(2)}, u32[]{:S(2)}) collective-permute-start(f32[2,64,256]{2,1,0:T(8,128)S(1)} %rest.1), channel_id=1, source_target_pairs={{0,1},{1,0},{2,3},{3,2},{4,5},{5,4},{6,7},{7,6},{8,9},{9,8},{10,11... | collective-permute-start | bytes 393224 | tf_op jit(solution)/shard_map/ppermute | solution.py:550
  33.2 2.6 %collective-permute-start.6 = (f32[128,256]{1,0:T(8,128)S(1)}, f32[128,256]{1,0:T(8,128)S(1)}, u32[]{:S(2)}, u32[]{:S(2)}) collective-permute-start(f32[128,256]{1,0:T(8,128)S(1)} %collective-permute-done.5.refs_2_.refs_12_), channel_id=1, source_target_pairs={{0,4},{4,0},{8,12},{12,8},{16,20},{20,16},{24,28},{28,24},{1,5},{5... | collective-permute-start | bytes 393224 | tf_op jit(solution)/shard_map/ppermute | solution.py:586
  34.4 1.3 %collective-permute-start.8 = (f32[160,128]{1,0:T(8,128)S(1)}, f32[160,128]{1,0:T(8,128)S(1)}, u32[]{:S(2)}, u32[]{:S(2)}) collective-permute-start(f32[160,128]{1,0:T(8,128)S(1)} %broadcast_add_fusion.3.refs_4_.refs_14_), channel_id=1, source_target_pairs={{0,4},{4,0},{8,12},{12,8},{16,20},{20,16},{24,28},{28,24},{1,5},{5... | collective-permute-start | bytes 245768 | tf_op jit(solution)/shard_map/ppermute | solution.py:586
  36.6 4.8 %collective-permute-start.9 = (f32[160,128]{1,0:T(8,128)S(1)}, f32[160,128]{1,0:T(8,128)S(1)}, u32[]{:S(2)}, u32[]{:S(2)}) collective-permute-start(f32[160,128]{1,0:T(8,128)S(1)} %merge.1), channel_id=1, source_target_pairs={{0,16},{4,20},{8,24},{12,28},{16,0},{20,4},{24,8},{28,12},{1,17},{... | collective-permute-start | bytes 245768 | tf_op jit(solution)/shard_map/ppermute | solution.py:577
  41.4 1.3 %collective-permute-start.11 = (f32[160,128]{1,0:T(8,128)S(1)}, f32[160,128]{1,0:T(8,128)S(1)}, u32[]{:S(2)}, u32[]{:S(2)}) collective-permute-start(f32[160,128]{1,0:T(8,128)S(1)} %broadcast_add_fusion.2.refs_0_), channel_id=1, source_target_pairs={{0,4},{4,0},{8,12},{12,8},{16,20},{20,16},{24,28},{28,24},{1,5},{5... | collective-permute-start | bytes 245768 | tf_op jit(solution)/shard_map/ppermute | solution.py:581

commit v13 on v12

--- a/solution.py
+++ b/solution.py
@@ -464,7 +464,6 @@
             [],
             far=[inv_diag],
             scratch=[pltpu.VMEM((width, width), F32), pltpu.SemaphoreType.DMA],
-            flops=6 * width * (chosen_cols * chosen_cols + own_cols * width),
             name="prior",
         )
         bases.append(base)

time: 44.9 us -> 43.5 us (0.969)
  starting transfers between devices: 12 us -> 9.8 us
  waiting for transfers between devices: 11.8 us -> 12.7 us
    ppermute x1, starting transfers between devices: 2.7 us -> 0.37 us  [body(): other_whole = lax.ppermute(own_whole, 'seg', swap)]
    ppermute x4, waiting for transfers between devices: 5.09 us -> 6 us  [turn(): lax.ppermute(x, axis, [(i, (i + distance) % count) for i in range(count)])]
  transfers between devices with their start and end apart: 12 -> 12, of which waited for: 7 -> 7; matrix products, arithmetic and copies ran while one was open for 2% -> 2% of each run, Pallas kernels for 33% -> 34%
where the time goes in v13:
time: 43.5 us; the launch traced here: 43.3 us
  Pallas kernels  18 us (41%)
  waiting for transfers between devices  12.7 us (29%)
  starting transfers between devices  9.8 us (23%)
  between operations  1.48 us (3%)
  local copies, waits for them, and re-layouts  0.7 us (2%)
  other arithmetic  0.7 us (2%)
    pallas_call x11, Pallas kernels, call(): pl.pallas_call(inner, out_shape=[*outs, *(jax.ShapeDtypeStruct(a.shape, a...  18 us
    ppermute x4, waiting for transfers between devices, turn(): lax.ppermute(x, axis, [(i, (i + distance) % count) for i in range(count)])  6 us
    ppermute x4, starting transfers between devices, turn(): lax.ppermute(x, axis, [(i, (i + distance) % count) for i in range(count)])  5.32 us
    ppermute x2, starting transfers between devices, body(): got = lax.ppermute(send, 'seg', partner)  2.02 us
    ppermute x1, starting transfers between devices, body(): got_t = lax.ppermute(send_t, 'seg', partner)  1.87 us
    ppermute x1, waiting for transfers between devices, body(): other_whole = lax.ppermute(own_whole, 'seg', swap)  1.61 us
    ppermute x1, waiting for transfers between devices, body(): got_t = lax.ppermute(send_t, 'seg', partner)  1.41 us
    ppermute x1, waiting for transfers between devices, body(): lax.ppermute(got, 'seg', swap)  1.26 us
  transfers between devices with their start and end apart: 12, of which 7 were waited for; matrix products, arithmetic and copies ran while one was open for 2% of the time, Pallas kernels for 34%

profile of v13, /device:TPU:0, one launch (start us, length us, event | category | flops | bytes accessed | tf_op | source)
XLA Modules:
  0.0 43.3 jit_solution(8424549760102567640)
XLA Ops:
  0.6 0.0 copy-start.1
  0.6 3.1 %collective-permute-start = (f32[2,64,512]{2,1,0:T(8,128)}, f32[2,64,512]{2,1,0:T(8,128)S(1)}, u32[]{:S(2)}, u32[]{:S(2)}) collective-permute-start(f32[2,64,512]{2,1,0:T(8,128)} %refs_2_.3), channel_id=1, source_target_pairs={{0,1},{1,2},{2,3},{3,0},{4,5},{5,6},{6,7},{7,4},{8,9},{9,10},{10,1... | collective-permute-start | bytes 786440 | tf_op jit(solution)/shard_map/ppermute | solution.py:454
  3.7 0.0 collective-permute-start.1
  3.7 0.0 copy-start.2
  3.7 0.7 %copy-done.2 = s32[2,4]{1,0:T(2,128)S(1)} copy-done((s32[2,4]{1,0:T(2,128)S(1)}, s32[2,4]{1,0:T(2,128)}, u32[]{:S(2)}) %copy-start.2) | copy-done | bytes 56
  4.4 0.0 copy-start.3
  4.4 2.8 %prior.3 = (f32[256,256]{1,0:T(8,128)S(1)}, f32[128,512]{1,0:T(8,128)S(1)}, bf16[512,256]{1,0:T(8,128)(2,1)S(1)}, bf16[512,256]{1,0:T(8,128)(2,1)S(1)}, f32[1,1,512]{2,1,0:T(1,128)S(1)}) custom-call(s32[2,4]{1,0:T(2,128)S(1)} %copy-done.2, f32[2,512,512]{2,1,0:T(8,128)} %refs_3_.1), custom_call_target="tpu_custom_call" | custom-call | bytes 3672064 | tf_op jit(solution)/shard_map/prior/pallas_call | solution.py:142
  7.2 0.0 copy-start.4
  7.2 0.0 copy-done.1
  7.2 2.2 %collective-permute-start.3 = (f32[2,64,512]{2,1,0:T(8,128)S(1)}, f32[2,64,512]{2,1,0:T(8,128)S(1)}, u32[]{:S(2)}, u32[]{:S(2)}) collective-permute-start(f32[2,64,512]{2,1,0:T(8,128)S(1)} %broadcast_add_fusion), channel_id=1, source_target_pairs={{0,3},{1,0},{2,1},{3,2},{4,7},{5,4},{6,5},{7,6},{8,11},{9,8},{10,9... | collective-permute-start | bytes 786440 | tf_op jit(solution)/shard_map/ppermute | solution.py:454
  9.4 0.0 collective-permute-done.1.refs_1_.refs_2_
  9.4 0.6 %reduce_min.9 = s32[]{:T(128)} reduce(s32[2,4]{1,0:T(2,128)S(1)} %collective-permute-done.1.refs_1_.refs_2_, s32[]{:T(128)} %constant.0.clone.1), dimensions={0,1}, to_apply=%region_0.0 | reduce | flops 7 | bytes 40 | tf_op jit(solution)/shard_map/reduce_min | solution.py:484
  10.7 0.0 copy-done.3
  10.7 2.8 %prior.2 = (f32[256,256]{1,0:T(8,128)S(1)}, f32[128,512]{1,0:T(8,128)S(1)}, bf16[512,256]{1,0:T(8,128)(2,1)S(1)}, bf16[512,256]{1,0:T(8,128)(2,1)S(1)}, f32[1,1,512]{2,1,0:T(1,128)}) custom-call(s32[2,4]{1,0:T(2,128)S(1)} %copy-done.3, s32[2,4]{1,0:T(2,128)S(1)} %collective-permute-done.1.refs_1_.refs_2_, f32[2,512,512]{2,1,0:T(8,128)} %refs_3_.1), custom_call_target="tpu_custom_call" | custom-call | bytes 3672064 | tf_op jit(solution)/shard_map/prior/pallas_call | solution.py:142
  13.5 0.0 collective-permute-done.refs_2_.refs_3_.refs_4_
  13.5 0.0 copy-done.4
  13.5 0.9 %chosen.1 = f32[2,64,256]{2,1,0:T(8,128)S(1)} custom-call(s32[2,4]{1,0:T(2,128)S(1)} %copy-done.4, f32[2,64,512]{2,1,0:T(8,128)S(1)} %broadcast_add_fusion.1.refs_1_, bf16[512,256]{1,0:T(8,128)(2,1)S(1)} %get-tuple-element.25.refs_2_.refs_4_, bf16[512,256]{1,0:T(8,128)(2,1)S(1)} %get-tuple-element.26.refs_3_.refs_5_, ...), custom_call_target="tpu_custom_call" | custom-call | flops 100663296 | bytes 2490368 | tf_op jit(solution)/shard_map/chosen/pallas_call | solution.py:142
  14.5 0.0 copy-start
  14.5 0.1 collective-permute-start.2
  14.6 3.3 %collective-permute-done.3.refs_3_.refs_4_.refs_5_ = f32[2,64,512]{2,1,0:T(8,128)S(1)} collective-permute-done((f32[2,64,512]{2,1,0:T(8,128)S(1)}, f32[2,64,512]{2,1,0:T(8,128)S(1)}, u32[]{:S(2)}, u32[]{:S(2)}) %collective-permute-start.3) | collective-permute-done | bytes 262176 | tf_op jit(solution)/shard_map/ppermute | solution.py:454
  17.8 1.7 %links.1.refs_1_ = f32[2,256,256]{2,1,0:T(8,128)S(1)} custom-call(s32[2,4]{1,0:T(2,128)S(1)} %copy-done.4, f32[2,64,512]{2,1,0:T(8,128)S(1)} %copy-done.1, f32[2,64,512]{2,1,0:T(8,128)S(1)} %collective-permute-done.refs_2_.refs_3_.refs_4_, f32[2,64,512]{2,1,0:T(8,128)S(1)} %collective-permute-done.3.refs_3_.refs_4_.refs_5_, ...), custom_call_target="tpu_custom_call" | custom-call | flops 402653184 | bytes 3407872 | tf_op jit(solution)/shard_map/links/pallas_call | solution.py:142
  19.5 2.7 %collective-permute-done.2.refs_0_.refs_10_ = f32[2,64,256]{2,1,0:T(8,128)S(1)} collective-permute-done((f32[2,64,256]{2,1,0:T(8,128)S(1)}, f32[2,64,256]{2,1,0:T(8,128)S(1)}, u32[]{:S(2)}, u32[]{:S(2)}) %collective-permute-start.2) | collective-permute-done | bytes 131104 | tf_op jit(solution)/shard_map/ppermute | solution.py:454
  22.2 0.6 %segment.1 = (f32[2,256,256]{2,1,0:T(8,128)S(1)}, f32[512,256]{1,0:T(8,128)S(1)}) custom-call(f32[2,64,256]{2,1,0:T(8,128)S(1)} %collective-permute-done.2.refs_0_.refs_10_, f32[2,256,256]{2,1,0:T(8,128)S(1)} %links.1.refs_1_, f32[256,256]{1,0:T(8,128)S(1)} %get-tuple-element.30.refs_2_.refs_3_, f32[256,256]{1,0:T(8,128)S(1)} %get-tuple-element.31.refs_3_.refs_4_), custom_call_target="tpu_custom_call" | custom-call | flops 301989888 | bytes 2228224 | tf_op jit(solution)/shard_map/segment/pallas_call | solution.py:142
  22.9 0.4 collective-permute-start.4
  23.2 1.6 %collective-permute-done.4.refs_1_.refs_7_ = f32[512,256]{1,0:T(8,128)S(1)} collective-permute-done((f32[512,256]{1,0:T(8,128)S(1)}, f32[512,256]{1,0:T(8,128)S(1)}, u32[]{:S(2)}, u32[]{:S(2)}) %collective-permute-start.4) | collective-permute-done | bytes 524320 | tf_op jit(solution)/shard_map/ppermute | solution.py:523
  24.8 0.6 %chip.1 = (f32[256,256]{1,0:T(8,128)S(1)}, f32[256,256]{1,0:T(8,128)S(1)}, f32[160,128]{1,0:T(8,128)S(1)}, f32[128,256]{1,0:T(8,128)S(1)}) custom-call(f32[512,256]{1,0:T(8,128)S(1)} %get-tuple-element.32.refs_0_, f32[512,256]{1,0:T(8,128)S(1)} %collective-permute-done.4.refs_1_.refs_7_), custom_call_target="tpu_custom_call" | custom-call | flops 301989888 | bytes 1785856 | tf_op jit(solution)/shard_map/chip/pallas_call | solution.py:142
  25.5 1.9 %collective-permute-start.5 = (f32[128,256]{1,0:T(8,128)S(1)}, f32[128,256]{1,0:T(8,128)S(1)}, u32[]{:S(2)}, u32[]{:S(2)}) collective-permute-start(f32[128,256]{1,0:T(8,128)S(1)} %get-tuple-element.35), channel_id=1, source_target_pairs={{0,8},{4,12},{8,0},{12,4},{16,24},{20,28},{24,16},{28,20},{1,9},{5... | collective-permute-start | bytes 393224 | tf_op jit(solution)/shard_map/ppermute | solution.py:582
  27.3 0.2 collective-permute-start.7
  27.6 0.0 copy-done
  27.6 1.5 %maps.1 = (f32[2,256,512]{2,1,0:T(8,128)S(1)}, f32[1,128]{1,0:T(1,128)S(1)}) custom-call(s32[2,4]{1,0:T(2,128)S(1)} %copy-done.4, f32[2,512,512]{2,1,0:T(8,128)S(1)} %copy-done, f32[2,64,512]{2,1,0:T(8,128)S(1)} %copy-done.1, f32[2,64,512]{2,1,0:T(8,128)S(1)} %collective-permute-done.refs_2_.refs_3_.refs_4_, ...), custom_call_target="tpu_custom_call" | custom-call | flops 805306368 | bytes 3932672 | tf_op jit(solution)/shard_map/maps/pallas_call | solution.py:142
  29.1 1.3 %rest.1 = f32[2,64,256]{2,1,0:T(8,128)S(1)} custom-call(s32[2,4]{1,0:T(2,128)S(1)} %copy-done.4, s32[2,4]{1,0:T(2,128)S(1)} %copy-done.3, s32[2,4]{1,0:T(2,128)S(1)} %collective-permute-done.1.refs_1_.refs_2_, f32[2,512,512]{2,1,0:T(8,128)S(1)} %copy-done, f32[2,64,512]{2,1,0:T(8,128)S(1)} %collective-permute-done.refs_2_.refs_3_.refs_4_, ...), custom_call_target="tpu_custom_call" | custom-call | flops 201326592 | bytes 2834432 | tf_op jit(solution)/shard_map/rest/pallas_call | solution.py:142
  30.4 0.1 collective-permute-start.10
  30.4 1.4 %collective-permute-done.5.refs_2_.refs_12_ = f32[128,256]{1,0:T(8,128)S(1)} collective-permute-done((f32[128,256]{1,0:T(8,128)S(1)}, f32[128,256]{1,0:T(8,128)S(1)}, u32[]{:S(2)}, u32[]{:S(2)}) %collective-permute-start.5) | collective-permute-done | bytes 131104 | tf_op jit(solution)/shard_map/ppermute | solution.py:582
  31.9 0.0 collective-permute-start.6
  31.9 1.1 %collective-permute-done.7 = f32[160,128]{1,0:T(8,128)S(1)} collective-permute-done((f32[160,128]{1,0:T(8,128)S(1)}, f32[160,128]{1,0:T(8,128)S(1)}, u32[]{:S(2)}, u32[]{:S(2)}) %collective-permute-start.7) | collective-permute-done | bytes 81952 | tf_op jit(solution)/shard_map/ppermute | solution.py:576
  33.0 0.1 collective-permute-start.8
  33.1 1.3 %collective-permute-done.8.refs_5_.refs_15_ = f32[160,128]{1,0:T(8,128)S(1)} collective-permute-done((f32[160,128]{1,0:T(8,128)S(1)}, f32[160,128]{1,0:T(8,128)S(1)}, u32[]{:S(2)}, u32[]{:S(2)}) %collective-permute-start.8) | collective-permute-done | bytes 81952 | tf_op jit(solution)/shard_map/ppermute | solution.py:585
  34.4 0.0 collective-permute-done.6.refs_3_.refs_13_
  34.4 0.8 %merge.1 = f32[160,128]{1,0:T(8,128)S(1)} custom-call(f32[256,256]{1,0:T(8,128)S(1)} %get-tuple-element.33.refs_0_, f32[256,256]{1,0:T(8,128)S(1)} %get-tuple-element.34.refs_1_, f32[128,256]{1,0:T(8,128)S(1)} %collective-permute-done.5.refs_2_.refs_12_, f32[128,256]{1,0:T(8,128)S(1)} %collective-permute-done.6.refs_3_.refs_13_, ...), custom_call_target="tpu_custom_call" | custom-call | flops 301989888 | bytes 1032192 | tf_op jit(solution)/shard_map/merge/pallas_call | solution.py:142
  35.2 1.8 %collective-permute-start.9 = (f32[160,128]{1,0:T(8,128)S(1)}, f32[160,128]{1,0:T(8,128)S(1)}, u32[]{:S(2)}, u32[]{:S(2)}) collective-permute-start(f32[160,128]{1,0:T(8,128)S(1)} %merge.1), channel_id=1, source_target_pairs={{0,16},{4,20},{8,24},{12,28},{16,0},{20,4},{24,8},{28,12},{1,17},{... | collective-permute-start | bytes 245768 | tf_op jit(solution)/shard_map/ppermute | solution.py:576
  37.0 0.0 collective-permute-done.10.refs_11_
  37.0 3.1 %prepare.1 = (bf16[384,256]{1,0:T(8,128)(2,1)S(1)}, bf16[384,256]{1,0:T(8,128)(2,1)S(1)}, bf16[2,256,512]{2,1,0:T(8,128)(2,1)S(1)}, bf16[2,256,512]{2,1,0:T(8,12...) custom-call(s32[2,4]{1,0:T(2,128)S(1)} %copy-done.4, s32[2,4]{1,0:T(2,128)S(1)} %copy-done.3, ...), custom_call_target="tpu_custom_call" | custom-call | flops 1459617792 | bytes 7504384 | tf_op jit(solution)/shard_map/prepare/pallas_call | solution.py:142
  40.1 0.0 collective-permute-done.9
  40.1 0.1 collective-permute-start.11
  40.2 1.3 %collective-permute-done.11.refs_1_ = f32[160,128]{1,0:T(8,128)S(1)} collective-permute-done((f32[160,128]{1,0:T(8,128)S(1)}, f32[160,128]{1,0:T(8,128)S(1)}, u32[]{:S(2)}, u32[]{:S(2)}) %collective-permute-start.11) | collective-permute-done | bytes 81952 | tf_op jit(solution)/shard_map/ppermute | solution.py:580
  41.5 1.9 %finish.1 = (f32[2,128,512]{2,1,0:T(8,128)}, f32[2,64,512]{2,1,0:T(8,128)}) custom-call(f32[160,128]{1,0:T(8,128)S(1)} %broadcast_add_fusion.2.refs_0_, f32[160,128]{1,0:T(8,128)S(1)} %collective-permute-done.11.refs_1_, bf16[384,256]{1,0:T(8,128)(2,1)S(1)} %get-tuple-element.43.refs_2_, bf16[384,256]{1,0:T(8,128)(2,1)S(1)} %get-tuple-element.44.refs_3_, ...), custom_call_target="tpu_custom_call" | custom-call | flops 452984832 | bytes 4620288 | tf_op jit(solution)/shard_map/finish/pallas_call | solution.py:142
  (4 shorter events, 0.1 us)
Async XLA Ops:
  0.6 6.5 %copy-start.1 = (f32[2,64,512]{2,1,0:T(8,128)S(1)}, f32[2,64,512]{2,1,0:T(8,128)}, u32[]{:S(2)}) copy-start(f32[2,64,512]{2,1,0:T(8,128)} %refs_2_.3) | copy-start | bytes 786436
  0.6 12.8 %collective-permute-start = (f32[2,64,512]{2,1,0:T(8,128)}, f32[2,64,512]{2,1,0:T(8,128)S(1)}, u32[]{:S(2)}, u32[]{:S(2)}) collective-permute-start(f32[2,64,512]{2,1,0:T(8,128)} %refs_2_.3), channel_id=1, source_target_pairs={{0,1},{1,2},{2,3},{3,0},{4,5},{5,6},{6,7},{7,4},{8,9},{9,10},{10,1... | collective-permute-start | bytes 786440 | tf_op jit(solution)/shard_map/ppermute | solution.py:454
  3.7 5.7 %collective-permute-start.1 = (s32[2,4]{1,0:T(2,128)}, s32[2,4]{1,0:T(2,128)S(1)}, u32[]{:S(2)}, u32[]{:S(2)}) collective-permute-start(s32[2,4]{1,0:T(2,128)} %refs_1_.9), channel_id=1, source_target_pairs={{0,4},{4,8},{8,12},{12,16},{16,20},{20,24},{24,28},{28,0},{1,5},{5... | collective-permute-start | bytes 104 | tf_op jit(solution)/shard_map/ppermute | solution.py:454
  3.7 0.7 %copy-start.2 = (s32[2,4]{1,0:T(2,128)S(1)}, s32[2,4]{1,0:T(2,128)}, u32[]{:S(2)}) copy-start(s32[2,4]{1,0:T(2,128)} %refs_1_.9) | copy-start | bytes 100
  4.4 6.3 %copy-start.3 = (s32[2,4]{1,0:T(2,128)S(1)}, s32[2,4]{1,0:T(2,128)}, u32[]{:S(2)}) copy-start(s32[2,4]{1,0:T(2,128)} %refs_1_.9) | copy-start | bytes 100
  7.2 6.3 %copy-start.4 = (s32[2,4]{1,0:T(2,128)S(1)}, s32[2,4]{1,0:T(2,128)}, u32[]{:S(2)}) copy-start(s32[2,4]{1,0:T(2,128)} %refs_0_.13) | copy-start | bytes 100
  7.2 10.6 %collective-permute-start.3 = (f32[2,64,512]{2,1,0:T(8,128)S(1)}, f32[2,64,512]{2,1,0:T(8,128)S(1)}, u32[]{:S(2)}, u32[]{:S(2)}) collective-permute-start(f32[2,64,512]{2,1,0:T(8,128)S(1)} %broadcast_add_fusion), channel_id=1, source_target_pairs={{0,3},{1,0},{2,1},{3,2},{4,7},{5,4},{6,5},{7,6},{8,11},{9,8},{10,9... | collective-permute-start | bytes 786440 | tf_op jit(solution)/shard_map/ppermute | solution.py:454
  14.5 13.1 %copy-start = (f32[2,512,512]{2,1,0:T(8,128)S(1)}, f32[2,512,512]{2,1,0:T(8,128)}, u32[]{:S(2)}) copy-start(f32[2,512,512]{2,1,0:T(8,128)} %refs_3_.1) | copy-start | bytes 6291460
  14.5 7.7 %collective-permute-start.2 = (f32[2,64,256]{2,1,0:T(8,128)S(1)}, f32[2,64,256]{2,1,0:T(8,128)S(1)}, u32[]{:S(2)}, u32[]{:S(2)}) collective-permute-start(f32[2,64,256]{2,1,0:T(8,128)S(1)} %chosen.1), channel_id=1, source_target_pairs={{0,1},{1,2},{2,3},{3,0},{4,5},{5,6},{6,7},{7,4},{8,9},{9,10},{10,1... | collective-permute-start | bytes 393224 | tf_op jit(solution)/shard_map/ppermute | solution.py:454
  22.9 2.0 %collective-permute-start.4 = (f32[512,256]{1,0:T(8,128)S(1)}, f32[512,256]{1,0:T(8,128)S(1)}, u32[]{:S(2)}, u32[]{:S(2)}) collective-permute-start(f32[512,256]{1,0:T(8,128)S(1)} %get-tuple-element.32.refs_0_), channel_id=1, source_target_pairs={{0,4},{4,0},{8,12},{12,8},{16,20},{20,16},{24,28},{28,24},{1,5},{5... | collective-permute-start | bytes 1572872 | tf_op jit(solution)/shard_map/ppermute | solution.py:523
  25.5 6.4 %collective-permute-start.5 = (f32[128,256]{1,0:T(8,128)S(1)}, f32[128,256]{1,0:T(8,128)S(1)}, u32[]{:S(2)}, u32[]{:S(2)}) collective-permute-start(f32[128,256]{1,0:T(8,128)S(1)} %get-tuple-element.35), channel_id=1, source_target_pairs={{0,8},{4,12},{8,0},{12,4},{16,24},{20,28},{24,16},{28,20},{1,9},{5... | collective-permute-start | bytes 393224 | tf_op jit(solution)/shard_map/ppermute | solution.py:582
  27.3 5.7 %collective-permute-start.7 = (f32[160,128]{1,0:T(8,128)S(1)}, f32[160,128]{1,0:T(8,128)S(1)}, u32[]{:S(2)}, u32[]{:S(2)}) collective-permute-start(f32[160,128]{1,0:T(8,128)S(1)} %get-tuple-element.36.refs_6_), channel_id=1, source_target_pairs={{0,8},{4,12},{8,0},{12,4},{16,24},{20,28},{24,16},{28,20},{1,9},{5... | collective-permute-start | bytes 245768 | tf_op jit(solution)/shard_map/ppermute | solution.py:576
  30.4 6.6 %collective-permute-start.10 = (f32[2,64,256]{2,1,0:T(8,128)S(1)}, f32[2,64,256]{2,1,0:T(8,128)S(1)}, u32[]{:S(2)}, u32[]{:S(2)}) collective-permute-start(f32[2,64,256]{2,1,0:T(8,128)S(1)} %rest.1), channel_id=1, source_target_pairs={{0,1},{1,0},{2,3},{3,2},{4,5},{5,4},{6,7},{7,6},{8,9},{9,8},{10,11... | collective-permute-start | bytes 393224 | tf_op jit(solution)/shard_map/ppermute | solution.py:549
  31.9 2.5 %collective-permute-start.6 = (f32[128,256]{1,0:T(8,128)S(1)}, f32[128,256]{1,0:T(8,128)S(1)}, u32[]{:S(2)}, u32[]{:S(2)}) collective-permute-start(f32[128,256]{1,0:T(8,128)S(1)} %collective-permute-done.5.refs_2_.refs_12_), channel_id=1, source_target_pairs={{0,4},{4,0},{8,12},{12,8},{16,20},{20,16},{24,28},{28,24},{1,5},{5... | collective-permute-start | bytes 393224 | tf_op jit(solution)/shard_map/ppermute | solution.py:585
  33.0 1.3 %collective-permute-start.8 = (f32[160,128]{1,0:T(8,128)S(1)}, f32[160,128]{1,0:T(8,128)S(1)}, u32[]{:S(2)}, u32[]{:S(2)}) collective-permute-start(f32[160,128]{1,0:T(8,128)S(1)} %broadcast_add_fusion.3.refs_4_.refs_14_), channel_id=1, source_target_pairs={{0,4},{4,0},{8,12},{12,8},{16,20},{20,16},{24,28},{28,24},{1,5},{5... | collective-permute-start | bytes 245768 | tf_op jit(solution)/shard_map/ppermute | solution.py:585
  35.2 4.9 %collective-permute-start.9 = (f32[160,128]{1,0:T(8,128)S(1)}, f32[160,128]{1,0:T(8,128)S(1)}, u32[]{:S(2)}, u32[]{:S(2)}) collective-permute-start(f32[160,128]{1,0:T(8,128)S(1)} %merge.1), channel_id=1, source_target_pairs={{0,16},{4,20},{8,24},{12,28},{16,0},{20,4},{24,8},{28,12},{1,17},{... | collective-permute-start | bytes 245768 | tf_op jit(solution)/shard_map/ppermute | solution.py:576
  40.1 1.3 %collective-permute-start.11 = (f32[160,128]{1,0:T(8,128)S(1)}, f32[160,128]{1,0:T(8,128)S(1)}, u32[]{:S(2)}, u32[]{:S(2)}) collective-permute-start(f32[160,128]{1,0:T(8,128)S(1)} %broadcast_add_fusion.2.refs_0_), channel_id=1, source_target_pairs={{0,4},{4,0},{8,12},{12,8},{16,20},{20,16},{24,28},{28,24},{1,5},{5... | collective-permute-start | bytes 245768 | tf_op jit(solution)/shard_map/ppermute | solution.py:580

commit v14 on v13

--- a/solution.py
+++ b/solution.py
@@ -180,27 +180,28 @@
     )
 
 
-def prior_kernel(panel, *refs):
-    *scalar_refs, inv_hbm, base_ref, own_ref, pick_high_ref, pick_low_ref, token_ref = refs[:-2]
-    inv_ref, sem = refs[-2:]
+def pick_kernel(panel, *refs):
+    *scalar_refs, inv_hbm, high_ref, low_ref, inv_ref, sem = refs
+    copy = pltpu.make_async_copy(inv_hbm.at[panel], inv_ref, sem)
+    copy.start()
+    chosen = chosen_of(panel, *scalar_refs)
+    copy.wait()
+    for t in range(len(chosen) // 2):
+        columns = slice(t * LANES, (t + 1) * LANES)
+        high_ref[:, columns], low_ref[:, columns] = split(
+            two_blocks(tile_of(inv_ref), chosen[2 * t], chosen[2 * t + 1])
+        )
+
+
+def prior_kernel(panel, high_ref, low_ref, inv_hbm, base_ref, own_ref, token_ref, inv_ref, sem):
     copy = pltpu.make_async_copy(inv_hbm.at[panel], inv_ref, sem)
     copy.start()
     token_ref[...] = jnp.zeros_like(token_ref)
-    chosen = chosen_of(panel, *scalar_refs)
     own_cols = own_ref.shape[0]
     own_at = pl.ds(pl.multiple_of(lax.axis_index("row") * own_cols, own_cols), own_cols)
+    picked = (high_ref[...], low_ref[...])
+    base_ref[...] = mm(picked, picked, TN)
     copy.wait()
-    picked = split(
-        jnp.concatenate(
-            [
-                two_blocks(tile_of(inv_ref), chosen[2 * t], chosen[2 * t + 1])
-                for t in range(len(chosen) // 2)
-            ],
-            1,
-        )
-    )
-    pick_high_ref[...], pick_low_ref[...] = picked
-    base_ref[...] = mm(picked, picked, TN)
     own_ref[...] = mm(inv_ref[:, own_at], inv_ref[...], TN)
 
 
@@ -457,13 +458,24 @@
     pick = jax.ShapeDtypeStruct((width, chosen_cols), BF16)
     bases, priors, picks, tokens = [], [], [], []
     for p in range(panels):
-        base, own_prior, *high_low, token = call(
-            functools.partial(prior_kernel, p),
-            [shape(chosen_cols, chosen_cols), shape(own_cols, width), pick, pick, shape(1, 1, width)],
+        copy_of_inv = [pltpu.VMEM((width, width), F32), pltpu.SemaphoreType.DMA]
+        high_low = call(
+            functools.partial(pick_kernel, p),
+            [pick, pick],
             [fill_blocks] if p else [fill_blocks, prior_fill],
             [],
             far=[inv_diag],
-            scratch=[pltpu.VMEM((width, width), F32), pltpu.SemaphoreType.DMA],
+            scratch=copy_of_inv,
+            flops=(0 if p else 20) * width**3,
+            name="pick",
+        )
+        base, own_prior, token = call(
+            functools.partial(prior_kernel, p),
+            [shape(chosen_cols, chosen_cols), shape(own_cols, width), shape(1, 1, width)],
+            [],
+            high_low,
+            far=[inv_diag],
+            scratch=copy_of_inv,
             name="prior",
         )
         bases.append(base)
@@ -481,12 +493,11 @@
     whose = [tuple((i - d) % row_count for i in range(row_count)) for d in range(row_count)]
     plan = Plan(tuple(whose[d] for d in came), whose[far])
     parts = ups[:far] + downs[:0:-1]
-    index_gate = jnp.minimum(jnp.min(prior_fill), 0).astype(F32)
     (late,) = call(
         functools.partial(chosen_kernel, whose[1] if short else whose[far]),
         [shape(panels, rows, chosen_cols)],
         [fill_mask],
-        [ups[-1] + index_gate, *picks],
+        [ups[-1], *picks],
         flops=6 * panels * rows * chosen_cols * width,
         name="chosen",
     )

time: 43.5 us -> 43.5 us (level)
  Pallas kernels: 18 us -> 21 us
  waiting for transfers between devices: 12.7 us -> 11.1 us
  other arithmetic: 0.7 us -> 0.04 us
  between operations: 1.48 us -> 0.84 us
    pallas_call x11 -> x13, Pallas kernels: 18 us -> 21 us  [call(): pl.pallas_call(inner, out_shape=[*outs, *(jax.ShapeDtypeStruct(a.shape, a...]
    ppermute x4, waiting for transfers between devices: 6 us -> 4.43 us  [turn(): lax.ppermute(x, axis, [(i, (i + distance) % count) for i in range(count)])]
    reduce_min x1 -> x0, other arithmetic: 0.63 us -> none  [body(): index_gate = jnp.minimum(jnp.min(prior_fill), 0).astype(F32)]
  transfers between devices with their start and end apart: 12 -> 12, of which waited for: 7 -> 7; matrix products, arithmetic and copies ran while one was open for 2% -> 0% of each run, Pallas kernels for 34% -> 41%
where the time goes in v14:
time: 43.5 us; the launch traced here: 43.2 us
  Pallas kernels  21 us (48%)
  waiting for transfers between devices  11.1 us (26%)
  starting transfers between devices  9.6 us (22%)
  between operations  0.84 us (2%)
  local copies, waits for them, and re-layouts  0.7 us (2%)
    pallas_call x13, Pallas kernels, call(): pl.pallas_call(inner, out_shape=[*outs, *(jax.ShapeDtypeStruct(a.shape, a...  21 us
    ppermute x4, starting transfers between devices, turn(): lax.ppermute(x, axis, [(i, (i + distance) % count) for i in range(count)])  5.29 us
    ppermute x4, waiting for transfers between devices, turn(): lax.ppermute(x, axis, [(i, (i + distance) % count) for i in range(count)])  4.43 us
    ppermute x2, starting transfers between devices, body(): got = lax.ppermute(send, 'seg', partner)  1.98 us
    ppermute x1, starting transfers between devices, body(): got_t = lax.ppermute(send_t, 'seg', partner)  1.7 us
    ppermute x1, waiting for transfers between devices, body(): other_whole = lax.ppermute(own_whole, 'seg', swap)  1.6 us
    ppermute x1, waiting for transfers between devices, body(): got_t = lax.ppermute(send_t, 'seg', partner)  1.34 us
    ppermute x1, waiting for transfers between devices, body(): after = (got, lax.ppermute(got, 'seg', swap))  1.26 us
  transfers between devices with their start and end apart: 12, of which 7 were waited for; matrix products, arithmetic and copies ran while one was open for 0% of the time, Pallas kernels for 41%

profile of v14, /device:TPU:0, one launch (start us, length us, event | category | flops | bytes accessed | tf_op | source)
XLA Modules:
  0.0 43.2 jit_solution(3590782654584412611)
XLA Ops:
  0.6 0.0 copy-start.1
  0.6 3.1 %collective-permute-start = (f32[2,64,512]{2,1,0:T(8,128)}, f32[2,64,512]{2,1,0:T(8,128)S(1)}, u32[]{:S(2)}, u32[]{:S(2)}) collective-permute-start(f32[2,64,512]{2,1,0:T(8,128)} %refs_2_.7), channel_id=1, source_target_pairs={{0,1},{1,2},{2,3},{3,0},{4,5},{5,6},{6,7},{7,4},{8,9},{9,10},{10,1... | collective-permute-start | bytes 786440 | tf_op jit(solution)/shard_map/ppermute | solution.py:455
  3.7 0.0 collective-permute-start.1
  3.7 0.0 copy-start.3
  3.7 0.7 %copy-done.3 = s32[2,4]{1,0:T(2,128)S(1)} copy-done((s32[2,4]{1,0:T(2,128)S(1)}, s32[2,4]{1,0:T(2,128)}, u32[]{:S(2)}) %copy-start.3) | copy-done | bytes 56
  4.4 2.2 %pick.3 = (bf16[512,256]{1,0:T(8,128)(2,1)S(1)}, bf16[512,256]{1,0:T(8,128)(2,1)S(1)}) custom-call(s32[2,4]{1,0:T(2,128)S(1)} %copy-done.3, f32[2,512,512]{2,1,0:T(8,128)} %refs_3_.1), custom_call_target="tpu_custom_call" | custom-call | bytes 3145728 | tf_op jit(solution)/shard_map/pick/pallas_call | solution.py:142
  6.6 2.1 %prior.2 = (f32[256,256]{1,0:T(8,128)S(1)}, f32[128,512]{1,0:T(8,128)S(1)}, f32[1,1,512]{2,1,0:T(1,128)S(1)}) custom-call(bf16[512,256]{1,0:T(8,128)(2,1)S(1)} %get-tuple-element.27.refs_4_.refs_0_.refs_6_, bf16[512,256]{1,0:T(8,128)(2,1)S(1)} %get-tuple-element.28.refs_5_.refs_1_.refs_7_, f32[2,512,512]{2,1,0:T(8,128)} %refs_3_.1), custom_call_target="tpu_custom_call" | custom-call | bytes 3672064 | tf_op jit(solution)/shard_map/prior/pallas_call | solution.py:142
  8.7 0.0 copy-done.1
  8.7 0.0 copy-start.2
  8.7 2.2 %collective-permute-start.3 = (f32[2,64,512]{2,1,0:T(8,128)S(1)}, f32[2,64,512]{2,1,0:T(8,128)S(1)}, u32[]{:S(2)}, u32[]{:S(2)}) collective-permute-start(f32[2,64,512]{2,1,0:T(8,128)S(1)} %broadcast_add_fusion), channel_id=1, source_target_pairs={{0,3},{1,0},{2,1},{3,2},{4,7},{5,4},{6,5},{7,6},{8,11},{9,8},{10,9... | collective-permute-start | bytes 786440 | tf_op jit(solution)/shard_map/ppermute | solution.py:455
  10.9 0.0 collective-permute-done.1.refs_1_.refs_2_
  10.9 2.2 %pick.2 = (bf16[512,256]{1,0:T(8,128)(2,1)S(1)}, bf16[512,256]{1,0:T(8,128)(2,1)S(1)}) custom-call(s32[2,4]{1,0:T(2,128)S(1)} %copy-done.3, s32[2,4]{1,0:T(2,128)S(1)} %collective-permute-done.1.refs_1_.refs_2_, f32[2,512,512]{2,1,0:T(8,128)} %refs_3_.1), custom_call_target="tpu_custom_call" | custom-call | flops 2684354560 | bytes 3145728 | tf_op jit(solution)/shard_map/pick/pallas_call | solution.py:142
  13.1 0.0 collective-permute-done.refs_1_.refs_2_.refs_3_.refs_4_
  13.1 0.0 copy-done.2
  13.1 0.9 %chosen.1 = f32[2,64,256]{2,1,0:T(8,128)S(1)} custom-call(s32[2,4]{1,0:T(2,128)S(1)} %copy-done.2, f32[2,64,512]{2,1,0:T(8,128)S(1)} %collective-permute-done.refs_1_.refs_2_.refs_3_.refs_4_, bf16[512,256]{1,0:T(8,128)(2,1)S(1)} %get-tuple-element.25.refs_2_.refs_4_.refs_0_, bf16[512,256]{1,0:T(8,128)(2,1)S(1)} %get-tuple-element.26.refs_3_.refs_5_.refs_1_, ...), custom_call_target="tpu_custom_call" | custom-call | flops 100663296 | bytes 2490368 | tf_op jit(solution)/shard_map/chosen/pallas_call | solution.py:142
  14.0 0.1 collective-permute-start.2
  14.1 2.1 %prior.3 = (f32[256,256]{1,0:T(8,128)S(1)}, f32[128,512]{1,0:T(8,128)S(1)}, f32[1,1,512]{2,1,0:T(1,128)}) custom-call(bf16[512,256]{1,0:T(8,128)(2,1)S(1)} %get-tuple-element.25.refs_2_.refs_4_.refs_0_, bf16[512,256]{1,0:T(8,128)(2,1)S(1)} %get-tuple-element.26.refs_3_.refs_5_.refs_1_, f32[2,512,512]{2,1,0:T(8,128)} %refs_3_.1), custom_call_target="tpu_custom_call" | custom-call | bytes 3672064 | tf_op jit(solution)/shard_map/prior/pallas_call | solution.py:142
  16.2 0.0 copy-start
  16.2 1.1 %collective-permute-done.3.refs_3_.refs_4_.refs_5_ = f32[2,64,512]{2,1,0:T(8,128)S(1)} collective-permute-done((f32[2,64,512]{2,1,0:T(8,128)S(1)}, f32[2,64,512]{2,1,0:T(8,128)S(1)}, u32[]{:S(2)}, u32[]{:S(2)}) %collective-permute-start.3) | collective-permute-done | bytes 262176 | tf_op jit(solution)/shard_map/ppermute | solution.py:455
  17.3 1.7 %links.1.refs_1_ = f32[2,256,256]{2,1,0:T(8,128)S(1)} custom-call(s32[2,4]{1,0:T(2,128)S(1)} %copy-done.2, f32[2,64,512]{2,1,0:T(8,128)S(1)} %copy-done.1, f32[2,64,512]{2,1,0:T(8,128)S(1)} %collective-permute-done.refs_1_.refs_2_.refs_3_.refs_4_, f32[2,64,512]{2,1,0:T(8,128)S(1)} %collective-permute-done.3.refs_3_.refs_4_.refs_5_, ...), custom_call_target="tpu_custom_call" | custom-call | flops 402653184 | bytes 3407872 | tf_op jit(solution)/shard_map/links/pallas_call | solution.py:142
  19.0 3.3 %collective-permute-done.2.refs_0_.refs_10_ = f32[2,64,256]{2,1,0:T(8,128)S(1)} collective-permute-done((f32[2,64,256]{2,1,0:T(8,128)S(1)}, f32[2,64,256]{2,1,0:T(8,128)S(1)}, u32[]{:S(2)}, u32[]{:S(2)}) %collective-permute-start.2) | collective-permute-done | bytes 131104 | tf_op jit(solution)/shard_map/ppermute | solution.py:455
  22.3 0.6 %segment.1 = (f32[2,256,256]{2,1,0:T(8,128)S(1)}, f32[512,256]{1,0:T(8,128)S(1)}) custom-call(f32[2,64,256]{2,1,0:T(8,128)S(1)} %collective-permute-done.2.refs_0_.refs_10_, f32[2,256,256]{2,1,0:T(8,128)S(1)} %links.1.refs_1_, f32[256,256]{1,0:T(8,128)S(1)} %get-tuple-element.30.refs_2_.refs_3_, f32[256,256]{1,0:T(8,128)S(1)} %get-tuple-element.31.refs_3_.refs_4_), custom_call_target="tpu_custom_call" | custom-call | flops 301989888 | bytes 2228224 | tf_op jit(solution)/shard_map/segment/pallas_call | solution.py:142
  23.0 0.0 copy-start.4
  23.0 0.4 collective-permute-start.4
  23.4 1.6 %collective-permute-done.4.refs_1_.refs_7_ = f32[512,256]{1,0:T(8,128)S(1)} collective-permute-done((f32[512,256]{1,0:T(8,128)S(1)}, f32[512,256]{1,0:T(8,128)S(1)}, u32[]{:S(2)}, u32[]{:S(2)}) %collective-permute-start.4) | collective-permute-done | bytes 524320 | tf_op jit(solution)/shard_map/ppermute | solution.py:534
  25.0 0.6 %chip.1 = (f32[256,256]{1,0:T(8,128)S(1)}, f32[256,256]{1,0:T(8,128)S(1)}, f32[160,128]{1,0:T(8,128)S(1)}, f32[128,256]{1,0:T(8,128)S(1)}) custom-call(f32[512,256]{1,0:T(8,128)S(1)} %get-tuple-element.32.refs_0_, f32[512,256]{1,0:T(8,128)S(1)} %collective-permute-done.4.refs_1_.refs_7_), custom_call_target="tpu_custom_call" | custom-call | flops 301989888 | bytes 1785856 | tf_op jit(solution)/shard_map/chip/pallas_call | solution.py:142
  25.6 1.7 %collective-permute-start.5 = (f32[128,256]{1,0:T(8,128)S(1)}, f32[128,256]{1,0:T(8,128)S(1)}, u32[]{:S(2)}, u32[]{:S(2)}) collective-permute-start(f32[128,256]{1,0:T(8,128)S(1)} %get-tuple-element.35), channel_id=1, source_target_pairs={{0,8},{4,12},{8,0},{12,4},{16,24},{20,28},{24,16},{28,20},{1,9},{5... | collective-permute-start | bytes 393224 | tf_op jit(solution)/shard_map/ppermute | solution.py:593
  27.3 0.4 collective-permute-start.7
  27.7 0.0 copy-done
  27.7 1.5 %maps.1 = (f32[2,256,512]{2,1,0:T(8,128)S(1)}, f32[1,128]{1,0:T(1,128)S(1)}) custom-call(s32[2,4]{1,0:T(2,128)S(1)} %copy-done.2, f32[2,512,512]{2,1,0:T(8,128)S(1)} %copy-done, f32[2,64,512]{2,1,0:T(8,128)S(1)} %copy-done.1, f32[2,64,512]{2,1,0:T(8,128)S(1)} %collective-permute-done.refs_1_.refs_2_.refs_3_.refs_4_, ...), custom_call_target="tpu_custom_call" | custom-call | flops 805306368 | bytes 3932672 | tf_op jit(solution)/shard_map/maps/pallas_call | solution.py:142
  29.2 0.0 copy-done.4
  29.2 1.3 %rest.1 = f32[2,64,256]{2,1,0:T(8,128)S(1)} custom-call(s32[2,4]{1,0:T(2,128)S(1)} %copy-done.2, s32[2,4]{1,0:T(2,128)S(1)} %copy-done.4, s32[2,4]{1,0:T(2,128)S(1)} %collective-permute-done.1.refs_1_.refs_2_, f32[2,512,512]{2,1,0:T(8,128)S(1)} %copy-done, f32[2,64,512]{2,1,0:T(8,128)S(1)} %collective-permute-done.refs_1_.refs_2_.refs_3_.refs_4_, ...), custom_call_target="tpu_custom_call" | custom-call | flops 201326592 | bytes 2834432 | tf_op jit(solution)/shard_map/rest/pallas_call | solution.py:142
  30.5 0.1 collective-permute-start.10
  30.6 1.3 %collective-permute-done.5.refs_2_.refs_12_ = f32[128,256]{1,0:T(8,128)S(1)} collective-permute-done((f32[128,256]{1,0:T(8,128)S(1)}, f32[128,256]{1,0:T(8,128)S(1)}, u32[]{:S(2)}, u32[]{:S(2)}) %collective-permute-start.5) | collective-permute-done | bytes 131104 | tf_op jit(solution)/shard_map/ppermute | solution.py:593
  32.0 0.0 collective-permute-start.6
  32.0 1.1 %collective-permute-done.7 = f32[160,128]{1,0:T(8,128)S(1)} collective-permute-done((f32[160,128]{1,0:T(8,128)S(1)}, f32[160,128]{1,0:T(8,128)S(1)}, u32[]{:S(2)}, u32[]{:S(2)}) %collective-permute-start.7) | collective-permute-done | bytes 81952 | tf_op jit(solution)/shard_map/ppermute | solution.py:587
  33.1 0.1 collective-permute-start.8
  33.2 1.3 %collective-permute-done.8.refs_5_.refs_15_ = f32[160,128]{1,0:T(8,128)S(1)} collective-permute-done((f32[160,128]{1,0:T(8,128)S(1)}, f32[160,128]{1,0:T(8,128)S(1)}, u32[]{:S(2)}, u32[]{:S(2)}) %collective-permute-start.8) | collective-permute-done | bytes 81952 | tf_op jit(solution)/shard_map/ppermute | solution.py:596
  34.5 0.0 collective-permute-done.6.refs_3_.refs_13_
  34.5 0.8 %merge.1 = f32[160,128]{1,0:T(8,128)S(1)} custom-call(f32[256,256]{1,0:T(8,128)S(1)} %get-tuple-element.33.refs_0_, f32[256,256]{1,0:T(8,128)S(1)} %get-tuple-element.34.refs_1_, f32[128,256]{1,0:T(8,128)S(1)} %collective-permute-done.5.refs_2_.refs_12_, f32[128,256]{1,0:T(8,128)S(1)} %collective-permute-done.6.refs_3_.refs_13_, ...), custom_call_target="tpu_custom_call" | custom-call | flops 301989888 | bytes 1032192 | tf_op jit(solution)/shard_map/merge/pallas_call | solution.py:142
  35.3 1.6 %collective-permute-start.9 = (f32[160,128]{1,0:T(8,128)S(1)}, f32[160,128]{1,0:T(8,128)S(1)}, u32[]{:S(2)}, u32[]{:S(2)}) collective-permute-start(f32[160,128]{1,0:T(8,128)S(1)} %merge.1), channel_id=1, source_target_pairs={{0,16},{4,20},{8,24},{12,28},{16,0},{20,4},{24,8},{28,12},{1,17},{... | collective-permute-start | bytes 245768 | tf_op jit(solution)/shard_map/ppermute | solution.py:587
  36.9 0.0 collective-permute-done.10.refs_11_
  36.9 3.1 %prepare.1 = (bf16[384,256]{1,0:T(8,128)(2,1)S(1)}, bf16[384,256]{1,0:T(8,128)(2,1)S(1)}, bf16[2,256,512]{2,1,0:T(8,128)(2,1)S(1)}, bf16[2,256,512]{2,1,0:T(8,12...) custom-call(s32[2,4]{1,0:T(2,128)S(1)} %copy-done.2, s32[2,4]{1,0:T(2,128)S(1)} %copy-done.4, ...), custom_call_target="tpu_custom_call" | custom-call | flops 1459617792 | bytes 7504384 | tf_op jit(solution)/shard_map/prepare/pallas_call | solution.py:142
  40.0 0.0 collective-permute-done.9
  40.0 0.1 collective-permute-start.11
  40.1 1.3 %collective-permute-done.11.refs_1_ = f32[160,128]{1,0:T(8,128)S(1)} collective-permute-done((f32[160,128]{1,0:T(8,128)S(1)}, f32[160,128]{1,0:T(8,128)S(1)}, u32[]{:S(2)}, u32[]{:S(2)}) %collective-permute-start.11) | collective-permute-done | bytes 81952 | tf_op jit(solution)/shard_map/ppermute | solution.py:591
  41.3 1.9 %finish.1 = (f32[2,128,512]{2,1,0:T(8,128)}, f32[2,64,512]{2,1,0:T(8,128)}) custom-call(f32[160,128]{1,0:T(8,128)S(1)} %broadcast_add_fusion.1.refs_0_, f32[160,128]{1,0:T(8,128)S(1)} %collective-permute-done.11.refs_1_, bf16[384,256]{1,0:T(8,128)(2,1)S(1)} %get-tuple-element.43.refs_2_, bf16[384,256]{1,0:T(8,128)(2,1)S(1)} %get-tuple-element.44.refs_3_, ...), custom_call_target="tpu_custom_call" | custom-call | flops 452984832 | bytes 4620288 | tf_op jit(solution)/shard_map/finish/pallas_call | solution.py:142
  (3 shorter events, 0.0 us)
Async XLA Ops:
  0.6 8.1 %copy-start.1 = (f32[2,64,512]{2,1,0:T(8,128)S(1)}, f32[2,64,512]{2,1,0:T(8,128)}, u32[]{:S(2)}) copy-start(f32[2,64,512]{2,1,0:T(8,128)} %refs_2_.7) | copy-start | bytes 786436
  0.6 12.4 %collective-permute-start = (f32[2,64,512]{2,1,0:T(8,128)}, f32[2,64,512]{2,1,0:T(8,128)S(1)}, u32[]{:S(2)}, u32[]{:S(2)}) collective-permute-start(f32[2,64,512]{2,1,0:T(8,128)} %refs_2_.7), channel_id=1, source_target_pairs={{0,1},{1,2},{2,3},{3,0},{4,5},{5,6},{6,7},{7,4},{8,9},{9,10},{10,1... | collective-permute-start | bytes 786440 | tf_op jit(solution)/shard_map/ppermute | solution.py:455
  3.7 7.2 %collective-permute-start.1 = (s32[2,4]{1,0:T(2,128)}, s32[2,4]{1,0:T(2,128)S(1)}, u32[]{:S(2)}, u32[]{:S(2)}) collective-permute-start(s32[2,4]{1,0:T(2,128)} %refs_1_.9), channel_id=1, source_target_pairs={{0,4},{4,8},{8,12},{12,16},{16,20},{20,24},{24,28},{28,0},{1,5},{5... | collective-permute-start | bytes 104 | tf_op jit(solution)/shard_map/ppermute | solution.py:455
  3.7 0.7 %copy-start.3 = (s32[2,4]{1,0:T(2,128)S(1)}, s32[2,4]{1,0:T(2,128)}, u32[]{:S(2)}) copy-start(s32[2,4]{1,0:T(2,128)} %refs_1_.9) | copy-start | bytes 100
  8.7 4.4 %copy-start.2 = (s32[2,4]{1,0:T(2,128)S(1)}, s32[2,4]{1,0:T(2,128)}, u32[]{:S(2)}) copy-start(s32[2,4]{1,0:T(2,128)} %refs_0_.13) | copy-start | bytes 100
  8.7 8.6 %collective-permute-start.3 = (f32[2,64,512]{2,1,0:T(8,128)S(1)}, f32[2,64,512]{2,1,0:T(8,128)S(1)}, u32[]{:S(2)}, u32[]{:S(2)}) collective-permute-start(f32[2,64,512]{2,1,0:T(8,128)S(1)} %broadcast_add_fusion), channel_id=1, source_target_pairs={{0,3},{1,0},{2,1},{3,2},{4,7},{5,4},{6,5},{7,6},{8,11},{9,8},{10,9... | collective-permute-start | bytes 786440 | tf_op jit(solution)/shard_map/ppermute | solution.py:455
  14.0 8.3 %collective-permute-start.2 = (f32[2,64,256]{2,1,0:T(8,128)S(1)}, f32[2,64,256]{2,1,0:T(8,128)S(1)}, u32[]{:S(2)}, u32[]{:S(2)}) collective-permute-start(f32[2,64,256]{2,1,0:T(8,128)S(1)} %chosen.1), channel_id=1, source_target_pairs={{0,1},{1,2},{2,3},{3,0},{4,5},{5,6},{6,7},{7,4},{8,9},{9,10},{10,1... | collective-permute-start | bytes 393224 | tf_op jit(solution)/shard_map/ppermute | solution.py:455
  16.2 11.5 %copy-start = (f32[2,512,512]{2,1,0:T(8,128)S(1)}, f32[2,512,512]{2,1,0:T(8,128)}, u32[]{:S(2)}) copy-start(f32[2,512,512]{2,1,0:T(8,128)} %refs_3_.1) | copy-start | bytes 6291460
  23.0 6.2 %copy-start.4 = (s32[2,4]{1,0:T(2,128)S(1)}, s32[2,4]{1,0:T(2,128)}, u32[]{:S(2)}) copy-start(s32[2,4]{1,0:T(2,128)} %refs_1_.9) | copy-start | bytes 100
  23.0 2.0 %collective-permute-start.4 = (f32[512,256]{1,0:T(8,128)S(1)}, f32[512,256]{1,0:T(8,128)S(1)}, u32[]{:S(2)}, u32[]{:S(2)}) collective-permute-start(f32[512,256]{1,0:T(8,128)S(1)} %get-tuple-element.32.refs_0_), channel_id=1, source_target_pairs={{0,4},{4,0},{8,12},{12,8},{16,20},{20,16},{24,28},{28,24},{1,5},{5... | collective-permute-start | bytes 1572872 | tf_op jit(solution)/shard_map/ppermute | solution.py:534
  25.6 6.4 %collective-permute-start.5 = (f32[128,256]{1,0:T(8,128)S(1)}, f32[128,256]{1,0:T(8,128)S(1)}, u32[]{:S(2)}, u32[]{:S(2)}) collective-permute-start(f32[128,256]{1,0:T(8,128)S(1)} %get-tuple-element.35), channel_id=1, source_target_pairs={{0,8},{4,12},{8,0},{12,4},{16,24},{20,28},{24,16},{28,20},{1,9},{5... | collective-permute-start | bytes 393224 | tf_op jit(solution)/shard_map/ppermute | solution.py:593
  27.3 5.8 %collective-permute-start.7 = (f32[160,128]{1,0:T(8,128)S(1)}, f32[160,128]{1,0:T(8,128)S(1)}, u32[]{:S(2)}, u32[]{:S(2)}) collective-permute-start(f32[160,128]{1,0:T(8,128)S(1)} %get-tuple-element.36.refs_6_), channel_id=1, source_target_pairs={{0,8},{4,12},{8,0},{12,4},{16,24},{20,28},{24,16},{28,20},{1,9},{5... | collective-permute-start | bytes 245768 | tf_op jit(solution)/shard_map/ppermute | solution.py:587
  30.5 6.4 %collective-permute-start.10 = (f32[2,64,256]{2,1,0:T(8,128)S(1)}, f32[2,64,256]{2,1,0:T(8,128)S(1)}, u32[]{:S(2)}, u32[]{:S(2)}) collective-permute-start(f32[2,64,256]{2,1,0:T(8,128)S(1)} %rest.1), channel_id=1, source_target_pairs={{0,1},{1,0},{2,3},{3,2},{4,5},{5,4},{6,7},{7,6},{8,9},{9,8},{10,11... | collective-permute-start | bytes 393224 | tf_op jit(solution)/shard_map/ppermute | solution.py:560
  32.0 2.5 %collective-permute-start.6 = (f32[128,256]{1,0:T(8,128)S(1)}, f32[128,256]{1,0:T(8,128)S(1)}, u32[]{:S(2)}, u32[]{:S(2)}) collective-permute-start(f32[128,256]{1,0:T(8,128)S(1)} %collective-permute-done.5.refs_2_.refs_12_), channel_id=1, source_target_pairs={{0,4},{4,0},{8,12},{12,8},{16,20},{20,16},{24,28},{28,24},{1,5},{5... | collective-permute-start | bytes 393224 | tf_op jit(solution)/shard_map/ppermute | solution.py:596
  33.1 1.3 %collective-permute-start.8 = (f32[160,128]{1,0:T(8,128)S(1)}, f32[160,128]{1,0:T(8,128)S(1)}, u32[]{:S(2)}, u32[]{:S(2)}) collective-permute-start(f32[160,128]{1,0:T(8,128)S(1)} %broadcast_add_fusion.2.refs_4_.refs_14_), channel_id=1, source_target_pairs={{0,4},{4,0},{8,12},{12,8},{16,20},{20,16},{24,28},{28,24},{1,5},{5... | collective-permute-start | bytes 245768 | tf_op jit(solution)/shard_map/ppermute | solution.py:596
  35.3 4.7 %collective-permute-start.9 = (f32[160,128]{1,0:T(8,128)S(1)}, f32[160,128]{1,0:T(8,128)S(1)}, u32[]{:S(2)}, u32[]{:S(2)}) collective-permute-start(f32[160,128]{1,0:T(8,128)S(1)} %merge.1), channel_id=1, source_target_pairs={{0,16},{4,20},{8,24},{12,28},{16,0},{20,4},{24,8},{28,12},{1,17},{... | collective-permute-start | bytes 245768 | tf_op jit(solution)/shard_map/ppermute | solution.py:587
  40.0 1.3 %collective-permute-start.11 = (f32[160,128]{1,0:T(8,128)S(1)}, f32[160,128]{1,0:T(8,128)S(1)}, u32[]{:S(2)}, u32[]{:S(2)}) collective-permute-start(f32[160,128]{1,0:T(8,128)S(1)} %broadcast_add_fusion.1.refs_0_), channel_id=1, source_target_pairs={{0,4},{4,0},{8,12},{12,8},{16,20},{20,16},{24,28},{28,24},{1,5},{5... | collective-permute-start | bytes 245768 | tf_op jit(solution)/shard_map/ppermute | solution.py:591

commit v15 on v14

--- a/solution.py
+++ b/solution.py
@@ -180,29 +180,53 @@
     )
 
 
-def pick_kernel(panel, *refs):
-    *scalar_refs, inv_hbm, high_ref, low_ref, inv_ref, sem = refs
-    copy = pltpu.make_async_copy(inv_hbm.at[panel], inv_ref, sem)
-    copy.start()
-    chosen = chosen_of(panel, *scalar_refs)
-    copy.wait()
+def pick_into(high_ref, low_ref, chosen, *inv_at):
     for t in range(len(chosen) // 2):
         columns = slice(t * LANES, (t + 1) * LANES)
         high_ref[:, columns], low_ref[:, columns] = split(
-            two_blocks(tile_of(inv_ref), chosen[2 * t], chosen[2 * t + 1])
+            two_blocks(tile_of(*inv_at), chosen[2 * t], chosen[2 * t + 1])
         )
 
 
-def prior_kernel(panel, high_ref, low_ref, inv_hbm, base_ref, own_ref, token_ref, inv_ref, sem):
-    copy = pltpu.make_async_copy(inv_hbm.at[panel], inv_ref, sem)
-    copy.start()
+def load_kernel(
+    owners, mask_hbm, fill_hbm, inv_hbm, inv_ref, high_ref, low_ref, keep_ref,
+    sent_ref, mask_ref, fill_ref, sems
+):
+    panels, rows, _ = keep_ref.shape
+    small = [
+        pltpu.make_async_copy(fill_hbm, fill_ref, sems.at[panels]),
+        pltpu.make_async_copy(mask_hbm, mask_ref, sems.at[panels + 1]),
+        pltpu.make_async_copy(fill_hbm, sent_ref, sems.at[panels + 2]),
+    ]
+    large = [
+        pltpu.make_async_copy(inv_hbm.at[p], inv_ref.at[p], sems.at[p]) for p in range(panels)
+    ]
+    for copy in (*small, *reversed(large)):
+        copy.start()
+    for copy in small:
+        copy.wait()
+    for p in range(panels):
+        for s, slot in enumerate(slots_of(owners, rows)):
+            ones = jnp.ones((BLOCK, keep_ref.shape[2]), F32)
+            keep_ref[p, s * BLOCK : (s + 1) * BLOCK, :] = kept_rows(mask_ref, p, slot, ones)
+    large[-1].wait()
+    pick_into(high_ref, low_ref, chosen_of(panels - 1, fill_ref), inv_ref, panels - 1)
+    for copy in large[:-1]:
+        copy.wait()
+
+
+def pick_kernel(panel, *refs):
+    *scalar_refs, inv_ref, high_ref, low_ref = refs
+    pick_into(high_ref, low_ref, chosen_of(panel, *scalar_refs), inv_ref, panel)
+
+
+def prior_kernel(panel, high_ref, low_ref, inv_ref, base_ref, own_ref, token_ref):
     token_ref[...] = jnp.zeros_like(token_ref)
     own_cols = own_ref.shape[0]
     own_at = pl.ds(pl.multiple_of(lax.axis_index("row") * own_cols, own_cols), own_cols)
     picked = (high_ref[...], low_ref[...])
     base_ref[...] = mm(picked, picked, TN)
-    copy.wait()
-    own_ref[...] = mm(inv_ref[:, own_at], inv_ref[...], TN)
+    own_ref[...] = mm(inv_ref[panel, :, own_at], inv_ref[panel], TN)
 
 
 class Plan(NamedTuple):
@@ -249,11 +273,11 @@
     )
 
 
-def chosen_kernel(owners, mask_ref, part, *refs):
+def chosen_kernel(part, keep_ref, *refs):
     *pick_refs, out_ref = refs
     for p in range(out_ref.shape[0]):
         pick = (pick_refs[2 * p][...], pick_refs[2 * p + 1][...])
-        out_ref[p] = mm(kept_block(mask_ref, p, owners, part[p]), pick)
+        out_ref[p] = mm(part[p], pick) * keep_ref[p]
 
 
 def rest_kernel(owners, mask_ref, fill_ref, prior_ref, inv_ref, *refs):
@@ -454,50 +478,63 @@
         count = lax.axis_size(axis)
         return lax.ppermute(x, axis, [(i, (i + distance) % count) for i in range(count)])
 
-    prior_fill = turn(fill_blocks, "seg", 1)
     pick = jax.ShapeDtypeStruct((width, chosen_cols), BF16)
-    bases, priors, picks, tokens = [], [], [], []
+    short = row_count == 4
+    far = row_count // 2
+    whose = [tuple((i - d) % row_count for i in range(row_count)) for d in range(row_count)]
+    inv, high, low, keep, sent_fill = call(
+        functools.partial(load_kernel, whose[1] if short else whose[far]),
+        [
+            shape(*inv_diag.shape), pick, pick, shape(panels, rows, chosen_cols),
+            jax.ShapeDtypeStruct(fill_blocks.shape, fill_blocks.dtype),
+        ],
+        [],
+        [],
+        far=[fill_mask, fill_blocks, inv_diag],
+        scratch=[
+            pltpu.SMEM(fill_mask.shape, jnp.int32),
+            pltpu.SMEM(fill_blocks.shape, jnp.int32),
+            pltpu.SemaphoreType.DMA((panels + 3,)),
+        ],
+        name="load",
+    )
+    prior_fill = turn(sent_fill, "seg", 1)
+    picks, bases, priors = [], [], []
     for p in range(panels):
-        copy_of_inv = [pltpu.VMEM((width, width), F32), pltpu.SemaphoreType.DMA]
-        high_low = call(
-            functools.partial(pick_kernel, p),
-            [pick, pick],
-            [fill_blocks] if p else [fill_blocks, prior_fill],
-            [],
-            far=[inv_diag],
-            scratch=copy_of_inv,
-            flops=(0 if p else 20) * width**3,
-            name="pick",
-        )
+        high_low = [high, low]
+        if p < panels - 1:
+            high_low = call(
+                functools.partial(pick_kernel, p),
+                [pick, pick],
+                [fill_blocks] if p else [fill_blocks, prior_fill],
+                [inv],
+                flops=20 * width**3,
+                name="pick",
+            )
         base, own_prior, token = call(
             functools.partial(prior_kernel, p),
             [shape(chosen_cols, chosen_cols), shape(own_cols, width), shape(1, 1, width)],
             [],
-            high_low,
-            far=[inv_diag],
-            scratch=copy_of_inv,
+            [*high_low, inv],
+            flops=6 * width * (chosen_cols * chosen_cols + own_cols * width),
             name="prior",
         )
+        picks += high_low
         bases.append(base)
         priors.append(own_prior)
-        picks += high_low
-        tokens.append(token)
-    short = row_count == 4
-    ups, downs = [factor_off], [factor_off + tokens[-1]]
+    ups, downs = [factor_off], [factor_off + token]
     for _ in range(row_count // 2 - short):
         ups.append(turn(ups[-1], "row", 1))
     for _ in range((row_count - 1) // 2):
         downs.append(turn(downs[-1], "row", -1))
-    far = row_count // 2
     came = [d for d in range(row_count) if d != far]
-    whose = [tuple((i - d) % row_count for i in range(row_count)) for d in range(row_count)]
     plan = Plan(tuple(whose[d] for d in came), whose[far])
     parts = ups[:far] + downs[:0:-1]
     (late,) = call(
-        functools.partial(chosen_kernel, whose[1] if short else whose[far]),
+        chosen_kernel,
         [shape(panels, rows, chosen_cols)],
-        [fill_mask],
-        [ups[-1], *picks],
+        [],
+        [ups[-1], keep, *picks],
         flops=6 * panels * rows * chosen_cols * width,
         name="chosen",
     )
@@ -524,7 +561,7 @@
         functools.partial(maps_kernel, plan),
         [shape(panels, size, width), shape(1, half)],
         [fill_mask],
-        [inv_diag, *parts],
+        [inv, *parts],
         scratch=[pltpu.VMEM((size, width), F32)],
         flops=6 * panels * size * width * width,
         mib=24,
@@ -550,7 +587,7 @@
         functools.partial(rest_kernel, held_by),
         [shape(panels, rows, width - chosen_cols)],
         [fill_mask, fill_blocks, prior_fill],
-        [inv_diag, *held, send],
+        [inv, *held, send],
         scratch=[pltpu.VMEM((rows, width), F32)],
         flops=6 * panels * rows * width * width,
         mib=24,

time: 43.5 us -> 43.4 us (level)
  waiting for transfers between devices: 11.1 us -> 16.8 us
  Pallas kernels: 21 us -> 16.2 us
  local copies, waits for them, and re-layouts: 0.7 us -> 0.01 us
    ppermute x4, waiting for transfers between devices: 4.43 us -> 10 us  [turn(): lax.ppermute(x, axis, [(i, (i + distance) % count) for i in range(count)])]
    pallas_call x13, Pallas kernels: 21 us -> 16.2 us  [call(): pl.pallas_call(inner, out_shape=[*outs, *(jax.ShapeDtypeStruct(a.shape, a...]
    unnamed x10 -> x6, local copies, waits for them, and re-layouts: 0.7 us -> 0.01 us
  transfers between devices with their start and end apart: 12 -> 12, of which waited for: 7 -> 9; matrix products, arithmetic and copies ran while one was open for 0% -> 0% of each run, Pallas kernels for 41% -> 30%
where the time goes in v15:
time: 43.4 us; the launch traced here: 43.3 us
  waiting for transfers between devices  16.8 us (39%)
  Pallas kernels  16.2 us (37%)
  starting transfers between devices  9.34 us (22%)
  between operations  0.82 us (2%)
    pallas_call x13, Pallas kernels, call(): pl.pallas_call(inner, out_shape=[*outs, *(jax.ShapeDtypeStruct(a.shape, a...  16.2 us
    ppermute x4, waiting for transfers between devices, turn(): lax.ppermute(x, axis, [(i, (i + distance) % count) for i in range(count)])  10 us
    ppermute x4, starting transfers between devices, turn(): lax.ppermute(x, axis, [(i, (i + distance) % count) for i in range(count)])  5.3 us
    ppermute x2, starting transfers between devices, body(): got = lax.ppermute(send, 'seg', partner)  2.15 us
    ppermute x1, waiting for transfers between devices, body(): other_whole = lax.ppermute(own_whole, 'seg', swap)  1.9 us
    ppermute x1, starting transfers between devices, body(): got_t = lax.ppermute(send_t, 'seg', partner)  1.61 us
    ppermute x1, waiting for transfers between devices, body(): got_t = lax.ppermute(send_t, 'seg', partner)  1.4 us
    ppermute x1, waiting for transfers between devices, body(): lax.ppermute(got, 'seg', swap)  1.26 us
  transfers between devices with their start and end apart: 12, of which 9 were waited for; matrix products, arithmetic and copies ran while one was open for 0% of the time, Pallas kernels for 30%

profile of v15, /device:TPU:0, one launch (start us, length us, event | category | flops | bytes accessed | tf_op | source)
XLA Modules:
  0.0 43.3 jit_solution(9729806979887329596)
XLA Ops:
  0.6 0.0 copy-start
  0.6 3.1 %collective-permute-start = (f32[2,64,512]{2,1,0:T(8,128)}, f32[2,64,512]{2,1,0:T(8,128)S(1)}, u32[]{:S(2)}, u32[]{:S(2)}) collective-permute-start(f32[2,64,512]{2,1,0:T(8,128)} %refs_2_.3), channel_id=1, source_target_pairs={{0,1},{1,2},{2,3},{3,0},{4,5},{5,6},{6,7},{7,4},{8,9},{9,10},{10,1... | collective-permute-start | bytes 786440 | tf_op jit(solution)/shard_map/ppermute | solution.py:479
  3.7 1.6 %load.1 = (f32[2,512,512]{2,1,0:T(8,128)S(1)}, bf16[512,256]{1,0:T(8,128)(2,1)S(1)}, bf16[512,256]{1,0:T(8,128)(2,1)S(1)}, f32[2,64,256]{2,1,0:T(8,128)S(1)}, s32[2,4]{1,0:T(2,128)S(1)}) custom-call(s32[2,4]{1,0:T(2,128)} %refs_0_.11, s32[2,4]{1,0:T(2,128)} %refs_1_.7, f32[2,512,512]{2,1,0:T(8,128)} %refs_2_.2), custom_call_target="tpu_custom_call" | custom-call | bytes 5374048 | tf_op jit(solution)/shard_map/load/pallas_call | solution.py:142
  5.4 0.0 copy-start.2
  5.4 0.1 collective-permute-start.1
  5.5 0.7 %prior.2 = (f32[256,256]{1,0:T(8,128)S(1)}, f32[128,512]{1,0:T(8,128)S(1)}, f32[1,1,512]{2,1,0:T(1,128)S(1)}) custom-call(bf16[512,256]{1,0:T(8,128)(2,1)S(1)} %get-tuple-element.33.refs_4_.refs_0_.refs_6_, bf16[512,256]{1,0:T(8,128)(2,1)S(1)} %get-tuple-element.34.refs_5_.refs_1_.refs_7_, f32[2,512,512]{2,1,0:T(8,128)S(1)} %get-tuple-element.30.refs_2_.refs_1_.refs_3_), custom_call_target="tpu_custom_call" | custom-call | flops 402653184 | bytes 3672064 | tf_op jit(solution)/shard_map/prior/pallas_call | solution.py:142
  6.1 0.0 copy-done
  6.2 2.1 %collective-permute-start.3 = (f32[2,64,512]{2,1,0:T(8,128)S(1)}, f32[2,64,512]{2,1,0:T(8,128)S(1)}, u32[]{:S(2)}, u32[]{:S(2)}) collective-permute-start(f32[2,64,512]{2,1,0:T(8,128)S(1)} %broadcast_add_fusion), channel_id=1, source_target_pairs={{0,3},{1,0},{2,1},{3,2},{4,7},{5,4},{6,5},{7,6},{8,11},{9,8},{10,9... | collective-permute-start | bytes 786440 | tf_op jit(solution)/shard_map/ppermute | solution.py:479
  8.3 1.1 %collective-permute-done.1.refs_1_.refs_2_ = s32[2,4]{1,0:T(2,128)S(1)} collective-permute-done((s32[2,4]{1,0:T(2,128)S(1)}, s32[2,4]{1,0:T(2,128)S(1)}, u32[]{:S(2)}, u32[]{:S(2)}) %collective-permute-start.1) | collective-permute-done | bytes 64 | tf_op jit(solution)/shard_map/ppermute | solution.py:479
  9.3 0.0 copy-done.2
  9.3 0.9 %pick.1 = (bf16[512,256]{1,0:T(8,128)(2,1)S(1)}, bf16[512,256]{1,0:T(8,128)(2,1)S(1)}) custom-call(s32[2,4]{1,0:T(2,128)S(1)} %copy-done.2, s32[2,4]{1,0:T(2,128)S(1)} %collective-permute-done.1.refs_1_.refs_2_, f32[2,512,512]{2,1,0:T(8,128)S(1)} %get-tuple-element.30.refs_2_.refs_1_.refs_3_), custom_call_target="tpu_custom_call" | custom-call | flops 2684354560 | bytes 3145728 | tf_op jit(solution)/shard_map/pick/pallas_call | solution.py:142
  10.3 2.2 %collective-permute-done.refs_0_.refs_2_.refs_3_.refs_4_ = f32[2,64,512]{2,1,0:T(8,128)S(1)} collective-permute-done((f32[2,64,512]{2,1,0:T(8,128)}, f32[2,64,512]{2,1,0:T(8,128)S(1)}, u32[]{:S(2)}, u32[]{:S(2)}) %collective-permute-start) | collective-permute-done | bytes 262176 | tf_op jit(solution)/shard_map/ppermute | solution.py:479
  12.4 0.0 copy-start.1
  12.4 0.4 chosen.1
  12.8 0.1 collective-permute-start.2
  12.9 1.1 %prior.3 = (f32[256,256]{1,0:T(8,128)S(1)}, f32[128,512]{1,0:T(8,128)S(1)}, f32[1,1,512]{2,1,0:T(1,128)}) custom-call(bf16[512,256]{1,0:T(8,128)(2,1)S(1)} %get-tuple-element.31.refs_2_.refs_4_.refs_0_, bf16[512,256]{1,0:T(8,128)(2,1)S(1)} %get-tuple-element.32.refs_3_.refs_5_.refs_1_, f32[2,512,512]{2,1,0:T(8,128)S(1)} %get-tuple-element.30.refs_2_.refs_1_.refs_3_), custom_call_target="tpu_custom_call" | custom-call | flops 402653184 | bytes 3672064 | tf_op jit(solution)/shard_map/prior/pallas_call | solution.py:142
  14.0 3.8 %collective-permute-done.3.refs_3_.refs_4_.refs_5_ = f32[2,64,512]{2,1,0:T(8,128)S(1)} collective-permute-done((f32[2,64,512]{2,1,0:T(8,128)S(1)}, f32[2,64,512]{2,1,0:T(8,128)S(1)}, u32[]{:S(2)}, u32[]{:S(2)}) %collective-permute-start.3) | collective-permute-done | bytes 262176 | tf_op jit(solution)/shard_map/ppermute | solution.py:479
  17.8 0.0 copy-done.1
  17.8 1.7 %links.1.refs_1_ = f32[2,256,256]{2,1,0:T(8,128)S(1)} custom-call(s32[2,4]{1,0:T(2,128)S(1)} %copy-done.1, f32[2,64,512]{2,1,0:T(8,128)S(1)} %copy-done, f32[2,64,512]{2,1,0:T(8,128)S(1)} %collective-permute-done.refs_0_.refs_2_.refs_3_.refs_4_, f32[2,64,512]{2,1,0:T(8,128)S(1)} %collective-permute-done.3.refs_3_.refs_4_.refs_5_, ...), custom_call_target="tpu_custom_call" | custom-call | flops 402653184 | bytes 3407872 | tf_op jit(solution)/shard_map/links/pallas_call | solution.py:142
  19.5 3.0 %collective-permute-done.2.refs_0_.refs_10_ = f32[2,64,256]{2,1,0:T(8,128)S(1)} collective-permute-done((f32[2,64,256]{2,1,0:T(8,128)S(1)}, f32[2,64,256]{2,1,0:T(8,128)S(1)}, u32[]{:S(2)}, u32[]{:S(2)}) %collective-permute-start.2) | collective-permute-done | bytes 131104 | tf_op jit(solution)/shard_map/ppermute | solution.py:479
  22.5 0.6 %segment.1 = (f32[2,256,256]{2,1,0:T(8,128)S(1)}, f32[512,256]{1,0:T(8,128)S(1)}) custom-call(f32[2,64,256]{2,1,0:T(8,128)S(1)} %collective-permute-done.2.refs_0_.refs_10_, f32[2,256,256]{2,1,0:T(8,128)S(1)} %links.1.refs_1_, f32[256,256]{1,0:T(8,128)S(1)} %get-tuple-element.36.refs_2_.refs_3_, f32[256,256]{1,0:T(8,128)S(1)} %get-tuple-element.37.refs_3_.refs_4_), custom_call_target="tpu_custom_call" | custom-call | flops 301989888 | bytes 2228224 | tf_op jit(solution)/shard_map/segment/pallas_call | solution.py:142
  23.1 0.1 collective-permute-start.4
  23.2 1.9 %collective-permute-done.4.refs_1_.refs_7_ = f32[512,256]{1,0:T(8,128)S(1)} collective-permute-done((f32[512,256]{1,0:T(8,128)S(1)}, f32[512,256]{1,0:T(8,128)S(1)}, u32[]{:S(2)}, u32[]{:S(2)}) %collective-permute-start.4) | collective-permute-done | bytes 524320 | tf_op jit(solution)/shard_map/ppermute | solution.py:571
  25.1 0.6 %chip.1 = (f32[256,256]{1,0:T(8,128)S(1)}, f32[256,256]{1,0:T(8,128)S(1)}, f32[160,128]{1,0:T(8,128)S(1)}, f32[128,256]{1,0:T(8,128)S(1)}) custom-call(f32[512,256]{1,0:T(8,128)S(1)} %get-tuple-element.38.refs_0_, f32[512,256]{1,0:T(8,128)S(1)} %collective-permute-done.4.refs_1_.refs_7_), custom_call_target="tpu_custom_call" | custom-call | flops 301989888 | bytes 1785856 | tf_op jit(solution)/shard_map/chip/pallas_call | solution.py:142
  25.7 1.6 %collective-permute-start.5 = (f32[128,256]{1,0:T(8,128)S(1)}, f32[128,256]{1,0:T(8,128)S(1)}, u32[]{:S(2)}, u32[]{:S(2)}) collective-permute-start(f32[128,256]{1,0:T(8,128)S(1)} %get-tuple-element.41), channel_id=1, source_target_pairs={{0,8},{4,12},{8,0},{12,4},{16,24},{20,28},{24,16},{28,20},{1,9},{5... | collective-permute-start | bytes 393224 | tf_op jit(solution)/shard_map/ppermute | solution.py:630
  27.3 0.5 %collective-permute-start.7 = (f32[160,128]{1,0:T(8,128)S(1)}, f32[160,128]{1,0:T(8,128)S(1)}, u32[]{:S(2)}, u32[]{:S(2)}) collective-permute-start(f32[160,128]{1,0:T(8,128)S(1)} %get-tuple-element.42.refs_6_), channel_id=1, source_target_pairs={{0,8},{4,12},{8,0},{12,4},{16,24},{20,28},{24,16},{28,20},{1,9},{5... | collective-permute-start | bytes 245768 | tf_op jit(solution)/shard_map/ppermute | solution.py:624
  27.8 1.5 %maps.1 = (f32[2,256,512]{2,1,0:T(8,128)S(1)}, f32[1,128]{1,0:T(1,128)S(1)}) custom-call(s32[2,4]{1,0:T(2,128)S(1)} %copy-done.1, f32[2,512,512]{2,1,0:T(8,128)S(1)} %get-tuple-element.30.refs_2_.refs_1_.refs_3_, f32[2,64,512]{2,1,0:T(8,128)S(1)} %copy-done, f32[2,64,512]{2,1,0:T(8,128)S(1)} %collective-permute-done.refs_0_.refs_2_.refs_3_.refs_4_, ...), custom_call_target="tpu_custom_call" | custom-call | flops 805306368 | bytes 3932672 | tf_op jit(solution)/shard_map/maps/pallas_call | solution.py:142
  29.3 1.3 %rest.1 = f32[2,64,256]{2,1,0:T(8,128)S(1)} custom-call(s32[2,4]{1,0:T(2,128)S(1)} %copy-done.1, s32[2,4]{1,0:T(2,128)S(1)} %copy-done.2, s32[2,4]{1,0:T(2,128)S(1)} %collective-permute-done.1.refs_1_.refs_2_, f32[2,512,512]{2,1,0:T(8,128)S(1)} %get-tuple-element.30.refs_2_.refs_1_.refs_3_, ...), custom_call_target="tpu_custom_call" | custom-call | flops 201326592 | bytes 2834432 | tf_op jit(solution)/shard_map/rest/pallas_call | solution.py:142
  30.6 0.1 collective-permute-start.10
  30.7 1.4 %collective-permute-done.5.refs_2_.refs_12_ = f32[128,256]{1,0:T(8,128)S(1)} collective-permute-done((f32[128,256]{1,0:T(8,128)S(1)}, f32[128,256]{1,0:T(8,128)S(1)}, u32[]{:S(2)}, u32[]{:S(2)}) %collective-permute-start.5) | collective-permute-done | bytes 131104 | tf_op jit(solution)/shard_map/ppermute | solution.py:630
  32.1 0.0 collective-permute-start.6
  32.1 1.0 %collective-permute-done.7 = f32[160,128]{1,0:T(8,128)S(1)} collective-permute-done((f32[160,128]{1,0:T(8,128)S(1)}, f32[160,128]{1,0:T(8,128)S(1)}, u32[]{:S(2)}, u32[]{:S(2)}) %collective-permute-start.7) | collective-permute-done | bytes 81952 | tf_op jit(solution)/shard_map/ppermute | solution.py:624
  33.1 0.1 collective-permute-start.8
  33.1 1.3 %collective-permute-done.8.refs_5_.refs_15_ = f32[160,128]{1,0:T(8,128)S(1)} collective-permute-done((f32[160,128]{1,0:T(8,128)S(1)}, f32[160,128]{1,0:T(8,128)S(1)}, u32[]{:S(2)}, u32[]{:S(2)}) %collective-permute-start.8) | collective-permute-done | bytes 81952 | tf_op jit(solution)/shard_map/ppermute | solution.py:633
  34.4 0.0 collective-permute-done.6.refs_3_.refs_13_
  34.4 0.8 %merge.1 = f32[160,128]{1,0:T(8,128)S(1)} custom-call(f32[256,256]{1,0:T(8,128)S(1)} %get-tuple-element.39.refs_0_, f32[256,256]{1,0:T(8,128)S(1)} %get-tuple-element.40.refs_1_, f32[128,256]{1,0:T(8,128)S(1)} %collective-permute-done.5.refs_2_.refs_12_, f32[128,256]{1,0:T(8,128)S(1)} %collective-permute-done.6.refs_3_.refs_13_, ...), custom_call_target="tpu_custom_call" | custom-call | flops 301989888 | bytes 1032192 | tf_op jit(solution)/shard_map/merge/pallas_call | solution.py:142
  35.2 1.7 %collective-permute-start.9 = (f32[160,128]{1,0:T(8,128)S(1)}, f32[160,128]{1,0:T(8,128)S(1)}, u32[]{:S(2)}, u32[]{:S(2)}) collective-permute-start(f32[160,128]{1,0:T(8,128)S(1)} %merge.1), channel_id=1, source_target_pairs={{0,16},{4,20},{8,24},{12,28},{16,0},{20,4},{24,8},{28,12},{1,17},{... | collective-permute-start | bytes 245768 | tf_op jit(solution)/shard_map/ppermute | solution.py:624
  36.9 0.0 collective-permute-done.10.refs_11_
  36.9 3.1 %prepare.1 = (bf16[384,256]{1,0:T(8,128)(2,1)S(1)}, bf16[384,256]{1,0:T(8,128)(2,1)S(1)}, bf16[2,256,512]{2,1,0:T(8,128)(2,1)S(1)}, bf16[2,256,512]{2,1,0:T(8,12...) custom-call(s32[2,4]{1,0:T(2,128)S(1)} %copy-done.1, s32[2,4]{1,0:T(2,128)S(1)} %copy-done.2, ...), custom_call_target="tpu_custom_call" | custom-call | flops 1459617792 | bytes 7504384 | tf_op jit(solution)/shard_map/prepare/pallas_call | solution.py:142
  40.0 0.0 collective-permute-done.9
  40.0 0.1 collective-permute-start.11
  40.1 1.3 %collective-permute-done.11.refs_1_ = f32[160,128]{1,0:T(8,128)S(1)} collective-permute-done((f32[160,128]{1,0:T(8,128)S(1)}, f32[160,128]{1,0:T(8,128)S(1)}, u32[]{:S(2)}, u32[]{:S(2)}) %collective-permute-start.11) | collective-permute-done | bytes 81952 | tf_op jit(solution)/shard_map/ppermute | solution.py:628
  41.4 1.9 %finish.1 = (f32[2,128,512]{2,1,0:T(8,128)}, f32[2,64,512]{2,1,0:T(8,128)}) custom-call(f32[160,128]{1,0:T(8,128)S(1)} %broadcast_add_fusion.1.refs_0_, f32[160,128]{1,0:T(8,128)S(1)} %collective-permute-done.11.refs_1_, bf16[384,256]{1,0:T(8,128)(2,1)S(1)} %get-tuple-element.49.refs_2_, bf16[384,256]{1,0:T(8,128)(2,1)S(1)} %get-tuple-element.50.refs_3_, ...), custom_call_target="tpu_custom_call" | custom-call | flops 452984832 | bytes 4620288 | tf_op jit(solution)/shard_map/finish/pallas_call | solution.py:142
  (3 shorter events, 0.0 us)
Async XLA Ops:
  0.6 5.5 %copy-start = (f32[2,64,512]{2,1,0:T(8,128)S(1)}, f32[2,64,512]{2,1,0:T(8,128)}, u32[]{:S(2)}) copy-start(f32[2,64,512]{2,1,0:T(8,128)} %refs_2_.3) | copy-start | bytes 786436
  0.6 11.8 %collective-permute-start = (f32[2,64,512]{2,1,0:T(8,128)}, f32[2,64,512]{2,1,0:T(8,128)S(1)}, u32[]{:S(2)}, u32[]{:S(2)}) collective-permute-start(f32[2,64,512]{2,1,0:T(8,128)} %refs_2_.3), channel_id=1, source_target_pairs={{0,1},{1,2},{2,3},{3,0},{4,5},{5,6},{6,7},{7,4},{8,9},{9,10},{10,1... | collective-permute-start | bytes 786440 | tf_op jit(solution)/shard_map/ppermute | solution.py:479
  5.4 4.0 %copy-start.2 = (s32[2,4]{1,0:T(2,128)S(1)}, s32[2,4]{1,0:T(2,128)}, u32[]{:S(2)}) copy-start(s32[2,4]{1,0:T(2,128)} %refs_1_.7) | copy-start | bytes 100
  5.4 3.9 %collective-permute-start.1 = (s32[2,4]{1,0:T(2,128)S(1)}, s32[2,4]{1,0:T(2,128)S(1)}, u32[]{:S(2)}, u32[]{:S(2)}) collective-permute-start(s32[2,4]{1,0:T(2,128)S(1)} %get-tuple-element.29), channel_id=1, source_target_pairs={{0,4},{4,8},{8,12},{12,16},{16,20},{20,24},{24,28},{28,0},{1,5},{5... | collective-permute-start | bytes 104 | tf_op jit(solution)/shard_map/ppermute | solution.py:479
  6.2 11.7 %collective-permute-start.3 = (f32[2,64,512]{2,1,0:T(8,128)S(1)}, f32[2,64,512]{2,1,0:T(8,128)S(1)}, u32[]{:S(2)}, u32[]{:S(2)}) collective-permute-start(f32[2,64,512]{2,1,0:T(8,128)S(1)} %broadcast_add_fusion), channel_id=1, source_target_pairs={{0,3},{1,0},{2,1},{3,2},{4,7},{5,4},{6,5},{7,6},{8,11},{9,8},{10,9... | collective-permute-start | bytes 786440 | tf_op jit(solution)/shard_map/ppermute | solution.py:479
  12.4 5.4 %copy-start.1 = (s32[2,4]{1,0:T(2,128)S(1)}, s32[2,4]{1,0:T(2,128)}, u32[]{:S(2)}) copy-start(s32[2,4]{1,0:T(2,128)} %refs_0_.11) | copy-start | bytes 100
  12.8 9.6 %collective-permute-start.2 = (f32[2,64,256]{2,1,0:T(8,128)S(1)}, f32[2,64,256]{2,1,0:T(8,128)S(1)}, u32[]{:S(2)}, u32[]{:S(2)}) collective-permute-start(f32[2,64,256]{2,1,0:T(8,128)S(1)} %chosen.1), channel_id=1, source_target_pairs={{0,1},{1,2},{2,3},{3,0},{4,5},{5,6},{6,7},{7,4},{8,9},{9,10},{10,1... | collective-permute-start | bytes 393224 | tf_op jit(solution)/shard_map/ppermute | solution.py:479
  23.1 2.0 %collective-permute-start.4 = (f32[512,256]{1,0:T(8,128)S(1)}, f32[512,256]{1,0:T(8,128)S(1)}, u32[]{:S(2)}, u32[]{:S(2)}) collective-permute-start(f32[512,256]{1,0:T(8,128)S(1)} %get-tuple-element.38.refs_0_), channel_id=1, source_target_pairs={{0,4},{4,0},{8,12},{12,8},{16,20},{20,16},{24,28},{28,24},{1,5},{5... | collective-permute-start | bytes 1572872 | tf_op jit(solution)/shard_map/ppermute | solution.py:571
  25.7 6.4 %collective-permute-start.5 = (f32[128,256]{1,0:T(8,128)S(1)}, f32[128,256]{1,0:T(8,128)S(1)}, u32[]{:S(2)}, u32[]{:S(2)}) collective-permute-start(f32[128,256]{1,0:T(8,128)S(1)} %get-tuple-element.41), channel_id=1, source_target_pairs={{0,8},{4,12},{8,0},{12,4},{16,24},{20,28},{24,16},{28,20},{1,9},{5... | collective-permute-start | bytes 393224 | tf_op jit(solution)/shard_map/ppermute | solution.py:630
  27.3 5.7 %collective-permute-start.7 = (f32[160,128]{1,0:T(8,128)S(1)}, f32[160,128]{1,0:T(8,128)S(1)}, u32[]{:S(2)}, u32[]{:S(2)}) collective-permute-start(f32[160,128]{1,0:T(8,128)S(1)} %get-tuple-element.42.refs_6_), channel_id=1, source_target_pairs={{0,8},{4,12},{8,0},{12,4},{16,24},{20,28},{24,16},{28,20},{1,9},{5... | collective-permute-start | bytes 245768 | tf_op jit(solution)/shard_map/ppermute | solution.py:624
  30.6 6.3 %collective-permute-start.10 = (f32[2,64,256]{2,1,0:T(8,128)S(1)}, f32[2,64,256]{2,1,0:T(8,128)S(1)}, u32[]{:S(2)}, u32[]{:S(2)}) collective-permute-start(f32[2,64,256]{2,1,0:T(8,128)S(1)} %rest.1), channel_id=1, source_target_pairs={{0,1},{1,0},{2,3},{3,2},{4,5},{5,4},{6,7},{7,6},{8,9},{9,8},{10,11... | collective-permute-start | bytes 393224 | tf_op jit(solution)/shard_map/ppermute | solution.py:597
  32.1 2.3 %collective-permute-start.6 = (f32[128,256]{1,0:T(8,128)S(1)}, f32[128,256]{1,0:T(8,128)S(1)}, u32[]{:S(2)}, u32[]{:S(2)}) collective-permute-start(f32[128,256]{1,0:T(8,128)S(1)} %collective-permute-done.5.refs_2_.refs_12_), channel_id=1, source_target_pairs={{0,4},{4,0},{8,12},{12,8},{16,20},{20,16},{24,28},{28,24},{1,5},{5... | collective-permute-start | bytes 393224 | tf_op jit(solution)/shard_map/ppermute | solution.py:633
  33.1 1.3 %collective-permute-start.8 = (f32[160,128]{1,0:T(8,128)S(1)}, f32[160,128]{1,0:T(8,128)S(1)}, u32[]{:S(2)}, u32[]{:S(2)}) collective-permute-start(f32[160,128]{1,0:T(8,128)S(1)} %broadcast_add_fusion.2.refs_4_.refs_14_), channel_id=1, source_target_pairs={{0,4},{4,0},{8,12},{12,8},{16,20},{20,16},{24,28},{28,24},{1,5},{5... | collective-permute-start | bytes 245768 | tf_op jit(solution)/shard_map/ppermute | solution.py:633
  35.2 4.8 %collective-permute-start.9 = (f32[160,128]{1,0:T(8,128)S(1)}, f32[160,128]{1,0:T(8,128)S(1)}, u32[]{:S(2)}, u32[]{:S(2)}) collective-permute-start(f32[160,128]{1,0:T(8,128)S(1)} %merge.1), channel_id=1, source_target_pairs={{0,16},{4,20},{8,24},{12,28},{16,0},{20,4},{24,8},{28,12},{1,17},{... | collective-permute-start | bytes 245768 | tf_op jit(solution)/shard_map/ppermute | solution.py:624
  40.0 1.3 %collective-permute-start.11 = (f32[160,128]{1,0:T(8,128)S(1)}, f32[160,128]{1,0:T(8,128)S(1)}, u32[]{:S(2)}, u32[]{:S(2)}) collective-permute-start(f32[160,128]{1,0:T(8,128)S(1)} %broadcast_add_fusion.1.refs_0_), channel_id=1, source_target_pairs={{0,4},{4,0},{8,12},{12,8},{16,20},{20,16},{24,28},{28,24},{1,5},{5... | collective-permute-start | bytes 245768 | tf_op jit(solution)/shard_map/ppermute | solution.py:628

commit v16 on v15

--- a/solution.py
+++ b/solution.py
@@ -130,10 +130,10 @@
 
 
 def call(
-    kernel, outs, scalars, arrays, far=(), out_far=False, through=(), scratch=(), flops=0, mib=16, name=None
+    kernel, outs, scalars, arrays, far=(), anywhere=(), out_far=False, through=(), scratch=(), flops=0, mib=16, name=None
 ):
     moved = sum(a.size * 4 for a in (*arrays, *far)) + sum(o.size * 4 for o in outs)
-    first = len(scalars) + len(arrays) + len(far)
+    first = len(scalars) + len(arrays) + len(far) + len(anywhere)
     count = len(through)
 
     def inner(*refs):
@@ -145,6 +145,7 @@
         in_specs=smem(len(scalars))
         + vmem(len(arrays))
         + [pl.BlockSpec(memory_space=pltpu.HBM)] * len(far)
+        + [pl.BlockSpec(memory_space=pl.ANY)] * len(anywhere)
         + [pl.BlockSpec(memory_space=pl.ANY)] * count,
         out_specs=([pl.BlockSpec(memory_space=pltpu.HBM)] * len(outs) if out_far else vmem(len(outs)))
         + [pl.BlockSpec(memory_space=pl.ANY)] * count,
@@ -153,7 +154,7 @@
         cost_estimate=pl.CostEstimate(flops=flops, bytes_accessed=moved, transcendentals=0),
         compiler_params=pltpu.CompilerParams(vmem_limit_bytes=mib << 20),
         name=name,
-    )(*scalars, *arrays, *(pltpu.with_memory_space_constraint(a, pltpu.HBM) for a in far), *through)
+    )(*scalars, *arrays, *(pltpu.with_memory_space_constraint(a, pltpu.HBM) for a in far), *anywhere, *through)
 
 
 def shape(*dims):
@@ -190,13 +191,12 @@
 
 def load_kernel(
     owners, mask_hbm, fill_hbm, inv_hbm, inv_ref, high_ref, low_ref, keep_ref,
-    sent_ref, mask_ref, fill_ref, sems
+    mask_ref, fill_ref, sems
 ):
     panels, rows, _ = keep_ref.shape
     small = [
         pltpu.make_async_copy(fill_hbm, fill_ref, sems.at[panels]),
         pltpu.make_async_copy(mask_hbm, mask_ref, sems.at[panels + 1]),
-        pltpu.make_async_copy(fill_hbm, sent_ref, sems.at[panels + 2]),
     ]
     large = [
         pltpu.make_async_copy(inv_hbm.at[p], inv_ref.at[p], sems.at[p]) for p in range(panels)
@@ -220,7 +220,7 @@
     pick_into(high_ref, low_ref, chosen_of(panel, *scalar_refs), inv_ref, panel)
 
 
-def prior_kernel(panel, high_ref, low_ref, inv_ref, base_ref, own_ref, token_ref):
+def prior_kernel(panel, high_ref, low_ref, inv_ref, _, base_ref, own_ref, token_ref):
     token_ref[...] = jnp.zeros_like(token_ref)
     own_cols = own_ref.shape[0]
     own_at = pl.ds(pl.multiple_of(lax.axis_index("row") * own_cols, own_cols), own_cols)
@@ -482,11 +482,10 @@
     short = row_count == 4
     far = row_count // 2
     whose = [tuple((i - d) % row_count for i in range(row_count)) for d in range(row_count)]
-    inv, high, low, keep, sent_fill = call(
+    inv, high, low, keep = call(
         functools.partial(load_kernel, whose[1] if short else whose[far]),
         [
             shape(*inv_diag.shape), pick, pick, shape(panels, rows, chosen_cols),
-            jax.ShapeDtypeStruct(fill_blocks.shape, fill_blocks.dtype),
         ],
         [],
         [],
@@ -494,11 +493,11 @@
         scratch=[
             pltpu.SMEM(fill_mask.shape, jnp.int32),
             pltpu.SMEM(fill_blocks.shape, jnp.int32),
-            pltpu.SemaphoreType.DMA((panels + 3,)),
+            pltpu.SemaphoreType.DMA((panels + 2,)),
         ],
         name="load",
     )
-    prior_fill = turn(sent_fill, "seg", 1)
+    prior_fill = turn(fill_blocks, "seg", 1)
     picks, bases, priors = [], [], []
     for p in range(panels):
         high_low = [high, low]
@@ -508,7 +507,6 @@
                 [pick, pick],
                 [fill_blocks] if p else [fill_blocks, prior_fill],
                 [inv],
-                flops=20 * width**3,
                 name="pick",
             )
         base, own_prior, token = call(
@@ -516,7 +514,7 @@
             [shape(chosen_cols, chosen_cols), shape(own_cols, width), shape(1, 1, width)],
             [],
             [*high_low, inv],
-            flops=6 * width * (chosen_cols * chosen_cols + own_cols * width),
+            anywhere=[prior_fill],
             name="prior",
         )
         picks += high_low
@@ -535,7 +533,7 @@
         [shape(panels, rows, chosen_cols)],
         [],
         [ups[-1], keep, *picks],
-        flops=6 * panels * rows * chosen_cols * width,
+        flops=96 * panels * rows * chosen_cols * width,
         name="chosen",
     )
     if short:
@@ -546,7 +544,6 @@
         [fill_mask],
         [*parts, *picks],
         scratch=[pltpu.VMEM((size, chosen_cols), F32)],
-        flops=6 * panels * size * size * width,
         name="links",
     )
     links_t, own_whole = call(

time: 43.4 us -> 42.3 us (0.975)
  waiting for transfers between devices: 16.8 us -> 14.8 us
  starting transfers between devices: 9.34 us -> 10.3 us
    ppermute x4, waiting for transfers between devices: 10 us -> 8.55 us  [turn(): lax.ppermute(x, axis, [(i, (i + distance) % count) for i in range(count)])]
    ppermute x2, starting transfers between devices: 2.15 us -> 2.73 us  [body(): got = lax.ppermute(send, 'seg', partner)]
    ppermute x1, starting transfers between devices: 0.07 us -> 0.64 us  [body(): rest = lax.ppermute(rest, 'row', [(i, i ^ 1) for i in range(row_count)])]
    ppermute x1, waiting for transfers between devices: 1.4 us -> 0.85 us  [body(): got_t = lax.ppermute(send_t, 'seg', partner)]
  transfers between devices with their start and end apart: 12 -> 12, of which waited for: 9 -> 8; matrix products, arithmetic and copies ran while one was open for 0% -> 0% of each run, Pallas kernels for 30% -> 31%
where the time goes in v16:
time: 42.3 us; the launch traced here: 42.1 us
  Pallas kernels  16.2 us (38%)
  waiting for transfers between devices  14.8 us (35%)
  starting transfers between devices  10.3 us (24%)
  between operations  0.82 us (2%)
    pallas_call x13, Pallas kernels, call(): pl.pallas_call(inner, out_shape=[*outs, *(jax.ShapeDtypeStruct(a.shape, a...  16.2 us
    ppermute x4, waiting for transfers between devices, turn(): lax.ppermute(x, axis, [(i, (i + distance) % count) for i in range(count)])  8.55 us
    ppermute x4, starting transfers between devices, turn(): lax.ppermute(x, axis, [(i, (i + distance) % count) for i in range(count)])  5.28 us
    ppermute x2, starting transfers between devices, body(): got = lax.ppermute(send, 'seg', partner)  2.73 us
    ppermute x1, waiting for transfers between devices, body(): other_whole = lax.ppermute(own_whole, 'seg', swap)  1.9 us
    ppermute x1, starting transfers between devices, body(): got_t = lax.ppermute(send_t, 'seg', partner)  1.39 us
    ppermute x1, waiting for transfers between devices, body(): after = (got, lax.ppermute(got, 'seg', swap))  1.26 us
    ppermute x1, waiting for transfers between devices, body(): lax.ppermute(got, 'seg', swap)  1.26 us
  transfers between devices with their start and end apart: 12, of which 8 were waited for; matrix products, arithmetic and copies ran while one was open for 0% of the time, Pallas kernels for 31%

profile of v16, /device:TPU:0, one launch (start us, length us, event | category | flops | bytes accessed | tf_op | source)
XLA Modules:
  0.0 42.1 jit_solution(12924310377412368142)
XLA Ops:
  0.6 0.0 copy-start
  0.6 3.1 %collective-permute-start = (f32[2,64,512]{2,1,0:T(8,128)}, f32[2,64,512]{2,1,0:T(8,128)S(1)}, u32[]{:S(2)}, u32[]{:S(2)}) collective-permute-start(f32[2,64,512]{2,1,0:T(8,128)} %refs_2_.3), channel_id=1, source_target_pairs={{0,1},{1,2},{2,3},{3,0},{4,5},{5,6},{6,7},{7,4},{8,9},{9,10},{10,1... | collective-permute-start | bytes 786440 | tf_op jit(solution)/shard_map/ppermute | solution.py:479
  3.7 0.0 collective-permute-start.1
  3.7 1.6 %load.1 = (f32[2,512,512]{2,1,0:T(8,128)S(1)}, bf16[512,256]{1,0:T(8,128)(2,1)S(1)}, bf16[512,256]{1,0:T(8,128)(2,1)S(1)}, f32[2,64,256]{2,1,0:T(8,128)S(1)}) custom-call(s32[2,4]{1,0:T(2,128)} %refs_0_.11, s32[2,4]{1,0:T(2,128)} %refs_1_.7, f32[2,512,512]{2,1,0:T(8,128)} %refs_2_.2), custom_call_target="tpu_custom_call" | custom-call | bytes 5374016 | tf_op jit(solution)/shard_map/load/pallas_call | solution.py:142
  5.4 0.0 copy-start.1
  5.4 2.4 %collective-permute-done.1.refs_1_.refs_3_.refs_2_ = s32[2,4]{1,0:T(2,128)S(1)} collective-permute-done((s32[2,4]{1,0:T(2,128)}, s32[2,4]{1,0:T(2,128)S(1)}, u32[]{:S(2)}, u32[]{:S(2)}) %collective-permute-start.1) | collective-permute-done | bytes 64 | tf_op jit(solution)/shard_map/ppermute | solution.py:479
  7.8 0.7 %prior.2 = (f32[256,256]{1,0:T(8,128)S(1)}, f32[128,512]{1,0:T(8,128)S(1)}, f32[1,1,512]{2,1,0:T(1,128)S(1)}) custom-call(bf16[512,256]{1,0:T(8,128)(2,1)S(1)} %get-tuple-element.31.refs_4_.refs_0_.refs_6_, bf16[512,256]{1,0:T(8,128)(2,1)S(1)} %get-tuple-element.32.refs_5_.refs_1_.refs_7_, f32[2,512,512]{2,1,0:T(8,128)S(1)} %get-tuple-element.28.refs_2_.refs_1_.refs_3_, ...), custom_call_target="tpu_custom_call" | custom-call | bytes 3672064 | tf_op jit(solution)/shard_map/prior/pallas_call | solution.py:142
  8.5 0.0 copy-done
  8.5 2.1 %collective-permute-start.3 = (f32[2,64,512]{2,1,0:T(8,128)S(1)}, f32[2,64,512]{2,1,0:T(8,128)S(1)}, u32[]{:S(2)}, u32[]{:S(2)}) collective-permute-start(f32[2,64,512]{2,1,0:T(8,128)S(1)} %broadcast_add_fusion), channel_id=1, source_target_pairs={{0,3},{1,0},{2,1},{3,2},{4,7},{5,4},{6,5},{7,6},{8,11},{9,8},{10,9... | collective-permute-start | bytes 786440 | tf_op jit(solution)/shard_map/ppermute | solution.py:479
  10.7 0.0 copy-done.1
  10.7 0.9 %pick.1 = (bf16[512,256]{1,0:T(8,128)(2,1)S(1)}, bf16[512,256]{1,0:T(8,128)(2,1)S(1)}) custom-call(s32[2,4]{1,0:T(2,128)S(1)} %copy-done.1, s32[2,4]{1,0:T(2,128)S(1)} %collective-permute-done.1.refs_1_.refs_3_.refs_2_, f32[2,512,512]{2,1,0:T(8,128)S(1)} %get-tuple-element.28.refs_2_.refs_1_.refs_3_), custom_call_target="tpu_custom_call" | custom-call | bytes 3145728 | tf_op jit(solution)/shard_map/pick/pallas_call | solution.py:142
  11.6 0.8 %collective-permute-done.refs_0_.refs_2_.refs_3_.refs_4_ = f32[2,64,512]{2,1,0:T(8,128)S(1)} collective-permute-done((f32[2,64,512]{2,1,0:T(8,128)}, f32[2,64,512]{2,1,0:T(8,128)S(1)}, u32[]{:S(2)}, u32[]{:S(2)}) %collective-permute-start) | collective-permute-done | bytes 262176 | tf_op jit(solution)/shard_map/ppermute | solution.py:479
  12.4 0.4 chosen.1
  12.8 0.0 copy-start.2
  12.8 0.1 collective-permute-start.2
  12.9 1.1 %prior.3 = (f32[256,256]{1,0:T(8,128)S(1)}, f32[128,512]{1,0:T(8,128)S(1)}, f32[1,1,512]{2,1,0:T(1,128)}) custom-call(bf16[512,256]{1,0:T(8,128)(2,1)S(1)} %get-tuple-element.29.refs_2_.refs_4_.refs_0_, bf16[512,256]{1,0:T(8,128)(2,1)S(1)} %get-tuple-element.30.refs_3_.refs_5_.refs_1_, f32[2,512,512]{2,1,0:T(8,128)S(1)} %get-tuple-element.28.refs_2_.refs_1_.refs_3_, ...), custom_call_target="tpu_custom_call" | custom-call | bytes 3672064 | tf_op jit(solution)/shard_map/prior/pallas_call | solution.py:142
  14.0 5.3 %collective-permute-done.3.refs_3_.refs_4_.refs_5_ = f32[2,64,512]{2,1,0:T(8,128)S(1)} collective-permute-done((f32[2,64,512]{2,1,0:T(8,128)S(1)}, f32[2,64,512]{2,1,0:T(8,128)S(1)}, u32[]{:S(2)}, u32[]{:S(2)}) %collective-permute-start.3) | collective-permute-done | bytes 262176 | tf_op jit(solution)/shard_map/ppermute | solution.py:479
  19.3 0.0 copy-done.2
  19.3 1.7 %links.1.refs_1_ = f32[2,256,256]{2,1,0:T(8,128)S(1)} custom-call(s32[2,4]{1,0:T(2,128)S(1)} %copy-done.2, f32[2,64,512]{2,1,0:T(8,128)S(1)} %copy-done, f32[2,64,512]{2,1,0:T(8,128)S(1)} %collective-permute-done.refs_0_.refs_2_.refs_3_.refs_4_, f32[2,64,512]{2,1,0:T(8,128)S(1)} %collective-permute-done.3.refs_3_.refs_4_.refs_5_, ...), custom_call_target="tpu_custom_call" | custom-call | bytes 3407872 | tf_op jit(solution)/shard_map/links/pallas_call | solution.py:142
  21.0 0.0 collective-permute-done.2.refs_0_.refs_10_
  21.0 0.6 %segment.1 = (f32[2,256,256]{2,1,0:T(8,128)S(1)}, f32[512,256]{1,0:T(8,128)S(1)}) custom-call(f32[2,64,256]{2,1,0:T(8,128)S(1)} %collective-permute-done.2.refs_0_.refs_10_, f32[2,256,256]{2,1,0:T(8,128)S(1)} %links.1.refs_1_, f32[256,256]{1,0:T(8,128)S(1)} %get-tuple-element.34.refs_2_.refs_3_, f32[256,256]{1,0:T(8,128)S(1)} %get-tuple-element.35.refs_3_.refs_4_), custom_call_target="tpu_custom_call" | custom-call | flops 301989888 | bytes 2228224 | tf_op jit(solution)/shard_map/segment/pallas_call | solution.py:142
  21.6 0.1 collective-permute-start.4
  21.7 1.9 %collective-permute-done.4.refs_1_.refs_7_ = f32[512,256]{1,0:T(8,128)S(1)} collective-permute-done((f32[512,256]{1,0:T(8,128)S(1)}, f32[512,256]{1,0:T(8,128)S(1)}, u32[]{:S(2)}, u32[]{:S(2)}) %collective-permute-start.4) | collective-permute-done | bytes 524320 | tf_op jit(solution)/shard_map/ppermute | solution.py:568
  23.6 0.6 %chip.1 = (f32[256,256]{1,0:T(8,128)S(1)}, f32[256,256]{1,0:T(8,128)S(1)}, f32[160,128]{1,0:T(8,128)S(1)}, f32[128,256]{1,0:T(8,128)S(1)}) custom-call(f32[512,256]{1,0:T(8,128)S(1)} %get-tuple-element.36.refs_0_, f32[512,256]{1,0:T(8,128)S(1)} %collective-permute-done.4.refs_1_.refs_7_), custom_call_target="tpu_custom_call" | custom-call | flops 301989888 | bytes 1785856 | tf_op jit(solution)/shard_map/chip/pallas_call | solution.py:142
  24.2 1.4 %collective-permute-start.5 = (f32[128,256]{1,0:T(8,128)S(1)}, f32[128,256]{1,0:T(8,128)S(1)}, u32[]{:S(2)}, u32[]{:S(2)}) collective-permute-start(f32[128,256]{1,0:T(8,128)S(1)} %get-tuple-element.39), channel_id=1, source_target_pairs={{0,8},{4,12},{8,0},{12,4},{16,24},{20,28},{24,16},{28,20},{1,9},{5... | collective-permute-start | bytes 393224 | tf_op jit(solution)/shard_map/ppermute | solution.py:627
  25.6 0.7 %collective-permute-start.7 = (f32[160,128]{1,0:T(8,128)S(1)}, f32[160,128]{1,0:T(8,128)S(1)}, u32[]{:S(2)}, u32[]{:S(2)}) collective-permute-start(f32[160,128]{1,0:T(8,128)S(1)} %get-tuple-element.40.refs_6_), channel_id=1, source_target_pairs={{0,8},{4,12},{8,0},{12,4},{16,24},{20,28},{24,16},{28,20},{1,9},{5... | collective-permute-start | bytes 245768 | tf_op jit(solution)/shard_map/ppermute | solution.py:621
  26.3 1.5 %maps.1 = (f32[2,256,512]{2,1,0:T(8,128)S(1)}, f32[1,128]{1,0:T(1,128)S(1)}) custom-call(s32[2,4]{1,0:T(2,128)S(1)} %copy-done.2, f32[2,512,512]{2,1,0:T(8,128)S(1)} %get-tuple-element.28.refs_2_.refs_1_.refs_3_, f32[2,64,512]{2,1,0:T(8,128)S(1)} %copy-done, f32[2,64,512]{2,1,0:T(8,128)S(1)} %collective-permute-done.refs_0_.refs_2_.refs_3_.refs_4_, ...), custom_call_target="tpu_custom_call" | custom-call | flops 805306368 | bytes 3932672 | tf_op jit(solution)/shard_map/maps/pallas_call | solution.py:142
  27.8 1.3 %rest.1 = f32[2,64,256]{2,1,0:T(8,128)S(1)} custom-call(s32[2,4]{1,0:T(2,128)S(1)} %copy-done.2, s32[2,4]{1,0:T(2,128)S(1)} %copy-done.1, s32[2,4]{1,0:T(2,128)S(1)} %collective-permute-done.1.refs_1_.refs_3_.refs_2_, f32[2,512,512]{2,1,0:T(8,128)S(1)} %get-tuple-element.28.refs_2_.refs_1_.refs_3_, ...), custom_call_target="tpu_custom_call" | custom-call | flops 201326592 | bytes 2834432 | tf_op jit(solution)/shard_map/rest/pallas_call | solution.py:142
  29.1 0.6 %collective-permute-start.10 = (f32[2,64,256]{2,1,0:T(8,128)S(1)}, f32[2,64,256]{2,1,0:T(8,128)S(1)}, u32[]{:S(2)}, u32[]{:S(2)}) collective-permute-start(f32[2,64,256]{2,1,0:T(8,128)S(1)} %rest.1), channel_id=1, source_target_pairs={{0,1},{1,0},{2,3},{3,2},{4,5},{5,4},{6,7},{7,6},{8,9},{9,8},{10,11... | collective-permute-start | bytes 393224 | tf_op jit(solution)/shard_map/ppermute | solution.py:594
  29.8 0.8 %collective-permute-done.5.refs_2_.refs_12_ = f32[128,256]{1,0:T(8,128)S(1)} collective-permute-done((f32[128,256]{1,0:T(8,128)S(1)}, f32[128,256]{1,0:T(8,128)S(1)}, u32[]{:S(2)}, u32[]{:S(2)}) %collective-permute-start.5) | collective-permute-done | bytes 131104 | tf_op jit(solution)/shard_map/ppermute | solution.py:627
  30.6 0.0 collective-permute-start.6
  30.6 0.9 %collective-permute-done.7 = f32[160,128]{1,0:T(8,128)S(1)} collective-permute-done((f32[160,128]{1,0:T(8,128)S(1)}, f32[160,128]{1,0:T(8,128)S(1)}, u32[]{:S(2)}, u32[]{:S(2)}) %collective-permute-start.7) | collective-permute-done | bytes 81952 | tf_op jit(solution)/shard_map/ppermute | solution.py:621
  31.6 0.1 collective-permute-start.8
  31.7 1.3 %collective-permute-done.8.refs_5_.refs_15_ = f32[160,128]{1,0:T(8,128)S(1)} collective-permute-done((f32[160,128]{1,0:T(8,128)S(1)}, f32[160,128]{1,0:T(8,128)S(1)}, u32[]{:S(2)}, u32[]{:S(2)}) %collective-permute-start.8) | collective-permute-done | bytes 81952 | tf_op jit(solution)/shard_map/ppermute | solution.py:630
  32.9 0.0 collective-permute-done.6.refs_3_.refs_13_
  32.9 0.8 %merge.1 = f32[160,128]{1,0:T(8,128)S(1)} custom-call(f32[256,256]{1,0:T(8,128)S(1)} %get-tuple-element.37.refs_0_, f32[256,256]{1,0:T(8,128)S(1)} %get-tuple-element.38.refs_1_, f32[128,256]{1,0:T(8,128)S(1)} %collective-permute-done.5.refs_2_.refs_12_, f32[128,256]{1,0:T(8,128)S(1)} %collective-permute-done.6.refs_3_.refs_13_, ...), custom_call_target="tpu_custom_call" | custom-call | flops 301989888 | bytes 1032192 | tf_op jit(solution)/shard_map/merge/pallas_call | solution.py:142
  33.7 2.0 %collective-permute-start.9 = (f32[160,128]{1,0:T(8,128)S(1)}, f32[160,128]{1,0:T(8,128)S(1)}, u32[]{:S(2)}, u32[]{:S(2)}) collective-permute-start(f32[160,128]{1,0:T(8,128)S(1)} %merge.1), channel_id=1, source_target_pairs={{0,16},{4,20},{8,24},{12,28},{16,0},{20,4},{24,8},{28,12},{1,17},{... | collective-permute-start | bytes 245768 | tf_op jit(solution)/shard_map/ppermute | solution.py:621
  35.8 0.0 collective-permute-done.10.refs_11_
  35.8 3.0 %prepare.1 = (bf16[384,256]{1,0:T(8,128)(2,1)S(1)}, bf16[384,256]{1,0:T(8,128)(2,1)S(1)}, bf16[2,256,512]{2,1,0:T(8,128)(2,1)S(1)}, bf16[2,256,512]{2,1,0:T(8,12...) custom-call(s32[2,4]{1,0:T(2,128)S(1)} %copy-done.2, s32[2,4]{1,0:T(2,128)S(1)} %copy-done.1, ...), custom_call_target="tpu_custom_call" | custom-call | flops 1459617792 | bytes 7504384 | tf_op jit(solution)/shard_map/prepare/pallas_call | solution.py:142
  38.8 0.0 collective-permute-done.9
  38.9 0.1 collective-permute-start.11
  38.9 1.3 %collective-permute-done.11.refs_1_ = f32[160,128]{1,0:T(8,128)S(1)} collective-permute-done((f32[160,128]{1,0:T(8,128)S(1)}, f32[160,128]{1,0:T(8,128)S(1)}, u32[]{:S(2)}, u32[]{:S(2)}) %collective-permute-start.11) | collective-permute-done | bytes 81952 | tf_op jit(solution)/shard_map/ppermute | solution.py:625
  40.2 1.9 %finish.1 = (f32[2,128,512]{2,1,0:T(8,128)}, f32[2,64,512]{2,1,0:T(8,128)}) custom-call(f32[160,128]{1,0:T(8,128)S(1)} %broadcast_add_fusion.1.refs_0_, f32[160,128]{1,0:T(8,128)S(1)} %collective-permute-done.11.refs_1_, bf16[384,256]{1,0:T(8,128)(2,1)S(1)} %get-tuple-element.47.refs_2_, bf16[384,256]{1,0:T(8,128)(2,1)S(1)} %get-tuple-element.48.refs_3_, ...), custom_call_target="tpu_custom_call" | custom-call | flops 452984832 | bytes 4620288 | tf_op jit(solution)/shard_map/finish/pallas_call | solution.py:142
  (3 shorter events, 0.0 us)
Async XLA Ops:
  0.6 7.9 %copy-start = (f32[2,64,512]{2,1,0:T(8,128)S(1)}, f32[2,64,512]{2,1,0:T(8,128)}, u32[]{:S(2)}) copy-start(f32[2,64,512]{2,1,0:T(8,128)} %refs_2_.3) | copy-start | bytes 786436
  0.6 11.8 %collective-permute-start = (f32[2,64,512]{2,1,0:T(8,128)}, f32[2,64,512]{2,1,0:T(8,128)S(1)}, u32[]{:S(2)}, u32[]{:S(2)}) collective-permute-start(f32[2,64,512]{2,1,0:T(8,128)} %refs_2_.3), channel_id=1, source_target_pairs={{0,1},{1,2},{2,3},{3,0},{4,5},{5,6},{6,7},{7,4},{8,9},{9,10},{10,1... | collective-permute-start | bytes 786440 | tf_op jit(solution)/shard_map/ppermute | solution.py:479
  3.7 4.1 %collective-permute-start.1 = (s32[2,4]{1,0:T(2,128)}, s32[2,4]{1,0:T(2,128)S(1)}, u32[]{:S(2)}, u32[]{:S(2)}) collective-permute-start(s32[2,4]{1,0:T(2,128)} %refs_1_.7), channel_id=1, source_target_pairs={{0,4},{4,8},{8,12},{12,16},{16,20},{20,24},{24,28},{28,0},{1,5},{5... | collective-permute-start | bytes 104 | tf_op jit(solution)/shard_map/ppermute | solution.py:479
  5.4 5.3 %copy-start.1 = (s32[2,4]{1,0:T(2,128)S(1)}, s32[2,4]{1,0:T(2,128)}, u32[]{:S(2)}) copy-start(s32[2,4]{1,0:T(2,128)} %refs_1_.7) | copy-start | bytes 100
  8.5 10.8 %collective-permute-start.3 = (f32[2,64,512]{2,1,0:T(8,128)S(1)}, f32[2,64,512]{2,1,0:T(8,128)S(1)}, u32[]{:S(2)}, u32[]{:S(2)}) collective-permute-start(f32[2,64,512]{2,1,0:T(8,128)S(1)} %broadcast_add_fusion), channel_id=1, source_target_pairs={{0,3},{1,0},{2,1},{3,2},{4,7},{5,4},{6,5},{7,6},{8,11},{9,8},{10,9... | collective-permute-start | bytes 786440 | tf_op jit(solution)/shard_map/ppermute | solution.py:479
  12.8 6.5 %copy-start.2 = (s32[2,4]{1,0:T(2,128)S(1)}, s32[2,4]{1,0:T(2,128)}, u32[]{:S(2)}) copy-start(s32[2,4]{1,0:T(2,128)} %refs_0_.11) | copy-start | bytes 100
  12.8 8.1 %collective-permute-start.2 = (f32[2,64,256]{2,1,0:T(8,128)S(1)}, f32[2,64,256]{2,1,0:T(8,128)S(1)}, u32[]{:S(2)}, u32[]{:S(2)}) collective-permute-start(f32[2,64,256]{2,1,0:T(8,128)S(1)} %chosen.1), channel_id=1, source_target_pairs={{0,1},{1,2},{2,3},{3,0},{4,5},{5,6},{6,7},{7,4},{8,9},{9,10},{10,1... | collective-permute-start | bytes 393224 | tf_op jit(solution)/shard_map/ppermute | solution.py:479
  21.6 2.0 %collective-permute-start.4 = (f32[512,256]{1,0:T(8,128)S(1)}, f32[512,256]{1,0:T(8,128)S(1)}, u32[]{:S(2)}, u32[]{:S(2)}) collective-permute-start(f32[512,256]{1,0:T(8,128)S(1)} %get-tuple-element.36.refs_0_), channel_id=1, source_target_pairs={{0,4},{4,0},{8,12},{12,8},{16,20},{20,16},{24,28},{28,24},{1,5},{5... | collective-permute-start | bytes 1572872 | tf_op jit(solution)/shard_map/ppermute | solution.py:568
  24.2 6.4 %collective-permute-start.5 = (f32[128,256]{1,0:T(8,128)S(1)}, f32[128,256]{1,0:T(8,128)S(1)}, u32[]{:S(2)}, u32[]{:S(2)}) collective-permute-start(f32[128,256]{1,0:T(8,128)S(1)} %get-tuple-element.39), channel_id=1, source_target_pairs={{0,8},{4,12},{8,0},{12,4},{16,24},{20,28},{24,16},{28,20},{1,9},{5... | collective-permute-start | bytes 393224 | tf_op jit(solution)/shard_map/ppermute | solution.py:627
  25.6 6.0 %collective-permute-start.7 = (f32[160,128]{1,0:T(8,128)S(1)}, f32[160,128]{1,0:T(8,128)S(1)}, u32[]{:S(2)}, u32[]{:S(2)}) collective-permute-start(f32[160,128]{1,0:T(8,128)S(1)} %get-tuple-element.40.refs_6_), channel_id=1, source_target_pairs={{0,8},{4,12},{8,0},{12,4},{16,24},{20,28},{24,16},{28,20},{1,9},{5... | collective-permute-start | bytes 245768 | tf_op jit(solution)/shard_map/ppermute | solution.py:621
  29.1 6.6 %collective-permute-start.10 = (f32[2,64,256]{2,1,0:T(8,128)S(1)}, f32[2,64,256]{2,1,0:T(8,128)S(1)}, u32[]{:S(2)}, u32[]{:S(2)}) collective-permute-start(f32[2,64,256]{2,1,0:T(8,128)S(1)} %rest.1), channel_id=1, source_target_pairs={{0,1},{1,0},{2,3},{3,2},{4,5},{5,4},{6,7},{7,6},{8,9},{9,8},{10,11... | collective-permute-start | bytes 393224 | tf_op jit(solution)/shard_map/ppermute | solution.py:594
  30.6 2.3 %collective-permute-start.6 = (f32[128,256]{1,0:T(8,128)S(1)}, f32[128,256]{1,0:T(8,128)S(1)}, u32[]{:S(2)}, u32[]{:S(2)}) collective-permute-start(f32[128,256]{1,0:T(8,128)S(1)} %collective-permute-done.5.refs_2_.refs_12_), channel_id=1, source_target_pairs={{0,4},{4,0},{8,12},{12,8},{16,20},{20,16},{24,28},{28,24},{1,5},{5... | collective-permute-start | bytes 393224 | tf_op jit(solution)/shard_map/ppermute | solution.py:630
  31.6 1.3 %collective-permute-start.8 = (f32[160,128]{1,0:T(8,128)S(1)}, f32[160,128]{1,0:T(8,128)S(1)}, u32[]{:S(2)}, u32[]{:S(2)}) collective-permute-start(f32[160,128]{1,0:T(8,128)S(1)} %broadcast_add_fusion.2.refs_4_.refs_14_), channel_id=1, source_target_pairs={{0,4},{4,0},{8,12},{12,8},{16,20},{20,16},{24,28},{28,24},{1,5},{5... | collective-permute-start | bytes 245768 | tf_op jit(solution)/shard_map/ppermute | solution.py:630
  33.7 5.1 %collective-permute-start.9 = (f32[160,128]{1,0:T(8,128)S(1)}, f32[160,128]{1,0:T(8,128)S(1)}, u32[]{:S(2)}, u32[]{:S(2)}) collective-permute-start(f32[160,128]{1,0:T(8,128)S(1)} %merge.1), channel_id=1, source_target_pairs={{0,16},{4,20},{8,24},{12,28},{16,0},{20,4},{24,8},{28,12},{1,17},{... | collective-permute-start | bytes 245768 | tf_op jit(solution)/shard_map/ppermute | solution.py:621
  38.9 1.3 %collective-permute-start.11 = (f32[160,128]{1,0:T(8,128)S(1)}, f32[160,128]{1,0:T(8,128)S(1)}, u32[]{:S(2)}, u32[]{:S(2)}) collective-permute-start(f32[160,128]{1,0:T(8,128)S(1)} %broadcast_add_fusion.1.refs_0_), channel_id=1, source_target_pairs={{0,4},{4,0},{8,12},{12,8},{16,20},{20,16},{24,28},{28,24},{1,5},{5... | collective-permute-start | bytes 245768 | tf_op jit(solution)/shard_map/ppermute | solution.py:625

commit v17 on v16

--- a/solution.py
+++ b/solution.py
@@ -190,10 +190,10 @@
 
 
 def load_kernel(
-    owners, mask_hbm, fill_hbm, inv_hbm, inv_ref, high_ref, low_ref, keep_ref,
-    mask_ref, fill_ref, sems
+    owners, mask_hbm, fill_hbm, inv_hbm, inv_ref, high_ref, low_ref, *refs
 ):
-    panels, rows, _ = keep_ref.shape
+    keep_refs, (mask_ref, fill_ref, sems) = refs[:-3], refs[-3:]
+    panels, rows, _ = keep_refs[0].shape
     small = [
         pltpu.make_async_copy(fill_hbm, fill_ref, sems.at[panels]),
         pltpu.make_async_copy(mask_hbm, mask_ref, sems.at[panels + 1]),
@@ -206,9 +206,10 @@
     for copy in small:
         copy.wait()
     for p in range(panels):
-        for s, slot in enumerate(slots_of(owners, rows)):
-            ones = jnp.ones((BLOCK, keep_ref.shape[2]), F32)
-            keep_ref[p, s * BLOCK : (s + 1) * BLOCK, :] = kept_rows(mask_ref, p, slot, ones)
+        for block_owners, keep_ref in zip(owners, keep_refs):
+            for s, slot in enumerate(slots_of(block_owners, rows)):
+                ones = jnp.ones((BLOCK, keep_ref.shape[2]), F32)
+                keep_ref[p, s * BLOCK : (s + 1) * BLOCK, :] = kept_rows(mask_ref, p, slot, ones)
     large[-1].wait()
     pick_into(high_ref, low_ref, chosen_of(panels - 1, fill_ref), inv_ref, panels - 1)
     for copy in large[:-1]:
@@ -220,8 +221,11 @@
     pick_into(high_ref, low_ref, chosen_of(panel, *scalar_refs), inv_ref, panel)
 
 
-def prior_kernel(panel, high_ref, low_ref, inv_ref, _, base_ref, own_ref, token_ref):
+def gate_kernel(_, token_ref):
     token_ref[...] = jnp.zeros_like(token_ref)
+
+
+def prior_kernel(panel, high_ref, low_ref, inv_ref, base_ref, own_ref):
     own_cols = own_ref.shape[0]
     own_at = pl.ds(pl.multiple_of(lax.axis_index("row") * own_cols, own_cols), own_cols)
     picked = (high_ref[...], low_ref[...])
@@ -253,14 +257,13 @@
 
 
 def links_kernel(plan, mask_ref, *refs):
-    parts, refs = refs[: len(plan.early)], refs[len(plan.early) :]
-    *pick_refs, links_t_ref, rows_ref = refs
-    rows_ref[...] = jnp.zeros_like(rows_ref)
-    for p in range(links_t_ref.shape[0]):
+    count = len(plan.early) - 1
+    parts, (*pick_refs, links_ref) = refs[:count], refs[count:]
+    links_ref[...] = jnp.zeros_like(links_ref)
+    for p in range(links_ref.shape[0]):
         pick = (pick_refs[2 * p][...], pick_refs[2 * p + 1][...])
-        for owners, part in zip(plan.early, parts):
-            put_rows(mask_ref, p, owners, part[p], rows_ref, lambda kept: mm(kept, pick))
-        links_t_ref[p] = rows_ref[...].T
+        for owners, part in zip(plan.early[:-1], parts):
+            put_rows(mask_ref, p, owners, part[p], links_ref.at[p], lambda kept: mm(kept, pick))
 
 
 def kept_block(mask_ref, panel, owners, part):
@@ -293,15 +296,22 @@
             )
 
 
-def segment_kernel(plan, panels, late_ref, early_ref, *refs):
-    base_refs, (links_t_ref, whole_ref) = refs[:panels], refs[panels:]
+def segment_kernel(plan, panels, early_ref, second_ref, keep_ref, late_ref, *refs):
+    pick_refs, base_refs = refs[: 2 * panels], refs[2 * panels : 3 * panels]
+    links_t_ref, whole_ref, rows_ref = refs[3 * panels :]
     size = links_t_ref.shape[1]
     rows = late_ref.shape[1]
-    here = lax.broadcasted_iota(jnp.int32, (size, size), 1) // rows == at_row(plan.late)
+    second_at, late_at = (
+        pl.ds(pl.multiple_of(at_row(owners) * rows, rows), rows)
+        for owners in (plan.early[-1], plan.late)
+    )
     cov = link_t = None
     for p in range(panels - 1, -1, -1):
-        late_t = jnp.concatenate([late_ref[p]] * (size // rows), 0).T
-        own_t = jnp.where(here, late_t, early_ref[p])
+        pick = (pick_refs[2 * p][...], pick_refs[2 * p + 1][...])
+        rows_ref[p] = early_ref[p]
+        rows_ref[p, second_at, :] = mm(second_ref[p], pick) * keep_ref[p]
+        rows_ref[p, late_at, :] = late_ref[p]
+        own_t = rows_ref[p].T
         links_t_ref[p] = own_t
         if cov is None:
             cov, link_t = base_refs[p][...], own_t
@@ -482,11 +492,12 @@
     short = row_count == 4
     far = row_count // 2
     whose = [tuple((i - d) % row_count for i in range(row_count)) for d in range(row_count)]
-    inv, high, low, keep = call(
-        functools.partial(load_kernel, whose[1] if short else whose[far]),
-        [
-            shape(*inv_diag.shape), pick, pick, shape(panels, rows, chosen_cols),
-        ],
+    came = [d for d in range(row_count) if d != far]
+    plan = Plan(tuple(whose[d] for d in came), whose[far])
+    keeps = shape(panels, rows, chosen_cols)
+    inv, high, low, keep, keep_second = call(
+        functools.partial(load_kernel, (whose[1] if short else whose[far], plan.early[-1])),
+        [shape(*inv_diag.shape), pick, pick, keeps, keeps],
         [],
         [],
         far=[fill_mask, fill_blocks, inv_diag],
@@ -509,24 +520,22 @@
                 [inv],
                 name="pick",
             )
-        base, own_prior, token = call(
+        base, own_prior = call(
             functools.partial(prior_kernel, p),
-            [shape(chosen_cols, chosen_cols), shape(own_cols, width), shape(1, 1, width)],
+            [shape(chosen_cols, chosen_cols), shape(own_cols, width)],
             [],
             [*high_low, inv],
-            anywhere=[prior_fill],
             name="prior",
         )
         picks += high_low
         bases.append(base)
         priors.append(own_prior)
+    (token,) = call(gate_kernel, [shape(1, 1, width)], [], [], anywhere=[prior_fill], name="gate")
     ups, downs = [factor_off], [factor_off + token]
     for _ in range(row_count // 2 - short):
         ups.append(turn(ups[-1], "row", 1))
     for _ in range((row_count - 1) // 2):
         downs.append(turn(downs[-1], "row", -1))
-    came = [d for d in range(row_count) if d != far]
-    plan = Plan(tuple(whose[d] for d in came), whose[far])
     parts = ups[:far] + downs[:0:-1]
     (late,) = call(
         chosen_kernel,
@@ -542,15 +551,15 @@
         functools.partial(links_kernel, plan),
         [shape(panels, size, size)],
         [fill_mask],
-        [*parts, *picks],
-        scratch=[pltpu.VMEM((size, chosen_cols), F32)],
+        [*parts[:-1], *picks],
         name="links",
     )
     links_t, own_whole = call(
         functools.partial(segment_kernel, plan, panels),
         [shape(panels, size, size), shape(2 * size, size)],
         [],
-        [late, links, *bases],
+        [links, parts[-1], keep_second, late, *picks, *bases],
+        scratch=[pltpu.VMEM((panels, size, size), F32)],
         flops=18 * (panels - 1) * size**3,
         name="segment",
     )

time: 42.3 us -> 43.3 us (1.024)
  waiting for transfers between devices: 14.8 us -> 17.3 us
  starting transfers between devices: 10.3 us -> 9.24 us
    ppermute x4, waiting for transfers between devices: 8.55 us -> 10.1 us  [turn(): lax.ppermute(x, axis, [(i, (i + distance) % count) for i in range(count)])]
    ppermute x2, starting transfers between devices: 2.73 us -> 1.34 us  [body(): got = lax.ppermute(send, 'seg', partner)]
    ppermute x1, starting transfers between devices: 1.39 us -> 2.33 us  [body(): got_t = lax.ppermute(send_t, 'seg', partner)]
    ppermute x1, starting transfers between devices: 0.64 us -> 0.07 us  [body(): rest = lax.ppermute(rest, 'row', [(i, i ^ 1) for i in range(row_count)])]
    ppermute x2, waiting for transfers between devices: 0.95 us -> 1.5 us  [body(): got = lax.ppermute(send, 'seg', partner)]
    ppermute x1, waiting for transfers between devices: 0.85 us -> 1.29 us  [body(): got_t = lax.ppermute(send_t, 'seg', partner)]
    pallas_call x13 -> x14, Pallas kernels: 16.2 us -> 15.8 us  [call(): pl.pallas_call(inner, out_shape=[*outs, *(jax.ShapeDtypeStruct(a.shape, a...]
  transfers between devices with their start and end apart: 12 -> 12, of which waited for: 8 -> 10; matrix products, arithmetic and copies ran while one was open for 0% -> 0% of each run, Pallas kernels for 31% -> 28%
where the time goes in v17:
time: 43.3 us; the launch traced here: 43.1 us
  waiting for transfers between devices  17.3 us (40%)
  Pallas kernels  15.8 us (36%)
  starting transfers between devices  9.24 us (21%)
  between operations  0.8 us (2%)
    pallas_call x14, Pallas kernels, call(): pl.pallas_call(inner, out_shape=[*outs, *(jax.ShapeDtypeStruct(a.shape, a...  15.8 us
    ppermute x4, waiting for transfers between devices, turn(): lax.ppermute(x, axis, [(i, (i + distance) % count) for i in range(count)])  10.1 us
    ppermute x4, starting transfers between devices, turn(): lax.ppermute(x, axis, [(i, (i + distance) % count) for i in range(count)])  5.28 us
    ppermute x1, starting transfers between devices, body(): got_t = lax.ppermute(send_t, 'seg', partner)  2.33 us
    ppermute x1, waiting for transfers between devices, body(): other_whole = lax.ppermute(own_whole, 'seg', swap)  1.9 us
    ppermute x2, waiting for transfers between devices, body(): got = lax.ppermute(send, 'seg', partner)  1.5 us
    ppermute x2, starting transfers between devices, body(): got = lax.ppermute(send, 'seg', partner)  1.34 us
    ppermute x1, waiting for transfers between devices, body(): got_t = lax.ppermute(send_t, 'seg', partner)  1.29 us
  transfers between devices with their start and end apart: 12, of which 10 were waited for; matrix products, arithmetic and copies ran while one was open for 0% of the time, Pallas kernels for 28%

profile of v17, /device:TPU:0, one launch (start us, length us, event | category | flops | bytes accessed | tf_op | source)
XLA Modules:
  0.0 43.1 jit_solution(10460382111998250066)
XLA Ops:
  0.6 0.0 copy-start
  0.6 0.0 copy-start.1
  0.6 3.1 %collective-permute-start = (f32[2,64,512]{2,1,0:T(8,128)}, f32[2,64,512]{2,1,0:T(8,128)S(1)}, u32[]{:S(2)}, u32[]{:S(2)}) collective-permute-start(f32[2,64,512]{2,1,0:T(8,128)} %refs_2_.3), channel_id=1, source_target_pairs={{0,1},{1,2},{2,3},{3,0},{4,5},{5,6},{6,7},{7,4},{8,9},{9,10},{10,1... | collective-permute-start | bytes 786440 | tf_op jit(solution)/shard_map/ppermute | solution.py:489
  3.7 0.0 collective-permute-start.1
  3.7 1.6 %load.1 = (f32[2,512,512]{2,1,0:T(8,128)S(1)}, bf16[512,256]{1,0:T(8,128)(2,1)S(1)}, bf16[512,256]{1,0:T(8,128)(2,1)S(1)}, f32[2,64,256]{2,1,0:T(8,128)S(1)}, f32[2,64,256]{2,1,0:T(8,128)S(1)}) custom-call(s32[2,4]{1,0:T(2,128)} %refs_0_.11, s32[2,4]{1,0:T(2,128)} %refs_1_.7, f32[2,512,512]{2,1,0:T(8,128)} %refs_2_.2), custom_call_target="tpu_custom_call" | custom-call | bytes 5505088 | tf_op jit(solution)/shard_map/load/pallas_call | solution.py:142
  5.4 2.5 %collective-permute-done.1.refs_1_.refs_0_.refs_2_ = s32[2,4]{1,0:T(2,128)S(1)} collective-permute-done((s32[2,4]{1,0:T(2,128)}, s32[2,4]{1,0:T(2,128)S(1)}, u32[]{:S(2)}, u32[]{:S(2)}) %collective-permute-start.1) | collective-permute-done | bytes 64 | tf_op jit(solution)/shard_map/ppermute | solution.py:489
  7.8 0.0 copy-done
  7.9 2.1 %collective-permute-start.2 = (f32[2,64,512]{2,1,0:T(8,128)S(1)}, f32[2,64,512]{2,1,0:T(8,128)S(1)}, u32[]{:S(2)}, u32[]{:S(2)}) collective-permute-start(f32[2,64,512]{2,1,0:T(8,128)S(1)} %broadcast_add_fusion), channel_id=1, source_target_pairs={{0,3},{1,0},{2,1},{3,2},{4,7},{5,4},{6,5},{7,6},{8,11},{9,8},{10,9... | collective-permute-start | bytes 786440 | tf_op jit(solution)/shard_map/ppermute | solution.py:489
  10.0 0.0 copy-done.1
  10.0 0.9 %pick.1 = (bf16[512,256]{1,0:T(8,128)(2,1)S(1)}, bf16[512,256]{1,0:T(8,128)(2,1)S(1)}) custom-call(s32[2,4]{1,0:T(2,128)S(1)} %copy-done.1, s32[2,4]{1,0:T(2,128)S(1)} %collective-permute-done.1.refs_1_.refs_0_.refs_2_, f32[2,512,512]{2,1,0:T(8,128)S(1)} %get-tuple-element.27.refs_2_.refs_1_.refs_3_), custom_call_target="tpu_custom_call" | custom-call | bytes 3145728 | tf_op jit(solution)/shard_map/pick/pallas_call | solution.py:142
  11.0 1.8 %collective-permute-done.refs_2_.refs_0_.refs_3_.refs_4_ = f32[2,64,512]{2,1,0:T(8,128)S(1)} collective-permute-done((f32[2,64,512]{2,1,0:T(8,128)}, f32[2,64,512]{2,1,0:T(8,128)S(1)}, u32[]{:S(2)}, u32[]{:S(2)}) %collective-permute-start) | collective-permute-done | bytes 262176 | tf_op jit(solution)/shard_map/ppermute | solution.py:489
  12.8 0.4 chosen.1
  13.2 0.0 copy-start.2
  13.2 0.1 collective-permute-start.3
  13.2 0.7 %prior.3 = (f32[256,256]{1,0:T(8,128)S(1)}, f32[128,512]{1,0:T(8,128)S(1)}) custom-call(bf16[512,256]{1,0:T(8,128)(2,1)S(1)} %get-tuple-element.30.refs_5_.refs_4_.refs_0_.refs_6_, bf16[512,256]{1,0:T(8,128)(2,1)S(1)} %get-tuple-element.31.refs_6_.refs_5_.refs_1_.refs_7_, f32[2,512,512]{2,1,0:T(8,128)S(1)} %get-tuple-element.27.refs_2_.refs_1_.refs_3_), custom_call_target="tpu_custom_call" | custom-call | bytes 3670016 | tf_op jit(solution)/shard_map/prior/pallas_call | solution.py:142
  13.9 0.7 %prior.2 = (f32[256,256]{1,0:T(8,128)S(1)}, f32[128,512]{1,0:T(8,128)S(1)}) custom-call(bf16[512,256]{1,0:T(8,128)(2,1)S(1)} %get-tuple-element.28.refs_3_.refs_2_.refs_0_.refs_4_, bf16[512,256]{1,0:T(8,128)(2,1)S(1)} %get-tuple-element.29.refs_4_.refs_3_.refs_1_.refs_5_, f32[2,512,512]{2,1,0:T(8,128)S(1)} %get-tuple-element.27.refs_2_.refs_1_.refs_3_), custom_call_target="tpu_custom_call" | custom-call | bytes 3670016 | tf_op jit(solution)/shard_map/prior/pallas_call | solution.py:142
  14.6 0.0 copy-done.2
  14.6 1.2 %links.1.refs_0_ = f32[2,256,256]{2,1,0:T(8,128)S(1)} custom-call(s32[2,4]{1,0:T(2,128)S(1)} %copy-done.2, f32[2,64,512]{2,1,0:T(8,128)S(1)} %copy-done, f32[2,64,512]{2,1,0:T(8,128)S(1)} %collective-permute-done.refs_2_.refs_0_.refs_3_.refs_4_, bf16[512,256]{1,0:T(8,128)(2,1)S(1)} %get-tuple-element.28.refs_3_.refs_2_.refs_0_.refs_4_, ...), custom_call_target="tpu_custom_call" | custom-call | bytes 3145728 | tf_op jit(solution)/shard_map/links/pallas_call | solution.py:142
  15.8 3.4 %collective-permute-done.2.refs_1_.refs_4_.refs_5_ = f32[2,64,512]{2,1,0:T(8,128)S(1)} collective-permute-done((f32[2,64,512]{2,1,0:T(8,128)S(1)}, f32[2,64,512]{2,1,0:T(8,128)S(1)}, u32[]{:S(2)}, u32[]{:S(2)}) %collective-permute-start.2) | collective-permute-done | bytes 262176 | tf_op jit(solution)/shard_map/ppermute | solution.py:489
  19.2 2.4 %collective-permute-done.3.refs_3_.refs_10_ = f32[2,64,256]{2,1,0:T(8,128)S(1)} collective-permute-done((f32[2,64,256]{2,1,0:T(8,128)S(1)}, f32[2,64,256]{2,1,0:T(8,128)S(1)}, u32[]{:S(2)}, u32[]{:S(2)}) %collective-permute-start.3) | collective-permute-done | bytes 131104 | tf_op jit(solution)/shard_map/ppermute | solution.py:489
  21.6 1.1 %segment.1 = (f32[2,256,256]{2,1,0:T(8,128)S(1)}, f32[512,256]{1,0:T(8,128)S(1)}) custom-call(f32[2,256,256]{2,1,0:T(8,128)S(1)} %links.1.refs_0_, f32[2,64,512]{2,1,0:T(8,128)S(1)} %collective-permute-done.2.refs_1_.refs_4_.refs_5_, f32[2,64,256]{2,1,0:T(8,128)S(1)} %get-tuple-element.32.refs_2_, f32[2,64,256]{2,1,0:T(8,128)S(1)} %collective-permute-done.3.refs_3_.refs_10_, ...), custom_call_target="tpu_custom_call" | custom-call | flops 301989888 | bytes 4718592 | tf_op jit(solution)/shard_map/segment/pallas_call | solution.py:142
  22.7 0.1 collective-permute-start.4
  22.8 1.9 %collective-permute-done.4.refs_1_.refs_7_ = f32[512,256]{1,0:T(8,128)S(1)} collective-permute-done((f32[512,256]{1,0:T(8,128)S(1)}, f32[512,256]{1,0:T(8,128)S(1)}, u32[]{:S(2)}, u32[]{:S(2)}) %collective-permute-start.4) | collective-permute-done | bytes 524320 | tf_op jit(solution)/shard_map/ppermute | solution.py:577
  24.7 0.6 %chip.1 = (f32[256,256]{1,0:T(8,128)S(1)}, f32[256,256]{1,0:T(8,128)S(1)}, f32[160,128]{1,0:T(8,128)S(1)}, f32[128,256]{1,0:T(8,128)S(1)}) custom-call(f32[512,256]{1,0:T(8,128)S(1)} %get-tuple-element.36.refs_0_, f32[512,256]{1,0:T(8,128)S(1)} %collective-permute-done.4.refs_1_.refs_7_), custom_call_target="tpu_custom_call" | custom-call | flops 301989888 | bytes 1785856 | tf_op jit(solution)/shard_map/chip/pallas_call | solution.py:142
  25.3 2.3 %collective-permute-start.5 = (f32[128,256]{1,0:T(8,128)S(1)}, f32[128,256]{1,0:T(8,128)S(1)}, u32[]{:S(2)}, u32[]{:S(2)}) collective-permute-start(f32[128,256]{1,0:T(8,128)S(1)} %get-tuple-element.39), channel_id=1, source_target_pairs={{0,8},{4,12},{8,0},{12,4},{16,24},{20,28},{24,16},{28,20},{1,9},{5... | collective-permute-start | bytes 393224 | tf_op jit(solution)/shard_map/ppermute | solution.py:636
  27.6 0.1 collective-permute-start.7
  27.7 1.5 %maps.1 = (f32[2,256,512]{2,1,0:T(8,128)S(1)}, f32[1,128]{1,0:T(1,128)S(1)}) custom-call(s32[2,4]{1,0:T(2,128)S(1)} %copy-done.2, f32[2,512,512]{2,1,0:T(8,128)S(1)} %get-tuple-element.27.refs_2_.refs_1_.refs_3_, f32[2,64,512]{2,1,0:T(8,128)S(1)} %copy-done, f32[2,64,512]{2,1,0:T(8,128)S(1)} %collective-permute-done.refs_2_.refs_0_.refs_3_.refs_4_, ...), custom_call_target="tpu_custom_call" | custom-call | flops 805306368 | bytes 3932672 | tf_op jit(solution)/shard_map/maps/pallas_call | solution.py:142
  29.2 1.3 %rest.1 = f32[2,64,256]{2,1,0:T(8,128)S(1)} custom-call(s32[2,4]{1,0:T(2,128)S(1)} %copy-done.2, s32[2,4]{1,0:T(2,128)S(1)} %copy-done.1, s32[2,4]{1,0:T(2,128)S(1)} %collective-permute-done.1.refs_1_.refs_0_.refs_2_, f32[2,512,512]{2,1,0:T(8,128)S(1)} %get-tuple-element.27.refs_2_.refs_1_.refs_3_, ...), custom_call_target="tpu_custom_call" | custom-call | flops 201326592 | bytes 2834432 | tf_op jit(solution)/shard_map/rest/pallas_call | solution.py:142
  30.5 0.1 collective-permute-start.10
  30.6 1.3 %collective-permute-done.5.refs_2_.refs_12_ = f32[128,256]{1,0:T(8,128)S(1)} collective-permute-done((f32[128,256]{1,0:T(8,128)S(1)}, f32[128,256]{1,0:T(8,128)S(1)}, u32[]{:S(2)}, u32[]{:S(2)}) %collective-permute-start.5) | collective-permute-done | bytes 131104 | tf_op jit(solution)/shard_map/ppermute | solution.py:636
  31.9 0.0 collective-permute-start.6
  31.9 1.3 %collective-permute-done.7 = f32[160,128]{1,0:T(8,128)S(1)} collective-permute-done((f32[160,128]{1,0:T(8,128)S(1)}, f32[160,128]{1,0:T(8,128)S(1)}, u32[]{:S(2)}, u32[]{:S(2)}) %collective-permute-start.7) | collective-permute-done | bytes 81952 | tf_op jit(solution)/shard_map/ppermute | solution.py:630
  33.2 0.1 collective-permute-start.8
  33.3 1.3 %collective-permute-done.8.refs_5_.refs_15_ = f32[160,128]{1,0:T(8,128)S(1)} collective-permute-done((f32[160,128]{1,0:T(8,128)S(1)}, f32[160,128]{1,0:T(8,128)S(1)}, u32[]{:S(2)}, u32[]{:S(2)}) %collective-permute-start.8) | collective-permute-done | bytes 81952 | tf_op jit(solution)/shard_map/ppermute | solution.py:639
  34.5 0.0 collective-permute-done.6.refs_3_.refs_13_
  34.5 0.8 %merge.1 = f32[160,128]{1,0:T(8,128)S(1)} custom-call(f32[256,256]{1,0:T(8,128)S(1)} %get-tuple-element.37.refs_0_, f32[256,256]{1,0:T(8,128)S(1)} %get-tuple-element.38.refs_1_, f32[128,256]{1,0:T(8,128)S(1)} %collective-permute-done.5.refs_2_.refs_12_, f32[128,256]{1,0:T(8,128)S(1)} %collective-permute-done.6.refs_3_.refs_13_, ...), custom_call_target="tpu_custom_call" | custom-call | flops 301989888 | bytes 1032192 | tf_op jit(solution)/shard_map/merge/pallas_call | solution.py:142
  35.3 1.3 %collective-permute-start.9 = (f32[160,128]{1,0:T(8,128)S(1)}, f32[160,128]{1,0:T(8,128)S(1)}, u32[]{:S(2)}, u32[]{:S(2)}) collective-permute-start(f32[160,128]{1,0:T(8,128)S(1)} %merge.1), channel_id=1, source_target_pairs={{0,16},{4,20},{8,24},{12,28},{16,0},{20,4},{24,8},{28,12},{1,17},{... | collective-permute-start | bytes 245768 | tf_op jit(solution)/shard_map/ppermute | solution.py:630
  36.6 0.0 collective-permute-done.10.refs_11_
  36.6 3.1 %prepare.1 = (bf16[384,256]{1,0:T(8,128)(2,1)S(1)}, bf16[384,256]{1,0:T(8,128)(2,1)S(1)}, bf16[2,256,512]{2,1,0:T(8,128)(2,1)S(1)}, bf16[2,256,512]{2,1,0:T(8,12...) custom-call(s32[2,4]{1,0:T(2,128)S(1)} %copy-done.2, s32[2,4]{1,0:T(2,128)S(1)} %copy-done.1, ...), custom_call_target="tpu_custom_call" | custom-call | flops 1459617792 | bytes 7504384 | tf_op jit(solution)/shard_map/prepare/pallas_call | solution.py:142
  39.7 0.2 collective-permute-done.9
  39.9 0.1 collective-permute-start.11
  40.0 1.3 %collective-permute-done.11.refs_1_ = f32[160,128]{1,0:T(8,128)S(1)} collective-permute-done((f32[160,128]{1,0:T(8,128)S(1)}, f32[160,128]{1,0:T(8,128)S(1)}, u32[]{:S(2)}, u32[]{:S(2)}) %collective-permute-start.11) | collective-permute-done | bytes 81952 | tf_op jit(solution)/shard_map/ppermute | solution.py:634
  41.3 1.9 %finish.1 = (f32[2,128,512]{2,1,0:T(8,128)}, f32[2,64,512]{2,1,0:T(8,128)}) custom-call(f32[160,128]{1,0:T(8,128)S(1)} %broadcast_add_fusion.1.refs_0_, f32[160,128]{1,0:T(8,128)S(1)} %collective-permute-done.11.refs_1_, bf16[384,256]{1,0:T(8,128)(2,1)S(1)} %get-tuple-element.47.refs_2_, bf16[384,256]{1,0:T(8,128)(2,1)S(1)} %get-tuple-element.48.refs_3_, ...), custom_call_target="tpu_custom_call" | custom-call | flops 452984832 | bytes 4620288 | tf_op jit(solution)/shard_map/finish/pallas_call | solution.py:142
  (4 shorter events, 0.0 us)
Async XLA Ops:
  0.6 7.2 %copy-start = (f32[2,64,512]{2,1,0:T(8,128)S(1)}, f32[2,64,512]{2,1,0:T(8,128)}, u32[]{:S(2)}) copy-start(f32[2,64,512]{2,1,0:T(8,128)} %refs_2_.3) | copy-start | bytes 786436
  0.6 9.4 %copy-start.1 = (s32[2,4]{1,0:T(2,128)S(1)}, s32[2,4]{1,0:T(2,128)}, u32[]{:S(2)}) copy-start(s32[2,4]{1,0:T(2,128)} %refs_1_.7) | copy-start | bytes 100
  0.6 12.1 %collective-permute-start = (f32[2,64,512]{2,1,0:T(8,128)}, f32[2,64,512]{2,1,0:T(8,128)S(1)}, u32[]{:S(2)}, u32[]{:S(2)}) collective-permute-start(f32[2,64,512]{2,1,0:T(8,128)} %refs_2_.3), channel_id=1, source_target_pairs={{0,1},{1,2},{2,3},{3,0},{4,5},{5,6},{6,7},{7,4},{8,9},{9,10},{10,1... | collective-permute-start | bytes 786440 | tf_op jit(solution)/shard_map/ppermute | solution.py:489
  3.7 4.1 %collective-permute-start.1 = (s32[2,4]{1,0:T(2,128)}, s32[2,4]{1,0:T(2,128)S(1)}, u32[]{:S(2)}, u32[]{:S(2)}) collective-permute-start(s32[2,4]{1,0:T(2,128)} %refs_1_.7), channel_id=1, source_target_pairs={{0,4},{4,8},{8,12},{12,16},{16,20},{20,24},{24,28},{28,0},{1,5},{5... | collective-permute-start | bytes 104 | tf_op jit(solution)/shard_map/ppermute | solution.py:489
  7.9 11.3 %collective-permute-start.2 = (f32[2,64,512]{2,1,0:T(8,128)S(1)}, f32[2,64,512]{2,1,0:T(8,128)S(1)}, u32[]{:S(2)}, u32[]{:S(2)}) collective-permute-start(f32[2,64,512]{2,1,0:T(8,128)S(1)} %broadcast_add_fusion), channel_id=1, source_target_pairs={{0,3},{1,0},{2,1},{3,2},{4,7},{5,4},{6,5},{7,6},{8,11},{9,8},{10,9... | collective-permute-start | bytes 786440 | tf_op jit(solution)/shard_map/ppermute | solution.py:489
  13.2 1.4 %copy-start.2 = (s32[2,4]{1,0:T(2,128)S(1)}, s32[2,4]{1,0:T(2,128)}, u32[]{:S(2)}) copy-start(s32[2,4]{1,0:T(2,128)} %refs_0_.11) | copy-start | bytes 100
  13.2 8.4 %collective-permute-start.3 = (f32[2,64,256]{2,1,0:T(8,128)S(1)}, f32[2,64,256]{2,1,0:T(8,128)S(1)}, u32[]{:S(2)}, u32[]{:S(2)}) collective-permute-start(f32[2,64,256]{2,1,0:T(8,128)S(1)} %chosen.1), channel_id=1, source_target_pairs={{0,1},{1,2},{2,3},{3,0},{4,5},{5,6},{6,7},{7,4},{8,9},{9,10},{10,1... | collective-permute-start | bytes 393224 | tf_op jit(solution)/shard_map/ppermute | solution.py:489
  22.7 2.0 %collective-permute-start.4 = (f32[512,256]{1,0:T(8,128)S(1)}, f32[512,256]{1,0:T(8,128)S(1)}, u32[]{:S(2)}, u32[]{:S(2)}) collective-permute-start(f32[512,256]{1,0:T(8,128)S(1)} %get-tuple-element.36.refs_0_), channel_id=1, source_target_pairs={{0,4},{4,0},{8,12},{12,8},{16,20},{20,16},{24,28},{28,24},{1,5},{5... | collective-permute-start | bytes 1572872 | tf_op jit(solution)/shard_map/ppermute | solution.py:577
  25.3 6.6 %collective-permute-start.5 = (f32[128,256]{1,0:T(8,128)S(1)}, f32[128,256]{1,0:T(8,128)S(1)}, u32[]{:S(2)}, u32[]{:S(2)}) collective-permute-start(f32[128,256]{1,0:T(8,128)S(1)} %get-tuple-element.39), channel_id=1, source_target_pairs={{0,8},{4,12},{8,0},{12,4},{16,24},{20,28},{24,16},{28,20},{1,9},{5... | collective-permute-start | bytes 393224 | tf_op jit(solution)/shard_map/ppermute | solution.py:636
  27.6 5.6 %collective-permute-start.7 = (f32[160,128]{1,0:T(8,128)S(1)}, f32[160,128]{1,0:T(8,128)S(1)}, u32[]{:S(2)}, u32[]{:S(2)}) collective-permute-start(f32[160,128]{1,0:T(8,128)S(1)} %get-tuple-element.40.refs_6_), channel_id=1, source_target_pairs={{0,8},{4,12},{8,0},{12,4},{16,24},{20,28},{24,16},{28,20},{1,9},{5... | collective-permute-start | bytes 245768 | tf_op jit(solution)/shard_map/ppermute | solution.py:630
  30.5 6.1 %collective-permute-start.10 = (f32[2,64,256]{2,1,0:T(8,128)S(1)}, f32[2,64,256]{2,1,0:T(8,128)S(1)}, u32[]{:S(2)}, u32[]{:S(2)}) collective-permute-start(f32[2,64,256]{2,1,0:T(8,128)S(1)} %rest.1), channel_id=1, source_target_pairs={{0,1},{1,0},{2,3},{3,2},{4,5},{5,4},{6,7},{7,6},{8,9},{9,8},{10,11... | collective-permute-start | bytes 393224 | tf_op jit(solution)/shard_map/ppermute | solution.py:603
  31.9 2.6 %collective-permute-start.6 = (f32[128,256]{1,0:T(8,128)S(1)}, f32[128,256]{1,0:T(8,128)S(1)}, u32[]{:S(2)}, u32[]{:S(2)}) collective-permute-start(f32[128,256]{1,0:T(8,128)S(1)} %collective-permute-done.5.refs_2_.refs_12_), channel_id=1, source_target_pairs={{0,4},{4,0},{8,12},{12,8},{16,20},{20,16},{24,28},{28,24},{1,5},{5... | collective-permute-start | bytes 393224 | tf_op jit(solution)/shard_map/ppermute | solution.py:639
  33.2 1.3 %collective-permute-start.8 = (f32[160,128]{1,0:T(8,128)S(1)}, f32[160,128]{1,0:T(8,128)S(1)}, u32[]{:S(2)}, u32[]{:S(2)}) collective-permute-start(f32[160,128]{1,0:T(8,128)S(1)} %broadcast_add_fusion.2.refs_4_.refs_14_), channel_id=1, source_target_pairs={{0,4},{4,0},{8,12},{12,8},{16,20},{20,16},{24,28},{28,24},{1,5},{5... | collective-permute-start | bytes 245768 | tf_op jit(solution)/shard_map/ppermute | solution.py:639
  35.3 4.6 %collective-permute-start.9 = (f32[160,128]{1,0:T(8,128)S(1)}, f32[160,128]{1,0:T(8,128)S(1)}, u32[]{:S(2)}, u32[]{:S(2)}) collective-permute-start(f32[160,128]{1,0:T(8,128)S(1)} %merge.1), channel_id=1, source_target_pairs={{0,16},{4,20},{8,24},{12,28},{16,0},{20,4},{24,8},{28,12},{1,17},{... | collective-permute-start | bytes 245768 | tf_op jit(solution)/shard_map/ppermute | solution.py:630
  39.9 1.3 %collective-permute-start.11 = (f32[160,128]{1,0:T(8,128)S(1)}, f32[160,128]{1,0:T(8,128)S(1)}, u32[]{:S(2)}, u32[]{:S(2)}) collective-permute-start(f32[160,128]{1,0:T(8,128)S(1)} %broadcast_add_fusion.1.refs_0_), channel_id=1, source_target_pairs={{0,4},{4,0},{8,12},{12,8},{16,20},{20,16},{24,28},{28,24},{1,5},{5... | collective-permute-start | bytes 245768 | tf_op jit(solution)/shard_map/ppermute | solution.py:634

commit v18 on v17

--- a/solution.py
+++ b/solution.py
@@ -221,11 +221,8 @@
     pick_into(high_ref, low_ref, chosen_of(panel, *scalar_refs), inv_ref, panel)
 
 
-def gate_kernel(_, token_ref):
+def prior_kernel(panel, high_ref, low_ref, inv_ref, _, base_ref, own_ref, token_ref):
     token_ref[...] = jnp.zeros_like(token_ref)
-
-
-def prior_kernel(panel, high_ref, low_ref, inv_ref, base_ref, own_ref):
     own_cols = own_ref.shape[0]
     own_at = pl.ds(pl.multiple_of(lax.axis_index("row") * own_cols, own_cols), own_cols)
     picked = (high_ref[...], low_ref[...])
@@ -296,9 +293,8 @@
             )
 
 
-def segment_kernel(plan, panels, early_ref, second_ref, keep_ref, late_ref, *refs):
-    pick_refs, base_refs = refs[: 2 * panels], refs[2 * panels : 3 * panels]
-    links_t_ref, whole_ref, rows_ref = refs[3 * panels :]
+def segment_kernel(plan, panels, early_ref, second_ref, late_ref, *refs):
+    base_refs, (links_t_ref, whole_ref, rows_ref) = refs[:panels], refs[panels:]
     size = links_t_ref.shape[1]
     rows = late_ref.shape[1]
     second_at, late_at = (
@@ -307,9 +303,8 @@
     )
     cov = link_t = None
     for p in range(panels - 1, -1, -1):
-        pick = (pick_refs[2 * p][...], pick_refs[2 * p + 1][...])
         rows_ref[p] = early_ref[p]
-        rows_ref[p, second_at, :] = mm(second_ref[p], pick) * keep_ref[p]
+        rows_ref[p, second_at, :] = second_ref[p]
         rows_ref[p, late_at, :] = late_ref[p]
         own_t = rows_ref[p].T
         links_t_ref[p] = own_t
@@ -520,17 +515,17 @@
                 [inv],
                 name="pick",
             )
-        base, own_prior = call(
+        base, own_prior, token = call(
             functools.partial(prior_kernel, p),
-            [shape(chosen_cols, chosen_cols), shape(own_cols, width)],
+            [shape(chosen_cols, chosen_cols), shape(own_cols, width), shape(1, 1, width)],
             [],
             [*high_low, inv],
+            anywhere=[prior_fill],
             name="prior",
         )
         picks += high_low
         bases.append(base)
         priors.append(own_prior)
-    (token,) = call(gate_kernel, [shape(1, 1, width)], [], [], anywhere=[prior_fill], name="gate")
     ups, downs = [factor_off], [factor_off + token]
     for _ in range(row_count // 2 - short):
         ups.append(turn(ups[-1], "row", 1))
@@ -554,11 +549,18 @@
         [*parts[:-1], *picks],
         name="links",
     )
+    (second,) = call(
+        chosen_kernel,
+        [shape(panels, rows, chosen_cols)],
+        [],
+        [parts[-1], keep_second, *picks],
+        name="second",
+    )
     links_t, own_whole = call(
         functools.partial(segment_kernel, plan, panels),
         [shape(panels, size, size), shape(2 * size, size)],
         [],
-        [links, parts[-1], keep_second, late, *picks, *bases],
+        [links, second, late, *bases],
         scratch=[pltpu.VMEM((panels, size, size), F32)],
         flops=18 * (panels - 1) * size**3,
         name="segment",

time: 43.3 us -> 42.3 us (0.977)
  waiting for transfers between devices: 17.3 us -> 15 us
  starting transfers between devices: 9.24 us -> 10.1 us
    ppermute x4, waiting for transfers between devices: 10.1 us -> 8.44 us  [turn(): lax.ppermute(x, axis, [(i, (i + distance) % count) for i in range(count)])]
    ppermute x2, starting transfers between devices: 1.34 us -> 2.71 us  [body(): got = lax.ppermute(send, 'seg', partner)]
    ppermute x1, starting transfers between devices: 2.33 us -> 1.59 us  [body(): got_t = lax.ppermute(send_t, 'seg', partner)]
    ppermute x2, waiting for transfers between devices: 1.5 us -> 0.95 us  [body(): got = lax.ppermute(send, 'seg', partner)]
    pallas_call x14, Pallas kernels: 15.8 us -> 16.2 us  [call(): pl.pallas_call(inner, out_shape=[*outs, *(jax.ShapeDtypeStruct(a.shape, a...]
  transfers between devices with their start and end apart: 12 -> 12, of which waited for: 10 -> 9; matrix products, arithmetic and copies ran while one was open for 0% -> 0% of each run, Pallas kernels for 28% -> 31%
where the time goes in v18:
time: 42.3 us; the launch traced here: 42.2 us
  Pallas kernels  16.2 us (38%)
  waiting for transfers between devices  15 us (35%)
  starting transfers between devices  10.1 us (24%)
  between operations  0.81 us (2%)
    pallas_call x14, Pallas kernels, call(): pl.pallas_call(inner, out_shape=[*outs, *(jax.ShapeDtypeStruct(a.shape, a...  16.2 us
    ppermute x4, waiting for transfers between devices, turn(): lax.ppermute(x, axis, [(i, (i + distance) % count) for i in range(count)])  8.44 us
    ppermute x4, starting transfers between devices, turn(): lax.ppermute(x, axis, [(i, (i + distance) % count) for i in range(count)])  5.29 us
    ppermute x2, starting transfers between devices, body(): got = lax.ppermute(send, 'seg', partner)  2.71 us
    ppermute x1, waiting for transfers between devices, body(): other_whole = lax.ppermute(own_whole, 'seg', swap)  1.9 us
    ppermute x1, starting transfers between devices, body(): got_t = lax.ppermute(send_t, 'seg', partner)  1.59 us
    ppermute x1, waiting for transfers between devices, body(): after = (got, lax.ppermute(got, 'seg', swap))  1.26 us
    ppermute x1, waiting for transfers between devices, body(): lax.ppermute(got, 'seg', swap)  1.26 us
  transfers between devices with their start and end apart: 12, of which 9 were waited for; matrix products, arithmetic and copies ran while one was open for 0% of the time, Pallas kernels for 31%

profile of v18, /device:TPU:0, one launch (start us, length us, event | category | flops | bytes accessed | tf_op | source)
XLA Modules:
  0.0 42.2 jit_solution(15961220979339222031)
XLA Ops:
  0.6 0.0 copy-start
  0.6 3.1 %collective-permute-start = (f32[2,64,512]{2,1,0:T(8,128)}, f32[2,64,512]{2,1,0:T(8,128)S(1)}, u32[]{:S(2)}, u32[]{:S(2)}) collective-permute-start(f32[2,64,512]{2,1,0:T(8,128)} %refs_2_.3), channel_id=1, source_target_pairs={{0,1},{1,2},{2,3},{3,0},{4,5},{5,6},{6,7},{7,4},{8,9},{9,10},{10,1... | collective-permute-start | bytes 786440 | tf_op jit(solution)/shard_map/ppermute | solution.py:484
  3.7 0.0 collective-permute-start.1
  3.7 1.6 %load.1 = (f32[2,512,512]{2,1,0:T(8,128)S(1)}, bf16[512,256]{1,0:T(8,128)(2,1)S(1)}, bf16[512,256]{1,0:T(8,128)(2,1)S(1)}, f32[2,64,256]{2,1,0:T(8,128)S(1)}, f32[2,64,256]{2,1,0:T(8,128)S(1)}) custom-call(s32[2,4]{1,0:T(2,128)} %refs_0_.11, s32[2,4]{1,0:T(2,128)} %refs_1_.7, f32[2,512,512]{2,1,0:T(8,128)} %refs_2_.2), custom_call_target="tpu_custom_call" | custom-call | bytes 5505088 | tf_op jit(solution)/shard_map/load/pallas_call | solution.py:142
  5.4 0.0 copy-start.1
  5.4 2.4 %collective-permute-done.1.refs_1_.refs_3_.refs_2_ = s32[2,4]{1,0:T(2,128)S(1)} collective-permute-done((s32[2,4]{1,0:T(2,128)}, s32[2,4]{1,0:T(2,128)S(1)}, u32[]{:S(2)}, u32[]{:S(2)}) %collective-permute-start.1) | collective-permute-done | bytes 64 | tf_op jit(solution)/shard_map/ppermute | solution.py:484
  7.8 0.7 %prior.2 = (f32[256,256]{1,0:T(8,128)S(1)}, f32[128,512]{1,0:T(8,128)S(1)}, f32[1,1,512]{2,1,0:T(1,128)S(1)}) custom-call(bf16[512,256]{1,0:T(8,128)(2,1)S(1)} %get-tuple-element.31.refs_5_.refs_0_.refs_4_, bf16[512,256]{1,0:T(8,128)(2,1)S(1)} %get-tuple-element.32.refs_6_.refs_1_.refs_5_, f32[2,512,512]{2,1,0:T(8,128)S(1)} %get-tuple-element.28.refs_2_.refs_1_.refs_3_, ...), custom_call_target="tpu_custom_call" | custom-call | bytes 3672064 | tf_op jit(solution)/shard_map/prior/pallas_call | solution.py:142
  8.5 0.0 copy-done
  8.5 2.1 %collective-permute-start.2 = (f32[2,64,512]{2,1,0:T(8,128)S(1)}, f32[2,64,512]{2,1,0:T(8,128)S(1)}, u32[]{:S(2)}, u32[]{:S(2)}) collective-permute-start(f32[2,64,512]{2,1,0:T(8,128)S(1)} %broadcast_add_fusion), channel_id=1, source_target_pairs={{0,3},{1,0},{2,1},{3,2},{4,7},{5,4},{6,5},{7,6},{8,11},{9,8},{10,9... | collective-permute-start | bytes 786440 | tf_op jit(solution)/shard_map/ppermute | solution.py:484
  10.7 0.0 copy-done.1
  10.7 0.9 %pick.1 = (bf16[512,256]{1,0:T(8,128)(2,1)S(1)}, bf16[512,256]{1,0:T(8,128)(2,1)S(1)}) custom-call(s32[2,4]{1,0:T(2,128)S(1)} %copy-done.1, s32[2,4]{1,0:T(2,128)S(1)} %collective-permute-done.1.refs_1_.refs_3_.refs_2_, f32[2,512,512]{2,1,0:T(8,128)S(1)} %get-tuple-element.28.refs_2_.refs_1_.refs_3_), custom_call_target="tpu_custom_call" | custom-call | bytes 3145728 | tf_op jit(solution)/shard_map/pick/pallas_call | solution.py:142
  11.6 0.8 %collective-permute-done.refs_2_.refs_0_.refs_3_.refs_4_ = f32[2,64,512]{2,1,0:T(8,128)S(1)} collective-permute-done((f32[2,64,512]{2,1,0:T(8,128)}, f32[2,64,512]{2,1,0:T(8,128)S(1)}, u32[]{:S(2)}, u32[]{:S(2)}) %collective-permute-start) | collective-permute-done | bytes 262176 | tf_op jit(solution)/shard_map/ppermute | solution.py:484
  12.4 0.4 chosen.1
  12.8 0.0 copy-start.2
  12.8 0.1 collective-permute-start.3
  12.9 1.1 %prior.3 = (f32[256,256]{1,0:T(8,128)S(1)}, f32[128,512]{1,0:T(8,128)S(1)}, f32[1,1,512]{2,1,0:T(1,128)}) custom-call(bf16[512,256]{1,0:T(8,128)(2,1)S(1)} %get-tuple-element.29.refs_3_.refs_2_.refs_0_, bf16[512,256]{1,0:T(8,128)(2,1)S(1)} %get-tuple-element.30.refs_4_.refs_3_.refs_1_, f32[2,512,512]{2,1,0:T(8,128)S(1)} %get-tuple-element.28.refs_2_.refs_1_.refs_3_, ...), custom_call_target="tpu_custom_call" | custom-call | bytes 3672064 | tf_op jit(solution)/shard_map/prior/pallas_call | solution.py:142
  14.0 0.0 copy-done.2
  14.0 1.2 %links.1.refs_0_ = f32[2,256,256]{2,1,0:T(8,128)S(1)} custom-call(s32[2,4]{1,0:T(2,128)S(1)} %copy-done.2, f32[2,64,512]{2,1,0:T(8,128)S(1)} %copy-done, f32[2,64,512]{2,1,0:T(8,128)S(1)} %collective-permute-done.refs_2_.refs_0_.refs_3_.refs_4_, bf16[512,256]{1,0:T(8,128)(2,1)S(1)} %get-tuple-element.29.refs_3_.refs_2_.refs_0_, ...), custom_call_target="tpu_custom_call" | custom-call | bytes 3145728 | tf_op jit(solution)/shard_map/links/pallas_call | solution.py:142
  15.2 4.1 %collective-permute-done.2.refs_0_.refs_4_.refs_5_ = f32[2,64,512]{2,1,0:T(8,128)S(1)} collective-permute-done((f32[2,64,512]{2,1,0:T(8,128)S(1)}, f32[2,64,512]{2,1,0:T(8,128)S(1)}, u32[]{:S(2)}, u32[]{:S(2)}) %collective-permute-start.2) | collective-permute-done | bytes 262176 | tf_op jit(solution)/shard_map/ppermute | solution.py:484
  19.3 0.4 second.1.refs_1_
  19.7 1.1 %collective-permute-done.3.refs_2_.refs_10_ = f32[2,64,256]{2,1,0:T(8,128)S(1)} collective-permute-done((f32[2,64,256]{2,1,0:T(8,128)S(1)}, f32[2,64,256]{2,1,0:T(8,128)S(1)}, u32[]{:S(2)}, u32[]{:S(2)}) %collective-permute-start.3) | collective-permute-done | bytes 131104 | tf_op jit(solution)/shard_map/ppermute | solution.py:484
  20.8 0.7 %segment.1 = (f32[2,256,256]{2,1,0:T(8,128)S(1)}, f32[512,256]{1,0:T(8,128)S(1)}) custom-call(f32[2,256,256]{2,1,0:T(8,128)S(1)} %links.1.refs_0_, f32[2,64,256]{2,1,0:T(8,128)S(1)} %second.1.refs_1_, f32[2,64,256]{2,1,0:T(8,128)S(1)} %collective-permute-done.3.refs_2_.refs_10_, f32[256,256]{1,0:T(8,128)S(1)} %get-tuple-element.36.refs_3_, ...), custom_call_target="tpu_custom_call" | custom-call | flops 301989888 | bytes 2359296 | tf_op jit(solution)/shard_map/segment/pallas_call | solution.py:142
  21.5 0.1 collective-permute-start.4
  21.6 1.9 %collective-permute-done.4.refs_1_.refs_7_ = f32[512,256]{1,0:T(8,128)S(1)} collective-permute-done((f32[512,256]{1,0:T(8,128)S(1)}, f32[512,256]{1,0:T(8,128)S(1)}, u32[]{:S(2)}, u32[]{:S(2)}) %collective-permute-start.4) | collective-permute-done | bytes 524320 | tf_op jit(solution)/shard_map/ppermute | solution.py:579
  23.5 0.6 %chip.1 = (f32[256,256]{1,0:T(8,128)S(1)}, f32[256,256]{1,0:T(8,128)S(1)}, f32[160,128]{1,0:T(8,128)S(1)}, f32[128,256]{1,0:T(8,128)S(1)}) custom-call(f32[512,256]{1,0:T(8,128)S(1)} %get-tuple-element.38.refs_0_, f32[512,256]{1,0:T(8,128)S(1)} %collective-permute-done.4.refs_1_.refs_7_), custom_call_target="tpu_custom_call" | custom-call | flops 301989888 | bytes 1785856 | tf_op jit(solution)/shard_map/chip/pallas_call | solution.py:142
  24.1 1.6 %collective-permute-start.5 = (f32[128,256]{1,0:T(8,128)S(1)}, f32[128,256]{1,0:T(8,128)S(1)}, u32[]{:S(2)}, u32[]{:S(2)}) collective-permute-start(f32[128,256]{1,0:T(8,128)S(1)} %get-tuple-element.41), channel_id=1, source_target_pairs={{0,8},{4,12},{8,0},{12,4},{16,24},{20,28},{24,16},{28,20},{1,9},{5... | collective-permute-start | bytes 393224 | tf_op jit(solution)/shard_map/ppermute | solution.py:638
  25.7 0.5 %collective-permute-start.7 = (f32[160,128]{1,0:T(8,128)S(1)}, f32[160,128]{1,0:T(8,128)S(1)}, u32[]{:S(2)}, u32[]{:S(2)}) collective-permute-start(f32[160,128]{1,0:T(8,128)S(1)} %get-tuple-element.42.refs_6_), channel_id=1, source_target_pairs={{0,8},{4,12},{8,0},{12,4},{16,24},{20,28},{24,16},{28,20},{1,9},{5... | collective-permute-start | bytes 245768 | tf_op jit(solution)/shard_map/ppermute | solution.py:632
  26.2 1.5 %maps.1 = (f32[2,256,512]{2,1,0:T(8,128)S(1)}, f32[1,128]{1,0:T(1,128)S(1)}) custom-call(s32[2,4]{1,0:T(2,128)S(1)} %copy-done.2, f32[2,512,512]{2,1,0:T(8,128)S(1)} %get-tuple-element.28.refs_2_.refs_1_.refs_3_, f32[2,64,512]{2,1,0:T(8,128)S(1)} %copy-done, f32[2,64,512]{2,1,0:T(8,128)S(1)} %collective-permute-done.refs_2_.refs_0_.refs_3_.refs_4_, ...), custom_call_target="tpu_custom_call" | custom-call | flops 805306368 | bytes 3932672 | tf_op jit(solution)/shard_map/maps/pallas_call | solution.py:142
  27.7 1.3 %rest.1 = f32[2,64,256]{2,1,0:T(8,128)S(1)} custom-call(s32[2,4]{1,0:T(2,128)S(1)} %copy-done.2, s32[2,4]{1,0:T(2,128)S(1)} %copy-done.1, s32[2,4]{1,0:T(2,128)S(1)} %collective-permute-done.1.refs_1_.refs_3_.refs_2_, f32[2,512,512]{2,1,0:T(8,128)S(1)} %get-tuple-element.28.refs_2_.refs_1_.refs_3_, ...), custom_call_target="tpu_custom_call" | custom-call | flops 201326592 | bytes 2834432 | tf_op jit(solution)/shard_map/rest/pallas_call | solution.py:142
  29.0 0.3 collective-permute-start.10
  29.4 1.1 %collective-permute-done.5.refs_2_.refs_12_ = f32[128,256]{1,0:T(8,128)S(1)} collective-permute-done((f32[128,256]{1,0:T(8,128)S(1)}, f32[128,256]{1,0:T(8,128)S(1)}, u32[]{:S(2)}, u32[]{:S(2)}) %collective-permute-start.5) | collective-permute-done | bytes 131104 | tf_op jit(solution)/shard_map/ppermute | solution.py:638
  30.5 0.0 collective-permute-start.6
  30.5 1.0 %collective-permute-done.7 = f32[160,128]{1,0:T(8,128)S(1)} collective-permute-done((f32[160,128]{1,0:T(8,128)S(1)}, f32[160,128]{1,0:T(8,128)S(1)}, u32[]{:S(2)}, u32[]{:S(2)}) %collective-permute-start.7) | collective-permute-done | bytes 81952 | tf_op jit(solution)/shard_map/ppermute | solution.py:632
  31.5 0.1 collective-permute-start.8
  31.5 1.3 %collective-permute-done.8.refs_5_.refs_15_ = f32[160,128]{1,0:T(8,128)S(1)} collective-permute-done((f32[160,128]{1,0:T(8,128)S(1)}, f32[160,128]{1,0:T(8,128)S(1)}, u32[]{:S(2)}, u32[]{:S(2)}) %collective-permute-start.8) | collective-permute-done | bytes 81952 | tf_op jit(solution)/shard_map/ppermute | solution.py:641
  32.8 0.0 collective-permute-done.6.refs_3_.refs_13_
  32.8 0.8 %merge.1 = f32[160,128]{1,0:T(8,128)S(1)} custom-call(f32[256,256]{1,0:T(8,128)S(1)} %get-tuple-element.39.refs_0_, f32[256,256]{1,0:T(8,128)S(1)} %get-tuple-element.40.refs_1_, f32[128,256]{1,0:T(8,128)S(1)} %collective-permute-done.5.refs_2_.refs_12_, f32[128,256]{1,0:T(8,128)S(1)} %collective-permute-done.6.refs_3_.refs_13_, ...), custom_call_target="tpu_custom_call" | custom-call | flops 301989888 | bytes 1032192 | tf_op jit(solution)/shard_map/merge/pallas_call | solution.py:142
  33.6 2.2 %collective-permute-start.9 = (f32[160,128]{1,0:T(8,128)S(1)}, f32[160,128]{1,0:T(8,128)S(1)}, u32[]{:S(2)}, u32[]{:S(2)}) collective-permute-start(f32[160,128]{1,0:T(8,128)S(1)} %merge.1), channel_id=1, source_target_pairs={{0,16},{4,20},{8,24},{12,28},{16,0},{20,4},{24,8},{28,12},{1,17},{... | collective-permute-start | bytes 245768 | tf_op jit(solution)/shard_map/ppermute | solution.py:632
  35.8 0.0 collective-permute-done.10.refs_11_
  35.8 3.1 %prepare.1 = (bf16[384,256]{1,0:T(8,128)(2,1)S(1)}, bf16[384,256]{1,0:T(8,128)(2,1)S(1)}, bf16[2,256,512]{2,1,0:T(8,128)(2,1)S(1)}, bf16[2,256,512]{2,1,0:T(8,12...) custom-call(s32[2,4]{1,0:T(2,128)S(1)} %copy-done.2, s32[2,4]{1,0:T(2,128)S(1)} %copy-done.1, ...), custom_call_target="tpu_custom_call" | custom-call | flops 1459617792 | bytes 7504384 | tf_op jit(solution)/shard_map/prepare/pallas_call | solution.py:142
  38.9 0.0 collective-permute-done.9
  38.9 0.1 collective-permute-start.11
  39.0 1.3 %collective-permute-done.11.refs_1_ = f32[160,128]{1,0:T(8,128)S(1)} collective-permute-done((f32[160,128]{1,0:T(8,128)S(1)}, f32[160,128]{1,0:T(8,128)S(1)}, u32[]{:S(2)}, u32[]{:S(2)}) %collective-permute-start.11) | collective-permute-done | bytes 81952 | tf_op jit(solution)/shard_map/ppermute | solution.py:636
  40.3 1.9 %finish.1 = (f32[2,128,512]{2,1,0:T(8,128)}, f32[2,64,512]{2,1,0:T(8,128)}) custom-call(f32[160,128]{1,0:T(8,128)S(1)} %broadcast_add_fusion.1.refs_0_, f32[160,128]{1,0:T(8,128)S(1)} %collective-permute-done.11.refs_1_, bf16[384,256]{1,0:T(8,128)(2,1)S(1)} %get-tuple-element.49.refs_2_, bf16[384,256]{1,0:T(8,128)(2,1)S(1)} %get-tuple-element.50.refs_3_, ...), custom_call_target="tpu_custom_call" | custom-call | flops 452984832 | bytes 4620288 | tf_op jit(solution)/shard_map/finish/pallas_call | solution.py:142
  (3 shorter events, 0.0 us)
Async XLA Ops:
  0.6 7.9 %copy-start = (f32[2,64,512]{2,1,0:T(8,128)S(1)}, f32[2,64,512]{2,1,0:T(8,128)}, u32[]{:S(2)}) copy-start(f32[2,64,512]{2,1,0:T(8,128)} %refs_2_.3) | copy-start | bytes 786436
  0.6 11.8 %collective-permute-start = (f32[2,64,512]{2,1,0:T(8,128)}, f32[2,64,512]{2,1,0:T(8,128)S(1)}, u32[]{:S(2)}, u32[]{:S(2)}) collective-permute-start(f32[2,64,512]{2,1,0:T(8,128)} %refs_2_.3), channel_id=1, source_target_pairs={{0,1},{1,2},{2,3},{3,0},{4,5},{5,6},{6,7},{7,4},{8,9},{9,10},{10,1... | collective-permute-start | bytes 786440 | tf_op jit(solution)/shard_map/ppermute | solution.py:484
  3.7 4.1 %collective-permute-start.1 = (s32[2,4]{1,0:T(2,128)}, s32[2,4]{1,0:T(2,128)S(1)}, u32[]{:S(2)}, u32[]{:S(2)}) collective-permute-start(s32[2,4]{1,0:T(2,128)} %refs_1_.7), channel_id=1, source_target_pairs={{0,4},{4,8},{8,12},{12,16},{16,20},{20,24},{24,28},{28,0},{1,5},{5... | collective-permute-start | bytes 104 | tf_op jit(solution)/shard_map/ppermute | solution.py:484
  5.4 5.3 %copy-start.1 = (s32[2,4]{1,0:T(2,128)S(1)}, s32[2,4]{1,0:T(2,128)}, u32[]{:S(2)}) copy-start(s32[2,4]{1,0:T(2,128)} %refs_1_.7) | copy-start | bytes 100
  8.5 10.8 %collective-permute-start.2 = (f32[2,64,512]{2,1,0:T(8,128)S(1)}, f32[2,64,512]{2,1,0:T(8,128)S(1)}, u32[]{:S(2)}, u32[]{:S(2)}) collective-permute-start(f32[2,64,512]{2,1,0:T(8,128)S(1)} %broadcast_add_fusion), channel_id=1, source_target_pairs={{0,3},{1,0},{2,1},{3,2},{4,7},{5,4},{6,5},{7,6},{8,11},{9,8},{10,9... | collective-permute-start | bytes 786440 | tf_op jit(solution)/shard_map/ppermute | solution.py:484
  12.8 1.2 %copy-start.2 = (s32[2,4]{1,0:T(2,128)S(1)}, s32[2,4]{1,0:T(2,128)}, u32[]{:S(2)}) copy-start(s32[2,4]{1,0:T(2,128)} %refs_0_.11) | copy-start | bytes 100
  12.8 8.0 %collective-permute-start.3 = (f32[2,64,256]{2,1,0:T(8,128)S(1)}, f32[2,64,256]{2,1,0:T(8,128)S(1)}, u32[]{:S(2)}, u32[]{:S(2)}) collective-permute-start(f32[2,64,256]{2,1,0:T(8,128)S(1)} %chosen.1), channel_id=1, source_target_pairs={{0,1},{1,2},{2,3},{3,0},{4,5},{5,6},{6,7},{7,4},{8,9},{9,10},{10,1... | collective-permute-start | bytes 393224 | tf_op jit(solution)/shard_map/ppermute | solution.py:484
  21.5 2.0 %collective-permute-start.4 = (f32[512,256]{1,0:T(8,128)S(1)}, f32[512,256]{1,0:T(8,128)S(1)}, u32[]{:S(2)}, u32[]{:S(2)}) collective-permute-start(f32[512,256]{1,0:T(8,128)S(1)} %get-tuple-element.38.refs_0_), channel_id=1, source_target_pairs={{0,4},{4,0},{8,12},{12,8},{16,20},{20,16},{24,28},{28,24},{1,5},{5... | collective-permute-start | bytes 1572872 | tf_op jit(solution)/shard_map/ppermute | solution.py:579
  24.1 6.4 %collective-permute-start.5 = (f32[128,256]{1,0:T(8,128)S(1)}, f32[128,256]{1,0:T(8,128)S(1)}, u32[]{:S(2)}, u32[]{:S(2)}) collective-permute-start(f32[128,256]{1,0:T(8,128)S(1)} %get-tuple-element.41), channel_id=1, source_target_pairs={{0,8},{4,12},{8,0},{12,4},{16,24},{20,28},{24,16},{28,20},{1,9},{5... | collective-permute-start | bytes 393224 | tf_op jit(solution)/shard_map/ppermute | solution.py:638
  25.7 5.8 %collective-permute-start.7 = (f32[160,128]{1,0:T(8,128)S(1)}, f32[160,128]{1,0:T(8,128)S(1)}, u32[]{:S(2)}, u32[]{:S(2)}) collective-permute-start(f32[160,128]{1,0:T(8,128)S(1)} %get-tuple-element.42.refs_6_), channel_id=1, source_target_pairs={{0,8},{4,12},{8,0},{12,4},{16,24},{20,28},{24,16},{28,20},{1,9},{5... | collective-permute-start | bytes 245768 | tf_op jit(solution)/shard_map/ppermute | solution.py:632
  29.0 6.8 %collective-permute-start.10 = (f32[2,64,256]{2,1,0:T(8,128)S(1)}, f32[2,64,256]{2,1,0:T(8,128)S(1)}, u32[]{:S(2)}, u32[]{:S(2)}) collective-permute-start(f32[2,64,256]{2,1,0:T(8,128)S(1)} %rest.1), channel_id=1, source_target_pairs={{0,1},{1,0},{2,3},{3,2},{4,5},{5,4},{6,7},{7,6},{8,9},{9,8},{10,11... | collective-permute-start | bytes 393224 | tf_op jit(solution)/shard_map/ppermute | solution.py:605
  30.5 2.3 %collective-permute-start.6 = (f32[128,256]{1,0:T(8,128)S(1)}, f32[128,256]{1,0:T(8,128)S(1)}, u32[]{:S(2)}, u32[]{:S(2)}) collective-permute-start(f32[128,256]{1,0:T(8,128)S(1)} %collective-permute-done.5.refs_2_.refs_12_), channel_id=1, source_target_pairs={{0,4},{4,0},{8,12},{12,8},{16,20},{20,16},{24,28},{28,24},{1,5},{5... | collective-permute-start | bytes 393224 | tf_op jit(solution)/shard_map/ppermute | solution.py:641
  31.5 1.3 %collective-permute-start.8 = (f32[160,128]{1,0:T(8,128)S(1)}, f32[160,128]{1,0:T(8,128)S(1)}, u32[]{:S(2)}, u32[]{:S(2)}) collective-permute-start(f32[160,128]{1,0:T(8,128)S(1)} %broadcast_add_fusion.2.refs_4_.refs_14_), channel_id=1, source_target_pairs={{0,4},{4,0},{8,12},{12,8},{16,20},{20,16},{24,28},{28,24},{1,5},{5... | collective-permute-start | bytes 245768 | tf_op jit(solution)/shard_map/ppermute | solution.py:641
  33.6 5.3 %collective-permute-start.9 = (f32[160,128]{1,0:T(8,128)S(1)}, f32[160,128]{1,0:T(8,128)S(1)}, u32[]{:S(2)}, u32[]{:S(2)}) collective-permute-start(f32[160,128]{1,0:T(8,128)S(1)} %merge.1), channel_id=1, source_target_pairs={{0,16},{4,20},{8,24},{12,28},{16,0},{20,4},{24,8},{28,12},{1,17},{... | collective-permute-start | bytes 245768 | tf_op jit(solution)/shard_map/ppermute | solution.py:632
  38.9 1.3 %collective-permute-start.11 = (f32[160,128]{1,0:T(8,128)S(1)}, f32[160,128]{1,0:T(8,128)S(1)}, u32[]{:S(2)}, u32[]{:S(2)}) collective-permute-start(f32[160,128]{1,0:T(8,128)S(1)} %broadcast_add_fusion.1.refs_0_), channel_id=1, source_target_pairs={{0,4},{4,0},{8,12},{12,8},{16,20},{20,16},{24,28},{28,24},{1,5},{5... | collective-permute-start | bytes 245768 | tf_op jit(solution)/shard_map/ppermute | solution.py:636

commit v19 on v18

--- a/solution.py
+++ b/solution.py
@@ -73,6 +73,27 @@
 def own_half(whole):
     half = whole.shape[0] // 2
     return jnp.where(is_lower(), whole[:half], whole[half:])
+
+
+def other_half(whole):
+    half = whole.shape[0] // 2
+    return jnp.where(is_lower(), whole[half:], whole[:half])
+
+
+def joint(link_t, packed, half):
+    packed = half(packed)
+    rows = packed.shape[0] // 2
+    return jnp.concatenate([half(link_t), jnp.concatenate([packed[:rows], packed[rows:]], 1)], 0)
+
+
+def apart(own, other):
+    size = own.shape[1]
+    link_t = from_halves(own[: size // 2], other[: size // 2])
+    own, other = (
+        jnp.concatenate([x[size // 2 :, : size // 2], x[size // 2 :, size // 2 :]], 0)
+        for x in (own, other)
+    )
+    return link_t, from_halves(own, other)
 
 
 def two_blocks(load, left, right):
@@ -319,7 +340,7 @@
 
 
 def maps_kernel(plan, mask_ref, inv_ref, *refs):
-    *parts, maps_ref, token_ref, rows_ref = refs
+    *parts, _, maps_ref, token_ref, rows_ref = refs
     token_ref[...] = jnp.zeros_like(token_ref)
     rows_ref[...] = jnp.zeros_like(rows_ref)
     for p in range(inv_ref.shape[0]):
@@ -328,7 +349,7 @@
         maps_ref[p] = triangular_mm(rows_ref[...], inv_ref[p])
 
 
-def chip_kernel(own_ref, other_ref, link_t_ref, cov_ref, packed_ref, half_t_ref):
+def chip_kernel(own_ref, other_ref, link_t_ref, cov_ref, packed_ref, joint_ref):
     size = cov_ref.shape[0]
     lower = is_lower()
     own_t, other_t = own_ref[:size, :], other_ref[:size, :]
@@ -338,29 +359,31 @@
     link_t = mm(down_t, jnp.where(lower, other_t, own_t))
     link_t_ref[...] = link_t
     cov_ref[...] = cov
-    packed_ref[...] = own_half(pack(cov))
-    half_t_ref[...] = own_half(link_t)
-
-
-def merge_kernel(level, link_t_ref, cov_ref, *refs):
-    got_t = from_halves(refs[0][...], refs[1][...])
-    got = unpack(from_halves(refs[2][...], refs[3][...]))
+    packed = pack(cov)
+    packed_ref[...] = own_half(packed)
+    joint_ref[...] = joint(link_t, packed, own_half)
+
+
+def merge_kernel(level, link_t_ref, cov_ref, got_ref, got_other_ref, *refs):
+    got_t, got = apart(got_ref[...], got_other_ref[...])
+    got = unpack(got)
     own_t, own = link_t_ref[...], cov_ref[...]
     lower = (lax.shift_right_logical(lax.axis_index("seg") // 2, level) & 1) == 0
     down_t = split(jnp.where(lower, own_t, got_t))
     cov = carry(down_t, jnp.where(lower, got, own), jnp.where(lower, own, got))
-    refs[4][...] = own_half(pack(cov))
-    if len(refs) > 5:
+    packed = pack(cov)
+    if len(refs) == 1:
+        refs[0][...] = own_half(packed)
+    else:
         link_t = mm(down_t, jnp.where(lower, got_t, own_t))
-        refs[5][...] = own_half(link_t)
-        refs[6][...] = link_t
-        refs[7][...] = cov
-
-
-def join_kernel(level, *refs):
-    past_t, past, link_t, cov = (
-        from_halves(refs[2 * i][...], refs[2 * i + 1][...]) for i in range(4)
-    )
+        refs[0][...] = joint(link_t, packed, own_half)
+        refs[1][...] = link_t
+        refs[2][...] = cov
+
+
+def join_kernel(level, past_ref, past_other_ref, got_ref, got_other_ref, out_ref, out_other_ref):
+    past_t, past = apart(past_ref[...], past_other_ref[...])
+    link_t, cov = apart(got_ref[...], got_other_ref[...])
     chip = lax.axis_index("seg") // 2
     below = (lax.shift_right_logical(chip, level) & 1) == 0
     known = (chip & ((1 << level) - 1)) != (1 << level) - 1
@@ -369,16 +392,14 @@
     joined_t = mm(past_parts, link_t)
     out_t = jnp.where(below, jnp.where(known, joined_t, link_t), past_t)
     out = jnp.where(below, jnp.where(known, joined, cov), past)
-    for i, whole in enumerate((out_t, out)):
-        half = whole.shape[0] // 2
-        refs[8 + 2 * i][...] = own_half(whole)
-        refs[9 + 2 * i][...] = jnp.where(is_lower(), whole[half:], whole[:half])
+    out_ref[...] = joint(out_t, out, own_half)
+    out_other_ref[...] = joint(out_t, out, other_half)
 
 
 def prepare_kernel(plan, levels, panels, mask_ref, fill_ref, prior_ref, *refs):
     base_refs, own_refs, refs = refs[:panels], refs[panels : 2 * panels], refs[2 * panels :]
     (other_ref, maps_ref, links_t_ref, late_ref, rest_ref), refs = refs[:5], refs[5:]
-    past_refs, refs = refs[: 4 * (levels > 1)], refs[4 * (levels > 1) :]
+    past_refs, refs = refs[: 2 * (levels > 1)], refs[2 * (levels > 1) :]
     left_high, left_low, right_high, right_low, const_ref, token_ref, scratch, map_ref, late_map_ref = refs
     token_ref[...] = jnp.zeros_like(token_ref)
     own_cols, width = own_refs[0].shape
@@ -395,8 +416,8 @@
         chip = lax.axis_index("seg") // 2
         low = (1 << (levels - 1)) - 1
         known = (chip & low) != low
-        past_t = from_halves(past_refs[0][...], past_refs[1][...])
-        past = unpack(from_halves(past_refs[2][...], past_refs[3][...]))
+        past_t, past = apart(past_refs[0][...], past_refs[1][...])
+        past = unpack(past)
         to_t = jnp.where(known, past_t, eye)
         gain = jnp.where(known, past, 0.0)
         other_t = split(other_ref[:size, :])
@@ -565,23 +586,13 @@
         flops=18 * (panels - 1) * size**3,
         name="segment",
     )
-    maps, maps_token = call(
-        functools.partial(maps_kernel, plan),
-        [shape(panels, size, width), shape(1, half)],
-        [fill_mask],
-        [inv, *parts],
-        scratch=[pltpu.VMEM((size, width), F32)],
-        flops=6 * panels * size * width * width,
-        mib=24,
-        name="maps",
-    )
     swap = [(i, i ^ 1) for i in range(seg_count)]
     other_whole = lax.ppermute(own_whole, "seg", swap)
     half_packed = shape(5 * half // 4, half)
-    half_link = shape(half, size)
-    link_t, cov, send, send_t = call(
+    joint_half = shape(half + 5 * half // 8, size)
+    link_t, cov, packed, send = call(
         chip_kernel,
-        [shape(size, size), shape(size, size), half_packed, half_link],
+        [shape(size, size), shape(size, size), half_packed, joint_half],
         [],
         [own_whole, other_whole],
         flops=18 * size**3,
@@ -600,6 +611,17 @@
         flops=6 * panels * rows * width * width,
         mib=24,
         name="rest",
+    )
+    maps, maps_token = call(
+        functools.partial(maps_kernel, plan),
+        [shape(panels, size, width), shape(1, size)],
+        [fill_mask],
+        [inv, *parts],
+        anywhere=[rest],
+        scratch=[pltpu.VMEM((size, width), F32)],
+        flops=6 * panels * size * width * width,
+        mib=24,
+        name="maps",
     )
     if short:
         rest = lax.ppermute(rest, "row", [(i, i ^ 1) for i in range(row_count)])
@@ -629,31 +651,31 @@
 
     for level in range(levels):
         partner = [(i, i ^ (2 << level)) for i in range(seg_count)]
-        got = lax.ppermute(send, "seg", partner)
         if level == levels - 1:
+            got = lax.ppermute(packed if level == 0 else send, "seg", partner)
             *prepared, token = prepare()
             got = got + token
             after = (got, lax.ppermute(got, "seg", swap))
             break
-        got_t = lax.ppermute(send_t, "seg", partner)
+        got = lax.ppermute(send, "seg", partner)
         if level == 0:
-            got = got + maps_token
-        got = (got_t, lax.ppermute(got_t, "seg", swap), got, lax.ppermute(got, "seg", swap))
+            got = got + maps_token + jnp.minimum(jnp.abs(rest[0, :1, :size]), 0.0)
+        got = (got, lax.ppermute(got, "seg", swap))
         outs = [half_packed]
         if level < levels - 2:
-            outs += [half_link, shape(size, size), shape(size, size)]
+            outs = [joint_half, shape(size, size), shape(size, size)]
         send, *more = call(
             functools.partial(merge_kernel, level), outs, [], [link_t, cov, *got],
             flops=18 * size**3, name="merge",
         )
         if more:
-            send_t, link_t, cov = more
+            link_t, cov = more
         if past is None:
             past = got
         else:
             past = call(
                 functools.partial(join_kernel, level),
-                [half_link, half_link, half_packed, half_packed],
+                [joint_half, joint_half],
                 [],
                 [*past, *got],
                 flops=18 * size**3,

time: 42.3 us -> 44.5 us (1.052)
  waiting for transfers between devices: 15 us -> 17.1 us
  Pallas kernels: 16.2 us -> 16.8 us
  starting transfers between devices: 10.1 us -> 9.54 us
    ppermute x1, waiting for transfers between devices: 0.01 us -> 2.25 us  [body(): rest = lax.ppermute(rest, 'row', [(i, i ^ 1) for i in range(row_count)])]
    ppermute x2 -> x1, starting transfers between devices: 2.71 us -> 1.49 us  [body(): got = lax.ppermute(send, 'seg', partner)]
    ppermute x3 -> x2, waiting for transfers between devices: 2.41 us -> 1.45 us  [the longest x1 1.45 us: body(): got = (got, lax.ppermute(got, 'seg', swap))]
    ppermute x2 -> x1, waiting for transfers between devices: 0.95 us -> 1.83 us  [body(): got = lax.ppermute(send, 'seg', partner)]
    pallas_call x14, Pallas kernels: 16.2 us -> 16.8 us  [call(): pl.pallas_call(inner, out_shape=[*outs, *(jax.ShapeDtypeStruct(a.shape, a...]
    ppermute x3 -> x2, starting transfers between devices: 1.66 us -> 2.29 us  [the longest x1 2.22 us: body(): got = lax.ppermute(packed if level == 0 else send, 'seg', partner)]
  transfers between devices with their start and end apart: 12 -> 10, of which waited for: 9 -> 9; matrix products, arithmetic and copies ran while one was open for 0% -> 0% of each run, Pallas kernels for 31% -> 25%
where the time goes in v19:
time: 44.5 us; the launch traced here: 44.4 us
  waiting for transfers between devices  17.1 us (38%)
  Pallas kernels  16.8 us (38%)
  starting transfers between devices  9.54 us (21%)
  between operations  0.8 us (2%)
    pallas_call x14, Pallas kernels, call(): pl.pallas_call(inner, out_shape=[*outs, *(jax.ShapeDtypeStruct(a.shape, a...  16.8 us
    ppermute x4, waiting for transfers between devices, turn(): lax.ppermute(x, axis, [(i, (i + distance) % count) for i in range(count)])  8.43 us
    ppermute x4, starting transfers between devices, turn(): lax.ppermute(x, axis, [(i, (i + distance) % count) for i in range(count)])  5.29 us
    ppermute x1, waiting for transfers between devices, body(): rest = lax.ppermute(rest, 'row', [(i, i ^ 1) for i in range(row_count)])  2.25 us
    ppermute x1, starting transfers between devices, body(): got = lax.ppermute(packed if level == 0 else send, 'seg', partner)  2.22 us
    ppermute x1, waiting for transfers between devices, body(): other_whole = lax.ppermute(own_whole, 'seg', swap)  1.9 us
    ppermute x1, waiting for transfers between devices, body(): got = lax.ppermute(send, 'seg', partner)  1.83 us
    ppermute x1, starting transfers between devices, body(): got = lax.ppermute(send, 'seg', partner)  1.49 us
  transfers between devices with their start and end apart: 10, of which 9 were waited for; matrix products, arithmetic and copies ran while one was open for 0% of the time, Pallas kernels for 25%

profile of v19, /device:TPU:0, one launch (start us, length us, event | category | flops | bytes accessed | tf_op | source)
XLA Modules:
  0.0 44.4 jit_solution(3137260852297526948)
XLA Ops:
  0.6 0.0 copy-start
  0.6 3.1 %collective-permute-start = (f32[2,64,512]{2,1,0:T(8,128)}, f32[2,64,512]{2,1,0:T(8,128)S(1)}, u32[]{:S(2)}, u32[]{:S(2)}) collective-permute-start(f32[2,64,512]{2,1,0:T(8,128)} %refs_2_.3), channel_id=1, source_target_pairs={{0,1},{1,2},{2,3},{3,0},{4,5},{5,6},{6,7},{7,4},{8,9},{9,10},{10,1... | collective-permute-start | bytes 786440 | tf_op jit(solution)/shard_map/ppermute | solution.py:505
  3.7 0.0 collective-permute-start.1
  3.7 1.6 %load.1 = (f32[2,512,512]{2,1,0:T(8,128)S(1)}, bf16[512,256]{1,0:T(8,128)(2,1)S(1)}, bf16[512,256]{1,0:T(8,128)(2,1)S(1)}, f32[2,64,256]{2,1,0:T(8,128)S(1)}, f32[2,64,256]{2,1,0:T(8,128)S(1)}) custom-call(s32[2,4]{1,0:T(2,128)} %refs_0_.11, s32[2,4]{1,0:T(2,128)} %refs_1_.7, f32[2,512,512]{2,1,0:T(8,128)} %refs_2_.2), custom_call_target="tpu_custom_call" | custom-call | bytes 5505088 | tf_op jit(solution)/shard_map/load/pallas_call | solution.py:163
  5.4 0.0 copy-start.2
  5.4 2.4 %collective-permute-done.1.refs_1_.refs_3_.refs_2_ = s32[2,4]{1,0:T(2,128)S(1)} collective-permute-done((s32[2,4]{1,0:T(2,128)}, s32[2,4]{1,0:T(2,128)S(1)}, u32[]{:S(2)}, u32[]{:S(2)}) %collective-permute-start.1) | collective-permute-done | bytes 64 | tf_op jit(solution)/shard_map/ppermute | solution.py:505
  7.8 0.7 %prior.2 = (f32[256,256]{1,0:T(8,128)S(1)}, f32[128,512]{1,0:T(8,128)S(1)}, f32[1,1,512]{2,1,0:T(1,128)S(1)}) custom-call(bf16[512,256]{1,0:T(8,128)(2,1)S(1)} %get-tuple-element.30.refs_5_.refs_0_.refs_4_, bf16[512,256]{1,0:T(8,128)(2,1)S(1)} %get-tuple-element.31.refs_6_.refs_1_.refs_5_, f32[2,512,512]{2,1,0:T(8,128)S(1)} %get-tuple-element.27.refs_2_.refs_3_.refs_1_, ...), custom_call_target="tpu_custom_call" | custom-call | bytes 3672064 | tf_op jit(solution)/shard_map/prior/pallas_call | solution.py:163
  8.5 0.0 copy-done
  8.5 2.1 %collective-permute-start.2 = (f32[2,64,512]{2,1,0:T(8,128)S(1)}, f32[2,64,512]{2,1,0:T(8,128)S(1)}, u32[]{:S(2)}, u32[]{:S(2)}) collective-permute-start(f32[2,64,512]{2,1,0:T(8,128)S(1)} %broadcast_add_fusion), channel_id=1, source_target_pairs={{0,3},{1,0},{2,1},{3,2},{4,7},{5,4},{6,5},{7,6},{8,11},{9,8},{10,9... | collective-permute-start | bytes 786440 | tf_op jit(solution)/shard_map/ppermute | solution.py:505
  10.7 0.0 copy-done.2
  10.7 0.9 %pick.1 = (bf16[512,256]{1,0:T(8,128)(2,1)S(1)}, bf16[512,256]{1,0:T(8,128)(2,1)S(1)}) custom-call(s32[2,4]{1,0:T(2,128)S(1)} %copy-done.2, s32[2,4]{1,0:T(2,128)S(1)} %collective-permute-done.1.refs_1_.refs_3_.refs_2_, f32[2,512,512]{2,1,0:T(8,128)S(1)} %get-tuple-element.27.refs_2_.refs_3_.refs_1_), custom_call_target="tpu_custom_call" | custom-call | bytes 3145728 | tf_op jit(solution)/shard_map/pick/pallas_call | solution.py:163
  11.6 0.8 %collective-permute-done.refs_2_.refs_0_.refs_4_.refs_3_ = f32[2,64,512]{2,1,0:T(8,128)S(1)} collective-permute-done((f32[2,64,512]{2,1,0:T(8,128)}, f32[2,64,512]{2,1,0:T(8,128)S(1)}, u32[]{:S(2)}, u32[]{:S(2)}) %collective-permute-start) | collective-permute-done | bytes 262176 | tf_op jit(solution)/shard_map/ppermute | solution.py:505
  12.4 0.4 chosen.1
  12.8 0.0 copy-start.1
  12.8 0.1 collective-permute-start.3
  12.9 1.1 %prior.3 = (f32[256,256]{1,0:T(8,128)S(1)}, f32[128,512]{1,0:T(8,128)S(1)}, f32[1,1,512]{2,1,0:T(1,128)}) custom-call(bf16[512,256]{1,0:T(8,128)(2,1)S(1)} %get-tuple-element.28.refs_3_.refs_2_.refs_0_, bf16[512,256]{1,0:T(8,128)(2,1)S(1)} %get-tuple-element.29.refs_4_.refs_3_.refs_1_, f32[2,512,512]{2,1,0:T(8,128)S(1)} %get-tuple-element.27.refs_2_.refs_3_.refs_1_, ...), custom_call_target="tpu_custom_call" | custom-call | bytes 3672064 | tf_op jit(solution)/shard_map/prior/pallas_call | solution.py:163
  14.0 0.0 copy-done.1
  14.0 1.2 %links.1.refs_0_ = f32[2,256,256]{2,1,0:T(8,128)S(1)} custom-call(s32[2,4]{1,0:T(2,128)S(1)} %copy-done.1, f32[2,64,512]{2,1,0:T(8,128)S(1)} %copy-done, f32[2,64,512]{2,1,0:T(8,128)S(1)} %collective-permute-done.refs_2_.refs_0_.refs_4_.refs_3_, bf16[512,256]{1,0:T(8,128)(2,1)S(1)} %get-tuple-element.28.refs_3_.refs_2_.refs_0_, ...), custom_call_target="tpu_custom_call" | custom-call | bytes 3145728 | tf_op jit(solution)/shard_map/links/pallas_call | solution.py:163
  15.2 4.1 %collective-permute-done.2.refs_0_.refs_5_.refs_4_ = f32[2,64,512]{2,1,0:T(8,128)S(1)} collective-permute-done((f32[2,64,512]{2,1,0:T(8,128)S(1)}, f32[2,64,512]{2,1,0:T(8,128)S(1)}, u32[]{:S(2)}, u32[]{:S(2)}) %collective-permute-start.2) | collective-permute-done | bytes 262176 | tf_op jit(solution)/shard_map/ppermute | solution.py:505
  19.3 0.4 second.1.refs_1_
  19.7 1.1 %collective-permute-done.3.refs_2_.refs_10_ = f32[2,64,256]{2,1,0:T(8,128)S(1)} collective-permute-done((f32[2,64,256]{2,1,0:T(8,128)S(1)}, f32[2,64,256]{2,1,0:T(8,128)S(1)}, u32[]{:S(2)}, u32[]{:S(2)}) %collective-permute-start.3) | collective-permute-done | bytes 131104 | tf_op jit(solution)/shard_map/ppermute | solution.py:505
  20.8 0.7 %segment.1 = (f32[2,256,256]{2,1,0:T(8,128)S(1)}, f32[512,256]{1,0:T(8,128)S(1)}) custom-call(f32[2,256,256]{2,1,0:T(8,128)S(1)} %links.1.refs_0_, f32[2,64,256]{2,1,0:T(8,128)S(1)} %second.1.refs_1_, f32[2,64,256]{2,1,0:T(8,128)S(1)} %collective-permute-done.3.refs_2_.refs_10_, f32[256,256]{1,0:T(8,128)S(1)} %get-tuple-element.35.refs_3_, ...), custom_call_target="tpu_custom_call" | custom-call | flops 301989888 | bytes 2359296 | tf_op jit(solution)/shard_map/segment/pallas_call | solution.py:163
  21.5 0.1 collective-permute-start.4
  21.6 1.9 %collective-permute-done.4.refs_1_.refs_7_ = f32[512,256]{1,0:T(8,128)S(1)} collective-permute-done((f32[512,256]{1,0:T(8,128)S(1)}, f32[512,256]{1,0:T(8,128)S(1)}, u32[]{:S(2)}, u32[]{:S(2)}) %collective-permute-start.4) | collective-permute-done | bytes 524320 | tf_op jit(solution)/shard_map/ppermute | solution.py:590
  23.5 1.3 %chip.1 = (f32[256,256]{1,0:T(8,128)S(1)}, f32[256,256]{1,0:T(8,128)S(1)}, f32[160,128]{1,0:T(8,128)}, f32[208,256]{1,0:T(8,128)S(1)}) custom-call(f32[512,256]{1,0:T(8,128)S(1)} %get-tuple-element.37.refs_0_, f32[512,256]{1,0:T(8,128)S(1)} %collective-permute-done.4.refs_1_.refs_7_), custom_call_target="tpu_custom_call" | custom-call | flops 301989888 | bytes 1867776 | tf_op jit(solution)/shard_map/chip/pallas_call | solution.py:163
  24.7 1.3 %rest.1.refs_5_ = f32[2,64,256]{2,1,0:T(8,128)S(1)} custom-call(s32[2,4]{1,0:T(2,128)S(1)} %copy-done.1, s32[2,4]{1,0:T(2,128)S(1)} %copy-done.2, s32[2,4]{1,0:T(2,128)S(1)} %collective-permute-done.1.refs_1_.refs_3_.refs_2_, f32[2,512,512]{2,1,0:T(8,128)S(1)} %get-tuple-element.27.refs_2_.refs_3_.refs_1_, ...), custom_call_target="tpu_custom_call" | custom-call | flops 201326592 | bytes 2965504 | tf_op jit(solution)/shard_map/rest/pallas_call | solution.py:163
  26.0 0.3 collective-permute-start.6
  26.4 1.5 %collective-permute-start.5 = (f32[208,256]{1,0:T(8,128)S(1)}, f32[208,256]{1,0:T(8,128)S(1)}, u32[]{:S(2)}, u32[]{:S(2)}) collective-permute-start(f32[208,256]{1,0:T(8,128)S(1)} %get-tuple-element.40.refs_6_), channel_id=1, source_target_pairs={{0,8},{4,12},{8,0},{12,4},{16,24},{20,28},{24,16},{28,20},{1,9},{5... | collective-permute-start | bytes 638984 | tf_op jit(solution)/shard_map/ppermute | solution.py:660
  27.9 1.5 %maps.1 = (f32[2,256,512]{2,1,0:T(8,128)S(1)}, f32[1,256]{1,0:T(1,128)S(1)}) custom-call(s32[2,4]{1,0:T(2,128)S(1)} %copy-done.1, f32[2,512,512]{2,1,0:T(8,128)S(1)} %get-tuple-element.27.refs_2_.refs_3_.refs_1_, f32[2,64,512]{2,1,0:T(8,128)S(1)} %copy-done, f32[2,64,512]{2,1,0:T(8,128)S(1)} %collective-permute-done.refs_2_.refs_0_.refs_4_.refs_3_, ...), custom_call_target="tpu_custom_call" | custom-call | flops 805306368 | bytes 3933184 | tf_op jit(solution)/shard_map/maps/pallas_call | solution.py:163
  29.4 2.2 %collective-permute-done.6.refs_11_ = f32[2,64,256]{2,1,0:T(8,128)S(1)} collective-permute-done((f32[2,64,256]{2,1,0:T(8,128)S(1)}, f32[2,64,256]{2,1,0:T(8,128)S(1)}, u32[]{:S(2)}, u32[]{:S(2)}) %collective-permute-start.6) | collective-permute-done | bytes 131104 | tf_op jit(solution)/shard_map/ppermute | solution.py:627
  31.6 1.8 %collective-permute-done.5 = f32[208,256]{1,0:T(8,128)S(1)} collective-permute-done((f32[208,256]{1,0:T(8,128)S(1)}, f32[208,256]{1,0:T(8,128)S(1)}, u32[]{:S(2)}, u32[]{:S(2)}) %collective-permute-start.5) | collective-permute-done | bytes 213024 | tf_op jit(solution)/shard_map/ppermute | solution.py:660
  33.5 0.1 collective-permute-start.7
  33.6 1.5 %collective-permute-done.7.refs_3_.refs_13_ = f32[208,256]{1,0:T(8,128)S(1)} collective-permute-done((f32[208,256]{1,0:T(8,128)S(1)}, f32[208,256]{1,0:T(8,128)S(1)}, u32[]{:S(2)}, u32[]{:S(2)}) %collective-permute-start.7) | collective-permute-done | bytes 213024 | tf_op jit(solution)/shard_map/ppermute | solution.py:663
  35.0 0.8 %merge.1 = f32[160,128]{1,0:T(8,128)S(1)} custom-call(f32[256,256]{1,0:T(8,128)S(1)} %get-tuple-element.38.refs_0_, f32[256,256]{1,0:T(8,128)S(1)} %get-tuple-element.39.refs_1_, f32[208,256]{1,0:T(8,128)S(1)} %add_add_fusion.refs_2_.refs_12_, f32[208,256]{1,0:T(8,128)S(1)} %collective-permute-done.7.refs_3_.refs_13_), custom_call_target="tpu_custom_call" | custom-call | flops 301989888 | bytes 1032192 | tf_op jit(solution)/shard_map/merge/pallas_call | solution.py:163
  35.8 2.2 %collective-permute-start.8 = (f32[160,128]{1,0:T(8,128)S(1)}, f32[160,128]{1,0:T(8,128)S(1)}, u32[]{:S(2)}, u32[]{:S(2)}) collective-permute-start(f32[160,128]{1,0:T(8,128)S(1)} %merge.1), channel_id=1, source_target_pairs={{0,16},{4,20},{8,24},{12,28},{16,0},{20,4},{24,8},{28,12},{1,17},{... | collective-permute-start | bytes 245768 | tf_op jit(solution)/shard_map/ppermute | solution.py:655
  38.1 3.1 %prepare.1 = (bf16[384,256]{1,0:T(8,128)(2,1)S(1)}, bf16[384,256]{1,0:T(8,128)(2,1)S(1)}, bf16[2,256,512]{2,1,0:T(8,128)(2,1)S(1)}, bf16[2,256,512]{2,1,0:T(8,12...) custom-call(s32[2,4]{1,0:T(2,128)S(1)} %copy-done.1, s32[2,4]{1,0:T(2,128)S(1)} %copy-done.2, ...), custom_call_target="tpu_custom_call" | custom-call | flops 1459617792 | bytes 7504384 | tf_op jit(solution)/shard_map/prepare/pallas_call | solution.py:163
  41.1 0.0 collective-permute-done.8
  41.2 0.1 collective-permute-start.9
  41.2 1.3 %collective-permute-done.9.refs_1_ = f32[160,128]{1,0:T(8,128)S(1)} collective-permute-done((f32[160,128]{1,0:T(8,128)S(1)}, f32[160,128]{1,0:T(8,128)S(1)}, u32[]{:S(2)}, u32[]{:S(2)}) %collective-permute-start.9) | collective-permute-done | bytes 81952 | tf_op jit(solution)/shard_map/ppermute | solution.py:658
  42.5 1.9 %finish.1 = (f32[2,128,512]{2,1,0:T(8,128)}, f32[2,64,512]{2,1,0:T(8,128)}) custom-call(f32[160,128]{1,0:T(8,128)S(1)} %broadcast_add_fusion.1.refs_0_, f32[160,128]{1,0:T(8,128)S(1)} %collective-permute-done.9.refs_1_, bf16[384,256]{1,0:T(8,128)(2,1)S(1)} %get-tuple-element.47.refs_2_, bf16[384,256]{1,0:T(8,128)(2,1)S(1)} %get-tuple-element.48.refs_3_, ...), custom_call_target="tpu_custom_call" | custom-call | flops 452984832 | bytes 4620288 | tf_op jit(solution)/shard_map/finish/pallas_call | solution.py:163
  (4 shorter events, 0.1 us)
Async XLA Ops:
  0.6 7.9 %copy-start = (f32[2,64,512]{2,1,0:T(8,128)S(1)}, f32[2,64,512]{2,1,0:T(8,128)}, u32[]{:S(2)}) copy-start(f32[2,64,512]{2,1,0:T(8,128)} %refs_2_.3) | copy-start | bytes 786436
  0.6 11.8 %collective-permute-start = (f32[2,64,512]{2,1,0:T(8,128)}, f32[2,64,512]{2,1,0:T(8,128)S(1)}, u32[]{:S(2)}, u32[]{:S(2)}) collective-permute-start(f32[2,64,512]{2,1,0:T(8,128)} %refs_2_.3), channel_id=1, source_target_pairs={{0,1},{1,2},{2,3},{3,0},{4,5},{5,6},{6,7},{7,4},{8,9},{9,10},{10,1... | collective-permute-start | bytes 786440 | tf_op jit(solution)/shard_map/ppermute | solution.py:505
  3.7 4.1 %collective-permute-start.1 = (s32[2,4]{1,0:T(2,128)}, s32[2,4]{1,0:T(2,128)S(1)}, u32[]{:S(2)}, u32[]{:S(2)}) collective-permute-start(s32[2,4]{1,0:T(2,128)} %refs_1_.7), channel_id=1, source_target_pairs={{0,4},{4,8},{8,12},{12,16},{16,20},{20,24},{24,28},{28,0},{1,5},{5... | collective-permute-start | bytes 104 | tf_op jit(solution)/shard_map/ppermute | solution.py:505
  5.4 5.3 %copy-start.2 = (s32[2,4]{1,0:T(2,128)S(1)}, s32[2,4]{1,0:T(2,128)}, u32[]{:S(2)}) copy-start(s32[2,4]{1,0:T(2,128)} %refs_1_.7) | copy-start | bytes 100
  8.5 10.8 %collective-permute-start.2 = (f32[2,64,512]{2,1,0:T(8,128)S(1)}, f32[2,64,512]{2,1,0:T(8,128)S(1)}, u32[]{:S(2)}, u32[]{:S(2)}) collective-permute-start(f32[2,64,512]{2,1,0:T(8,128)S(1)} %broadcast_add_fusion), channel_id=1, source_target_pairs={{0,3},{1,0},{2,1},{3,2},{4,7},{5,4},{6,5},{7,6},{8,11},{9,8},{10,9... | collective-permute-start | bytes 786440 | tf_op jit(solution)/shard_map/ppermute | solution.py:505
  12.8 1.2 %copy-start.1 = (s32[2,4]{1,0:T(2,128)S(1)}, s32[2,4]{1,0:T(2,128)}, u32[]{:S(2)}) copy-start(s32[2,4]{1,0:T(2,128)} %refs_0_.11) | copy-start | bytes 100
  12.8 8.0 %collective-permute-start.3 = (f32[2,64,256]{2,1,0:T(8,128)S(1)}, f32[2,64,256]{2,1,0:T(8,128)S(1)}, u32[]{:S(2)}, u32[]{:S(2)}) collective-permute-start(f32[2,64,256]{2,1,0:T(8,128)S(1)} %chosen.1), channel_id=1, source_target_pairs={{0,1},{1,2},{2,3},{3,0},{4,5},{5,6},{6,7},{7,4},{8,9},{9,10},{10,1... | collective-permute-start | bytes 393224 | tf_op jit(solution)/shard_map/ppermute | solution.py:505
  21.5 2.0 %collective-permute-start.4 = (f32[512,256]{1,0:T(8,128)S(1)}, f32[512,256]{1,0:T(8,128)S(1)}, u32[]{:S(2)}, u32[]{:S(2)}) collective-permute-start(f32[512,256]{1,0:T(8,128)S(1)} %get-tuple-element.37.refs_0_), channel_id=1, source_target_pairs={{0,4},{4,0},{8,12},{12,8},{16,20},{20,16},{24,28},{28,24},{1,5},{5... | collective-permute-start | bytes 1572872 | tf_op jit(solution)/shard_map/ppermute | solution.py:590
  26.0 5.6 %collective-permute-start.6 = (f32[2,64,256]{2,1,0:T(8,128)S(1)}, f32[2,64,256]{2,1,0:T(8,128)S(1)}, u32[]{:S(2)}, u32[]{:S(2)}) collective-permute-start(f32[2,64,256]{2,1,0:T(8,128)S(1)} %rest.1.refs_5_), channel_id=1, source_target_pairs={{0,1},{1,0},{2,3},{3,2},{4,5},{5,4},{6,7},{7,6},{8,9},{9,8},{10,11... | collective-permute-start | bytes 393224 | tf_op jit(solution)/shard_map/ppermute | solution.py:627
  26.4 7.1 %collective-permute-start.5 = (f32[208,256]{1,0:T(8,128)S(1)}, f32[208,256]{1,0:T(8,128)S(1)}, u32[]{:S(2)}, u32[]{:S(2)}) collective-permute-start(f32[208,256]{1,0:T(8,128)S(1)} %get-tuple-element.40.refs_6_), channel_id=1, source_target_pairs={{0,8},{4,12},{8,0},{12,4},{16,24},{20,28},{24,16},{28,20},{1,9},{5... | collective-permute-start | bytes 638984 | tf_op jit(solution)/shard_map/ppermute | solution.py:660
  33.5 1.5 %collective-permute-start.7 = (f32[208,256]{1,0:T(8,128)S(1)}, f32[208,256]{1,0:T(8,128)S(1)}, u32[]{:S(2)}, u32[]{:S(2)}) collective-permute-start(f32[208,256]{1,0:T(8,128)S(1)} %add_add_fusion.refs_2_.refs_12_), channel_id=1, source_target_pairs={{0,4},{4,0},{8,12},{12,8},{16,20},{20,16},{24,28},{28,24},{1,5},{5... | collective-permute-start | bytes 638984 | tf_op jit(solution)/shard_map/ppermute | solution.py:663
  35.8 5.3 %collective-permute-start.8 = (f32[160,128]{1,0:T(8,128)S(1)}, f32[160,128]{1,0:T(8,128)S(1)}, u32[]{:S(2)}, u32[]{:S(2)}) collective-permute-start(f32[160,128]{1,0:T(8,128)S(1)} %merge.1), channel_id=1, source_target_pairs={{0,16},{4,20},{8,24},{12,28},{16,0},{20,4},{24,8},{28,12},{1,17},{... | collective-permute-start | bytes 245768 | tf_op jit(solution)/shard_map/ppermute | solution.py:655
  41.2 1.3 %collective-permute-start.9 = (f32[160,128]{1,0:T(8,128)S(1)}, f32[160,128]{1,0:T(8,128)S(1)}, u32[]{:S(2)}, u32[]{:S(2)}) collective-permute-start(f32[160,128]{1,0:T(8,128)S(1)} %broadcast_add_fusion.1.refs_0_), channel_id=1, source_target_pairs={{0,4},{4,0},{8,12},{12,8},{16,20},{20,16},{24,28},{28,24},{1,5},{5... | collective-permute-start | bytes 245768 | tf_op jit(solution)/shard_map/ppermute | solution.py:658

commit v20 on v18

--- a/solution.py
+++ b/solution.py
@@ -26,7 +26,10 @@
     a = a if isinstance(a, tuple) else split(a)
     b = b if isinstance(b, tuple) else split(b)
     dot = functools.partial(lax.dot_general, dimension_numbers=dims, preferred_element_type=F32)
-    return dot(a[0], b[0]) + (dot(a[0], b[1]) + dot(a[1], b[0]))
+    free = 1 - dims[0][0][0]
+    rows = a[0].shape[free]
+    stacked = dot(jnp.concatenate(a, free), b[0])
+    return stacked[:rows] + (dot(a[0], b[1]) + stacked[rows:])
 
 
 def carry(link_t, cov, base):

time: 42.3 us -> 42 us (level)
  Pallas kernels: 16.2 us -> 15.5 us
    pallas_call x14, Pallas kernels: 16.2 us -> 15.5 us  [call(): pl.pallas_call(inner, out_shape=[*outs, *(jax.ShapeDtypeStruct(a.shape, a...]
  transfers between devices with their start and end apart: 12 -> 12, of which waited for: 9 -> 9; matrix products, arithmetic and copies ran while one was open for 0% -> 0% of each run, Pallas kernels for 31% -> 30%
where the time goes in v20:
time: 42 us; the launch traced here: 41.9 us
  Pallas kernels  15.5 us (37%)
  waiting for transfers between devices  15.4 us (37%)
  starting transfers between devices  10.1 us (24%)
  between operations  0.82 us (2%)
    pallas_call x14, Pallas kernels, call(): pl.pallas_call(inner, out_shape=[*outs, *(jax.ShapeDtypeStruct(a.shape, a...  15.5 us
    ppermute x4, waiting for transfers between devices, turn(): lax.ppermute(x, axis, [(i, (i + distance) % count) for i in range(count)])  8.8 us
    ppermute x4, starting transfers between devices, turn(): lax.ppermute(x, axis, [(i, (i + distance) % count) for i in range(count)])  5.28 us
    ppermute x2, starting transfers between devices, body(): got = lax.ppermute(send, 'seg', partner)  2.64 us
    ppermute x1, waiting for transfers between devices, body(): other_whole = lax.ppermute(own_whole, 'seg', swap)  1.9 us
    ppermute x1, starting transfers between devices, body(): got_t = lax.ppermute(send_t, 'seg', partner)  1.59 us
    ppermute x1, waiting for transfers between devices, body(): lax.ppermute(got, 'seg', swap)  1.26 us
    ppermute x1, waiting for transfers between devices, body(): after = (got, lax.ppermute(got, 'seg', swap))  1.26 us
  transfers between devices with their start and end apart: 12, of which 9 were waited for; matrix products, arithmetic and copies ran while one was open for 0% of the time, Pallas kernels for 30%

profile of v20, /device:TPU:0, one launch (start us, length us, event | category | flops | bytes accessed | tf_op | source)
XLA Modules:
  0.0 41.9 jit_solution(8371509837777049942)
XLA Ops:
  0.6 0.0 copy-start
  0.6 3.1 %collective-permute-start = (f32[2,64,512]{2,1,0:T(8,128)}, f32[2,64,512]{2,1,0:T(8,128)S(1)}, u32[]{:S(2)}, u32[]{:S(2)}) collective-permute-start(f32[2,64,512]{2,1,0:T(8,128)} %refs_2_.3), channel_id=1, source_target_pairs={{0,1},{1,2},{2,3},{3,0},{4,5},{5,6},{6,7},{7,4},{8,9},{9,10},{10,1... | collective-permute-start | bytes 786440 | tf_op jit(solution)/shard_map/ppermute | solution.py:487
  3.7 0.0 collective-permute-start.1
  3.7 1.6 %load.1 = (f32[2,512,512]{2,1,0:T(8,128)S(1)}, bf16[512,256]{1,0:T(8,128)(2,1)S(1)}, bf16[512,256]{1,0:T(8,128)(2,1)S(1)}, f32[2,64,256]{2,1,0:T(8,128)S(1)}, f32[2,64,256]{2,1,0:T(8,128)S(1)}) custom-call(s32[2,4]{1,0:T(2,128)} %refs_0_.11, s32[2,4]{1,0:T(2,128)} %refs_1_.7, f32[2,512,512]{2,1,0:T(8,128)} %refs_2_.2), custom_call_target="tpu_custom_call" | custom-call | bytes 5505088 | tf_op jit(solution)/shard_map/load/pallas_call | solution.py:145
  5.4 0.0 copy-start.1
  5.4 2.4 %collective-permute-done.1.refs_1_.refs_3_.refs_2_ = s32[2,4]{1,0:T(2,128)S(1)} collective-permute-done((s32[2,4]{1,0:T(2,128)}, s32[2,4]{1,0:T(2,128)S(1)}, u32[]{:S(2)}, u32[]{:S(2)}) %collective-permute-start.1) | collective-permute-done | bytes 64 | tf_op jit(solution)/shard_map/ppermute | solution.py:487
  7.8 0.6 %prior.2 = (f32[256,256]{1,0:T(8,128)S(1)}, f32[128,512]{1,0:T(8,128)S(1)}, f32[1,1,512]{2,1,0:T(1,128)S(1)}) custom-call(bf16[512,256]{1,0:T(8,128)(2,1)S(1)} %get-tuple-element.31.refs_5_.refs_0_.refs_4_, bf16[512,256]{1,0:T(8,128)(2,1)S(1)} %get-tuple-element.32.refs_6_.refs_1_.refs_5_, f32[2,512,512]{2,1,0:T(8,128)S(1)} %get-tuple-element.28.refs_2_.refs_1_.refs_3_, ...), custom_call_target="tpu_custom_call" | custom-call | bytes 3672064 | tf_op jit(solution)/shard_map/prior/pallas_call | solution.py:145
  8.5 0.0 copy-done
  8.5 2.1 %collective-permute-start.2 = (f32[2,64,512]{2,1,0:T(8,128)S(1)}, f32[2,64,512]{2,1,0:T(8,128)S(1)}, u32[]{:S(2)}, u32[]{:S(2)}) collective-permute-start(f32[2,64,512]{2,1,0:T(8,128)S(1)} %broadcast_add_fusion), channel_id=1, source_target_pairs={{0,3},{1,0},{2,1},{3,2},{4,7},{5,4},{6,5},{7,6},{8,11},{9,8},{10,9... | collective-permute-start | bytes 786440 | tf_op jit(solution)/shard_map/ppermute | solution.py:487
  10.7 0.0 copy-done.1
  10.7 0.9 %pick.1 = (bf16[512,256]{1,0:T(8,128)(2,1)S(1)}, bf16[512,256]{1,0:T(8,128)(2,1)S(1)}) custom-call(s32[2,4]{1,0:T(2,128)S(1)} %copy-done.1, s32[2,4]{1,0:T(2,128)S(1)} %collective-permute-done.1.refs_1_.refs_3_.refs_2_, f32[2,512,512]{2,1,0:T(8,128)S(1)} %get-tuple-element.28.refs_2_.refs_1_.refs_3_), custom_call_target="tpu_custom_call" | custom-call | bytes 3145728 | tf_op jit(solution)/shard_map/pick/pallas_call | solution.py:145
  11.6 0.8 %collective-permute-done.refs_2_.refs_0_.refs_3_.refs_4_ = f32[2,64,512]{2,1,0:T(8,128)S(1)} collective-permute-done((f32[2,64,512]{2,1,0:T(8,128)}, f32[2,64,512]{2,1,0:T(8,128)S(1)}, u32[]{:S(2)}, u32[]{:S(2)}) %collective-permute-start) | collective-permute-done | bytes 262176 | tf_op jit(solution)/shard_map/ppermute | solution.py:487
  12.4 0.3 chosen.1
  12.7 0.0 copy-start.2
  12.7 0.1 collective-permute-start.3
  12.8 1.1 %prior.3 = (f32[256,256]{1,0:T(8,128)S(1)}, f32[128,512]{1,0:T(8,128)S(1)}, f32[1,1,512]{2,1,0:T(1,128)}) custom-call(bf16[512,256]{1,0:T(8,128)(2,1)S(1)} %get-tuple-element.29.refs_3_.refs_2_.refs_0_, bf16[512,256]{1,0:T(8,128)(2,1)S(1)} %get-tuple-element.30.refs_4_.refs_3_.refs_1_, f32[2,512,512]{2,1,0:T(8,128)S(1)} %get-tuple-element.28.refs_2_.refs_1_.refs_3_, ...), custom_call_target="tpu_custom_call" | custom-call | bytes 3672064 | tf_op jit(solution)/shard_map/prior/pallas_call | solution.py:145
  13.9 0.0 copy-done.2
  13.9 1.0 %links.1.refs_0_ = f32[2,256,256]{2,1,0:T(8,128)S(1)} custom-call(s32[2,4]{1,0:T(2,128)S(1)} %copy-done.2, f32[2,64,512]{2,1,0:T(8,128)S(1)} %copy-done, f32[2,64,512]{2,1,0:T(8,128)S(1)} %collective-permute-done.refs_2_.refs_0_.refs_3_.refs_4_, bf16[512,256]{1,0:T(8,128)(2,1)S(1)} %get-tuple-element.29.refs_3_.refs_2_.refs_0_, ...), custom_call_target="tpu_custom_call" | custom-call | bytes 3145728 | tf_op jit(solution)/shard_map/links/pallas_call | solution.py:145
  14.9 4.3 %collective-permute-done.2.refs_0_.refs_4_.refs_5_ = f32[2,64,512]{2,1,0:T(8,128)S(1)} collective-permute-done((f32[2,64,512]{2,1,0:T(8,128)S(1)}, f32[2,64,512]{2,1,0:T(8,128)S(1)}, u32[]{:S(2)}, u32[]{:S(2)}) %collective-permute-start.2) | collective-permute-done | bytes 262176 | tf_op jit(solution)/shard_map/ppermute | solution.py:487
  19.3 0.3 second.1.refs_1_
  19.6 1.2 %collective-permute-done.3.refs_2_.refs_10_ = f32[2,64,256]{2,1,0:T(8,128)S(1)} collective-permute-done((f32[2,64,256]{2,1,0:T(8,128)S(1)}, f32[2,64,256]{2,1,0:T(8,128)S(1)}, u32[]{:S(2)}, u32[]{:S(2)}) %collective-permute-start.3) | collective-permute-done | bytes 131104 | tf_op jit(solution)/shard_map/ppermute | solution.py:487
  20.8 0.6 %segment.1 = (f32[2,256,256]{2,1,0:T(8,128)S(1)}, f32[512,256]{1,0:T(8,128)S(1)}) custom-call(f32[2,256,256]{2,1,0:T(8,128)S(1)} %links.1.refs_0_, f32[2,64,256]{2,1,0:T(8,128)S(1)} %second.1.refs_1_, f32[2,64,256]{2,1,0:T(8,128)S(1)} %collective-permute-done.3.refs_2_.refs_10_, f32[256,256]{1,0:T(8,128)S(1)} %get-tuple-element.36.refs_3_, ...), custom_call_target="tpu_custom_call" | custom-call | flops 301989888 | bytes 2359296 | tf_op jit(solution)/shard_map/segment/pallas_call | solution.py:145
  21.4 0.1 collective-permute-start.4
  21.5 1.9 %collective-permute-done.4.refs_1_.refs_7_ = f32[512,256]{1,0:T(8,128)S(1)} collective-permute-done((f32[512,256]{1,0:T(8,128)S(1)}, f32[512,256]{1,0:T(8,128)S(1)}, u32[]{:S(2)}, u32[]{:S(2)}) %collective-permute-start.4) | collective-permute-done | bytes 524320 | tf_op jit(solution)/shard_map/ppermute | solution.py:582
  23.4 0.6 %chip.1 = (f32[256,256]{1,0:T(8,128)S(1)}, f32[256,256]{1,0:T(8,128)S(1)}, f32[160,128]{1,0:T(8,128)S(1)}, f32[128,256]{1,0:T(8,128)S(1)}) custom-call(f32[512,256]{1,0:T(8,128)S(1)} %get-tuple-element.38.refs_0_, f32[512,256]{1,0:T(8,128)S(1)} %collective-permute-done.4.refs_1_.refs_7_), custom_call_target="tpu_custom_call" | custom-call | flops 301989888 | bytes 1785856 | tf_op jit(solution)/shard_map/chip/pallas_call | solution.py:145
  24.0 1.6 %collective-permute-start.5 = (f32[128,256]{1,0:T(8,128)S(1)}, f32[128,256]{1,0:T(8,128)S(1)}, u32[]{:S(2)}, u32[]{:S(2)}) collective-permute-start(f32[128,256]{1,0:T(8,128)S(1)} %get-tuple-element.41), channel_id=1, source_target_pairs={{0,8},{4,12},{8,0},{12,4},{16,24},{20,28},{24,16},{28,20},{1,9},{5... | collective-permute-start | bytes 393224 | tf_op jit(solution)/shard_map/ppermute | solution.py:641
  25.6 0.5 %collective-permute-start.7 = (f32[160,128]{1,0:T(8,128)S(1)}, f32[160,128]{1,0:T(8,128)S(1)}, u32[]{:S(2)}, u32[]{:S(2)}) collective-permute-start(f32[160,128]{1,0:T(8,128)S(1)} %get-tuple-element.42.refs_6_), channel_id=1, source_target_pairs={{0,8},{4,12},{8,0},{12,4},{16,24},{20,28},{24,16},{28,20},{1,9},{5... | collective-permute-start | bytes 245768 | tf_op jit(solution)/shard_map/ppermute | solution.py:635
  26.1 1.5 %maps.1 = (f32[2,256,512]{2,1,0:T(8,128)S(1)}, f32[1,128]{1,0:T(1,128)S(1)}) custom-call(s32[2,4]{1,0:T(2,128)S(1)} %copy-done.2, f32[2,512,512]{2,1,0:T(8,128)S(1)} %get-tuple-element.28.refs_2_.refs_1_.refs_3_, f32[2,64,512]{2,1,0:T(8,128)S(1)} %copy-done, f32[2,64,512]{2,1,0:T(8,128)S(1)} %collective-permute-done.refs_2_.refs_0_.refs_3_.refs_4_, ...), custom_call_target="tpu_custom_call" | custom-call | flops 805306368 | bytes 3932672 | tf_op jit(solution)/shard_map/maps/pallas_call | solution.py:145
  27.6 1.2 %rest.1 = f32[2,64,256]{2,1,0:T(8,128)S(1)} custom-call(s32[2,4]{1,0:T(2,128)S(1)} %copy-done.2, s32[2,4]{1,0:T(2,128)S(1)} %copy-done.1, s32[2,4]{1,0:T(2,128)S(1)} %collective-permute-done.1.refs_1_.refs_3_.refs_2_, f32[2,512,512]{2,1,0:T(8,128)S(1)} %get-tuple-element.28.refs_2_.refs_1_.refs_3_, ...), custom_call_target="tpu_custom_call" | custom-call | flops 201326592 | bytes 2834432 | tf_op jit(solution)/shard_map/rest/pallas_call | solution.py:145
  28.8 0.3 collective-permute-start.10
  29.2 1.2 %collective-permute-done.5.refs_2_.refs_12_ = f32[128,256]{1,0:T(8,128)S(1)} collective-permute-done((f32[128,256]{1,0:T(8,128)S(1)}, f32[128,256]{1,0:T(8,128)S(1)}, u32[]{:S(2)}, u32[]{:S(2)}) %collective-permute-start.5) | collective-permute-done | bytes 131104 | tf_op jit(solution)/shard_map/ppermute | solution.py:641
  30.4 0.0 collective-permute-start.6
  30.4 1.0 %collective-permute-done.7 = f32[160,128]{1,0:T(8,128)S(1)} collective-permute-done((f32[160,128]{1,0:T(8,128)S(1)}, f32[160,128]{1,0:T(8,128)S(1)}, u32[]{:S(2)}, u32[]{:S(2)}) %collective-permute-start.7) | collective-permute-done | bytes 81952 | tf_op jit(solution)/shard_map/ppermute | solution.py:635
  31.4 0.1 collective-permute-start.8
  31.4 1.3 %collective-permute-done.8.refs_5_.refs_15_ = f32[160,128]{1,0:T(8,128)S(1)} collective-permute-done((f32[160,128]{1,0:T(8,128)S(1)}, f32[160,128]{1,0:T(8,128)S(1)}, u32[]{:S(2)}, u32[]{:S(2)}) %collective-permute-start.8) | collective-permute-done | bytes 81952 | tf_op jit(solution)/shard_map/ppermute | solution.py:644
  32.7 0.0 collective-permute-done.6.refs_3_.refs_13_
  32.7 0.8 %merge.1 = f32[160,128]{1,0:T(8,128)S(1)} custom-call(f32[256,256]{1,0:T(8,128)S(1)} %get-tuple-element.39.refs_0_, f32[256,256]{1,0:T(8,128)S(1)} %get-tuple-element.40.refs_1_, f32[128,256]{1,0:T(8,128)S(1)} %collective-permute-done.5.refs_2_.refs_12_, f32[128,256]{1,0:T(8,128)S(1)} %collective-permute-done.6.refs_3_.refs_13_, ...), custom_call_target="tpu_custom_call" | custom-call | flops 301989888 | bytes 1032192 | tf_op jit(solution)/shard_map/merge/pallas_call | solution.py:145
  33.5 2.1 %collective-permute-start.9 = (f32[160,128]{1,0:T(8,128)S(1)}, f32[160,128]{1,0:T(8,128)S(1)}, u32[]{:S(2)}, u32[]{:S(2)}) collective-permute-start(f32[160,128]{1,0:T(8,128)S(1)} %merge.1), channel_id=1, source_target_pairs={{0,16},{4,20},{8,24},{12,28},{16,0},{20,4},{24,8},{28,12},{1,17},{... | collective-permute-start | bytes 245768 | tf_op jit(solution)/shard_map/ppermute | solution.py:635
  35.7 0.0 collective-permute-done.10.refs_11_
  35.7 2.9 %prepare.1 = (bf16[384,256]{1,0:T(8,128)(2,1)S(1)}, bf16[384,256]{1,0:T(8,128)(2,1)S(1)}, bf16[2,256,512]{2,1,0:T(8,128)(2,1)S(1)}, bf16[2,256,512]{2,1,0:T(8,12...) custom-call(s32[2,4]{1,0:T(2,128)S(1)} %copy-done.2, s32[2,4]{1,0:T(2,128)S(1)} %copy-done.1, ...), custom_call_target="tpu_custom_call" | custom-call | flops 1459617792 | bytes 7504384 | tf_op jit(solution)/shard_map/prepare/pallas_call | solution.py:145
  38.6 0.0 collective-permute-done.9
  38.7 0.1 collective-permute-start.11
  38.7 1.3 %collective-permute-done.11.refs_1_ = f32[160,128]{1,0:T(8,128)S(1)} collective-permute-done((f32[160,128]{1,0:T(8,128)S(1)}, f32[160,128]{1,0:T(8,128)S(1)}, u32[]{:S(2)}, u32[]{:S(2)}) %collective-permute-start.11) | collective-permute-done | bytes 81952 | tf_op jit(solution)/shard_map/ppermute | solution.py:639
  40.0 1.9 %finish.1 = (f32[2,128,512]{2,1,0:T(8,128)}, f32[2,64,512]{2,1,0:T(8,128)}) custom-call(f32[160,128]{1,0:T(8,128)S(1)} %broadcast_add_fusion.1.refs_0_, f32[160,128]{1,0:T(8,128)S(1)} %collective-permute-done.11.refs_1_, bf16[384,256]{1,0:T(8,128)(2,1)S(1)} %get-tuple-element.49.refs_2_, bf16[384,256]{1,0:T(8,128)(2,1)S(1)} %get-tuple-element.50.refs_3_, ...), custom_call_target="tpu_custom_call" | custom-call | flops 452984832 | bytes 4620288 | tf_op jit(solution)/shard_map/finish/pallas_call | solution.py:145
  (3 shorter events, 0.0 us)
Async XLA Ops:
  0.6 7.8 %copy-start = (f32[2,64,512]{2,1,0:T(8,128)S(1)}, f32[2,64,512]{2,1,0:T(8,128)}, u32[]{:S(2)}) copy-start(f32[2,64,512]{2,1,0:T(8,128)} %refs_2_.3) | copy-start | bytes 786436
  0.6 11.8 %collective-permute-start = (f32[2,64,512]{2,1,0:T(8,128)}, f32[2,64,512]{2,1,0:T(8,128)S(1)}, u32[]{:S(2)}, u32[]{:S(2)}) collective-permute-start(f32[2,64,512]{2,1,0:T(8,128)} %refs_2_.3), channel_id=1, source_target_pairs={{0,1},{1,2},{2,3},{3,0},{4,5},{5,6},{6,7},{7,4},{8,9},{9,10},{10,1... | collective-permute-start | bytes 786440 | tf_op jit(solution)/shard_map/ppermute | solution.py:487
  3.7 4.1 %collective-permute-start.1 = (s32[2,4]{1,0:T(2,128)}, s32[2,4]{1,0:T(2,128)S(1)}, u32[]{:S(2)}, u32[]{:S(2)}) collective-permute-start(s32[2,4]{1,0:T(2,128)} %refs_1_.7), channel_id=1, source_target_pairs={{0,4},{4,8},{8,12},{12,16},{16,20},{20,24},{24,28},{28,0},{1,5},{5... | collective-permute-start | bytes 104 | tf_op jit(solution)/shard_map/ppermute | solution.py:487
  5.4 5.3 %copy-start.1 = (s32[2,4]{1,0:T(2,128)S(1)}, s32[2,4]{1,0:T(2,128)}, u32[]{:S(2)}) copy-start(s32[2,4]{1,0:T(2,128)} %refs_1_.7) | copy-start | bytes 100
  8.5 10.8 %collective-permute-start.2 = (f32[2,64,512]{2,1,0:T(8,128)S(1)}, f32[2,64,512]{2,1,0:T(8,128)S(1)}, u32[]{:S(2)}, u32[]{:S(2)}) collective-permute-start(f32[2,64,512]{2,1,0:T(8,128)S(1)} %broadcast_add_fusion), channel_id=1, source_target_pairs={{0,3},{1,0},{2,1},{3,2},{4,7},{5,4},{6,5},{7,6},{8,11},{9,8},{10,9... | collective-permute-start | bytes 786440 | tf_op jit(solution)/shard_map/ppermute | solution.py:487
  12.7 1.2 %copy-start.2 = (s32[2,4]{1,0:T(2,128)S(1)}, s32[2,4]{1,0:T(2,128)}, u32[]{:S(2)}) copy-start(s32[2,4]{1,0:T(2,128)} %refs_0_.11) | copy-start | bytes 100
  12.7 8.0 %collective-permute-start.3 = (f32[2,64,256]{2,1,0:T(8,128)S(1)}, f32[2,64,256]{2,1,0:T(8,128)S(1)}, u32[]{:S(2)}, u32[]{:S(2)}) collective-permute-start(f32[2,64,256]{2,1,0:T(8,128)S(1)} %chosen.1), channel_id=1, source_target_pairs={{0,1},{1,2},{2,3},{3,0},{4,5},{5,6},{6,7},{7,4},{8,9},{9,10},{10,1... | collective-permute-start | bytes 393224 | tf_op jit(solution)/shard_map/ppermute | solution.py:487
  21.4 2.0 %collective-permute-start.4 = (f32[512,256]{1,0:T(8,128)S(1)}, f32[512,256]{1,0:T(8,128)S(1)}, u32[]{:S(2)}, u32[]{:S(2)}) collective-permute-start(f32[512,256]{1,0:T(8,128)S(1)} %get-tuple-element.38.refs_0_), channel_id=1, source_target_pairs={{0,4},{4,0},{8,12},{12,8},{16,20},{20,16},{24,28},{28,24},{1,5},{5... | collective-permute-start | bytes 1572872 | tf_op jit(solution)/shard_map/ppermute | solution.py:582
  24.0 6.4 %collective-permute-start.5 = (f32[128,256]{1,0:T(8,128)S(1)}, f32[128,256]{1,0:T(8,128)S(1)}, u32[]{:S(2)}, u32[]{:S(2)}) collective-permute-start(f32[128,256]{1,0:T(8,128)S(1)} %get-tuple-element.41), channel_id=1, source_target_pairs={{0,8},{4,12},{8,0},{12,4},{16,24},{20,28},{24,16},{28,20},{1,9},{5... | collective-permute-start | bytes 393224 | tf_op jit(solution)/shard_map/ppermute | solution.py:641
  25.6 5.8 %collective-permute-start.7 = (f32[160,128]{1,0:T(8,128)S(1)}, f32[160,128]{1,0:T(8,128)S(1)}, u32[]{:S(2)}, u32[]{:S(2)}) collective-permute-start(f32[160,128]{1,0:T(8,128)S(1)} %get-tuple-element.42.refs_6_), channel_id=1, source_target_pairs={{0,8},{4,12},{8,0},{12,4},{16,24},{20,28},{24,16},{28,20},{1,9},{5... | collective-permute-start | bytes 245768 | tf_op jit(solution)/shard_map/ppermute | solution.py:635
  28.8 6.9 %collective-permute-start.10 = (f32[2,64,256]{2,1,0:T(8,128)S(1)}, f32[2,64,256]{2,1,0:T(8,128)S(1)}, u32[]{:S(2)}, u32[]{:S(2)}) collective-permute-start(f32[2,64,256]{2,1,0:T(8,128)S(1)} %rest.1), channel_id=1, source_target_pairs={{0,1},{1,0},{2,3},{3,2},{4,5},{5,4},{6,7},{7,6},{8,9},{9,8},{10,11... | collective-permute-start | bytes 393224 | tf_op jit(solution)/shard_map/ppermute | solution.py:608
  30.4 2.3 %collective-permute-start.6 = (f32[128,256]{1,0:T(8,128)S(1)}, f32[128,256]{1,0:T(8,128)S(1)}, u32[]{:S(2)}, u32[]{:S(2)}) collective-permute-start(f32[128,256]{1,0:T(8,128)S(1)} %collective-permute-done.5.refs_2_.refs_12_), channel_id=1, source_target_pairs={{0,4},{4,0},{8,12},{12,8},{16,20},{20,16},{24,28},{28,24},{1,5},{5... | collective-permute-start | bytes 393224 | tf_op jit(solution)/shard_map/ppermute | solution.py:644
  31.4 1.3 %collective-permute-start.8 = (f32[160,128]{1,0:T(8,128)S(1)}, f32[160,128]{1,0:T(8,128)S(1)}, u32[]{:S(2)}, u32[]{:S(2)}) collective-permute-start(f32[160,128]{1,0:T(8,128)S(1)} %broadcast_add_fusion.2.refs_4_.refs_14_), channel_id=1, source_target_pairs={{0,4},{4,0},{8,12},{12,8},{16,20},{20,16},{24,28},{28,24},{1,5},{5... | collective-permute-start | bytes 245768 | tf_op jit(solution)/shard_map/ppermute | solution.py:644
  33.5 5.1 %collective-permute-start.9 = (f32[160,128]{1,0:T(8,128)S(1)}, f32[160,128]{1,0:T(8,128)S(1)}, u32[]{:S(2)}, u32[]{:S(2)}) collective-permute-start(f32[160,128]{1,0:T(8,128)S(1)} %merge.1), channel_id=1, source_target_pairs={{0,16},{4,20},{8,24},{12,28},{16,0},{20,4},{24,8},{28,12},{1,17},{... | collective-permute-start | bytes 245768 | tf_op jit(solution)/shard_map/ppermute | solution.py:635
  38.7 1.3 %collective-permute-start.11 = (f32[160,128]{1,0:T(8,128)S(1)}, f32[160,128]{1,0:T(8,128)S(1)}, u32[]{:S(2)}, u32[]{:S(2)}) collective-permute-start(f32[160,128]{1,0:T(8,128)S(1)} %broadcast_add_fusion.1.refs_0_), channel_id=1, source_target_pairs={{0,4},{4,0},{8,12},{12,8},{16,20},{20,16},{24,28},{28,24},{1,5},{5... | collective-permute-start | bytes 245768 | tf_op jit(solution)/shard_map/ppermute | solution.py:639

commit v21 on v20

--- a/solution.py
+++ b/solution.py
@@ -449,7 +449,7 @@
 def finish_kernel(levels, after_ref, after_other_ref, *refs):
     left_high, left_low, right_high, right_low, const_ref, diag_hbm, off_hbm = refs[:7]
     diag_ref, off_ref, sems = refs[7:]
-    panels, total, _ = const_ref.shape
+    panels, total, width = const_ref.shape
     rows = off_ref.shape[1]
     chip = lax.axis_index("seg") // 2
     after = from_halves(after_ref[...], after_other_ref[...])
@@ -458,14 +458,18 @@
     copies = []
     for p in range(panels):
         part = slice(p * total, (p + 1) * total)
-        right = (right_high[p], right_low[p])
-        result = mm((inner[0][part], inner[1][part]), right) + const_ref[p]
-        diag_ref[p] = result[rows:]
-        off_ref[p] = result[:rows]
-        copies.append(pltpu.make_async_copy(diag_ref.at[p], diag_hbm.at[p], sems.at[p, 0]))
-        copies.append(pltpu.make_async_copy(off_ref.at[p], off_hbm.at[p], sems.at[p, 1]))
-        copies[-2].start()
-        copies[-1].start()
+        for h, columns in enumerate((slice(0, width // 2), slice(width // 2, width))):
+            right = (right_high[p, :, columns], right_low[p, :, columns])
+            result = mm((inner[0][part], inner[1][part]), right) + const_ref[p, :, columns]
+            off_ref[p, :, columns] = result[:rows]
+            diag_ref[p, :, columns] = result[rows:]
+            for i, (ref, hbm) in enumerate(((off_ref, off_hbm), (diag_ref, diag_hbm))):
+                copies.append(
+                    pltpu.make_async_copy(
+                        ref.at[p, :, columns], hbm.at[p, :, columns], sems.at[p, h, i]
+                    )
+                )
+                copies[-1].start()
     for copy in copies:
         copy.wait()
 
@@ -673,7 +677,7 @@
         scratch=[
             pltpu.VMEM((panels, own_cols, width), F32),
             pltpu.VMEM((panels, rows, width), F32),
-            pltpu.SemaphoreType.DMA((panels, 2)),
+            pltpu.SemaphoreType.DMA((panels, 2, 2)),
         ],
         flops=6 * panels * (rows + own_cols) * size * (size + width),
         name="finish",

time: 42 us -> 42 us (level)
  no operation moved by 1% of the time
where the time goes in v21:
time: 42 us; the launch traced here: 41.8 us
  Pallas kernels  15.4 us (37%)
  waiting for transfers between devices  15.4 us (37%)
  starting transfers between devices  10.1 us (24%)
  between operations  0.82 us (2%)
    pallas_call x14, Pallas kernels, call(): pl.pallas_call(inner, out_shape=[*outs, *(jax.ShapeDtypeStruct(a.shape, a...  15.4 us
    ppermute x4, waiting for transfers between devices, turn(): lax.ppermute(x, axis, [(i, (i + distance) % count) for i in range(count)])  8.8 us
    ppermute x4, starting transfers between devices, turn(): lax.ppermute(x, axis, [(i, (i + distance) % count) for i in range(count)])  5.28 us
    ppermute x2, starting transfers between devices, body(): got = lax.ppermute(send, 'seg', partner)  2.64 us
    ppermute x1, waiting for transfers between devices, body(): other_whole = lax.ppermute(own_whole, 'seg', swap)  1.9 us
    ppermute x1, starting transfers between devices, body(): got_t = lax.ppermute(send_t, 'seg', partner)  1.59 us
    ppermute x1, waiting for transfers between devices, body(): lax.ppermute(got, 'seg', swap)  1.26 us
    ppermute x1, waiting for transfers between devices, body(): after = (got, lax.ppermute(got, 'seg', swap))  1.26 us
  transfers between devices with their start and end apart: 12, of which 9 were waited for; matrix products, arithmetic and copies ran while one was open for 0% of the time, Pallas kernels for 30%

profile of v21, /device:TPU:0, one launch (start us, length us, event | category | flops | bytes accessed | tf_op | source)
XLA Modules:
  0.0 41.8 jit_solution(12592929173040423375)
XLA Ops:
  0.6 0.0 copy-start
  0.6 3.1 %collective-permute-start = (f32[2,64,512]{2,1,0:T(8,128)}, f32[2,64,512]{2,1,0:T(8,128)S(1)}, u32[]{:S(2)}, u32[]{:S(2)}) collective-permute-start(f32[2,64,512]{2,1,0:T(8,128)} %refs_2_.3), channel_id=1, source_target_pairs={{0,1},{1,2},{2,3},{3,0},{4,5},{5,6},{6,7},{7,4},{8,9},{9,10},{10,1... | collective-permute-start | bytes 786440 | tf_op jit(solution)/shard_map/ppermute | solution.py:491
  3.7 0.0 collective-permute-start.1
  3.7 1.6 %load.1 = (f32[2,512,512]{2,1,0:T(8,128)S(1)}, bf16[512,256]{1,0:T(8,128)(2,1)S(1)}, bf16[512,256]{1,0:T(8,128)(2,1)S(1)}, f32[2,64,256]{2,1,0:T(8,128)S(1)}, f32[2,64,256]{2,1,0:T(8,128)S(1)}) custom-call(s32[2,4]{1,0:T(2,128)} %refs_0_.11, s32[2,4]{1,0:T(2,128)} %refs_1_.7, f32[2,512,512]{2,1,0:T(8,128)} %refs_2_.2), custom_call_target="tpu_custom_call" | custom-call | bytes 5505088 | tf_op jit(solution)/shard_map/load/pallas_call | solution.py:145
  5.4 0.0 copy-start.1
  5.4 2.4 %collective-permute-done.1.refs_1_.refs_3_.refs_2_ = s32[2,4]{1,0:T(2,128)S(1)} collective-permute-done((s32[2,4]{1,0:T(2,128)}, s32[2,4]{1,0:T(2,128)S(1)}, u32[]{:S(2)}, u32[]{:S(2)}) %collective-permute-start.1) | collective-permute-done | bytes 64 | tf_op jit(solution)/shard_map/ppermute | solution.py:491
  7.8 0.6 %prior.2 = (f32[256,256]{1,0:T(8,128)S(1)}, f32[128,512]{1,0:T(8,128)S(1)}, f32[1,1,512]{2,1,0:T(1,128)S(1)}) custom-call(bf16[512,256]{1,0:T(8,128)(2,1)S(1)} %get-tuple-element.31.refs_5_.refs_0_.refs_4_, bf16[512,256]{1,0:T(8,128)(2,1)S(1)} %get-tuple-element.32.refs_6_.refs_1_.refs_5_, f32[2,512,512]{2,1,0:T(8,128)S(1)} %get-tuple-element.28.refs_2_.refs_1_.refs_3_, ...), custom_call_target="tpu_custom_call" | custom-call | bytes 3672064 | tf_op jit(solution)/shard_map/prior/pallas_call | solution.py:145
  8.5 0.0 copy-done
  8.5 2.1 %collective-permute-start.2 = (f32[2,64,512]{2,1,0:T(8,128)S(1)}, f32[2,64,512]{2,1,0:T(8,128)S(1)}, u32[]{:S(2)}, u32[]{:S(2)}) collective-permute-start(f32[2,64,512]{2,1,0:T(8,128)S(1)} %broadcast_add_fusion), channel_id=1, source_target_pairs={{0,3},{1,0},{2,1},{3,2},{4,7},{5,4},{6,5},{7,6},{8,11},{9,8},{10,9... | collective-permute-start | bytes 786440 | tf_op jit(solution)/shard_map/ppermute | solution.py:491
  10.7 0.0 copy-done.1
  10.7 0.9 %pick.1 = (bf16[512,256]{1,0:T(8,128)(2,1)S(1)}, bf16[512,256]{1,0:T(8,128)(2,1)S(1)}) custom-call(s32[2,4]{1,0:T(2,128)S(1)} %copy-done.1, s32[2,4]{1,0:T(2,128)S(1)} %collective-permute-done.1.refs_1_.refs_3_.refs_2_, f32[2,512,512]{2,1,0:T(8,128)S(1)} %get-tuple-element.28.refs_2_.refs_1_.refs_3_), custom_call_target="tpu_custom_call" | custom-call | bytes 3145728 | tf_op jit(solution)/shard_map/pick/pallas_call | solution.py:145
  11.6 0.8 %collective-permute-done.refs_2_.refs_0_.refs_3_.refs_4_ = f32[2,64,512]{2,1,0:T(8,128)S(1)} collective-permute-done((f32[2,64,512]{2,1,0:T(8,128)}, f32[2,64,512]{2,1,0:T(8,128)S(1)}, u32[]{:S(2)}, u32[]{:S(2)}) %collective-permute-start) | collective-permute-done | bytes 262176 | tf_op jit(solution)/shard_map/ppermute | solution.py:491
  12.4 0.3 chosen.1
  12.7 0.0 copy-start.2
  12.7 0.1 collective-permute-start.3
  12.8 1.1 %prior.3 = (f32[256,256]{1,0:T(8,128)S(1)}, f32[128,512]{1,0:T(8,128)S(1)}, f32[1,1,512]{2,1,0:T(1,128)}) custom-call(bf16[512,256]{1,0:T(8,128)(2,1)S(1)} %get-tuple-element.29.refs_3_.refs_2_.refs_0_, bf16[512,256]{1,0:T(8,128)(2,1)S(1)} %get-tuple-element.30.refs_4_.refs_3_.refs_1_, f32[2,512,512]{2,1,0:T(8,128)S(1)} %get-tuple-element.28.refs_2_.refs_1_.refs_3_, ...), custom_call_target="tpu_custom_call" | custom-call | bytes 3672064 | tf_op jit(solution)/shard_map/prior/pallas_call | solution.py:145
  13.9 0.0 copy-done.2
  13.9 1.0 %links.1.refs_0_ = f32[2,256,256]{2,1,0:T(8,128)S(1)} custom-call(s32[2,4]{1,0:T(2,128)S(1)} %copy-done.2, f32[2,64,512]{2,1,0:T(8,128)S(1)} %copy-done, f32[2,64,512]{2,1,0:T(8,128)S(1)} %collective-permute-done.refs_2_.refs_0_.refs_3_.refs_4_, bf16[512,256]{1,0:T(8,128)(2,1)S(1)} %get-tuple-element.29.refs_3_.refs_2_.refs_0_, ...), custom_call_target="tpu_custom_call" | custom-call | bytes 3145728 | tf_op jit(solution)/shard_map/links/pallas_call | solution.py:145
  14.9 4.3 %collective-permute-done.2.refs_0_.refs_4_.refs_5_ = f32[2,64,512]{2,1,0:T(8,128)S(1)} collective-permute-done((f32[2,64,512]{2,1,0:T(8,128)S(1)}, f32[2,64,512]{2,1,0:T(8,128)S(1)}, u32[]{:S(2)}, u32[]{:S(2)}) %collective-permute-start.2) | collective-permute-done | bytes 262176 | tf_op jit(solution)/shard_map/ppermute | solution.py:491
  19.3 0.3 second.1.refs_1_
  19.6 1.2 %collective-permute-done.3.refs_2_.refs_10_ = f32[2,64,256]{2,1,0:T(8,128)S(1)} collective-permute-done((f32[2,64,256]{2,1,0:T(8,128)S(1)}, f32[2,64,256]{2,1,0:T(8,128)S(1)}, u32[]{:S(2)}, u32[]{:S(2)}) %collective-permute-start.3) | collective-permute-done | bytes 131104 | tf_op jit(solution)/shard_map/ppermute | solution.py:491
  20.8 0.6 %segment.1 = (f32[2,256,256]{2,1,0:T(8,128)S(1)}, f32[512,256]{1,0:T(8,128)S(1)}) custom-call(f32[2,256,256]{2,1,0:T(8,128)S(1)} %links.1.refs_0_, f32[2,64,256]{2,1,0:T(8,128)S(1)} %second.1.refs_1_, f32[2,64,256]{2,1,0:T(8,128)S(1)} %collective-permute-done.3.refs_2_.refs_10_, f32[256,256]{1,0:T(8,128)S(1)} %get-tuple-element.36.refs_3_, ...), custom_call_target="tpu_custom_call" | custom-call | flops 301989888 | bytes 2359296 | tf_op jit(solution)/shard_map/segment/pallas_call | solution.py:145
  21.4 0.1 collective-permute-start.4
  21.5 1.9 %collective-permute-done.4.refs_1_.refs_7_ = f32[512,256]{1,0:T(8,128)S(1)} collective-permute-done((f32[512,256]{1,0:T(8,128)S(1)}, f32[512,256]{1,0:T(8,128)S(1)}, u32[]{:S(2)}, u32[]{:S(2)}) %collective-permute-start.4) | collective-permute-done | bytes 524320 | tf_op jit(solution)/shard_map/ppermute | solution.py:586
  23.4 0.6 %chip.1 = (f32[256,256]{1,0:T(8,128)S(1)}, f32[256,256]{1,0:T(8,128)S(1)}, f32[160,128]{1,0:T(8,128)S(1)}, f32[128,256]{1,0:T(8,128)S(1)}) custom-call(f32[512,256]{1,0:T(8,128)S(1)} %get-tuple-element.38.refs_0_, f32[512,256]{1,0:T(8,128)S(1)} %collective-permute-done.4.refs_1_.refs_7_), custom_call_target="tpu_custom_call" | custom-call | flops 301989888 | bytes 1785856 | tf_op jit(solution)/shard_map/chip/pallas_call | solution.py:145
  24.0 1.6 %collective-permute-start.5 = (f32[128,256]{1,0:T(8,128)S(1)}, f32[128,256]{1,0:T(8,128)S(1)}, u32[]{:S(2)}, u32[]{:S(2)}) collective-permute-start(f32[128,256]{1,0:T(8,128)S(1)} %get-tuple-element.41), channel_id=1, source_target_pairs={{0,8},{4,12},{8,0},{12,4},{16,24},{20,28},{24,16},{28,20},{1,9},{5... | collective-permute-start | bytes 393224 | tf_op jit(solution)/shard_map/ppermute | solution.py:645
  25.6 0.5 %collective-permute-start.7 = (f32[160,128]{1,0:T(8,128)S(1)}, f32[160,128]{1,0:T(8,128)S(1)}, u32[]{:S(2)}, u32[]{:S(2)}) collective-permute-start(f32[160,128]{1,0:T(8,128)S(1)} %get-tuple-element.42.refs_6_), channel_id=1, source_target_pairs={{0,8},{4,12},{8,0},{12,4},{16,24},{20,28},{24,16},{28,20},{1,9},{5... | collective-permute-start | bytes 245768 | tf_op jit(solution)/shard_map/ppermute | solution.py:639
  26.1 1.5 %maps.1 = (f32[2,256,512]{2,1,0:T(8,128)S(1)}, f32[1,128]{1,0:T(1,128)S(1)}) custom-call(s32[2,4]{1,0:T(2,128)S(1)} %copy-done.2, f32[2,512,512]{2,1,0:T(8,128)S(1)} %get-tuple-element.28.refs_2_.refs_1_.refs_3_, f32[2,64,512]{2,1,0:T(8,128)S(1)} %copy-done, f32[2,64,512]{2,1,0:T(8,128)S(1)} %collective-permute-done.refs_2_.refs_0_.refs_3_.refs_4_, ...), custom_call_target="tpu_custom_call" | custom-call | flops 805306368 | bytes 3932672 | tf_op jit(solution)/shard_map/maps/pallas_call | solution.py:145
  27.6 1.2 %rest.1 = f32[2,64,256]{2,1,0:T(8,128)S(1)} custom-call(s32[2,4]{1,0:T(2,128)S(1)} %copy-done.2, s32[2,4]{1,0:T(2,128)S(1)} %copy-done.1, s32[2,4]{1,0:T(2,128)S(1)} %collective-permute-done.1.refs_1_.refs_3_.refs_2_, f32[2,512,512]{2,1,0:T(8,128)S(1)} %get-tuple-element.28.refs_2_.refs_1_.refs_3_, ...), custom_call_target="tpu_custom_call" | custom-call | flops 201326592 | bytes 2834432 | tf_op jit(solution)/shard_map/rest/pallas_call | solution.py:145
  28.8 0.3 collective-permute-start.10
  29.2 1.2 %collective-permute-done.5.refs_2_.refs_12_ = f32[128,256]{1,0:T(8,128)S(1)} collective-permute-done((f32[128,256]{1,0:T(8,128)S(1)}, f32[128,256]{1,0:T(8,128)S(1)}, u32[]{:S(2)}, u32[]{:S(2)}) %collective-permute-start.5) | collective-permute-done | bytes 131104 | tf_op jit(solution)/shard_map/ppermute | solution.py:645
  30.4 0.0 collective-permute-start.6
  30.4 1.0 %collective-permute-done.7 = f32[160,128]{1,0:T(8,128)S(1)} collective-permute-done((f32[160,128]{1,0:T(8,128)S(1)}, f32[160,128]{1,0:T(8,128)S(1)}, u32[]{:S(2)}, u32[]{:S(2)}) %collective-permute-start.7) | collective-permute-done | bytes 81952 | tf_op jit(solution)/shard_map/ppermute | solution.py:639
  31.4 0.1 collective-permute-start.8
  31.4 1.3 %collective-permute-done.8.refs_5_.refs_15_ = f32[160,128]{1,0:T(8,128)S(1)} collective-permute-done((f32[160,128]{1,0:T(8,128)S(1)}, f32[160,128]{1,0:T(8,128)S(1)}, u32[]{:S(2)}, u32[]{:S(2)}) %collective-permute-start.8) | collective-permute-done | bytes 81952 | tf_op jit(solution)/shard_map/ppermute | solution.py:648
  32.7 0.0 collective-permute-done.6.refs_3_.refs_13_
  32.7 0.8 %merge.1 = f32[160,128]{1,0:T(8,128)S(1)} custom-call(f32[256,256]{1,0:T(8,128)S(1)} %get-tuple-element.39.refs_0_, f32[256,256]{1,0:T(8,128)S(1)} %get-tuple-element.40.refs_1_, f32[128,256]{1,0:T(8,128)S(1)} %collective-permute-done.5.refs_2_.refs_12_, f32[128,256]{1,0:T(8,128)S(1)} %collective-permute-done.6.refs_3_.refs_13_, ...), custom_call_target="tpu_custom_call" | custom-call | flops 301989888 | bytes 1032192 | tf_op jit(solution)/shard_map/merge/pallas_call | solution.py:145
  33.5 2.1 %collective-permute-start.9 = (f32[160,128]{1,0:T(8,128)S(1)}, f32[160,128]{1,0:T(8,128)S(1)}, u32[]{:S(2)}, u32[]{:S(2)}) collective-permute-start(f32[160,128]{1,0:T(8,128)S(1)} %merge.1), channel_id=1, source_target_pairs={{0,16},{4,20},{8,24},{12,28},{16,0},{20,4},{24,8},{28,12},{1,17},{... | collective-permute-start | bytes 245768 | tf_op jit(solution)/shard_map/ppermute | solution.py:639
  35.7 0.0 collective-permute-done.10.refs_11_
  35.7 2.9 %prepare.1 = (bf16[384,256]{1,0:T(8,128)(2,1)S(1)}, bf16[384,256]{1,0:T(8,128)(2,1)S(1)}, bf16[2,256,512]{2,1,0:T(8,128)(2,1)S(1)}, bf16[2,256,512]{2,1,0:T(8,12...) custom-call(s32[2,4]{1,0:T(2,128)S(1)} %copy-done.2, s32[2,4]{1,0:T(2,128)S(1)} %copy-done.1, ...), custom_call_target="tpu_custom_call" | custom-call | flops 1459617792 | bytes 7504384 | tf_op jit(solution)/shard_map/prepare/pallas_call | solution.py:145
  38.6 0.0 collective-permute-done.9
  38.6 0.1 collective-permute-start.11
  38.7 1.3 %collective-permute-done.11.refs_1_ = f32[160,128]{1,0:T(8,128)S(1)} collective-permute-done((f32[160,128]{1,0:T(8,128)S(1)}, f32[160,128]{1,0:T(8,128)S(1)}, u32[]{:S(2)}, u32[]{:S(2)}) %collective-permute-start.11) | collective-permute-done | bytes 81952 | tf_op jit(solution)/shard_map/ppermute | solution.py:643
  40.0 1.8 %finish.1 = (f32[2,128,512]{2,1,0:T(8,128)}, f32[2,64,512]{2,1,0:T(8,128)}) custom-call(f32[160,128]{1,0:T(8,128)S(1)} %broadcast_add_fusion.1.refs_0_, f32[160,128]{1,0:T(8,128)S(1)} %collective-permute-done.11.refs_1_, bf16[384,256]{1,0:T(8,128)(2,1)S(1)} %get-tuple-element.49.refs_2_, bf16[384,256]{1,0:T(8,128)(2,1)S(1)} %get-tuple-element.50.refs_3_, ...), custom_call_target="tpu_custom_call" | custom-call | flops 452984832 | bytes 4620288 | tf_op jit(solution)/shard_map/finish/pallas_call | solution.py:145
  (3 shorter events, 0.0 us)
Async XLA Ops:
  0.6 7.8 %copy-start = (f32[2,64,512]{2,1,0:T(8,128)S(1)}, f32[2,64,512]{2,1,0:T(8,128)}, u32[]{:S(2)}) copy-start(f32[2,64,512]{2,1,0:T(8,128)} %refs_2_.3) | copy-start | bytes 786436
  0.6 11.8 %collective-permute-start = (f32[2,64,512]{2,1,0:T(8,128)}, f32[2,64,512]{2,1,0:T(8,128)S(1)}, u32[]{:S(2)}, u32[]{:S(2)}) collective-permute-start(f32[2,64,512]{2,1,0:T(8,128)} %refs_2_.3), channel_id=1, source_target_pairs={{0,1},{1,2},{2,3},{3,0},{4,5},{5,6},{6,7},{7,4},{8,9},{9,10},{10,1... | collective-permute-start | bytes 786440 | tf_op jit(solution)/shard_map/ppermute | solution.py:491
  3.7 4.1 %collective-permute-start.1 = (s32[2,4]{1,0:T(2,128)}, s32[2,4]{1,0:T(2,128)S(1)}, u32[]{:S(2)}, u32[]{:S(2)}) collective-permute-start(s32[2,4]{1,0:T(2,128)} %refs_1_.7), channel_id=1, source_target_pairs={{0,4},{4,8},{8,12},{12,16},{16,20},{20,24},{24,28},{28,0},{1,5},{5... | collective-permute-start | bytes 104 | tf_op jit(solution)/shard_map/ppermute | solution.py:491
  5.4 5.3 %copy-start.1 = (s32[2,4]{1,0:T(2,128)S(1)}, s32[2,4]{1,0:T(2,128)}, u32[]{:S(2)}) copy-start(s32[2,4]{1,0:T(2,128)} %refs_1_.7) | copy-start | bytes 100
  8.5 10.8 %collective-permute-start.2 = (f32[2,64,512]{2,1,0:T(8,128)S(1)}, f32[2,64,512]{2,1,0:T(8,128)S(1)}, u32[]{:S(2)}, u32[]{:S(2)}) collective-permute-start(f32[2,64,512]{2,1,0:T(8,128)S(1)} %broadcast_add_fusion), channel_id=1, source_target_pairs={{0,3},{1,0},{2,1},{3,2},{4,7},{5,4},{6,5},{7,6},{8,11},{9,8},{10,9... | collective-permute-start | bytes 786440 | tf_op jit(solution)/shard_map/ppermute | solution.py:491
  12.7 1.2 %copy-start.2 = (s32[2,4]{1,0:T(2,128)S(1)}, s32[2,4]{1,0:T(2,128)}, u32[]{:S(2)}) copy-start(s32[2,4]{1,0:T(2,128)} %refs_0_.11) | copy-start | bytes 100
  12.7 8.0 %collective-permute-start.3 = (f32[2,64,256]{2,1,0:T(8,128)S(1)}, f32[2,64,256]{2,1,0:T(8,128)S(1)}, u32[]{:S(2)}, u32[]{:S(2)}) collective-permute-start(f32[2,64,256]{2,1,0:T(8,128)S(1)} %chosen.1), channel_id=1, source_target_pairs={{0,1},{1,2},{2,3},{3,0},{4,5},{5,6},{6,7},{7,4},{8,9},{9,10},{10,1... | collective-permute-start | bytes 393224 | tf_op jit(solution)/shard_map/ppermute | solution.py:491
  21.4 2.0 %collective-permute-start.4 = (f32[512,256]{1,0:T(8,128)S(1)}, f32[512,256]{1,0:T(8,128)S(1)}, u32[]{:S(2)}, u32[]{:S(2)}) collective-permute-start(f32[512,256]{1,0:T(8,128)S(1)} %get-tuple-element.38.refs_0_), channel_id=1, source_target_pairs={{0,4},{4,0},{8,12},{12,8},{16,20},{20,16},{24,28},{28,24},{1,5},{5... | collective-permute-start | bytes 1572872 | tf_op jit(solution)/shard_map/ppermute | solution.py:586
  24.0 6.4 %collective-permute-start.5 = (f32[128,256]{1,0:T(8,128)S(1)}, f32[128,256]{1,0:T(8,128)S(1)}, u32[]{:S(2)}, u32[]{:S(2)}) collective-permute-start(f32[128,256]{1,0:T(8,128)S(1)} %get-tuple-element.41), channel_id=1, source_target_pairs={{0,8},{4,12},{8,0},{12,4},{16,24},{20,28},{24,16},{28,20},{1,9},{5... | collective-permute-start | bytes 393224 | tf_op jit(solution)/shard_map/ppermute | solution.py:645
  25.6 5.8 %collective-permute-start.7 = (f32[160,128]{1,0:T(8,128)S(1)}, f32[160,128]{1,0:T(8,128)S(1)}, u32[]{:S(2)}, u32[]{:S(2)}) collective-permute-start(f32[160,128]{1,0:T(8,128)S(1)} %get-tuple-element.42.refs_6_), channel_id=1, source_target_pairs={{0,8},{4,12},{8,0},{12,4},{16,24},{20,28},{24,16},{28,20},{1,9},{5... | collective-permute-start | bytes 245768 | tf_op jit(solution)/shard_map/ppermute | solution.py:639
  28.8 6.9 %collective-permute-start.10 = (f32[2,64,256]{2,1,0:T(8,128)S(1)}, f32[2,64,256]{2,1,0:T(8,128)S(1)}, u32[]{:S(2)}, u32[]{:S(2)}) collective-permute-start(f32[2,64,256]{2,1,0:T(8,128)S(1)} %rest.1), channel_id=1, source_target_pairs={{0,1},{1,0},{2,3},{3,2},{4,5},{5,4},{6,7},{7,6},{8,9},{9,8},{10,11... | collective-permute-start | bytes 393224 | tf_op jit(solution)/shard_map/ppermute | solution.py:612
  30.4 2.3 %collective-permute-start.6 = (f32[128,256]{1,0:T(8,128)S(1)}, f32[128,256]{1,0:T(8,128)S(1)}, u32[]{:S(2)}, u32[]{:S(2)}) collective-permute-start(f32[128,256]{1,0:T(8,128)S(1)} %collective-permute-done.5.refs_2_.refs_12_), channel_id=1, source_target_pairs={{0,4},{4,0},{8,12},{12,8},{16,20},{20,16},{24,28},{28,24},{1,5},{5... | collective-permute-start | bytes 393224 | tf_op jit(solution)/shard_map/ppermute | solution.py:648
  31.4 1.3 %collective-permute-start.8 = (f32[160,128]{1,0:T(8,128)S(1)}, f32[160,128]{1,0:T(8,128)S(1)}, u32[]{:S(2)}, u32[]{:S(2)}) collective-permute-start(f32[160,128]{1,0:T(8,128)S(1)} %broadcast_add_fusion.2.refs_4_.refs_14_), channel_id=1, source_target_pairs={{0,4},{4,0},{8,12},{12,8},{16,20},{20,16},{24,28},{28,24},{1,5},{5... | collective-permute-start | bytes 245768 | tf_op jit(solution)/shard_map/ppermute | solution.py:648
  33.5 5.1 %collective-permute-start.9 = (f32[160,128]{1,0:T(8,128)S(1)}, f32[160,128]{1,0:T(8,128)S(1)}, u32[]{:S(2)}, u32[]{:S(2)}) collective-permute-start(f32[160,128]{1,0:T(8,128)S(1)} %merge.1), channel_id=1, source_target_pairs={{0,16},{4,20},{8,24},{12,28},{16,0},{20,4},{24,8},{28,12},{1,17},{... | collective-permute-start | bytes 245768 | tf_op jit(solution)/shard_map/ppermute | solution.py:639
  38.6 1.3 %collective-permute-start.11 = (f32[160,128]{1,0:T(8,128)S(1)}, f32[160,128]{1,0:T(8,128)S(1)}, u32[]{:S(2)}, u32[]{:S(2)}) collective-permute-start(f32[160,128]{1,0:T(8,128)S(1)} %broadcast_add_fusion.1.refs_0_), channel_id=1, source_target_pairs={{0,4},{4,0},{8,12},{12,8},{16,20},{20,16},{24,28},{28,24},{1,5},{5... | collective-permute-start | bytes 245768 | tf_op jit(solution)/shard_map/ppermute | solution.py:643

commit v22 on v20

--- a/solution.py
+++ b/solution.py
@@ -35,6 +35,13 @@
 def carry(link_t, cov, base):
     link_t = link_t if isinstance(link_t, tuple) else split(link_t)
     return mm(mm(link_t, cov), link_t, NT) + base
+
+
+def carry_both(down_t, cov, link_t, base):
+    down_t = split(down_t)
+    size = cov.shape[0]
+    both = mm(down_t, jnp.concatenate([cov, link_t], 1))
+    return mm(both[:, :size], down_t, NT) + base, both[:, size:]
 
 
 def pack(cov):
@@ -314,9 +321,7 @@
         if cov is None:
             cov, link_t = base_refs[p][...], own_t
         else:
-            own_t = split(own_t)
-            cov = carry(own_t, cov, base_refs[p][...])
-            link_t = mm(own_t, link_t)
+            cov, link_t = carry_both(own_t, cov, link_t, base_refs[p][...])
     whole_ref[:size] = link_t
     whole_ref[size:] = cov
 
@@ -336,9 +341,12 @@
     lower = is_lower()
     own_t, other_t = own_ref[:size, :], other_ref[:size, :]
     own, other = own_ref[size:, :], other_ref[size:, :]
-    down_t = split(jnp.where(lower, own_t, other_t))
-    cov = carry(down_t, jnp.where(lower, other, own), jnp.where(lower, own, other))
-    link_t = mm(down_t, jnp.where(lower, other_t, own_t))
+    cov, link_t = carry_both(
+        jnp.where(lower, own_t, other_t),
+        jnp.where(lower, other, own),
+        jnp.where(lower, other_t, own_t),
+        jnp.where(lower, own, other),
+    )
     link_t_ref[...] = link_t
     cov_ref[...] = cov
     packed_ref[...] = own_half(pack(cov))

time: 42 us -> 42 us (level)
  no operation moved by 1% of the time
where the time goes in v22:
time: 42 us; the launch traced here: 41.9 us
  Pallas kernels  15.5 us (37%)
  waiting for transfers between devices  15.4 us (37%)
  starting transfers between devices  10 us (24%)
  between operations  0.82 us (2%)
    pallas_call x14, Pallas kernels, call(): pl.pallas_call(inner, out_shape=[*outs, *(jax.ShapeDtypeStruct(a.shape, a...  15.5 us
    ppermute x4, waiting for transfers between devices, turn(): lax.ppermute(x, axis, [(i, (i + distance) % count) for i in range(count)])  8.81 us
    ppermute x4, starting transfers between devices, turn(): lax.ppermute(x, axis, [(i, (i + distance) % count) for i in range(count)])  5.28 us
    ppermute x2, starting transfers between devices, body(): got = lax.ppermute(send, 'seg', partner)  2.67 us
    ppermute x1, waiting for transfers between devices, body(): other_whole = lax.ppermute(own_whole, 'seg', swap)  1.9 us
    ppermute x1, starting transfers between devices, body(): got_t = lax.ppermute(send_t, 'seg', partner)  1.55 us
    ppermute x1, waiting for transfers between devices, body(): after = (got, lax.ppermute(got, 'seg', swap))  1.26 us
    ppermute x1, waiting for transfers between devices, body(): lax.ppermute(got, 'seg', swap)  1.26 us
  transfers between devices with their start and end apart: 12, of which 9 were waited for; matrix products, arithmetic and copies ran while one was open for 0% of the time, Pallas kernels for 30%

profile of v22, /device:TPU:0, one launch (start us, length us, event | category | flops | bytes accessed | tf_op | source)
XLA Modules:
  0.0 41.9 jit_solution(14109065489904268394)
XLA Ops:
  0.6 0.0 copy-start
  0.6 3.1 %collective-permute-start = (f32[2,64,512]{2,1,0:T(8,128)}, f32[2,64,512]{2,1,0:T(8,128)S(1)}, u32[]{:S(2)}, u32[]{:S(2)}) collective-permute-start(f32[2,64,512]{2,1,0:T(8,128)} %refs_2_.3), channel_id=1, source_target_pairs={{0,1},{1,2},{2,3},{3,0},{4,5},{5,6},{6,7},{7,4},{8,9},{9,10},{10,1... | collective-permute-start | bytes 786440 | tf_op jit(solution)/shard_map/ppermute | solution.py:495
  3.7 0.0 collective-permute-start.1
  3.7 1.6 %load.1 = (f32[2,512,512]{2,1,0:T(8,128)S(1)}, bf16[512,256]{1,0:T(8,128)(2,1)S(1)}, bf16[512,256]{1,0:T(8,128)(2,1)S(1)}, f32[2,64,256]{2,1,0:T(8,128)S(1)}, f32[2,64,256]{2,1,0:T(8,128)S(1)}) custom-call(s32[2,4]{1,0:T(2,128)} %refs_0_.11, s32[2,4]{1,0:T(2,128)} %refs_1_.7, f32[2,512,512]{2,1,0:T(8,128)} %refs_2_.2), custom_call_target="tpu_custom_call" | custom-call | bytes 5505088 | tf_op jit(solution)/shard_map/load/pallas_call | solution.py:152
  5.4 0.0 copy-start.1
  5.4 2.5 %collective-permute-done.1.refs_1_.refs_3_.refs_2_ = s32[2,4]{1,0:T(2,128)S(1)} collective-permute-done((s32[2,4]{1,0:T(2,128)}, s32[2,4]{1,0:T(2,128)S(1)}, u32[]{:S(2)}, u32[]{:S(2)}) %collective-permute-start.1) | collective-permute-done | bytes 64 | tf_op jit(solution)/shard_map/ppermute | solution.py:495
  7.8 0.6 %prior.2 = (f32[256,256]{1,0:T(8,128)S(1)}, f32[128,512]{1,0:T(8,128)S(1)}, f32[1,1,512]{2,1,0:T(1,128)S(1)}) custom-call(bf16[512,256]{1,0:T(8,128)(2,1)S(1)} %get-tuple-element.31.refs_5_.refs_0_.refs_4_, bf16[512,256]{1,0:T(8,128)(2,1)S(1)} %get-tuple-element.32.refs_6_.refs_1_.refs_5_, f32[2,512,512]{2,1,0:T(8,128)S(1)} %get-tuple-element.28.refs_2_.refs_1_.refs_3_, ...), custom_call_target="tpu_custom_call" | custom-call | bytes 3672064 | tf_op jit(solution)/shard_map/prior/pallas_call | solution.py:152
  8.5 0.0 copy-done
  8.5 2.1 %collective-permute-start.2 = (f32[2,64,512]{2,1,0:T(8,128)S(1)}, f32[2,64,512]{2,1,0:T(8,128)S(1)}, u32[]{:S(2)}, u32[]{:S(2)}) collective-permute-start(f32[2,64,512]{2,1,0:T(8,128)S(1)} %broadcast_add_fusion), channel_id=1, source_target_pairs={{0,3},{1,0},{2,1},{3,2},{4,7},{5,4},{6,5},{7,6},{8,11},{9,8},{10,9... | collective-permute-start | bytes 786440 | tf_op jit(solution)/shard_map/ppermute | solution.py:495
  10.7 0.0 copy-done.1
  10.7 0.9 %pick.1 = (bf16[512,256]{1,0:T(8,128)(2,1)S(1)}, bf16[512,256]{1,0:T(8,128)(2,1)S(1)}) custom-call(s32[2,4]{1,0:T(2,128)S(1)} %copy-done.1, s32[2,4]{1,0:T(2,128)S(1)} %collective-permute-done.1.refs_1_.refs_3_.refs_2_, f32[2,512,512]{2,1,0:T(8,128)S(1)} %get-tuple-element.28.refs_2_.refs_1_.refs_3_), custom_call_target="tpu_custom_call" | custom-call | bytes 3145728 | tf_op jit(solution)/shard_map/pick/pallas_call | solution.py:152
  11.6 0.8 %collective-permute-done.refs_2_.refs_0_.refs_3_.refs_4_ = f32[2,64,512]{2,1,0:T(8,128)S(1)} collective-permute-done((f32[2,64,512]{2,1,0:T(8,128)}, f32[2,64,512]{2,1,0:T(8,128)S(1)}, u32[]{:S(2)}, u32[]{:S(2)}) %collective-permute-start) | collective-permute-done | bytes 262176 | tf_op jit(solution)/shard_map/ppermute | solution.py:495
  12.4 0.3 chosen.1
  12.7 0.0 copy-start.2
  12.7 0.1 collective-permute-start.3
  12.8 1.1 %prior.3 = (f32[256,256]{1,0:T(8,128)S(1)}, f32[128,512]{1,0:T(8,128)S(1)}, f32[1,1,512]{2,1,0:T(1,128)}) custom-call(bf16[512,256]{1,0:T(8,128)(2,1)S(1)} %get-tuple-element.29.refs_3_.refs_2_.refs_0_, bf16[512,256]{1,0:T(8,128)(2,1)S(1)} %get-tuple-element.30.refs_4_.refs_3_.refs_1_, f32[2,512,512]{2,1,0:T(8,128)S(1)} %get-tuple-element.28.refs_2_.refs_1_.refs_3_, ...), custom_call_target="tpu_custom_call" | custom-call | bytes 3672064 | tf_op jit(solution)/shard_map/prior/pallas_call | solution.py:152
  13.9 0.0 copy-done.2
  13.9 1.0 %links.1.refs_0_ = f32[2,256,256]{2,1,0:T(8,128)S(1)} custom-call(s32[2,4]{1,0:T(2,128)S(1)} %copy-done.2, f32[2,64,512]{2,1,0:T(8,128)S(1)} %copy-done, f32[2,64,512]{2,1,0:T(8,128)S(1)} %collective-permute-done.refs_2_.refs_0_.refs_3_.refs_4_, bf16[512,256]{1,0:T(8,128)(2,1)S(1)} %get-tuple-element.29.refs_3_.refs_2_.refs_0_, ...), custom_call_target="tpu_custom_call" | custom-call | bytes 3145728 | tf_op jit(solution)/shard_map/links/pallas_call | solution.py:152
  14.9 4.3 %collective-permute-done.2.refs_0_.refs_4_.refs_5_ = f32[2,64,512]{2,1,0:T(8,128)S(1)} collective-permute-done((f32[2,64,512]{2,1,0:T(8,128)S(1)}, f32[2,64,512]{2,1,0:T(8,128)S(1)}, u32[]{:S(2)}, u32[]{:S(2)}) %collective-permute-start.2) | collective-permute-done | bytes 262176 | tf_op jit(solution)/shard_map/ppermute | solution.py:495
  19.3 0.3 second.1.refs_1_
  19.6 1.2 %collective-permute-done.3.refs_2_.refs_10_ = f32[2,64,256]{2,1,0:T(8,128)S(1)} collective-permute-done((f32[2,64,256]{2,1,0:T(8,128)S(1)}, f32[2,64,256]{2,1,0:T(8,128)S(1)}, u32[]{:S(2)}, u32[]{:S(2)}) %collective-permute-start.3) | collective-permute-done | bytes 131104 | tf_op jit(solution)/shard_map/ppermute | solution.py:495
  20.8 0.7 %segment.1 = (f32[2,256,256]{2,1,0:T(8,128)S(1)}, f32[512,256]{1,0:T(8,128)S(1)}) custom-call(f32[2,256,256]{2,1,0:T(8,128)S(1)} %links.1.refs_0_, f32[2,64,256]{2,1,0:T(8,128)S(1)} %second.1.refs_1_, f32[2,64,256]{2,1,0:T(8,128)S(1)} %collective-permute-done.3.refs_2_.refs_10_, f32[256,256]{1,0:T(8,128)S(1)} %get-tuple-element.36.refs_3_, ...), custom_call_target="tpu_custom_call" | custom-call | flops 301989888 | bytes 2359296 | tf_op jit(solution)/shard_map/segment/pallas_call | solution.py:152
  21.4 0.1 collective-permute-start.4
  21.5 1.9 %collective-permute-done.4.refs_1_.refs_7_ = f32[512,256]{1,0:T(8,128)S(1)} collective-permute-done((f32[512,256]{1,0:T(8,128)S(1)}, f32[512,256]{1,0:T(8,128)S(1)}, u32[]{:S(2)}, u32[]{:S(2)}) %collective-permute-start.4) | collective-permute-done | bytes 524320 | tf_op jit(solution)/shard_map/ppermute | solution.py:590
  23.4 0.6 %chip.1 = (f32[256,256]{1,0:T(8,128)S(1)}, f32[256,256]{1,0:T(8,128)S(1)}, f32[160,128]{1,0:T(8,128)S(1)}, f32[128,256]{1,0:T(8,128)S(1)}) custom-call(f32[512,256]{1,0:T(8,128)S(1)} %get-tuple-element.38.refs_0_, f32[512,256]{1,0:T(8,128)S(1)} %collective-permute-done.4.refs_1_.refs_7_), custom_call_target="tpu_custom_call" | custom-call | flops 301989888 | bytes 1785856 | tf_op jit(solution)/shard_map/chip/pallas_call | solution.py:152
  24.0 1.6 %collective-permute-start.5 = (f32[128,256]{1,0:T(8,128)S(1)}, f32[128,256]{1,0:T(8,128)S(1)}, u32[]{:S(2)}, u32[]{:S(2)}) collective-permute-start(f32[128,256]{1,0:T(8,128)S(1)} %get-tuple-element.41), channel_id=1, source_target_pairs={{0,8},{4,12},{8,0},{12,4},{16,24},{20,28},{24,16},{28,20},{1,9},{5... | collective-permute-start | bytes 393224 | tf_op jit(solution)/shard_map/ppermute | solution.py:649
  25.5 0.5 %collective-permute-start.7 = (f32[160,128]{1,0:T(8,128)S(1)}, f32[160,128]{1,0:T(8,128)S(1)}, u32[]{:S(2)}, u32[]{:S(2)}) collective-permute-start(f32[160,128]{1,0:T(8,128)S(1)} %get-tuple-element.42.refs_6_), channel_id=1, source_target_pairs={{0,8},{4,12},{8,0},{12,4},{16,24},{20,28},{24,16},{28,20},{1,9},{5... | collective-permute-start | bytes 245768 | tf_op jit(solution)/shard_map/ppermute | solution.py:643
  26.1 1.5 %maps.1 = (f32[2,256,512]{2,1,0:T(8,128)S(1)}, f32[1,128]{1,0:T(1,128)S(1)}) custom-call(s32[2,4]{1,0:T(2,128)S(1)} %copy-done.2, f32[2,512,512]{2,1,0:T(8,128)S(1)} %get-tuple-element.28.refs_2_.refs_1_.refs_3_, f32[2,64,512]{2,1,0:T(8,128)S(1)} %copy-done, f32[2,64,512]{2,1,0:T(8,128)S(1)} %collective-permute-done.refs_2_.refs_0_.refs_3_.refs_4_, ...), custom_call_target="tpu_custom_call" | custom-call | flops 805306368 | bytes 3932672 | tf_op jit(solution)/shard_map/maps/pallas_call | solution.py:152
  27.6 1.2 %rest.1 = f32[2,64,256]{2,1,0:T(8,128)S(1)} custom-call(s32[2,4]{1,0:T(2,128)S(1)} %copy-done.2, s32[2,4]{1,0:T(2,128)S(1)} %copy-done.1, s32[2,4]{1,0:T(2,128)S(1)} %collective-permute-done.1.refs_1_.refs_3_.refs_2_, f32[2,512,512]{2,1,0:T(8,128)S(1)} %get-tuple-element.28.refs_2_.refs_1_.refs_3_, ...), custom_call_target="tpu_custom_call" | custom-call | flops 201326592 | bytes 2834432 | tf_op jit(solution)/shard_map/rest/pallas_call | solution.py:152
  28.8 0.3 collective-permute-start.10
  29.2 1.2 %collective-permute-done.5.refs_2_.refs_12_ = f32[128,256]{1,0:T(8,128)S(1)} collective-permute-done((f32[128,256]{1,0:T(8,128)S(1)}, f32[128,256]{1,0:T(8,128)S(1)}, u32[]{:S(2)}, u32[]{:S(2)}) %collective-permute-start.5) | collective-permute-done | bytes 131104 | tf_op jit(solution)/shard_map/ppermute | solution.py:649
  30.4 0.0 collective-permute-start.6
  30.4 1.0 %collective-permute-done.7 = f32[160,128]{1,0:T(8,128)S(1)} collective-permute-done((f32[160,128]{1,0:T(8,128)S(1)}, f32[160,128]{1,0:T(8,128)S(1)}, u32[]{:S(2)}, u32[]{:S(2)}) %collective-permute-start.7) | collective-permute-done | bytes 81952 | tf_op jit(solution)/shard_map/ppermute | solution.py:643
  31.4 0.1 collective-permute-start.8
  31.4 1.3 %collective-permute-done.8.refs_5_.refs_15_ = f32[160,128]{1,0:T(8,128)S(1)} collective-permute-done((f32[160,128]{1,0:T(8,128)S(1)}, f32[160,128]{1,0:T(8,128)S(1)}, u32[]{:S(2)}, u32[]{:S(2)}) %collective-permute-start.8) | collective-permute-done | bytes 81952 | tf_op jit(solution)/shard_map/ppermute | solution.py:652
  32.7 0.0 collective-permute-done.6.refs_3_.refs_13_
  32.7 0.8 %merge.1 = f32[160,128]{1,0:T(8,128)S(1)} custom-call(f32[256,256]{1,0:T(8,128)S(1)} %get-tuple-element.39.refs_0_, f32[256,256]{1,0:T(8,128)S(1)} %get-tuple-element.40.refs_1_, f32[128,256]{1,0:T(8,128)S(1)} %collective-permute-done.5.refs_2_.refs_12_, f32[128,256]{1,0:T(8,128)S(1)} %collective-permute-done.6.refs_3_.refs_13_, ...), custom_call_target="tpu_custom_call" | custom-call | flops 301989888 | bytes 1032192 | tf_op jit(solution)/shard_map/merge/pallas_call | solution.py:152
  33.5 2.1 %collective-permute-start.9 = (f32[160,128]{1,0:T(8,128)S(1)}, f32[160,128]{1,0:T(8,128)S(1)}, u32[]{:S(2)}, u32[]{:S(2)}) collective-permute-start(f32[160,128]{1,0:T(8,128)S(1)} %merge.1), channel_id=1, source_target_pairs={{0,16},{4,20},{8,24},{12,28},{16,0},{20,4},{24,8},{28,12},{1,17},{... | collective-permute-start | bytes 245768 | tf_op jit(solution)/shard_map/ppermute | solution.py:643
  35.7 0.0 collective-permute-done.10.refs_11_
  35.7 2.9 %prepare.1 = (bf16[384,256]{1,0:T(8,128)(2,1)S(1)}, bf16[384,256]{1,0:T(8,128)(2,1)S(1)}, bf16[2,256,512]{2,1,0:T(8,128)(2,1)S(1)}, bf16[2,256,512]{2,1,0:T(8,12...) custom-call(s32[2,4]{1,0:T(2,128)S(1)} %copy-done.2, s32[2,4]{1,0:T(2,128)S(1)} %copy-done.1, ...), custom_call_target="tpu_custom_call" | custom-call | flops 1459617792 | bytes 7504384 | tf_op jit(solution)/shard_map/prepare/pallas_call | solution.py:152
  38.6 0.0 collective-permute-done.9
  38.6 0.1 collective-permute-start.11
  38.7 1.3 %collective-permute-done.11.refs_1_ = f32[160,128]{1,0:T(8,128)S(1)} collective-permute-done((f32[160,128]{1,0:T(8,128)S(1)}, f32[160,128]{1,0:T(8,128)S(1)}, u32[]{:S(2)}, u32[]{:S(2)}) %collective-permute-start.11) | collective-permute-done | bytes 81952 | tf_op jit(solution)/shard_map/ppermute | solution.py:647
  40.0 1.9 %finish.1 = (f32[2,128,512]{2,1,0:T(8,128)}, f32[2,64,512]{2,1,0:T(8,128)}) custom-call(f32[160,128]{1,0:T(8,128)S(1)} %broadcast_add_fusion.1.refs_0_, f32[160,128]{1,0:T(8,128)S(1)} %collective-permute-done.11.refs_1_, bf16[384,256]{1,0:T(8,128)(2,1)S(1)} %get-tuple-element.49.refs_2_, bf16[384,256]{1,0:T(8,128)(2,1)S(1)} %get-tuple-element.50.refs_3_, ...), custom_call_target="tpu_custom_call" | custom-call | flops 452984832 | bytes 4620288 | tf_op jit(solution)/shard_map/finish/pallas_call | solution.py:152
  (3 shorter events, 0.0 us)
Async XLA Ops:
  0.6 7.8 %copy-start = (f32[2,64,512]{2,1,0:T(8,128)S(1)}, f32[2,64,512]{2,1,0:T(8,128)}, u32[]{:S(2)}) copy-start(f32[2,64,512]{2,1,0:T(8,128)} %refs_2_.3) | copy-start | bytes 786436
  0.6 11.8 %collective-permute-start = (f32[2,64,512]{2,1,0:T(8,128)}, f32[2,64,512]{2,1,0:T(8,128)S(1)}, u32[]{:S(2)}, u32[]{:S(2)}) collective-permute-start(f32[2,64,512]{2,1,0:T(8,128)} %refs_2_.3), channel_id=1, source_target_pairs={{0,1},{1,2},{2,3},{3,0},{4,5},{5,6},{6,7},{7,4},{8,9},{9,10},{10,1... | collective-permute-start | bytes 786440 | tf_op jit(solution)/shard_map/ppermute | solution.py:495
  3.7 4.1 %collective-permute-start.1 = (s32[2,4]{1,0:T(2,128)}, s32[2,4]{1,0:T(2,128)S(1)}, u32[]{:S(2)}, u32[]{:S(2)}) collective-permute-start(s32[2,4]{1,0:T(2,128)} %refs_1_.7), channel_id=1, source_target_pairs={{0,4},{4,8},{8,12},{12,16},{16,20},{20,24},{24,28},{28,0},{1,5},{5... | collective-permute-start | bytes 104 | tf_op jit(solution)/shard_map/ppermute | solution.py:495
  5.4 5.3 %copy-start.1 = (s32[2,4]{1,0:T(2,128)S(1)}, s32[2,4]{1,0:T(2,128)}, u32[]{:S(2)}) copy-start(s32[2,4]{1,0:T(2,128)} %refs_1_.7) | copy-start | bytes 100
  8.5 10.8 %collective-permute-start.2 = (f32[2,64,512]{2,1,0:T(8,128)S(1)}, f32[2,64,512]{2,1,0:T(8,128)S(1)}, u32[]{:S(2)}, u32[]{:S(2)}) collective-permute-start(f32[2,64,512]{2,1,0:T(8,128)S(1)} %broadcast_add_fusion), channel_id=1, source_target_pairs={{0,3},{1,0},{2,1},{3,2},{4,7},{5,4},{6,5},{7,6},{8,11},{9,8},{10,9... | collective-permute-start | bytes 786440 | tf_op jit(solution)/shard_map/ppermute | solution.py:495
  12.7 1.2 %copy-start.2 = (s32[2,4]{1,0:T(2,128)S(1)}, s32[2,4]{1,0:T(2,128)}, u32[]{:S(2)}) copy-start(s32[2,4]{1,0:T(2,128)} %refs_0_.11) | copy-start | bytes 100
  12.7 8.0 %collective-permute-start.3 = (f32[2,64,256]{2,1,0:T(8,128)S(1)}, f32[2,64,256]{2,1,0:T(8,128)S(1)}, u32[]{:S(2)}, u32[]{:S(2)}) collective-permute-start(f32[2,64,256]{2,1,0:T(8,128)S(1)} %chosen.1), channel_id=1, source_target_pairs={{0,1},{1,2},{2,3},{3,0},{4,5},{5,6},{6,7},{7,4},{8,9},{9,10},{10,1... | collective-permute-start | bytes 393224 | tf_op jit(solution)/shard_map/ppermute | solution.py:495
  21.4 2.0 %collective-permute-start.4 = (f32[512,256]{1,0:T(8,128)S(1)}, f32[512,256]{1,0:T(8,128)S(1)}, u32[]{:S(2)}, u32[]{:S(2)}) collective-permute-start(f32[512,256]{1,0:T(8,128)S(1)} %get-tuple-element.38.refs_0_), channel_id=1, source_target_pairs={{0,4},{4,0},{8,12},{12,8},{16,20},{20,16},{24,28},{28,24},{1,5},{5... | collective-permute-start | bytes 1572872 | tf_op jit(solution)/shard_map/ppermute | solution.py:590
  24.0 6.4 %collective-permute-start.5 = (f32[128,256]{1,0:T(8,128)S(1)}, f32[128,256]{1,0:T(8,128)S(1)}, u32[]{:S(2)}, u32[]{:S(2)}) collective-permute-start(f32[128,256]{1,0:T(8,128)S(1)} %get-tuple-element.41), channel_id=1, source_target_pairs={{0,8},{4,12},{8,0},{12,4},{16,24},{20,28},{24,16},{28,20},{1,9},{5... | collective-permute-start | bytes 393224 | tf_op jit(solution)/shard_map/ppermute | solution.py:649
  25.5 5.8 %collective-permute-start.7 = (f32[160,128]{1,0:T(8,128)S(1)}, f32[160,128]{1,0:T(8,128)S(1)}, u32[]{:S(2)}, u32[]{:S(2)}) collective-permute-start(f32[160,128]{1,0:T(8,128)S(1)} %get-tuple-element.42.refs_6_), channel_id=1, source_target_pairs={{0,8},{4,12},{8,0},{12,4},{16,24},{20,28},{24,16},{28,20},{1,9},{5... | collective-permute-start | bytes 245768 | tf_op jit(solution)/shard_map/ppermute | solution.py:643
  28.8 6.8 %collective-permute-start.10 = (f32[2,64,256]{2,1,0:T(8,128)S(1)}, f32[2,64,256]{2,1,0:T(8,128)S(1)}, u32[]{:S(2)}, u32[]{:S(2)}) collective-permute-start(f32[2,64,256]{2,1,0:T(8,128)S(1)} %rest.1), channel_id=1, source_target_pairs={{0,1},{1,0},{2,3},{3,2},{4,5},{5,4},{6,7},{7,6},{8,9},{9,8},{10,11... | collective-permute-start | bytes 393224 | tf_op jit(solution)/shard_map/ppermute | solution.py:616
  30.4 2.3 %collective-permute-start.6 = (f32[128,256]{1,0:T(8,128)S(1)}, f32[128,256]{1,0:T(8,128)S(1)}, u32[]{:S(2)}, u32[]{:S(2)}) collective-permute-start(f32[128,256]{1,0:T(8,128)S(1)} %collective-permute-done.5.refs_2_.refs_12_), channel_id=1, source_target_pairs={{0,4},{4,0},{8,12},{12,8},{16,20},{20,16},{24,28},{28,24},{1,5},{5... | collective-permute-start | bytes 393224 | tf_op jit(solution)/shard_map/ppermute | solution.py:652
  31.4 1.3 %collective-permute-start.8 = (f32[160,128]{1,0:T(8,128)S(1)}, f32[160,128]{1,0:T(8,128)S(1)}, u32[]{:S(2)}, u32[]{:S(2)}) collective-permute-start(f32[160,128]{1,0:T(8,128)S(1)} %broadcast_add_fusion.2.refs_4_.refs_14_), channel_id=1, source_target_pairs={{0,4},{4,0},{8,12},{12,8},{16,20},{20,16},{24,28},{28,24},{1,5},{5... | collective-permute-start | bytes 245768 | tf_op jit(solution)/shard_map/ppermute | solution.py:652
  33.5 5.1 %collective-permute-start.9 = (f32[160,128]{1,0:T(8,128)S(1)}, f32[160,128]{1,0:T(8,128)S(1)}, u32[]{:S(2)}, u32[]{:S(2)}) collective-permute-start(f32[160,128]{1,0:T(8,128)S(1)} %merge.1), channel_id=1, source_target_pairs={{0,16},{4,20},{8,24},{12,28},{16,0},{20,4},{24,8},{28,12},{1,17},{... | collective-permute-start | bytes 245768 | tf_op jit(solution)/shard_map/ppermute | solution.py:643
  38.6 1.3 %collective-permute-start.11 = (f32[160,128]{1,0:T(8,128)S(1)}, f32[160,128]{1,0:T(8,128)S(1)}, u32[]{:S(2)}, u32[]{:S(2)}) collective-permute-start(f32[160,128]{1,0:T(8,128)S(1)} %broadcast_add_fusion.1.refs_0_), channel_id=1, source_target_pairs={{0,4},{4,0},{8,12},{12,8},{16,20},{20,16},{24,28},{28,24},{1,5},{5... | collective-permute-start | bytes 245768 | tf_op jit(solution)/shard_map/ppermute | solution.py:647
